TPU v7x, 32 devices: a whole 2x2x4 slice. The times are simulated.
32 devices in a mesh: dp: 2 (over x), roll: 4 (over z), tp: 4 (over y, core).
Axes of the slice: x: 2, y: 2, z: 4, core: 2. Of those that a mesh axis runs over, the one named last changes fastest.
Arguments:
- train_inputs: bfloat16 [3072, 4096], P(('dp', 'roll'), 'tp'), may hold values from -75 to 75
- train_cotangent: bfloat16 [3072, 4096], P(('dp', 'roll'), 'tp'), may hold values from -75 to 75
- factor_a: float32 [4096, 128], P('tp'), may hold values from -0.09375 to 0.09375
- factor_b: float32 [128, 4096], P(None, 'tp'), may hold values from -0.18 to 0.18
- base_weight: bfloat16 [4096, 4096], P('tp'), may hold values from -0.09375 to 0.09375
- incoming: bfloat16 [2, 2048, 4096], P(None, ('dp', 'roll'), 'tp'), may hold values from -75 to 75
- norm_gain: float32 [4096], P('tp'), may hold values from 0.1 to 1.9
- positions: int32 [2048], P(('dp', 'roll')), may hold values from 0 to 8191
Outputs:
- new_a: float32 [4096, 128], P('tp')
- new_b: float32 [128, 4096], P(None, 'tp')
- queries: bfloat16 [2, 2048, 4096], P(None, ('dp', 'roll'), 'tp')
All inputs are finite; a program needn't handle non-finite values.
Results may differ from a plain program's by a relative error of at most 0.015.
Values may be sent and summed in bfloat16 or wider, within the bound.
No kernel may reach another device: no remote copies, remote signals or barrier semaphores. Data moves between devices by JAX's collectives and lax.ppermute only.
A program may use at most 128 MiB of HBM per device.

v0:
```python
import jax
import jax.numpy as jnp
from jax import lax
from jax.sharding import PartitionSpec as P

D = 4096
HEAD = 128


SCALE = 2.0
LEARN = 3.0
EPS = 1e-05
NORM_EPS = 1e-06


def rotate(values, angle_pos):
    count = values.shape[0]
    heads = values.reshape(count, -1, HEAD)
    half = HEAD // 2
    freq = 10000.0 ** (-jnp.arange(half, dtype=jnp.float32) / half)
    angle = angle_pos[:, None] * freq[None, :]
    cosine = jnp.cos(angle)[:, None, :]
    sine = jnp.sin(angle)[:, None, :]
    first = heads[..., :half]
    second = heads[..., half:]
    turned = jnp.concatenate(
        [first * cosine - second * sine, second * cosine + first * sine], axis=-1
    )
    return turned.reshape(count, -1)


def on_device(
    train_inputs, train_cotangent, factor_a, factor_b, base_weight, incoming, norm_gain, positions
):
    a_half = factor_a.astype(jnp.bfloat16)
    b_half = factor_b.astype(jnp.bfloat16)
    part_u = jnp.dot(train_inputs, a_half, preferred_element_type=jnp.float32)
    part_v = lax.dot_general(
        train_cotangent, b_half, (((1,), (1,)), ((), ())), preferred_element_type=jnp.float32
    )
    low_u, low_v = (
        lax.psum(part_u.astype(jnp.bfloat16), "tp").astype(jnp.float32),
        lax.psum(part_v.astype(jnp.bfloat16), "tp").astype(jnp.float32),
    )
    low_u = low_u.astype(jnp.bfloat16)
    low_v = low_v.astype(jnp.bfloat16)
    grad_a = SCALE * lax.dot_general(
        train_inputs, low_v, (((0,), (0,)), ((), ())), preferred_element_type=jnp.float32
    )
    grad_b = SCALE * lax.dot_general(
        low_u, train_cotangent, (((0,), (0,)), ((), ())), preferred_element_type=jnp.float32
    )
    grad_a, grad_b = lax.psum((grad_a, grad_b), ("dp", "roll"))
    total = lax.psum(jnp.sum(grad_a * grad_a) + jnp.sum(grad_b * grad_b), "tp")
    rate = LEARN * lax.rsqrt(total + NORM_EPS)
    new_a = factor_a - rate * grad_a
    new_b = factor_b - rate * grad_b
    full_b = lax.all_gather(new_b.astype(jnp.bfloat16), "tp", axis=1, tiled=True)
    merged = (
        base_weight.astype(jnp.float32)
        + SCALE * jnp.dot(new_a.astype(jnp.bfloat16), full_b, preferred_element_type=jnp.float32)
    ).astype(jnp.bfloat16)
    gain_row = norm_gain[None, :]
    results = []
    for stepnum in range(2):
        wide = incoming[stepnum].astype(jnp.float32)
        sumsq = lax.psum(jnp.sum(wide * wide, axis=-1), "tp")
        normed = (wide * lax.rsqrt(sumsq[:, None] / D + EPS) * gain_row).astype(jnp.bfloat16)
        terms = jnp.dot(normed, merged, preferred_element_type=jnp.float32)
        query = lax.psum_scatter(
            terms.astype(jnp.bfloat16), "tp", scatter_dimension=1, tiled=True
        ).astype(jnp.float32)
        angle_pos = positions.astype(jnp.float32) + float(stepnum)
        results.append(rotate(query, angle_pos).astype(jnp.bfloat16))
    return (new_a, new_b, jnp.stack(results))


def solution(mesh):
    return jax.shard_map(
        on_device,
        mesh=mesh,
        in_specs=(
            P(("dp", "roll"), "tp"),
            P(("dp", "roll"), "tp"),
            P("tp", None),
            P(None, "tp"),
            P("tp", None),
            P(None, ("dp", "roll"), "tp"),
            P("tp"),
            P(("dp", "roll")),
        ),
        out_specs=(P("tp", None), P(None, "tp"), P(None, ("dp", "roll"), "tp")),
        check_vma=False,
    )
```

profile of v0, /device:TPU:0, one launch (start us, length us, event | category | flops | bytes accessed | tf_op | source)
XLA Modules:
  0.0 249.1 jit_solution(11773319912181676642)
XLA Ops:
  7.2 0.0 copy-start
  7.2 0.0 copy-start.3
  7.2 0.0 all-reduce.8.cloned.1.call-start
  7.2 2.4 convolution_convert_fusion.2
  9.7 2.1 convolution_convert_fusion.3
  11.7 0.0 all-reduce.8.cloned.1.call-update
  11.8 0.0 all-reduce.6.cloned.1.call-start
  11.8 34.6 %all-reduce.8.cloned.1.call-done = (bf16[384,128]{1,0:T(8,128)(2,1)}, bf16[384,128]{1,0:T(8,128)(2,1)}) async-done(((bf16[384,128]{1,0:T(8,128)(2,1)}, bf16[384,128]{1,0:T(8,128)(2,1)}), (bf16[384,128]{1,0:T(8,128)(2,1)}, bf16[384,128]{1,0:T(8,128)(2,1)})) %all-reduce.8.cloned.1.call-update) | async-done | bytes 196624 | tf_op jit(solution)/shard_map/psum | solution.py:43
  46.4 2.0 convolution_multiply_fusion
  48.4 2.3 fusion
  50.7 0.0 all-reduce.6.cloned.1.call-update
  50.8 0.0 all-gather.2.cloned.1.call-start
  50.8 1.5 fusion.1
  52.3 76.9 %all-reduce.6.cloned.1.call-done = (f32[1024,128]{0,1:T(8,128)}, f32[128,1024]{1,0:T(8,128)}) async-done(((f32[1024,128]{0,1:T(8,128)}, f32[128,1024]{1,0:T(8,128)}), (f32[1024,128]{0,1:T(8,128)}, f32[128,1024]{1,0:T(8,128)})) %all-reduce.6.cloned.1.call-update) | async-done | bytes 1048592 | tf_op jit(solution)/shard_map/psum | solution.py:53
  129.2 1.8 multiply_reduce_fusion
  131.0 1.8 multiply_reduce_fusion.1
  134.1 6.4 %all-reduce.1 = (f32[]{:T(128)}, f32[256]{0:T(256)S(1)}, f32[256]{0:T(256)S(1)}) all-reduce(f32[]{:T(128)S(6)} %add.47, f32[256]{0:T(256)S(1)} %get-tuple-element.7, f32[256]{0:T(256)S(1)} %get-tuple-element.6), channel_id=1, replica_groups=mesh['dp'=2,'roll'=4,'tp'=4] {'tp'}, use_global_device_ids=true, to_apply=%region_6.0 | all-reduce | flops 513 | bytes 4104 | tf_op jit(solution)/shard_map/psum | solution.py:54
  141.2 0.0 copy-done.3
  141.2 2.0 fusion.20
  143.2 0.0 all-gather.2.cloned.1.call-update
  143.2 0.0 reduce-scatter.3.cloned.1.call-start
  143.3 0.2 copy.11
  143.5 1.1 multiply_subtract_fusion.1
  144.6 0.0 copy-start.4
  144.6 0.0 copy-start.6
  144.6 15.0 %all-gather.2.cloned.1.call-done = bf16[128,4096]{1,0:T(8,128)(2,1)} async-done(((bf16[128,1024]{1,0:T(8,128)(2,1)}), bf16[128,4096]{1,0:T(8,128)(2,1)}) %all-gather.2.cloned.1.call-update) | async-done | bytes 1048592 | tf_op jit(solution)/shard_map/all_gather | solution.py:58
  159.6 6.1 %add_convert_fusion = bf16[1024,4096]{1,0:T(8,128)(2,1)S(1)} fusion(bf16[1024,4096]{1,0:T(8,128)(2,1)} %param.12, bf16[128,4096]{1,0:T(8,128)(2,1)} %all-gather.2.cloned.1.call-done, f32[1024,128]{0,1:T(8,128)S(1)} %multiply_subtract_fusion.1), kind=kOutput, calls=%fused_computation | convolution fusion | flops 1090650112 | bytes 18350080 | tf_op jit(solution)/shard_map/dot_general | solution.py:61
  165.7 3.2 %copy-done.1 = bf16[1024,4096]{1,0:T(8,128)(2,1)} copy-done((bf16[1024,4096]{1,0:T(8,128)(2,1)}, bf16[1024,4096]{1,0:T(8,128)(2,1)S(1)}, u32[]{:S(2)}) %copy-start.1) | copy-done | bytes 8388632
  168.9 3.8 %convolution_convert_fusion.1 = bf16[256,4096]{1,0:T(8,128)(2,1)} fusion(bf16[1024,4096]{1,0:T(8,128)(2,1)S(1)} %add_convert_fusion, f32[1024]{0:T(1024)S(1)} %copy-done.6, f32[256]{0:T(256)S(1)} %add_rsqrt_fusion.1, bf16[2,256,1024]{2,1,0:T(8,128)(2,1)S(1)} %copy-done.4), kind=kOutput, calls=%fused_computation.2 | convolution fusion | flops 2149580800 | bytes 11015168 | tf_op jit(solution)/shard_map/dot_general | solution.py:69
  172.7 0.0 reduce-scatter.3.cloned.1.call-update
  172.7 0.2 reduce-scatter.5.cloned.1.call-start
  173.0 0.0 copy-start.5
  173.0 7.1 %convolution_convert_fusion = bf16[256,4096]{1,0:T(8,128)(2,1)} fusion(bf16[1024,4096]{1,0:T(8,128)(2,1)} %copy-done.1, f32[256]{0:T(256)S(1)} %add_rsqrt_fusion, f32[1024]{0:T(1024)S(1)} %copy-done.6, bf16[2,256,1024]{2,1,0:T(8,128)(2,1)S(1)} %copy-done.4), kind=kOutput, calls=%fused_computation.1 | convolution fusion | flops 2149580800 | bytes 11015168 | tf_op jit(solution)/shard_map/dot_general | solution.py:69
  180.1 0.0 reduce-scatter.5.cloned.1.call-update
  180.2 1.0 multiply_cosine_fusion.1
  181.2 1.0 copy.12
  182.2 22.1 %reduce-scatter.3.cloned.1.call-done = bf16[256,1024]{1,0:T(8,128)(2,1)} async-done(((bf16[256,4096]{1,0:T(8,128)(2,1)}), bf16[256,1024]{1,0:T(8,128)(2,1)}) %reduce-scatter.3.cloned.1.call-update) | async-done | bytes 524304 | tf_op jit(solution)/shard_map/reduce_scatter | solution.py:70
  204.3 1.1 convert_bitcast_fusion.1
  205.5 0.2 copy.13
  205.7 32.6 %reduce-scatter.5.cloned.1.call-done = bf16[256,1024]{1,0:T(8,128)(2,1)} async-done(((bf16[256,4096]{1,0:T(8,128)(2,1)}), bf16[256,1024]{1,0:T(8,128)(2,1)}) %reduce-scatter.5.cloned.1.call-update) | async-done | bytes 524304 | tf_op jit(solution)/shard_map/reduce_scatter | solution.py:70
  238.3 1.1 convert_bitcast_fusion
  239.5 0.2 copy.14
  239.7 0.8 subtract_convert_fusion
  240.4 0.3 pad_maximum_fusion.1
  240.7 0.2 convert_element_type.93
  241.0 0.3 pad_maximum_fusion.2
  241.3 0.2 convert_element_type.98
  241.5 1.1 pad_maximum_fusion
  (12 shorter events, 0.0 us)
Async XLA Ops:
  7.2 2.5 %copy-start = (bf16[384,1024]{1,0:T(8,128)(2,1)S(1)}, bf16[384,1024]{1,0:T(8,128)(2,1)}, u32[]{:S(2)}) copy-start(bf16[384,1024]{1,0:T(8,128)(2,1)} %param.9) | copy-start | bytes 2359300
  7.2 136.1 %copy-start.2 = (f32[1024,128]{1,0:T(8,128)S(1)}, f32[1024,128]{1,0:T(8,128)}, u32[]{:S(2)}) copy-start(f32[1024,128]{1,0:T(8,128)} %param.10) | copy-start | bytes 1572868
  7.2 134.0 %copy-start.3 = (f32[128,1024]{1,0:T(8,128)S(1)}, f32[128,1024]{1,0:T(8,128)}, u32[]{:S(2)}) copy-start(f32[128,1024]{1,0:T(8,128)} %param.11) | copy-start | bytes 1572868
  7.2 39.2 %all-reduce.8.cloned.1.call-start = ((), (), s32[]{:S(2)}) async-start(), calls=%async_computation.6 | async-start | bytes 393216 | tf_op jit(solution)/shard_map/psum | solution.py:43
  11.8 117.5 %all-reduce.6.cloned.1.call-start = ((), (), s32[]{:S(2)}) async-start(), calls=%async_computation.5 | async-start | bytes 2097152 | tf_op jit(solution)/shard_map/psum | solution.py:53
  50.8 108.9 %all-gather.2.cloned.1.call-start = ((), (), s32[]{:S(2)}) async-start(), calls=%async_computation.2 | async-start | bytes 1310720 | tf_op jit(solution)/shard_map/all_gather | solution.py:58
  143.2 61.1 %reduce-scatter.3.cloned.1.call-start = ((), (), s32[]{:S(2)}) async-start(), calls=%async_computation.3 | async-start | bytes 2621440 | tf_op jit(solution)/shard_map/reduce_scatter | solution.py:70
  144.6 24.4 %copy-start.4 = (bf16[2,256,1024]{2,1,0:T(8,128)(2,1)S(1)}, bf16[2,256,1024]{2,1,0:T(8,128)(2,1)}, u32[]{:S(2)}) copy-start(bf16[2,256,1024]{2,1,0:T(8,128)(2,1)} %param.13) | copy-start | bytes 3145732
  144.6 24.3 %copy-start.6 = (f32[1024]{0:T(1024)S(1)}, f32[1024]{0:T(1024)}, u32[]{:S(2)}) copy-start(f32[1024]{0:T(1024)} %param.14) | copy-start | bytes 12292
  165.7 3.2 %copy-start.1 = (bf16[1024,4096]{1,0:T(8,128)(2,1)}, bf16[1024,4096]{1,0:T(8,128)(2,1)S(1)}, u32[]{:S(2)}) copy-start(bf16[1024,4096]{1,0:T(8,128)(2,1)S(1)} %add_convert_fusion) | copy-start | bytes 25165828
  172.7 65.6 %reduce-scatter.5.cloned.1.call-start = ((), (), s32[]{:S(2)}) async-start(), calls=%async_computation.4 | async-start | bytes 2621440 | tf_op jit(solution)/shard_map/reduce_scatter | solution.py:70
  173.0 7.2 %copy-start.5 = (s32[256]{0:T(256)S(1)}, s32[256]{0:T(256)}, u32[]{:S(2)}) copy-start(s32[256]{0:T(256)} %param.15) | copy-start | bytes 3076
Sparse Core Ops, SparseCore 0:
  11.9 34.4 all-reduce.7
  51.0 78.2 all-reduce.5
  143.3 16.2 all-gather.1
  172.9 31.4 reduce-scatter.2
  206.9 31.3 reduce-scatter.4
where the time goes:
time: 250 us; the launch traced here: 249 us
  waiting for transfers between devices  181 us (72%)
  matrix products  25.8 us (10%)
  between operations  16 us (6%)
  other arithmetic  13.8 us (6%)
  blocking collectives  6.39 us (3%)
  local copies, waits for them, and re-layouts  5.29 us (2%)
    psum x1, waiting for transfers between devices, on_device(): grad_a, grad_b = lax.psum((grad_a, grad_b), ('dp', 'roll'))  76.9 us
    reduce_scatter x2, waiting for transfers between devices, on_device(): lax.psum_scatter(terms.astype(jnp.bfloat16), 'tp', scatter_dimension=1, t...  54.8 us
    psum x1, waiting for transfers between devices, on_device(): lax.psum(part_v.astype(jnp.bfloat16), 'tp').astype(jnp.float32)  34.6 us
    all_gather x1, waiting for transfers between devices, on_device(): lax.all_gather(new_b.astype(jnp.bfloat16), 'tp', axis=1, tiled=True)  15 us
    dot_general x2, matrix products, on_device(): terms = jnp.dot(normed, merged, preferred_element_type=jnp.float32)  10.9 us
    psum x1, blocking collectives, on_device(): total = lax.psum(jnp.sum(grad_a * grad_a) + jnp.sum(grad_b * grad_b), 'tp')  6.39 us
    dot_general x1, matrix products, on_device(): jnp.dot(new_a.astype(jnp.bfloat16), full_b, preferred_element_type=jnp.fl...  6.09 us
  transfers between devices with their start and end apart: 5, of which 5 were waited for; matrix products, arithmetic and copies ran while one was open for 5% of the time, Pallas kernels for 0%

commit v1 on v0

v1 whole, which is shorter than its diff:
```python
import jax
import jax.numpy as jnp
from jax import lax
from jax.sharding import PartitionSpec as P

D = 4096
HEAD = 128
SCALE = 2.0
LEARN = 3.0
EPS = 1e-05
NORM_EPS = 1e-06

BF = jnp.bfloat16
F32 = jnp.float32


def swap(x, axis, n, k):
    return lax.ppermute(x, axis, [(i, i ^ k) for i in range(n)])


def turn_tables(positions, steps):
    half = HEAD // 2
    freq = 10000.0 ** (-jnp.arange(half, dtype=F32) / half)
    cos, sin = [], []
    for step in range(steps):
        angle = (positions.astype(F32) + float(step))[:, None] * freq[None, :]
        c, s = jnp.cos(angle), jnp.sin(angle)
        cos.append(jnp.concatenate([c, c], axis=-1))
        sin.append(jnp.concatenate([-s, s], axis=-1))
    return jnp.stack(cos), jnp.stack(sin)


def build(n_dp, n_roll, n_tp):
    def scatter_sum(x, axis, n):
        me = lax.axis_index(axis)
        total = lax.dynamic_index_in_dim(x, me, 0, keepdims=False)
        got = [
            swap(lax.dynamic_index_in_dim(x, me ^ k, 0, keepdims=False).astype(BF), axis, n, k)
            for k in range(1, n)
        ]
        for g in got:
            total = total + g.astype(F32)
        return total

    def gather(x, axis, n):
        me = lax.axis_index(axis)
        out = jnp.zeros((n,) + x.shape, x.dtype)
        out = lax.dynamic_update_index_in_dim(out, x, me, 0)
        for k in range(1, n):
            out = lax.dynamic_update_index_in_dim(out, swap(x, axis, n, k), me ^ k, 0)
        return out

    def sum_tp(x):
        x = x + swap(x.astype(BF), "tp", n_tp, 1).astype(F32)
        return x + swap(x.astype(BF), "tp", n_tp, 2).astype(F32)

    def on_device(
        train_inputs, train_cotangent, factor_a, factor_b, base_weight, incoming, norm_gain, positions
    ):
        steps, rows, width = incoming.shape
        rank = factor_a.shape[1]
        tp = lax.axis_index("tp")
        part_u = jnp.dot(train_inputs, factor_a.astype(BF), preferred_element_type=F32)
        part_v = lax.dot_general(
            train_cotangent, factor_b.astype(BF), (((1,), (1,)), ((), ())), preferred_element_type=F32
        )
        low = sum_tp(jnp.stack([part_u, part_v])).astype(BF)

        wide = incoming.reshape(steps * rows, width).astype(F32)
        sumsq = jnp.sum(wide * wide, axis=-1)
        sumsq = sumsq + swap(sumsq, "tp", n_tp, 1)
        sumsq = sumsq + swap(sumsq, "tp", n_tp, 2)
        scale = lax.rsqrt(sumsq / D + EPS)[:, None]
        gained = (wide * norm_gain[None, :]).astype(BF)
        part_q = jnp.dot(gained, base_weight, preferred_element_type=F32).astype(BF)
        blocks = [
            lax.dynamic_slice_in_dim(part_q, (tp ^ k) * width, width, 1) for k in range(n_tp)
        ]
        far = (blocks[2].astype(F32) + swap(blocks[3], "tp", n_tp, 1).astype(F32)).astype(BF)
        base = blocks[0].astype(F32) + swap(blocks[1], "tp", n_tp, 1).astype(F32)
        base = base + swap(far, "tp", n_tp, 2).astype(F32)
        low_q = sum_tp(jnp.dot(gained, factor_a.astype(BF), preferred_element_type=F32))

        grad_a = SCALE * lax.dot_general(
            train_inputs, low[1], (((0,), (0,)), ((), ())), preferred_element_type=F32
        )
        grad_b = SCALE * lax.dot_general(
            train_cotangent, low[0], (((0,), (0,)), ((), ())), preferred_element_type=F32
        )
        grads = jnp.stack([grad_a, grad_b], axis=1)
        chunk = scatter_sum(grads.reshape(n_dp, width // n_dp, 2, rank), "dp", n_dp)
        chunk = scatter_sum(chunk.reshape(n_roll, -1, 2, rank), "roll", n_roll)
        grads = gather(gather(chunk.astype(BF), "roll", n_roll), "dp", n_dp)
        grads = grads.reshape(width, 2, rank)
        grad_a16, grad_b16 = grads[:, 0], grads[:, 1]
        grad_a = grad_a16.astype(F32)
        grad_b = grad_b16.astype(F32)
        total = jnp.sum(grad_a * grad_a) + jnp.sum(grad_b * grad_b)
        total = total + swap(total, "tp", n_tp, 1)
        total = total + swap(total, "tp", n_tp, 2)
        low_g = sum_tp(jnp.dot(gained, grad_a16, preferred_element_type=F32))
        rate = LEARN * lax.rsqrt(total + NORM_EPS)
        new_a = factor_a - rate * grad_a
        new_b = factor_b - rate * grad_b.T
        mix = (low_q - rate * low_g) * scale
        query = base * scale + SCALE * jnp.dot(
            mix.astype(BF), new_b.astype(BF), preferred_element_type=F32
        )
        cos, sin = turn_tables(positions, steps)
        heads = query.reshape(steps, rows, -1, HEAD)
        other = jnp.concatenate([heads[..., HEAD // 2 :], heads[..., : HEAD // 2]], axis=-1)
        turned = heads * cos[:, :, None, :] + other * sin[:, :, None, :]
        return new_a, new_b, turned.reshape(steps, rows, width).astype(BF)

    return on_device


def solution(mesh):
    n_dp, n_roll, n_tp = (mesh.shape[a] for a in ("dp", "roll", "tp"))
    return jax.shard_map(
        build(n_dp, n_roll, n_tp),
        mesh=mesh,
        in_specs=(
            P(("dp", "roll"), "tp"),
            P(("dp", "roll"), "tp"),
            P("tp", None),
            P(None, "tp"),
            P("tp", None),
            P(None, ("dp", "roll"), "tp"),
            P("tp"),
            P(("dp", "roll")),
        ),
        out_specs=(P("tp", None), P(None, "tp"), P(None, ("dp", "roll"), "tp")),
        check_vma=False,
    )
```

time: 250 us -> 118 us (0.47)
  waiting for transfers between devices: 181 us -> 24.9 us
  starting transfers between devices: 0.39 us -> 35 us
  between operations: 16 us -> 3.46 us
  local copies, waits for them, and re-layouts: 5.29 us -> 15.8 us
  matrix products: 25.8 us -> 18.5 us
  blocking collectives: 6.39 us -> 0 us
  other arithmetic: 13.8 us -> 20.1 us
    psum x2 -> x0, waiting for transfers between devices: 112 us -> none  [the longest x1 76.9 us: on_device(): grad_a, grad_b = lax.psum((grad_a, grad_b), ('dp', 'roll'))]
    reduce_scatter x2 -> x0, waiting for transfers between devices: 54.8 us -> none  [on_device(): lax.psum_scatter(terms.astype(jnp.bfloat16), 'tp', scatter_dimension=1, t...]
    ppermute x0 -> x21, starting transfers between devices: none -> 35 us  [swap(): return lax.ppermute(x, axis, [(i, i ^ k) for i in range(n)])]
    ppermute x0 -> x21, waiting for transfers between devices: none -> 24.9 us  [swap(): return lax.ppermute(x, axis, [(i, i ^ k) for i in range(n)])]
    all_gather x1 -> x0, waiting for transfers between devices: 15 us -> none  [on_device(): lax.all_gather(new_b.astype(jnp.bfloat16), 'tp', axis=1, tiled=True)]
    convert_element_type x2 -> x11, other arithmetic: 2 us -> 12.9 us  [the longest x1 3.73 us: on_device(): return (new_a, new_b, turned.reshape(steps, rows, width).astype(BF))]
    dot_general x7 -> x8, matrix products: 25.8 us -> 18.5 us  [the longest x1 8.1 us: on_device(): part_q = jnp.dot(gained, base_weight, preferred_element_type=F32).astype(BF)]
    psum x1 -> x0, blocking collectives: 6.39 us -> none  [on_device(): total = lax.psum(jnp.sum(grad_a * grad_a) + jnp.sum(grad_b * grad_b), 'tp')]
  transfers between devices with their start and end apart: 5 -> 21, of which waited for: 5 -> 11; matrix products, arithmetic and copies ran while one was open for 5% -> 31% of each run, Pallas kernels for 0% -> 0%
where the time goes in v1:
time: 118 us
  starting transfers between devices  35 us (30%)
  waiting for transfers between devices  24.9 us (21%)
  other arithmetic  20.1 us (17%)
  matrix products  18.5 us (16%)
  local copies, waits for them, and re-layouts  15.8 us (13%)
  between operations  3.46 us (3%)
    ppermute x21, starting transfers between devices, swap(): return lax.ppermute(x, axis, [(i, i ^ k) for i in range(n)])  35 us
    ppermute x21, waiting for transfers between devices, swap(): return lax.ppermute(x, axis, [(i, i ^ k) for i in range(n)])  24.9 us
    dot_general x1, matrix products, on_device(): part_q = jnp.dot(gained, base_weight, preferred_element_type=F32).astype(BF)  8.1 us
    unnamed x38, local copies, waits for them, and re-layouts  4.55 us
    mul x3, local copies, waits for them, and re-layouts, on_device(): turned = heads * cos[:, :, None, :] + other * sin[:, :, None, :]  4.45 us
    convert_element_type x1, other arithmetic, on_device(): return (new_a, new_b, turned.reshape(steps, rows, width).astype(BF))  3.73 us
    convert_element_type x1, other arithmetic, on_device(): (blocks[2].astype(F32) + swap(blocks[3], 'tp', n_tp, 1).astype(F32)).asty...  3 us
    convert_element_type x3, other arithmetic, sum_tp(): return x + swap(x.astype(BF), 'tp', n_tp, 2).astype(F32)  2.74 us
  transfers between devices with their start and end apart: 21, of which 11 were waited for; matrix products, arithmetic and copies ran while one was open for 31% of the time, Pallas kernels for 0%

profile of v1, /device:TPU:0, one launch (start us, length us, event | category | flops | bytes accessed | tf_op | source)
XLA Modules:
  0.0 117.7 jit_solution(14048411989137779762)
XLA Ops:
  0.7 1.8 %convolution_bitcast_fusion = f32[1,384,128]{2,1,0:T(8,128)S(1)} fusion(bf16[384,1024]{1,0:T(8,128)(2,1)} %param.9, f32[128,1024]{1,0:T(8,128)} %param.11), kind=kOutput, calls=%fused_computation.17 | convolution fusion | flops 100794368 | bytes 1507328 | tf_op jit(solution)/shard_map/dot_general | solution.py:64
  2.5 1.4 %convolution_bitcast_fusion.1 = f32[1,384,128]{2,1,0:T(8,128)S(1)} fusion(bf16[384,1024]{1,0:T(8,128)(2,1)S(1)} %copy-done, f32[1024,128]{1,0:T(8,128)} %param.10), kind=kOutput, calls=%fused_computation.18 | convolution fusion | flops 100794368 | bytes 1507328 | tf_op jit(solution)/shard_map/dot_general | solution.py:63
  5.3 8.1 %convolution_convert_fusion = bf16[512,4096]{1,0:T(8,128)(2,1)S(1)} fusion(bf16[512,1024]{1,0:T(8,128)(2,1)S(1)} %fusion, bf16[1024,4096]{1,0:T(8,128)(2,1)} %param.12), kind=kOutput, calls=%fused_computation | convolution fusion | flops 4297064448 | bytes 13631488 | tf_op jit(solution)/shard_map/dot_general | solution.py:75
  13.5 1.7 %constant_dynamic-slice_fusion.1 = (bf16[512,1024]{1,0:T(8,128)(2,1)}, bf16[512,1024]{1,0:T(8,128)(2,1)}) fusion(bf16[512,4096]{1,0:T(8,128)(2,1)S(1)} %convolution_convert_fusion, s32[]{:T(128)S(6)} %select_n.47, s32[]{:T(128)S(6)} %select_n.49), kind=kLoop, calls=%fused_computation.83 | loop fusion | bytes 4194312 | tf_op jit(solution)/shard_map/dynamic_slice | solution.py:77
  15.1 1.0 copy-done.3
  16.1 1.4 %multiply_convert_fusion = (bf16[2,256,1024]{2,1,0:T(8,128)(2,1)}, f32[2,256]{1,0:T(2,128)S(1)}) fusion(bf16[2,256,1024]{2,1,0:T(8,128)(2,1)S(1)} %copy-done.2, f32[1024]{0:T(1024)S(1)} %copy-done.15), kind=kLoop, calls=%fused_computation.6 | loop fusion | flops 2620928 | bytes 2103296 | tf_op jit(solution)/shard_map/convert_element_type | solution.py:74
  18.0 1.0 multiply_cosine_fusion.1
  19.2 1.1 fusion.18
  20.3 2.6 %collective-permute-start.1 = (bf16[2,384,128]{2,1,0:T(8,128)(2,1)S(1)}, bf16[2,384,128]{2,1,0:T(8,128)(2,1)S(1)}, u32[]{:S(2)}, u32[]{:S(2)}) collective-permute-start(bf16[2,384,128]{2,1,0:T(8,128)(2,1)S(1)} %fusion.18), channel_id=1, source_target_pairs={{0,2},{1,3},{2,0},{3,1},{4,6},{5,7},{6,4},{7,5},{8,10},{9,11},{10,... | collective-permute-start | bytes 589832 | tf_op jit(solution)/shard_map/ppermute | solution.py:18
  23.7 0.8 maximum_bitcast_fusion
  24.4 4.1 %collective-permute-done.1 = bf16[2,384,128]{2,1,0:T(8,128)(2,1)S(1)} collective-permute-done((bf16[2,384,128]{2,1,0:T(8,128)(2,1)S(1)}, bf16[2,384,128]{2,1,0:T(8,128)(2,1)S(1)}, u32[]{:S(2)}, u32[]{:S(2)}) %collective-permute-start.1) | collective-permute-done | bytes 196640 | tf_op jit(solution)/shard_map/ppermute | solution.py:18
  28.5 1.0 add_convert_fusion.2
  29.5 1.1 fusion.2
  30.6 1.1 fusion.1
  31.7 1.2 %copy.36 = f32[1024,128]{1,0:T(8,128)S(1)} copy(f32[1024,128]{0,1:T(8,128)} %fusion.2) | data formatting | bytes 1048576 | tf_op jit(solution)/shard_map/stack | solution.py:90
  33.0 1.2 %copy.37 = f32[1024,128]{1,0:T(8,128)S(1)} copy(f32[1024,128]{0,1:T(8,128)} %fusion.1) | data formatting | bytes 1048576 | tf_op jit(solution)/shard_map/stack | solution.py:90
  34.3 1.8 %collective-permute-start.2 = (bf16[512,2,128]{2,0,1:T(8,128)(2,1)S(1)}, bf16[512,2,128]{2,0,1:T(8,128)(2,1)S(1)}, u32[]{:S(2)}, u32[]{:S(2)}) collective-permute-start(bf16[512,2,128]{2,0,1:T(8,128)(2,1)S(1)} %fusion.14), channel_id=1, source_target_pairs={{0,16},{16,0},{1,17},{17,1},{2,18},{18,2},{3,19},{19,3},{4,20},{20... | collective-permute-start | bytes 786440 | tf_op jit(solution)/shard_map/ppermute | solution.py:18
  36.1 1.2 %fusion.40 = (bf16[512,128]{1,0:T(8,128)(2,1)}, f32[512,128]{1,0:T(8,128)}) fusion(bf16[512,1024]{1,0:T(8,128)(2,1)S(1)} %fusion, f32[1024,128]{1,0:T(8,128)S(1)} %copy-done.1), kind=kOutput, calls=%fused_computation.91 | convolution fusion | flops 134414336 | bytes 1966080 | tf_op jit(solution)/shard_map/dot_general | solution.py:82
  37.3 5.2 %collective-permute-done.2 = bf16[512,2,128]{2,0,1:T(8,128)(2,1)S(1)} collective-permute-done((bf16[512,2,128]{2,0,1:T(8,128)(2,1)S(1)}, bf16[512,2,128]{2,0,1:T(8,128)(2,1)S(1)}, u32[]{:S(2)}, u32[]{:S(2)}) %collective-permute-start.2) | collective-permute-done | bytes 262176 | tf_op jit(solution)/shard_map/ppermute | solution.py:18
  42.5 0.8 copy-done.12
  44.0 1.6 %collective-permute-start.3 = (bf16[128,2,128]{2,0,1:T(8,128)(2,1)}, bf16[128,2,128]{2,0,1:T(8,128)(2,1)S(1)}, u32[]{:S(2)}, u32[]{:S(2)}) collective-permute-start(bf16[128,2,128]{2,0,1:T(8,128)(2,1)} %get-tuple-element.20), channel_id=1, source_target_pairs={{0,4},{4,0},{8,12},{12,8},{1,5},{5,1},{9,13},{13,9},{2,6},{6,2},{1... | collective-permute-start | bytes 196616 | tf_op jit(solution)/shard_map/ppermute | solution.py:18
  45.6 2.6 %collective-permute-start.4 = (bf16[128,2,128]{2,0,1:T(8,128)(2,1)}, bf16[128,2,128]{2,0,1:T(8,128)(2,1)S(1)}, u32[]{:S(2)}, u32[]{:S(2)}) collective-permute-start(bf16[128,2,128]{2,0,1:T(8,128)(2,1)} %get-tuple-element.21), channel_id=1, source_target_pairs={{0,8},{4,12},{8,0},{12,4},{1,9},{5,13},{9,1},{13,5},{2,10},{6,14},... | collective-permute-start | bytes 196616 | tf_op jit(solution)/shard_map/ppermute | solution.py:18
  48.4 1.0 copy.34
  49.6 1.6 %mul.178 = f32[2,256,1024]{2,1,0:T(8,128)} reshape(f32[2,256,8,128]{3,2,1,0:T(8,128)S(1)} %mul.177) | data formatting | bytes 4194304 | tf_op jit(solution)/shard_map/mul | solution.py:112
  52.4 1.5 %collective-permute-start.16 = (f32[512]{0:T(512)S(1)}, f32[512]{0:T(512)S(1)}, u32[]{:S(2)}, u32[]{:S(2)}) collective-permute-start(f32[512]{0:T(512)S(1)} %add.139), channel_id=1, source_target_pairs={{0,2},{1,3},{2,0},{3,1},{4,6},{5,7},{6,4},{7,5},{8,10},{9,11},{10,... | collective-permute-start | bytes 6152 | tf_op jit(solution)/shard_map/ppermute | solution.py:18
  54.3 1.0 bitcast_dynamic-update-slice_fusion.3
  56.0 2.6 %collective-permute-start.7 = (bf16[128,2,128]{2,0,1:T(8,128)(2,1)S(1)}, bf16[128,2,128]{2,0,1:T(8,128)(2,1)S(1)}, u32[]{:S(2)}, u32[]{:S(2)}) collective-permute-start(bf16[128,2,128]{2,0,1:T(8,128)(2,1)S(1)} %get-tuple-element.13), channel_id=1, source_target_pairs={{0,8},{4,12},{8,0},{12,4},{1,9},{5,13},{9,1},{13,5},{2,10},{6,14},... | collective-permute-start | bytes 196616 | tf_op jit(solution)/shard_map/ppermute | solution.py:18
  58.6 1.7 %collective-permute-done.6 = bf16[128,2,128]{2,0,1:T(8,128)(2,1)S(1)} collective-permute-done((bf16[128,2,128]{2,0,1:T(8,128)(2,1)S(1)}, bf16[128,2,128]{2,0,1:T(8,128)(2,1)S(1)}, u32[]{:S(2)}, u32[]{:S(2)}) %collective-permute-start.6) | collective-permute-done | bytes 65568 | tf_op jit(solution)/shard_map/ppermute | solution.py:18
  60.3 2.4 %collective-permute-start.8 = (bf16[128,2,128]{2,0,1:T(8,128)(2,1)S(1)}, bf16[128,2,128]{2,0,1:T(8,128)(2,1)S(1)}, u32[]{:S(2)}, u32[]{:S(2)}) collective-permute-start(bf16[128,2,128]{2,0,1:T(8,128)(2,1)S(1)} %get-tuple-element.13), channel_id=1, source_target_pairs={{0,12},{4,8},{8,4},{12,0},{1,13},{5,9},{9,5},{13,1},{2,14},{6,10},... | collective-permute-start | bytes 196616 | tf_op jit(solution)/shard_map/ppermute | solution.py:18
  63.2 3.1 %collective-permute-done.8 = bf16[128,2,128]{2,0,1:T(8,128)(2,1)S(1)} collective-permute-done((bf16[128,2,128]{2,0,1:T(8,128)(2,1)S(1)}, bf16[128,2,128]{2,0,1:T(8,128)(2,1)S(1)}, u32[]{:S(2)}, u32[]{:S(2)}) %collective-permute-start.8) | collective-permute-done | bytes 65568 | tf_op jit(solution)/shard_map/ppermute | solution.py:18
  66.4 1.6 %collective-permute-start.9 = (bf16[4,128,2,128]{3,1,2,0:T(8,128)(2,1)S(1)}, bf16[4,128,2,128]{3,1,2,0:T(8,128)(2,1)S(1)}, u32[]{:S(2)}, u32[]{:S(2)}) collective-permute-start(bf16[4,128,2,128]{3,1,2,0:T(8,128)(2,1)S(1)} %bitcast_dynamic-update-slice_fusion), channel_id=1, source_target_pairs={{0,16},{16,0},{1,17},{17,1},{2,18},{18,2},{3,19},{19,3},{4,20},{20... | collective-permute-start | bytes 786440 | tf_op jit(solution)/shard_map/ppermute | solution.py:18
  68.6 0.8 collective-permute-start.18
  70.0 2.8 %collective-permute-done.9 = bf16[4,128,2,128]{3,1,2,0:T(8,128)(2,1)S(1)} collective-permute-done((bf16[4,128,2,128]{3,1,2,0:T(8,128)(2,1)S(1)}, bf16[4,128,2,128]{3,1,2,0:T(8,128)(2,1)S(1)}, u32[]{:S(2)}, u32[]{:S(2)}) %collective-permute-start.9) | collective-permute-done | bytes 262176 | tf_op jit(solution)/shard_map/ppermute | solution.py:18
  73.6 3.0 %add_convert_fusion.1 = bf16[512,1024]{1,0:T(8,128)(2,1)} fusion(bf16[512,1024]{1,0:T(8,128)(2,1)} %collective-permute-done.13, bf16[512,4096]{1,0:T(8,128)(2,1)} %copy-done.3, s32[]{:T(128)S(6)} %select_n.48), kind=kLoop, calls=%fused_computation.8 | loop fusion | flops 2097152 | bytes 3145732 | tf_op jit(solution)/shard_map/convert_element_type | solution.py:79
  76.6 0.8 collective-permute-start.14
  77.4 1.1 fusion.39
  78.5 0.7 fusion.3
  81.2 1.5 %collective-permute-start.10 = (f32[]{:T(128)}, f32[]{:T(128)}, u32[]{:S(2)}, u32[]{:S(2)}) collective-permute-start(f32[]{:T(128)} %add.128), channel_id=1, source_target_pairs={{0,1},{1,0},{2,3},{3,2},{4,5},{5,4},{6,7},{7,6},{8,9},{9,8},{10,11... | collective-permute-start | bytes 20 | tf_op jit(solution)/shard_map/ppermute | solution.py:18
  83.3 12.5 %collective-permute-start.11 = (f32[]{:T(128)}, f32[]{:T(128)}, u32[]{:S(2)}, u32[]{:S(2)}) collective-permute-start(f32[]{:T(128)} %add.129), channel_id=1, source_target_pairs={{0,2},{1,3},{2,0},{3,1},{4,6},{5,7},{6,4},{7,5},{8,10},{9,11},{10,... | collective-permute-start | bytes 20 | tf_op jit(solution)/shard_map/ppermute | solution.py:18
  95.8 1.7 %collective-permute-done.11 = f32[]{:T(128)} collective-permute-done((f32[]{:T(128)}, f32[]{:T(128)}, u32[]{:S(2)}, u32[]{:S(2)}) %collective-permute-start.11) | collective-permute-done | bytes 36 | tf_op jit(solution)/shard_map/ppermute | solution.py:18
  98.2 1.0 copy.35
  99.2 0.9 fusion.21
  100.1 0.9 collective-permute-start.20
  101.1 4.0 %collective-permute-done.20 = bf16[512,128]{1,0:T(8,128)(2,1)S(1)} collective-permute-done((bf16[512,128]{1,0:T(8,128)(2,1)S(1)}, bf16[512,128]{1,0:T(8,128)(2,1)S(1)}, u32[]{:S(2)}, u32[]{:S(2)}) %collective-permute-start.20) | collective-permute-done | bytes 131104 | tf_op jit(solution)/shard_map/ppermute | solution.py:18
  105.2 2.7 %multiply_add_fusion = f32[512,1024]{1,0:T(8,128)S(1)} fusion(bf16[512,1024]{1,0:T(8,128)(2,1)} %collective-permute-done.14, bf16[512,1024]{1,0:T(8,128)(2,1)} %collective-permute-done.12, f32[512]{0:T(512)S(1)} %add_rsqrt_fusion, bf16[512,4096]{1,0:T(8,128)(2,1)} %copy-done.3, s32[]{:T(128)S(6)} %select_n.46, f32[128,1024]{1,0:T(8,128)S(1)} %fusion.7, ...), kind=kOutput, calls=%fused_computation.5 | convolution fusion | flops 139329536 | bytes 6819848 | tf_op jit(solution)/shard_map/dot_general | solution.py:106
  109.3 1.9 %maximum_multiply_fusion = f32[2,256,8,128]{3,2,1,0:T(8,128)} fusion(f32[2,256,8,64]{3,2,1,0:T(8,128)S(1)} %get-tuple-element.17, f32[2,256,8,64]{3,2,1,0:T(8,128)S(1)} %get-tuple-element.16, f32[2,256,128]{2,1,0:T(8,128)S(1)} %copy-done.13), kind=kLoop, calls=%fused_computation.1 | loop fusion | flops 1048576 | bytes 4456448 | tf_op jit(solution)/shard_map/mul | solution.py:112
  111.2 2.7 %mul.182 = f32[2,256,1024]{2,1,0:T(8,128)} reshape(f32[2,256,8,128]{3,2,1,0:T(8,128)} %maximum_multiply_fusion) | data formatting | bytes 4194304 | tf_op jit(solution)/shard_map/mul | solution.py:112
  114.0 3.7 %add_convert_fusion = bf16[2,256,1024]{2,1,0:T(8,128)(2,1)} fusion(f32[2,256,1024]{2,1,0:T(8,128)} %mul.182, f32[2,256,1024]{2,1,0:T(8,128)S(1)} %bitcast.109, f32[2,256,1024]{2,1,0:T(8,128)} %mul.178), kind=kLoop, calls=%fused_computation.4 | loop fusion | flops 1572864 | bytes 7340032 | tf_op jit(solution)/shard_map/convert_element_type | solution.py:113
  (85 shorter events, 11.1 us)
Async XLA Ops:
  0.6 1.8 %copy-start = (bf16[384,1024]{1,0:T(8,128)(2,1)S(1)}, bf16[384,1024]{1,0:T(8,128)(2,1)}, u32[]{:S(2)}) copy-start(bf16[384,1024]{1,0:T(8,128)(2,1)} %param.8) | copy-start | bytes 2359300
  0.6 4.4 %copy-start.2 = (bf16[2,256,1024]{2,1,0:T(8,128)(2,1)S(1)}, bf16[2,256,1024]{2,1,0:T(8,128)(2,1)}, u32[]{:S(2)}) copy-start(bf16[2,256,1024]{2,1,0:T(8,128)(2,1)} %param.13) | copy-start | bytes 3145732
  0.7 4.4 %copy-start.15 = (f32[1024]{0:T(1024)S(1)}, f32[1024]{0:T(1024)}, u32[]{:S(2)}) copy-start(f32[1024]{0:T(1024)} %param.14) | copy-start | bytes 12292
  3.9 9.6 %copy-start.6 = (f32[1,384,128]{2,1,0:T(8,128)}, f32[1,384,128]{2,1,0:T(8,128)S(1)}, u32[]{:S(2)}) copy-start(f32[1,384,128]{2,1,0:T(8,128)S(1)} %convolution_bitcast_fusion.1) | copy-start | bytes 589828
  4.6 14.6 %collective-permute-start = (bf16[2,384,128]{2,1,0:T(8,128)(2,1)}, bf16[2,384,128]{2,1,0:T(8,128)(2,1)}, u32[]{:S(2)}, u32[]{:S(2)}) collective-permute-start(bf16[2,384,128]{2,1,0:T(8,128)(2,1)} %fusion.13), channel_id=1, source_target_pairs={{0,1},{1,0},{2,3},{3,2},{4,5},{5,4},{6,7},{7,6},{8,9},{9,8},{10,11... | collective-permute-start | bytes 589832 | tf_op jit(solution)/shard_map/ppermute | solution.py:18
  13.4 2.6 %copy-start.3 = (bf16[512,4096]{1,0:T(8,128)(2,1)}, bf16[512,4096]{1,0:T(8,128)(2,1)S(1)}, u32[]{:S(2)}) copy-start(bf16[512,4096]{1,0:T(8,128)(2,1)S(1)} %convolution_convert_fusion) | copy-start | bytes 12582916
  16.1 1.9 %copy-start.16 = (s32[256]{0:T(256)S(1)}, s32[256]{0:T(256)}, u32[]{:S(2)}) copy-start(s32[256]{0:T(256)} %param.15) | copy-start | bytes 3076
  16.1 57.5 %collective-permute-start.13 = (bf16[512,1024]{1,0:T(8,128)(2,1)}, bf16[512,1024]{1,0:T(8,128)(2,1)}, u32[]{:S(2)}, u32[]{:S(2)}) collective-permute-start(bf16[512,1024]{1,0:T(8,128)(2,1)} %get-tuple-element.15), channel_id=1, source_target_pairs={{0,1},{1,0},{2,3},{3,2},{4,5},{5,4},{6,7},{7,6},{8,9},{9,8},{10,11... | collective-permute-start | bytes 3145736 | tf_op jit(solution)/shard_map/ppermute | solution.py:18
  17.5 11.0 %copy-start.7 = (f32[1,384,128]{2,1,0:T(8,128)S(1)}, f32[1,384,128]{2,1,0:T(8,128)}, u32[]{:S(2)}) copy-start(f32[1,384,128]{2,1,0:T(8,128)} %copy-done.6) | copy-start | bytes 589828
  17.5 33.6 %collective-permute-start.15 = (f32[512]{0:T(512)S(1)}, f32[512]{0:T(512)S(1)}, u32[]{:S(2)}, u32[]{:S(2)}) collective-permute-start(f32[512]{0:T(512)S(1)} %bitcast.121), channel_id=1, source_target_pairs={{0,1},{1,0},{2,3},{3,2},{4,5},{5,4},{6,7},{7,6},{8,9},{9,8},{10,11... | collective-permute-start | bytes 6152 | tf_op jit(solution)/shard_map/ppermute | solution.py:18
  19.2 11.4 %copy-start.5 = (bf16[384,1024]{1,0:T(8,128)(2,1)S(1)}, bf16[384,1024]{1,0:T(8,128)(2,1)}, u32[]{:S(2)}) copy-start(bf16[384,1024]{1,0:T(8,128)(2,1)} %param.9) | copy-start | bytes 2359300
  20.3 8.2 %collective-permute-start.1 = (bf16[2,384,128]{2,1,0:T(8,128)(2,1)S(1)}, bf16[2,384,128]{2,1,0:T(8,128)(2,1)S(1)}, u32[]{:S(2)}, u32[]{:S(2)}) collective-permute-start(bf16[2,384,128]{2,1,0:T(8,128)(2,1)S(1)} %fusion.18), channel_id=1, source_target_pairs={{0,2},{1,3},{2,0},{3,1},{4,6},{5,7},{6,4},{7,5},{8,10},{9,11},{10,... | collective-permute-start | bytes 589832 | tf_op jit(solution)/shard_map/ppermute | solution.py:18
  30.6 5.4 %copy-start.1 = (f32[1024,128]{1,0:T(8,128)S(1)}, f32[1024,128]{1,0:T(8,128)}, u32[]{:S(2)}) copy-start(f32[1024,128]{1,0:T(8,128)} %param.10) | copy-start | bytes 1572868
  34.3 14.1 %copy-start.14 = (f32[1,256,128]{2,1,0:T(8,128)S(1)}, f32[1,256,128]{2,1,0:T(8,128)}, u32[]{:S(2)}) copy-start(f32[1,256,128]{2,1,0:T(8,128)} %get-tuple-element.37) | copy-start | bytes 393220
  34.3 8.2 %collective-permute-start.2 = (bf16[512,2,128]{2,0,1:T(8,128)(2,1)S(1)}, bf16[512,2,128]{2,0,1:T(8,128)(2,1)S(1)}, u32[]{:S(2)}, u32[]{:S(2)}) collective-permute-start(bf16[512,2,128]{2,0,1:T(8,128)(2,1)S(1)} %fusion.14), channel_id=1, source_target_pairs={{0,16},{16,0},{1,17},{17,1},{2,18},{18,2},{3,19},{19,3},{4,20},{20... | collective-permute-start | bytes 786440 | tf_op jit(solution)/shard_map/ppermute | solution.py:18
  42.5 0.8 copy-start.12
  44.0 7.2 %collective-permute-start.3 = (bf16[128,2,128]{2,0,1:T(8,128)(2,1)}, bf16[128,2,128]{2,0,1:T(8,128)(2,1)S(1)}, u32[]{:S(2)}, u32[]{:S(2)}) collective-permute-start(bf16[128,2,128]{2,0,1:T(8,128)(2,1)} %get-tuple-element.20), channel_id=1, source_target_pairs={{0,4},{4,0},{8,12},{12,8},{1,5},{5,1},{9,13},{13,9},{2,6},{6,2},{1... | collective-permute-start | bytes 196616 | tf_op jit(solution)/shard_map/ppermute | solution.py:18
  45.6 6.8 %collective-permute-start.4 = (bf16[128,2,128]{2,0,1:T(8,128)(2,1)}, bf16[128,2,128]{2,0,1:T(8,128)(2,1)S(1)}, u32[]{:S(2)}, u32[]{:S(2)}) collective-permute-start(bf16[128,2,128]{2,0,1:T(8,128)(2,1)} %get-tuple-element.21), channel_id=1, source_target_pairs={{0,8},{4,12},{8,0},{12,4},{1,9},{5,13},{9,1},{13,5},{2,10},{6,14},... | collective-permute-start | bytes 196616 | tf_op jit(solution)/shard_map/ppermute | solution.py:18
  48.2 6.1 %collective-permute-start.5 = (bf16[128,2,128]{2,0,1:T(8,128)(2,1)S(1)}, bf16[128,2,128]{2,0,1:T(8,128)(2,1)S(1)}, u32[]{:S(2)}, u32[]{:S(2)}) collective-permute-start(bf16[128,2,128]{2,0,1:T(8,128)(2,1)S(1)} %get-tuple-element.22), channel_id=1, source_target_pairs={{0,12},{4,8},{8,4},{12,0},{1,13},{5,9},{9,5},{13,1},{2,14},{6,10},... | collective-permute-start | bytes 196616 | tf_op jit(solution)/shard_map/ppermute | solution.py:18
  49.6 18.4 %copy-start.8 = (f32[512,128]{1,0:T(8,128)S(1)}, f32[512,128]{1,0:T(8,128)}, u32[]{:S(2)}) copy-start(f32[512,128]{1,0:T(8,128)} %get-tuple-element.35) | copy-start | bytes 786436
  51.1 50.0 %collective-permute-start.12 = (bf16[512,1024]{1,0:T(8,128)(2,1)}, bf16[512,1024]{1,0:T(8,128)(2,1)}, u32[]{:S(2)}, u32[]{:S(2)}) collective-permute-start(bf16[512,1024]{1,0:T(8,128)(2,1)} %get-tuple-element.14), channel_id=1, source_target_pairs={{0,1},{1,0},{2,3},{3,2},{4,5},{5,4},{6,7},{7,6},{8,9},{9,8},{10,11... | collective-permute-start | bytes 3145736 | tf_op jit(solution)/shard_map/ppermute | solution.py:18
  51.2 16.8 %collective-permute-start.17 = (bf16[512,128]{1,0:T(8,128)(2,1)}, bf16[512,128]{1,0:T(8,128)(2,1)S(1)}, u32[]{:S(2)}, u32[]{:S(2)}) collective-permute-start(bf16[512,128]{1,0:T(8,128)(2,1)} %get-tuple-element.34), channel_id=1, source_target_pairs={{0,1},{1,0},{2,3},{3,2},{4,5},{5,4},{6,7},{7,6},{8,9},{9,8},{10,11... | collective-permute-start | bytes 393224 | tf_op jit(solution)/shard_map/ppermute | solution.py:18
  52.4 3.6 %collective-permute-start.16 = (f32[512]{0:T(512)S(1)}, f32[512]{0:T(512)S(1)}, u32[]{:S(2)}, u32[]{:S(2)}) collective-permute-start(f32[512]{0:T(512)S(1)} %add.139), channel_id=1, source_target_pairs={{0,2},{1,3},{2,0},{3,1},{4,6},{5,7},{6,4},{7,5},{8,10},{9,11},{10,... | collective-permute-start | bytes 6152 | tf_op jit(solution)/shard_map/ppermute | solution.py:18
  55.2 5.0 %collective-permute-start.6 = (bf16[128,2,128]{2,0,1:T(8,128)(2,1)S(1)}, bf16[128,2,128]{2,0,1:T(8,128)(2,1)S(1)}, u32[]{:S(2)}, u32[]{:S(2)}) collective-permute-start(bf16[128,2,128]{2,0,1:T(8,128)(2,1)S(1)} %get-tuple-element.13), channel_id=1, source_target_pairs={{0,4},{4,0},{8,12},{12,8},{1,5},{5,1},{9,13},{13,9},{2,6},{6,2},{1... | collective-permute-start | bytes 196616 | tf_op jit(solution)/shard_map/ppermute | solution.py:18
  56.0 7.2 %collective-permute-start.7 = (bf16[128,2,128]{2,0,1:T(8,128)(2,1)S(1)}, bf16[128,2,128]{2,0,1:T(8,128)(2,1)S(1)}, u32[]{:S(2)}, u32[]{:S(2)}) collective-permute-start(bf16[128,2,128]{2,0,1:T(8,128)(2,1)S(1)} %get-tuple-element.13), channel_id=1, source_target_pairs={{0,8},{4,12},{8,0},{12,4},{1,9},{5,13},{9,1},{13,5},{2,10},{6,14},... | collective-permute-start | bytes 196616 | tf_op jit(solution)/shard_map/ppermute | solution.py:18
  60.3 6.1 %collective-permute-start.8 = (bf16[128,2,128]{2,0,1:T(8,128)(2,1)S(1)}, bf16[128,2,128]{2,0,1:T(8,128)(2,1)S(1)}, u32[]{:S(2)}, u32[]{:S(2)}) collective-permute-start(bf16[128,2,128]{2,0,1:T(8,128)(2,1)S(1)} %get-tuple-element.13), channel_id=1, source_target_pairs={{0,12},{4,8},{8,4},{12,0},{1,13},{5,9},{9,5},{13,1},{2,14},{6,10},... | collective-permute-start | bytes 196616 | tf_op jit(solution)/shard_map/ppermute | solution.py:18
  66.4 6.4 %collective-permute-start.9 = (bf16[4,128,2,128]{3,1,2,0:T(8,128)(2,1)S(1)}, bf16[4,128,2,128]{3,1,2,0:T(8,128)(2,1)S(1)}, u32[]{:S(2)}, u32[]{:S(2)}) collective-permute-start(bf16[4,128,2,128]{3,1,2,0:T(8,128)(2,1)S(1)} %bitcast_dynamic-update-slice_fusion), channel_id=1, source_target_pairs={{0,16},{16,0},{1,17},{17,1},{2,18},{18,2},{3,19},{19,3},{4,20},{20... | collective-permute-start | bytes 786440 | tf_op jit(solution)/shard_map/ppermute | solution.py:18
  68.6 32.5 %collective-permute-start.18 = (bf16[512,128]{1,0:T(8,128)(2,1)}, bf16[512,128]{1,0:T(8,128)(2,1)}, u32[]{:S(2)}, u32[]{:S(2)}) collective-permute-start(bf16[512,128]{1,0:T(8,128)(2,1)} %fusion.20), channel_id=1, source_target_pairs={{0,2},{1,3},{2,0},{3,1},{4,6},{5,7},{6,4},{7,5},{8,10},{9,11},{10,... | collective-permute-start | bytes 393224 | tf_op jit(solution)/shard_map/ppermute | solution.py:18
  73.2 4.2 %copy-start.4 = (bf16[2,256,1024]{2,1,0:T(8,128)(2,1)S(1)}, bf16[2,256,1024]{2,1,0:T(8,128)(2,1)}, u32[]{:S(2)}) copy-start(bf16[2,256,1024]{2,1,0:T(8,128)(2,1)} %get-tuple-element.18) | copy-start | bytes 3145732
  73.6 24.6 %copy-start.10 = (f32[1024,128]{0,1:T(8,128)S(1)}, f32[1024,128]{0,1:T(8,128)}, u32[]{:S(2)}) copy-start(f32[1024,128]{0,1:T(8,128)} %copy.34) | copy-start | bytes 1572868
  76.6 28.6 %collective-permute-start.14 = (bf16[512,1024]{1,0:T(8,128)(2,1)}, bf16[512,1024]{1,0:T(8,128)(2,1)}, u32[]{:S(2)}, u32[]{:S(2)}) collective-permute-start(bf16[512,1024]{1,0:T(8,128)(2,1)} %add_convert_fusion.1), channel_id=1, source_target_pairs={{0,2},{1,3},{2,0},{3,1},{4,6},{5,7},{6,4},{7,5},{8,10},{9,11},{10,... | collective-permute-start | bytes 3145736 | tf_op jit(solution)/shard_map/ppermute | solution.py:18
  78.5 22.5 %copy-start.9 = (f32[128,1024]{1,0:T(8,128)S(1)}, f32[128,1024]{1,0:T(8,128)}, u32[]{:S(2)}) copy-start(f32[128,1024]{1,0:T(8,128)} %param.11) | copy-start | bytes 1572868
  78.5 20.7 %collective-permute-start.19 = (bf16[512,128]{1,0:T(8,128)(2,1)}, bf16[512,128]{1,0:T(8,128)(2,1)}, u32[]{:S(2)}, u32[]{:S(2)}) collective-permute-start(bf16[512,128]{1,0:T(8,128)(2,1)} %get-tuple-element.32), channel_id=1, source_target_pairs={{0,1},{1,0},{2,3},{3,2},{4,5},{5,4},{6,7},{7,6},{8,9},{9,8},{10,11... | collective-permute-start | bytes 393224 | tf_op jit(solution)/shard_map/ppermute | solution.py:18
  81.2 1.5 %collective-permute-start.10 = (f32[]{:T(128)}, f32[]{:T(128)}, u32[]{:S(2)}, u32[]{:S(2)}) collective-permute-start(f32[]{:T(128)} %add.128), channel_id=1, source_target_pairs={{0,1},{1,0},{2,3},{3,2},{4,5},{5,4},{6,7},{7,6},{8,9},{9,8},{10,11... | collective-permute-start | bytes 20 | tf_op jit(solution)/shard_map/ppermute | solution.py:18
  83.3 14.2 %collective-permute-start.11 = (f32[]{:T(128)}, f32[]{:T(128)}, u32[]{:S(2)}, u32[]{:S(2)}) collective-permute-start(f32[]{:T(128)} %add.129), channel_id=1, source_target_pairs={{0,2},{1,3},{2,0},{3,1},{4,6},{5,7},{6,4},{7,5},{8,10},{9,11},{10,... | collective-permute-start | bytes 20 | tf_op jit(solution)/shard_map/ppermute | solution.py:18
  100.1 5.0 %collective-permute-start.20 = (bf16[512,128]{1,0:T(8,128)(2,1)S(1)}, bf16[512,128]{1,0:T(8,128)(2,1)S(1)}, u32[]{:S(2)}, u32[]{:S(2)}) collective-permute-start(bf16[512,128]{1,0:T(8,128)(2,1)S(1)} %fusion.21), channel_id=1, source_target_pairs={{0,2},{1,3},{2,0},{3,1},{4,6},{5,7},{6,4},{7,5},{8,10},{9,11},{10,... | collective-permute-start | bytes 393224 | tf_op jit(solution)/shard_map/ppermute | solution.py:18
  101.1 6.8 %copy-start.11 = (f32[128,1024]{1,0:T(8,128)}, f32[128,1024]{1,0:T(8,128)S(1)}, u32[]{:S(2)}) copy-start(f32[128,1024]{1,0:T(8,128)S(1)} %fusion.7) | copy-start | bytes 1572868
  108.4 1.0 copy-start.13

commit v2 on v1

v2 whole, which is shorter than its diff:
```python
import functools

import jax
import jax.numpy as jnp
from jax import lax
from jax.experimental import pallas as pl
from jax.experimental.pallas import tpu as pltpu
from jax.sharding import PartitionSpec as P

D = 4096
HEAD = 128
SCALE = 2.0
LEARN = 3.0
EPS = 1e-05
NORM_EPS = 1e-06
LANES = 128
EXTRA = 32

BF = jnp.bfloat16
F32 = jnp.float32
VMEM = pl.BlockSpec(memory_space=pltpu.VMEM)
SMEM = pl.BlockSpec(memory_space=pltpu.SMEM)
ANY = pl.BlockSpec(memory_space=pl.ANY)
PARAMS = pltpu.CompilerParams(vmem_limit_bytes=32 * 1024 * 1024)


def shape(dims, dtype):
    return jax.ShapeDtypeStruct(dims, dtype)


def dot(a, b, dims=((1,), (0,))):
    return lax.dot_general(a, b, (dims, ((), ())), preferred_element_type=F32)


def swap(x, axis, n, k):
    return lax.ppermute(x, axis, [(i, i ^ k) for i in range(n)])


def split_terms(values):
    high = values.astype(BF)
    rest = values - high.astype(F32)
    middle = rest.astype(BF)
    last = (rest - middle.astype(F32)).astype(BF)
    return jnp.concatenate([high, middle, last, jnp.zeros_like(last)], axis=0)


def join_terms(ref, count):
    x = ref[count : count + EXTRA, :].astype(F32)
    return (x[0:8] + x[8:16]) + x[16:24]


def rank_kernel(x_ref, v_ref, a_ref, b_ref, out_ref):
    count = x_ref.shape[0]
    out_ref[:count] = dot(x_ref[...], a_ref[...].astype(BF)).astype(BF)
    out_ref[count:] = dot(v_ref[...], b_ref[...].astype(BF), ((1,), (1,))).astype(BF)


def store_block(per, block, one_ref, two_ref):
    step = pl.program_id(0)

    @pl.when(step < per)
    def _():
        one_ref[...] = block

    @pl.when(step >= per)
    def _():
        two_ref[...] = block


def first_query_kernel(per, cols, h_ref, gain_ref, w_ref, a_ref, one_ref, two_ref, hg_ref, pack_ref):
    @pl.when(pl.program_id(0) == 0)
    def _():
        wide = h_ref[...].astype(F32)
        hg_ref[...] = (wide * gain_ref[...]).astype(BF)
        count = wide.shape[0]
        sums = jnp.sum(wide * wide, axis=-1, keepdims=True)
        rows = []
        for i in range(count // LANES):
            block = jnp.broadcast_to(sums[i * LANES : (i + 1) * LANES], (LANES, LANES))
            rows.append(block.T[0:1])
        rows.append(jnp.zeros((8 - len(rows), LANES), F32))
        pack_ref[count:] = split_terms(jnp.concatenate(rows, axis=0))
        pack_ref[:count] = dot(hg_ref[...], a_ref[...].astype(BF)).astype(BF)

    store_block(per, dot(hg_ref[...], w_ref[...]).astype(BF), one_ref, two_ref)


def second_query_kernel(per, cols, hg_ref, w_ref, pos_ref, after_ref, one_ref, two_ref, pos_out):
    @pl.when(pl.program_id(0) == 0)
    def _():
        pos_out[...] = pos_ref[...].astype(F32)

    store_block(per, dot(hg_ref[...], w_ref[...]).astype(BF), one_ref, two_ref)


def merge_kernel(a_ref, b_ref, out_ref):
    count = a_ref.shape[0] - EXTRA
    out_ref[:count] = (a_ref[:count].astype(F32) + b_ref[:count].astype(F32)).astype(BF)
    out_ref[count:] = split_terms(join_terms(a_ref, count) + join_terms(b_ref, count))


def grad_kernel(sizes, at, x_ref, v_ref, s_ref, r_ref, *rest):
    n_dp, n_roll = sizes
    outs, (ga, gb) = rest[:-2], rest[-2:]
    count, width = x_ref.shape
    low = (s_ref[...].astype(F32) + r_ref[...].astype(F32)).astype(BF)
    ga[...] = SCALE * dot(x_ref[...], low[count:], ((0,), (0,)))
    turned = SCALE * dot(low[:count], v_ref[...], ((0,), (0,)))
    for j in range(width // LANES):
        gb[j * LANES : (j + 1) * LANES] = turned[:, j * LANES : (j + 1) * LANES]
    size = width // (n_dp * n_roll)
    for kx in range(n_dp):
        for kz in range(n_roll):
            start = ((at[1] ^ kx) * n_roll + (at[2] ^ kz)) * size
            rows = pl.ds(pl.multiple_of(start, size), size)
            out = outs[kx * n_roll + kz]
            out[0] = ga[rows].astype(out.dtype)
            out[1] = gb[rows].astype(out.dtype)


def far_kernel(a_ref, b_ref, after_ref, out_ref):
    out_ref[...] = (a_ref[...].astype(F32) + b_ref[...].astype(F32)).astype(BF)


def low_kernel(sizes, at, hg_ref, *rest):
    n_dp, n_roll = sizes
    pieces, (pack_ref, ga_ref, gb_ref) = rest[:-3], rest[-3:]
    size = pieces[0].shape[1]
    for kx in range(n_dp):
        for kz in range(n_roll):
            start = ((at[1] ^ kx) * n_roll + (at[2] ^ kz)) * size
            rows = pl.ds(pl.multiple_of(start, size), size)
            piece = pieces[kx * n_roll + kz]
            ga_ref[rows] = piece[0]
            gb_ref[rows] = piece[1]
    count = hg_ref.shape[0]
    pack_ref[:count] = dot(hg_ref[...], ga_ref[...]).astype(BF)
    ga = ga_ref[...].astype(F32)
    gb = gb_ref[...].astype(F32)
    total = jnp.sum(ga * ga + gb * gb)
    pack_ref[count:] = split_terms(jnp.broadcast_to(total, (8, LANES)))


def base_kernel(p_ref, near_ref, far_ref, a_ref, b_ref, after_ref, base_ref, low_ref, scale_ref):
    step = pl.program_id(0)
    count = a_ref.shape[0] - EXTRA
    sums = join_terms(a_ref, count) + join_terms(b_ref, count)
    scale = lax.rsqrt(sums / D + EPS)
    row = scale[0:1]
    for i in range(1, count // LANES):
        row = jnp.where(step == i, scale[i : i + 1], row)
    block = jnp.broadcast_to(row, (LANES, LANES)).T
    rows = pl.ds(pl.multiple_of(step * LANES, LANES), LANES)
    scale_ref[...] = block
    low_ref[...] = (a_ref[rows].astype(F32) + b_ref[rows].astype(F32)) * block
    for j in range(p_ref.shape[1] // LANES):
        at = slice(j * LANES, (j + 1) * LANES)
        total = p_ref[:, at].astype(F32) + near_ref[:, at].astype(F32) + far_ref[:, at].astype(F32)
        base_ref[:, at] = total * block


def final_kernel(
    base_ref, low_ref, scale_ref, s_ref, r_ref, ga_ref, gb_ref, a_ref, b_ref, cos_ref, sin_ref,
    new_a, new_b, out_ref, half_b,
):
    step = pl.program_id(0)
    count = s_ref.shape[0] - EXTRA
    total = join_terms(s_ref, count) + join_terms(r_ref, count)
    rate = (LEARN * lax.rsqrt(total + NORM_EPS))[0:1]

    @pl.when(step == 0)
    def _():
        new_a[...] = a_ref[...] - rate * ga_ref[...].astype(F32)
        for j in range(b_ref.shape[1] // LANES):
            at = slice(j * LANES, (j + 1) * LANES)
            fresh = b_ref[:, at] - rate * gb_ref[at].astype(F32)
            new_b[:, at] = fresh
            half_b[:, at] = fresh.astype(BF)

    rows = pl.ds(pl.multiple_of(step * LANES, LANES), LANES)
    low = s_ref[rows].astype(F32) + r_ref[rows].astype(F32)
    mix = (low_ref[...] - rate * (low * scale_ref[...])) * SCALE
    update = dot(mix.astype(BF), half_b[...])
    cos, sin = cos_ref[...], sin_ref[...]
    for j in range(base_ref.shape[1] // HEAD):
        at = slice(j * HEAD, (j + 1) * HEAD)
        query = base_ref[:, at] + update[:, at]
        other = pltpu.roll(query, HEAD // 2, 1)
        out_ref[:, at] = (query * cos + other * sin).astype(BF)


def turn_tables(places, steps):
    half = HEAD // 2
    freq = 10000.0 ** (-jnp.arange(half, dtype=F32) / half)
    cos, sin = [], []
    for step in range(steps):
        angle = (places + float(step))[:, None] * freq[None, :]
        c, s = jnp.cos(angle), jnp.sin(angle)
        cos.append(jnp.concatenate([c, c], axis=-1))
        sin.append(jnp.concatenate([-s, s], axis=-1))
    return jnp.concatenate(cos), jnp.concatenate(sin)


def build(n_dp, n_roll, n_tp):
    def on_device(
        train_inputs, train_cotangent, factor_a, factor_b, base_weight, incoming, norm_gain, positions
    ):
        steps, rows, width = incoming.shape
        tokens = train_inputs.shape[0]
        rank = factor_a.shape[1]
        count = steps * rows
        full = base_weight.shape[1]
        tp, dp, roll = (lax.axis_index(a) for a in ("tp", "dp", "roll"))
        at = jnp.stack([tp, dp, roll]).astype(jnp.int32)

        part = pl.pallas_call(
            rank_kernel,
            out_shape=shape((2 * tokens, rank), BF),
            in_specs=[VMEM] * 4,
            out_specs=VMEM,
            compiler_params=PARAMS,
            name="rank",
        )(train_inputs, train_cotangent, factor_a, factor_b)
        part_got = swap(part, "tp", n_tp, 1)

        cut = 512
        per = width // cut
        whole = lambda *dims: pl.BlockSpec(dims, lambda i, c: (0,) * len(dims))

        def query_call(kernel, top, ins, in_specs, outs, out_specs, name):
            w_spec = pl.BlockSpec(
                (width, cut), lambda i, c: (0, (c[0] ^ (top - i // per)) * per + i % per)
            )
            one_spec = pl.BlockSpec((count, cut), lambda i, c: (0, jnp.minimum(i, per - 1)))
            two_spec = pl.BlockSpec((count, cut), lambda i, c: (0, jnp.maximum(i - per, 0)))
            return pl.pallas_call(
                functools.partial(kernel, per),
                out_shape=[shape((count, width), BF)] * 2 + outs,
                grid_spec=pltpu.PrefetchScalarGridSpec(
                    num_scalar_prefetch=1,
                    grid=(2 * per,),
                    in_specs=[w_spec if s is None else s for s in in_specs],
                    out_specs=[one_spec, two_spec] + out_specs,
                ),
                compiler_params=PARAMS,
                name=name,
            )(at, *ins)

        diag, distant, gained, low_pack = query_call(
            first_query_kernel,
            3,
            (incoming.reshape(count, width), norm_gain[None, :], base_weight, factor_a),
            [whole(count, width), whole(1, width), None, whole(width, rank)],
            [shape((count, width), BF), shape((count + EXTRA, rank), BF)],
            [whole(count, width), whole(count + EXTRA, rank)],
            "query_first",
        )
        diag_got = swap(diag, "tp", n_tp, 1)
        part_sum = (part.astype(F32) + part_got.astype(F32)).astype(BF)
        part_far = swap(part_sum, "tp", n_tp, 2)
        beside, close, places = query_call(
            second_query_kernel,
            1,
            (gained, base_weight, positions.reshape(-1, LANES), part_sum),
            [whole(count, width), None, whole(rows // LANES, LANES), ANY],
            [shape((rows // LANES, LANES), F32)],
            [whole(rows // LANES, LANES)],
            "query_second",
        )
        close_got = swap(beside, "tp", n_tp, 1)
        merge = pl.pallas_call(
            merge_kernel,
            out_shape=shape((count + EXTRA, rank), BF),
            in_specs=[VMEM] * 2,
            out_specs=VMEM,
            compiler_params=PARAMS,
            name="merge",
        )
        low_sum = merge(low_pack, swap(low_pack, "tp", n_tp, 1))
        low_far = swap(low_sum, "tp", n_tp, 2)

        size = width // (n_dp * n_roll)
        piece = (2, size, rank)
        grads = pl.pallas_call(
            functools.partial(grad_kernel, (n_dp, n_roll)),
            out_shape=[shape(piece, F32)] * n_roll + [shape(piece, BF)] * ((n_dp - 1) * n_roll),
            in_specs=[SMEM] + [VMEM] * 4,
            out_specs=[VMEM] * (n_dp * n_roll),
            scratch_shapes=[pltpu.VMEM((width, rank), F32), pltpu.VMEM((width, rank), F32)],
            compiler_params=PARAMS,
            name="grads",
        )(at, train_inputs, train_cotangent, part_sum, part_far)
        sums = list(grads[:n_roll])
        for kz in reversed(range(n_roll)):
            for kx in range(1, n_dp):
                sums[kz] = sums[kz] + swap(grads[kx * n_roll + kz], "dp", n_dp, kx).astype(F32)
        far = pl.pallas_call(
            far_kernel,
            out_shape=shape((count, width), BF),
            grid=(4,),
            in_specs=[pl.BlockSpec((count // 4, width), lambda i: (i, 0)),
                      pl.BlockSpec((count // 4, width), lambda i: (i, 0)), ANY],
            out_specs=pl.BlockSpec((count // 4, width), lambda i: (i, 0)),
            compiler_params=PARAMS,
            name="far",
        )(distant, diag_got, grads[-1])
        far_got = swap(far, "tp", n_tp, 2)

        chunk = sums[0]
        for kz in reversed(range(1, n_roll)):
            chunk = chunk + swap(sums[kz].astype(BF), "roll", n_roll, kz).astype(F32)
        chunk = chunk.astype(BF)
        pieces = [chunk] + [swap(chunk, "roll", n_roll, kz) for kz in range(1, n_roll)]
        for kx in range(1, n_dp):
            pieces += [swap(pieces[kz], "dp", n_dp, kx) for kz in range(n_roll)]
        step_pack, grad_a, grad_b = pl.pallas_call(
            functools.partial(low_kernel, (n_dp, n_roll)),
            out_shape=[shape((count + EXTRA, rank), BF), shape((width, rank), BF), shape((width, rank), BF)],
            in_specs=[SMEM] + [VMEM] * (1 + len(pieces)),
            out_specs=[VMEM] * 3,
            compiler_params=PARAMS,
            name="low_rank",
        )(at, gained, *pieces)
        step_sum = merge(step_pack, swap(step_pack, "tp", n_tp, 1))
        step_far = swap(step_sum, "tp", n_tp, 2)

        tall = lambda cols: pl.BlockSpec((LANES, cols), lambda i: (i, 0))
        fixed = lambda *dims: pl.BlockSpec(dims, lambda i: (0,) * len(dims))
        base, low, scale = pl.pallas_call(
            base_kernel,
            out_shape=[shape((count, width), F32), shape((count, rank), F32), shape((count, LANES), F32)],
            grid=(count // LANES,),
            in_specs=[tall(width), tall(width), tall(width),
                      fixed(count + EXTRA, rank), fixed(count + EXTRA, rank), ANY],
            out_specs=[tall(width), tall(rank), tall(LANES)],
            compiler_params=PARAMS,
            name="base",
        )(close, close_got, far_got, low_sum, low_far, step_pack)
        cos, sin = turn_tables(places.reshape(rows), steps)
        new_a, new_b, queries = pl.pallas_call(
            final_kernel,
            out_shape=[shape((width, rank), F32), shape((rank, width), F32), shape((count, width), BF)],
            grid=(count // LANES,),
            in_specs=[tall(width), tall(rank), tall(LANES), fixed(count + EXTRA, rank), fixed(count + EXTRA, rank),
                      fixed(width, rank), fixed(width, rank), fixed(width, rank), fixed(rank, width),
                      tall(LANES), tall(LANES)],
            out_specs=[fixed(width, rank), fixed(rank, width), tall(width)],
            scratch_shapes=[pltpu.VMEM((rank, width), BF)],
            compiler_params=PARAMS,
            name="final",
        )(base, low, scale, step_sum, step_far, grad_a, grad_b, factor_a, factor_b, cos, sin)
        return new_a, new_b, queries.reshape(steps, rows, width)

    return on_device


def solution(mesh):
    n_dp, n_roll, n_tp = (mesh.shape[a] for a in ("dp", "roll", "tp"))
    return jax.shard_map(
        build(n_dp, n_roll, n_tp),
        mesh=mesh,
        in_specs=(
            P(("dp", "roll"), "tp"),
            P(("dp", "roll"), "tp"),
            P("tp", None),
            P(None, "tp"),
            P("tp", None),
            P(None, ("dp", "roll"), "tp"),
            P("tp"),
            P(("dp", "roll")),
        ),
        out_specs=(P("tp", None), P(None, "tp"), P(None, ("dp", "roll"), "tp")),
        check_vma=False,
    )
```

time: 118 us -> 77.7 us (0.66)
  other arithmetic: 20.1 us -> 1.45 us
  matrix products: 18.5 us -> 0 us
  Pallas kernels: 0 us -> 15.7 us
  starting transfers between devices: 35 us -> 26.1 us
  local copies, waits for them, and re-layouts: 15.8 us -> 10.7 us
  between operations: 3.46 us -> 0.8 us
  waiting for transfers between devices: 24.9 us -> 22.5 us
    dot_general x8 -> x0, matrix products: 18.5 us -> none  [the longest x1 8.1 us: on_device(): part_q = jnp.dot(gained, base_weight, preferred_element_type=F32).astype(BF)]
    pallas_call x0 -> x10, Pallas kernels: none -> 15.7 us  [the longest x2 9.15 us: query_call(): pl.pallas_call(functools.partial(kernel, per), out_shape=[shape((count, w...]
    convert_element_type x11 -> x5, other arithmetic: 12.9 us -> 0.16 us  [the longest x3 0.06 us: on_device(): chunk = chunk + swap(sums[kz].astype(BF), 'roll', n_roll, kz).astype(F32)]
    ppermute x21 -> x23, starting transfers between devices: 35 us -> 26.1 us  [swap(): return lax.ppermute(x, axis, [(i, i ^ k) for i in range(n)])]
    unnamed x38 -> x28, local copies, waits for them, and re-layouts: 4.55 us -> 10.7 us
    mul x3 -> x0, local copies, waits for them, and re-layouts: 4.45 us -> none  [on_device(): turned = heads * cos[:, :, None, :] + other * sin[:, :, None, :]]
    another operation x2 -> x0, local copies, waits for them, and re-layouts: 2.46 us -> none  [on_device(): grads = jnp.stack([grad_a, grad_b], axis=1)]
    ppermute x21 -> x23, waiting for transfers between devices: 24.9 us -> 22.5 us  [swap(): return lax.ppermute(x, axis, [(i, i ^ k) for i in range(n)])]
  transfers between devices with their start and end apart: 21 -> 23, of which waited for: 11 -> 10; matrix products, arithmetic and copies ran while one was open for 31% -> 2% of each run, Pallas kernels for 0% -> 16%
where the time goes in v2:
time: 77.7 us; the launch traced here: 77.3 us
  starting transfers between devices  26.1 us (34%)
  waiting for transfers between devices  22.5 us (29%)
  Pallas kernels  15.7 us (20%)
  local copies, waits for them, and re-layouts  10.7 us (14%)
  other arithmetic  1.45 us (2%)
  between operations  0.8 us (1%)
    ppermute x23, starting transfers between devices, swap(): return lax.ppermute(x, axis, [(i, i ^ k) for i in range(n)])  26.1 us
    ppermute x23, waiting for transfers between devices, swap(): return lax.ppermute(x, axis, [(i, i ^ k) for i in range(n)])  22.5 us
    unnamed x28, local copies, waits for them, and re-layouts  10.7 us
    pallas_call x2, Pallas kernels, query_call(): pl.pallas_call(functools.partial(kernel, per), out_shape=[shape((count, w...  9.15 us
    pallas_call x1, Pallas kernels, on_device(): pl.pallas_call(final_kernel, out_shape=[shape((width, rank), F32), shape(...  2.89 us
  transfers between devices with their start and end apart: 23, of which 10 were waited for; matrix products, arithmetic and copies ran while one was open for 2% of the time, Pallas kernels for 16%

profile of v2, /device:TPU:0, one launch (start us, length us, event | category | flops | bytes accessed | tf_op | source)
XLA Modules:
  0.0 77.3 jit_solution(16773801180052910376)
XLA Ops:
  0.6 1.0 %copy-done.2 = f32[1024,128]{1,0:T(8,128)S(1)} copy-done((f32[1024,128]{1,0:T(8,128)S(1)}, f32[1024,128]{1,0:T(8,128)}, u32[]{:S(2)}) %copy-start.2) | copy-done | bytes 524312
  1.7 1.1 %copy-done.5 = bf16[384,1024]{1,0:T(8,128)(2,1)S(1)} copy-done((bf16[384,1024]{1,0:T(8,128)(2,1)S(1)}, bf16[384,1024]{1,0:T(8,128)(2,1)}, u32[]{:S(2)}) %copy-start.5) | copy-done | bytes 786456
  2.8 1.1 %copy-done.7 = bf16[384,1024]{1,0:T(8,128)(2,1)S(1)} copy-done((bf16[384,1024]{1,0:T(8,128)(2,1)S(1)}, bf16[384,1024]{1,0:T(8,128)(2,1)}, u32[]{:S(2)}) %copy-start.7) | copy-done | bytes 786456
  3.9 1.0 %copy-done.9 = f32[128,1024]{1,0:T(8,128)S(1)} copy-done((f32[128,1024]{1,0:T(8,128)S(1)}, f32[128,1024]{1,0:T(8,128)}, u32[]{:S(2)}) %copy-start.9) | copy-done | bytes 524312
  5.0 0.6 rank.1
  5.6 0.5 collective-permute-start
  6.2 3.4 %copy-done = bf16[1024,4096]{1,0:T(8,128)(2,1)S(1)} copy-done((bf16[1024,4096]{1,0:T(8,128)(2,1)S(1)}, bf16[1024,4096]{1,0:T(8,128)(2,1)}, u32[]{:S(2)}) %copy-start) | copy-done | bytes 8388632
  9.5 1.0 %copy-done.3 = f32[1024,128]{1,0:T(8,128)S(1)} copy-done((f32[1024,128]{1,0:T(8,128)S(1)}, f32[1024,128]{1,0:T(8,128)}, u32[]{:S(2)}) %copy-start.3) | copy-done | bytes 524312
  10.6 1.2 %copy-done.11 = bf16[2,256,1024]{2,1,0:T(8,128)(2,1)S(1)} copy-done((bf16[2,256,1024]{2,1,0:T(8,128)(2,1)S(1)}, bf16[2,256,1024]{2,1,0:T(8,128)(2,1)}, u32[]{:S(2)}) %copy-start.11) | copy-done | bytes 1048600
  11.8 0.7 copy-done.12
  12.5 4.9 %query_first.1 = (bf16[512,1024]{1,0:T(8,128)(2,1)S(1)}, bf16[512,1024]{1,0:T(8,128)(2,1)S(1)}, bf16[512,1024]{1,0:T(8,128)(2,1)S(1)}, bf16[544,128]{1,0:T(8,128)(2,1)S(1)}) custom-call(s32[3]{0:T(128)S(1)} %pad_add_fusion.cols.at, bf16[512,1024]{1,0:T(8,128)(2,1)S(1)} %bitcast.9, f32[1,1024]{1,0:T(1,128)S(1)} %bitcast.10, bf16[1024,4096]{1,0:T(8,128)(2,1)S(1)} %copy-done, ...), custom_call_target="tpu_custom_call" | custom-call | tf_op jit(solution)/shard_map/query_first/pallas_call | solution.py:236
  17.4 0.1 collective-permute-start.2
  17.6 3.0 %collective-permute-start.3 = (bf16[768,128]{1,0:T(8,128)(2,1)S(1)}, bf16[768,128]{1,0:T(8,128)(2,1)S(1)}, u32[]{:S(2)}, u32[]{:S(2)}) collective-permute-start(bf16[768,128]{1,0:T(8,128)(2,1)S(1)} %add_convert_fusion.after_ref.s_ref), channel_id=1, source_target_pairs={{0,2},{1,3},{2,0},{3,1},{4,6},{5,7},{6,4},{7,5},{8,10},{9,11},{10,... | collective-permute-start | bytes 589832 | tf_op jit(solution)/shard_map/ppermute | solution.py:36
  20.6 5.1 %collective-permute-done.3.r_ref = bf16[768,128]{1,0:T(8,128)(2,1)S(1)} collective-permute-done((bf16[768,128]{1,0:T(8,128)(2,1)S(1)}, bf16[768,128]{1,0:T(8,128)(2,1)S(1)}, u32[]{:S(2)}, u32[]{:S(2)}) %collective-permute-start.3) | collective-permute-done | bytes 196640 | tf_op jit(solution)/shard_map/ppermute | solution.py:36
  25.7 1.1 %grads.1 = (f32[2,128,128]{2,1,0:T(8,128)S(1)}, f32[2,128,128]{2,1,0:T(8,128)S(1)}, f32[2,128,128]{2,1,0:T(8,128)S(1)}, f32[2,128,128]{2,1,0:T(8,128)S(1)}, bf16...) custom-call(s32[3]{0:T(128)S(1)} %pad_add_fusion.cols.at, ...), custom_call_target="tpu_custom_call" | custom-call | tf_op jit(solution)/shard_map/grads/pallas_call | solution.py:284
  26.8 1.8 %collective-permute-start.12 = (bf16[2,128,128]{2,1,0:T(8,128)(2,1)S(1)}, bf16[2,128,128]{2,1,0:T(8,128)(2,1)S(1)}, u32[]{:S(2)}, u32[]{:S(2)}) collective-permute-start(bf16[2,128,128]{2,1,0:T(8,128)(2,1)S(1)} %get-tuple-element.40), channel_id=1, source_target_pairs={{0,16},{16,0},{1,17},{17,1},{2,18},{18,2},{3,19},{19,3},{4,20},{20... | collective-permute-start | bytes 196616 | tf_op jit(solution)/shard_map/ppermute | solution.py:36
  28.6 0.3 collective-permute-start.10
  28.9 1.7 %collective-permute-start.8 = (bf16[2,128,128]{2,1,0:T(8,128)(2,1)S(1)}, bf16[2,128,128]{2,1,0:T(8,128)(2,1)S(1)}, u32[]{:S(2)}, u32[]{:S(2)}) collective-permute-start(bf16[2,128,128]{2,1,0:T(8,128)(2,1)S(1)} %get-tuple-element.32.after_ref), channel_id=1, source_target_pairs={{0,16},{16,0},{1,17},{17,1},{2,18},{18,2},{3,19},{19,3},{4,20},{20... | collective-permute-start | bytes 196616 | tf_op jit(solution)/shard_map/ppermute | solution.py:36
  30.6 0.3 collective-permute-start.7
  30.9 0.8 %collective-permute-done.12 = bf16[2,128,128]{2,1,0:T(8,128)(2,1)S(1)} collective-permute-done((bf16[2,128,128]{2,1,0:T(8,128)(2,1)S(1)}, bf16[2,128,128]{2,1,0:T(8,128)(2,1)S(1)}, u32[]{:S(2)}, u32[]{:S(2)}) %collective-permute-start.12) | collective-permute-done | bytes 65568 | tf_op jit(solution)/shard_map/ppermute | solution.py:36
  31.8 1.9 %collective-permute-start.13 = (bf16[2,128,128]{2,1,0:T(8,128)(2,1)S(1)}, bf16[2,128,128]{2,1,0:T(8,128)(2,1)S(1)}, u32[]{:S(2)}, u32[]{:S(2)}) collective-permute-start(bf16[2,128,128]{2,1,0:T(8,128)(2,1)S(1)} %add_convert_fusion.2), channel_id=1, source_target_pairs={{0,4},{4,0},{8,12},{12,8},{1,5},{5,1},{9,13},{13,9},{2,6},{6,2},{1... | collective-permute-start | bytes 196616 | tf_op jit(solution)/shard_map/ppermute | solution.py:36
  33.7 2.7 %collective-permute-start.11 = (bf16[2,128,128]{2,1,0:T(8,128)(2,1)S(1)}, bf16[2,128,128]{2,1,0:T(8,128)(2,1)S(1)}, u32[]{:S(2)}, u32[]{:S(2)}) collective-permute-start(bf16[2,128,128]{2,1,0:T(8,128)(2,1)S(1)} %add_convert_fusion.3), channel_id=1, source_target_pairs={{0,8},{4,12},{8,0},{12,4},{1,9},{5,13},{9,1},{13,5},{2,10},{6,14},... | collective-permute-start | bytes 196616 | tf_op jit(solution)/shard_map/ppermute | solution.py:36
  36.4 1.6 %collective-permute-start.9 = (bf16[2,128,128]{2,1,0:T(8,128)(2,1)S(1)}, bf16[2,128,128]{2,1,0:T(8,128)(2,1)S(1)}, u32[]{:S(2)}, u32[]{:S(2)}) collective-permute-start(bf16[2,128,128]{2,1,0:T(8,128)(2,1)S(1)} %add_convert_fusion.4), channel_id=1, source_target_pairs={{0,12},{4,8},{8,4},{12,0},{1,13},{5,9},{9,5},{13,1},{2,14},{6,10},... | collective-permute-start | bytes 196616 | tf_op jit(solution)/shard_map/ppermute | solution.py:36
  38.0 4.3 %query_second.1 = (bf16[512,1024]{1,0:T(8,128)(2,1)S(1)}, bf16[512,1024]{1,0:T(8,128)(2,1)S(1)}, f32[2,128]{1,0:T(2,128)S(1)}) custom-call(s32[3]{0:T(128)S(1)} %pad_add_fusion.cols.at, bf16[512,1024]{1,0:T(8,128)(2,1)S(1)} %get-tuple-element.27.hg_ref, bf16[1024,4096]{1,0:T(8,128)(2,1)S(1)} %copy-done.1, s32[2,128]{1,0:T(2,128)S(1)} %bitcast.12, ...), custom_call_target="tpu_custom_call" | custom-call | tf_op jit(solution)/shard_map/query_second/pallas_call | solution.py:236
  42.4 0.3 far.1
  42.7 0.5 collective-permute-start.1
  43.3 1.6 %collective-permute-start.4 = (bf16[512,1024]{1,0:T(8,128)(2,1)S(1)}, bf16[512,1024]{1,0:T(8,128)(2,1)S(1)}, u32[]{:S(2)}, u32[]{:S(2)}) collective-permute-start(bf16[512,1024]{1,0:T(8,128)(2,1)S(1)} %far.1), channel_id=1, source_target_pairs={{0,2},{1,3},{2,0},{3,1},{4,6},{5,7},{6,4},{7,5},{8,10},{9,11},{10,... | collective-permute-start | bytes 3145736 | tf_op jit(solution)/shard_map/ppermute | solution.py:36
  45.0 2.8 %collective-permute-start.15 = (bf16[2,128,128]{2,1,0:T(8,128)(2,1)S(1)}, bf16[2,128,128]{2,1,0:T(8,128)(2,1)S(1)}, u32[]{:S(2)}, u32[]{:S(2)}) collective-permute-start(bf16[2,128,128]{2,1,0:T(8,128)(2,1)S(1)} %add_convert_fusion.1.rest_0_), channel_id=1, source_target_pairs={{0,8},{4,12},{8,0},{12,4},{1,9},{5,13},{9,1},{13,5},{2,10},{6,14},... | collective-permute-start | bytes 196616 | tf_op jit(solution)/shard_map/ppermute | solution.py:36
  47.7 1.6 %collective-permute-start.16 = (bf16[2,128,128]{2,1,0:T(8,128)(2,1)S(1)}, bf16[2,128,128]{2,1,0:T(8,128)(2,1)S(1)}, u32[]{:S(2)}, u32[]{:S(2)}) collective-permute-start(bf16[2,128,128]{2,1,0:T(8,128)(2,1)S(1)} %add_convert_fusion.1.rest_0_), channel_id=1, source_target_pairs={{0,12},{4,8},{8,4},{12,0},{1,13},{5,9},{9,5},{13,1},{2,14},{6,10},... | collective-permute-start | bytes 196616 | tf_op jit(solution)/shard_map/ppermute | solution.py:36
  49.3 0.5 collective-permute-done.14.rest_1_
  49.9 1.2 %collective-permute-start.17 = (bf16[2,128,128]{2,1,0:T(8,128)(2,1)S(1)}, bf16[2,128,128]{2,1,0:T(8,128)(2,1)S(1)}, u32[]{:S(2)}, u32[]{:S(2)}) collective-permute-start(bf16[2,128,128]{2,1,0:T(8,128)(2,1)S(1)} %add_convert_fusion.1.rest_0_), channel_id=1, source_target_pairs={{0,16},{16,0},{1,17},{17,1},{2,18},{18,2},{3,19},{19,3},{4,20},{20... | collective-permute-start | bytes 196616 | tf_op jit(solution)/shard_map/ppermute | solution.py:36
  51.0 1.8 %collective-permute-done.15.rest_2_ = bf16[2,128,128]{2,1,0:T(8,128)(2,1)S(1)} collective-permute-done((bf16[2,128,128]{2,1,0:T(8,128)(2,1)S(1)}, bf16[2,128,128]{2,1,0:T(8,128)(2,1)S(1)}, u32[]{:S(2)}, u32[]{:S(2)}) %collective-permute-start.15) | collective-permute-done | bytes 65568 | tf_op jit(solution)/shard_map/ppermute | solution.py:36
  52.9 1.2 %collective-permute-start.18 = (bf16[2,128,128]{2,1,0:T(8,128)(2,1)S(1)}, bf16[2,128,128]{2,1,0:T(8,128)(2,1)S(1)}, u32[]{:S(2)}, u32[]{:S(2)}) collective-permute-start(bf16[2,128,128]{2,1,0:T(8,128)(2,1)S(1)} %collective-permute-done.14.rest_1_), channel_id=1, source_target_pairs={{0,16},{16,0},{1,17},{17,1},{2,18},{18,2},{3,19},{19,3},{4,20},{20... | collective-permute-start | bytes 196616 | tf_op jit(solution)/shard_map/ppermute | solution.py:36
  54.1 1.4 %collective-permute-start.19 = (bf16[2,128,128]{2,1,0:T(8,128)(2,1)S(1)}, bf16[2,128,128]{2,1,0:T(8,128)(2,1)S(1)}, u32[]{:S(2)}, u32[]{:S(2)}) collective-permute-start(bf16[2,128,128]{2,1,0:T(8,128)(2,1)S(1)} %collective-permute-done.15.rest_2_), channel_id=1, source_target_pairs={{0,16},{16,0},{1,17},{17,1},{2,18},{18,2},{3,19},{19,3},{4,20},{20... | collective-permute-start | bytes 196616 | tf_op jit(solution)/shard_map/ppermute | solution.py:36
  55.5 0.7 collective-permute-start.20
  56.2 1.0 %collective-permute-done.18.rest_5_ = bf16[2,128,128]{2,1,0:T(8,128)(2,1)S(1)} collective-permute-done((bf16[2,128,128]{2,1,0:T(8,128)(2,1)S(1)}, bf16[2,128,128]{2,1,0:T(8,128)(2,1)S(1)}, u32[]{:S(2)}, u32[]{:S(2)}) %collective-permute-start.18) | collective-permute-done | bytes 65568 | tf_op jit(solution)/shard_map/ppermute | solution.py:36
  57.2 0.5 collective-permute-start.6
  57.7 0.7 collective-permute-done.19.rest_6_
  58.4 1.4 %collective-permute-done.20.rest_7_ = bf16[2,128,128]{2,1,0:T(8,128)(2,1)S(1)} collective-permute-done((bf16[2,128,128]{2,1,0:T(8,128)(2,1)S(1)}, bf16[2,128,128]{2,1,0:T(8,128)(2,1)S(1)}, u32[]{:S(2)}, u32[]{:S(2)}) %collective-permute-start.20) | collective-permute-done | bytes 65568 | tf_op jit(solution)/shard_map/ppermute | solution.py:36
  59.8 1.0 %low_rank.1 = (bf16[544,128]{1,0:T(8,128)(2,1)S(1)}, bf16[1024,128]{1,0:T(8,128)(2,1)S(1)}, bf16[1024,128]{1,0:T(8,128)(2,1)S(1)}) custom-call(s32[3]{0:T(128)S(1)} %pad_add_fusion.cols.at, bf16[512,1024]{1,0:T(8,128)(2,1)S(1)} %get-tuple-element.27.hg_ref, bf16[2,128,128]{2,1,0:T(8,128)(2,1)S(1)} %add_convert_fusion.1.rest_0_, ...), custom_call_target="tpu_custom_call" | custom-call | tf_op jit(solution)/shard_map/low_rank/pallas_call | solution.py:316
  60.9 1.3 %collective-permute-done.21.b_ref = bf16[544,128]{1,0:T(8,128)(2,1)S(1)} collective-permute-done((bf16[544,128]{1,0:T(8,128)(2,1)S(1)}, bf16[544,128]{1,0:T(8,128)(2,1)S(1)}, u32[]{:S(2)}, u32[]{:S(2)}) %collective-permute-start.21) | collective-permute-done | bytes 139296 | tf_op jit(solution)/shard_map/ppermute | solution.py:36
  62.2 0.6 collective-permute-start.22
  62.8 1.0 %fusion = (f32[256,64]{1,0:T(8,128)S(1)}, f32[256,64]{1,0:T(8,128)S(1)}, f32[256,64]{1,0:T(8,128)S(1)}, f32[256,64]{1,0:T(8,128)S(1)}, f32[256,64]{1,0:T(8,128)S(1)}, /*index=5*/f32[256,64]{1,0:T(8,128)S(1)}) fusion(f32[64]{0:T(128)S(1)} %multiply_power_fusion, f32[256]{0:T(256)S(1)} %bitcast.11, f32[256]{0:T(256)S(1)} %broadcast_add_fusion), kind=kLoop, calls=%fused_computation.11 | loop fusion | flops 65536 | bytes 395520 | tf_op jit(solution)/shard_map/neg | solution.py:200
  63.8 0.2 maximum_maximum_fusion
  64.0 8.2 %collective-permute-done.6.b_ref = bf16[544,128]{1,0:T(8,128)(2,1)S(1)} collective-permute-done((bf16[544,128]{1,0:T(8,128)(2,1)S(1)}, bf16[544,128]{1,0:T(8,128)(2,1)S(1)}, u32[]{:S(2)}, u32[]{:S(2)}) %collective-permute-start.6) | collective-permute-done | bytes 139296 | tf_op jit(solution)/shard_map/ppermute | solution.py:36
  72.3 0.6 base.1
  72.9 1.5 %collective-permute-done.22.r_ref = bf16[544,128]{1,0:T(8,128)(2,1)S(1)} collective-permute-done((bf16[544,128]{1,0:T(8,128)(2,1)S(1)}, bf16[544,128]{1,0:T(8,128)(2,1)S(1)}, u32[]{:S(2)}, u32[]{:S(2)}) %collective-permute-start.22) | collective-permute-done | bytes 139296 | tf_op jit(solution)/shard_map/ppermute | solution.py:36
  74.4 2.9 %final.1 = (f32[1024,128]{1,0:T(8,128)}, f32[128,1024]{1,0:T(8,128)}, bf16[512,1024]{1,0:T(8,128)(2,1)}) custom-call(f32[512,1024]{1,0:T(8,128)S(1)} %get-tuple-element.42.base_ref, f32[512,128]{1,0:T(8,128)S(1)} %get-tuple-element.43.low_ref, f32[512,128]{1,0:T(8,128)S(1)} %get-tuple-element.44.scale_ref, bf16[544,128]{1,0:T(8,128)(2,1)S(1)} %merge.3.s_ref, ...), custom_call_target="tpu_custom_call" | custom-call | tf_op jit(solution)/shard_map/final/pallas_call | solution.py:340
  (46 shorter events, 0.6 us)
Async XLA Ops:
  0.6 1.0 %copy-start.2 = (f32[1024,128]{1,0:T(8,128)S(1)}, f32[1024,128]{1,0:T(8,128)}, u32[]{:S(2)}) copy-start(f32[1024,128]{1,0:T(8,128)} %a_ref.5) | copy-start | bytes 1572868
  1.7 1.1 %copy-start.5 = (bf16[384,1024]{1,0:T(8,128)(2,1)S(1)}, bf16[384,1024]{1,0:T(8,128)(2,1)}, u32[]{:S(2)}) copy-start(bf16[384,1024]{1,0:T(8,128)(2,1)} %x_ref.3) | copy-start | bytes 2359300
  2.8 1.1 %copy-start.7 = (bf16[384,1024]{1,0:T(8,128)(2,1)S(1)}, bf16[384,1024]{1,0:T(8,128)(2,1)}, u32[]{:S(2)}) copy-start(bf16[384,1024]{1,0:T(8,128)(2,1)} %v_ref.3) | copy-start | bytes 2359300
  3.9 1.0 %copy-start.9 = (f32[128,1024]{1,0:T(8,128)S(1)}, f32[128,1024]{1,0:T(8,128)}, u32[]{:S(2)}) copy-start(f32[128,1024]{1,0:T(8,128)} %b_ref.3) | copy-start | bytes 1572868
  5.0 20.7 %copy-start.6 = (bf16[384,1024]{1,0:T(8,128)(2,1)S(1)}, bf16[384,1024]{1,0:T(8,128)(2,1)}, u32[]{:S(2)}) copy-start(bf16[384,1024]{1,0:T(8,128)(2,1)} %x_ref.3) | copy-start | bytes 2359300
  5.0 20.7 %copy-start.8 = (bf16[384,1024]{1,0:T(8,128)(2,1)S(1)}, bf16[384,1024]{1,0:T(8,128)(2,1)}, u32[]{:S(2)}) copy-start(bf16[384,1024]{1,0:T(8,128)(2,1)} %v_ref.3) | copy-start | bytes 2359300
  5.0 33.0 %copy-start.13 = (s32[256]{0:T(256)S(1)}, s32[256]{0:T(256)}, u32[]{:S(2)}) copy-start(s32[256]{0:T(256)} %param.15) | copy-start | bytes 3076
  5.6 11.9 %collective-permute-start = (bf16[768,128]{1,0:T(8,128)(2,1)S(1)}, bf16[768,128]{1,0:T(8,128)(2,1)S(1)}, u32[]{:S(2)}, u32[]{:S(2)}) collective-permute-start(bf16[768,128]{1,0:T(8,128)(2,1)S(1)} %rank.1), channel_id=1, source_target_pairs={{0,1},{1,0},{2,3},{3,2},{4,5},{5,4},{6,7},{7,6},{8,9},{9,8},{10,11... | collective-permute-start | bytes 589832 | tf_op jit(solution)/shard_map/ppermute | solution.py:36
  6.2 3.4 %copy-start = (bf16[1024,4096]{1,0:T(8,128)(2,1)S(1)}, bf16[1024,4096]{1,0:T(8,128)(2,1)}, u32[]{:S(2)}) copy-start(bf16[1024,4096]{1,0:T(8,128)(2,1)} %w_ref.3) | copy-start | bytes 25165828
  9.5 1.0 %copy-start.3 = (f32[1024,128]{1,0:T(8,128)S(1)}, f32[1024,128]{1,0:T(8,128)}, u32[]{:S(2)}) copy-start(f32[1024,128]{1,0:T(8,128)} %a_ref.5) | copy-start | bytes 1572868
  10.6 1.2 %copy-start.11 = (bf16[2,256,1024]{2,1,0:T(8,128)(2,1)S(1)}, bf16[2,256,1024]{2,1,0:T(8,128)(2,1)}, u32[]{:S(2)}) copy-start(bf16[2,256,1024]{2,1,0:T(8,128)(2,1)} %param.13) | copy-start | bytes 3145732
  11.8 0.7 copy-start.12
  12.5 25.5 %copy-start.1 = (bf16[1024,4096]{1,0:T(8,128)(2,1)S(1)}, bf16[1024,4096]{1,0:T(8,128)(2,1)}, u32[]{:S(2)}) copy-start(bf16[1024,4096]{1,0:T(8,128)(2,1)} %w_ref.3) | copy-start | bytes 25165828
  17.4 24.9 %collective-permute-start.2 = (bf16[512,1024]{1,0:T(8,128)(2,1)S(1)}, bf16[512,1024]{1,0:T(8,128)(2,1)S(1)}, u32[]{:S(2)}, u32[]{:S(2)}) collective-permute-start(bf16[512,1024]{1,0:T(8,128)(2,1)S(1)} %get-tuple-element.31), channel_id=1, source_target_pairs={{0,1},{1,0},{2,3},{3,2},{4,5},{5,4},{6,7},{7,6},{8,9},{9,8},{10,11... | collective-permute-start | bytes 3145736 | tf_op jit(solution)/shard_map/ppermute | solution.py:36
  17.6 8.1 %collective-permute-start.3 = (bf16[768,128]{1,0:T(8,128)(2,1)S(1)}, bf16[768,128]{1,0:T(8,128)(2,1)S(1)}, u32[]{:S(2)}, u32[]{:S(2)}) collective-permute-start(bf16[768,128]{1,0:T(8,128)(2,1)S(1)} %add_convert_fusion.after_ref.s_ref), channel_id=1, source_target_pairs={{0,2},{1,3},{2,0},{3,1},{4,6},{5,7},{6,4},{7,5},{8,10},{9,11},{10,... | collective-permute-start | bytes 589832 | tf_op jit(solution)/shard_map/ppermute | solution.py:36
  26.8 4.9 %collective-permute-start.12 = (bf16[2,128,128]{2,1,0:T(8,128)(2,1)S(1)}, bf16[2,128,128]{2,1,0:T(8,128)(2,1)S(1)}, u32[]{:S(2)}, u32[]{:S(2)}) collective-permute-start(bf16[2,128,128]{2,1,0:T(8,128)(2,1)S(1)} %get-tuple-element.40), channel_id=1, source_target_pairs={{0,16},{16,0},{1,17},{17,1},{2,18},{18,2},{3,19},{19,3},{4,20},{20... | collective-permute-start | bytes 196616 | tf_op jit(solution)/shard_map/ppermute | solution.py:36
  28.6 5.1 %collective-permute-start.10 = (bf16[2,128,128]{2,1,0:T(8,128)(2,1)S(1)}, bf16[2,128,128]{2,1,0:T(8,128)(2,1)S(1)}, u32[]{:S(2)}, u32[]{:S(2)}) collective-permute-start(bf16[2,128,128]{2,1,0:T(8,128)(2,1)S(1)} %get-tuple-element.38), channel_id=1, source_target_pairs={{0,16},{16,0},{1,17},{17,1},{2,18},{18,2},{3,19},{19,3},{4,20},{20... | collective-permute-start | bytes 196616 | tf_op jit(solution)/shard_map/ppermute | solution.py:36
  28.9 7.5 %collective-permute-start.8 = (bf16[2,128,128]{2,1,0:T(8,128)(2,1)S(1)}, bf16[2,128,128]{2,1,0:T(8,128)(2,1)S(1)}, u32[]{:S(2)}, u32[]{:S(2)}) collective-permute-start(bf16[2,128,128]{2,1,0:T(8,128)(2,1)S(1)} %get-tuple-element.32.after_ref), channel_id=1, source_target_pairs={{0,16},{16,0},{1,17},{17,1},{2,18},{18,2},{3,19},{19,3},{4,20},{20... | collective-permute-start | bytes 196616 | tf_op jit(solution)/shard_map/ppermute | solution.py:36
  30.6 12.1 %collective-permute-start.7 = (bf16[2,128,128]{2,1,0:T(8,128)(2,1)S(1)}, bf16[2,128,128]{2,1,0:T(8,128)(2,1)S(1)}, u32[]{:S(2)}, u32[]{:S(2)}) collective-permute-start(bf16[2,128,128]{2,1,0:T(8,128)(2,1)S(1)} %get-tuple-element.35), channel_id=1, source_target_pairs={{0,16},{16,0},{1,17},{17,1},{2,18},{18,2},{3,19},{19,3},{4,20},{20... | collective-permute-start | bytes 196616 | tf_op jit(solution)/shard_map/ppermute | solution.py:36
  31.8 11.5 %collective-permute-start.13 = (bf16[2,128,128]{2,1,0:T(8,128)(2,1)S(1)}, bf16[2,128,128]{2,1,0:T(8,128)(2,1)S(1)}, u32[]{:S(2)}, u32[]{:S(2)}) collective-permute-start(bf16[2,128,128]{2,1,0:T(8,128)(2,1)S(1)} %add_convert_fusion.2), channel_id=1, source_target_pairs={{0,4},{4,0},{8,12},{12,8},{1,5},{5,1},{9,13},{13,9},{2,6},{6,2},{1... | collective-permute-start | bytes 196616 | tf_op jit(solution)/shard_map/ppermute | solution.py:36
  33.7 11.1 %collective-permute-start.11 = (bf16[2,128,128]{2,1,0:T(8,128)(2,1)S(1)}, bf16[2,128,128]{2,1,0:T(8,128)(2,1)S(1)}, u32[]{:S(2)}, u32[]{:S(2)}) collective-permute-start(bf16[2,128,128]{2,1,0:T(8,128)(2,1)S(1)} %add_convert_fusion.3), channel_id=1, source_target_pairs={{0,8},{4,12},{8,0},{12,4},{1,9},{5,13},{9,1},{13,5},{2,10},{6,14},... | collective-permute-start | bytes 196616 | tf_op jit(solution)/shard_map/ppermute | solution.py:36
  36.4 8.4 %collective-permute-start.9 = (bf16[2,128,128]{2,1,0:T(8,128)(2,1)S(1)}, bf16[2,128,128]{2,1,0:T(8,128)(2,1)S(1)}, u32[]{:S(2)}, u32[]{:S(2)}) collective-permute-start(bf16[2,128,128]{2,1,0:T(8,128)(2,1)S(1)} %add_convert_fusion.4), channel_id=1, source_target_pairs={{0,12},{4,8},{8,4},{12,0},{1,13},{5,9},{9,5},{13,1},{2,14},{6,10},... | collective-permute-start | bytes 196616 | tf_op jit(solution)/shard_map/ppermute | solution.py:36
  38.0 36.4 %copy-start.4 = (f32[1024,128]{1,0:T(8,128)S(1)}, f32[1024,128]{1,0:T(8,128)}, u32[]{:S(2)}) copy-start(f32[1024,128]{1,0:T(8,128)} %a_ref.5) | copy-start | bytes 1572868
  38.0 36.4 %copy-start.10 = (f32[128,1024]{1,0:T(8,128)S(1)}, f32[128,1024]{1,0:T(8,128)}, u32[]{:S(2)}) copy-start(f32[128,1024]{1,0:T(8,128)} %b_ref.3) | copy-start | bytes 1572868
  42.3 5.4 %collective-permute-start.5 = (bf16[544,128]{1,0:T(8,128)(2,1)S(1)}, bf16[544,128]{1,0:T(8,128)(2,1)S(1)}, u32[]{:S(2)}, u32[]{:S(2)}) collective-permute-start(bf16[544,128]{1,0:T(8,128)(2,1)S(1)} %get-tuple-element.33.a_ref), channel_id=1, source_target_pairs={{0,1},{1,0},{2,3},{3,2},{4,5},{5,4},{6,7},{7,6},{8,9},{9,8},{10,11... | collective-permute-start | bytes 417800 | tf_op jit(solution)/shard_map/ppermute | solution.py:36
  42.7 29.5 %collective-permute-start.1 = (bf16[512,1024]{1,0:T(8,128)(2,1)S(1)}, bf16[512,1024]{1,0:T(8,128)(2,1)S(1)}, u32[]{:S(2)}, u32[]{:S(2)}) collective-permute-start(bf16[512,1024]{1,0:T(8,128)(2,1)S(1)} %get-tuple-element.29), channel_id=1, source_target_pairs={{0,1},{1,0},{2,3},{3,2},{4,5},{5,4},{6,7},{7,6},{8,9},{9,8},{10,11... | collective-permute-start | bytes 3145736 | tf_op jit(solution)/shard_map/ppermute | solution.py:36
  43.3 29.0 %collective-permute-start.4 = (bf16[512,1024]{1,0:T(8,128)(2,1)S(1)}, bf16[512,1024]{1,0:T(8,128)(2,1)S(1)}, u32[]{:S(2)}, u32[]{:S(2)}) collective-permute-start(bf16[512,1024]{1,0:T(8,128)(2,1)S(1)} %far.1), channel_id=1, source_target_pairs={{0,2},{1,3},{2,0},{3,1},{4,6},{5,7},{6,4},{7,5},{8,10},{9,11},{10,... | collective-permute-start | bytes 3145736 | tf_op jit(solution)/shard_map/ppermute | solution.py:36
  44.9 5.0 %collective-permute-start.14 = (bf16[2,128,128]{2,1,0:T(8,128)(2,1)S(1)}, bf16[2,128,128]{2,1,0:T(8,128)(2,1)S(1)}, u32[]{:S(2)}, u32[]{:S(2)}) collective-permute-start(bf16[2,128,128]{2,1,0:T(8,128)(2,1)S(1)} %add_convert_fusion.1.rest_0_), channel_id=1, source_target_pairs={{0,4},{4,0},{8,12},{12,8},{1,5},{5,1},{9,13},{13,9},{2,6},{6,2},{1... | collective-permute-start | bytes 196616 | tf_op jit(solution)/shard_map/ppermute | solution.py:36
  45.0 7.9 %collective-permute-start.15 = (bf16[2,128,128]{2,1,0:T(8,128)(2,1)S(1)}, bf16[2,128,128]{2,1,0:T(8,128)(2,1)S(1)}, u32[]{:S(2)}, u32[]{:S(2)}) collective-permute-start(bf16[2,128,128]{2,1,0:T(8,128)(2,1)S(1)} %add_convert_fusion.1.rest_0_), channel_id=1, source_target_pairs={{0,8},{4,12},{8,0},{12,4},{1,9},{5,13},{9,1},{13,5},{2,10},{6,14},... | collective-permute-start | bytes 196616 | tf_op jit(solution)/shard_map/ppermute | solution.py:36
  47.7 6.4 %collective-permute-start.16 = (bf16[2,128,128]{2,1,0:T(8,128)(2,1)S(1)}, bf16[2,128,128]{2,1,0:T(8,128)(2,1)S(1)}, u32[]{:S(2)}, u32[]{:S(2)}) collective-permute-start(bf16[2,128,128]{2,1,0:T(8,128)(2,1)S(1)} %add_convert_fusion.1.rest_0_), channel_id=1, source_target_pairs={{0,12},{4,8},{8,4},{12,0},{1,13},{5,9},{9,5},{13,1},{2,14},{6,10},... | collective-permute-start | bytes 196616 | tf_op jit(solution)/shard_map/ppermute | solution.py:36
  49.9 5.6 %collective-permute-start.17 = (bf16[2,128,128]{2,1,0:T(8,128)(2,1)S(1)}, bf16[2,128,128]{2,1,0:T(8,128)(2,1)S(1)}, u32[]{:S(2)}, u32[]{:S(2)}) collective-permute-start(bf16[2,128,128]{2,1,0:T(8,128)(2,1)S(1)} %add_convert_fusion.1.rest_0_), channel_id=1, source_target_pairs={{0,16},{16,0},{1,17},{17,1},{2,18},{18,2},{3,19},{19,3},{4,20},{20... | collective-permute-start | bytes 196616 | tf_op jit(solution)/shard_map/ppermute | solution.py:36
  52.9 4.3 %collective-permute-start.18 = (bf16[2,128,128]{2,1,0:T(8,128)(2,1)S(1)}, bf16[2,128,128]{2,1,0:T(8,128)(2,1)S(1)}, u32[]{:S(2)}, u32[]{:S(2)}) collective-permute-start(bf16[2,128,128]{2,1,0:T(8,128)(2,1)S(1)} %collective-permute-done.14.rest_1_), channel_id=1, source_target_pairs={{0,16},{16,0},{1,17},{17,1},{2,18},{18,2},{3,19},{19,3},{4,20},{20... | collective-permute-start | bytes 196616 | tf_op jit(solution)/shard_map/ppermute | solution.py:36
  54.1 4.3 %collective-permute-start.19 = (bf16[2,128,128]{2,1,0:T(8,128)(2,1)S(1)}, bf16[2,128,128]{2,1,0:T(8,128)(2,1)S(1)}, u32[]{:S(2)}, u32[]{:S(2)}) collective-permute-start(bf16[2,128,128]{2,1,0:T(8,128)(2,1)S(1)} %collective-permute-done.15.rest_2_), channel_id=1, source_target_pairs={{0,16},{16,0},{1,17},{17,1},{2,18},{18,2},{3,19},{19,3},{4,20},{20... | collective-permute-start | bytes 196616 | tf_op jit(solution)/shard_map/ppermute | solution.py:36
  55.5 4.3 %collective-permute-start.20 = (bf16[2,128,128]{2,1,0:T(8,128)(2,1)S(1)}, bf16[2,128,128]{2,1,0:T(8,128)(2,1)S(1)}, u32[]{:S(2)}, u32[]{:S(2)}) collective-permute-start(bf16[2,128,128]{2,1,0:T(8,128)(2,1)S(1)} %collective-permute-done.16.rest_3_), channel_id=1, source_target_pairs={{0,16},{16,0},{1,17},{17,1},{2,18},{18,2},{3,19},{19,3},{4,20},{20... | collective-permute-start | bytes 196616 | tf_op jit(solution)/shard_map/ppermute | solution.py:36
  57.2 15.1 %collective-permute-start.6 = (bf16[544,128]{1,0:T(8,128)(2,1)S(1)}, bf16[544,128]{1,0:T(8,128)(2,1)S(1)}, u32[]{:S(2)}, u32[]{:S(2)}) collective-permute-start(bf16[544,128]{1,0:T(8,128)(2,1)S(1)} %merge.2.a_ref), channel_id=1, source_target_pairs={{0,2},{1,3},{2,0},{3,1},{4,6},{5,7},{6,4},{7,5},{8,10},{9,11},{10,... | collective-permute-start | bytes 417800 | tf_op jit(solution)/shard_map/ppermute | solution.py:36
  60.8 1.4 %collective-permute-start.21 = (bf16[544,128]{1,0:T(8,128)(2,1)S(1)}, bf16[544,128]{1,0:T(8,128)(2,1)S(1)}, u32[]{:S(2)}, u32[]{:S(2)}) collective-permute-start(bf16[544,128]{1,0:T(8,128)(2,1)S(1)} %get-tuple-element.41.after_ref.a_ref), channel_id=1, source_target_pairs={{0,1},{1,0},{2,3},{3,2},{4,5},{5,4},{6,7},{7,6},{8,9},{9,8},{10,11... | collective-permute-start | bytes 417800 | tf_op jit(solution)/shard_map/ppermute | solution.py:36
  62.2 12.1 %collective-permute-start.22 = (bf16[544,128]{1,0:T(8,128)(2,1)S(1)}, bf16[544,128]{1,0:T(8,128)(2,1)S(1)}, u32[]{:S(2)}, u32[]{:S(2)}) collective-permute-start(bf16[544,128]{1,0:T(8,128)(2,1)S(1)} %merge.3.s_ref), channel_id=1, source_target_pairs={{0,2},{1,3},{2,0},{3,1},{4,6},{5,7},{6,4},{7,5},{8,10},{9,11},{10,... | collective-permute-start | bytes 417800 | tf_op jit(solution)/shard_map/ppermute | solution.py:36

commit v3 on v1

v3 whole, which is shorter than its diff:
```python
import functools

import jax
import jax.numpy as jnp
from jax import lax
from jax.experimental import pallas as pl
from jax.experimental.pallas import tpu as pltpu
from jax.sharding import PartitionSpec as P

D = 4096
HEAD = 128
SCALE = 2.0
LEARN = 3.0
EPS = 1e-05
NORM_EPS = 1e-06
LANES = 128
EXTRA = 32

BF = jnp.bfloat16
F32 = jnp.float32
VMEM = pl.BlockSpec(memory_space=pltpu.VMEM)
SMEM = pl.BlockSpec(memory_space=pltpu.SMEM)
ANY = pl.BlockSpec(memory_space=pl.ANY)
HBM = pl.BlockSpec(memory_space=pltpu.HBM)


def shape(dims, dtype):
    return jax.ShapeDtypeStruct(dims, dtype)


def dot(a, b, dims=((1,), (0,))):
    return lax.dot_general(a, b, (dims, ((), ())), preferred_element_type=F32)


def swap(x, axis, n, k):
    return lax.ppermute(x, axis, [(i, i ^ k) for i in range(n)])


def split_terms(values):
    high = values.astype(BF)
    rest = values - high.astype(F32)
    middle = rest.astype(BF)
    last = (rest - middle.astype(F32)).astype(BF)
    return jnp.concatenate([high, middle, last, jnp.zeros_like(last)], axis=0)


def join_terms(terms):
    x = terms.astype(F32)
    return (x[0:8] + x[8:16]) + x[16:24]


def fetch(sources, targets, sems):
    copies = [pltpu.make_async_copy(s, t, sems.at[i]) for i, (s, t) in enumerate(zip(sources, targets))]
    for copy in copies:
        copy.start()
    return copies


def place(at, sizes, kx, kz, size):
    start = ((at[1] ^ kx) * sizes[1] + (at[2] ^ kz)) * size
    return pl.ds(pl.multiple_of(start, size), size)


def blocks_of(count):
    return [slice(i, i + LANES) for i in range(0, count, LANES)]


def rank_kernel(x_hbm, v_hbm, a_hbm, b_hbm, out_ref, x_ref, v_ref, a_ref, b_ref, sems):
    copies = fetch((x_hbm, a_hbm, v_hbm, b_hbm), (x_ref, a_ref, v_ref, b_ref), sems)
    count = x_ref.shape[0]
    copies[0].wait()
    copies[1].wait()
    out_ref[:count] = dot(x_ref[...], a_ref[...].astype(BF)).astype(BF)
    copies[2].wait()
    copies[3].wait()
    out_ref[count:] = dot(v_ref[...], b_ref[...].astype(BF), ((1,), (1,))).astype(BF)


def prep_kernel(h_hbm, gain_hbm, a_hbm, hg_ref, pack_ref, h_ref, gain_ref, a_ref, sems):
    count = h_ref.shape[0]
    blocks = blocks_of(count)
    copies = fetch(
        [gain_hbm] + [h_hbm.at[b] for b in blocks] + [a_hbm],
        [gain_ref] + [h_ref.at[b] for b in blocks] + [a_ref],
        sems,
    )
    copies[0].wait()
    rows = []
    for i, b in enumerate(blocks):
        copies[1 + i].wait()
        wide = h_ref[b].astype(F32)
        hg_ref[b] = (wide * gain_ref[...]).astype(BF)
        sums = jnp.sum(wide * wide, axis=-1, keepdims=True)
        rows.append(jnp.broadcast_to(sums, (LANES, LANES)).T[0:1])
    if len(rows) < 8:
        rows.append(jnp.zeros((8 - len(rows), LANES), F32))
    pack_ref[count:] = split_terms(jnp.concatenate(rows, axis=0))
    copies[-1].wait()
    pack_ref[:count] = dot(hg_ref[...], a_ref[...].astype(BF)).astype(BF)


def query_kernel(peers, cut, at, hg_ref, w_hbm, pack_ref, after_ref, one_ref, two_ref, w_ref, sems):
    count, width = hg_ref.shape
    per = width // cut
    sources = []
    for i in range(2 * per):
        start = (at[0] ^ peers[i // per]) * width + (i % per) * cut
        sources.append(w_hbm.at[:, pl.ds(pl.multiple_of(start, cut), cut)])
    copies = fetch(sources, [w_ref.at[i] for i in range(2 * per)], sems)
    if one_ref.shape[0] > count:
        one_ref[count:, :width] = jnp.zeros((EXTRA, width), BF)
        one_ref[:, width:] = pack_ref[...]
    for i in range(2 * per):
        copies[i].wait()
        out = one_ref if i < per else two_ref
        out[:count, (i % per) * cut : (i % per + 1) * cut] = dot(hg_ref[...], w_ref[i]).astype(BF)


def far_kernel(mine_ref, diag_ref, got_ref, after_ref, out_ref):
    count, width = mine_ref.shape
    out_ref[:count, :width] = (mine_ref[...].astype(F32) + got_ref[:count, :width].astype(F32)).astype(BF)
    out_ref[count:, :width] = jnp.zeros((EXTRA, width), BF)
    out_ref[:count, width:] = (diag_ref[:count, width:].astype(F32) + got_ref[:count, width:].astype(F32)).astype(BF)
    out_ref[count:, width:] = split_terms(join_terms(diag_ref[count:, width:]) + join_terms(got_ref[count:, width:]))


def merge_kernel(a_ref, b_ref, out_ref):
    count = a_ref.shape[0] - EXTRA
    out_ref[:count] = (a_ref[:count].astype(F32) + b_ref[:count].astype(F32)).astype(BF)
    out_ref[count:] = split_terms(join_terms(a_ref[count:]) + join_terms(b_ref[count:]))


def grad_kernel(sizes, at, x_ref, v_ref, s_ref, r_ref, *rest):
    outs, (ga, gb) = rest[:-2], rest[-2:]
    count, width = x_ref.shape
    low = (s_ref[...].astype(F32) + r_ref[...].astype(F32)).astype(BF)
    ga[...] = SCALE * dot(x_ref[...], low[count:], ((0,), (0,)))
    turned = SCALE * dot(low[:count], v_ref[...], ((0,), (0,)))
    for b in blocks_of(width):
        gb[b] = turned[:, b]
    size = width // (sizes[0] * sizes[1])
    for kx, out in enumerate(outs):
        for kz in range(sizes[1]):
            rows = place(at, sizes, kx, kz, size)
            out[kz, 0] = ga[rows].astype(out.dtype)
            out[kz, 1] = gb[rows].astype(out.dtype)


def cross_kernel(n_dp, own_ref, *rest):
    got, (pos_ref, after_ref, keep_ref), sends = rest[: n_dp - 1], rest[n_dp - 1 : n_dp + 2], rest[n_dp + 2 : -1]
    rest[-1][...] = pos_ref[...].astype(F32)
    for kz, out in enumerate((keep_ref,) + sends):
        total = own_ref[kz]
        for g in got:
            total = total + g[kz].astype(F32)
        out[...] = total.astype(out.dtype)


def chunk_kernel(keep_ref, *rest):
    got, (a_ref, b_ref) = rest[:-2], rest[-2:]
    total = keep_ref[...]
    for g in got:
        total = total + g[...].astype(F32)
    size = total.shape[1]
    a_ref[:size] = total[0].astype(BF)
    b_ref[...] = total[1].astype(BF)
    squares = total[0] * total[0] + total[1] * total[1]
    a_ref[size:] = split_terms(jnp.broadcast_to(jnp.sum(squares), (8, LANES)))


def hold_kernel(x_ref, after_ref, out_ref):
    out_ref[...] = x_ref[...]


def stack_kernel(*refs):
    for k, ref in enumerate(refs[:-1]):
        refs[-1][k] = ref[...]


def low_kernel(sizes, at, hg_ref, *rest):
    pieces, (pack_ref, ga_ref, sums_ref) = rest[:-3], rest[-3:]
    size = pieces[0].shape[0] - EXTRA
    for kx in range(sizes[0]):
        for kz in range(sizes[1]):
            piece = pieces[kx * sizes[1] + kz]
            ga_ref[place(at, sizes, kx, kz, size)] = piece[:size]
            sums_ref[place(at, sizes, kx, kz, 8)] = join_terms(piece[size:])
    count = hg_ref.shape[0]
    pack_ref[:count] = dot(hg_ref[...], ga_ref[...]).astype(BF)
    total = sums_ref[0:8]
    for i in range(1, len(pieces)):
        total = total + sums_ref[8 * i : 8 * i + 8]
    pack_ref[count:] = split_terms(total)


def base_kernel(mine_ref, near_ref, far_ref, far_got, after_ref, base_ref, low_ref, scale_ref):
    count, width = mine_ref.shape
    sums = join_terms(far_ref[count:, width:]) + join_terms(far_got[count:, width:])
    scale = lax.rsqrt(sums / D + EPS)
    for i, b in enumerate(blocks_of(count)):
        block = jnp.broadcast_to(scale[i : i + 1], (LANES, LANES)).T
        scale_ref[b] = block
        low_ref[b] = (far_ref[b, width:].astype(F32) + far_got[b, width:].astype(F32)) * block
        for c in blocks_of(width):
            total = mine_ref[b, c].astype(F32) + near_ref[b, c].astype(F32) + far_got[b, c].astype(F32)
            base_ref[b, c] = total * block


def final_kernel(sizes, at, base_ref, low_ref, scale_ref, s_ref, r_ref, ga_ref, a_ref, b_ref, cos_ref, sin_ref, *rest):
    parts, (a_hbm, b_hbm, q_hbm, gb, new_a, new_b, half_b, out, sems) = rest[:-9], rest[-9:]
    count, width = base_ref.shape
    total = join_terms(s_ref[count:]) + join_terms(r_ref[count:])
    rate = (LEARN * lax.rsqrt(total + NORM_EPS))[0:1]
    size = parts[0].shape[1]
    for kx, part in enumerate(parts):
        for kz in range(sizes[1]):
            gb[place(at, sizes, kx, kz, size)] = part[kz]
    for c in blocks_of(width):
        fresh = b_ref[:, c] - rate * gb[c].astype(F32)
        new_b[:, c] = fresh
        half_b[:, c] = fresh.astype(BF)
    copies = [pltpu.make_async_copy(new_b, b_hbm, sems.at[0])]
    copies[-1].start()
    new_a[...] = a_ref[...] - rate * ga_ref[...].astype(F32)
    copies.append(pltpu.make_async_copy(new_a, a_hbm, sems.at[1]))
    copies[-1].start()
    for i, b in enumerate(blocks_of(count)):
        low = s_ref[b].astype(F32) + r_ref[b].astype(F32)
        mix = (low_ref[b] - rate * (low * scale_ref[b])) * SCALE
        update = dot(mix.astype(BF), half_b[...])
        cos, sin = cos_ref[b], sin_ref[b]
        for c in blocks_of(width):
            query = base_ref[b, c] + update[:, c]
            other = pltpu.roll(query, HEAD // 2, 1)
            out[b, c] = (query * cos + other * sin).astype(BF)
        copies.append(pltpu.make_async_copy(out.at[b], q_hbm.at[b], sems.at[2 + i]))
        copies[-1].start()
    for copy in copies:
        copy.wait()


def call(kernel, outs, in_specs, args, name, scratch=(), out_specs=None, limit=32):
    return pl.pallas_call(
        kernel,
        out_shape=outs,
        in_specs=in_specs,
        out_specs=out_specs if out_specs is not None else jax.tree.map(lambda _: VMEM, outs),
        scratch_shapes=list(scratch),
        compiler_params=pltpu.CompilerParams(vmem_limit_bytes=int(limit * 1024 * 1024)),
        name=name,
    )(*args)


def turn_tables(places, steps):
    half = HEAD // 2
    freq = 10000.0 ** (-jnp.arange(half, dtype=F32) / half)
    cos, sin = [], []
    for step in range(steps):
        angle = (places + float(step))[:, None] * freq[None, :]
        c, s = jnp.cos(angle), jnp.sin(angle)
        cos.append(jnp.concatenate([c, c], axis=-1))
        sin.append(jnp.concatenate([-s, s], axis=-1))
    return jnp.concatenate(cos), jnp.concatenate(sin)


def build(n_dp, n_roll, n_tp):
    sizes = (n_dp, n_roll)

    def on_device(
        train_inputs, train_cotangent, factor_a, factor_b, base_weight, incoming, norm_gain, positions
    ):
        steps, rows, width = incoming.shape
        tokens = train_inputs.shape[0]
        rank = factor_a.shape[1]
        count = steps * rows
        tp, dp, roll = (lax.axis_index(a) for a in ("tp", "dp", "roll"))
        at = jnp.stack([tp, dp, roll]).astype(jnp.int32)
        dma = lambda n: pltpu.SemaphoreType.DMA((n,))

        part = call(
            rank_kernel,
            shape((2 * tokens, rank), BF),
            [HBM] * 4,
            (train_inputs, train_cotangent, factor_a, factor_b),
            "rank",
            [pltpu.VMEM(train_inputs.shape, BF), pltpu.VMEM(train_inputs.shape, BF),
             pltpu.VMEM(factor_a.shape, F32), pltpu.VMEM(factor_b.shape, F32), dma(4)],
            limit=63.5,
        )
        part_got = swap(part, "tp", n_tp, 1)
        gained, pack = call(
            prep_kernel,
            [shape((count, width), BF), shape((count + EXTRA, rank), BF)],
            [HBM] * 3,
            (incoming.reshape(count, width), norm_gain[None, :], factor_a),
            "prep",
            [pltpu.VMEM((count, width), BF), pltpu.VMEM((1, width), F32), pltpu.VMEM(factor_a.shape, F32),
             dma(2 + count // LANES)],
            limit=60,
        )
        part_sum = (part.astype(F32) + part_got.astype(F32)).astype(BF)
        part_far = swap(part_sum, "tp", n_tp, 2)

        cut = 512
        wide = shape((count + EXTRA, width + rank), BF)
        tall = shape((count, width), BF)

        def query(peers, outs, after, name):
            return call(
                functools.partial(query_kernel, peers, cut),
                outs,
                [SMEM, VMEM, HBM, VMEM, ANY],
                (at, gained, base_weight, pack, after),
                name,
                [pltpu.VMEM((2 * width // cut, width, cut), BF), dma(2 * width // cut)],
                limit=56,
            )

        diag, distant = query((3, 2), [wide, tall], part_sum, "query_first")
        diag_got = swap(diag, "tp", n_tp, 1)

        size = width // (n_dp * n_roll)
        grads = call(
            functools.partial(grad_kernel, sizes),
            [shape((n_roll, 2, size, rank), F32)] + [shape((n_roll, 2, size, rank), BF)] * (n_dp - 1),
            [SMEM] + [VMEM] * 4,
            (at, train_inputs, train_cotangent, part_sum, part_far),
            "grads",
            [pltpu.VMEM((width, rank), F32), pltpu.VMEM((width, rank), F32)],
        )
        grads_got = [swap(grads[kx], "dp", n_dp, kx) for kx in range(1, n_dp)]
        far = call(far_kernel, wide, [VMEM] * 3 + [ANY], (distant, diag, diag_got, grads[-1]), "far")
        far_got = swap(far, "tp", n_tp, 2)
        beside, close = query((1, 0), [tall, tall], far, "query_second")
        beside_got = swap(beside, "tp", n_tp, 1)

        pos = positions.reshape(-1, LANES)
        crossed = call(
            functools.partial(cross_kernel, n_dp),
            [shape((2, size, rank), F32)] + [shape((2, size, rank), BF)] * (n_roll - 1) + [shape(pos.shape, F32)],
            [VMEM] * (n_dp + 1) + [ANY],
            (grads[0], *grads_got, pos, close),
            "cross",
        )
        places = crossed[-1].reshape(rows)
        chunk_a, chunk_b = call(
            chunk_kernel,
            [shape((size + EXTRA, rank), BF), shape((size, rank), BF)],
            [VMEM] * n_roll,
            (crossed[0], *[swap(crossed[kz], "roll", n_roll, kz) for kz in range(1, n_roll)]),
            "chunk",
        )
        pieces = [chunk_a] + [swap(chunk_a, "roll", n_roll, kz) for kz in range(1, n_roll)]
        chunk_b = call(hold_kernel, shape((size, rank), BF), [VMEM, ANY], (chunk_b, pieces[-1]), "hold")
        for kx in range(1, n_dp):
            pieces += [swap(pieces[kz], "dp", n_dp, kx) for kz in range(n_roll)]
        step_pack, grad_a = call(
            functools.partial(low_kernel, sizes),
            [shape((count + EXTRA, rank), BF), shape((width, rank), BF)],
            [SMEM] + [VMEM] * (1 + len(pieces)),
            (at, gained, *pieces),
            "low_rank",
            [pltpu.VMEM((8 * len(pieces), LANES), F32)],
        )
        step_got = swap(step_pack, "tp", n_tp, 1)
        parts_b = [chunk_b] + [swap(chunk_b, "roll", n_roll, kz) for kz in range(1, n_roll)]
        stack_b = call(stack_kernel, shape((n_roll, size, rank), BF), [VMEM] * n_roll, parts_b, "stack")
        grad_b = [stack_b] + [swap(stack_b, "dp", n_dp, kx) for kx in range(1, n_dp)]
        step_sum = call(merge_kernel, shape((count + EXTRA, rank), BF), [VMEM] * 2, (step_pack, step_got), "merge")
        step_far = swap(step_sum, "tp", n_tp, 2)
        base, low, scale = call(
            base_kernel,
            [shape((count, width), F32), shape((count, rank), F32), shape((count, LANES), F32)],
            [VMEM] * 4 + [ANY],
            (close, beside_got, far, far_got, step_pack),
            "base",
        )
        cos, sin = turn_tables(places, steps)
        new_a, new_b, queries = call(
            functools.partial(final_kernel, sizes),
            [shape((width, rank), F32), shape((rank, width), F32), tall],
            [SMEM] + [VMEM] * (10 + n_dp),
            (at, base, low, scale, step_sum, step_far, grad_a, factor_a, factor_b, cos, sin, *grad_b),
            "final",
            [pltpu.VMEM((width, rank), BF), pltpu.VMEM((width, rank), F32), pltpu.VMEM((rank, width), F32),
             pltpu.VMEM((rank, width), BF), pltpu.VMEM((count, width), BF), dma(2 + count // LANES)],
            [HBM] * 3,
        )
        return new_a, new_b, queries.reshape(steps, rows, width)

    return on_device


def solution(mesh):
    n_dp, n_roll, n_tp = (mesh.shape[a] for a in ("dp", "roll", "tp"))
    return jax.shard_map(
        build(n_dp, n_roll, n_tp),
        mesh=mesh,
        in_specs=(
            P(("dp", "roll"), "tp"),
            P(("dp", "roll"), "tp"),
            P("tp", None),
            P(None, "tp"),
            P("tp", None),
            P(None, ("dp", "roll"), "tp"),
            P("tp"),
            P(("dp", "roll")),
        ),
        out_specs=(P("tp", None), P(None, "tp"), P(None, ("dp", "roll"), "tp")),
        check_vma=False,
    )
```

time: 118 us -> 78.2 us (0.66)
  Pallas kernels: 0 us -> 24.4 us
  matrix products: 18.5 us -> 0 us
  other arithmetic: 20.1 us -> 2.56 us
  starting transfers between devices: 35 us -> 21.2 us
  local copies, waits for them, and re-layouts: 15.8 us -> 2.57 us
  between operations: 3.46 us -> 0.92 us
  waiting for transfers between devices: 24.9 us -> 26.2 us
    pallas_call x0 -> x14, Pallas kernels: none -> 24.4 us  [call(): pl.pallas_call(kernel, out_shape=outs, in_specs=in_specs, out_specs=out_s...]
    dot_general x8 -> x0, matrix products: 18.5 us -> none  [the longest x1 8.1 us: on_device(): part_q = jnp.dot(gained, base_weight, preferred_element_type=F32).astype(BF)]
    ppermute x21 -> x22, starting transfers between devices: 35 us -> 21.2 us  [swap(): return lax.ppermute(x, axis, [(i, i ^ k) for i in range(n)])]
    convert_element_type x11 -> x1, other arithmetic: 12.9 us -> 0.73 us  [on_device(): part_sum = (part.astype(F32) + part_got.astype(F32)).astype(BF)]
    mul x3 -> x0, local copies, waits for them, and re-layouts: 4.45 us -> none  [on_device(): turned = heads * cos[:, :, None, :] + other * sin[:, :, None, :]]
    another operation x2 -> x0, local copies, waits for them, and re-layouts: 2.46 us -> none  [on_device(): grads = jnp.stack([grad_a, grad_b], axis=1)]
    unnamed x38 -> x32, local copies, waits for them, and re-layouts: 4.55 us -> 2.57 us
    mul x1 -> x0, other arithmetic: 1.94 us -> none  [on_device(): turned = heads * cos[:, :, None, :] + other * sin[:, :, None, :]]
  transfers between devices with their start and end apart: 21 -> 22, of which waited for: 11 -> 12; matrix products, arithmetic and copies ran while one was open for 31% -> 2% of each run, Pallas kernels for 0% -> 16%
where the time goes in v3:
time: 78.2 us; the launch traced here: 77.9 us
  waiting for transfers between devices  26.2 us (34%)
  Pallas kernels  24.4 us (31%)
  starting transfers between devices  21.2 us (27%)
  local copies, waits for them, and re-layouts  2.57 us (3%)
  other arithmetic  2.56 us (3%)
  between operations  0.92 us (1%)
    ppermute x22, waiting for transfers between devices, swap(): return lax.ppermute(x, axis, [(i, i ^ k) for i in range(n)])  26.2 us
    pallas_call x14, Pallas kernels, call(): pl.pallas_call(kernel, out_shape=outs, in_specs=in_specs, out_specs=out_s...  24.4 us
    ppermute x22, starting transfers between devices, swap(): return lax.ppermute(x, axis, [(i, i ^ k) for i in range(n)])  21.2 us
    unnamed x32, local copies, waits for them, and re-layouts  2.57 us
  transfers between devices with their start and end apart: 22, of which 12 were waited for; matrix products, arithmetic and copies ran while one was open for 2% of the time, Pallas kernels for 16%

profile of v3, /device:TPU:0, one launch (start us, length us, event | category | flops | bytes accessed | tf_op | source)
XLA Modules:
  0.0 77.9 jit_solution(431861411140527836)
XLA Ops:
  0.6 3.1 %rank.1 = bf16[768,128]{1,0:T(8,128)(2,1)} custom-call(bf16[384,1024]{1,0:T(8,128)(2,1)} %x_ref.1, bf16[384,1024]{1,0:T(8,128)(2,1)} %v_ref.1, f32[1024,128]{1,0:T(8,128)} %a_ref.1, f32[128,1024]{1,0:T(8,128)} %b_ref.1), custom_call_target="tpu_custom_call" | custom-call | tf_op jit(solution)/shard_map/rank/pallas_call | solution.py:243
  3.8 0.5 collective-permute-start
  4.3 2.9 %prep.1 = (bf16[512,1024]{1,0:T(8,128)(2,1)}, bf16[544,128]{1,0:T(8,128)(2,1)}) custom-call(bf16[512,1024]{1,0:T(8,128)(2,1)} %bitcast.11, f32[1,1024]{1,0:T(1,128)} %bitcast.12, f32[1024,128]{1,0:T(8,128)} %a_ref.1), custom_call_target="tpu_custom_call" | custom-call | tf_op jit(solution)/shard_map/prep/pallas_call | solution.py:243
  7.2 0.6 pad_add_fusion.at
  7.8 0.7 add_convert_fusion.after_ref.s_ref
  8.5 6.5 %query_first.1 = (bf16[544,1152]{1,0:T(8,128)(2,1)}, bf16[512,1024]{1,0:T(8,128)(2,1)}) custom-call(s32[3]{0:T(128)} %pad_add_fusion.at, bf16[512,1024]{1,0:T(8,128)(2,1)} %get-tuple-element.26.hg_ref, bf16[1024,4096]{1,0:T(8,128)(2,1)} %w_hbm.3, bf16[544,128]{1,0:T(8,128)(2,1)} %get-tuple-element.27.pack_ref, bf16[768,128]{1,0:T(8,128)(2,1)} %add_convert_fusion.after_ref.s_ref), custom_call_target="tpu_custom_call" | custom-call | tf_op jit(solution)/shard_map/query_first/pallas_call | solution.py:243
  15.0 0.1 collective-permute-start.1
  15.2 3.0 %collective-permute-start.2 = (bf16[768,128]{1,0:T(8,128)(2,1)S(1)}, bf16[768,128]{1,0:T(8,128)(2,1)S(1)}, u32[]{:S(2)}, u32[]{:S(2)}) collective-permute-start(bf16[768,128]{1,0:T(8,128)(2,1)S(1)} %copy-done.9), channel_id=1, source_target_pairs={{0,2},{1,3},{2,0},{3,1},{4,6},{5,7},{6,4},{7,5},{8,10},{9,11},{10,... | collective-permute-start | bytes 589832 | tf_op jit(solution)/shard_map/ppermute | solution.py:36
  18.1 5.2 %collective-permute-done.2.r_ref = bf16[768,128]{1,0:T(8,128)(2,1)S(1)} collective-permute-done((bf16[768,128]{1,0:T(8,128)(2,1)S(1)}, bf16[768,128]{1,0:T(8,128)(2,1)S(1)}, u32[]{:S(2)}, u32[]{:S(2)}) %collective-permute-start.2) | collective-permute-done | bytes 196640 | tf_op jit(solution)/shard_map/ppermute | solution.py:36
  23.3 1.1 %grads.1 = (f32[4,2,128,128]{3,2,1,0:T(8,128)S(1)}, bf16[4,2,128,128]{3,2,1,0:T(8,128)(2,1)S(1)}) custom-call(s32[3]{0:T(128)S(1)} %copy-done.12, bf16[384,1024]{1,0:T(8,128)(2,1)S(1)} %copy-done.6, bf16[384,1024]{1,0:T(8,128)(2,1)S(1)} %copy-done.7, bf16[768,128]{1,0:T(8,128)(2,1)S(1)} %copy-done.9, bf16[768,128]{1,0:T(8,128)(2,1)S(1)} %collective-permute-done.2.r_ref), custom_call_target="tpu_custom_call" | custom-call | tf_op jit(solution)/shard_map/grads/pallas_call | solution.py:243
  24.4 1.2 %copy-done.11 = bf16[512,1024]{1,0:T(8,128)(2,1)S(1)} copy-done((bf16[512,1024]{1,0:T(8,128)(2,1)S(1)}, bf16[512,1024]{1,0:T(8,128)(2,1)}, u32[]{:S(2)}) %copy-start.11) | copy-done | bytes 1048600
  25.7 0.3 far.1.after_ref.far_ref
  26.0 1.8 %collective-permute-start.4 = (bf16[544,1152]{1,0:T(8,128)(2,1)S(1)}, bf16[544,1152]{1,0:T(8,128)(2,1)S(1)}, u32[]{:S(2)}, u32[]{:S(2)}) collective-permute-start(bf16[544,1152]{1,0:T(8,128)(2,1)S(1)} %far.1.after_ref.far_ref), channel_id=1, source_target_pairs={{0,2},{1,3},{2,0},{3,1},{4,6},{5,7},{6,4},{7,5},{8,10},{9,11},{10,... | collective-permute-start | bytes 3760136 | tf_op jit(solution)/shard_map/ppermute | solution.py:36
  27.8 1.5 %collective-permute-start.5 = (bf16[4,2,128,128]{3,2,1,0:T(8,128)(2,1)S(1)}, bf16[4,2,128,128]{3,2,1,0:T(8,128)(2,1)S(1)}, u32[]{:S(2)}, u32[]{:S(2)}) collective-permute-start(bf16[4,2,128,128]{3,2,1,0:T(8,128)(2,1)S(1)} %get-tuple-element.30.after_ref), channel_id=1, source_target_pairs={{0,16},{16,0},{1,17},{17,1},{2,18},{18,2},{3,19},{19,3},{4,20},{20... | collective-permute-start | bytes 786440 | tf_op jit(solution)/shard_map/ppermute | solution.py:36
  29.3 6.3 %query_second.1 = (bf16[512,1024]{1,0:T(8,128)(2,1)}, bf16[512,1024]{1,0:T(8,128)(2,1)}) custom-call(s32[3]{0:T(128)} %pad_add_fusion.at, bf16[512,1024]{1,0:T(8,128)(2,1)} %get-tuple-element.26.hg_ref, bf16[1024,4096]{1,0:T(8,128)(2,1)} %w_hbm.3, bf16[544,128]{1,0:T(8,128)(2,1)} %get-tuple-element.27.pack_ref, bf16[544,1152]{1,0:T(8,128)(2,1)} %copy-done), custom_call_target="tpu_custom_call" | custom-call | tf_op jit(solution)/shard_map/query_second/pallas_call | solution.py:243
  35.7 0.1 collective-permute-start.3
  35.8 1.3 %copy-done.4 = bf16[512,1024]{1,0:T(8,128)(2,1)S(1)} copy-done((bf16[512,1024]{1,0:T(8,128)(2,1)S(1)}, bf16[512,1024]{1,0:T(8,128)(2,1)}, u32[]{:S(2)}) %copy-start.4) | copy-done | bytes 1048600
  37.1 1.6 %collective-permute-start.6 = (bf16[2,128,128]{2,1,0:T(8,128)(2,1)S(1)}, bf16[2,128,128]{2,1,0:T(8,128)(2,1)S(1)}, u32[]{:S(2)}, u32[]{:S(2)}) collective-permute-start(bf16[2,128,128]{2,1,0:T(8,128)(2,1)S(1)} %get-tuple-element.35), channel_id=1, source_target_pairs={{0,4},{4,0},{8,12},{12,8},{1,5},{5,1},{9,13},{13,9},{2,6},{6,2},{1... | collective-permute-start | bytes 196616 | tf_op jit(solution)/shard_map/ppermute | solution.py:36
  38.7 2.6 %collective-permute-start.7 = (bf16[2,128,128]{2,1,0:T(8,128)(2,1)S(1)}, bf16[2,128,128]{2,1,0:T(8,128)(2,1)S(1)}, u32[]{:S(2)}, u32[]{:S(2)}) collective-permute-start(bf16[2,128,128]{2,1,0:T(8,128)(2,1)S(1)} %get-tuple-element.36), channel_id=1, source_target_pairs={{0,8},{4,12},{8,0},{12,4},{1,9},{5,13},{9,1},{13,5},{2,10},{6,14},... | collective-permute-start | bytes 196616 | tf_op jit(solution)/shard_map/ppermute | solution.py:36
  41.3 0.2 collective-permute-start.8
  41.6 4.9 %collective-permute-done.7.rest_1_ = bf16[2,128,128]{2,1,0:T(8,128)(2,1)S(1)} collective-permute-done((bf16[2,128,128]{2,1,0:T(8,128)(2,1)S(1)}, bf16[2,128,128]{2,1,0:T(8,128)(2,1)S(1)}, u32[]{:S(2)}, u32[]{:S(2)}) %collective-permute-start.7) | collective-permute-done | bytes 65568 | tf_op jit(solution)/shard_map/ppermute | solution.py:36
  46.4 1.0 %collective-permute-done.8.rest_2_ = bf16[2,128,128]{2,1,0:T(8,128)(2,1)S(1)} collective-permute-done((bf16[2,128,128]{2,1,0:T(8,128)(2,1)S(1)}, bf16[2,128,128]{2,1,0:T(8,128)(2,1)S(1)}, u32[]{:S(2)}, u32[]{:S(2)}) %collective-permute-start.8) | collective-permute-done | bytes 65568 | tf_op jit(solution)/shard_map/ppermute | solution.py:36
  47.5 0.2 chunk.1
  47.6 1.3 %collective-permute-start.9 = (bf16[160,128]{1,0:T(8,128)(2,1)S(1)}, bf16[160,128]{1,0:T(8,128)(2,1)S(1)}, u32[]{:S(2)}, u32[]{:S(2)}) collective-permute-start(bf16[160,128]{1,0:T(8,128)(2,1)S(1)} %get-tuple-element.38.rest_0_), channel_id=1, source_target_pairs={{0,4},{4,0},{8,12},{12,8},{1,5},{5,1},{9,13},{13,9},{2,6},{6,2},{1... | collective-permute-start | bytes 122888 | tf_op jit(solution)/shard_map/ppermute | solution.py:36
  48.9 2.4 %collective-permute-start.11 = (bf16[160,128]{1,0:T(8,128)(2,1)S(1)}, bf16[160,128]{1,0:T(8,128)(2,1)S(1)}, u32[]{:S(2)}, u32[]{:S(2)}) collective-permute-start(bf16[160,128]{1,0:T(8,128)(2,1)S(1)} %get-tuple-element.38.rest_0_), channel_id=1, source_target_pairs={{0,12},{4,8},{8,4},{12,0},{1,13},{5,9},{9,5},{13,1},{2,14},{6,10},... | collective-permute-start | bytes 122888 | tf_op jit(solution)/shard_map/ppermute | solution.py:36
  51.3 0.4 collective-permute-done.9.rest_1_
  51.7 0.7 collective-permute-start.12
  52.5 2.3 %collective-permute-done.11.rest_3_.after_ref = bf16[160,128]{1,0:T(8,128)(2,1)S(1)} collective-permute-done((bf16[160,128]{1,0:T(8,128)(2,1)S(1)}, bf16[160,128]{1,0:T(8,128)(2,1)S(1)}, u32[]{:S(2)}, u32[]{:S(2)}) %collective-permute-start.11) | collective-permute-done | bytes 40992 | tf_op jit(solution)/shard_map/ppermute | solution.py:36
  54.7 0.5 collective-permute-start.13
  55.2 1.0 %collective-permute-done.10.rest_2_ = bf16[160,128]{1,0:T(8,128)(2,1)S(1)} collective-permute-done((bf16[160,128]{1,0:T(8,128)(2,1)S(1)}, bf16[160,128]{1,0:T(8,128)(2,1)S(1)}, u32[]{:S(2)}, u32[]{:S(2)}) %collective-permute-start.10) | collective-permute-done | bytes 40992 | tf_op jit(solution)/shard_map/ppermute | solution.py:36
  56.2 0.6 collective-permute-start.15
  56.8 1.9 %collective-permute-done.13.rest_5_ = bf16[160,128]{1,0:T(8,128)(2,1)S(1)} collective-permute-done((bf16[160,128]{1,0:T(8,128)(2,1)S(1)}, bf16[160,128]{1,0:T(8,128)(2,1)S(1)}, u32[]{:S(2)}, u32[]{:S(2)}) %collective-permute-start.13) | collective-permute-done | bytes 40992 | tf_op jit(solution)/shard_map/ppermute | solution.py:36
  58.7 0.5 collective-permute-start.14
  59.2 3.5 %collective-permute-done.14.rest_6_ = bf16[160,128]{1,0:T(8,128)(2,1)S(1)} collective-permute-done((bf16[160,128]{1,0:T(8,128)(2,1)S(1)}, bf16[160,128]{1,0:T(8,128)(2,1)S(1)}, u32[]{:S(2)}, u32[]{:S(2)}) %collective-permute-start.14) | collective-permute-done | bytes 40992 | tf_op jit(solution)/shard_map/ppermute | solution.py:36
  62.7 1.2 %collective-permute-start.19 = (bf16[128,128]{1,0:T(8,128)(2,1)S(1)}, bf16[128,128]{1,0:T(8,128)(2,1)S(1)}, u32[]{:S(2)}, u32[]{:S(2)}) collective-permute-start(bf16[128,128]{1,0:T(8,128)(2,1)S(1)} %hold.1.refs_0_), channel_id=1, source_target_pairs={{0,8},{4,12},{8,0},{12,4},{1,9},{5,13},{9,1},{13,5},{2,10},{6,14},... | collective-permute-start | bytes 98312 | tf_op jit(solution)/shard_map/ppermute | solution.py:36
  63.9 1.2 %collective-permute-start.20 = (bf16[128,128]{1,0:T(8,128)(2,1)S(1)}, bf16[128,128]{1,0:T(8,128)(2,1)S(1)}, u32[]{:S(2)}, u32[]{:S(2)}) collective-permute-start(bf16[128,128]{1,0:T(8,128)(2,1)S(1)} %hold.1.refs_0_), channel_id=1, source_target_pairs={{0,12},{4,8},{8,4},{12,0},{1,13},{5,9},{9,5},{13,1},{2,14},{6,10},... | collective-permute-start | bytes 98312 | tf_op jit(solution)/shard_map/ppermute | solution.py:36
  65.1 1.0 %low_rank.1 = (bf16[544,128]{1,0:T(8,128)(2,1)S(1)}, bf16[1024,128]{1,0:T(8,128)(2,1)S(1)}) custom-call(s32[3]{0:T(128)S(1)} %copy-done.13, bf16[512,1024]{1,0:T(8,128)(2,1)S(1)} %copy-done.2, bf16[160,128]{1,0:T(8,128)(2,1)S(1)} %get-tuple-element.38.rest_0_, bf16[160,128]{1,0:T(8,128)(2,1)S(1)} %collective-permute-done.9.rest_1_, ...), custom_call_target="tpu_custom_call" | custom-call | tf_op jit(solution)/shard_map/low_rank/pallas_call | solution.py:243
  66.2 0.1 collective-permute-start.16
  66.3 1.3 %collective-permute-done.19.refs_2_ = bf16[128,128]{1,0:T(8,128)(2,1)S(1)} collective-permute-done((bf16[128,128]{1,0:T(8,128)(2,1)S(1)}, bf16[128,128]{1,0:T(8,128)(2,1)S(1)}, u32[]{:S(2)}, u32[]{:S(2)}) %collective-permute-start.19) | collective-permute-done | bytes 32800 | tf_op jit(solution)/shard_map/ppermute | solution.py:36
  67.5 2.1 %collective-permute-done.20.refs_3_ = bf16[128,128]{1,0:T(8,128)(2,1)S(1)} collective-permute-done((bf16[128,128]{1,0:T(8,128)(2,1)S(1)}, bf16[128,128]{1,0:T(8,128)(2,1)S(1)}, u32[]{:S(2)}, u32[]{:S(2)}) %collective-permute-start.20) | collective-permute-done | bytes 32800 | tf_op jit(solution)/shard_map/ppermute | solution.py:36
  69.7 0.7 collective-permute-start.21
  70.4 0.6 collective-permute-start.17
  71.0 1.0 %fusion = (f32[256,64]{1,0:T(8,128)S(1)}, f32[256,64]{1,0:T(8,128)S(1)}, f32[256,64]{1,0:T(8,128)S(1)}, f32[256,64]{1,0:T(8,128)S(1)}, f32[256,64]{1,0:T(8,128)S(1)}, /*index=5*/f32[256,64]{1,0:T(8,128)S(1)}) fusion(f32[64]{0:T(128)S(1)} %multiply_power_fusion, f32[256]{0:T(256)S(1)} %bitcast.9, f32[256]{0:T(256)S(1)} %broadcast_add_fusion), kind=kLoop, calls=%fused_computation.7 | loop fusion | flops 65536 | bytes 395520 | tf_op jit(solution)/shard_map/neg | solution.py:262
  72.0 0.2 maximum_maximum_fusion
  72.3 0.5 base.1
  72.8 1.9 %collective-permute-done.21.rest_1_ = bf16[4,128,128]{2,1,0:T(8,128)(2,1)S(1)} collective-permute-done((bf16[4,128,128]{2,1,0:T(8,128)(2,1)S(1)}, bf16[4,128,128]{2,1,0:T(8,128)(2,1)S(1)}, u32[]{:S(2)}, u32[]{:S(2)}) %collective-permute-start.21) | collective-permute-done | bytes 131104 | tf_op jit(solution)/shard_map/ppermute | solution.py:36
  74.7 0.8 %collective-permute-done.17.r_ref = bf16[544,128]{1,0:T(8,128)(2,1)S(1)} collective-permute-done((bf16[544,128]{1,0:T(8,128)(2,1)S(1)}, bf16[544,128]{1,0:T(8,128)(2,1)S(1)}, u32[]{:S(2)}, u32[]{:S(2)}) %collective-permute-start.17) | collective-permute-done | bytes 139296 | tf_op jit(solution)/shard_map/ppermute | solution.py:36
  75.6 2.3 %final.1 = (f32[1024,128]{1,0:T(8,128)}, f32[128,1024]{1,0:T(8,128)}, bf16[512,1024]{1,0:T(8,128)(2,1)}) custom-call(s32[3]{0:T(128)S(1)} %copy-done.13, f32[512,1024]{1,0:T(8,128)S(1)} %get-tuple-element.40.base_ref, f32[512,128]{1,0:T(8,128)S(1)} %get-tuple-element.41.low_ref, f32[512,128]{1,0:T(8,128)S(1)} %get-tuple-element.42.scale_ref, ...), custom_call_target="tpu_custom_call" | custom-call | tf_op jit(solution)/shard_map/final/pallas_call | solution.py:243
  (48 shorter events, 0.3 us)
Async XLA Ops:
  3.7 4.1 %copy-start.15 = (bf16[768,128]{1,0:T(8,128)(2,1)S(1)}, bf16[768,128]{1,0:T(8,128)(2,1)}, u32[]{:S(2)}) copy-start(bf16[768,128]{1,0:T(8,128)(2,1)} %rank.1) | copy-start | bytes 589828
  3.8 4.0 %collective-permute-start = (bf16[768,128]{1,0:T(8,128)(2,1)}, bf16[768,128]{1,0:T(8,128)(2,1)S(1)}, u32[]{:S(2)}, u32[]{:S(2)}) collective-permute-start(bf16[768,128]{1,0:T(8,128)(2,1)} %rank.1), channel_id=1, source_target_pairs={{0,1},{1,0},{2,3},{3,2},{4,5},{5,4},{6,7},{7,6},{8,9},{9,8},{10,11... | collective-permute-start | bytes 589832 | tf_op jit(solution)/shard_map/ppermute | solution.py:36
  8.5 6.6 %copy-start.9 = (bf16[768,128]{1,0:T(8,128)(2,1)S(1)}, bf16[768,128]{1,0:T(8,128)(2,1)}, u32[]{:S(2)}) copy-start(bf16[768,128]{1,0:T(8,128)(2,1)} %add_convert_fusion.after_ref.s_ref) | copy-start | bytes 589828
  8.5 14.7 %copy-start.6 = (bf16[384,1024]{1,0:T(8,128)(2,1)S(1)}, bf16[384,1024]{1,0:T(8,128)(2,1)}, u32[]{:S(2)}) copy-start(bf16[384,1024]{1,0:T(8,128)(2,1)} %x_ref.1) | copy-start | bytes 2359300
  8.5 14.7 %copy-start.7 = (bf16[384,1024]{1,0:T(8,128)(2,1)S(1)}, bf16[384,1024]{1,0:T(8,128)(2,1)}, u32[]{:S(2)}) copy-start(bf16[384,1024]{1,0:T(8,128)(2,1)} %v_ref.1) | copy-start | bytes 2359300
  8.5 14.7 %copy-start.12 = (s32[3]{0:T(128)S(1)}, s32[3]{0:T(128)}, u32[]{:S(2)}) copy-start(s32[3]{0:T(128)} %pad_add_fusion.at) | copy-start | bytes 40
  15.0 9.4 %copy-start.10 = (bf16[544,1152]{1,0:T(8,128)(2,1)S(1)}, bf16[544,1152]{1,0:T(8,128)(2,1)}, u32[]{:S(2)}) copy-start(bf16[544,1152]{1,0:T(8,128)(2,1)} %get-tuple-element.29.diag_ref) | copy-start | bytes 3760132
  15.0 9.4 %collective-permute-start.1 = (bf16[544,1152]{1,0:T(8,128)(2,1)}, bf16[544,1152]{1,0:T(8,128)(2,1)S(1)}, u32[]{:S(2)}, u32[]{:S(2)}) collective-permute-start(bf16[544,1152]{1,0:T(8,128)(2,1)} %get-tuple-element.29.diag_ref), channel_id=1, source_target_pairs={{0,1},{1,0},{2,3},{3,2},{4,5},{5,4},{6,7},{7,6},{8,9},{9,8},{10,11... | collective-permute-start | bytes 3760136 | tf_op jit(solution)/shard_map/ppermute | solution.py:36
  15.2 8.1 %collective-permute-start.2 = (bf16[768,128]{1,0:T(8,128)(2,1)S(1)}, bf16[768,128]{1,0:T(8,128)(2,1)S(1)}, u32[]{:S(2)}, u32[]{:S(2)}) collective-permute-start(bf16[768,128]{1,0:T(8,128)(2,1)S(1)} %copy-done.9), channel_id=1, source_target_pairs={{0,2},{1,3},{2,0},{3,1},{4,6},{5,7},{6,4},{7,5},{8,10},{9,11},{10,... | collective-permute-start | bytes 589832 | tf_op jit(solution)/shard_map/ppermute | solution.py:36
  24.4 1.2 %copy-start.11 = (bf16[512,1024]{1,0:T(8,128)(2,1)S(1)}, bf16[512,1024]{1,0:T(8,128)(2,1)}, u32[]{:S(2)}) copy-start(bf16[512,1024]{1,0:T(8,128)(2,1)} %get-tuple-element.28.mine_ref) | copy-start | bytes 3145732
  26.0 3.3 %copy-start = (bf16[544,1152]{1,0:T(8,128)(2,1)}, bf16[544,1152]{1,0:T(8,128)(2,1)S(1)}, u32[]{:S(2)}) copy-start(bf16[544,1152]{1,0:T(8,128)(2,1)S(1)} %far.1.after_ref.far_ref) | copy-start | bytes 3760132
  26.0 9.8 %copy-start.14 = (s32[256]{0:T(256)S(1)}, s32[256]{0:T(256)}, u32[]{:S(2)}) copy-start(s32[256]{0:T(256)} %param.15) | copy-start | bytes 3076
  26.0 46.2 %collective-permute-start.4 = (bf16[544,1152]{1,0:T(8,128)(2,1)S(1)}, bf16[544,1152]{1,0:T(8,128)(2,1)S(1)}, u32[]{:S(2)}, u32[]{:S(2)}) collective-permute-start(bf16[544,1152]{1,0:T(8,128)(2,1)S(1)} %far.1.after_ref.far_ref), channel_id=1, source_target_pairs={{0,2},{1,3},{2,0},{3,1},{4,6},{5,7},{6,4},{7,5},{8,10},{9,11},{10,... | collective-permute-start | bytes 3760136 | tf_op jit(solution)/shard_map/ppermute | solution.py:36
  27.8 7.9 %collective-permute-start.5 = (bf16[4,2,128,128]{3,2,1,0:T(8,128)(2,1)S(1)}, bf16[4,2,128,128]{3,2,1,0:T(8,128)(2,1)S(1)}, u32[]{:S(2)}, u32[]{:S(2)}) collective-permute-start(bf16[4,2,128,128]{3,2,1,0:T(8,128)(2,1)S(1)} %get-tuple-element.30.after_ref), channel_id=1, source_target_pairs={{0,16},{16,0},{1,17},{17,1},{2,18},{18,2},{3,19},{19,3},{4,20},{20... | collective-permute-start | bytes 786440 | tf_op jit(solution)/shard_map/ppermute | solution.py:36
  29.3 35.8 %copy-start.13 = (s32[3]{0:T(128)S(1)}, s32[3]{0:T(128)}, u32[]{:S(2)}) copy-start(s32[3]{0:T(128)} %pad_add_fusion.at) | copy-start | bytes 40
  35.6 29.5 %copy-start.2 = (bf16[512,1024]{1,0:T(8,128)(2,1)S(1)}, bf16[512,1024]{1,0:T(8,128)(2,1)}, u32[]{:S(2)}) copy-start(bf16[512,1024]{1,0:T(8,128)(2,1)} %get-tuple-element.26.hg_ref) | copy-start | bytes 3145732
  35.7 36.6 %collective-permute-start.3 = (bf16[512,1024]{1,0:T(8,128)(2,1)}, bf16[512,1024]{1,0:T(8,128)(2,1)S(1)}, u32[]{:S(2)}, u32[]{:S(2)}) collective-permute-start(bf16[512,1024]{1,0:T(8,128)(2,1)} %get-tuple-element.32), channel_id=1, source_target_pairs={{0,1},{1,0},{2,3},{3,2},{4,5},{5,4},{6,7},{7,6},{8,9},{9,8},{10,11... | collective-permute-start | bytes 3145736 | tf_op jit(solution)/shard_map/ppermute | solution.py:36
  35.8 1.3 %copy-start.4 = (bf16[512,1024]{1,0:T(8,128)(2,1)S(1)}, bf16[512,1024]{1,0:T(8,128)(2,1)}, u32[]{:S(2)}) copy-start(bf16[512,1024]{1,0:T(8,128)(2,1)} %get-tuple-element.31.rest_2_.mine_ref) | copy-start | bytes 3145732
  37.1 4.5 %collective-permute-start.6 = (bf16[2,128,128]{2,1,0:T(8,128)(2,1)S(1)}, bf16[2,128,128]{2,1,0:T(8,128)(2,1)S(1)}, u32[]{:S(2)}, u32[]{:S(2)}) collective-permute-start(bf16[2,128,128]{2,1,0:T(8,128)(2,1)S(1)} %get-tuple-element.35), channel_id=1, source_target_pairs={{0,4},{4,0},{8,12},{12,8},{1,5},{5,1},{9,13},{13,9},{2,6},{6,2},{1... | collective-permute-start | bytes 196616 | tf_op jit(solution)/shard_map/ppermute | solution.py:36
  38.7 7.7 %collective-permute-start.7 = (bf16[2,128,128]{2,1,0:T(8,128)(2,1)S(1)}, bf16[2,128,128]{2,1,0:T(8,128)(2,1)S(1)}, u32[]{:S(2)}, u32[]{:S(2)}) collective-permute-start(bf16[2,128,128]{2,1,0:T(8,128)(2,1)S(1)} %get-tuple-element.36), channel_id=1, source_target_pairs={{0,8},{4,12},{8,0},{12,4},{1,9},{5,13},{9,1},{13,5},{2,10},{6,14},... | collective-permute-start | bytes 196616 | tf_op jit(solution)/shard_map/ppermute | solution.py:36
  41.3 6.1 %collective-permute-start.8 = (bf16[2,128,128]{2,1,0:T(8,128)(2,1)S(1)}, bf16[2,128,128]{2,1,0:T(8,128)(2,1)S(1)}, u32[]{:S(2)}, u32[]{:S(2)}) collective-permute-start(bf16[2,128,128]{2,1,0:T(8,128)(2,1)S(1)} %get-tuple-element.37), channel_id=1, source_target_pairs={{0,12},{4,8},{8,4},{12,0},{1,13},{5,9},{9,5},{13,1},{2,14},{6,10},... | collective-permute-start | bytes 196616 | tf_op jit(solution)/shard_map/ppermute | solution.py:36
  47.6 4.1 %collective-permute-start.9 = (bf16[160,128]{1,0:T(8,128)(2,1)S(1)}, bf16[160,128]{1,0:T(8,128)(2,1)S(1)}, u32[]{:S(2)}, u32[]{:S(2)}) collective-permute-start(bf16[160,128]{1,0:T(8,128)(2,1)S(1)} %get-tuple-element.38.rest_0_), channel_id=1, source_target_pairs={{0,4},{4,0},{8,12},{12,8},{1,5},{5,1},{9,13},{13,9},{2,6},{6,2},{1... | collective-permute-start | bytes 122888 | tf_op jit(solution)/shard_map/ppermute | solution.py:36
  48.9 5.8 %collective-permute-start.11 = (bf16[160,128]{1,0:T(8,128)(2,1)S(1)}, bf16[160,128]{1,0:T(8,128)(2,1)S(1)}, u32[]{:S(2)}, u32[]{:S(2)}) collective-permute-start(bf16[160,128]{1,0:T(8,128)(2,1)S(1)} %get-tuple-element.38.rest_0_), channel_id=1, source_target_pairs={{0,12},{4,8},{8,4},{12,0},{1,13},{5,9},{9,5},{13,1},{2,14},{6,10},... | collective-permute-start | bytes 122888 | tf_op jit(solution)/shard_map/ppermute | solution.py:36
  51.3 4.9 %collective-permute-start.10 = (bf16[160,128]{1,0:T(8,128)(2,1)S(1)}, bf16[160,128]{1,0:T(8,128)(2,1)S(1)}, u32[]{:S(2)}, u32[]{:S(2)}) collective-permute-start(bf16[160,128]{1,0:T(8,128)(2,1)S(1)} %get-tuple-element.38.rest_0_), channel_id=1, source_target_pairs={{0,8},{4,12},{8,0},{12,4},{1,9},{5,13},{9,1},{13,5},{2,10},{6,14},... | collective-permute-start | bytes 122888 | tf_op jit(solution)/shard_map/ppermute | solution.py:36
  51.7 4.5 %collective-permute-start.12 = (bf16[160,128]{1,0:T(8,128)(2,1)S(1)}, bf16[160,128]{1,0:T(8,128)(2,1)S(1)}, u32[]{:S(2)}, u32[]{:S(2)}) collective-permute-start(bf16[160,128]{1,0:T(8,128)(2,1)S(1)} %get-tuple-element.38.rest_0_), channel_id=1, source_target_pairs={{0,16},{16,0},{1,17},{17,1},{2,18},{18,2},{3,19},{19,3},{4,20},{20... | collective-permute-start | bytes 122888 | tf_op jit(solution)/shard_map/ppermute | solution.py:36
  54.7 4.0 %collective-permute-start.13 = (bf16[160,128]{1,0:T(8,128)(2,1)S(1)}, bf16[160,128]{1,0:T(8,128)(2,1)S(1)}, u32[]{:S(2)}, u32[]{:S(2)}) collective-permute-start(bf16[160,128]{1,0:T(8,128)(2,1)S(1)} %collective-permute-done.9.rest_1_), channel_id=1, source_target_pairs={{0,16},{16,0},{1,17},{17,1},{2,18},{18,2},{3,19},{19,3},{4,20},{20... | collective-permute-start | bytes 122888 | tf_op jit(solution)/shard_map/ppermute | solution.py:36
  56.2 10.0 %collective-permute-start.18 = (bf16[128,128]{1,0:T(8,128)(2,1)S(1)}, bf16[128,128]{1,0:T(8,128)(2,1)S(1)}, u32[]{:S(2)}, u32[]{:S(2)}) collective-permute-start(bf16[128,128]{1,0:T(8,128)(2,1)S(1)} %hold.1.refs_0_), channel_id=1, source_target_pairs={{0,4},{4,0},{8,12},{12,8},{1,5},{5,1},{9,13},{13,9},{2,6},{6,2},{1... | collective-permute-start | bytes 98312 | tf_op jit(solution)/shard_map/ppermute | solution.py:36
  56.2 7.7 %collective-permute-start.15 = (bf16[160,128]{1,0:T(8,128)(2,1)S(1)}, bf16[160,128]{1,0:T(8,128)(2,1)S(1)}, u32[]{:S(2)}, u32[]{:S(2)}) collective-permute-start(bf16[160,128]{1,0:T(8,128)(2,1)S(1)} %collective-permute-done.11.rest_3_.after_ref), channel_id=1, source_target_pairs={{0,16},{16,0},{1,17},{17,1},{2,18},{18,2},{3,19},{19,3},{4,20},{20... | collective-permute-start | bytes 122888 | tf_op jit(solution)/shard_map/ppermute | solution.py:36
  58.7 4.0 %collective-permute-start.14 = (bf16[160,128]{1,0:T(8,128)(2,1)S(1)}, bf16[160,128]{1,0:T(8,128)(2,1)S(1)}, u32[]{:S(2)}, u32[]{:S(2)}) collective-permute-start(bf16[160,128]{1,0:T(8,128)(2,1)S(1)} %collective-permute-done.10.rest_2_), channel_id=1, source_target_pairs={{0,16},{16,0},{1,17},{17,1},{2,18},{18,2},{3,19},{19,3},{4,20},{20... | collective-permute-start | bytes 122888 | tf_op jit(solution)/shard_map/ppermute | solution.py:36
  62.7 4.8 %collective-permute-start.19 = (bf16[128,128]{1,0:T(8,128)(2,1)S(1)}, bf16[128,128]{1,0:T(8,128)(2,1)S(1)}, u32[]{:S(2)}, u32[]{:S(2)}) collective-permute-start(bf16[128,128]{1,0:T(8,128)(2,1)S(1)} %hold.1.refs_0_), channel_id=1, source_target_pairs={{0,8},{4,12},{8,0},{12,4},{1,9},{5,13},{9,1},{13,5},{2,10},{6,14},... | collective-permute-start | bytes 98312 | tf_op jit(solution)/shard_map/ppermute | solution.py:36
  63.9 5.7 %collective-permute-start.20 = (bf16[128,128]{1,0:T(8,128)(2,1)S(1)}, bf16[128,128]{1,0:T(8,128)(2,1)S(1)}, u32[]{:S(2)}, u32[]{:S(2)}) collective-permute-start(bf16[128,128]{1,0:T(8,128)(2,1)S(1)} %hold.1.refs_0_), channel_id=1, source_target_pairs={{0,12},{4,8},{8,4},{12,0},{1,13},{5,9},{9,5},{13,1},{2,14},{6,10},... | collective-permute-start | bytes 98312 | tf_op jit(solution)/shard_map/ppermute | solution.py:36
  66.2 4.2 %collective-permute-start.16 = (bf16[544,128]{1,0:T(8,128)(2,1)S(1)}, bf16[544,128]{1,0:T(8,128)(2,1)S(1)}, u32[]{:S(2)}, u32[]{:S(2)}) collective-permute-start(bf16[544,128]{1,0:T(8,128)(2,1)S(1)} %get-tuple-element.39.after_ref.a_ref), channel_id=1, source_target_pairs={{0,1},{1,0},{2,3},{3,2},{4,5},{5,4},{6,7},{7,6},{8,9},{9,8},{10,11... | collective-permute-start | bytes 417800 | tf_op jit(solution)/shard_map/ppermute | solution.py:36
  69.7 2.6 %copy-start.1 = (bf16[544,1152]{1,0:T(8,128)(2,1)S(1)}, bf16[544,1152]{1,0:T(8,128)(2,1)}, u32[]{:S(2)}) copy-start(bf16[544,1152]{1,0:T(8,128)(2,1)} %copy-done) | copy-start | bytes 3760132
  69.7 2.6 %copy-start.5 = (bf16[512,1024]{1,0:T(8,128)(2,1)S(1)}, bf16[512,1024]{1,0:T(8,128)(2,1)}, u32[]{:S(2)}) copy-start(bf16[512,1024]{1,0:T(8,128)(2,1)} %get-tuple-element.31.rest_2_.mine_ref) | copy-start | bytes 3145732
  69.7 5.0 %collective-permute-start.21 = (bf16[4,128,128]{2,1,0:T(8,128)(2,1)S(1)}, bf16[4,128,128]{2,1,0:T(8,128)(2,1)S(1)}, u32[]{:S(2)}, u32[]{:S(2)}) collective-permute-start(bf16[4,128,128]{2,1,0:T(8,128)(2,1)S(1)} %stack.17.rest_0_), channel_id=1, source_target_pairs={{0,16},{16,0},{1,17},{17,1},{2,18},{18,2},{3,19},{19,3},{4,20},{20... | collective-permute-start | bytes 393224 | tf_op jit(solution)/shard_map/ppermute | solution.py:36
  70.4 5.1 %collective-permute-start.17 = (bf16[544,128]{1,0:T(8,128)(2,1)S(1)}, bf16[544,128]{1,0:T(8,128)(2,1)S(1)}, u32[]{:S(2)}, u32[]{:S(2)}) collective-permute-start(bf16[544,128]{1,0:T(8,128)(2,1)S(1)} %merge.1.s_ref), channel_id=1, source_target_pairs={{0,2},{1,3},{2,0},{3,1},{4,6},{5,7},{6,4},{7,5},{8,10},{9,11},{10,... | collective-permute-start | bytes 417800 | tf_op jit(solution)/shard_map/ppermute | solution.py:36
  72.2 3.3 %copy-start.3 = (f32[1024,128]{1,0:T(8,128)S(1)}, f32[1024,128]{1,0:T(8,128)}, u32[]{:S(2)}) copy-start(f32[1024,128]{1,0:T(8,128)} %a_ref.1) | copy-start | bytes 1572868
  72.2 3.3 %copy-start.8 = (f32[128,1024]{1,0:T(8,128)S(1)}, f32[128,1024]{1,0:T(8,128)}, u32[]{:S(2)}) copy-start(f32[128,1024]{1,0:T(8,128)} %b_ref.1) | copy-start | bytes 1572868

commit v4 on v3

v4 whole, which is shorter than its diff:
```python
import functools

import jax
import jax.numpy as jnp
from jax import lax
from jax.experimental import pallas as pl
from jax.experimental.pallas import tpu as pltpu
from jax.sharding import PartitionSpec as P

D = 4096
HEAD = 128
SCALE = 2.0
LEARN = 3.0
EPS = 1e-05
NORM_EPS = 1e-06
LANES = 128
EXTRA = 32

BF = jnp.bfloat16
F32 = jnp.float32
VMEM = pl.BlockSpec(memory_space=pltpu.VMEM)
SMEM = pl.BlockSpec(memory_space=pltpu.SMEM)
ANY = pl.BlockSpec(memory_space=pl.ANY)
HBM = pl.BlockSpec(memory_space=pltpu.HBM)


def shape(dims, dtype):
    return jax.ShapeDtypeStruct(dims, dtype)


def dot(a, b, dims=((1,), (0,))):
    return lax.dot_general(a, b, (dims, ((), ())), preferred_element_type=F32)


def swap(x, axis, n, k):
    return lax.ppermute(x, axis, [(i, i ^ k) for i in range(n)])


def split_terms(values):
    high = values.astype(BF)
    rest = values - high.astype(F32)
    middle = rest.astype(BF)
    last = (rest - middle.astype(F32)).astype(BF)
    return jnp.concatenate([high, middle, last, jnp.zeros_like(last)], axis=0)


def join_terms(terms):
    x = terms.astype(F32)
    return (x[0:8] + x[8:16]) + x[16:24]


def fetch(sources, targets, sems):
    copies = [pltpu.make_async_copy(s, t, sems.at[i]) for i, (s, t) in enumerate(zip(sources, targets))]
    for copy in copies:
        copy.start()
    return copies


def blocks_of(count):
    return [slice(i, i + LANES) for i in range(0, count, LANES)]


def rank_kernel(x_hbm, v_hbm, a_hbm, b_hbm, out_ref, x_ref, v_ref, a_ref, b_ref, sems):
    copies = fetch((x_hbm, a_hbm, v_hbm, b_hbm), (x_ref, a_ref, v_ref, b_ref), sems)
    count = x_ref.shape[0]
    copies[0].wait()
    copies[1].wait()
    out_ref[:count] = dot(x_ref[...], a_ref[...].astype(BF)).astype(BF)
    copies[2].wait()
    copies[3].wait()
    out_ref[count:] = dot(v_ref[...], b_ref[...].astype(BF), ((1,), (1,))).astype(BF)


def weight_blocks(at, peers, w_hbm, w_ref):
    _, width, cut = w_ref.shape
    sources = []
    for peer in peers:
        for i in range(width // cut):
            start = (at[0] ^ peer) * width + i * cut
            sources.append(w_hbm.at[:, pl.ds(pl.multiple_of(start, cut), cut)])
    return sources, [w_ref.at[i] for i in range(len(sources))]


def prep_kernel(at, h_hbm, gain_hbm, a_hbm, w_hbm, after_ref, hg_ref, wide_ref, h_ref, gain_ref, a_ref, w_ref, sems):
    count, width = h_ref.shape
    blocks = blocks_of(count)
    sources, targets = weight_blocks(at, (3,), w_hbm, w_ref)
    copies = fetch(
        [gain_hbm] + [h_hbm.at[b] for b in blocks] + [a_hbm] + sources,
        [gain_ref] + [h_ref.at[b] for b in blocks] + [a_ref] + targets,
        sems,
    )
    copies[0].wait()
    rows = []
    for i, b in enumerate(blocks):
        copies[1 + i].wait()
        wide = h_ref[b].astype(F32)
        hg_ref[b] = (wide * gain_ref[...]).astype(BF)
        sums = jnp.sum(wide * wide, axis=-1, keepdims=True)
        rows.append(jnp.broadcast_to(sums, (LANES, LANES)).T[0:1])
    if len(rows) < 8:
        rows.append(jnp.zeros((8 - len(rows), LANES), F32))
    wide_ref[count:, width:] = split_terms(jnp.concatenate(rows, axis=0))
    wide_ref[count:, :width] = jnp.zeros((EXTRA, width), BF)
    copies[1 + len(blocks)].wait()
    wide_ref[:count, width:] = dot(hg_ref[...], a_ref[...].astype(BF)).astype(BF)
    cut = w_ref.shape[2]
    for i in range(width // cut):
        copies[2 + len(blocks) + i].wait()
        wide_ref[:count, i * cut : (i + 1) * cut] = dot(hg_ref[...], w_ref[i]).astype(BF)


def query_kernel(peers, at, hg_ref, w_hbm, pos_ref, after_ref, *rest):
    outs, (pos_out, w_ref, sems) = rest[:-3], rest[-3:]
    _, width, cut = w_ref.shape
    copies = fetch(*weight_blocks(at, peers, w_hbm, w_ref), sems)
    pos_out[...] = pos_ref[...].astype(F32)
    per = width // cut
    for i, copy in enumerate(copies):
        copy.wait()
        outs[i // per][:, i % per * cut : (i % per + 1) * cut] = dot(hg_ref[...], w_ref[i]).astype(BF)


def far_kernel(mine_ref, diag_ref, got_ref, pass_ref, out_ref, pass_out):
    count, width = mine_ref.shape
    out_ref[:count, :width] = (mine_ref[...].astype(F32) + got_ref[:count, :width].astype(F32)).astype(BF)
    out_ref[count:, :width] = jnp.zeros((EXTRA, width), BF)
    out_ref[:count, width:] = (diag_ref[:count, width:].astype(F32) + got_ref[:count, width:].astype(F32)).astype(BF)
    out_ref[count:, width:] = split_terms(join_terms(diag_ref[count:, width:]) + join_terms(got_ref[count:, width:]))


def merge_kernel(a_ref, b_ref, out_ref):
    count = a_ref.shape[0] - EXTRA
    out_ref[:count] = (a_ref[:count].astype(F32) + b_ref[:count].astype(F32)).astype(BF)
    out_ref[count:] = split_terms(join_terms(a_ref[count:]) + join_terms(b_ref[count:]))


def grad_kernel(x_ref, v_ref, s_ref, r_ref, out_ref):
    count, width = x_ref.shape
    parts, _, size, _ = out_ref.shape
    low = (s_ref[...].astype(F32) + r_ref[...].astype(F32)).astype(BF)
    ga = SCALE * dot(x_ref[...], low[count:], ((0,), (0,)))
    gb = SCALE * dot(low[:count], v_ref[...], ((0,), (0,)))
    per = LANES // size
    for i in range(parts):
        out_ref[i, 0] = ga[i * size : (i + 1) * size].astype(BF)
        col, row = i // per * LANES, i % per * size
        out_ref[i, 1] = gb[row : row + size, col : col + LANES].astype(BF)


def chunk_kernel(x_ref, a_ref, b_ref):
    parts, _, size, _ = x_ref.shape
    total = x_ref[0].astype(F32)
    for i in range(1, parts):
        total = total + x_ref[i].astype(F32)
    squares = total[0] * total[0] + total[1] * total[1]
    terms = split_terms(jnp.broadcast_to(jnp.sum(squares), (8, LANES)))
    half = total.astype(BF)
    for i in range(parts):
        a_ref[i, :size] = half[0]
        a_ref[i, size:] = terms
        b_ref[i] = half[1]


def hold_kernel(x_ref, after_ref, out_ref):
    out_ref[...] = x_ref[...]


def low_kernel(hg_ref, x_ref, pack_ref, ga_ref):
    parts, size, _ = x_ref.shape
    size -= EXTRA
    total = join_terms(x_ref[0, size:])
    for i in range(parts):
        ga_ref[i * size : (i + 1) * size] = x_ref[i, :size]
        if i:
            total = total + join_terms(x_ref[i, size:])
    count = hg_ref.shape[0]
    pack_ref[:count] = dot(hg_ref[...], ga_ref[...]).astype(BF)
    pack_ref[count:] = split_terms(total)


def base_kernel(mine_ref, near_ref, far_ref, far_got, after_ref, base_ref, low_ref, scale_ref):
    count, width = mine_ref.shape
    sums = join_terms(far_ref[count:, width:]) + join_terms(far_got[count:, width:])
    scale = lax.rsqrt(sums / D + EPS)
    for i, b in enumerate(blocks_of(count)):
        block = jnp.broadcast_to(scale[i : i + 1], (LANES, LANES)).T
        scale_ref[b] = block
        low_ref[b] = (far_ref[b, width:].astype(F32) + far_got[b, width:].astype(F32)) * block
        for c in blocks_of(width):
            total = mine_ref[b, c].astype(F32) + near_ref[b, c].astype(F32) + far_got[b, c].astype(F32)
            base_ref[b, c] = total * block


def final_kernel(
    base_ref, low_ref, scale_ref, s_ref, r_ref, ga_ref, gb_ref, a_ref, b_ref, cos_ref, sin_ref,
    a_hbm, b_hbm, q_hbm, new_a, new_b, half_b, out, sems,
):
    count, width = base_ref.shape
    total = join_terms(s_ref[count:]) + join_terms(r_ref[count:])
    rate = (LEARN * lax.rsqrt(total + NORM_EPS))[0:1]
    for c in blocks_of(width):
        fresh = b_ref[:, c] - rate * gb_ref[c].astype(F32)
        new_b[:, c] = fresh
        half_b[:, c] = fresh.astype(BF)
    copies = [pltpu.make_async_copy(new_b, b_hbm, sems.at[0])]
    copies[-1].start()
    new_a[...] = a_ref[...] - rate * ga_ref[...].astype(F32)
    copies.append(pltpu.make_async_copy(new_a, a_hbm, sems.at[1]))
    copies[-1].start()
    for i, b in enumerate(blocks_of(count)):
        low = s_ref[b].astype(F32) + r_ref[b].astype(F32)
        mix = (low_ref[b] - rate * (low * scale_ref[b])) * SCALE
        update = dot(mix.astype(BF), half_b[...])
        cos, sin = cos_ref[b], sin_ref[b]
        for c in blocks_of(width):
            query = base_ref[b, c] + update[:, c]
            other = pltpu.roll(query, HEAD // 2, 1)
            out[b, c] = (query * cos + other * sin).astype(BF)
        copies.append(pltpu.make_async_copy(out.at[b], q_hbm.at[b], sems.at[2 + i]))
        copies[-1].start()
    for copy in copies:
        copy.wait()


def keep_hbm(x):
    return pltpu.with_memory_space_constraint(x, pltpu.HBM)


def call(kernel, outs, in_specs, args, name, scratch=(), out_specs=None, limit=32, aliases=None):
    return pl.pallas_call(
        kernel,
        out_shape=outs,
        in_specs=in_specs,
        out_specs=out_specs if out_specs is not None else jax.tree.map(lambda _: VMEM, outs),
        scratch_shapes=list(scratch),
        compiler_params=pltpu.CompilerParams(vmem_limit_bytes=int(limit * 1024 * 1024)),
        input_output_aliases=aliases or {},
        name=name,
    )(*args)


def turn_tables(places, steps):
    half = HEAD // 2
    freq = 10000.0 ** (-jnp.arange(half, dtype=F32) / half)
    cos, sin = [], []
    for step in range(steps):
        angle = (places + float(step))[:, None] * freq[None, :]
        c, s = jnp.cos(angle), jnp.sin(angle)
        cos.append(jnp.concatenate([c, c], axis=-1))
        sin.append(jnp.concatenate([-s, s], axis=-1))
    return jnp.concatenate(cos), jnp.concatenate(sin)


def build(n_dp, n_roll, n_tp):
    n_parts = n_dp * n_roll
    spread = lambda x: lax.all_to_all(x, ("dp", "roll"), 0, 0, tiled=True)

    def on_device(
        train_inputs, train_cotangent, factor_a, factor_b, base_weight, incoming, norm_gain, positions
    ):
        steps, rows, width = incoming.shape
        tokens = train_inputs.shape[0]
        rank = factor_a.shape[1]
        count = steps * rows
        at = lax.axis_index("tp").astype(jnp.int32)[None]
        dma = lambda n: pltpu.SemaphoreType.DMA((n,))

        part = call(
            rank_kernel,
            shape((2 * tokens, rank), BF),
            [HBM] * 4,
            tuple(map(keep_hbm, (train_inputs, train_cotangent, factor_a, factor_b))),
            "rank",
            [pltpu.VMEM(train_inputs.shape, BF), pltpu.VMEM(train_inputs.shape, BF),
             pltpu.VMEM(factor_a.shape, F32), pltpu.VMEM(factor_b.shape, F32), dma(4)],
        )
        part_got = swap(part, "tp", n_tp, 1)
        cut = 512
        wide = shape((count + EXTRA, width + rank), BF)
        tall = shape((count, width), BF)
        pos = positions.reshape(-1, LANES)
        gained, diag = call(
            prep_kernel,
            [tall, wide],
            [SMEM] + [HBM] * 4 + [ANY],
            (at, *map(keep_hbm, (incoming.reshape(count, width), norm_gain[None, :], factor_a, base_weight)), part),
            "prep",
            [pltpu.VMEM((count, width), BF), pltpu.VMEM((1, width), F32), pltpu.VMEM(factor_a.shape, F32),
             pltpu.VMEM((width // cut, width, cut), BF), dma(2 + count // LANES + width // cut)],
        )
        diag_got = swap(diag, "tp", n_tp, 1)
        part_sum = (part.astype(F32) + part_got.astype(F32)).astype(BF)
        part_far = swap(part_sum, "tp", n_tp, 2)

        def query(peers, pos, after, name):
            blocks = len(peers) * width // cut
            return call(
                functools.partial(query_kernel, peers),
                [tall] * len(peers) + [shape(pos.shape, F32)],
                [SMEM, VMEM, HBM, VMEM, ANY],
                (at, gained, keep_hbm(base_weight), pos, after),
                name,
                [pltpu.VMEM((blocks, width, cut), BF), dma(blocks)],
            )

        distant, beside, places = query((2, 1), pos, part_sum, "query_first")
        beside_got = swap(beside, "tp", n_tp, 1)
        cos, sin = turn_tables(places.reshape(rows), steps)
        size = width // n_parts
        grads = call(
            grad_kernel,
            shape((n_parts, 2, size, rank), BF),
            [VMEM] * 4,
            (train_inputs, train_cotangent, part_sum, part_far),
            "grads",
        )
        far, grads = call(
            far_kernel,
            [wide, shape(grads.shape, BF)],
            [VMEM] * 3 + [ANY],
            (distant, diag, diag_got, grads),
            "far",
            out_specs=[VMEM, ANY],
            aliases={3: 1},
        )
        far_got = swap(far, "tp", n_tp, 2)
        chunk_a, chunk_b = call(
            chunk_kernel,
            [shape((n_parts, size + EXTRA, rank), BF), shape((n_parts, size, rank), BF)],
            [VMEM],
            (spread(grads),),
            "chunk",
        )
        pieces = spread(chunk_a)
        step_pack, grad_a = call(
            low_kernel,
            [shape((count + EXTRA, rank), BF), shape((width, rank), BF)],
            [VMEM] * 2,
            (gained, pieces),
            "low_rank",
        )
        step_got = swap(step_pack, "tp", n_tp, 1)
        step_sum = call(merge_kernel, shape((count + EXTRA, rank), BF), [VMEM] * 2, (step_pack, step_got), "merge")
        step_far = swap(step_sum, "tp", n_tp, 2)
        chunk_b = call(hold_kernel, shape(chunk_b.shape, BF), [VMEM, ANY], (chunk_b, step_sum), "hold")
        grad_b = spread(chunk_b).reshape(width, rank)
        close, _ = query((0,), pos, step_sum, "query_second")
        base, low, scale = call(
            base_kernel,
            [shape((count, width), F32), shape((count, rank), F32), shape((count, LANES), F32)],
            [VMEM] * 4 + [ANY],
            (close, beside_got, far, far_got, step_pack),
            "base",
        )
        new_a, new_b, queries = call(
            final_kernel,
            [shape((width, rank), F32), shape((rank, width), F32), tall],
            [VMEM] * 11,
            (base, low, scale, step_sum, step_far, grad_a, grad_b, factor_a, factor_b, cos, sin),
            "final",
            [pltpu.VMEM((width, rank), F32), pltpu.VMEM((rank, width), F32),
             pltpu.VMEM((rank, width), BF), pltpu.VMEM((count, width), BF), dma(2 + count // LANES)],
            [HBM] * 3,
        )
        return new_a, new_b, queries.reshape(steps, rows, width)

    return on_device


def solution(mesh):
    n_dp, n_roll, n_tp = (mesh.shape[a] for a in ("dp", "roll", "tp"))
    return jax.shard_map(
        build(n_dp, n_roll, n_tp),
        mesh=mesh,
        in_specs=(
            P(("dp", "roll"), "tp"),
            P(("dp", "roll"), "tp"),
            P("tp", None),
            P(None, "tp"),
            P("tp", None),
            P(None, ("dp", "roll"), "tp"),
            P("tp"),
            P(("dp", "roll")),
        ),
        out_specs=(P("tp", None), P(None, "tp"), P(None, ("dp", "roll"), "tp")),
        check_vma=False,
    )
```

time: 78.2 us -> 86.5 us (1.11)
  blocking collectives: 0 us -> 21 us
  starting transfers between devices: 21.2 us -> 12.7 us
  waiting for transfers between devices: 26.2 us -> 19.3 us
  local copies, waits for them, and re-layouts: 2.57 us -> 9.09 us
  Pallas kernels: 24.4 us -> 21 us
    all_to_all x0 -> x1, blocking collectives: none -> 21 us  [build(): spread = lambda x: lax.all_to_all(x, ('dp', 'roll'), 0, 0, tiled=True)]
    ppermute x22 -> x7, starting transfers between devices: 21.2 us -> 5.27 us  [swap(): return lax.ppermute(x, axis, [(i, i ^ k) for i in range(n)])]
    ppermute x22 -> x7, waiting for transfers between devices: 26.2 us -> 10.5 us  [swap(): return lax.ppermute(x, axis, [(i, i ^ k) for i in range(n)])]
    all_to_all x0 -> x2, waiting for transfers between devices: none -> 8.77 us  [build(): spread = lambda x: lax.all_to_all(x, ('dp', 'roll'), 0, 0, tiled=True)]
    all_to_all x0 -> x2, starting transfers between devices: none -> 7.47 us  [build(): spread = lambda x: lax.all_to_all(x, ('dp', 'roll'), 0, 0, tiled=True)]
    unnamed x32 -> x38, local copies, waits for them, and re-layouts: 2.57 us -> 9.09 us
    pallas_call x14 -> x12, Pallas kernels: 24.4 us -> 21 us  [call(): pl.pallas_call(kernel, out_shape=outs, in_specs=in_specs, out_specs=out_s...]
  transfers between devices with their start and end apart: 22 -> 9, of which waited for: 12 -> 4; matrix products, arithmetic and copies ran while one was open for 2% -> 2% of each run, Pallas kernels for 16% -> 13%
where the time goes in v4:
time: 86.5 us; the launch traced here: 86 us
  Pallas kernels  21 us (24%)
  blocking collectives  21 us (24%)
  waiting for transfers between devices  19.3 us (22%)
  starting transfers between devices  12.7 us (15%)
  local copies, waits for them, and re-layouts  9.09 us (11%)
  other arithmetic  1.95 us (2%)
    pallas_call x12, Pallas kernels, call(): pl.pallas_call(kernel, out_shape=outs, in_specs=in_specs, out_specs=out_s...  21 us
    all_to_all x1, blocking collectives, build(): spread = lambda x: lax.all_to_all(x, ('dp', 'roll'), 0, 0, tiled=True)  21 us
    ppermute x7, waiting for transfers between devices, swap(): return lax.ppermute(x, axis, [(i, i ^ k) for i in range(n)])  10.5 us
    unnamed x38, local copies, waits for them, and re-layouts  9.09 us
    all_to_all x2, waiting for transfers between devices, build(): spread = lambda x: lax.all_to_all(x, ('dp', 'roll'), 0, 0, tiled=True)  8.77 us
    all_to_all x2, starting transfers between devices, build(): spread = lambda x: lax.all_to_all(x, ('dp', 'roll'), 0, 0, tiled=True)  7.47 us
    ppermute x7, starting transfers between devices, swap(): return lax.ppermute(x, axis, [(i, i ^ k) for i in range(n)])  5.27 us
  transfers between devices with their start and end apart: 9, of which 4 were waited for; matrix products, arithmetic and copies ran while one was open for 2% of the time, Pallas kernels for 13%

profile of v4, /device:TPU:0, one launch (start us, length us, event | category | flops | bytes accessed | tf_op | source)
XLA Modules:
  0.0 86.0 jit_solution(15065871526668197471)
XLA Ops:
  0.6 2.4 %rank.1.after_ref = bf16[768,128]{1,0:T(8,128)(2,1)S(1)} custom-call(bf16[384,1024]{1,0:T(8,128)(2,1)} %x_ref.1, bf16[384,1024]{1,0:T(8,128)(2,1)} %v_ref.1, f32[1024,128]{1,0:T(8,128)} %a_ref.1, f32[128,1024]{1,0:T(8,128)} %b_ref.1), custom_call_target="tpu_custom_call" | custom-call | tf_op jit(solution)/shard_map/rank/pallas_call | solution.py:231
  3.1 0.0 copy-start.17
  3.1 3.7 %prep.1 = (bf16[512,1024]{1,0:T(8,128)(2,1)S(1)}, bf16[544,1152]{1,0:T(8,128)(2,1)S(1)}) custom-call(s32[1]{0:T(128)} %bitcast.at, bf16[512,1024]{1,0:T(8,128)(2,1)} %bitcast.11, f32[1,1024]{1,0:T(1,128)} %bitcast.12, f32[1024,128]{1,0:T(8,128)} %a_ref.1, bf16[1024,4096]{1,0:T(8,128)(2,1)} %w_hbm.5, bf16[768,128]{1,0:T(8,128)(2,1)S(1)} %rank.1.after_ref), custom_call_target="tpu_custom_call" | custom-call | tf_op jit(solution)/shard_map/prep/pallas_call | solution.py:231
  6.8 0.5 collective-permute-start.1
  7.3 0.1 collective-permute-start
  7.4 2.8 %collective-permute-done = bf16[768,128]{1,0:T(8,128)(2,1)S(1)} collective-permute-done((bf16[768,128]{1,0:T(8,128)(2,1)S(1)}, bf16[768,128]{1,0:T(8,128)(2,1)S(1)}, u32[]{:S(2)}, u32[]{:S(2)}) %collective-permute-start) | collective-permute-done | bytes 196640 | tf_op jit(solution)/shard_map/ppermute | solution.py:36
  10.1 0.1 add_convert_fusion.after_ref.s_ref
  10.2 3.0 %collective-permute-start.2 = (bf16[768,128]{1,0:T(8,128)(2,1)S(1)}, bf16[768,128]{1,0:T(8,128)(2,1)S(1)}, u32[]{:S(2)}, u32[]{:S(2)}) collective-permute-start(bf16[768,128]{1,0:T(8,128)(2,1)S(1)} %add_convert_fusion.after_ref.s_ref), channel_id=1, source_target_pairs={{0,2},{1,3},{2,0},{3,1},{4,6},{5,7},{6,4},{7,5},{8,10},{9,11},{10,... | collective-permute-start | bytes 589832 | tf_op jit(solution)/shard_map/ppermute | solution.py:36
  13.2 4.2 %query_first.1 = (bf16[512,1024]{1,0:T(8,128)(2,1)S(1)}, bf16[512,1024]{1,0:T(8,128)(2,1)S(1)}, f32[2,128]{1,0:T(2,128)S(1)}) custom-call(s32[1]{0:T(128)} %bitcast.at, bf16[512,1024]{1,0:T(8,128)(2,1)S(1)} %get-tuple-element.21.hg_ref, bf16[1024,4096]{1,0:T(8,128)(2,1)} %w_hbm.5, s32[2,128]{1,0:T(2,128)S(1)} %bitcast.8, ...), custom_call_target="tpu_custom_call" | custom-call | tf_op jit(solution)/shard_map/query_first/pallas_call | solution.py:231
  17.4 0.0 copy-start.18
  17.4 1.0 %copy-done.18 = bf16[512,1024]{1,0:T(8,128)(2,1)} copy-done((bf16[512,1024]{1,0:T(8,128)(2,1)}, bf16[512,1024]{1,0:T(8,128)(2,1)S(1)}, u32[]{:S(2)}) %copy-start.18) | copy-done | bytes 1048600
  18.4 0.0 collective-permute-done.2.r_ref
  18.4 0.5 grads.1.pass_ref
  18.9 0.0 collective-permute-done.1.got_ref
  18.9 0.3 far.1
  19.3 21.0 %all_to_all.15.x_ref = bf16[8,2,128,128]{3,2,1,0:T(8,128)(2,1)S(1)} all-to-all(bf16[8,2,128,128]{3,2,1,0:T(8,128)(2,1)S(1)} %get-tuple-element.24), channel_id=1, replica_groups=mesh['dp'=2,'roll'=4,'tp'=4] {'dp','roll'}, dimensions={0} | all-to-all | bytes 1048576 | tf_op jit(solution)/shard_map/all_to_all | solution.py:257
  40.3 0.9 %chunk.1 = (bf16[8,160,128]{2,1,0:T(8,128)(2,1)}, bf16[8,128,128]{2,1,0:T(8,128)(2,1)S(1)}) custom-call(bf16[8,2,128,128]{3,2,1,0:T(8,128)(2,1)S(1)} %all_to_all.15.x_ref), custom_call_target="tpu_custom_call" | custom-call | tf_op jit(solution)/shard_map/chunk/pallas_call | solution.py:231
  41.2 3.4 %all-to-all-start.1 = ((bf16[8,160,128]{2,1,0:T(8,128)(2,1)}), bf16[8,160,128]{2,1,0:T(8,128)(2,1)S(1)}, u32[]{:S(2)}, u32[]{:S(2)}) async-start(bf16[8,160,128]{2,1,0:T(8,128)(2,1)} %get-tuple-element.25), calls=%async_computation.1 | async-start | bytes 655360 | tf_op jit(solution)/shard_map/all_to_all | solution.py:257
  44.7 1.2 %collective-permute-start.5 = (bf16[544,1152]{1,0:T(8,128)(2,1)S(1)}, bf16[544,1152]{1,0:T(8,128)(2,1)}, u32[]{:S(2)}, u32[]{:S(2)}) collective-permute-start(bf16[544,1152]{1,0:T(8,128)(2,1)S(1)} %get-tuple-element.29.far_ref), channel_id=1, source_target_pairs={{0,2},{1,3},{2,0},{3,1},{4,6},{5,7},{6,4},{7,5},{8,10},{9,11},{10,... | collective-permute-start | bytes 3760136 | tf_op jit(solution)/shard_map/ppermute | solution.py:36
  45.9 0.0 collective-permute-start.4
  45.9 8.8 %all-to-all-done.1.x_ref = bf16[8,160,128]{2,1,0:T(8,128)(2,1)S(1)} async-done(((bf16[8,160,128]{2,1,0:T(8,128)(2,1)}), bf16[8,160,128]{2,1,0:T(8,128)(2,1)S(1)}, u32[]{:S(2)}, u32[]{:S(2)}) %all-to-all-start.1) | async-done | bytes 327712 | tf_op jit(solution)/shard_map/all_to_all | solution.py:257
  54.7 0.5 low_rank.1
  55.2 0.7 copy-done.9
  55.9 0.0 collective-permute-start.3
  55.9 1.3 %collective-permute-done.3.b_ref = bf16[544,128]{1,0:T(8,128)(2,1)S(1)} collective-permute-done((bf16[544,128]{1,0:T(8,128)(2,1)S(1)}, bf16[544,128]{1,0:T(8,128)(2,1)S(1)}, u32[]{:S(2)}, u32[]{:S(2)}) %collective-permute-start.3) | collective-permute-done | bytes 139296 | tf_op jit(solution)/shard_map/ppermute | solution.py:36
  57.3 0.0 copy-start.7
  57.3 0.6 copy-done.7
  57.9 0.7 hold.1
  58.6 4.0 %all-to-all-start.2 = ((bf16[8,128,128]{2,1,0:T(8,128)(2,1)}), bf16[8,128,128]{2,1,0:T(8,128)(2,1)}, u32[]{:S(2)}, u32[]{:S(2)}) async-start(bf16[8,128,128]{2,1,0:T(8,128)(2,1)} %hold.1), calls=%async_computation.2 | async-start | bytes 524288 | tf_op jit(solution)/shard_map/all_to_all | solution.py:257
  62.7 0.5 collective-permute-start.6
  63.2 1.0 %fusion = (f32[256,64]{1,0:T(8,128)S(1)}, f32[256,64]{1,0:T(8,128)S(1)}, f32[256,64]{1,0:T(8,128)S(1)}, f32[256,64]{1,0:T(8,128)S(1)}, f32[256,64]{1,0:T(8,128)S(1)}, /*index=5*/f32[256,64]{1,0:T(8,128)S(1)}) fusion(f32[64]{0:T(128)S(1)} %multiply_power_fusion, f32[256]{0:T(256)S(1)} %bitcast.10, f32[256]{0:T(256)S(1)} %broadcast_add_fusion), kind=kLoop, calls=%fused_computation.7 | loop fusion | flops 65536 | bytes 395520 | tf_op jit(solution)/shard_map/neg | solution.py:251
  64.2 0.9 %maximum_maximum_fusion = (f32[512,128]{1,0:T(8,128)S(1)}, f32[512,128]{1,0:T(8,128)}) fusion(f32[256,64]{1,0:T(8,128)S(1)} %get-tuple-element.46, f32[256,64]{1,0:T(8,128)S(1)} %get-tuple-element.41, f32[256,64]{1,0:T(8,128)S(1)} %get-tuple-element.45, f32[256,64]{1,0:T(8,128)S(1)} %get-tuple-element.47, f32[256,64]{1,0:T(8,128)S(1)} %get-tuple-element.40, ...), kind=kLoop, calls=%fused_computation.1 | loop fusion | flops 393216 | bytes 917504 | tf_op jit(solution)/shard_map/concatenate | solution.py:252
  65.1 2.8 %query_second.1 = (bf16[512,1024]{1,0:T(8,128)(2,1)S(1)}, f32[2,128]{1,0:T(2,128)}) custom-call(s32[1]{0:T(128)} %bitcast.at, bf16[512,1024]{1,0:T(8,128)(2,1)S(1)} %get-tuple-element.21.hg_ref, bf16[1024,4096]{1,0:T(8,128)(2,1)} %w_hbm.5, s32[2,128]{1,0:T(2,128)S(1)} %bitcast.9, bf16[544,128]{1,0:T(8,128)(2,1)S(1)} %merge.1.after_ref.s_ref), custom_call_target="tpu_custom_call" | custom-call | tf_op jit(solution)/shard_map/query_second/pallas_call | solution.py:231
  67.8 0.0 collective-permute-done.4.near_ref
  67.9 6.4 %collective-permute-done.5.far_got = bf16[544,1152]{1,0:T(8,128)(2,1)} collective-permute-done((bf16[544,1152]{1,0:T(8,128)(2,1)S(1)}, bf16[544,1152]{1,0:T(8,128)(2,1)}, u32[]{:S(2)}, u32[]{:S(2)}) %collective-permute-start.5) | collective-permute-done | bytes 1253408 | tf_op jit(solution)/shard_map/ppermute | solution.py:36
  74.2 2.2 %base.1 = (f32[512,1024]{1,0:T(8,128)S(1)}, f32[512,128]{1,0:T(8,128)S(1)}, f32[512,128]{1,0:T(8,128)S(1)}) custom-call(bf16[512,1024]{1,0:T(8,128)(2,1)S(1)} %get-tuple-element.27.mine_ref, bf16[512,1024]{1,0:T(8,128)(2,1)} %collective-permute-done.4.near_ref, bf16[544,1152]{1,0:T(8,128)(2,1)S(1)} %copy-done.5, ...), custom_call_target="tpu_custom_call" | custom-call | tf_op jit(solution)/shard_map/base/pallas_call | solution.py:231
  76.4 0.0 copy-start.11
  76.5 0.7 copy-done.11
  77.1 0.7 copy-done.13
  77.8 0.0 collective-permute-done.6.r_ref
  77.9 0.7 copy-done.15
  78.5 0.0 all-to-all-done.2
  78.5 0.9 %copy-done.6 = f32[512,128]{1,0:T(8,128)S(1)} copy-done((f32[512,128]{1,0:T(8,128)S(1)}, f32[512,128]{1,0:T(8,128)}, u32[]{:S(2)}) %copy-start.6) | copy-done | bytes 262168
  79.5 0.9 %copy-done.10 = bf16[1024,128]{1,0:T(8,128)(2,1)S(1)} copy-done((bf16[1024,128]{1,0:T(8,128)(2,1)S(1)}, bf16[1024,128]{1,0:T(8,128)(2,1)}, u32[]{:S(2)}) %copy-start.10) | copy-done | bytes 262168
  80.4 0.9 %copy-done.12 = f32[512,128]{1,0:T(8,128)S(1)} copy-done((f32[512,128]{1,0:T(8,128)S(1)}, f32[512,128]{1,0:T(8,128)}, u32[]{:S(2)}) %copy-start.12) | copy-done | bytes 262168
  81.4 0.9 %copy-done.14 = f32[512,128]{1,0:T(8,128)S(1)} copy-done((f32[512,128]{1,0:T(8,128)S(1)}, f32[512,128]{1,0:T(8,128)}, u32[]{:S(2)}) %copy-start.14) | copy-done | bytes 262168
  82.3 0.9 %copy-done.16 = bf16[544,128]{1,0:T(8,128)(2,1)S(1)} copy-done((bf16[544,128]{1,0:T(8,128)(2,1)S(1)}, bf16[544,128]{1,0:T(8,128)(2,1)}, u32[]{:S(2)}) %copy-start.16) | copy-done | bytes 139288
  83.2 2.7 %final.1 = (f32[1024,128]{1,0:T(8,128)}, f32[128,1024]{1,0:T(8,128)}, bf16[512,1024]{1,0:T(8,128)(2,1)}) custom-call(f32[512,1024]{1,0:T(8,128)S(1)} %get-tuple-element.30.base_ref, f32[512,128]{1,0:T(8,128)S(1)} %copy-done.12, f32[512,128]{1,0:T(8,128)S(1)} %copy-done.14, bf16[544,128]{1,0:T(8,128)(2,1)S(1)} %merge.1.after_ref.s_ref, ...), custom_call_target="tpu_custom_call" | custom-call | tf_op jit(solution)/shard_map/final/pallas_call | solution.py:231
  (26 shorter events, 0.1 us)
Async XLA Ops:
  3.1 10.1 %copy-start.17 = (s32[256]{0:T(256)S(1)}, s32[256]{0:T(256)}, u32[]{:S(2)}) copy-start(s32[256]{0:T(256)} %param.15) | copy-start | bytes 3076
  6.8 12.2 %collective-permute-start.1 = (bf16[544,1152]{1,0:T(8,128)(2,1)S(1)}, bf16[544,1152]{1,0:T(8,128)(2,1)S(1)}, u32[]{:S(2)}, u32[]{:S(2)}) collective-permute-start(bf16[544,1152]{1,0:T(8,128)(2,1)S(1)} %get-tuple-element.23.diag_ref), channel_id=1, source_target_pairs={{0,1},{1,0},{2,3},{3,2},{4,5},{5,4},{6,7},{7,6},{8,9},{9,8},{10,11... | collective-permute-start | bytes 3760136 | tf_op jit(solution)/shard_map/ppermute | solution.py:36
  7.3 2.9 %collective-permute-start = (bf16[768,128]{1,0:T(8,128)(2,1)S(1)}, bf16[768,128]{1,0:T(8,128)(2,1)S(1)}, u32[]{:S(2)}, u32[]{:S(2)}) collective-permute-start(bf16[768,128]{1,0:T(8,128)(2,1)S(1)} %rank.1.after_ref), channel_id=1, source_target_pairs={{0,1},{1,0},{2,3},{3,2},{4,5},{5,4},{6,7},{7,6},{8,9},{9,8},{10,11... | collective-permute-start | bytes 589832 | tf_op jit(solution)/shard_map/ppermute | solution.py:36
  10.2 8.2 %collective-permute-start.2 = (bf16[768,128]{1,0:T(8,128)(2,1)S(1)}, bf16[768,128]{1,0:T(8,128)(2,1)S(1)}, u32[]{:S(2)}, u32[]{:S(2)}) collective-permute-start(bf16[768,128]{1,0:T(8,128)(2,1)S(1)} %add_convert_fusion.after_ref.s_ref), channel_id=1, source_target_pairs={{0,2},{1,3},{2,0},{3,1},{4,6},{5,7},{6,4},{7,5},{8,10},{9,11},{10,... | collective-permute-start | bytes 589832 | tf_op jit(solution)/shard_map/ppermute | solution.py:36
  13.2 5.2 %copy-start.1 = (bf16[384,1024]{1,0:T(8,128)(2,1)S(1)}, bf16[384,1024]{1,0:T(8,128)(2,1)}, u32[]{:S(2)}) copy-start(bf16[384,1024]{1,0:T(8,128)(2,1)} %x_ref.1) | copy-start | bytes 2359300
  13.2 5.2 %copy-start.2 = (bf16[384,1024]{1,0:T(8,128)(2,1)S(1)}, bf16[384,1024]{1,0:T(8,128)(2,1)}, u32[]{:S(2)}) copy-start(bf16[384,1024]{1,0:T(8,128)(2,1)} %v_ref.1) | copy-start | bytes 2359300
  17.4 1.0 %copy-start.18 = (bf16[512,1024]{1,0:T(8,128)(2,1)}, bf16[512,1024]{1,0:T(8,128)(2,1)S(1)}, u32[]{:S(2)}) copy-start(bf16[512,1024]{1,0:T(8,128)(2,1)S(1)} %get-tuple-element.28) | copy-start | bytes 3145732
  19.3 35.9 %copy-start.4 = (bf16[544,1152]{1,0:T(8,128)(2,1)}, bf16[544,1152]{1,0:T(8,128)(2,1)S(1)}, u32[]{:S(2)}) copy-start(bf16[544,1152]{1,0:T(8,128)(2,1)S(1)} %get-tuple-element.29.far_ref) | copy-start | bytes 3760132
  41.2 13.5 %all-to-all-start.1 = ((bf16[8,160,128]{2,1,0:T(8,128)(2,1)}), bf16[8,160,128]{2,1,0:T(8,128)(2,1)S(1)}, u32[]{:S(2)}, u32[]{:S(2)}) async-start(bf16[8,160,128]{2,1,0:T(8,128)(2,1)} %get-tuple-element.25), calls=%async_computation.1 | async-start | bytes 655360 | tf_op jit(solution)/shard_map/all_to_all | solution.py:257
  44.7 29.6 %collective-permute-start.5 = (bf16[544,1152]{1,0:T(8,128)(2,1)S(1)}, bf16[544,1152]{1,0:T(8,128)(2,1)}, u32[]{:S(2)}, u32[]{:S(2)}) collective-permute-start(bf16[544,1152]{1,0:T(8,128)(2,1)S(1)} %get-tuple-element.29.far_ref), channel_id=1, source_target_pairs={{0,2},{1,3},{2,0},{3,1},{4,6},{5,7},{6,4},{7,5},{8,10},{9,11},{10,... | collective-permute-start | bytes 3760136 | tf_op jit(solution)/shard_map/ppermute | solution.py:36
  45.9 21.9 %collective-permute-start.4 = (bf16[512,1024]{1,0:T(8,128)(2,1)}, bf16[512,1024]{1,0:T(8,128)(2,1)}, u32[]{:S(2)}, u32[]{:S(2)}) collective-permute-start(bf16[512,1024]{1,0:T(8,128)(2,1)} %copy-done.18), channel_id=1, source_target_pairs={{0,1},{1,0},{2,3},{3,2},{4,5},{5,4},{6,7},{7,6},{8,9},{9,8},{10,11... | collective-permute-start | bytes 3145736 | tf_op jit(solution)/shard_map/ppermute | solution.py:36
  55.2 0.7 copy-start.9
  55.9 1.4 %collective-permute-start.3 = (bf16[544,128]{1,0:T(8,128)(2,1)S(1)}, bf16[544,128]{1,0:T(8,128)(2,1)S(1)}, u32[]{:S(2)}, u32[]{:S(2)}) collective-permute-start(bf16[544,128]{1,0:T(8,128)(2,1)S(1)} %get-tuple-element.26.a_ref.after_ref), channel_id=1, source_target_pairs={{0,1},{1,0},{2,3},{3,2},{4,5},{5,4},{6,7},{7,6},{8,9},{9,8},{10,11... | collective-permute-start | bytes 417800 | tf_op jit(solution)/shard_map/ppermute | solution.py:36
  57.3 0.7 copy-start.7
  58.6 19.9 %all-to-all-start.2 = ((bf16[8,128,128]{2,1,0:T(8,128)(2,1)}), bf16[8,128,128]{2,1,0:T(8,128)(2,1)}, u32[]{:S(2)}, u32[]{:S(2)}) async-start(bf16[8,128,128]{2,1,0:T(8,128)(2,1)} %hold.1), calls=%async_computation.2 | async-start | bytes 524288 | tf_op jit(solution)/shard_map/all_to_all | solution.py:257
  62.7 15.2 %collective-permute-start.6 = (bf16[544,128]{1,0:T(8,128)(2,1)S(1)}, bf16[544,128]{1,0:T(8,128)(2,1)S(1)}, u32[]{:S(2)}, u32[]{:S(2)}) collective-permute-start(bf16[544,128]{1,0:T(8,128)(2,1)S(1)} %merge.1.after_ref.s_ref), channel_id=1, source_target_pairs={{0,2},{1,3},{2,0},{3,1},{4,6},{5,7},{6,4},{7,5},{8,10},{9,11},{10,... | collective-permute-start | bytes 417800 | tf_op jit(solution)/shard_map/ppermute | solution.py:36
  65.1 9.2 %copy-start.5 = (bf16[544,1152]{1,0:T(8,128)(2,1)S(1)}, bf16[544,1152]{1,0:T(8,128)(2,1)}, u32[]{:S(2)}) copy-start(bf16[544,1152]{1,0:T(8,128)(2,1)} %copy-done.4) | copy-start | bytes 3760132
  65.1 9.2 %copy-start.8 = (bf16[544,128]{1,0:T(8,128)(2,1)S(1)}, bf16[544,128]{1,0:T(8,128)(2,1)}, u32[]{:S(2)}) copy-start(bf16[544,128]{1,0:T(8,128)(2,1)} %copy-done.7) | copy-start | bytes 417796
  74.2 4.3 %copy-start = (f32[1024,128]{1,0:T(8,128)S(1)}, f32[1024,128]{1,0:T(8,128)}, u32[]{:S(2)}) copy-start(f32[1024,128]{1,0:T(8,128)} %a_ref.1) | copy-start | bytes 1572868
  74.2 4.3 %copy-start.3 = (f32[128,1024]{1,0:T(8,128)S(1)}, f32[128,1024]{1,0:T(8,128)}, u32[]{:S(2)}) copy-start(f32[128,1024]{1,0:T(8,128)} %b_ref.1) | copy-start | bytes 1572868
  76.4 0.7 copy-start.11
  77.1 0.7 copy-start.13
  77.9 0.7 copy-start.15
  78.5 1.0 %copy-start.6 = (f32[512,128]{1,0:T(8,128)S(1)}, f32[512,128]{1,0:T(8,128)}, u32[]{:S(2)}) copy-start(f32[512,128]{1,0:T(8,128)} %get-tuple-element.49.sin_ref) | copy-start | bytes 786436
  79.5 0.9 %copy-start.10 = (bf16[1024,128]{1,0:T(8,128)(2,1)S(1)}, bf16[1024,128]{1,0:T(8,128)(2,1)}, u32[]{:S(2)}) copy-start(bf16[1024,128]{1,0:T(8,128)(2,1)} %copy-done.9) | copy-start | bytes 786436
  80.4 0.9 %copy-start.12 = (f32[512,128]{1,0:T(8,128)S(1)}, f32[512,128]{1,0:T(8,128)}, u32[]{:S(2)}) copy-start(f32[512,128]{1,0:T(8,128)} %copy-done.11) | copy-start | bytes 786436
  81.4 0.9 %copy-start.14 = (f32[512,128]{1,0:T(8,128)S(1)}, f32[512,128]{1,0:T(8,128)}, u32[]{:S(2)}) copy-start(f32[512,128]{1,0:T(8,128)} %copy-done.13) | copy-start | bytes 786436
  82.3 0.9 %copy-start.16 = (bf16[544,128]{1,0:T(8,128)(2,1)S(1)}, bf16[544,128]{1,0:T(8,128)(2,1)}, u32[]{:S(2)}) copy-start(bf16[544,128]{1,0:T(8,128)(2,1)} %copy-done.15) | copy-start | bytes 417796

commit v5 on v4

--- a/solution.py
+++ b/solution.py
@@ -81,7 +81,7 @@
     return sources, [w_ref.at[i] for i in range(len(sources))]
 
 
-def prep_kernel(at, h_hbm, gain_hbm, a_hbm, w_hbm, after_ref, hg_ref, wide_ref, h_ref, gain_ref, a_ref, w_ref, sems):
+def prep_kernel(at, h_hbm, gain_hbm, a_hbm, w_hbm, hg_ref, wide_ref, h_ref, gain_ref, a_ref, w_ref, sems):
     count, width = h_ref.shape
     blocks = blocks_of(count)
     sources, targets = weight_blocks(at, (3,), w_hbm, w_ref)
@@ -110,18 +110,21 @@
         wide_ref[:count, i * cut : (i + 1) * cut] = dot(hg_ref[...], w_ref[i]).astype(BF)
 
 
-def query_kernel(peers, at, hg_ref, w_hbm, pos_ref, after_ref, *rest):
-    outs, (pos_out, w_ref, sems) = rest[:-3], rest[-3:]
+def part_kernel(x_ref, got_ref, pass_ref, out_ref, pass_out):
+    sum_kernel(x_ref, got_ref, None, out_ref)
+
+
+def query_kernel(peers, at, hg_ref, w_hbm, after_ref, *rest):
+    outs, (w_ref, sems) = rest[:-2], rest[-2:]
     _, width, cut = w_ref.shape
     copies = fetch(*weight_blocks(at, peers, w_hbm, w_ref), sems)
-    pos_out[...] = pos_ref[...].astype(F32)
     per = width // cut
     for i, copy in enumerate(copies):
         copy.wait()
         outs[i // per][:, i % per * cut : (i % per + 1) * cut] = dot(hg_ref[...], w_ref[i]).astype(BF)
 
 
-def far_kernel(mine_ref, diag_ref, got_ref, pass_ref, out_ref, pass_out):
+def far_kernel(mine_ref, diag_ref, got_ref, after_ref, pass_ref, out_ref, pass_out):
     count, width = mine_ref.shape
     out_ref[:count, :width] = (mine_ref[...].astype(F32) + got_ref[:count, :width].astype(F32)).astype(BF)
     out_ref[count:, :width] = jnp.zeros((EXTRA, width), BF)
@@ -135,48 +138,64 @@
     out_ref[count:] = split_terms(join_terms(a_ref[count:]) + join_terms(b_ref[count:]))
 
 
-def grad_kernel(x_ref, v_ref, s_ref, r_ref, out_ref):
+def halves(at, axis, bit, size):
+    mine = lax.rem(at[axis] // (1 << bit), 2) * size
+    other = size - mine
+    return pl.ds(pl.multiple_of(mine, size), size), pl.ds(pl.multiple_of(other, size), size)
+
+
+def halve(at, axis, bit, total_ref, keep_ref, send_ref):
+    mine, other = halves(at, axis, bit, keep_ref.shape[0])
+    keep_ref[...] = total_ref[mine]
+    send_ref[...] = total_ref[other].astype(BF)
+
+
+def grad_kernel(axes, at, x_ref, v_ref, s_ref, r_ref, pos_ref, keep_a, send_a, keep_b, send_b, pos_out, ga, gb):
     count, width = x_ref.shape
-    parts, _, size, _ = out_ref.shape
     low = (s_ref[...].astype(F32) + r_ref[...].astype(F32)).astype(BF)
-    ga = SCALE * dot(x_ref[...], low[count:], ((0,), (0,)))
-    gb = SCALE * dot(low[:count], v_ref[...], ((0,), (0,)))
-    per = LANES // size
-    for i in range(parts):
-        out_ref[i, 0] = ga[i * size : (i + 1) * size].astype(BF)
-        col, row = i // per * LANES, i % per * size
-        out_ref[i, 1] = gb[row : row + size, col : col + LANES].astype(BF)
-
-
-def chunk_kernel(x_ref, a_ref, b_ref):
-    parts, _, size, _ = x_ref.shape
-    total = x_ref[0].astype(F32)
-    for i in range(1, parts):
-        total = total + x_ref[i].astype(F32)
-    squares = total[0] * total[0] + total[1] * total[1]
-    terms = split_terms(jnp.broadcast_to(jnp.sum(squares), (8, LANES)))
-    half = total.astype(BF)
-    for i in range(parts):
-        a_ref[i, :size] = half[0]
-        a_ref[i, size:] = terms
-        b_ref[i] = half[1]
-
-
-def hold_kernel(x_ref, after_ref, out_ref):
-    out_ref[...] = x_ref[...]
-
-
-def low_kernel(hg_ref, x_ref, pack_ref, ga_ref):
-    parts, size, _ = x_ref.shape
-    size -= EXTRA
-    total = join_terms(x_ref[0, size:])
-    for i in range(parts):
-        ga_ref[i * size : (i + 1) * size] = x_ref[i, :size]
-        if i:
-            total = total + join_terms(x_ref[i, size:])
+    ga[...] = SCALE * dot(x_ref[...], low[count:], ((0,), (0,)))
+    halve(at, *axes[0], ga, keep_a, send_a)
+    turned = SCALE * dot(low[:count], v_ref[...], ((0,), (0,)))
+    for b in blocks_of(width):
+        gb[b] = turned[:, b]
+    halve(at, *axes[1], gb, keep_b, send_b)
+    pos_out[...] = pos_ref[...].astype(F32)
+
+
+def halve_kernel(axis, bit, at, keep_ref, got_ref, after_ref, keep_out, send_out, total):
+    total[...] = keep_ref[...] + got_ref[...].astype(F32)
+    halve(at, axis, bit, total, keep_out, send_out)
+
+
+def sum_kernel(keep_ref, got_ref, after_ref, out_ref):
+    out_ref[...] = (keep_ref[...].astype(F32) + got_ref[...].astype(F32)).astype(BF)
+
+
+def join_kernel(axis, bit, at, mine_ref, got_ref, out_ref):
+    mine, other = halves(at, axis, bit, mine_ref.shape[0])
+    out_ref[mine] = mine_ref[...]
+    out_ref[other] = got_ref[...]
+
+
+def square_terms(ref):
+    x = ref[...].astype(F32)
+    return split_terms(jnp.broadcast_to(jnp.sum(x * x), (8, LANES)))
+
+
+def low_kernel(axis, bit, at, hg_ref, mine_ref, got_ref, pack_ref, ga_ref):
+    join_kernel(axis, bit, at, mine_ref, got_ref, ga_ref)
     count = hg_ref.shape[0]
     pack_ref[:count] = dot(hg_ref[...], ga_ref[...]).astype(BF)
-    pack_ref[count:] = split_terms(total)
+    pack_ref[count:] = square_terms(ga_ref)
+
+
+def norm_kernel(axis, bit, at, mine_ref, got_ref, gb_ref, out_ref):
+    join_kernel(axis, bit, at, mine_ref, got_ref, gb_ref)
+    out_ref[...] = square_terms(gb_ref)
+
+
+def norm_merge_kernel(a_ref, b_ref, out_ref):
+    out_ref[...] = split_terms(join_terms(a_ref[...]) + join_terms(b_ref[...]))
 
 
 def base_kernel(mine_ref, near_ref, far_ref, far_got, after_ref, base_ref, low_ref, scale_ref):
@@ -193,11 +212,12 @@
 
 
 def final_kernel(
-    base_ref, low_ref, scale_ref, s_ref, r_ref, ga_ref, gb_ref, a_ref, b_ref, cos_ref, sin_ref,
+    base_ref, low_ref, scale_ref, s_ref, r_ref, sn_ref, rn_ref, ga_ref, gb_ref, a_ref, b_ref, cos_ref, sin_ref,
     a_hbm, b_hbm, q_hbm, new_a, new_b, half_b, out, sems,
 ):
     count, width = base_ref.shape
     total = join_terms(s_ref[count:]) + join_terms(r_ref[count:])
+    total = total + (join_terms(sn_ref[...]) + join_terms(rn_ref[...]))
     rate = (LEARN * lax.rsqrt(total + NORM_EPS))[0:1]
     for c in blocks_of(width):
         fresh = b_ref[:, c] - rate * gb_ref[c].astype(F32)
@@ -227,7 +247,7 @@
     return pltpu.with_memory_space_constraint(x, pltpu.HBM)
 
 
-def call(kernel, outs, in_specs, args, name, scratch=(), out_specs=None, limit=32, aliases=None):
+def call(kernel, outs, in_specs, args, name, scratch=(), out_specs=None, limit=16, aliases=None):
     return pl.pallas_call(
         kernel,
         out_shape=outs,
@@ -252,9 +272,17 @@
     return jnp.concatenate(cos), jnp.concatenate(sin)
 
 
+def bits_of(n):
+    return [b for b in range(n.bit_length() - 1)]
+
+
 def build(n_dp, n_roll, n_tp):
-    n_parts = n_dp * n_roll
-    spread = lambda x: lax.all_to_all(x, ("dp", "roll"), 0, 0, tiled=True)
+    z_bits = [(2, b) for b in bits_of(n_roll)]
+    x_bits = [(1, b) for b in bits_of(n_dp)]
+
+    def cross(x, axis, bit):
+        name, n = (("dp", n_dp), ("roll", n_roll))[axis - 1]
+        return swap(x, name, n, 1 << bit)
 
     def on_device(
         train_inputs, train_cotangent, factor_a, factor_b, base_weight, incoming, norm_gain, positions
@@ -263,8 +291,9 @@
         tokens = train_inputs.shape[0]
         rank = factor_a.shape[1]
         count = steps * rows
-        at = lax.axis_index("tp").astype(jnp.int32)[None]
+        at = jnp.stack([lax.axis_index(a) for a in ("tp", "dp", "roll")]).astype(jnp.int32)
         dma = lambda n: pltpu.SemaphoreType.DMA((n,))
+        vmem = lambda n, dtype=F32: pltpu.VMEM((n, rank), dtype)
 
         part = call(
             rank_kernel,
@@ -279,85 +308,140 @@
         cut = 512
         wide = shape((count + EXTRA, width + rank), BF)
         tall = shape((count, width), BF)
-        pos = positions.reshape(-1, LANES)
         gained, diag = call(
             prep_kernel,
             [tall, wide],
-            [SMEM] + [HBM] * 4 + [ANY],
-            (at, *map(keep_hbm, (incoming.reshape(count, width), norm_gain[None, :], factor_a, base_weight)), part),
+            [SMEM] + [HBM] * 4,
+            (at, *map(keep_hbm, (incoming.reshape(count, width), norm_gain[None, :], factor_a, base_weight))),
             "prep",
             [pltpu.VMEM((count, width), BF), pltpu.VMEM((1, width), F32), pltpu.VMEM(factor_a.shape, F32),
              pltpu.VMEM((width // cut, width, cut), BF), dma(2 + count // LANES + width // cut)],
         )
+        part_sum, diag = call(
+            part_kernel,
+            [shape(part.shape, BF), wide],
+            [VMEM] * 2 + [ANY],
+            (part, part_got, diag),
+            "part_sum",
+            out_specs=[VMEM, ANY],
+            aliases={2: 1},
+        )
+        part_far = swap(part_sum, "tp", n_tp, 2)
         diag_got = swap(diag, "tp", n_tp, 1)
-        part_sum = (part.astype(F32) + part_got.astype(F32)).astype(BF)
-        part_far = swap(part_sum, "tp", n_tp, 2)
-
-        def query(peers, pos, after, name):
+
+        def query(peers, after, name):
             blocks = len(peers) * width // cut
             return call(
                 functools.partial(query_kernel, peers),
-                [tall] * len(peers) + [shape(pos.shape, F32)],
-                [SMEM, VMEM, HBM, VMEM, ANY],
-                (at, gained, keep_hbm(base_weight), pos, after),
+                [tall] * len(peers),
+                [SMEM, VMEM, HBM, ANY],
+                (at, gained, keep_hbm(base_weight), after),
                 name,
                 [pltpu.VMEM((blocks, width, cut), BF), dma(blocks)],
             )
 
-        distant, beside, places = query((2, 1), pos, part_sum, "query_first")
-        beside_got = swap(beside, "tp", n_tp, 1)
-        cos, sin = turn_tables(places.reshape(rows), steps)
-        size = width // n_parts
-        grads = call(
-            grad_kernel,
-            shape((n_parts, 2, size, rank), BF),
-            [VMEM] * 4,
-            (train_inputs, train_cotangent, part_sum, part_far),
+        distant, beside = query((2, 1), part_sum, "query_first")
+        pos = positions.reshape(-1, LANES)
+        half = width // 2
+        a_axes, b_axes = z_bits, x_bits + z_bits
+        keep_a, send_a, keep_b, send_b, places = call(
+            functools.partial(grad_kernel, (a_axes[0], b_axes[0])),
+            [shape((half, rank), F32), shape((half, rank), BF)] * 2 + [shape(pos.shape, F32)],
+            [SMEM] + [VMEM] * 5,
+            (at, train_inputs, train_cotangent, part_sum, part_far, pos),
             "grads",
-        )
-        far, grads = call(
+            [vmem(width), vmem(width)],
+        )
+        far, beside = call(
             far_kernel,
-            [wide, shape(grads.shape, BF)],
-            [VMEM] * 3 + [ANY],
-            (distant, diag, diag_got, grads),
+            [wide, tall],
+            [VMEM] * 3 + [ANY] * 2,
+            (distant, diag, diag_got, send_a, beside),
             "far",
             out_specs=[VMEM, ANY],
-            aliases={3: 1},
+            aliases={4: 1},
         )
         far_got = swap(far, "tp", n_tp, 2)
-        chunk_a, chunk_b = call(
-            chunk_kernel,
-            [shape((n_parts, size + EXTRA, rank), BF), shape((n_parts, size, rank), BF)],
-            [VMEM],
-            (spread(grads),),
-            "chunk",
-        )
-        pieces = spread(chunk_a)
+        got_a = cross(send_a, *a_axes[0])
+        got_b = cross(send_b, *b_axes[0])
+        beside_got = swap(beside, "tp", n_tp, 1)
+
+        def halve_call(keep, got, axis, bit, after, name):
+            size = keep.shape[0] // 2
+            return call(
+                functools.partial(halve_kernel, axis, bit),
+                [shape((size, rank), F32), shape((size, rank), BF)],
+                [SMEM] + [VMEM] * 2 + [ANY],
+                (at, keep, got, after),
+                name,
+                [vmem(2 * size)],
+            )
+
+        def sum_call(keep, got, after, name):
+            return call(
+                sum_kernel, shape(keep.shape, BF), [VMEM] * 2 + [ANY], (keep, got, after), name
+            )
+
+        def join_call(mine, got, axis, bit, name):
+            return call(
+                functools.partial(join_kernel, axis, bit),
+                shape((2 * mine.shape[0], rank), BF),
+                [SMEM] + [VMEM] * 2,
+                (at, mine, got),
+                name,
+            )
+
+        (close,) = query((0,), far, "query_close")
+        after = close
+        for axis, bit in a_axes[1:]:
+            keep_a, send_a = halve_call(keep_a, got_a, axis, bit, after, "halve_a")
+            got_a = cross(send_a, axis, bit)
+        chunk_a = sum_call(keep_a, got_a, after, "chunk_a")
+        for axis, bit in x_bits:
+            chunk_a = sum_call(chunk_a, cross(chunk_a, axis, bit), after, "cross_a")
+        for axis, bit in reversed(a_axes[1:]):
+            chunk_a = join_call(chunk_a, cross(chunk_a, axis, bit), axis, bit, "join_a")
+
+        for axis, bit in b_axes[1:]:
+            keep_b, send_b = halve_call(keep_b, got_b, axis, bit, send_b, "halve_b")
+            got_b = cross(send_b, axis, bit)
+        chunk_b = sum_call(keep_b, got_b, send_b, "chunk_b")
+        for axis, bit in reversed(b_axes[1:]):
+            chunk_b = join_call(chunk_b, cross(chunk_b, axis, bit), axis, bit, "join_b")
+
         step_pack, grad_a = call(
-            low_kernel,
+            functools.partial(low_kernel, *a_axes[0]),
             [shape((count + EXTRA, rank), BF), shape((width, rank), BF)],
-            [VMEM] * 2,
-            (gained, pieces),
+            [SMEM] + [VMEM] * 3,
+            (at, gained, chunk_a, cross(chunk_a, *a_axes[0])),
             "low_rank",
         )
         step_got = swap(step_pack, "tp", n_tp, 1)
         step_sum = call(merge_kernel, shape((count + EXTRA, rank), BF), [VMEM] * 2, (step_pack, step_got), "merge")
         step_far = swap(step_sum, "tp", n_tp, 2)
-        chunk_b = call(hold_kernel, shape(chunk_b.shape, BF), [VMEM, ANY], (chunk_b, step_sum), "hold")
-        grad_b = spread(chunk_b).reshape(width, rank)
-        close, _ = query((0,), pos, step_sum, "query_second")
+        grad_b, norm = call(
+            functools.partial(norm_kernel, *b_axes[0]),
+            [shape((width, rank), BF), shape((EXTRA, LANES), BF)],
+            [SMEM] + [VMEM] * 2,
+            (at, chunk_b, cross(chunk_b, *b_axes[0])),
+            "norm",
+        )
+        norm_got = swap(norm, "tp", n_tp, 1)
+        norm_sum = call(norm_merge_kernel, shape((EXTRA, LANES), BF), [VMEM] * 2, (norm, norm_got), "norm_merge")
+        norm_far = swap(norm_sum, "tp", n_tp, 2)
         base, low, scale = call(
             base_kernel,
             [shape((count, width), F32), shape((count, rank), F32), shape((count, LANES), F32)],
             [VMEM] * 4 + [ANY],
-            (close, beside_got, far, far_got, step_pack),
+            (close, beside_got, far, far_got, step_sum),
             "base",
         )
+        cos, sin = turn_tables(places.reshape(rows), steps)
         new_a, new_b, queries = call(
             final_kernel,
             [shape((width, rank), F32), shape((rank, width), F32), tall],
-            [VMEM] * 11,
-            (base, low, scale, step_sum, step_far, grad_a, grad_b, factor_a, factor_b, cos, sin),
+            [VMEM] * 13,
+            (base, low, scale, step_sum, step_far, norm_sum, norm_far, grad_a, grad_b, factor_a, factor_b, cos, sin),
             "final",
             [pltpu.VMEM((width, rank), F32), pltpu.VMEM((rank, width), F32),
              pltpu.VMEM((rank, width), BF), pltpu.VMEM((count, width), BF), dma(2 + count // LANES)],

time: 86.5 us -> 68.8 us (0.80)
  blocking collectives: 21 us -> 0 us
  starting transfers between devices: 12.7 us -> 24.6 us
  local copies, waits for them, and re-layouts: 9.09 us -> 0.02 us
  Pallas kernels: 21 us -> 23.7 us
  waiting for transfers between devices: 19.3 us -> 18.2 us
    all_to_all x1 -> x0, blocking collectives: 21 us -> none  [build(): spread = lambda x: lax.all_to_all(x, ('dp', 'roll'), 0, 0, tiled=True)]
    ppermute x7 -> x20, starting transfers between devices: 5.27 us -> 24.6 us  [swap(): return lax.ppermute(x, axis, [(i, i ^ k) for i in range(n)])]
    unnamed x38 -> x10, local copies, waits for them, and re-layouts: 9.09 us -> 0.02 us
    all_to_all x2 -> x0, waiting for transfers between devices: 8.77 us -> none  [build(): spread = lambda x: lax.all_to_all(x, ('dp', 'roll'), 0, 0, tiled=True)]
    ppermute x7 -> x20, waiting for transfers between devices: 10.5 us -> 18.2 us  [swap(): return lax.ppermute(x, axis, [(i, i ^ k) for i in range(n)])]
    all_to_all x2 -> x0, starting transfers between devices: 7.47 us -> none  [build(): spread = lambda x: lax.all_to_all(x, ('dp', 'roll'), 0, 0, tiled=True)]
    pallas_call x12 -> x22, Pallas kernels: 21 us -> 23.7 us  [call(): pl.pallas_call(kernel, out_shape=outs, in_specs=in_specs, out_specs=out_s...]
  transfers between devices with their start and end apart: 9 -> 20, of which waited for: 4 -> 8; matrix products, arithmetic and copies ran while one was open for 2% -> 2% of each run, Pallas kernels for 13% -> 28%
where the time goes in v5:
time: 68.8 us; the launch traced here: 68.7 us
  starting transfers between devices  24.6 us (36%)
  Pallas kernels  23.7 us (34%)
  waiting for transfers between devices  18.2 us (26%)
  other arithmetic  1.28 us (2%)
  between operations  0.88 us (1%)
    ppermute x20, starting transfers between devices, swap(): return lax.ppermute(x, axis, [(i, i ^ k) for i in range(n)])  24.6 us
    pallas_call x22, Pallas kernels, call(): pl.pallas_call(kernel, out_shape=outs, in_specs=in_specs, out_specs=out_s...  23.7 us
    ppermute x20, waiting for transfers between devices, swap(): return lax.ppermute(x, axis, [(i, i ^ k) for i in range(n)])  18.2 us
  transfers between devices with their start and end apart: 20, of which 8 were waited for; matrix products, arithmetic and copies ran while one was open for 2% of the time, Pallas kernels for 28%

profile of v5, /device:TPU:0, one launch (start us, length us, event | category | flops | bytes accessed | tf_op | source)
XLA Modules:
  0.0 68.7 jit_solution(16467236365733650954)
XLA Ops:
  0.6 2.4 %rank.1.x_ref = bf16[768,128]{1,0:T(8,128)(2,1)S(1)} custom-call(bf16[384,1024]{1,0:T(8,128)(2,1)} %x_ref.1, bf16[384,1024]{1,0:T(8,128)(2,1)} %v_ref.1, f32[1024,128]{1,0:T(8,128)} %a_ref.1, f32[128,1024]{1,0:T(8,128)} %b_ref.1), custom_call_target="tpu_custom_call" | custom-call | tf_op jit(solution)/shard_map/rank/pallas_call | solution.py:251
  3.1 0.5 collective-permute-start
  3.6 0.1 pad_add_fusion.at
  3.7 4.2 %prep.1 = (bf16[512,1024]{1,0:T(8,128)(2,1)S(1)}, bf16[544,1152]{1,0:T(8,128)(2,1)S(1)}) custom-call(s32[3]{0:T(128)S(1)} %pad_add_fusion.at, bf16[512,1024]{1,0:T(8,128)(2,1)} %bitcast.11, f32[1,1024]{1,0:T(1,128)} %bitcast.12, f32[1024,128]{1,0:T(8,128)} %a_ref.1, bf16[1024,4096]{1,0:T(8,128)(2,1)} %w_hbm.5), custom_call_target="tpu_custom_call" | custom-call | tf_op jit(solution)/shard_map/prep/pallas_call | solution.py:251
  7.9 0.1 part_sum.1
  8.0 0.1 collective-permute-start.1
  8.1 3.0 %collective-permute-start.2 = (bf16[768,128]{1,0:T(8,128)(2,1)S(1)}, bf16[768,128]{1,0:T(8,128)(2,1)S(1)}, u32[]{:S(2)}, u32[]{:S(2)}) collective-permute-start(bf16[768,128]{1,0:T(8,128)(2,1)S(1)} %get-tuple-element.34.after_ref.s_ref), channel_id=1, source_target_pairs={{0,2},{1,3},{2,0},{3,1},{4,6},{5,7},{6,4},{7,5},{8,10},{9,11},{10,... | collective-permute-start | bytes 589832 | tf_op jit(solution)/shard_map/ppermute | solution.py:36
  11.1 4.6 %query_first.1 = (bf16[512,1024]{1,0:T(8,128)(2,1)S(1)}, bf16[512,1024]{1,0:T(8,128)(2,1)S(1)}) custom-call(s32[3]{0:T(128)S(1)} %pad_add_fusion.at, bf16[512,1024]{1,0:T(8,128)(2,1)S(1)} %get-tuple-element.32.hg_ref, bf16[1024,4096]{1,0:T(8,128)(2,1)} %w_hbm.5, bf16[768,128]{1,0:T(8,128)(2,1)S(1)} %get-tuple-element.34.after_ref.s_ref), custom_call_target="tpu_custom_call" | custom-call | tf_op jit(solution)/shard_map/query_first/pallas_call | solution.py:251
  15.7 0.5 collective-permute-done.2.r_ref
  16.2 1.2 %grads.1 = (f32[512,128]{1,0:T(8,128)S(1)}, bf16[512,128]{1,0:T(8,128)(2,1)S(1)}, f32[512,128]{1,0:T(8,128)S(1)}, bf16[512,128]{1,0:T(8,128)(2,1)S(1)}, f32[2,128]{1,0:T(2,128)S(1)}) custom-call(s32[3]{0:T(128)S(1)} %pad_add_fusion.at, bf16[384,1024]{1,0:T(8,128)(2,1)S(1)} %copy-done.1, bf16[384,1024]{1,0:T(8,128)(2,1)S(1)} %copy-done.2, ...), custom_call_target="tpu_custom_call" | custom-call | tf_op jit(solution)/shard_map/grads/pallas_call | solution.py:251
  17.5 0.3 far.1
  17.8 1.8 %collective-permute-start.4 = (bf16[544,1152]{1,0:T(8,128)(2,1)S(1)}, bf16[544,1152]{1,0:T(8,128)(2,1)S(1)}, u32[]{:S(2)}, u32[]{:S(2)}) collective-permute-start(bf16[544,1152]{1,0:T(8,128)(2,1)S(1)} %get-tuple-element.39.after_ref.far_ref), channel_id=1, source_target_pairs={{0,2},{1,3},{2,0},{3,1},{4,6},{5,7},{6,4},{7,5},{8,10},{9,11},{10,... | collective-permute-start | bytes 3760136 | tf_op jit(solution)/shard_map/ppermute | solution.py:36
  19.6 1.6 %collective-permute-start.5 = (bf16[512,128]{1,0:T(8,128)(2,1)S(1)}, bf16[512,128]{1,0:T(8,128)(2,1)S(1)}, u32[]{:S(2)}, u32[]{:S(2)}) collective-permute-start(bf16[512,128]{1,0:T(8,128)(2,1)S(1)} %get-tuple-element.37.after_ref), channel_id=1, source_target_pairs={{0,4},{4,0},{8,12},{12,8},{1,5},{5,1},{9,13},{13,9},{2,6},{6,2},{1... | collective-permute-start | bytes 393224 | tf_op jit(solution)/shard_map/ppermute | solution.py:36
  21.2 1.5 %collective-permute-start.12 = (bf16[512,128]{1,0:T(8,128)(2,1)S(1)}, bf16[512,128]{1,0:T(8,128)(2,1)S(1)}, u32[]{:S(2)}, u32[]{:S(2)}) collective-permute-start(bf16[512,128]{1,0:T(8,128)(2,1)S(1)} %get-tuple-element.49.after_ref), channel_id=1, source_target_pairs={{0,16},{16,0},{1,17},{17,1},{2,18},{18,2},{3,19},{19,3},{4,20},{20... | collective-permute-start | bytes 393224 | tf_op jit(solution)/shard_map/ppermute | solution.py:36
  22.7 3.2 %query_close.1.after_ref.mine_ref = bf16[512,1024]{1,0:T(8,128)(2,1)S(1)} custom-call(s32[3]{0:T(128)S(1)} %pad_add_fusion.at, bf16[512,1024]{1,0:T(8,128)(2,1)S(1)} %get-tuple-element.32.hg_ref, bf16[1024,4096]{1,0:T(8,128)(2,1)} %w_hbm.5, bf16[544,1152]{1,0:T(8,128)(2,1)S(1)} %get-tuple-element.39.after_ref.far_ref), custom_call_target="tpu_custom_call" | custom-call | tf_op jit(solution)/shard_map/query_close/pallas_call | solution.py:251
  25.9 0.6 halve_a.1
  26.5 2.7 %collective-permute-start.6 = (bf16[256,128]{1,0:T(8,128)(2,1)S(1)}, bf16[256,128]{1,0:T(8,128)(2,1)S(1)}, u32[]{:S(2)}, u32[]{:S(2)}) collective-permute-start(bf16[256,128]{1,0:T(8,128)(2,1)S(1)} %get-tuple-element.43), channel_id=1, source_target_pairs={{0,8},{4,12},{8,0},{12,4},{1,9},{5,13},{9,1},{13,5},{2,10},{6,14},... | collective-permute-start | bytes 196616 | tf_op jit(solution)/shard_map/ppermute | solution.py:36
  29.1 3.8 %collective-permute-done.6.got_ref = bf16[256,128]{1,0:T(8,128)(2,1)S(1)} collective-permute-done((bf16[256,128]{1,0:T(8,128)(2,1)S(1)}, bf16[256,128]{1,0:T(8,128)(2,1)S(1)}, u32[]{:S(2)}, u32[]{:S(2)}) %collective-permute-start.6) | collective-permute-done | bytes 65568 | tf_op jit(solution)/shard_map/ppermute | solution.py:36
  33.0 0.6 collective-permute-start.7
  33.6 0.6 halve_b.2
  34.2 0.2 collective-permute-start.13
  34.4 3.0 %collective-permute-done.7.got_ref = bf16[256,128]{1,0:T(8,128)(2,1)S(1)} collective-permute-done((bf16[256,128]{1,0:T(8,128)(2,1)S(1)}, bf16[256,128]{1,0:T(8,128)(2,1)S(1)}, u32[]{:S(2)}, u32[]{:S(2)}) %collective-permute-start.7) | collective-permute-done | bytes 65568 | tf_op jit(solution)/shard_map/ppermute | solution.py:36
  37.3 1.5 %collective-permute-start.8 = (bf16[256,128]{1,0:T(8,128)(2,1)S(1)}, bf16[256,128]{1,0:T(8,128)(2,1)S(1)}, u32[]{:S(2)}, u32[]{:S(2)}) collective-permute-start(bf16[256,128]{1,0:T(8,128)(2,1)S(1)} %cross_a.1.mine_ref), channel_id=1, source_target_pairs={{0,8},{4,12},{8,0},{12,4},{1,9},{5,13},{9,1},{13,5},{2,10},{6,14},... | collective-permute-start | bytes 196616 | tf_op jit(solution)/shard_map/ppermute | solution.py:36
  38.8 0.6 halve_b.3
  39.4 1.9 %collective-permute-start.14 = (bf16[128,128]{1,0:T(8,128)(2,1)S(1)}, bf16[128,128]{1,0:T(8,128)(2,1)S(1)}, u32[]{:S(2)}, u32[]{:S(2)}) collective-permute-start(bf16[128,128]{1,0:T(8,128)(2,1)S(1)} %get-tuple-element.53.after_ref), channel_id=1, source_target_pairs={{0,8},{4,12},{8,0},{12,4},{1,9},{5,13},{9,1},{13,5},{2,10},{6,14},... | collective-permute-start | bytes 98312 | tf_op jit(solution)/shard_map/ppermute | solution.py:36
  41.3 3.0 %collective-permute-done.14.got_ref = bf16[128,128]{1,0:T(8,128)(2,1)S(1)} collective-permute-done((bf16[128,128]{1,0:T(8,128)(2,1)S(1)}, bf16[128,128]{1,0:T(8,128)(2,1)S(1)}, u32[]{:S(2)}, u32[]{:S(2)}) %collective-permute-start.14) | collective-permute-done | bytes 32800 | tf_op jit(solution)/shard_map/ppermute | solution.py:36
  44.3 1.9 %collective-permute-start.15 = (bf16[128,128]{1,0:T(8,128)(2,1)S(1)}, bf16[128,128]{1,0:T(8,128)(2,1)S(1)}, u32[]{:S(2)}, u32[]{:S(2)}) collective-permute-start(bf16[128,128]{1,0:T(8,128)(2,1)S(1)} %chunk_b.1.mine_ref), channel_id=1, source_target_pairs={{0,8},{4,12},{8,0},{12,4},{1,9},{5,13},{9,1},{13,5},{2,10},{6,14},... | collective-permute-start | bytes 98312 | tf_op jit(solution)/shard_map/ppermute | solution.py:36
  46.2 0.6 join_a.1.mine_ref
  46.7 1.9 %collective-permute-start.9 = (bf16[512,128]{1,0:T(8,128)(2,1)S(1)}, bf16[512,128]{1,0:T(8,128)(2,1)S(1)}, u32[]{:S(2)}, u32[]{:S(2)}) collective-permute-start(bf16[512,128]{1,0:T(8,128)(2,1)S(1)} %join_a.1.mine_ref), channel_id=1, source_target_pairs={{0,4},{4,0},{8,12},{12,8},{1,5},{5,1},{9,13},{13,9},{2,6},{6,2},{1... | collective-permute-start | bytes 393224 | tf_op jit(solution)/shard_map/ppermute | solution.py:36
  48.6 0.5 collective-permute-done.15.got_ref
  49.1 0.6 join_b.2.mine_ref
  49.7 2.0 %collective-permute-start.16 = (bf16[256,128]{1,0:T(8,128)(2,1)S(1)}, bf16[256,128]{1,0:T(8,128)(2,1)S(1)}, u32[]{:S(2)}, u32[]{:S(2)}) collective-permute-start(bf16[256,128]{1,0:T(8,128)(2,1)S(1)} %join_b.2.mine_ref), channel_id=1, source_target_pairs={{0,4},{4,0},{8,12},{12,8},{1,5},{5,1},{9,13},{13,9},{2,6},{6,2},{1... | collective-permute-start | bytes 196616 | tf_op jit(solution)/shard_map/ppermute | solution.py:36
  51.7 2.3 %collective-permute-done.16.got_ref = bf16[256,128]{1,0:T(8,128)(2,1)S(1)} collective-permute-done((bf16[256,128]{1,0:T(8,128)(2,1)S(1)}, bf16[256,128]{1,0:T(8,128)(2,1)S(1)}, u32[]{:S(2)}, u32[]{:S(2)}) %collective-permute-start.16) | collective-permute-done | bytes 65568 | tf_op jit(solution)/shard_map/ppermute | solution.py:36
  54.0 0.6 join_b.3.mine_ref
  54.6 1.3 %collective-permute-start.17 = (bf16[512,128]{1,0:T(8,128)(2,1)S(1)}, bf16[512,128]{1,0:T(8,128)(2,1)S(1)}, u32[]{:S(2)}, u32[]{:S(2)}) collective-permute-start(bf16[512,128]{1,0:T(8,128)(2,1)S(1)} %join_b.3.mine_ref), channel_id=1, source_target_pairs={{0,16},{16,0},{1,17},{17,1},{2,18},{18,2},{3,19},{19,3},{4,20},{20... | collective-permute-start | bytes 393224 | tf_op jit(solution)/shard_map/ppermute | solution.py:36
  55.9 1.0 %low_rank.1 = (bf16[544,128]{1,0:T(8,128)(2,1)S(1)}, bf16[1024,128]{1,0:T(8,128)(2,1)S(1)}) custom-call(s32[3]{0:T(128)S(1)} %pad_add_fusion.at, bf16[512,1024]{1,0:T(8,128)(2,1)S(1)} %get-tuple-element.32.hg_ref, bf16[512,128]{1,0:T(8,128)(2,1)S(1)} %join_a.1.mine_ref, bf16[512,128]{1,0:T(8,128)(2,1)S(1)} %collective-permute-done.9.got_ref), custom_call_target="tpu_custom_call" | custom-call | tf_op jit(solution)/shard_map/low_rank/pallas_call | solution.py:251
  56.9 0.1 collective-permute-start.10
  57.0 2.7 %collective-permute-done.17.got_ref = bf16[512,128]{1,0:T(8,128)(2,1)S(1)} collective-permute-done((bf16[512,128]{1,0:T(8,128)(2,1)S(1)}, bf16[512,128]{1,0:T(8,128)(2,1)S(1)}, u32[]{:S(2)}, u32[]{:S(2)}) %collective-permute-start.17) | collective-permute-done | bytes 131104 | tf_op jit(solution)/shard_map/ppermute | solution.py:36
  59.6 0.8 %norm.1 = (bf16[1024,128]{1,0:T(8,128)(2,1)S(1)}, bf16[32,128]{1,0:T(8,128)(2,1)S(1)}) custom-call(s32[3]{0:T(128)S(1)} %pad_add_fusion.at, bf16[512,128]{1,0:T(8,128)(2,1)S(1)} %join_b.3.mine_ref, bf16[512,128]{1,0:T(8,128)(2,1)S(1)} %collective-permute-done.17.got_ref), custom_call_target="tpu_custom_call" | custom-call | tf_op jit(solution)/shard_map/norm/pallas_call | solution.py:251
  60.5 0.1 collective-permute-start.18
  60.6 0.6 collective-permute-start.11
  61.2 1.0 %fusion = (f32[256,64]{1,0:T(8,128)S(1)}, f32[256,64]{1,0:T(8,128)S(1)}, f32[256,64]{1,0:T(8,128)S(1)}, f32[256,64]{1,0:T(8,128)S(1)}, f32[256,64]{1,0:T(8,128)S(1)}, /*index=5*/f32[256,64]{1,0:T(8,128)S(1)}) fusion(f32[64]{0:T(128)S(1)} %multiply_power_fusion, f32[256]{0:T(256)S(1)} %bitcast.9, f32[256]{0:T(256)S(1)} %broadcast_add_fusion), kind=kLoop, calls=%fused_computation.6 | loop fusion | flops 65536 | bytes 395520 | tf_op jit(solution)/shard_map/neg | solution.py:271
  62.2 1.6 %collective-permute-start.19 = (bf16[32,128]{1,0:T(8,128)(2,1)S(1)}, bf16[32,128]{1,0:T(8,128)(2,1)S(1)}, u32[]{:S(2)}, u32[]{:S(2)}) collective-permute-start(bf16[32,128]{1,0:T(8,128)(2,1)S(1)} %norm_merge.1.sn_ref), channel_id=1, source_target_pairs={{0,2},{1,3},{2,0},{3,1},{4,6},{5,7},{6,4},{7,5},{8,10},{9,11},{10,... | collective-permute-start | bytes 24584 | tf_op jit(solution)/shard_map/ppermute | solution.py:36
  63.8 0.2 maximum_maximum_fusion
  64.0 0.0 copy-start
  64.1 0.5 base.1
  64.5 2.4 %collective-permute-done.19.rn_ref = bf16[32,128]{1,0:T(8,128)(2,1)S(1)} collective-permute-done((bf16[32,128]{1,0:T(8,128)(2,1)S(1)}, bf16[32,128]{1,0:T(8,128)(2,1)S(1)}, u32[]{:S(2)}, u32[]{:S(2)}) %collective-permute-start.19) | collective-permute-done | bytes 8224 | tf_op jit(solution)/shard_map/ppermute | solution.py:36
  66.9 1.7 %final.1 = (f32[1024,128]{1,0:T(8,128)}, f32[128,1024]{1,0:T(8,128)}, bf16[512,1024]{1,0:T(8,128)(2,1)}) custom-call(f32[512,1024]{1,0:T(8,128)S(1)} %get-tuple-element.45.base_ref, f32[512,128]{1,0:T(8,128)S(1)} %get-tuple-element.46.low_ref, f32[512,128]{1,0:T(8,128)S(1)} %get-tuple-element.47.scale_ref, bf16[544,128]{1,0:T(8,128)(2,1)S(1)} %merge.1.after_ref.s_ref, ...), custom_call_target="tpu_custom_call" | custom-call | tf_op jit(solution)/shard_map/final/pallas_call | solution.py:251
  (29 shorter events, 0.2 us)
Async XLA Ops:
  3.1 4.8 %collective-permute-start = (bf16[768,128]{1,0:T(8,128)(2,1)S(1)}, bf16[768,128]{1,0:T(8,128)(2,1)S(1)}, u32[]{:S(2)}, u32[]{:S(2)}) collective-permute-start(bf16[768,128]{1,0:T(8,128)(2,1)S(1)} %rank.1.x_ref), channel_id=1, source_target_pairs={{0,1},{1,0},{2,3},{3,2},{4,5},{5,4},{6,7},{7,6},{8,9},{9,8},{10,11... | collective-permute-start | bytes 589832 | tf_op jit(solution)/shard_map/ppermute | solution.py:36
  8.0 9.5 %collective-permute-start.1 = (bf16[544,1152]{1,0:T(8,128)(2,1)S(1)}, bf16[544,1152]{1,0:T(8,128)(2,1)S(1)}, u32[]{:S(2)}, u32[]{:S(2)}) collective-permute-start(bf16[544,1152]{1,0:T(8,128)(2,1)S(1)} %get-tuple-element.36.diag_ref), channel_id=1, source_target_pairs={{0,1},{1,0},{2,3},{3,2},{4,5},{5,4},{6,7},{7,6},{8,9},{9,8},{10,11... | collective-permute-start | bytes 3760136 | tf_op jit(solution)/shard_map/ppermute | solution.py:36
  8.1 8.1 %collective-permute-start.2 = (bf16[768,128]{1,0:T(8,128)(2,1)S(1)}, bf16[768,128]{1,0:T(8,128)(2,1)S(1)}, u32[]{:S(2)}, u32[]{:S(2)}) collective-permute-start(bf16[768,128]{1,0:T(8,128)(2,1)S(1)} %get-tuple-element.34.after_ref.s_ref), channel_id=1, source_target_pairs={{0,2},{1,3},{2,0},{3,1},{4,6},{5,7},{6,4},{7,5},{8,10},{9,11},{10,... | collective-permute-start | bytes 589832 | tf_op jit(solution)/shard_map/ppermute | solution.py:36
  11.0 5.1 %copy-start.1 = (bf16[384,1024]{1,0:T(8,128)(2,1)S(1)}, bf16[384,1024]{1,0:T(8,128)(2,1)}, u32[]{:S(2)}) copy-start(bf16[384,1024]{1,0:T(8,128)(2,1)} %x_ref.1) | copy-start | bytes 2359300
  11.0 5.1 %copy-start.2 = (bf16[384,1024]{1,0:T(8,128)(2,1)S(1)}, bf16[384,1024]{1,0:T(8,128)(2,1)}, u32[]{:S(2)}) copy-start(bf16[384,1024]{1,0:T(8,128)(2,1)} %v_ref.1) | copy-start | bytes 2359300
  11.0 5.1 %copy-start.4 = (s32[256]{0:T(256)S(1)}, s32[256]{0:T(256)}, u32[]{:S(2)}) copy-start(s32[256]{0:T(256)} %param.15) | copy-start | bytes 3076
  17.8 46.2 %collective-permute-start.4 = (bf16[544,1152]{1,0:T(8,128)(2,1)S(1)}, bf16[544,1152]{1,0:T(8,128)(2,1)S(1)}, u32[]{:S(2)}, u32[]{:S(2)}) collective-permute-start(bf16[544,1152]{1,0:T(8,128)(2,1)S(1)} %get-tuple-element.39.after_ref.far_ref), channel_id=1, source_target_pairs={{0,2},{1,3},{2,0},{3,1},{4,6},{5,7},{6,4},{7,5},{8,10},{9,11},{10,... | collective-permute-start | bytes 3760136 | tf_op jit(solution)/shard_map/ppermute | solution.py:36
  19.6 6.3 %collective-permute-start.5 = (bf16[512,128]{1,0:T(8,128)(2,1)S(1)}, bf16[512,128]{1,0:T(8,128)(2,1)S(1)}, u32[]{:S(2)}, u32[]{:S(2)}) collective-permute-start(bf16[512,128]{1,0:T(8,128)(2,1)S(1)} %get-tuple-element.37.after_ref), channel_id=1, source_target_pairs={{0,4},{4,0},{8,12},{12,8},{1,5},{5,1},{9,13},{13,9},{2,6},{6,2},{1... | collective-permute-start | bytes 393224 | tf_op jit(solution)/shard_map/ppermute | solution.py:36
  21.2 42.9 %collective-permute-start.3 = (bf16[512,1024]{1,0:T(8,128)(2,1)S(1)}, bf16[512,1024]{1,0:T(8,128)(2,1)S(1)}, u32[]{:S(2)}, u32[]{:S(2)}) collective-permute-start(bf16[512,1024]{1,0:T(8,128)(2,1)S(1)} %get-tuple-element.40), channel_id=1, source_target_pairs={{0,1},{1,0},{2,3},{3,2},{4,5},{5,4},{6,7},{7,6},{8,9},{9,8},{10,11... | collective-permute-start | bytes 3145736 | tf_op jit(solution)/shard_map/ppermute | solution.py:36
  21.2 12.4 %collective-permute-start.12 = (bf16[512,128]{1,0:T(8,128)(2,1)S(1)}, bf16[512,128]{1,0:T(8,128)(2,1)S(1)}, u32[]{:S(2)}, u32[]{:S(2)}) collective-permute-start(bf16[512,128]{1,0:T(8,128)(2,1)S(1)} %get-tuple-element.49.after_ref), channel_id=1, source_target_pairs={{0,16},{16,0},{1,17},{17,1},{2,18},{18,2},{3,19},{19,3},{4,20},{20... | collective-permute-start | bytes 393224 | tf_op jit(solution)/shard_map/ppermute | solution.py:36
  26.5 6.5 %collective-permute-start.6 = (bf16[256,128]{1,0:T(8,128)(2,1)S(1)}, bf16[256,128]{1,0:T(8,128)(2,1)S(1)}, u32[]{:S(2)}, u32[]{:S(2)}) collective-permute-start(bf16[256,128]{1,0:T(8,128)(2,1)S(1)} %get-tuple-element.43), channel_id=1, source_target_pairs={{0,8},{4,12},{8,0},{12,4},{1,9},{5,13},{9,1},{13,5},{2,10},{6,14},... | collective-permute-start | bytes 196616 | tf_op jit(solution)/shard_map/ppermute | solution.py:36
  33.0 4.3 %collective-permute-start.7 = (bf16[256,128]{1,0:T(8,128)(2,1)S(1)}, bf16[256,128]{1,0:T(8,128)(2,1)S(1)}, u32[]{:S(2)}, u32[]{:S(2)}) collective-permute-start(bf16[256,128]{1,0:T(8,128)(2,1)S(1)} %chunk_a.1.keep_ref), channel_id=1, source_target_pairs={{0,16},{16,0},{1,17},{17,1},{2,18},{18,2},{3,19},{19,3},{4,20},{20... | collective-permute-start | bytes 196616 | tf_op jit(solution)/shard_map/ppermute | solution.py:36
  34.2 4.6 %collective-permute-start.13 = (bf16[256,128]{1,0:T(8,128)(2,1)S(1)}, bf16[256,128]{1,0:T(8,128)(2,1)S(1)}, u32[]{:S(2)}, u32[]{:S(2)}) collective-permute-start(bf16[256,128]{1,0:T(8,128)(2,1)S(1)} %get-tuple-element.51.after_ref), channel_id=1, source_target_pairs={{0,4},{4,0},{8,12},{12,8},{1,5},{5,1},{9,13},{13,9},{2,6},{6,2},{1... | collective-permute-start | bytes 196616 | tf_op jit(solution)/shard_map/ppermute | solution.py:36
  37.3 8.8 %collective-permute-start.8 = (bf16[256,128]{1,0:T(8,128)(2,1)S(1)}, bf16[256,128]{1,0:T(8,128)(2,1)S(1)}, u32[]{:S(2)}, u32[]{:S(2)}) collective-permute-start(bf16[256,128]{1,0:T(8,128)(2,1)S(1)} %cross_a.1.mine_ref), channel_id=1, source_target_pairs={{0,8},{4,12},{8,0},{12,4},{1,9},{5,13},{9,1},{13,5},{2,10},{6,14},... | collective-permute-start | bytes 196616 | tf_op jit(solution)/shard_map/ppermute | solution.py:36
  39.4 4.9 %collective-permute-start.14 = (bf16[128,128]{1,0:T(8,128)(2,1)S(1)}, bf16[128,128]{1,0:T(8,128)(2,1)S(1)}, u32[]{:S(2)}, u32[]{:S(2)}) collective-permute-start(bf16[128,128]{1,0:T(8,128)(2,1)S(1)} %get-tuple-element.53.after_ref), channel_id=1, source_target_pairs={{0,8},{4,12},{8,0},{12,4},{1,9},{5,13},{9,1},{13,5},{2,10},{6,14},... | collective-permute-start | bytes 98312 | tf_op jit(solution)/shard_map/ppermute | solution.py:36
  44.3 4.9 %collective-permute-start.15 = (bf16[128,128]{1,0:T(8,128)(2,1)S(1)}, bf16[128,128]{1,0:T(8,128)(2,1)S(1)}, u32[]{:S(2)}, u32[]{:S(2)}) collective-permute-start(bf16[128,128]{1,0:T(8,128)(2,1)S(1)} %chunk_b.1.mine_ref), channel_id=1, source_target_pairs={{0,8},{4,12},{8,0},{12,4},{1,9},{5,13},{9,1},{13,5},{2,10},{6,14},... | collective-permute-start | bytes 98312 | tf_op jit(solution)/shard_map/ppermute | solution.py:36
  46.7 9.1 %collective-permute-start.9 = (bf16[512,128]{1,0:T(8,128)(2,1)S(1)}, bf16[512,128]{1,0:T(8,128)(2,1)S(1)}, u32[]{:S(2)}, u32[]{:S(2)}) collective-permute-start(bf16[512,128]{1,0:T(8,128)(2,1)S(1)} %join_a.1.mine_ref), channel_id=1, source_target_pairs={{0,4},{4,0},{8,12},{12,8},{1,5},{5,1},{9,13},{13,9},{2,6},{6,2},{1... | collective-permute-start | bytes 393224 | tf_op jit(solution)/shard_map/ppermute | solution.py:36
  49.7 4.3 %collective-permute-start.16 = (bf16[256,128]{1,0:T(8,128)(2,1)S(1)}, bf16[256,128]{1,0:T(8,128)(2,1)S(1)}, u32[]{:S(2)}, u32[]{:S(2)}) collective-permute-start(bf16[256,128]{1,0:T(8,128)(2,1)S(1)} %join_b.2.mine_ref), channel_id=1, source_target_pairs={{0,4},{4,0},{8,12},{12,8},{1,5},{5,1},{9,13},{13,9},{2,6},{6,2},{1... | collective-permute-start | bytes 196616 | tf_op jit(solution)/shard_map/ppermute | solution.py:36
  54.6 5.0 %collective-permute-start.17 = (bf16[512,128]{1,0:T(8,128)(2,1)S(1)}, bf16[512,128]{1,0:T(8,128)(2,1)S(1)}, u32[]{:S(2)}, u32[]{:S(2)}) collective-permute-start(bf16[512,128]{1,0:T(8,128)(2,1)S(1)} %join_b.3.mine_ref), channel_id=1, source_target_pairs={{0,16},{16,0},{1,17},{17,1},{2,18},{18,2},{3,19},{19,3},{4,20},{20... | collective-permute-start | bytes 393224 | tf_op jit(solution)/shard_map/ppermute | solution.py:36
  56.9 3.7 %collective-permute-start.10 = (bf16[544,128]{1,0:T(8,128)(2,1)S(1)}, bf16[544,128]{1,0:T(8,128)(2,1)S(1)}, u32[]{:S(2)}, u32[]{:S(2)}) collective-permute-start(bf16[544,128]{1,0:T(8,128)(2,1)S(1)} %get-tuple-element.44.a_ref), channel_id=1, source_target_pairs={{0,1},{1,0},{2,3},{3,2},{4,5},{5,4},{6,7},{7,6},{8,9},{9,8},{10,11... | collective-permute-start | bytes 417800 | tf_op jit(solution)/shard_map/ppermute | solution.py:36
  60.5 1.7 %collective-permute-start.18 = (bf16[32,128]{1,0:T(8,128)(2,1)S(1)}, bf16[32,128]{1,0:T(8,128)(2,1)S(1)}, u32[]{:S(2)}, u32[]{:S(2)}) collective-permute-start(bf16[32,128]{1,0:T(8,128)(2,1)S(1)} %get-tuple-element.54.a_ref), channel_id=1, source_target_pairs={{0,1},{1,0},{2,3},{3,2},{4,5},{5,4},{6,7},{7,6},{8,9},{9,8},{10,11... | collective-permute-start | bytes 24584 | tf_op jit(solution)/shard_map/ppermute | solution.py:36
  60.6 6.3 %collective-permute-start.11 = (bf16[544,128]{1,0:T(8,128)(2,1)S(1)}, bf16[544,128]{1,0:T(8,128)(2,1)S(1)}, u32[]{:S(2)}, u32[]{:S(2)}) collective-permute-start(bf16[544,128]{1,0:T(8,128)(2,1)S(1)} %merge.1.after_ref.s_ref), channel_id=1, source_target_pairs={{0,2},{1,3},{2,0},{3,1},{4,6},{5,7},{6,4},{7,5},{8,10},{9,11},{10,... | collective-permute-start | bytes 417800 | tf_op jit(solution)/shard_map/ppermute | solution.py:36
  62.2 4.7 %collective-permute-start.19 = (bf16[32,128]{1,0:T(8,128)(2,1)S(1)}, bf16[32,128]{1,0:T(8,128)(2,1)S(1)}, u32[]{:S(2)}, u32[]{:S(2)}) collective-permute-start(bf16[32,128]{1,0:T(8,128)(2,1)S(1)} %norm_merge.1.sn_ref), channel_id=1, source_target_pairs={{0,2},{1,3},{2,0},{3,1},{4,6},{5,7},{6,4},{7,5},{8,10},{9,11},{10,... | collective-permute-start | bytes 24584 | tf_op jit(solution)/shard_map/ppermute | solution.py:36
  64.0 2.9 %copy-start = (f32[1024,128]{1,0:T(8,128)S(1)}, f32[1024,128]{1,0:T(8,128)}, u32[]{:S(2)}) copy-start(f32[1024,128]{1,0:T(8,128)} %a_ref.1) | copy-start | bytes 1572868
  64.0 2.9 %copy-start.3 = (f32[128,1024]{1,0:T(8,128)S(1)}, f32[128,1024]{1,0:T(8,128)}, u32[]{:S(2)}) copy-start(f32[128,1024]{1,0:T(8,128)} %b_ref.1) | copy-start | bytes 1572868

commit v6 on v5

--- a/solution.py
+++ b/solution.py
@@ -19,7 +19,6 @@
 BF = jnp.bfloat16
 F32 = jnp.float32
 VMEM = pl.BlockSpec(memory_space=pltpu.VMEM)
-SMEM = pl.BlockSpec(memory_space=pltpu.SMEM)
 ANY = pl.BlockSpec(memory_space=pl.ANY)
 HBM = pl.BlockSpec(memory_space=pltpu.HBM)
 
@@ -71,20 +70,21 @@
     out_ref[count:] = dot(v_ref[...], b_ref[...].astype(BF), ((1,), (1,))).astype(BF)
 
 
-def weight_blocks(at, peers, w_hbm, w_ref):
+def weight_blocks(peers, w_hbm, w_ref):
     _, width, cut = w_ref.shape
+    mine = lax.axis_index("tp")
     sources = []
     for peer in peers:
         for i in range(width // cut):
-            start = (at[0] ^ peer) * width + i * cut
+            start = (mine ^ peer) * width + i * cut
             sources.append(w_hbm.at[:, pl.ds(pl.multiple_of(start, cut), cut)])
     return sources, [w_ref.at[i] for i in range(len(sources))]
 
 
-def prep_kernel(at, h_hbm, gain_hbm, a_hbm, w_hbm, hg_ref, wide_ref, h_ref, gain_ref, a_ref, w_ref, sems):
+def prep_kernel(h_hbm, gain_hbm, a_hbm, w_hbm, hg_ref, wide_ref, h_ref, gain_ref, a_ref, w_ref, sems):
     count, width = h_ref.shape
     blocks = blocks_of(count)
-    sources, targets = weight_blocks(at, (3,), w_hbm, w_ref)
+    sources, targets = weight_blocks((3,), w_hbm, w_ref)
     copies = fetch(
         [gain_hbm] + [h_hbm.at[b] for b in blocks] + [a_hbm] + sources,
         [gain_ref] + [h_ref.at[b] for b in blocks] + [a_ref] + targets,
@@ -111,13 +111,13 @@
 
 
 def part_kernel(x_ref, got_ref, pass_ref, out_ref, pass_out):
-    sum_kernel(x_ref, got_ref, None, out_ref)
-
-
-def query_kernel(peers, at, hg_ref, w_hbm, after_ref, *rest):
+    sum_kernel(x_ref, got_ref, out_ref)
+
+
+def query_kernel(peers, hg_ref, w_hbm, after_ref, *rest):
     outs, (w_ref, sems) = rest[:-2], rest[-2:]
     _, width, cut = w_ref.shape
-    copies = fetch(*weight_blocks(at, peers, w_hbm, w_ref), sems)
+    copies = fetch(*weight_blocks(peers, w_hbm, w_ref), sems)
     per = width // cut
     for i, copy in enumerate(copies):
         copy.wait()
@@ -138,43 +138,52 @@
     out_ref[count:] = split_terms(join_terms(a_ref[count:]) + join_terms(b_ref[count:]))
 
 
-def halves(at, axis, bit, size):
-    mine = lax.rem(at[axis] // (1 << bit), 2) * size
-    other = size - mine
-    return pl.ds(pl.multiple_of(mine, size), size), pl.ds(pl.multiple_of(other, size), size)
-
-
-def halve(at, axis, bit, total_ref, keep_ref, send_ref):
-    mine, other = halves(at, axis, bit, keep_ref.shape[0])
+def halves(axis, bit, size):
+    mine = lax.rem(lax.axis_index(axis) // (1 << bit), 2) * size
+    return pl.ds(pl.multiple_of(mine, size), size), pl.ds(pl.multiple_of(size - mine, size), size)
+
+
+def halve(axis, bit, total_ref, keep_ref, send_ref):
+    mine, other = halves(axis, bit, keep_ref.shape[0])
     keep_ref[...] = total_ref[mine]
     send_ref[...] = total_ref[other].astype(BF)
 
 
-def grad_kernel(axes, at, x_ref, v_ref, s_ref, r_ref, pos_ref, keep_a, send_a, keep_b, send_b, pos_out, ga, gb):
+def join(axis, bit, mine_ref, got_ref, out_ref):
+    mine, other = halves(axis, bit, mine_ref.shape[0])
+    out_ref[mine] = mine_ref[...]
+    out_ref[other] = got_ref[...]
+
+
+def grad_kernel(axes, x_ref, v_ref, s_ref, r_ref, pos_ref, keep_a, send_a, keep_b, send_b, pos_out, ga, gb):
     count, width = x_ref.shape
     low = (s_ref[...].astype(F32) + r_ref[...].astype(F32)).astype(BF)
     ga[...] = SCALE * dot(x_ref[...], low[count:], ((0,), (0,)))
-    halve(at, *axes[0], ga, keep_a, send_a)
+    halve(*axes[0], ga, keep_a, send_a)
     turned = SCALE * dot(low[:count], v_ref[...], ((0,), (0,)))
     for b in blocks_of(width):
         gb[b] = turned[:, b]
-    halve(at, *axes[1], gb, keep_b, send_b)
+    halve(*axes[1], gb, keep_b, send_b)
     pos_out[...] = pos_ref[...].astype(F32)
 
 
-def halve_kernel(axis, bit, at, keep_ref, got_ref, after_ref, keep_out, send_out, total):
-    total[...] = keep_ref[...] + got_ref[...].astype(F32)
-    halve(at, axis, bit, total, keep_out, send_out)
-
-
-def sum_kernel(keep_ref, got_ref, after_ref, out_ref):
+def sum_kernel(keep_ref, got_ref, out_ref):
     out_ref[...] = (keep_ref[...].astype(F32) + got_ref[...].astype(F32)).astype(BF)
 
 
-def join_kernel(axis, bit, at, mine_ref, got_ref, out_ref):
-    mine, other = halves(at, axis, bit, mine_ref.shape[0])
-    out_ref[mine] = mine_ref[...]
-    out_ref[other] = got_ref[...]
+def step_kernel(steps, *refs):
+    n = len(steps)
+    ins, outs = refs[: 2 * n], list(refs[2 * n + 1 :])
+    for i, (kind, axis, bit) in enumerate(steps):
+        mine, got = ins[2 * i], ins[2 * i + 1]
+        if kind == "halve":
+            total = outs.pop()
+            total[...] = mine[...] + got[...].astype(F32)
+            halve(axis, bit, total, outs.pop(0), outs.pop(0))
+        elif kind == "sum":
+            sum_kernel(mine, got, outs.pop(0))
+        else:
+            join(axis, bit, mine, got, outs.pop(0))
 
 
 def square_terms(ref):
@@ -182,16 +191,13 @@
     return split_terms(jnp.broadcast_to(jnp.sum(x * x), (8, LANES)))
 
 
-def low_kernel(axis, bit, at, hg_ref, mine_ref, got_ref, pack_ref, ga_ref):
-    join_kernel(axis, bit, at, mine_ref, got_ref, ga_ref)
+def low_kernel(axis, bit, hg_ref, mine_a, got_a, mine_b, got_b, pack_ref, ga_ref, gb_ref, norm_ref):
+    join(axis, bit, mine_a, got_a, ga_ref)
     count = hg_ref.shape[0]
     pack_ref[:count] = dot(hg_ref[...], ga_ref[...]).astype(BF)
     pack_ref[count:] = square_terms(ga_ref)
-
-
-def norm_kernel(axis, bit, at, mine_ref, got_ref, gb_ref, out_ref):
-    join_kernel(axis, bit, at, mine_ref, got_ref, gb_ref)
-    out_ref[...] = square_terms(gb_ref)
+    join(axis, bit, mine_b, got_b, gb_ref)
+    norm_ref[...] = square_terms(gb_ref)
 
 
 def norm_merge_kernel(a_ref, b_ref, out_ref):
@@ -212,9 +218,10 @@
 
 
 def final_kernel(
-    base_ref, low_ref, scale_ref, s_ref, r_ref, sn_ref, rn_ref, ga_ref, gb_ref, a_ref, b_ref, cos_ref, sin_ref,
-    a_hbm, b_hbm, q_hbm, new_a, new_b, half_b, out, sems,
+    axis, bit, base_ref, low_ref, scale_ref, s_ref, r_ref, sn_ref, rn_ref, ga_ref, mine_b, got_b, a_ref, b_ref,
+    cos_ref, sin_ref, a_hbm, b_hbm, q_hbm, gb_ref, new_a, new_b, half_b, out, sems,
 ):
+    join(axis, bit, mine_b, got_b, gb_ref)
     count, width = base_ref.shape
     total = join_terms(s_ref[count:]) + join_terms(r_ref[count:])
     total = total + (join_terms(sn_ref[...]) + join_terms(rn_ref[...]))
@@ -277,12 +284,19 @@
 
 
 def build(n_dp, n_roll, n_tp):
-    z_bits = [(2, b) for b in bits_of(n_roll)]
-    x_bits = [(1, b) for b in bits_of(n_dp)]
+    z_bits = [("roll", b) for b in bits_of(n_roll)]
+    x_bits = [("dp", b) for b in bits_of(n_dp)]
+    sizes = {"dp": n_dp, "roll": n_roll}
 
     def cross(x, axis, bit):
-        name, n = (("dp", n_dp), ("roll", n_roll))[axis - 1]
-        return swap(x, name, n, 1 << bit)
+        return swap(x, axis, sizes[axis], 1 << bit)
+
+    def path(down, across):
+        ways = down + across + down[::-1]
+        after = [("halve",) + way for way in down[1:]] + [("sum", None, None)] * (1 + len(across))
+        return list(zip(ways, after + [("join",) + way for way in down[::-1]]))
+
+    path_a, path_b = path(z_bits, x_bits), path(x_bits + z_bits, [])
 
     def on_device(
         train_inputs, train_cotangent, factor_a, factor_b, base_weight, incoming, norm_gain, positions
@@ -291,7 +305,6 @@
         tokens = train_inputs.shape[0]
         rank = factor_a.shape[1]
         count = steps * rows
-        at = jnp.stack([lax.axis_index(a) for a in ("tp", "dp", "roll")]).astype(jnp.int32)
         dma = lambda n: pltpu.SemaphoreType.DMA((n,))
         vmem = lambda n, dtype=F32: pltpu.VMEM((n, rank), dtype)
 
@@ -311,8 +324,8 @@
         gained, diag = call(
             prep_kernel,
             [tall, wide],
-            [SMEM] + [HBM] * 4,
-            (at, *map(keep_hbm, (incoming.reshape(count, width), norm_gain[None, :], factor_a, base_weight))),
+            [HBM] * 4,
+            tuple(map(keep_hbm, (incoming.reshape(count, width), norm_gain[None, :], factor_a, base_weight))),
             "prep",
             [pltpu.VMEM((count, width), BF), pltpu.VMEM((1, width), F32), pltpu.VMEM(factor_a.shape, F32),
              pltpu.VMEM((width // cut, width, cut), BF), dma(2 + count // LANES + width // cut)],
@@ -334,8 +347,8 @@
             return call(
                 functools.partial(query_kernel, peers),
                 [tall] * len(peers),
-                [SMEM, VMEM, HBM, ANY],
-                (at, gained, keep_hbm(base_weight), after),
+                [VMEM, HBM, ANY],
+                (gained, keep_hbm(base_weight), after),
                 name,
                 [pltpu.VMEM((blocks, width, cut), BF), dma(blocks)],
             )
@@ -343,12 +356,11 @@
         distant, beside = query((2, 1), part_sum, "query_first")
         pos = positions.reshape(-1, LANES)
         half = width // 2
-        a_axes, b_axes = z_bits, x_bits + z_bits
         keep_a, send_a, keep_b, send_b, places = call(
-            functools.partial(grad_kernel, (a_axes[0], b_axes[0])),
+            functools.partial(grad_kernel, (path_a[0][0], path_b[0][0])),
             [shape((half, rank), F32), shape((half, rank), BF)] * 2 + [shape(pos.shape, F32)],
-            [SMEM] + [VMEM] * 5,
-            (at, train_inputs, train_cotangent, part_sum, part_far, pos),
+            [VMEM] * 5,
+            (train_inputs, train_cotangent, part_sum, part_far, pos),
             "grads",
             [vmem(width), vmem(width)],
         )
@@ -362,73 +374,66 @@
             aliases={4: 1},
         )
         far_got = swap(far, "tp", n_tp, 2)
-        got_a = cross(send_a, *a_axes[0])
-        got_b = cross(send_b, *b_axes[0])
         beside_got = swap(beside, "tp", n_tp, 1)
-
-        def halve_call(keep, got, axis, bit, after, name):
-            size = keep.shape[0] // 2
-            return call(
-                functools.partial(halve_kernel, axis, bit),
-                [shape((size, rank), F32), shape((size, rank), BF)],
-                [SMEM] + [VMEM] * 2 + [ANY],
-                (at, keep, got, after),
+        (close,) = query((0,), far, "query_close")
+        cos, sin = turn_tables(places.reshape(rows), steps)
+
+        def step_call(steps, after, name):
+            ins, outs, scratch = [], [], []
+            for (kind, _, _), mine, got in steps:
+                size = mine.shape[0]
+                ins += [mine, got]
+                if kind == "halve":
+                    outs += [shape((size // 2, rank), F32), shape((size // 2, rank), BF)]
+                    scratch.append(vmem(size))
+                else:
+                    outs.append(shape((2 * size if kind == "join" else size, rank), BF))
+            made = call(
+                functools.partial(step_kernel, [step[0] for step in steps]),
+                outs,
+                [VMEM] * len(ins) + [ANY],
+                (*ins, after),
                 name,
-                [vmem(2 * size)],
+                scratch,
             )
-
-        def sum_call(keep, got, after, name):
-            return call(
-                sum_kernel, shape(keep.shape, BF), [VMEM] * 2 + [ANY], (keep, got, after), name
+            made, states = list(made), []
+            for (kind, _, _), _, _ in steps:
+                states.append((made.pop(0), made.pop(0)) if kind == "halve" else (made[0], made.pop(0)))
+            return states
+
+        state_a, state_b = (keep_a, send_a), (keep_b, send_b)
+        for i, ((way_a, step_a), (way_b, step_b)) in enumerate(zip(path_a[:-1], path_b)):
+            got_a, got_b = cross(state_a[1], *way_a), cross(state_b[1], *way_b)
+            after = close if i == 0 else cos if i == 1 else sin
+            state_a, state_b = step_call(
+                [(step_a, state_a[0], got_a), (step_b, state_b[0], got_b)], after, f"step_{i}"
             )
-
-        def join_call(mine, got, axis, bit, name):
-            return call(
-                functools.partial(join_kernel, axis, bit),
-                shape((2 * mine.shape[0], rank), BF),
-                [SMEM] + [VMEM] * 2,
-                (at, mine, got),
-                name,
-            )
-
-        (close,) = query((0,), far, "query_close")
-        after = close
-        for axis, bit in a_axes[1:]:
-            keep_a, send_a = halve_call(keep_a, got_a, axis, bit, after, "halve_a")
-            got_a = cross(send_a, axis, bit)
-        chunk_a = sum_call(keep_a, got_a, after, "chunk_a")
-        for axis, bit in x_bits:
-            chunk_a = sum_call(chunk_a, cross(chunk_a, axis, bit), after, "cross_a")
-        for axis, bit in reversed(a_axes[1:]):
-            chunk_a = join_call(chunk_a, cross(chunk_a, axis, bit), axis, bit, "join_a")
-
-        for axis, bit in b_axes[1:]:
-            keep_b, send_b = halve_call(keep_b, got_b, axis, bit, send_b, "halve_b")
-            got_b = cross(send_b, axis, bit)
-        chunk_b = sum_call(keep_b, got_b, send_b, "chunk_b")
-        for axis, bit in reversed(b_axes[1:]):
-            chunk_b = join_call(chunk_b, cross(chunk_b, axis, bit), axis, bit, "join_b")
-
-        step_pack, grad_a = call(
-            functools.partial(low_kernel, *a_axes[0]),
-            [shape((count + EXTRA, rank), BF), shape((width, rank), BF)],
-            [SMEM] + [VMEM] * 3,
-            (at, gained, chunk_a, cross(chunk_a, *a_axes[0])),
+        way = path_a[-1][0]
+        mine_a, mine_b = state_a[1], state_b[1]
+        got_a, got_b = cross(mine_a, *way), cross(mine_b, *way)
+        step_pack, grad_a, mine_b, norm = call(
+            functools.partial(low_kernel, *way),
+            [shape((count + EXTRA, rank), BF), shape((width, rank), BF), shape((2 * mine_b.shape[0], rank), BF),
+             shape((EXTRA, LANES), BF)],
+            [VMEM] * 5,
+            (gained, mine_a, got_a, mine_b, got_b),
             "low_rank",
         )
         step_got = swap(step_pack, "tp", n_tp, 1)
         step_sum = call(merge_kernel, shape((count + EXTRA, rank), BF), [VMEM] * 2, (step_pack, step_got), "merge")
         step_far = swap(step_sum, "tp", n_tp, 2)
-        grad_b, norm = call(
-            functools.partial(norm_kernel, *b_axes[0]),
-            [shape((width, rank), BF), shape((EXTRA, LANES), BF)],
-            [SMEM] + [VMEM] * 2,
-            (at, chunk_b, cross(chunk_b, *b_axes[0])),
-            "norm",
-        )
-        norm_got = swap(norm, "tp", n_tp, 1)
-        norm_sum = call(norm_merge_kernel, shape((EXTRA, LANES), BF), [VMEM] * 2, (norm, norm_got), "norm_merge")
-        norm_far = swap(norm_sum, "tp", n_tp, 2)
+
+        for (axis, bit), step in path_b[len(path_a) : -1]:
+            ((_, mine_b),) = step_call([(step, mine_b, cross(mine_b, axis, bit))], step_pack, "join_b")
+        got_b = cross(mine_b, *path_b[-1][0])
+
+        def norm_add(x, y):
+            return call(norm_merge_kernel, shape((EXTRA, LANES), BF), [VMEM] * 2, (x, y), "norm_merge")
+
+        for way in x_bits:
+            norm = norm_add(norm, cross(norm, *way))
+        norm = norm_add(norm, swap(norm, "tp", n_tp, 1))
+        norm_far = swap(norm, "tp", n_tp, 2)
         base, low, scale = call(
             base_kernel,
             [shape((count, width), F32), shape((count, rank), F32), shape((count, LANES), F32)],
@@ -436,14 +441,13 @@
             (close, beside_got, far, far_got, step_sum),
             "base",
         )
-        cos, sin = turn_tables(places.reshape(rows), steps)
         new_a, new_b, queries = call(
-            final_kernel,
+            functools.partial(final_kernel, *path_b[-1][0]),
             [shape((width, rank), F32), shape((rank, width), F32), tall],
-            [VMEM] * 13,
-            (base, low, scale, step_sum, step_far, norm_sum, norm_far, grad_a, grad_b, factor_a, factor_b, cos, sin),
+            [VMEM] * 14,
+            (base, low, scale, step_sum, step_far, norm, norm_far, grad_a, mine_b, got_b, factor_a, factor_b, cos, sin),
             "final",
-            [pltpu.VMEM((width, rank), F32), pltpu.VMEM((rank, width), F32),
+            [vmem(width, BF), pltpu.VMEM((width, rank), F32), pltpu.VMEM((rank, width), F32),
              pltpu.VMEM((rank, width), BF), pltpu.VMEM((count, width), BF), dma(2 + count // LANES)],
             [HBM] * 3,
         )

time: 68.8 us -> 65.9 us (0.958)
  Pallas kernels: 23.7 us -> 17.1 us
  waiting for transfers between devices: 18.2 us -> 24.3 us
  starting transfers between devices: 24.6 us -> 22.2 us
    pallas_call x22 -> x17, Pallas kernels: 23.7 us -> 17.1 us  [call(): pl.pallas_call(kernel, out_shape=outs, in_specs=in_specs, out_specs=out_s...]
    ppermute x20 -> x21, waiting for transfers between devices: 18.2 us -> 24.3 us  [swap(): return lax.ppermute(x, axis, [(i, i ^ k) for i in range(n)])]
    ppermute x20 -> x21, starting transfers between devices: 24.6 us -> 22.2 us  [swap(): return lax.ppermute(x, axis, [(i, i ^ k) for i in range(n)])]
  transfers between devices with their start and end apart: 20 -> 21, of which waited for: 8 -> 10; matrix products, arithmetic and copies ran while one was open for 2% -> 2% of each run, Pallas kernels for 28% -> 19%
where the time goes in v6:
time: 65.9 us; the launch traced here: 65.7 us
  waiting for transfers between devices  24.3 us (37%)
  starting transfers between devices  22.2 us (34%)
  Pallas kernels  17.1 us (26%)
  other arithmetic  1.28 us (2%)
  between operations  0.82 us (1%)
    ppermute x21, waiting for transfers between devices, swap(): return lax.ppermute(x, axis, [(i, i ^ k) for i in range(n)])  24.3 us
    ppermute x21, starting transfers between devices, swap(): return lax.ppermute(x, axis, [(i, i ^ k) for i in range(n)])  22.2 us
    pallas_call x17, Pallas kernels, call(): pl.pallas_call(kernel, out_shape=outs, in_specs=in_specs, out_specs=out_s...  17.1 us
  transfers between devices with their start and end apart: 21, of which 10 were waited for; matrix products, arithmetic and copies ran while one was open for 2% of the time, Pallas kernels for 19%

profile of v6, /device:TPU:0, one launch (start us, length us, event | category | flops | bytes accessed | tf_op | source)
XLA Modules:
  0.0 65.7 jit_solution(12161293236604829748)
XLA Ops:
  0.6 2.4 %rank.1.x_ref = bf16[768,128]{1,0:T(8,128)(2,1)S(1)} custom-call(bf16[384,1024]{1,0:T(8,128)(2,1)} %x_ref.1, bf16[384,1024]{1,0:T(8,128)(2,1)} %v_ref.1, f32[1024,128]{1,0:T(8,128)} %a_ref.1, f32[128,1024]{1,0:T(8,128)} %b_ref.1), custom_call_target="tpu_custom_call" | custom-call | tf_op jit(solution)/shard_map/rank/pallas_call | solution.py:258
  3.1 0.5 collective-permute-start
  3.6 3.7 %prep.1 = (bf16[512,1024]{1,0:T(8,128)(2,1)S(1)}, bf16[544,1152]{1,0:T(8,128)(2,1)S(1)}) custom-call(bf16[512,1024]{1,0:T(8,128)(2,1)} %bitcast.8, f32[1,1024]{1,0:T(1,128)} %bitcast.9, f32[1024,128]{1,0:T(8,128)} %a_ref.1, bf16[1024,4096]{1,0:T(8,128)(2,1)} %w_hbm.5), custom_call_target="tpu_custom_call" | custom-call | tf_op jit(solution)/shard_map/prep/pallas_call | solution.py:258
  7.3 0.0 collective-permute-done.got_ref
  7.3 0.1 part_sum.1
  7.3 0.1 collective-permute-start.1
  7.5 3.0 %collective-permute-start.2 = (bf16[768,128]{1,0:T(8,128)(2,1)S(1)}, bf16[768,128]{1,0:T(8,128)(2,1)S(1)}, u32[]{:S(2)}, u32[]{:S(2)}) collective-permute-start(bf16[768,128]{1,0:T(8,128)(2,1)S(1)} %get-tuple-element.39.after_ref.s_ref), channel_id=1, source_target_pairs={{0,2},{1,3},{2,0},{3,1},{4,6},{5,7},{6,4},{7,5},{8,10},{9,11},{10,... | collective-permute-start | bytes 589832 | tf_op jit(solution)/shard_map/ppermute | solution.py:35
  10.4 4.2 %query_first.1 = (bf16[512,1024]{1,0:T(8,128)(2,1)S(1)}, bf16[512,1024]{1,0:T(8,128)(2,1)S(1)}) custom-call(bf16[512,1024]{1,0:T(8,128)(2,1)S(1)} %get-tuple-element.37.hg_ref, bf16[1024,4096]{1,0:T(8,128)(2,1)} %w_hbm.5, bf16[768,128]{1,0:T(8,128)(2,1)S(1)} %get-tuple-element.39.after_ref.s_ref), custom_call_target="tpu_custom_call" | custom-call | tf_op jit(solution)/shard_map/query_first/pallas_call | solution.py:258
  14.7 0.9 %collective-permute-done.2.r_ref = bf16[768,128]{1,0:T(8,128)(2,1)S(1)} collective-permute-done((bf16[768,128]{1,0:T(8,128)(2,1)S(1)}, bf16[768,128]{1,0:T(8,128)(2,1)S(1)}, u32[]{:S(2)}, u32[]{:S(2)}) %collective-permute-start.2) | collective-permute-done | bytes 196640 | tf_op jit(solution)/shard_map/ppermute | solution.py:35
  15.6 0.7 %grads.1 = (f32[512,128]{1,0:T(8,128)S(1)}, bf16[512,128]{1,0:T(8,128)(2,1)S(1)}, f32[512,128]{1,0:T(8,128)S(1)}, bf16[512,128]{1,0:T(8,128)(2,1)S(1)}, f32[2,128]{1,0:T(2,128)S(1)}) custom-call(bf16[384,1024]{1,0:T(8,128)(2,1)S(1)} %copy-done.1, bf16[384,1024]{1,0:T(8,128)(2,1)S(1)} %copy-done.2, bf16[768,128]{1,0:T(8,128)(2,1)S(1)} %get-tuple-element.39.after_ref.s_ref, ...), custom_call_target="tpu_custom_call" | custom-call | tf_op jit(solution)/shard_map/grads/pallas_call | solution.py:258
  16.3 0.3 far.1
  16.6 1.8 %collective-permute-start.4 = (bf16[544,1152]{1,0:T(8,128)(2,1)S(1)}, bf16[544,1152]{1,0:T(8,128)(2,1)S(1)}, u32[]{:S(2)}, u32[]{:S(2)}) collective-permute-start(bf16[544,1152]{1,0:T(8,128)(2,1)S(1)} %get-tuple-element.44.after_ref.far_ref), channel_id=1, source_target_pairs={{0,2},{1,3},{2,0},{3,1},{4,6},{5,7},{6,4},{7,5},{8,10},{9,11},{10,... | collective-permute-start | bytes 3760136 | tf_op jit(solution)/shard_map/ppermute | solution.py:35
  18.4 1.6 %collective-permute-start.5 = (bf16[512,128]{1,0:T(8,128)(2,1)S(1)}, bf16[512,128]{1,0:T(8,128)(2,1)S(1)}, u32[]{:S(2)}, u32[]{:S(2)}) collective-permute-start(bf16[512,128]{1,0:T(8,128)(2,1)S(1)} %get-tuple-element.42.after_ref), channel_id=1, source_target_pairs={{0,4},{4,0},{8,12},{12,8},{1,5},{5,1},{9,13},{13,9},{2,6},{6,2},{1... | collective-permute-start | bytes 393224 | tf_op jit(solution)/shard_map/ppermute | solution.py:35
  20.0 1.5 %collective-permute-start.6 = (bf16[512,128]{1,0:T(8,128)(2,1)S(1)}, bf16[512,128]{1,0:T(8,128)(2,1)S(1)}, u32[]{:S(2)}, u32[]{:S(2)}) collective-permute-start(bf16[512,128]{1,0:T(8,128)(2,1)S(1)} %get-tuple-element.48), channel_id=1, source_target_pairs={{0,16},{16,0},{1,17},{17,1},{2,18},{18,2},{3,19},{19,3},{4,20},{20... | collective-permute-start | bytes 393224 | tf_op jit(solution)/shard_map/ppermute | solution.py:35
  21.5 1.0 %fusion = (f32[256,64]{1,0:T(8,128)S(1)}, f32[256,64]{1,0:T(8,128)S(1)}, f32[256,64]{1,0:T(8,128)S(1)}, f32[256,64]{1,0:T(8,128)S(1)}, f32[256,64]{1,0:T(8,128)S(1)}, /*index=5*/f32[256,64]{1,0:T(8,128)S(1)}) fusion(f32[64]{0:T(128)S(1)} %multiply_power_fusion, f32[256]{0:T(256)S(1)} %bitcast.6, f32[256]{0:T(256)S(1)} %broadcast_add_fusion), kind=kLoop, calls=%fused_computation.6 | loop fusion | flops 65536 | bytes 395520 | tf_op jit(solution)/shard_map/neg | solution.py:278
  22.5 2.7 %query_close.1.refs_4_.mine_ref = bf16[512,1024]{1,0:T(8,128)(2,1)S(1)} custom-call(bf16[512,1024]{1,0:T(8,128)(2,1)S(1)} %get-tuple-element.37.hg_ref, bf16[1024,4096]{1,0:T(8,128)(2,1)} %w_hbm.5, bf16[544,1152]{1,0:T(8,128)(2,1)S(1)} %get-tuple-element.44.after_ref.far_ref), custom_call_target="tpu_custom_call" | custom-call | tf_op jit(solution)/shard_map/query_close/pallas_call | solution.py:258
  25.2 0.0 collective-permute-done.5.refs_1_
  25.2 0.1 step_0.1
  25.3 2.7 %collective-permute-start.7 = (bf16[256,128]{1,0:T(8,128)(2,1)S(1)}, bf16[256,128]{1,0:T(8,128)(2,1)S(1)}, u32[]{:S(2)}, u32[]{:S(2)}) collective-permute-start(bf16[256,128]{1,0:T(8,128)(2,1)S(1)} %get-tuple-element.50), channel_id=1, source_target_pairs={{0,8},{4,12},{8,0},{12,4},{1,9},{5,13},{9,1},{13,5},{2,10},{6,14},... | collective-permute-start | bytes 196616 | tf_op jit(solution)/shard_map/ppermute | solution.py:35
  28.0 0.4 collective-permute-start.8
  28.4 0.1 maximum_maximum_fusion.refs_4_.cos_ref
  28.6 3.6 %collective-permute-done.7.refs_1_ = bf16[256,128]{1,0:T(8,128)(2,1)S(1)} collective-permute-done((bf16[256,128]{1,0:T(8,128)(2,1)S(1)}, bf16[256,128]{1,0:T(8,128)(2,1)S(1)}, u32[]{:S(2)}, u32[]{:S(2)}) %collective-permute-start.7) | collective-permute-done | bytes 65568 | tf_op jit(solution)/shard_map/ppermute | solution.py:35
  32.2 1.3 %collective-permute-done.8.refs_3_ = bf16[256,128]{1,0:T(8,128)(2,1)S(1)} collective-permute-done((bf16[256,128]{1,0:T(8,128)(2,1)S(1)}, bf16[256,128]{1,0:T(8,128)(2,1)S(1)}, u32[]{:S(2)}, u32[]{:S(2)}) %collective-permute-start.8) | collective-permute-done | bytes 65568 | tf_op jit(solution)/shard_map/ppermute | solution.py:35
  33.5 0.1 collective-permute-start.9
  33.6 1.1 %collective-permute-start.10 = (bf16[128,128]{1,0:T(8,128)(2,1)S(1)}, bf16[128,128]{1,0:T(8,128)(2,1)S(1)}, u32[]{:S(2)}, u32[]{:S(2)}) collective-permute-start(bf16[128,128]{1,0:T(8,128)(2,1)S(1)} %get-tuple-element.56), channel_id=1, source_target_pairs={{0,8},{4,12},{8,0},{12,4},{1,9},{5,13},{9,1},{13,5},{2,10},{6,14},... | collective-permute-start | bytes 98312 | tf_op jit(solution)/shard_map/ppermute | solution.py:35
  34.7 0.1 maximum_maximum_fusion.1.refs_4_.sin_ref
  34.8 3.6 %collective-permute-done.10.refs_3_ = bf16[128,128]{1,0:T(8,128)(2,1)S(1)} collective-permute-done((bf16[128,128]{1,0:T(8,128)(2,1)S(1)}, bf16[128,128]{1,0:T(8,128)(2,1)S(1)}, u32[]{:S(2)}, u32[]{:S(2)}) %collective-permute-start.10) | collective-permute-done | bytes 32800 | tf_op jit(solution)/shard_map/ppermute | solution.py:35
  38.5 1.1 %collective-permute-start.11 = (bf16[256,128]{1,0:T(8,128)(2,1)S(1)}, bf16[256,128]{1,0:T(8,128)(2,1)S(1)}, u32[]{:S(2)}, u32[]{:S(2)}) collective-permute-start(bf16[256,128]{1,0:T(8,128)(2,1)S(1)} %get-tuple-element.57.refs_0_), channel_id=1, source_target_pairs={{0,8},{4,12},{8,0},{12,4},{1,9},{5,13},{9,1},{13,5},{2,10},{6,14},... | collective-permute-start | bytes 196616 | tf_op jit(solution)/shard_map/ppermute | solution.py:35
  39.6 1.9 %collective-permute-start.12 = (bf16[128,128]{1,0:T(8,128)(2,1)S(1)}, bf16[128,128]{1,0:T(8,128)(2,1)S(1)}, u32[]{:S(2)}, u32[]{:S(2)}) collective-permute-start(bf16[128,128]{1,0:T(8,128)(2,1)S(1)} %get-tuple-element.58.refs_2_), channel_id=1, source_target_pairs={{0,8},{4,12},{8,0},{12,4},{1,9},{5,13},{9,1},{13,5},{2,10},{6,14},... | collective-permute-start | bytes 98312 | tf_op jit(solution)/shard_map/ppermute | solution.py:35
  41.5 3.6 %collective-permute-done.12.refs_3_ = bf16[128,128]{1,0:T(8,128)(2,1)S(1)} collective-permute-done((bf16[128,128]{1,0:T(8,128)(2,1)S(1)}, bf16[128,128]{1,0:T(8,128)(2,1)S(1)}, u32[]{:S(2)}, u32[]{:S(2)}) %collective-permute-start.12) | collective-permute-done | bytes 32800 | tf_op jit(solution)/shard_map/ppermute | solution.py:35
  45.2 0.3 collective-permute-start.13
  45.5 1.8 %collective-permute-start.14 = (bf16[256,128]{1,0:T(8,128)(2,1)S(1)}, bf16[256,128]{1,0:T(8,128)(2,1)S(1)}, u32[]{:S(2)}, u32[]{:S(2)}) collective-permute-start(bf16[256,128]{1,0:T(8,128)(2,1)S(1)} %get-tuple-element.60.mine_b), channel_id=1, source_target_pairs={{0,4},{4,0},{8,12},{12,8},{1,5},{5,1},{9,13},{13,9},{2,6},{6,2},{1... | collective-permute-start | bytes 196616 | tf_op jit(solution)/shard_map/ppermute | solution.py:35
  47.3 3.6 %collective-permute-done.14.got_b = bf16[256,128]{1,0:T(8,128)(2,1)S(1)} collective-permute-done((bf16[256,128]{1,0:T(8,128)(2,1)S(1)}, bf16[256,128]{1,0:T(8,128)(2,1)S(1)}, u32[]{:S(2)}, u32[]{:S(2)}) %collective-permute-start.14) | collective-permute-done | bytes 65568 | tf_op jit(solution)/shard_map/ppermute | solution.py:35
  50.9 0.5 low_rank.1
  51.4 0.1 collective-permute-start.15
  51.5 1.3 %collective-permute-done.15.b_ref = bf16[544,128]{1,0:T(8,128)(2,1)S(1)} collective-permute-done((bf16[544,128]{1,0:T(8,128)(2,1)S(1)}, bf16[544,128]{1,0:T(8,128)(2,1)S(1)}, u32[]{:S(2)}, u32[]{:S(2)}) %collective-permute-start.15) | collective-permute-done | bytes 139296 | tf_op jit(solution)/shard_map/ppermute | solution.py:35
  52.9 0.6 collective-permute-start.16
  53.5 1.5 %collective-permute-start.20 = (bf16[512,128]{1,0:T(8,128)(2,1)S(1)}, bf16[512,128]{1,0:T(8,128)(2,1)S(1)}, u32[]{:S(2)}, u32[]{:S(2)}) collective-permute-start(bf16[512,128]{1,0:T(8,128)(2,1)S(1)} %get-tuple-element.67.mine_b), channel_id=1, source_target_pairs={{0,16},{16,0},{1,17},{17,1},{2,18},{18,2},{3,19},{19,3},{4,20},{20... | collective-permute-start | bytes 393224 | tf_op jit(solution)/shard_map/ppermute | solution.py:35
  55.0 0.5 collective-permute-start.17
  55.5 3.4 %collective-permute-done.17.b_ref = bf16[32,128]{1,0:T(8,128)(2,1)S(1)} collective-permute-done((bf16[32,128]{1,0:T(8,128)(2,1)S(1)}, bf16[32,128]{1,0:T(8,128)(2,1)S(1)}, u32[]{:S(2)}, u32[]{:S(2)}) %collective-permute-start.17) | collective-permute-done | bytes 8224 | tf_op jit(solution)/shard_map/ppermute | solution.py:35
  58.9 0.1 collective-permute-start.18
  59.0 1.2 %collective-permute-done.18.b_ref = bf16[32,128]{1,0:T(8,128)(2,1)S(1)} collective-permute-done((bf16[32,128]{1,0:T(8,128)(2,1)S(1)}, bf16[32,128]{1,0:T(8,128)(2,1)S(1)}, u32[]{:S(2)}, u32[]{:S(2)}) %collective-permute-start.18) | collective-permute-done | bytes 8224 | tf_op jit(solution)/shard_map/ppermute | solution.py:35
  60.2 0.0 copy-start
  60.2 0.0 copy-start.3
  60.2 1.6 %collective-permute-start.19 = (bf16[32,128]{1,0:T(8,128)(2,1)S(1)}, bf16[32,128]{1,0:T(8,128)(2,1)S(1)}, u32[]{:S(2)}, u32[]{:S(2)}) collective-permute-start(bf16[32,128]{1,0:T(8,128)(2,1)S(1)} %norm_merge.3.sn_ref), channel_id=1, source_target_pairs={{0,2},{1,3},{2,0},{3,1},{4,6},{5,7},{6,4},{7,5},{8,10},{9,11},{10,... | collective-permute-start | bytes 24584 | tf_op jit(solution)/shard_map/ppermute | solution.py:35
  61.8 0.5 base.1
  62.3 1.6 %collective-permute-done.19.rn_ref = bf16[32,128]{1,0:T(8,128)(2,1)S(1)} collective-permute-done((bf16[32,128]{1,0:T(8,128)(2,1)S(1)}, bf16[32,128]{1,0:T(8,128)(2,1)S(1)}, u32[]{:S(2)}, u32[]{:S(2)}) %collective-permute-start.19) | collective-permute-done | bytes 8224 | tf_op jit(solution)/shard_map/ppermute | solution.py:35
  63.9 1.8 %final.1 = (f32[1024,128]{1,0:T(8,128)}, f32[128,1024]{1,0:T(8,128)}, bf16[512,1024]{1,0:T(8,128)(2,1)}) custom-call(f32[512,1024]{1,0:T(8,128)S(1)} %get-tuple-element.62.base_ref, f32[512,128]{1,0:T(8,128)S(1)} %get-tuple-element.63.low_ref, f32[512,128]{1,0:T(8,128)S(1)} %get-tuple-element.64.scale_ref, bf16[544,128]{1,0:T(8,128)(2,1)S(1)} %merge.1.after_ref.s_ref, ...), custom_call_target="tpu_custom_call" | custom-call | tf_op jit(solution)/shard_map/final/pallas_call | solution.py:258
  (26 shorter events, 0.2 us)
Async XLA Ops:
  3.1 4.2 %collective-permute-start = (bf16[768,128]{1,0:T(8,128)(2,1)S(1)}, bf16[768,128]{1,0:T(8,128)(2,1)S(1)}, u32[]{:S(2)}, u32[]{:S(2)}) collective-permute-start(bf16[768,128]{1,0:T(8,128)(2,1)S(1)} %rank.1.x_ref), channel_id=1, source_target_pairs={{0,1},{1,0},{2,3},{3,2},{4,5},{5,4},{6,7},{7,6},{8,9},{9,8},{10,11... | collective-permute-start | bytes 589832 | tf_op jit(solution)/shard_map/ppermute | solution.py:35
  7.3 8.9 %collective-permute-start.1 = (bf16[544,1152]{1,0:T(8,128)(2,1)S(1)}, bf16[544,1152]{1,0:T(8,128)(2,1)S(1)}, u32[]{:S(2)}, u32[]{:S(2)}) collective-permute-start(bf16[544,1152]{1,0:T(8,128)(2,1)S(1)} %get-tuple-element.41.diag_ref), channel_id=1, source_target_pairs={{0,1},{1,0},{2,3},{3,2},{4,5},{5,4},{6,7},{7,6},{8,9},{9,8},{10,11... | collective-permute-start | bytes 3760136 | tf_op jit(solution)/shard_map/ppermute | solution.py:35
  7.5 8.1 %collective-permute-start.2 = (bf16[768,128]{1,0:T(8,128)(2,1)S(1)}, bf16[768,128]{1,0:T(8,128)(2,1)S(1)}, u32[]{:S(2)}, u32[]{:S(2)}) collective-permute-start(bf16[768,128]{1,0:T(8,128)(2,1)S(1)} %get-tuple-element.39.after_ref.s_ref), channel_id=1, source_target_pairs={{0,2},{1,3},{2,0},{3,1},{4,6},{5,7},{6,4},{7,5},{8,10},{9,11},{10,... | collective-permute-start | bytes 589832 | tf_op jit(solution)/shard_map/ppermute | solution.py:35
  10.4 5.1 %copy-start.1 = (bf16[384,1024]{1,0:T(8,128)(2,1)S(1)}, bf16[384,1024]{1,0:T(8,128)(2,1)}, u32[]{:S(2)}) copy-start(bf16[384,1024]{1,0:T(8,128)(2,1)} %x_ref.1) | copy-start | bytes 2359300
  10.4 5.1 %copy-start.2 = (bf16[384,1024]{1,0:T(8,128)(2,1)S(1)}, bf16[384,1024]{1,0:T(8,128)(2,1)}, u32[]{:S(2)}) copy-start(bf16[384,1024]{1,0:T(8,128)(2,1)} %v_ref.1) | copy-start | bytes 2359300
  10.4 5.1 %copy-start.4 = (s32[256]{0:T(256)S(1)}, s32[256]{0:T(256)}, u32[]{:S(2)}) copy-start(s32[256]{0:T(256)} %param.15) | copy-start | bytes 3076
  16.6 45.2 %collective-permute-start.4 = (bf16[544,1152]{1,0:T(8,128)(2,1)S(1)}, bf16[544,1152]{1,0:T(8,128)(2,1)S(1)}, u32[]{:S(2)}, u32[]{:S(2)}) collective-permute-start(bf16[544,1152]{1,0:T(8,128)(2,1)S(1)} %get-tuple-element.44.after_ref.far_ref), channel_id=1, source_target_pairs={{0,2},{1,3},{2,0},{3,1},{4,6},{5,7},{6,4},{7,5},{8,10},{9,11},{10,... | collective-permute-start | bytes 3760136 | tf_op jit(solution)/shard_map/ppermute | solution.py:35
  18.4 6.8 %collective-permute-start.5 = (bf16[512,128]{1,0:T(8,128)(2,1)S(1)}, bf16[512,128]{1,0:T(8,128)(2,1)S(1)}, u32[]{:S(2)}, u32[]{:S(2)}) collective-permute-start(bf16[512,128]{1,0:T(8,128)(2,1)S(1)} %get-tuple-element.42.after_ref), channel_id=1, source_target_pairs={{0,4},{4,0},{8,12},{12,8},{1,5},{5,1},{9,13},{13,9},{2,6},{6,2},{1... | collective-permute-start | bytes 393224 | tf_op jit(solution)/shard_map/ppermute | solution.py:35
  20.0 5.2 %collective-permute-start.6 = (bf16[512,128]{1,0:T(8,128)(2,1)S(1)}, bf16[512,128]{1,0:T(8,128)(2,1)S(1)}, u32[]{:S(2)}, u32[]{:S(2)}) collective-permute-start(bf16[512,128]{1,0:T(8,128)(2,1)S(1)} %get-tuple-element.48), channel_id=1, source_target_pairs={{0,16},{16,0},{1,17},{17,1},{2,18},{18,2},{3,19},{19,3},{4,20},{20... | collective-permute-start | bytes 393224 | tf_op jit(solution)/shard_map/ppermute | solution.py:35
  21.5 40.3 %collective-permute-start.3 = (bf16[512,1024]{1,0:T(8,128)(2,1)S(1)}, bf16[512,1024]{1,0:T(8,128)(2,1)S(1)}, u32[]{:S(2)}, u32[]{:S(2)}) collective-permute-start(bf16[512,1024]{1,0:T(8,128)(2,1)S(1)} %get-tuple-element.45), channel_id=1, source_target_pairs={{0,1},{1,0},{2,3},{3,2},{4,5},{5,4},{6,7},{7,6},{8,9},{9,8},{10,11... | collective-permute-start | bytes 3145736 | tf_op jit(solution)/shard_map/ppermute | solution.py:35
  25.3 6.9 %collective-permute-start.7 = (bf16[256,128]{1,0:T(8,128)(2,1)S(1)}, bf16[256,128]{1,0:T(8,128)(2,1)S(1)}, u32[]{:S(2)}, u32[]{:S(2)}) collective-permute-start(bf16[256,128]{1,0:T(8,128)(2,1)S(1)} %get-tuple-element.50), channel_id=1, source_target_pairs={{0,8},{4,12},{8,0},{12,4},{1,9},{5,13},{9,1},{13,5},{2,10},{6,14},... | collective-permute-start | bytes 196616 | tf_op jit(solution)/shard_map/ppermute | solution.py:35
  28.0 5.5 %collective-permute-start.8 = (bf16[256,128]{1,0:T(8,128)(2,1)S(1)}, bf16[256,128]{1,0:T(8,128)(2,1)S(1)}, u32[]{:S(2)}, u32[]{:S(2)}) collective-permute-start(bf16[256,128]{1,0:T(8,128)(2,1)S(1)} %get-tuple-element.52), channel_id=1, source_target_pairs={{0,4},{4,0},{8,12},{12,8},{1,5},{5,1},{9,13},{13,9},{2,6},{6,2},{1... | collective-permute-start | bytes 196616 | tf_op jit(solution)/shard_map/ppermute | solution.py:35
  33.5 5.0 %collective-permute-start.9 = (bf16[256,128]{1,0:T(8,128)(2,1)S(1)}, bf16[256,128]{1,0:T(8,128)(2,1)S(1)}, u32[]{:S(2)}, u32[]{:S(2)}) collective-permute-start(bf16[256,128]{1,0:T(8,128)(2,1)S(1)} %get-tuple-element.54.refs_0_), channel_id=1, source_target_pairs={{0,16},{16,0},{1,17},{17,1},{2,18},{18,2},{3,19},{19,3},{4,20},{20... | collective-permute-start | bytes 196616 | tf_op jit(solution)/shard_map/ppermute | solution.py:35
  33.6 4.8 %collective-permute-start.10 = (bf16[128,128]{1,0:T(8,128)(2,1)S(1)}, bf16[128,128]{1,0:T(8,128)(2,1)S(1)}, u32[]{:S(2)}, u32[]{:S(2)}) collective-permute-start(bf16[128,128]{1,0:T(8,128)(2,1)S(1)} %get-tuple-element.56), channel_id=1, source_target_pairs={{0,8},{4,12},{8,0},{12,4},{1,9},{5,13},{9,1},{13,5},{2,10},{6,14},... | collective-permute-start | bytes 98312 | tf_op jit(solution)/shard_map/ppermute | solution.py:35
  38.5 6.6 %collective-permute-start.11 = (bf16[256,128]{1,0:T(8,128)(2,1)S(1)}, bf16[256,128]{1,0:T(8,128)(2,1)S(1)}, u32[]{:S(2)}, u32[]{:S(2)}) collective-permute-start(bf16[256,128]{1,0:T(8,128)(2,1)S(1)} %get-tuple-element.57.refs_0_), channel_id=1, source_target_pairs={{0,8},{4,12},{8,0},{12,4},{1,9},{5,13},{9,1},{13,5},{2,10},{6,14},... | collective-permute-start | bytes 196616 | tf_op jit(solution)/shard_map/ppermute | solution.py:35
  39.6 5.5 %collective-permute-start.12 = (bf16[128,128]{1,0:T(8,128)(2,1)S(1)}, bf16[128,128]{1,0:T(8,128)(2,1)S(1)}, u32[]{:S(2)}, u32[]{:S(2)}) collective-permute-start(bf16[128,128]{1,0:T(8,128)(2,1)S(1)} %get-tuple-element.58.refs_2_), channel_id=1, source_target_pairs={{0,8},{4,12},{8,0},{12,4},{1,9},{5,13},{9,1},{13,5},{2,10},{6,14},... | collective-permute-start | bytes 98312 | tf_op jit(solution)/shard_map/ppermute | solution.py:35
  45.2 5.7 %collective-permute-start.13 = (bf16[512,128]{1,0:T(8,128)(2,1)S(1)}, bf16[512,128]{1,0:T(8,128)(2,1)S(1)}, u32[]{:S(2)}, u32[]{:S(2)}) collective-permute-start(bf16[512,128]{1,0:T(8,128)(2,1)S(1)} %get-tuple-element.59.mine_a), channel_id=1, source_target_pairs={{0,4},{4,0},{8,12},{12,8},{1,5},{5,1},{9,13},{13,9},{2,6},{6,2},{1... | collective-permute-start | bytes 393224 | tf_op jit(solution)/shard_map/ppermute | solution.py:35
  45.5 5.4 %collective-permute-start.14 = (bf16[256,128]{1,0:T(8,128)(2,1)S(1)}, bf16[256,128]{1,0:T(8,128)(2,1)S(1)}, u32[]{:S(2)}, u32[]{:S(2)}) collective-permute-start(bf16[256,128]{1,0:T(8,128)(2,1)S(1)} %get-tuple-element.60.mine_b), channel_id=1, source_target_pairs={{0,4},{4,0},{8,12},{12,8},{1,5},{5,1},{9,13},{13,9},{2,6},{6,2},{1... | collective-permute-start | bytes 196616 | tf_op jit(solution)/shard_map/ppermute | solution.py:35
  51.4 1.4 %collective-permute-start.15 = (bf16[544,128]{1,0:T(8,128)(2,1)S(1)}, bf16[544,128]{1,0:T(8,128)(2,1)S(1)}, u32[]{:S(2)}, u32[]{:S(2)}) collective-permute-start(bf16[544,128]{1,0:T(8,128)(2,1)S(1)} %get-tuple-element.61.a_ref), channel_id=1, source_target_pairs={{0,1},{1,0},{2,3},{3,2},{4,5},{5,4},{6,7},{7,6},{8,9},{9,8},{10,11... | collective-permute-start | bytes 417800 | tf_op jit(solution)/shard_map/ppermute | solution.py:35
  52.9 11.0 %collective-permute-start.16 = (bf16[544,128]{1,0:T(8,128)(2,1)S(1)}, bf16[544,128]{1,0:T(8,128)(2,1)S(1)}, u32[]{:S(2)}, u32[]{:S(2)}) collective-permute-start(bf16[544,128]{1,0:T(8,128)(2,1)S(1)} %merge.1.after_ref.s_ref), channel_id=1, source_target_pairs={{0,2},{1,3},{2,0},{3,1},{4,6},{5,7},{6,4},{7,5},{8,10},{9,11},{10,... | collective-permute-start | bytes 417800 | tf_op jit(solution)/shard_map/ppermute | solution.py:35
  53.5 10.5 %collective-permute-start.20 = (bf16[512,128]{1,0:T(8,128)(2,1)S(1)}, bf16[512,128]{1,0:T(8,128)(2,1)S(1)}, u32[]{:S(2)}, u32[]{:S(2)}) collective-permute-start(bf16[512,128]{1,0:T(8,128)(2,1)S(1)} %get-tuple-element.67.mine_b), channel_id=1, source_target_pairs={{0,16},{16,0},{1,17},{17,1},{2,18},{18,2},{3,19},{19,3},{4,20},{20... | collective-permute-start | bytes 393224 | tf_op jit(solution)/shard_map/ppermute | solution.py:35
  55.0 3.9 %collective-permute-start.17 = (bf16[32,128]{1,0:T(8,128)(2,1)S(1)}, bf16[32,128]{1,0:T(8,128)(2,1)S(1)}, u32[]{:S(2)}, u32[]{:S(2)}) collective-permute-start(bf16[32,128]{1,0:T(8,128)(2,1)S(1)} %get-tuple-element.65.a_ref), channel_id=1, source_target_pairs={{0,16},{16,0},{1,17},{17,1},{2,18},{18,2},{3,19},{19,3},{4,20},{20... | collective-permute-start | bytes 24584 | tf_op jit(solution)/shard_map/ppermute | solution.py:35
  58.9 1.2 %collective-permute-start.18 = (bf16[32,128]{1,0:T(8,128)(2,1)S(1)}, bf16[32,128]{1,0:T(8,128)(2,1)S(1)}, u32[]{:S(2)}, u32[]{:S(2)}) collective-permute-start(bf16[32,128]{1,0:T(8,128)(2,1)S(1)} %norm_merge.2.a_ref), channel_id=1, source_target_pairs={{0,1},{1,0},{2,3},{3,2},{4,5},{5,4},{6,7},{7,6},{8,9},{9,8},{10,11... | collective-permute-start | bytes 24584 | tf_op jit(solution)/shard_map/ppermute | solution.py:35
  60.2 3.7 %copy-start = (f32[1024,128]{1,0:T(8,128)S(1)}, f32[1024,128]{1,0:T(8,128)}, u32[]{:S(2)}) copy-start(f32[1024,128]{1,0:T(8,128)} %a_ref.1) | copy-start | bytes 1572868
  60.2 3.7 %copy-start.3 = (f32[128,1024]{1,0:T(8,128)S(1)}, f32[128,1024]{1,0:T(8,128)}, u32[]{:S(2)}) copy-start(f32[128,1024]{1,0:T(8,128)} %b_ref.1) | copy-start | bytes 1572868
  60.2 3.7 %collective-permute-start.19 = (bf16[32,128]{1,0:T(8,128)(2,1)S(1)}, bf16[32,128]{1,0:T(8,128)(2,1)S(1)}, u32[]{:S(2)}, u32[]{:S(2)}) collective-permute-start(bf16[32,128]{1,0:T(8,128)(2,1)S(1)} %norm_merge.3.sn_ref), channel_id=1, source_target_pairs={{0,2},{1,3},{2,0},{3,1},{4,6},{5,7},{6,4},{7,5},{8,10},{9,11},{10,... | collective-permute-start | bytes 24584 | tf_op jit(solution)/shard_map/ppermute | solution.py:35

commit v7 on v6

--- a/solution.py
+++ b/solution.py
@@ -81,13 +81,12 @@
     return sources, [w_ref.at[i] for i in range(len(sources))]
 
 
-def prep_kernel(h_hbm, gain_hbm, a_hbm, w_hbm, hg_ref, wide_ref, h_ref, gain_ref, a_ref, w_ref, sems):
+def prep_kernel(h_hbm, gain_hbm, a_hbm, hg_ref, pack_ref, h_ref, gain_ref, a_ref, sems):
     count, width = h_ref.shape
     blocks = blocks_of(count)
-    sources, targets = weight_blocks((3,), w_hbm, w_ref)
     copies = fetch(
-        [gain_hbm] + [h_hbm.at[b] for b in blocks] + [a_hbm] + sources,
-        [gain_ref] + [h_ref.at[b] for b in blocks] + [a_ref] + targets,
+        [gain_hbm] + [h_hbm.at[b] for b in blocks] + [a_hbm],
+        [gain_ref] + [h_ref.at[b] for b in blocks] + [a_ref],
         sems,
     )
     copies[0].wait()
@@ -100,28 +99,28 @@
         rows.append(jnp.broadcast_to(sums, (LANES, LANES)).T[0:1])
     if len(rows) < 8:
         rows.append(jnp.zeros((8 - len(rows), LANES), F32))
-    wide_ref[count:, width:] = split_terms(jnp.concatenate(rows, axis=0))
-    wide_ref[count:, :width] = jnp.zeros((EXTRA, width), BF)
-    copies[1 + len(blocks)].wait()
-    wide_ref[:count, width:] = dot(hg_ref[...], a_ref[...].astype(BF)).astype(BF)
-    cut = w_ref.shape[2]
-    for i in range(width // cut):
-        copies[2 + len(blocks) + i].wait()
-        wide_ref[:count, i * cut : (i + 1) * cut] = dot(hg_ref[...], w_ref[i]).astype(BF)
-
-
-def part_kernel(x_ref, got_ref, pass_ref, out_ref, pass_out):
+    pack_ref[count:] = split_terms(jnp.concatenate(rows, axis=0))
+    copies[-1].wait()
+    pack_ref[:count] = dot(hg_ref[...], a_ref[...].astype(BF)).astype(BF)
+
+
+def part_kernel(x_ref, got_ref, after_ref, out_ref):
     sum_kernel(x_ref, got_ref, out_ref)
 
 
-def query_kernel(peers, hg_ref, w_hbm, after_ref, *rest):
+def query_kernel(peers, hg_ref, w_hbm, pack_ref, after_ref, *rest):
     outs, (w_ref, sems) = rest[:-2], rest[-2:]
     _, width, cut = w_ref.shape
     copies = fetch(*weight_blocks(peers, w_hbm, w_ref), sems)
+    count = hg_ref.shape[0]
+    if outs[0].shape[0] > count:
+        outs[0][count:, :width] = jnp.zeros((EXTRA, width), BF)
+        outs[0][:, width:] = pack_ref[...]
     per = width // cut
     for i, copy in enumerate(copies):
         copy.wait()
-        outs[i // per][:, i % per * cut : (i % per + 1) * cut] = dot(hg_ref[...], w_ref[i]).astype(BF)
+        block = dot(hg_ref[...], w_ref[i]).astype(BF)
+        outs[i // per][:count, i % per * cut : (i % per + 1) * cut] = block
 
 
 def far_kernel(mine_ref, diag_ref, got_ref, after_ref, pass_ref, out_ref, pass_out):
@@ -155,7 +154,14 @@
     out_ref[other] = got_ref[...]
 
 
-def grad_kernel(axes, x_ref, v_ref, s_ref, r_ref, pos_ref, keep_a, send_a, keep_b, send_b, pos_out, ga, gb):
+def join_some(axis, bit, mine_ref, got_ref, out_ref):
+    size = mine_ref.shape[0] - EXTRA
+    mine, other = halves(axis, bit, size)
+    out_ref[mine] = mine_ref[:size]
+    out_ref[other] = got_ref[:size]
+
+
+def grad_kernel(axes, x_ref, v_ref, s_ref, r_ref, pass_ref, keep_a, send_a, keep_b, send_b, pass_out, ga, gb):
     count, width = x_ref.shape
     low = (s_ref[...].astype(F32) + r_ref[...].astype(F32)).astype(BF)
     ga[...] = SCALE * dot(x_ref[...], low[count:], ((0,), (0,)))
@@ -164,44 +170,64 @@
     for b in blocks_of(width):
         gb[b] = turned[:, b]
     halve(*axes[1], gb, keep_b, send_b)
-    pos_out[...] = pos_ref[...].astype(F32)
 
 
 def sum_kernel(keep_ref, got_ref, out_ref):
     out_ref[...] = (keep_ref[...].astype(F32) + got_ref[...].astype(F32)).astype(BF)
 
 
-def step_kernel(steps, *refs):
-    n = len(steps)
-    ins, outs = refs[: 2 * n], list(refs[2 * n + 1 :])
-    for i, (kind, axis, bit) in enumerate(steps):
-        mine, got = ins[2 * i], ins[2 * i + 1]
+def tree_sum(values):
+    while len(values) > 1:
+        values = [a + b for a, b in zip(values[::2], values[1::2])]
+    return values[0]
+
+
+def step_kernel(plan, *refs):
+    ins, refs = refs[: sum(n for _, n in plan)], refs[sum(n for _, n in plan) + 1 :]
+    ins, outs = list(ins), list(refs)
+    for (kind, axis, bit), n in plan:
+        mine, got, terms = ins[0], ins[1], ins[2:n]
+        ins = ins[n:]
         if kind == "halve":
             total = outs.pop()
             total[...] = mine[...] + got[...].astype(F32)
             halve(axis, bit, total, outs.pop(0), outs.pop(0))
         elif kind == "sum":
             sum_kernel(mine, got, outs.pop(0))
+        elif kind == "norm":
+            size = mine.shape[0]
+            total = mine[...] + got[...].astype(F32)
+            out, sums = outs.pop(0), outs.pop(0)
+            out[:size] = total.astype(BF)
+            sums[...] = split_terms(jnp.broadcast_to(jnp.sum(total * total), (8, LANES)))
+            out[size:] = sums[...]
+        elif kind == "join":
+            join(axis, bit, mine, got, outs.pop(0))
         else:
-            join(axis, bit, mine, got, outs.pop(0))
-
-
-def square_terms(ref):
+            out = outs.pop(0)
+            join_some(axis, bit, mine, got, out)
+            half = len(terms) // 2
+            near = tree_sum([join_terms(mine[-EXTRA:])] + [join_terms(t[...]) for t in terms[:half]])
+            far = tree_sum([join_terms(got[-EXTRA:])] + [join_terms(t[...]) for t in terms[half:]])
+            out[-EXTRA:] = split_terms(near + far)
+
+
+def place_kernel(pos_ref, after_ref, out_ref):
+    out_ref[...] = pos_ref[...].astype(F32)
+
+
+def square_sum(ref):
     x = ref[...].astype(F32)
-    return split_terms(jnp.broadcast_to(jnp.sum(x * x), (8, LANES)))
-
-
-def low_kernel(axis, bit, hg_ref, mine_a, got_a, mine_b, got_b, pack_ref, ga_ref, gb_ref, norm_ref):
+    return jnp.broadcast_to(jnp.sum(x * x), (8, LANES))
+
+
+def low_kernel(axis, bit, hg_ref, mine_a, got_a, mine_b, got_b, pack_ref, ga_ref, gb_ref):
     join(axis, bit, mine_a, got_a, ga_ref)
     count = hg_ref.shape[0]
     pack_ref[:count] = dot(hg_ref[...], ga_ref[...]).astype(BF)
-    pack_ref[count:] = square_terms(ga_ref)
-    join(axis, bit, mine_b, got_b, gb_ref)
-    norm_ref[...] = square_terms(gb_ref)
-
-
-def norm_merge_kernel(a_ref, b_ref, out_ref):
-    out_ref[...] = split_terms(join_terms(a_ref[...]) + join_terms(b_ref[...]))
+    join_some(axis, bit, mine_b, got_b, gb_ref)
+    total = square_sum(ga_ref) + (join_terms(mine_b[-EXTRA:]) + join_terms(got_b[-EXTRA:]))
+    pack_ref[count:] = split_terms(total)
 
 
 def base_kernel(mine_ref, near_ref, far_ref, far_got, after_ref, base_ref, low_ref, scale_ref):
@@ -218,13 +244,12 @@
 
 
 def final_kernel(
-    axis, bit, base_ref, low_ref, scale_ref, s_ref, r_ref, sn_ref, rn_ref, ga_ref, mine_b, got_b, a_ref, b_ref,
+    axis, bit, base_ref, low_ref, scale_ref, s_ref, r_ref, ga_ref, mine_b, got_b, a_ref, b_ref,
     cos_ref, sin_ref, a_hbm, b_hbm, q_hbm, gb_ref, new_a, new_b, half_b, out, sems,
 ):
     join(axis, bit, mine_b, got_b, gb_ref)
     count, width = base_ref.shape
     total = join_terms(s_ref[count:]) + join_terms(r_ref[count:])
-    total = total + (join_terms(sn_ref[...]) + join_terms(rn_ref[...]))
     rate = (LEARN * lax.rsqrt(total + NORM_EPS))[0:1]
     for c in blocks_of(width):
         fresh = b_ref[:, c] - rate * gb_ref[c].astype(F32)
@@ -297,6 +322,17 @@
         return list(zip(ways, after + [("join",) + way for way in down[::-1]]))
 
     path_a, path_b = path(z_bits, x_bits), path(x_bits + z_bits, [])
+    whole_b = len(x_bits + z_bits) - 1
+    path_b = [
+        (way, ("norm", None, None) if i == whole_b else ("join_norm",) + step[1:] if whole_b < i < len(path_a) else step)
+        for i, (way, step) in enumerate(path_b)
+    ]
+
+    def others(x, axis, bit):
+        pairs = lambda kx, kz: [
+            (i, ((i // n_roll) ^ kx) * n_roll + ((i % n_roll) ^ kz)) for i in range(n_dp * n_roll)
+        ]
+        return [lax.ppermute(x, ("dp", "roll"), pairs(kx, kz)) for kz in (0, 1 << bit) for kx in range(1, n_dp)]
 
     def on_device(
         train_inputs, train_cotangent, factor_a, factor_b, base_weight, incoming, norm_gain, positions
@@ -321,49 +357,43 @@
         cut = 512
         wide = shape((count + EXTRA, width + rank), BF)
         tall = shape((count, width), BF)
-        gained, diag = call(
+        gained, pack = call(
             prep_kernel,
-            [tall, wide],
-            [HBM] * 4,
-            tuple(map(keep_hbm, (incoming.reshape(count, width), norm_gain[None, :], factor_a, base_weight))),
+            [tall, shape((count + EXTRA, rank), BF)],
+            [HBM] * 3,
+            tuple(map(keep_hbm, (incoming.reshape(count, width), norm_gain[None, :], factor_a))),
             "prep",
             [pltpu.VMEM((count, width), BF), pltpu.VMEM((1, width), F32), pltpu.VMEM(factor_a.shape, F32),
-             pltpu.VMEM((width // cut, width, cut), BF), dma(2 + count // LANES + width // cut)],
-        )
-        part_sum, diag = call(
-            part_kernel,
-            [shape(part.shape, BF), wide],
-            [VMEM] * 2 + [ANY],
-            (part, part_got, diag),
-            "part_sum",
-            out_specs=[VMEM, ANY],
-            aliases={2: 1},
-        )
+             dma(2 + count // LANES)],
+        )
+        part_sum = call(part_kernel, shape(part.shape, BF), [VMEM] * 2 + [ANY], (part, part_got, pack), "part_sum")
         part_far = swap(part_sum, "tp", n_tp, 2)
-        diag_got = swap(diag, "tp", n_tp, 1)
-
-        def query(peers, after, name):
+
+        def query(peers, outs, after, name):
             blocks = len(peers) * width // cut
             return call(
                 functools.partial(query_kernel, peers),
-                [tall] * len(peers),
-                [VMEM, HBM, ANY],
-                (gained, keep_hbm(base_weight), after),
+                outs,
+                [VMEM, HBM, VMEM, ANY],
+                (gained, keep_hbm(base_weight), pack, after),
                 name,
                 [pltpu.VMEM((blocks, width, cut), BF), dma(blocks)],
             )
 
-        distant, beside = query((2, 1), part_sum, "query_first")
-        pos = positions.reshape(-1, LANES)
+        diag, distant = query((3, 2), [wide, tall], part_sum, "query_far")
         half = width // 2
-        keep_a, send_a, keep_b, send_b, places = call(
+        keep_a, send_a, keep_b, send_b, diag = call(
             functools.partial(grad_kernel, (path_a[0][0], path_b[0][0])),
-            [shape((half, rank), F32), shape((half, rank), BF)] * 2 + [shape(pos.shape, F32)],
-            [VMEM] * 5,
-            (train_inputs, train_cotangent, part_sum, part_far, pos),
+            [shape((half, rank), F32), shape((half, rank), BF)] * 2 + [wide],
+            [VMEM] * 4 + [ANY],
+            (train_inputs, train_cotangent, part_sum, part_far, diag),
             "grads",
             [vmem(width), vmem(width)],
-        )
+            out_specs=[VMEM] * 4 + [ANY],
+            aliases={4: 4},
+        )
+        diag_got = swap(diag, "tp", n_tp, 1)
+        (beside,) = query((1,), [tall], send_a, "query_beside")
         far, beside = call(
             far_kernel,
             [wide, tall],
@@ -375,46 +405,52 @@
         )
         far_got = swap(far, "tp", n_tp, 2)
         beside_got = swap(beside, "tp", n_tp, 1)
-        (close,) = query((0,), far, "query_close")
-        cos, sin = turn_tables(places.reshape(rows), steps)
-
-        def step_call(steps, after, name):
+        def step_call(parts, after, name):
             ins, outs, scratch = [], [], []
-            for (kind, _, _), mine, got in steps:
-                size = mine.shape[0]
-                ins += [mine, got]
+            for (kind, _, _), arrays in parts:
+                size = arrays[0].shape[0]
+                ins += arrays
                 if kind == "halve":
                     outs += [shape((size // 2, rank), F32), shape((size // 2, rank), BF)]
                     scratch.append(vmem(size))
+                elif kind == "norm":
+                    outs += [shape((size + EXTRA, rank), BF), shape((EXTRA, rank), BF)]
                 else:
-                    outs.append(shape((2 * size if kind == "join" else size, rank), BF))
-            made = call(
-                functools.partial(step_kernel, [step[0] for step in steps]),
-                outs,
-                [VMEM] * len(ins) + [ANY],
-                (*ins, after),
-                name,
-                scratch,
+                    size = {"sum": size, "join": 2 * size, "join_norm": 2 * size - EXTRA}[kind]
+                    outs.append(shape((size, rank), BF))
+            made = list(
+                call(
+                    functools.partial(step_kernel, [(step, len(arrays)) for step, arrays in parts]),
+                    outs,
+                    [VMEM] * len(ins) + [ANY],
+                    (*ins, after),
+                    name,
+                    scratch,
+                )
             )
-            made, states = list(made), []
-            for (kind, _, _), _, _ in steps:
-                states.append((made.pop(0), made.pop(0)) if kind == "halve" else (made[0], made.pop(0)))
-            return states
-
-        state_a, state_b = (keep_a, send_a), (keep_b, send_b)
+            return [[made.pop(0) for _ in range(1 + (step[0] in ("halve", "norm")))] for step, _ in parts]
+
+        state_a, state_b, sums = [keep_a, send_a], [keep_b, send_b], []
         for i, ((way_a, step_a), (way_b, step_b)) in enumerate(zip(path_a[:-1], path_b)):
-            got_a, got_b = cross(state_a[1], *way_a), cross(state_b[1], *way_b)
-            after = close if i == 0 else cos if i == 1 else sin
-            state_a, state_b = step_call(
-                [(step_a, state_a[0], got_a), (step_b, state_b[0], got_b)], after, f"step_{i}"
-            )
+            arrays_a = [state_a[0], cross(state_a[-1], *way_a)]
+            arrays_b = [state_b[0], cross(state_b[-1], *way_b)] + sums
+            after = far if i == 0 else close if i == 1 else sin if i == 2 else far
+            state_a, state_b = step_call([(step_a, arrays_a), (step_b, arrays_b)], after, f"step_{i}")
+            sums = []
+            if step_b[0] == "norm":
+                sums = others(state_b.pop(), *path_b[i + 1][0])
+            if i == 0:
+                (close,) = query((0,), [tall], state_a[-1], "query_close")
+            if i == 1:
+                pos = positions.reshape(-1, LANES)
+                places = call(place_kernel, shape(pos.shape, F32), [VMEM, ANY], (pos, state_a[-1]), "places")
+                cos, sin = turn_tables(places.reshape(rows), steps)
         way = path_a[-1][0]
-        mine_a, mine_b = state_a[1], state_b[1]
+        mine_a, mine_b = state_a[-1], state_b[-1]
         got_a, got_b = cross(mine_a, *way), cross(mine_b, *way)
-        step_pack, grad_a, mine_b, norm = call(
+        step_pack, grad_a, mine_b = call(
             functools.partial(low_kernel, *way),
-            [shape((count + EXTRA, rank), BF), shape((width, rank), BF), shape((2 * mine_b.shape[0], rank), BF),
-             shape((EXTRA, LANES), BF)],
+            [shape((count + EXTRA, rank), BF), shape((width, rank), BF), shape((2 * (mine_b.shape[0] - EXTRA), rank), BF)],
             [VMEM] * 5,
             (gained, mine_a, got_a, mine_b, got_b),
             "low_rank",
@@ -424,16 +460,9 @@
         step_far = swap(step_sum, "tp", n_tp, 2)
 
         for (axis, bit), step in path_b[len(path_a) : -1]:
-            ((_, mine_b),) = step_call([(step, mine_b, cross(mine_b, axis, bit))], step_pack, "join_b")
+            ((mine_b,),) = step_call([(step, [mine_b, cross(mine_b, axis, bit)])], step_pack, "join_b")
         got_b = cross(mine_b, *path_b[-1][0])
 
-        def norm_add(x, y):
-            return call(norm_merge_kernel, shape((EXTRA, LANES), BF), [VMEM] * 2, (x, y), "norm_merge")
-
-        for way in x_bits:
-            norm = norm_add(norm, cross(norm, *way))
-        norm = norm_add(norm, swap(norm, "tp", n_tp, 1))
-        norm_far = swap(norm, "tp", n_tp, 2)
         base, low, scale = call(
             base_kernel,
             [shape((count, width), F32), shape((count, rank), F32), shape((count, LANES), F32)],
@@ -444,8 +473,8 @@
         new_a, new_b, queries = call(
             functools.partial(final_kernel, *path_b[-1][0]),
             [shape((width, rank), F32), shape((rank, width), F32), tall],
-            [VMEM] * 14,
-            (base, low, scale, step_sum, step_far, norm, norm_far, grad_a, mine_b, got_b, factor_a, factor_b, cos, sin),
+            [VMEM] * 12,
+            (base, low, scale, step_sum, step_far, grad_a, mine_b, got_b, factor_a, factor_b, cos, sin),
             "final",
             [vmem(width, BF), pltpu.VMEM((width, rank), F32), pltpu.VMEM((rank, width), F32),
              pltpu.VMEM((rank, width), BF), pltpu.VMEM((count, width), BF), dma(2 + count // LANES)],

time: 65.9 us -> 65.1 us (0.988)
  waiting for transfers between devices: 24.3 us -> 21.7 us
  Pallas kernels: 17.1 us -> 18.4 us
    ppermute x21 -> x18, waiting for transfers between devices: 24.3 us -> 14.6 us  [swap(): return lax.ppermute(x, axis, [(i, i ^ k) for i in range(n)])]
    ppermute x0 -> x2, waiting for transfers between devices: none -> 7.1 us  [others(): lax.ppermute(x, ('dp', 'roll'), pairs(kx, kz))]
    ppermute x0 -> x2, starting transfers between devices: none -> 2.16 us  [others(): lax.ppermute(x, ('dp', 'roll'), pairs(kx, kz))]
    ppermute x21 -> x18, starting transfers between devices: 22.2 us -> 20.5 us  [swap(): return lax.ppermute(x, axis, [(i, i ^ k) for i in range(n)])]
    pallas_call x17, Pallas kernels: 17.1 us -> 18.4 us  [call(): pl.pallas_call(kernel, out_shape=outs, in_specs=in_specs, out_specs=out_s...]
    cos x0 -> x1, other arithmetic: none -> 0.99 us  [turn_tables(): c, s = (jnp.cos(angle), jnp.sin(angle))]
    neg x1 -> x0, other arithmetic: 0.99 us -> none  [turn_tables(): sin.append(jnp.concatenate([-s, s], axis=-1))]
  transfers between devices with their start and end apart: 21 -> 20, of which waited for: 10 -> 9; matrix products, arithmetic and copies ran while one was open for 2% -> 2% of each run, Pallas kernels for 19% -> 21%
where the time goes in v7:
time: 65.1 us; the launch traced here: 64.9 us
  starting transfers between devices  22.6 us (35%)
  waiting for transfers between devices  21.7 us (33%)
  Pallas kernels  18.4 us (28%)
  other arithmetic  1.28 us (2%)
  between operations  0.83 us (1%)
    ppermute x18, starting transfers between devices, swap(): return lax.ppermute(x, axis, [(i, i ^ k) for i in range(n)])  20.5 us
    pallas_call x17, Pallas kernels, call(): pl.pallas_call(kernel, out_shape=outs, in_specs=in_specs, out_specs=out_s...  18.4 us
    ppermute x18, waiting for transfers between devices, swap(): return lax.ppermute(x, axis, [(i, i ^ k) for i in range(n)])  14.6 us
    ppermute x2, waiting for transfers between devices, others(): lax.ppermute(x, ('dp', 'roll'), pairs(kx, kz))  7.1 us
    ppermute x2, starting transfers between devices, others(): lax.ppermute(x, ('dp', 'roll'), pairs(kx, kz))  2.16 us
  transfers between devices with their start and end apart: 20, of which 9 were waited for; matrix products, arithmetic and copies ran while one was open for 2% of the time, Pallas kernels for 21%

profile of v7, /device:TPU:0, one launch (start us, length us, event | category | flops | bytes accessed | tf_op | source)
XLA Modules:
  0.0 64.9 jit_solution(1137181860454758473)
XLA Ops:
  0.6 2.4 %rank.1.x_ref = bf16[768,128]{1,0:T(8,128)(2,1)S(1)} custom-call(bf16[384,1024]{1,0:T(8,128)(2,1)} %x_ref.1, bf16[384,1024]{1,0:T(8,128)(2,1)} %v_ref.1, f32[1024,128]{1,0:T(8,128)} %a_ref.1, f32[128,1024]{1,0:T(8,128)} %b_ref.1), custom_call_target="tpu_custom_call" | custom-call | tf_op jit(solution)/shard_map/rank/pallas_call | solution.py:283
  3.1 0.5 collective-permute-start
  3.6 2.2 %prep.1 = (bf16[512,1024]{1,0:T(8,128)(2,1)S(1)}, bf16[544,128]{1,0:T(8,128)(2,1)S(1)}) custom-call(bf16[512,1024]{1,0:T(8,128)(2,1)} %bitcast.8, f32[1,1024]{1,0:T(1,128)} %bitcast.9, f32[1024,128]{1,0:T(8,128)} %a_ref.1), custom_call_target="tpu_custom_call" | custom-call | tf_op jit(solution)/shard_map/prep/pallas_call | solution.py:283
  5.9 2.6 %collective-permute-start.1 = (bf16[768,128]{1,0:T(8,128)(2,1)S(1)}, bf16[768,128]{1,0:T(8,128)(2,1)S(1)}, u32[]{:S(2)}, u32[]{:S(2)}) collective-permute-start(bf16[768,128]{1,0:T(8,128)(2,1)S(1)} %part_sum.1.after_ref.s_ref), channel_id=1, source_target_pairs={{0,2},{1,3},{2,0},{3,1},{4,6},{5,7},{6,4},{7,5},{8,10},{9,11},{10,... | collective-permute-start | bytes 589832 | tf_op jit(solution)/shard_map/ppermute | solution.py:35
  8.5 4.2 %query_far.1 = (bf16[544,1152]{1,0:T(8,128)(2,1)S(1)}, bf16[512,1024]{1,0:T(8,128)(2,1)S(1)}) custom-call(bf16[512,1024]{1,0:T(8,128)(2,1)S(1)} %get-tuple-element.35.hg_ref, bf16[1024,4096]{1,0:T(8,128)(2,1)} %w_hbm.5, bf16[544,128]{1,0:T(8,128)(2,1)S(1)} %get-tuple-element.36.after_ref.pack_ref, bf16[768,128]{1,0:T(8,128)(2,1)S(1)} %part_sum.1.after_ref.s_ref), custom_call_target="tpu_custom_call" | custom-call | tf_op jit(solution)/shard_map/query_far/pallas_call | solution.py:283
  12.7 1.3 %collective-permute-done.1.r_ref = bf16[768,128]{1,0:T(8,128)(2,1)S(1)} collective-permute-done((bf16[768,128]{1,0:T(8,128)(2,1)S(1)}, bf16[768,128]{1,0:T(8,128)(2,1)S(1)}, u32[]{:S(2)}, u32[]{:S(2)}) %collective-permute-start.1) | collective-permute-done | bytes 196640 | tf_op jit(solution)/shard_map/ppermute | solution.py:35
  14.1 0.7 %grads.1 = (f32[512,128]{1,0:T(8,128)S(1)}, bf16[512,128]{1,0:T(8,128)(2,1)S(1)}, f32[512,128]{1,0:T(8,128)S(1)}, bf16[512,128]{1,0:T(8,128)(2,1)S(1)}, bf16[544,1152]{1,0:T(8,128)(2,1)S(1)}) custom-call(bf16[384,1024]{1,0:T(8,128)(2,1)S(1)} %copy-done.1, bf16[384,1024]{1,0:T(8,128)(2,1)S(1)} %copy-done.2, ...), custom_call_target="tpu_custom_call", output_to_operand_aliasing={{4}: (4, {})} | custom-call | tf_op jit(solution)/shard_map/grads/pallas_call | solution.py:283
  14.7 0.1 collective-permute-start.4
  14.8 1.9 %collective-permute-start.2 = (bf16[512,128]{1,0:T(8,128)(2,1)S(1)}, bf16[512,128]{1,0:T(8,128)(2,1)S(1)}, u32[]{:S(2)}, u32[]{:S(2)}) collective-permute-start(bf16[512,128]{1,0:T(8,128)(2,1)S(1)} %get-tuple-element.39.after_ref), channel_id=1, source_target_pairs={{0,4},{4,0},{8,12},{12,8},{1,5},{5,1},{9,13},{13,9},{2,6},{6,2},{1... | collective-permute-start | bytes 393224 | tf_op jit(solution)/shard_map/ppermute | solution.py:35
  16.7 1.5 %collective-permute-start.3 = (bf16[512,128]{1,0:T(8,128)(2,1)S(1)}, bf16[512,128]{1,0:T(8,128)(2,1)S(1)}, u32[]{:S(2)}, u32[]{:S(2)}) collective-permute-start(bf16[512,128]{1,0:T(8,128)(2,1)S(1)} %get-tuple-element.41), channel_id=1, source_target_pairs={{0,16},{16,0},{1,17},{17,1},{2,18},{18,2},{3,19},{19,3},{4,20},{20... | collective-permute-start | bytes 393224 | tf_op jit(solution)/shard_map/ppermute | solution.py:35
  18.2 2.7 %query_beside.1.pass_ref = bf16[512,1024]{1,0:T(8,128)(2,1)S(1)} custom-call(bf16[512,1024]{1,0:T(8,128)(2,1)S(1)} %get-tuple-element.35.hg_ref, bf16[1024,4096]{1,0:T(8,128)(2,1)} %w_hbm.5, bf16[544,128]{1,0:T(8,128)(2,1)S(1)} %get-tuple-element.36.after_ref.pack_ref, bf16[512,128]{1,0:T(8,128)(2,1)S(1)} %get-tuple-element.39.after_ref), custom_call_target="tpu_custom_call" | custom-call | tf_op jit(solution)/shard_map/query_beside/pallas_call | solution.py:283
  20.9 0.0 collective-permute-done.4.got_ref
  20.9 0.3 far.1
  21.2 1.6 %collective-permute-start.6 = (bf16[544,1152]{1,0:T(8,128)(2,1)S(1)}, bf16[544,1152]{1,0:T(8,128)(2,1)S(1)}, u32[]{:S(2)}, u32[]{:S(2)}) collective-permute-start(bf16[544,1152]{1,0:T(8,128)(2,1)S(1)} %get-tuple-element.44.refs_4_.refs_6_.far_ref), channel_id=1, source_target_pairs={{0,2},{1,3},{2,0},{3,1},{4,6},{5,7},{6,4},{7,5},{8,10},{9,11},{10,... | collective-permute-start | bytes 3760136 | tf_op jit(solution)/shard_map/ppermute | solution.py:35
  22.8 0.1 step_0.1
  22.9 2.7 %collective-permute-start.7 = (bf16[256,128]{1,0:T(8,128)(2,1)S(1)}, bf16[256,128]{1,0:T(8,128)(2,1)S(1)}, u32[]{:S(2)}, u32[]{:S(2)}) collective-permute-start(bf16[256,128]{1,0:T(8,128)(2,1)S(1)} %get-tuple-element.45.after_ref), channel_id=1, source_target_pairs={{0,8},{4,12},{8,0},{12,4},{1,9},{5,13},{9,1},{13,5},{2,10},{6,14},... | collective-permute-start | bytes 196616 | tf_op jit(solution)/shard_map/ppermute | solution.py:35
  25.5 0.4 collective-permute-start.8
  26.0 2.7 %query_close.1.refs_4_.mine_ref = bf16[512,1024]{1,0:T(8,128)(2,1)S(1)} custom-call(bf16[512,1024]{1,0:T(8,128)(2,1)S(1)} %get-tuple-element.35.hg_ref, bf16[1024,4096]{1,0:T(8,128)(2,1)} %w_hbm.5, bf16[544,128]{1,0:T(8,128)(2,1)S(1)} %get-tuple-element.36.after_ref.pack_ref, bf16[256,128]{1,0:T(8,128)(2,1)S(1)} %get-tuple-element.45.after_ref), custom_call_target="tpu_custom_call" | custom-call | tf_op jit(solution)/shard_map/query_close/pallas_call | solution.py:283
  28.7 0.0 copy-start.4
  28.7 0.1 collective-permute-start.5
  28.8 0.1 collective-permute-done.7.refs_1_
  28.8 1.0 %collective-permute-done.8.refs_3_ = bf16[256,128]{1,0:T(8,128)(2,1)S(1)} collective-permute-done((bf16[256,128]{1,0:T(8,128)(2,1)S(1)}, bf16[256,128]{1,0:T(8,128)(2,1)S(1)}, u32[]{:S(2)}, u32[]{:S(2)}) %collective-permute-start.8) | collective-permute-done | bytes 65568 | tf_op jit(solution)/shard_map/ppermute | solution.py:35
  29.8 1.0 %collective-permute-start.9 = (bf16[256,128]{1,0:T(8,128)(2,1)S(1)}, bf16[256,128]{1,0:T(8,128)(2,1)S(1)}, u32[]{:S(2)}, u32[]{:S(2)}) collective-permute-start(bf16[256,128]{1,0:T(8,128)(2,1)S(1)} %get-tuple-element.50.after_ref.refs_0_), channel_id=1, source_target_pairs={{0,16},{16,0},{1,17},{17,1},{2,18},{18,2},{3,19},{19,3},{4,20},{20... | collective-permute-start | bytes 196616 | tf_op jit(solution)/shard_map/ppermute | solution.py:35
  30.9 0.9 %collective-permute-start.10 = (bf16[128,128]{1,0:T(8,128)(2,1)S(1)}, bf16[128,128]{1,0:T(8,128)(2,1)S(1)}, u32[]{:S(2)}, u32[]{:S(2)}) collective-permute-start(bf16[128,128]{1,0:T(8,128)(2,1)S(1)} %get-tuple-element.52), channel_id=1, source_target_pairs={{0,8},{4,12},{8,0},{12,4},{1,9},{5,13},{9,1},{13,5},{2,10},{6,14},... | collective-permute-start | bytes 98312 | tf_op jit(solution)/shard_map/ppermute | solution.py:35
  31.8 1.0 %multiply_cosine_fusion.1 = (f32[256,64]{1,0:T(8,128)S(1)}, f32[256,64]{1,0:T(8,128)S(1)}, f32[256,64]{1,0:T(8,128)S(1)}, f32[256,64]{1,0:T(8,128)S(1)}, f32[256,64]{1,0:T(8,128)S(1)}, /*index=5*/f32[256,64]{1,0:T(8,128)S(1)}) fusion(f32[64]{0:T(128)S(1)} %multiply_power_fusion, f32[256]{0:T(256)S(1)} %bitcast.6, f32[256]{0:T(256)S(1)} %broadcast_add_fusion), kind=kLoop, calls=%fused_computation.4 | loop fusion | flops 65536 | bytes 395520 | tf_op jit(solution)/shard_map/cos | solution.py:301
  32.8 0.1 maximum_maximum_fusion.refs_4_.sin_ref
  32.9 3.1 %collective-permute-done.10.refs_3_ = bf16[128,128]{1,0:T(8,128)(2,1)S(1)} collective-permute-done((bf16[128,128]{1,0:T(8,128)(2,1)S(1)}, bf16[128,128]{1,0:T(8,128)(2,1)S(1)}, u32[]{:S(2)}, u32[]{:S(2)}) %collective-permute-start.10) | collective-permute-done | bytes 32800 | tf_op jit(solution)/shard_map/ppermute | solution.py:35
  36.0 0.2 step_2.1
  36.2 0.6 collective-permute-start.11
  36.8 2.4 %collective-permute-start.12 = (bf16[160,128]{1,0:T(8,128)(2,1)S(1)}, bf16[160,128]{1,0:T(8,128)(2,1)S(1)}, u32[]{:S(2)}, u32[]{:S(2)}) collective-permute-start(bf16[160,128]{1,0:T(8,128)(2,1)S(1)} %get-tuple-element.54.refs_2_), channel_id=1, source_target_pairs={{0,8},{4,12},{8,0},{12,4},{1,9},{5,13},{9,1},{13,5},{2,10},{6,14},... | collective-permute-start | bytes 122888 | tf_op jit(solution)/shard_map/ppermute | solution.py:35
  39.2 1.1 %collective-permute-start.13 = (bf16[32,128]{1,0:T(8,128)(2,1)S(1)}, bf16[32,128]{1,0:T(8,128)(2,1)S(1)}, u32[]{:S(2)}, u32[]{:S(2)}) collective-permute-start(bf16[32,128]{1,0:T(8,128)(2,1)S(1)} %get-tuple-element.55), channel_id=1, source_target_pairs={{0,16},{4,20},{8,24},{12,28},{16,0},{20,4},{24,8},{28,12},{1,17},{... | collective-permute-start | bytes 24584 | tf_op jit(solution)/shard_map/ppermute | solution.py:335
  40.3 2.6 %collective-permute-done.13.refs_4_ = bf16[32,128]{1,0:T(8,128)(2,1)S(1)} collective-permute-done((bf16[32,128]{1,0:T(8,128)(2,1)S(1)}, bf16[32,128]{1,0:T(8,128)(2,1)S(1)}, u32[]{:S(2)}, u32[]{:S(2)}) %collective-permute-start.13) | collective-permute-done | bytes 8224 | tf_op jit(solution)/shard_map/ppermute | solution.py:335
  42.9 1.1 %collective-permute-start.14 = (bf16[32,128]{1,0:T(8,128)(2,1)S(1)}, bf16[32,128]{1,0:T(8,128)(2,1)S(1)}, u32[]{:S(2)}, u32[]{:S(2)}) collective-permute-start(bf16[32,128]{1,0:T(8,128)(2,1)S(1)} %get-tuple-element.55), channel_id=1, source_target_pairs={{0,24},{4,28},{8,16},{12,20},{16,8},{20,12},{24,0},{28,4},{1,25},{... | collective-permute-start | bytes 24584 | tf_op jit(solution)/shard_map/ppermute | solution.py:335
  44.0 4.5 %collective-permute-done.14.refs_5_ = bf16[32,128]{1,0:T(8,128)(2,1)S(1)} collective-permute-done((bf16[32,128]{1,0:T(8,128)(2,1)S(1)}, bf16[32,128]{1,0:T(8,128)(2,1)S(1)}, u32[]{:S(2)}, u32[]{:S(2)}) %collective-permute-start.14) | collective-permute-done | bytes 8224 | tf_op jit(solution)/shard_map/ppermute | solution.py:335
  48.5 0.5 collective-permute-start.15
  49.0 1.6 %collective-permute-start.16 = (bf16[288,128]{1,0:T(8,128)(2,1)S(1)}, bf16[288,128]{1,0:T(8,128)(2,1)S(1)}, u32[]{:S(2)}, u32[]{:S(2)}) collective-permute-start(bf16[288,128]{1,0:T(8,128)(2,1)S(1)} %get-tuple-element.57.mine_b), channel_id=1, source_target_pairs={{0,4},{4,0},{8,12},{12,8},{1,5},{5,1},{9,13},{13,9},{2,6},{6,2},{1... | collective-permute-start | bytes 221192 | tf_op jit(solution)/shard_map/ppermute | solution.py:35
  50.6 3.7 %collective-permute-done.16.got_b = bf16[288,128]{1,0:T(8,128)(2,1)S(1)} collective-permute-done((bf16[288,128]{1,0:T(8,128)(2,1)S(1)}, bf16[288,128]{1,0:T(8,128)(2,1)S(1)}, u32[]{:S(2)}, u32[]{:S(2)}) %collective-permute-start.16) | collective-permute-done | bytes 73760 | tf_op jit(solution)/shard_map/ppermute | solution.py:35
  54.3 0.5 low_rank.1
  54.8 0.1 collective-permute-start.17
  54.9 1.3 %collective-permute-done.17.b_ref = bf16[544,128]{1,0:T(8,128)(2,1)S(1)} collective-permute-done((bf16[544,128]{1,0:T(8,128)(2,1)S(1)}, bf16[544,128]{1,0:T(8,128)(2,1)S(1)}, u32[]{:S(2)}, u32[]{:S(2)}) %collective-permute-start.17) | collective-permute-done | bytes 139296 | tf_op jit(solution)/shard_map/ppermute | solution.py:35
  56.3 1.5 %collective-permute-start.18 = (bf16[544,128]{1,0:T(8,128)(2,1)S(1)}, bf16[544,128]{1,0:T(8,128)(2,1)S(1)}, u32[]{:S(2)}, u32[]{:S(2)}) collective-permute-start(bf16[544,128]{1,0:T(8,128)(2,1)S(1)} %merge.1.after_ref.s_ref), channel_id=1, source_target_pairs={{0,2},{1,3},{2,0},{3,1},{4,6},{5,7},{6,4},{7,5},{8,10},{9,11},{10,... | collective-permute-start | bytes 417800 | tf_op jit(solution)/shard_map/ppermute | solution.py:35
  57.8 0.6 collective-permute-start.19
  58.4 0.1 maximum_maximum_fusion.1.cos_ref
  58.5 0.0 copy-start
  58.5 0.0 copy-start.3
  58.6 0.5 base.1
  59.1 4.1 %collective-permute-done.19.got_b = bf16[512,128]{1,0:T(8,128)(2,1)S(1)} collective-permute-done((bf16[512,128]{1,0:T(8,128)(2,1)S(1)}, bf16[512,128]{1,0:T(8,128)(2,1)S(1)}, u32[]{:S(2)}, u32[]{:S(2)}) %collective-permute-start.19) | collective-permute-done | bytes 131104 | tf_op jit(solution)/shard_map/ppermute | solution.py:35
  63.1 1.8 %final.1 = (f32[1024,128]{1,0:T(8,128)}, f32[128,1024]{1,0:T(8,128)}, bf16[512,1024]{1,0:T(8,128)(2,1)}) custom-call(f32[512,1024]{1,0:T(8,128)S(1)} %get-tuple-element.59.base_ref, f32[512,128]{1,0:T(8,128)S(1)} %get-tuple-element.60.low_ref, f32[512,128]{1,0:T(8,128)S(1)} %get-tuple-element.61.scale_ref, bf16[544,128]{1,0:T(8,128)(2,1)S(1)} %merge.1.after_ref.s_ref, ...), custom_call_target="tpu_custom_call" | custom-call | tf_op jit(solution)/shard_map/final/pallas_call | solution.py:283
  (24 shorter events, 0.2 us)
Async XLA Ops:
  3.1 2.8 %collective-permute-start = (bf16[768,128]{1,0:T(8,128)(2,1)S(1)}, bf16[768,128]{1,0:T(8,128)(2,1)S(1)}, u32[]{:S(2)}, u32[]{:S(2)}) collective-permute-start(bf16[768,128]{1,0:T(8,128)(2,1)S(1)} %rank.1.x_ref), channel_id=1, source_target_pairs={{0,1},{1,0},{2,3},{3,2},{4,5},{5,4},{6,7},{7,6},{8,9},{9,8},{10,11... | collective-permute-start | bytes 589832 | tf_op jit(solution)/shard_map/ppermute | solution.py:35
  5.9 8.2 %collective-permute-start.1 = (bf16[768,128]{1,0:T(8,128)(2,1)S(1)}, bf16[768,128]{1,0:T(8,128)(2,1)S(1)}, u32[]{:S(2)}, u32[]{:S(2)}) collective-permute-start(bf16[768,128]{1,0:T(8,128)(2,1)S(1)} %part_sum.1.after_ref.s_ref), channel_id=1, source_target_pairs={{0,2},{1,3},{2,0},{3,1},{4,6},{5,7},{6,4},{7,5},{8,10},{9,11},{10,... | collective-permute-start | bytes 589832 | tf_op jit(solution)/shard_map/ppermute | solution.py:35
  8.5 5.6 %copy-start.1 = (bf16[384,1024]{1,0:T(8,128)(2,1)S(1)}, bf16[384,1024]{1,0:T(8,128)(2,1)}, u32[]{:S(2)}) copy-start(bf16[384,1024]{1,0:T(8,128)(2,1)} %x_ref.1) | copy-start | bytes 2359300
  8.5 5.6 %copy-start.2 = (bf16[384,1024]{1,0:T(8,128)(2,1)S(1)}, bf16[384,1024]{1,0:T(8,128)(2,1)}, u32[]{:S(2)}) copy-start(bf16[384,1024]{1,0:T(8,128)(2,1)} %v_ref.1) | copy-start | bytes 2359300
  14.7 6.1 %collective-permute-start.4 = (bf16[544,1152]{1,0:T(8,128)(2,1)S(1)}, bf16[544,1152]{1,0:T(8,128)(2,1)S(1)}, u32[]{:S(2)}, u32[]{:S(2)}) collective-permute-start(bf16[544,1152]{1,0:T(8,128)(2,1)S(1)} %get-tuple-element.43.diag_ref), channel_id=1, source_target_pairs={{0,1},{1,0},{2,3},{3,2},{4,5},{5,4},{6,7},{7,6},{8,9},{9,8},{10,11... | collective-permute-start | bytes 3760136 | tf_op jit(solution)/shard_map/ppermute | solution.py:35
  14.8 8.0 %collective-permute-start.2 = (bf16[512,128]{1,0:T(8,128)(2,1)S(1)}, bf16[512,128]{1,0:T(8,128)(2,1)S(1)}, u32[]{:S(2)}, u32[]{:S(2)}) collective-permute-start(bf16[512,128]{1,0:T(8,128)(2,1)S(1)} %get-tuple-element.39.after_ref), channel_id=1, source_target_pairs={{0,4},{4,0},{8,12},{12,8},{1,5},{5,1},{9,13},{13,9},{2,6},{6,2},{1... | collective-permute-start | bytes 393224 | tf_op jit(solution)/shard_map/ppermute | solution.py:35
  16.7 6.1 %collective-permute-start.3 = (bf16[512,128]{1,0:T(8,128)(2,1)S(1)}, bf16[512,128]{1,0:T(8,128)(2,1)S(1)}, u32[]{:S(2)}, u32[]{:S(2)}) collective-permute-start(bf16[512,128]{1,0:T(8,128)(2,1)S(1)} %get-tuple-element.41), channel_id=1, source_target_pairs={{0,16},{16,0},{1,17},{17,1},{2,18},{18,2},{3,19},{19,3},{4,20},{20... | collective-permute-start | bytes 393224 | tf_op jit(solution)/shard_map/ppermute | solution.py:35
  21.2 37.4 %collective-permute-start.6 = (bf16[544,1152]{1,0:T(8,128)(2,1)S(1)}, bf16[544,1152]{1,0:T(8,128)(2,1)S(1)}, u32[]{:S(2)}, u32[]{:S(2)}) collective-permute-start(bf16[544,1152]{1,0:T(8,128)(2,1)S(1)} %get-tuple-element.44.refs_4_.refs_6_.far_ref), channel_id=1, source_target_pairs={{0,2},{1,3},{2,0},{3,1},{4,6},{5,7},{6,4},{7,5},{8,10},{9,11},{10,... | collective-permute-start | bytes 3760136 | tf_op jit(solution)/shard_map/ppermute | solution.py:35
  22.9 5.9 %collective-permute-start.7 = (bf16[256,128]{1,0:T(8,128)(2,1)S(1)}, bf16[256,128]{1,0:T(8,128)(2,1)S(1)}, u32[]{:S(2)}, u32[]{:S(2)}) collective-permute-start(bf16[256,128]{1,0:T(8,128)(2,1)S(1)} %get-tuple-element.45.after_ref), channel_id=1, source_target_pairs={{0,8},{4,12},{8,0},{12,4},{1,9},{5,13},{9,1},{13,5},{2,10},{6,14},... | collective-permute-start | bytes 196616 | tf_op jit(solution)/shard_map/ppermute | solution.py:35
  25.5 4.3 %collective-permute-start.8 = (bf16[256,128]{1,0:T(8,128)(2,1)S(1)}, bf16[256,128]{1,0:T(8,128)(2,1)S(1)}, u32[]{:S(2)}, u32[]{:S(2)}) collective-permute-start(bf16[256,128]{1,0:T(8,128)(2,1)S(1)} %get-tuple-element.49), channel_id=1, source_target_pairs={{0,4},{4,0},{8,12},{12,8},{1,5},{5,1},{9,13},{13,9},{2,6},{6,2},{1... | collective-permute-start | bytes 196616 | tf_op jit(solution)/shard_map/ppermute | solution.py:35
  28.7 2.2 %copy-start.4 = (s32[256]{0:T(256)S(1)}, s32[256]{0:T(256)}, u32[]{:S(2)}) copy-start(s32[256]{0:T(256)} %param.15) | copy-start | bytes 3076
  28.7 29.9 %collective-permute-start.5 = (bf16[512,1024]{1,0:T(8,128)(2,1)S(1)}, bf16[512,1024]{1,0:T(8,128)(2,1)S(1)}, u32[]{:S(2)}, u32[]{:S(2)}) collective-permute-start(bf16[512,1024]{1,0:T(8,128)(2,1)S(1)} %get-tuple-element.46), channel_id=1, source_target_pairs={{0,1},{1,0},{2,3},{3,2},{4,5},{5,4},{6,7},{7,6},{8,9},{9,8},{10,11... | collective-permute-start | bytes 3145736 | tf_op jit(solution)/shard_map/ppermute | solution.py:35
  29.8 6.2 %collective-permute-start.9 = (bf16[256,128]{1,0:T(8,128)(2,1)S(1)}, bf16[256,128]{1,0:T(8,128)(2,1)S(1)}, u32[]{:S(2)}, u32[]{:S(2)}) collective-permute-start(bf16[256,128]{1,0:T(8,128)(2,1)S(1)} %get-tuple-element.50.after_ref.refs_0_), channel_id=1, source_target_pairs={{0,16},{16,0},{1,17},{17,1},{2,18},{18,2},{3,19},{19,3},{4,20},{20... | collective-permute-start | bytes 196616 | tf_op jit(solution)/shard_map/ppermute | solution.py:35
  30.9 5.2 %collective-permute-start.10 = (bf16[128,128]{1,0:T(8,128)(2,1)S(1)}, bf16[128,128]{1,0:T(8,128)(2,1)S(1)}, u32[]{:S(2)}, u32[]{:S(2)}) collective-permute-start(bf16[128,128]{1,0:T(8,128)(2,1)S(1)} %get-tuple-element.52), channel_id=1, source_target_pairs={{0,8},{4,12},{8,0},{12,4},{1,9},{5,13},{9,1},{13,5},{2,10},{6,14},... | collective-permute-start | bytes 98312 | tf_op jit(solution)/shard_map/ppermute | solution.py:35
  36.2 12.3 %collective-permute-start.11 = (bf16[256,128]{1,0:T(8,128)(2,1)S(1)}, bf16[256,128]{1,0:T(8,128)(2,1)S(1)}, u32[]{:S(2)}, u32[]{:S(2)}) collective-permute-start(bf16[256,128]{1,0:T(8,128)(2,1)S(1)} %get-tuple-element.53.refs_0_), channel_id=1, source_target_pairs={{0,8},{4,12},{8,0},{12,4},{1,9},{5,13},{9,1},{13,5},{2,10},{6,14},... | collective-permute-start | bytes 196616 | tf_op jit(solution)/shard_map/ppermute | solution.py:35
  36.8 11.6 %collective-permute-start.12 = (bf16[160,128]{1,0:T(8,128)(2,1)S(1)}, bf16[160,128]{1,0:T(8,128)(2,1)S(1)}, u32[]{:S(2)}, u32[]{:S(2)}) collective-permute-start(bf16[160,128]{1,0:T(8,128)(2,1)S(1)} %get-tuple-element.54.refs_2_), channel_id=1, source_target_pairs={{0,8},{4,12},{8,0},{12,4},{1,9},{5,13},{9,1},{13,5},{2,10},{6,14},... | collective-permute-start | bytes 122888 | tf_op jit(solution)/shard_map/ppermute | solution.py:35
  39.2 3.7 %collective-permute-start.13 = (bf16[32,128]{1,0:T(8,128)(2,1)S(1)}, bf16[32,128]{1,0:T(8,128)(2,1)S(1)}, u32[]{:S(2)}, u32[]{:S(2)}) collective-permute-start(bf16[32,128]{1,0:T(8,128)(2,1)S(1)} %get-tuple-element.55), channel_id=1, source_target_pairs={{0,16},{4,20},{8,24},{12,28},{16,0},{20,4},{24,8},{28,12},{1,17},{... | collective-permute-start | bytes 24584 | tf_op jit(solution)/shard_map/ppermute | solution.py:335
  42.9 5.6 %collective-permute-start.14 = (bf16[32,128]{1,0:T(8,128)(2,1)S(1)}, bf16[32,128]{1,0:T(8,128)(2,1)S(1)}, u32[]{:S(2)}, u32[]{:S(2)}) collective-permute-start(bf16[32,128]{1,0:T(8,128)(2,1)S(1)} %get-tuple-element.55), channel_id=1, source_target_pairs={{0,24},{4,28},{8,16},{12,20},{16,8},{20,12},{24,0},{28,4},{1,25},{... | collective-permute-start | bytes 24584 | tf_op jit(solution)/shard_map/ppermute | solution.py:335
  48.5 5.8 %collective-permute-start.15 = (bf16[512,128]{1,0:T(8,128)(2,1)S(1)}, bf16[512,128]{1,0:T(8,128)(2,1)S(1)}, u32[]{:S(2)}, u32[]{:S(2)}) collective-permute-start(bf16[512,128]{1,0:T(8,128)(2,1)S(1)} %get-tuple-element.56.mine_a), channel_id=1, source_target_pairs={{0,4},{4,0},{8,12},{12,8},{1,5},{5,1},{9,13},{13,9},{2,6},{6,2},{1... | collective-permute-start | bytes 393224 | tf_op jit(solution)/shard_map/ppermute | solution.py:35
  49.0 5.4 %collective-permute-start.16 = (bf16[288,128]{1,0:T(8,128)(2,1)S(1)}, bf16[288,128]{1,0:T(8,128)(2,1)S(1)}, u32[]{:S(2)}, u32[]{:S(2)}) collective-permute-start(bf16[288,128]{1,0:T(8,128)(2,1)S(1)} %get-tuple-element.57.mine_b), channel_id=1, source_target_pairs={{0,4},{4,0},{8,12},{12,8},{1,5},{5,1},{9,13},{13,9},{2,6},{6,2},{1... | collective-permute-start | bytes 221192 | tf_op jit(solution)/shard_map/ppermute | solution.py:35
  54.8 1.4 %collective-permute-start.17 = (bf16[544,128]{1,0:T(8,128)(2,1)S(1)}, bf16[544,128]{1,0:T(8,128)(2,1)S(1)}, u32[]{:S(2)}, u32[]{:S(2)}) collective-permute-start(bf16[544,128]{1,0:T(8,128)(2,1)S(1)} %get-tuple-element.58.a_ref), channel_id=1, source_target_pairs={{0,1},{1,0},{2,3},{3,2},{4,5},{5,4},{6,7},{7,6},{8,9},{9,8},{10,11... | collective-permute-start | bytes 417800 | tf_op jit(solution)/shard_map/ppermute | solution.py:35
  56.3 6.8 %collective-permute-start.18 = (bf16[544,128]{1,0:T(8,128)(2,1)S(1)}, bf16[544,128]{1,0:T(8,128)(2,1)S(1)}, u32[]{:S(2)}, u32[]{:S(2)}) collective-permute-start(bf16[544,128]{1,0:T(8,128)(2,1)S(1)} %merge.1.after_ref.s_ref), channel_id=1, source_target_pairs={{0,2},{1,3},{2,0},{3,1},{4,6},{5,7},{6,4},{7,5},{8,10},{9,11},{10,... | collective-permute-start | bytes 417800 | tf_op jit(solution)/shard_map/ppermute | solution.py:35
  57.8 5.3 %collective-permute-start.19 = (bf16[512,128]{1,0:T(8,128)(2,1)S(1)}, bf16[512,128]{1,0:T(8,128)(2,1)S(1)}, u32[]{:S(2)}, u32[]{:S(2)}) collective-permute-start(bf16[512,128]{1,0:T(8,128)(2,1)S(1)} %get-tuple-element.63.mine_b), channel_id=1, source_target_pairs={{0,16},{16,0},{1,17},{17,1},{2,18},{18,2},{3,19},{19,3},{4,20},{20... | collective-permute-start | bytes 393224 | tf_op jit(solution)/shard_map/ppermute | solution.py:35
  58.5 4.6 %copy-start = (f32[1024,128]{1,0:T(8,128)S(1)}, f32[1024,128]{1,0:T(8,128)}, u32[]{:S(2)}) copy-start(f32[1024,128]{1,0:T(8,128)} %a_ref.1) | copy-start | bytes 1572868
  58.5 4.6 %copy-start.3 = (f32[128,1024]{1,0:T(8,128)S(1)}, f32[128,1024]{1,0:T(8,128)}, u32[]{:S(2)}) copy-start(f32[128,1024]{1,0:T(8,128)} %b_ref.1) | copy-start | bytes 1572868

commit v8 on v7

--- a/solution.py
+++ b/solution.py
@@ -123,7 +123,7 @@
         outs[i // per][:count, i % per * cut : (i % per + 1) * cut] = block
 
 
-def far_kernel(mine_ref, diag_ref, got_ref, after_ref, pass_ref, out_ref, pass_out):
+def far_kernel(mine_ref, diag_ref, got_ref, after_ref, out_ref):
     count, width = mine_ref.shape
     out_ref[:count, :width] = (mine_ref[...].astype(F32) + got_ref[:count, :width].astype(F32)).astype(BF)
     out_ref[count:, :width] = jnp.zeros((EXTRA, width), BF)
@@ -152,13 +152,6 @@
     mine, other = halves(axis, bit, mine_ref.shape[0])
     out_ref[mine] = mine_ref[...]
     out_ref[other] = got_ref[...]
-
-
-def join_some(axis, bit, mine_ref, got_ref, out_ref):
-    size = mine_ref.shape[0] - EXTRA
-    mine, other = halves(axis, bit, size)
-    out_ref[mine] = mine_ref[:size]
-    out_ref[other] = got_ref[:size]
 
 
 def grad_kernel(axes, x_ref, v_ref, s_ref, r_ref, pass_ref, keep_a, send_a, keep_b, send_b, pass_out, ga, gb):
@@ -176,40 +169,25 @@
     out_ref[...] = (keep_ref[...].astype(F32) + got_ref[...].astype(F32)).astype(BF)
 
 
-def tree_sum(values):
-    while len(values) > 1:
-        values = [a + b for a, b in zip(values[::2], values[1::2])]
-    return values[0]
+def halved(plan):
+    return sum(step[0] == "halve" for step in plan)
 
 
 def step_kernel(plan, *refs):
-    ins, refs = refs[: sum(n for _, n in plan)], refs[sum(n for _, n in plan) + 1 :]
-    ins, outs = list(ins), list(refs)
-    for (kind, axis, bit), n in plan:
-        mine, got, terms = ins[0], ins[1], ins[2:n]
-        ins = ins[n:]
+    ins, outs = list(refs[: 2 * len(plan)]), list(refs[2 * len(plan) :])
+    waits, passed = plan[0][3]
+    outs = outs[waits + passed :]
+    outs = outs[: len(outs) - passed - halved(plan)] + outs[len(outs) - halved(plan) :]
+    for kind, axis, bit, _ in plan:
+        mine, got = ins.pop(0), ins.pop(0)
         if kind == "halve":
             total = outs.pop()
             total[...] = mine[...] + got[...].astype(F32)
             halve(axis, bit, total, outs.pop(0), outs.pop(0))
         elif kind == "sum":
             sum_kernel(mine, got, outs.pop(0))
-        elif kind == "norm":
-            size = mine.shape[0]
-            total = mine[...] + got[...].astype(F32)
-            out, sums = outs.pop(0), outs.pop(0)
-            out[:size] = total.astype(BF)
-            sums[...] = split_terms(jnp.broadcast_to(jnp.sum(total * total), (8, LANES)))
-            out[size:] = sums[...]
-        elif kind == "join":
+        else:
             join(axis, bit, mine, got, outs.pop(0))
-        else:
-            out = outs.pop(0)
-            join_some(axis, bit, mine, got, out)
-            half = len(terms) // 2
-            near = tree_sum([join_terms(mine[-EXTRA:])] + [join_terms(t[...]) for t in terms[:half]])
-            far = tree_sum([join_terms(got[-EXTRA:])] + [join_terms(t[...]) for t in terms[half:]])
-            out[-EXTRA:] = split_terms(near + far)
 
 
 def place_kernel(pos_ref, after_ref, out_ref):
@@ -225,9 +203,17 @@
     join(axis, bit, mine_a, got_a, ga_ref)
     count = hg_ref.shape[0]
     pack_ref[:count] = dot(hg_ref[...], ga_ref[...]).astype(BF)
-    join_some(axis, bit, mine_b, got_b, gb_ref)
-    total = square_sum(ga_ref) + (join_terms(mine_b[-EXTRA:]) + join_terms(got_b[-EXTRA:]))
-    pack_ref[count:] = split_terms(total)
+    pack_ref[count:] = split_terms(square_sum(ga_ref))
+    join(axis, bit, mine_b, got_b, gb_ref)
+
+
+def norm_kernel(axis, bit, mine_b, got_b, gb_ref, norm_ref):
+    join(axis, bit, mine_b, got_b, gb_ref)
+    norm_ref[...] = split_terms(square_sum(gb_ref))
+
+
+def norm_merge_kernel(a_ref, b_ref, out_ref):
+    out_ref[...] = split_terms(join_terms(a_ref[...]) + join_terms(b_ref[...]))
 
 
 def base_kernel(mine_ref, near_ref, far_ref, far_got, after_ref, base_ref, low_ref, scale_ref):
@@ -244,12 +230,12 @@
 
 
 def final_kernel(
-    axis, bit, base_ref, low_ref, scale_ref, s_ref, r_ref, ga_ref, mine_b, got_b, a_ref, b_ref,
-    cos_ref, sin_ref, a_hbm, b_hbm, q_hbm, gb_ref, new_a, new_b, half_b, out, sems,
+    base_ref, low_ref, scale_ref, s_ref, r_ref, sn_ref, rn_ref, ga_ref, gb_ref, a_ref, b_ref, cos_ref, sin_ref,
+    a_hbm, b_hbm, q_hbm, new_a, new_b, half_b, out, sems,
 ):
-    join(axis, bit, mine_b, got_b, gb_ref)
     count, width = base_ref.shape
     total = join_terms(s_ref[count:]) + join_terms(r_ref[count:])
+    total = total + (join_terms(sn_ref[...]) + join_terms(rn_ref[...]))
     rate = (LEARN * lax.rsqrt(total + NORM_EPS))[0:1]
     for c in blocks_of(width):
         fresh = b_ref[:, c] - rate * gb_ref[c].astype(F32)
@@ -322,17 +308,6 @@
         return list(zip(ways, after + [("join",) + way for way in down[::-1]]))
 
     path_a, path_b = path(z_bits, x_bits), path(x_bits + z_bits, [])
-    whole_b = len(x_bits + z_bits) - 1
-    path_b = [
-        (way, ("norm", None, None) if i == whole_b else ("join_norm",) + step[1:] if whole_b < i < len(path_a) else step)
-        for i, (way, step) in enumerate(path_b)
-    ]
-
-    def others(x, axis, bit):
-        pairs = lambda kx, kz: [
-            (i, ((i // n_roll) ^ kx) * n_roll + ((i % n_roll) ^ kz)) for i in range(n_dp * n_roll)
-        ]
-        return [lax.ppermute(x, ("dp", "roll"), pairs(kx, kz)) for kz in (0, 1 << bit) for kx in range(1, n_dp)]
 
     def on_device(
         train_inputs, train_cotangent, factor_a, factor_b, base_weight, incoming, norm_gain, positions
@@ -393,76 +368,79 @@
             aliases={4: 4},
         )
         diag_got = swap(diag, "tp", n_tp, 1)
-        (beside,) = query((1,), [tall], send_a, "query_beside")
-        far, beside = call(
-            far_kernel,
-            [wide, tall],
-            [VMEM] * 3 + [ANY] * 2,
-            (distant, diag, diag_got, send_a, beside),
-            "far",
-            out_specs=[VMEM, ANY],
-            aliases={4: 1},
-        )
+        far = call(far_kernel, wide, [VMEM] * 3 + [ANY], (distant, diag, diag_got, send_a), "far")
         far_got = swap(far, "tp", n_tp, 2)
-        beside_got = swap(beside, "tp", n_tp, 1)
-        def step_call(parts, after, name):
+
+        def step_call(parts, after, name, passed=()):
             ins, outs, scratch = [], [], []
-            for (kind, _, _), arrays in parts:
-                size = arrays[0].shape[0]
-                ins += arrays
-                if kind == "halve":
+            for step, (mine, got) in parts:
+                size = mine.shape[0]
+                ins += [mine, got]
+                if step[0] == "halve":
                     outs += [shape((size // 2, rank), F32), shape((size // 2, rank), BF)]
                     scratch.append(vmem(size))
-                elif kind == "norm":
-                    outs += [shape((size + EXTRA, rank), BF), shape((EXTRA, rank), BF)]
                 else:
-                    size = {"sum": size, "join": 2 * size, "join_norm": 2 * size - EXTRA}[kind]
-                    outs.append(shape((size, rank), BF))
-            made = list(
-                call(
-                    functools.partial(step_kernel, [(step, len(arrays)) for step, arrays in parts]),
-                    outs,
-                    [VMEM] * len(ins) + [ANY],
-                    (*ins, after),
-                    name,
-                    scratch,
-                )
+                    outs.append(shape((2 * size if step[0] == "join" else size, rank), BF))
+            first = len(ins) + len(after)
+            made = call(
+                functools.partial(step_kernel, [step + ((len(after), len(passed)),) for step, _ in parts]),
+                outs + [shape(x.shape, x.dtype) for x in passed],
+                [VMEM] * len(ins) + [ANY] * (len(after) + len(passed)),
+                (*ins, *after, *passed),
+                name,
+                scratch,
+                [VMEM] * len(outs) + [ANY] * len(passed),
+                aliases={first + i: len(outs) + i for i in range(len(passed))},
             )
-            return [[made.pop(0) for _ in range(1 + (step[0] in ("halve", "norm")))] for step, _ in parts]
-
-        state_a, state_b, sums = [keep_a, send_a], [keep_b, send_b], []
+            made = list(made)
+            return [[made.pop(0) for _ in range(1 + (step[0] == "halve"))] for step, _ in parts] + made
+
+        state_a, state_b, after, passed = [keep_a, send_a], [keep_b, send_b], [far], []
         for i, ((way_a, step_a), (way_b, step_b)) in enumerate(zip(path_a[:-1], path_b)):
-            arrays_a = [state_a[0], cross(state_a[-1], *way_a)]
-            arrays_b = [state_b[0], cross(state_b[-1], *way_b)] + sums
-            after = far if i == 0 else close if i == 1 else sin if i == 2 else far
-            state_a, state_b = step_call([(step_a, arrays_a), (step_b, arrays_b)], after, f"step_{i}")
-            sums = []
-            if step_b[0] == "norm":
-                sums = others(state_b.pop(), *path_b[i + 1][0])
+            got_a, got_b = cross(state_a[-1], *way_a), cross(state_b[-1], *way_b)
+            state_a, state_b, *made = step_call(
+                [(step_a, (state_a[0], got_a)), (step_b, (state_b[0], got_b))], after, f"step_{i}", passed
+            )
+            after, passed = [], []
+            if made:
+                beside_got = swap(made[0], "tp", n_tp, 1)
             if i == 0:
-                (close,) = query((0,), [tall], state_a[-1], "query_close")
+                after = query((0,), [tall], state_a[-1], "query_close")
+                (close,) = after
             if i == 1:
                 pos = positions.reshape(-1, LANES)
                 places = call(place_kernel, shape(pos.shape, F32), [VMEM, ANY], (pos, state_a[-1]), "places")
-                cos, sin = turn_tables(places.reshape(rows), steps)
+                after = list(turn_tables(places.reshape(rows), steps))
+                cos, sin = after
+            if i == 2:
+                passed = query((1,), [tall], state_a[-1], "query_beside")
         way = path_a[-1][0]
         mine_a, mine_b = state_a[-1], state_b[-1]
-        got_a, got_b = cross(mine_a, *way), cross(mine_b, *way)
         step_pack, grad_a, mine_b = call(
             functools.partial(low_kernel, *way),
-            [shape((count + EXTRA, rank), BF), shape((width, rank), BF), shape((2 * (mine_b.shape[0] - EXTRA), rank), BF)],
+            [shape((count + EXTRA, rank), BF), shape((width, rank), BF), shape((2 * mine_b.shape[0], rank), BF)],
             [VMEM] * 5,
-            (gained, mine_a, got_a, mine_b, got_b),
+            (gained, mine_a, cross(mine_a, *way), mine_b, cross(mine_b, *way)),
             "low_rank",
         )
         step_got = swap(step_pack, "tp", n_tp, 1)
         step_sum = call(merge_kernel, shape((count + EXTRA, rank), BF), [VMEM] * 2, (step_pack, step_got), "merge")
         step_far = swap(step_sum, "tp", n_tp, 2)
 
-        for (axis, bit), step in path_b[len(path_a) : -1]:
-            ((mine_b,),) = step_call([(step, [mine_b, cross(mine_b, axis, bit)])], step_pack, "join_b")
-        got_b = cross(mine_b, *path_b[-1][0])
-
+        for way_b, step_b in path_b[len(path_a) : -1]:
+            ((mine_b,),) = step_call([(step_b, (mine_b, cross(mine_b, *way_b)))], [], "join_b")
+        way = path_b[-1][0]
+        grad_b, norm = call(
+            functools.partial(norm_kernel, *way),
+            [shape((width, rank), BF), shape((EXTRA, LANES), BF)],
+            [VMEM] * 2,
+            (mine_b, cross(mine_b, *way)),
+            "norm",
+        )
+        norm = call(
+            norm_merge_kernel, shape((EXTRA, LANES), BF), [VMEM] * 2, (norm, swap(norm, "tp", n_tp, 1)), "norm_merge"
+        )
+        norm_far = swap(norm, "tp", n_tp, 2)
         base, low, scale = call(
             base_kernel,
             [shape((count, width), F32), shape((count, rank), F32), shape((count, LANES), F32)],
@@ -471,12 +449,12 @@
             "base",
         )
         new_a, new_b, queries = call(
-            functools.partial(final_kernel, *path_b[-1][0]),
+            final_kernel,
             [shape((width, rank), F32), shape((rank, width), F32), tall],
-            [VMEM] * 12,
-            (base, low, scale, step_sum, step_far, grad_a, mine_b, got_b, factor_a, factor_b, cos, sin),
+            [VMEM] * 13,
+            (base, low, scale, step_sum, step_far, norm, norm_far, grad_a, grad_b, factor_a, factor_b, cos, sin),
             "final",
-            [vmem(width, BF), pltpu.VMEM((width, rank), F32), pltpu.VMEM((rank, width), F32),
+            [pltpu.VMEM((width, rank), F32), pltpu.VMEM((rank, width), F32),
              pltpu.VMEM((rank, width), BF), pltpu.VMEM((count, width), BF), dma(2 + count // LANES)],
             [HBM] * 3,
         )

time: 65.1 us -> 63 us (0.968)
  waiting for transfers between devices: 21.7 us -> 19 us
  starting transfers between devices: 22.6 us -> 23.3 us
    ppermute x2 -> x0, waiting for transfers between devices: 7.1 us -> none  [others(): lax.ppermute(x, ('dp', 'roll'), pairs(kx, kz))]
    ppermute x18 -> x20, waiting for transfers between devices: 14.6 us -> 19 us  [swap(): return lax.ppermute(x, axis, [(i, i ^ k) for i in range(n)])]
    ppermute x18 -> x20, starting transfers between devices: 20.5 us -> 23.3 us  [swap(): return lax.ppermute(x, axis, [(i, i ^ k) for i in range(n)])]
    ppermute x2 -> x0, starting transfers between devices: 2.16 us -> none  [others(): lax.ppermute(x, ('dp', 'roll'), pairs(kx, kz))]
    cos x1 -> x0, other arithmetic: 0.99 us -> none  [turn_tables(): c, s = (jnp.cos(angle), jnp.sin(angle))]
    neg x0 -> x1, other arithmetic: none -> 0.99 us  [turn_tables(): sin.append(jnp.concatenate([-s, s], axis=-1))]
    pallas_call x17 -> x19, Pallas kernels: 18.4 us -> 18.5 us  [call(): pl.pallas_call(kernel, out_shape=outs, in_specs=in_specs, out_specs=out_s...]
where the time goes in v8:
time: 63 us; the launch traced here: 62.8 us
  starting transfers between devices  23.3 us (37%)
  waiting for transfers between devices  19 us (30%)
  Pallas kernels  18.5 us (29%)
  other arithmetic  1.22 us (2%)
  between operations  0.83 us (1%)
    ppermute x20, starting transfers between devices, swap(): return lax.ppermute(x, axis, [(i, i ^ k) for i in range(n)])  23.3 us
    ppermute x20, waiting for transfers between devices, swap(): return lax.ppermute(x, axis, [(i, i ^ k) for i in range(n)])  19 us
    pallas_call x19, Pallas kernels, call(): pl.pallas_call(kernel, out_shape=outs, in_specs=in_specs, out_specs=out_s...  18.5 us
  transfers between devices with their start and end apart: 20, of which 9 were waited for; matrix products, arithmetic and copies ran while one was open for 2% of the time, Pallas kernels for 21%

profile of v8, /device:TPU:0, one launch (start us, length us, event | category | flops | bytes accessed | tf_op | source)
XLA Modules:
  0.0 62.8 jit_solution(13185197421052420737)
XLA Ops:
  0.6 2.4 %rank.1.x_ref = bf16[768,128]{1,0:T(8,128)(2,1)S(1)} custom-call(bf16[384,1024]{1,0:T(8,128)(2,1)} %x_ref.1, bf16[384,1024]{1,0:T(8,128)(2,1)} %v_ref.1, f32[1024,128]{1,0:T(8,128)} %a_ref.1, f32[128,1024]{1,0:T(8,128)} %b_ref.1), custom_call_target="tpu_custom_call" | custom-call | tf_op jit(solution)/shard_map/rank/pallas_call | solution.py:269
  3.1 0.5 collective-permute-start
  3.6 2.2 %prep.1 = (bf16[512,1024]{1,0:T(8,128)(2,1)S(1)}, bf16[544,128]{1,0:T(8,128)(2,1)S(1)}) custom-call(bf16[512,1024]{1,0:T(8,128)(2,1)} %bitcast.8, f32[1,1024]{1,0:T(1,128)} %bitcast.9, f32[1024,128]{1,0:T(8,128)} %a_ref.1), custom_call_target="tpu_custom_call" | custom-call | tf_op jit(solution)/shard_map/prep/pallas_call | solution.py:269
  5.8 0.0 collective-permute-done.got_ref
  5.9 2.6 %collective-permute-start.1 = (bf16[768,128]{1,0:T(8,128)(2,1)S(1)}, bf16[768,128]{1,0:T(8,128)(2,1)S(1)}, u32[]{:S(2)}, u32[]{:S(2)}) collective-permute-start(bf16[768,128]{1,0:T(8,128)(2,1)S(1)} %part_sum.1.after_ref.s_ref), channel_id=1, source_target_pairs={{0,2},{1,3},{2,0},{3,1},{4,6},{5,7},{6,4},{7,5},{8,10},{9,11},{10,... | collective-permute-start | bytes 589832 | tf_op jit(solution)/shard_map/ppermute | solution.py:35
  8.5 4.2 %query_far.1 = (bf16[544,1152]{1,0:T(8,128)(2,1)S(1)}, bf16[512,1024]{1,0:T(8,128)(2,1)S(1)}) custom-call(bf16[512,1024]{1,0:T(8,128)(2,1)S(1)} %get-tuple-element.35.hg_ref, bf16[1024,4096]{1,0:T(8,128)(2,1)} %w_hbm.5, bf16[544,128]{1,0:T(8,128)(2,1)S(1)} %get-tuple-element.36.after_ref.pack_ref, bf16[768,128]{1,0:T(8,128)(2,1)S(1)} %part_sum.1.after_ref.s_ref), custom_call_target="tpu_custom_call" | custom-call | tf_op jit(solution)/shard_map/query_far/pallas_call | solution.py:269
  12.7 1.3 %collective-permute-done.1.r_ref = bf16[768,128]{1,0:T(8,128)(2,1)S(1)} collective-permute-done((bf16[768,128]{1,0:T(8,128)(2,1)S(1)}, bf16[768,128]{1,0:T(8,128)(2,1)S(1)}, u32[]{:S(2)}, u32[]{:S(2)}) %collective-permute-start.1) | collective-permute-done | bytes 196640 | tf_op jit(solution)/shard_map/ppermute | solution.py:35
  14.1 0.7 %grads.1 = (f32[512,128]{1,0:T(8,128)S(1)}, bf16[512,128]{1,0:T(8,128)(2,1)S(1)}, f32[512,128]{1,0:T(8,128)S(1)}, bf16[512,128]{1,0:T(8,128)(2,1)S(1)}, bf16[544,1152]{1,0:T(8,128)(2,1)S(1)}) custom-call(bf16[384,1024]{1,0:T(8,128)(2,1)S(1)} %copy-done.1, bf16[384,1024]{1,0:T(8,128)(2,1)S(1)} %copy-done.2, ...), custom_call_target="tpu_custom_call", output_to_operand_aliasing={{4}: (4, {})} | custom-call | tf_op jit(solution)/shard_map/grads/pallas_call | solution.py:269
  14.7 0.1 collective-permute-start.4
  14.8 1.9 %collective-permute-start.2 = (bf16[512,128]{1,0:T(8,128)(2,1)S(1)}, bf16[512,128]{1,0:T(8,128)(2,1)S(1)}, u32[]{:S(2)}, u32[]{:S(2)}) collective-permute-start(bf16[512,128]{1,0:T(8,128)(2,1)S(1)} %get-tuple-element.39.after_ref), channel_id=1, source_target_pairs={{0,4},{4,0},{8,12},{12,8},{1,5},{5,1},{9,13},{13,9},{2,6},{6,2},{1... | collective-permute-start | bytes 393224 | tf_op jit(solution)/shard_map/ppermute | solution.py:35
  16.7 1.5 %collective-permute-start.3 = (bf16[512,128]{1,0:T(8,128)(2,1)S(1)}, bf16[512,128]{1,0:T(8,128)(2,1)S(1)}, u32[]{:S(2)}, u32[]{:S(2)}) collective-permute-start(bf16[512,128]{1,0:T(8,128)(2,1)S(1)} %get-tuple-element.41), channel_id=1, source_target_pairs={{0,16},{16,0},{1,17},{17,1},{2,18},{18,2},{3,19},{19,3},{4,20},{20... | collective-permute-start | bytes 393224 | tf_op jit(solution)/shard_map/ppermute | solution.py:35
  18.2 0.0 collective-permute-done.4.got_ref
  18.2 0.3 far.1.refs_4_.far_ref
  18.5 2.3 %collective-permute-done.2.refs_1_ = bf16[512,128]{1,0:T(8,128)(2,1)S(1)} collective-permute-done((bf16[512,128]{1,0:T(8,128)(2,1)S(1)}, bf16[512,128]{1,0:T(8,128)(2,1)S(1)}, u32[]{:S(2)}, u32[]{:S(2)}) %collective-permute-start.2) | collective-permute-done | bytes 131104 | tf_op jit(solution)/shard_map/ppermute | solution.py:35
  20.8 1.5 %collective-permute-done.3.refs_3_ = bf16[512,128]{1,0:T(8,128)(2,1)S(1)} collective-permute-done((bf16[512,128]{1,0:T(8,128)(2,1)S(1)}, bf16[512,128]{1,0:T(8,128)(2,1)S(1)}, u32[]{:S(2)}, u32[]{:S(2)}) %collective-permute-start.3) | collective-permute-done | bytes 131104 | tf_op jit(solution)/shard_map/ppermute | solution.py:35
  22.3 0.1 step_0.1
  22.3 2.7 %collective-permute-start.5 = (bf16[256,128]{1,0:T(8,128)(2,1)S(1)}, bf16[256,128]{1,0:T(8,128)(2,1)S(1)}, u32[]{:S(2)}, u32[]{:S(2)}) collective-permute-start(bf16[256,128]{1,0:T(8,128)(2,1)S(1)} %get-tuple-element.44.after_ref), channel_id=1, source_target_pairs={{0,8},{4,12},{8,0},{12,4},{1,9},{5,13},{9,1},{13,5},{2,10},{6,14},... | collective-permute-start | bytes 196616 | tf_op jit(solution)/shard_map/ppermute | solution.py:35
  25.0 0.4 collective-permute-start.6
  25.5 2.7 %query_close.1.refs_4_.mine_ref = bf16[512,1024]{1,0:T(8,128)(2,1)S(1)} custom-call(bf16[512,1024]{1,0:T(8,128)(2,1)S(1)} %get-tuple-element.35.hg_ref, bf16[1024,4096]{1,0:T(8,128)(2,1)} %w_hbm.5, bf16[544,128]{1,0:T(8,128)(2,1)S(1)} %get-tuple-element.36.after_ref.pack_ref, bf16[256,128]{1,0:T(8,128)(2,1)S(1)} %get-tuple-element.44.after_ref), custom_call_target="tpu_custom_call" | custom-call | tf_op jit(solution)/shard_map/query_close/pallas_call | solution.py:269
  28.1 0.0 copy-start.4
  28.1 1.6 %collective-permute-start.12 = (bf16[544,1152]{1,0:T(8,128)(2,1)S(1)}, bf16[544,1152]{1,0:T(8,128)(2,1)S(1)}, u32[]{:S(2)}, u32[]{:S(2)}) collective-permute-start(bf16[544,1152]{1,0:T(8,128)(2,1)S(1)} %far.1.refs_4_.far_ref), channel_id=1, source_target_pairs={{0,2},{1,3},{2,0},{3,1},{4,6},{5,7},{6,4},{7,5},{8,10},{9,11},{10,... | collective-permute-start | bytes 3760136 | tf_op jit(solution)/shard_map/ppermute | solution.py:35
  29.8 1.6 %collective-permute-start.7 = (bf16[256,128]{1,0:T(8,128)(2,1)S(1)}, bf16[256,128]{1,0:T(8,128)(2,1)S(1)}, u32[]{:S(2)}, u32[]{:S(2)}) collective-permute-start(bf16[256,128]{1,0:T(8,128)(2,1)S(1)} %get-tuple-element.48.after_ref.refs_0_), channel_id=1, source_target_pairs={{0,16},{16,0},{1,17},{17,1},{2,18},{18,2},{3,19},{19,3},{4,20},{20... | collective-permute-start | bytes 196616 | tf_op jit(solution)/shard_map/ppermute | solution.py:35
  31.3 0.4 collective-permute-start.8
  31.8 1.0 %fusion = (f32[256,64]{1,0:T(8,128)S(1)}, f32[256,64]{1,0:T(8,128)S(1)}, f32[256,64]{1,0:T(8,128)S(1)}, f32[256,64]{1,0:T(8,128)S(1)}, f32[256,64]{1,0:T(8,128)S(1)}, /*index=5*/f32[256,64]{1,0:T(8,128)S(1)}) fusion(f32[64]{0:T(128)S(1)} %multiply_power_fusion, f32[256]{0:T(256)S(1)} %bitcast.6, f32[256]{0:T(256)S(1)} %broadcast_add_fusion), kind=kLoop, calls=%fused_computation.6 | loop fusion | flops 65536 | bytes 395520 | tf_op jit(solution)/shard_map/neg | solution.py:289
  32.8 0.2 maximum_maximum_fusion
  33.0 3.2 %collective-permute-done.8.refs_3_ = bf16[128,128]{1,0:T(8,128)(2,1)S(1)} collective-permute-done((bf16[128,128]{1,0:T(8,128)(2,1)S(1)}, bf16[128,128]{1,0:T(8,128)(2,1)S(1)}, u32[]{:S(2)}, u32[]{:S(2)}) %collective-permute-start.8) | collective-permute-done | bytes 32800 | tf_op jit(solution)/shard_map/ppermute | solution.py:35
  36.2 0.5 collective-permute-start.9
  36.7 2.5 %collective-permute-start.10 = (bf16[128,128]{1,0:T(8,128)(2,1)S(1)}, bf16[128,128]{1,0:T(8,128)(2,1)S(1)}, u32[]{:S(2)}, u32[]{:S(2)}) collective-permute-start(bf16[128,128]{1,0:T(8,128)(2,1)S(1)} %get-tuple-element.52.refs_2_), channel_id=1, source_target_pairs={{0,8},{4,12},{8,0},{12,4},{1,9},{5,13},{9,1},{13,5},{2,10},{6,14},... | collective-permute-start | bytes 98312 | tf_op jit(solution)/shard_map/ppermute | solution.py:35
  39.2 2.7 %query_beside.1.refs_4_ = bf16[512,1024]{1,0:T(8,128)(2,1)S(1)} custom-call(bf16[512,1024]{1,0:T(8,128)(2,1)S(1)} %get-tuple-element.35.hg_ref, bf16[1024,4096]{1,0:T(8,128)(2,1)} %w_hbm.5, bf16[544,128]{1,0:T(8,128)(2,1)S(1)} %get-tuple-element.36.after_ref.pack_ref, bf16[256,128]{1,0:T(8,128)(2,1)S(1)} %get-tuple-element.51.after_ref.refs_0_), custom_call_target="tpu_custom_call" | custom-call | tf_op jit(solution)/shard_map/query_beside/pallas_call | solution.py:269
  41.9 0.1 collective-permute-start.11
  42.0 1.7 %collective-permute-start.13 = (bf16[512,128]{1,0:T(8,128)(2,1)S(1)}, bf16[512,128]{1,0:T(8,128)(2,1)S(1)}, u32[]{:S(2)}, u32[]{:S(2)}) collective-permute-start(bf16[512,128]{1,0:T(8,128)(2,1)S(1)} %get-tuple-element.54.mine_a), channel_id=1, source_target_pairs={{0,4},{4,0},{8,12},{12,8},{1,5},{5,1},{9,13},{13,9},{2,6},{6,2},{1... | collective-permute-start | bytes 393224 | tf_op jit(solution)/shard_map/ppermute | solution.py:35
  43.6 0.4 collective-permute-start.14
  44.1 5.2 %collective-permute-done.14.got_b = bf16[256,128]{1,0:T(8,128)(2,1)S(1)} collective-permute-done((bf16[256,128]{1,0:T(8,128)(2,1)S(1)}, bf16[256,128]{1,0:T(8,128)(2,1)S(1)}, u32[]{:S(2)}, u32[]{:S(2)}) %collective-permute-start.14) | collective-permute-done | bytes 65568 | tf_op jit(solution)/shard_map/ppermute | solution.py:35
  49.3 0.5 low_rank.1
  49.8 0.1 collective-permute-start.15
  49.9 0.6 collective-permute-start.17
  50.5 0.8 %collective-permute-done.15.b_ref = bf16[544,128]{1,0:T(8,128)(2,1)S(1)} collective-permute-done((bf16[544,128]{1,0:T(8,128)(2,1)S(1)}, bf16[544,128]{1,0:T(8,128)(2,1)S(1)}, u32[]{:S(2)}, u32[]{:S(2)}) %collective-permute-start.15) | collective-permute-done | bytes 139296 | tf_op jit(solution)/shard_map/ppermute | solution.py:35
  51.3 2.1 %collective-permute-start.16 = (bf16[544,128]{1,0:T(8,128)(2,1)S(1)}, bf16[544,128]{1,0:T(8,128)(2,1)S(1)}, u32[]{:S(2)}, u32[]{:S(2)}) collective-permute-start(bf16[544,128]{1,0:T(8,128)(2,1)S(1)} %merge.1.after_ref.s_ref), channel_id=1, source_target_pairs={{0,2},{1,3},{2,0},{3,1},{4,6},{5,7},{6,4},{7,5},{8,10},{9,11},{10,... | collective-permute-start | bytes 417800 | tf_op jit(solution)/shard_map/ppermute | solution.py:35
  53.3 2.4 %collective-permute-done.17.got_b = bf16[512,128]{1,0:T(8,128)(2,1)S(1)} collective-permute-done((bf16[512,128]{1,0:T(8,128)(2,1)S(1)}, bf16[512,128]{1,0:T(8,128)(2,1)S(1)}, u32[]{:S(2)}, u32[]{:S(2)}) %collective-permute-start.17) | collective-permute-done | bytes 131104 | tf_op jit(solution)/shard_map/ppermute | solution.py:35
  55.8 0.3 norm.1
  56.1 0.1 collective-permute-start.18
  56.2 1.2 %collective-permute-done.18.b_ref = bf16[32,128]{1,0:T(8,128)(2,1)S(1)} collective-permute-done((bf16[32,128]{1,0:T(8,128)(2,1)S(1)}, bf16[32,128]{1,0:T(8,128)(2,1)S(1)}, u32[]{:S(2)}, u32[]{:S(2)}) %collective-permute-start.18) | collective-permute-done | bytes 8224 | tf_op jit(solution)/shard_map/ppermute | solution.py:35
  57.3 0.0 copy-start
  57.3 0.0 copy-start.3
  57.4 2.1 %collective-permute-start.19 = (bf16[32,128]{1,0:T(8,128)(2,1)S(1)}, bf16[32,128]{1,0:T(8,128)(2,1)S(1)}, u32[]{:S(2)}, u32[]{:S(2)}) collective-permute-start(bf16[32,128]{1,0:T(8,128)(2,1)S(1)} %norm_merge.1.sn_ref), channel_id=1, source_target_pairs={{0,2},{1,3},{2,0},{3,1},{4,6},{5,7},{6,4},{7,5},{8,10},{9,11},{10,... | collective-permute-start | bytes 24584 | tf_op jit(solution)/shard_map/ppermute | solution.py:35
  59.4 0.5 base.1
  59.9 1.2 %collective-permute-done.19.rn_ref = bf16[32,128]{1,0:T(8,128)(2,1)S(1)} collective-permute-done((bf16[32,128]{1,0:T(8,128)(2,1)S(1)}, bf16[32,128]{1,0:T(8,128)(2,1)S(1)}, u32[]{:S(2)}, u32[]{:S(2)}) %collective-permute-start.19) | collective-permute-done | bytes 8224 | tf_op jit(solution)/shard_map/ppermute | solution.py:35
  61.1 1.7 %final.1 = (f32[1024,128]{1,0:T(8,128)}, f32[128,1024]{1,0:T(8,128)}, bf16[512,1024]{1,0:T(8,128)(2,1)}) custom-call(f32[512,1024]{1,0:T(8,128)S(1)} %get-tuple-element.57.base_ref, f32[512,128]{1,0:T(8,128)S(1)} %get-tuple-element.58.low_ref, f32[512,128]{1,0:T(8,128)S(1)} %get-tuple-element.59.scale_ref, bf16[544,128]{1,0:T(8,128)(2,1)S(1)} %merge.1.after_ref.s_ref, ...), custom_call_target="tpu_custom_call" | custom-call | tf_op jit(solution)/shard_map/final/pallas_call | solution.py:269
  (25 shorter events, 0.3 us)
Async XLA Ops:
  3.1 2.8 %collective-permute-start = (bf16[768,128]{1,0:T(8,128)(2,1)S(1)}, bf16[768,128]{1,0:T(8,128)(2,1)S(1)}, u32[]{:S(2)}, u32[]{:S(2)}) collective-permute-start(bf16[768,128]{1,0:T(8,128)(2,1)S(1)} %rank.1.x_ref), channel_id=1, source_target_pairs={{0,1},{1,0},{2,3},{3,2},{4,5},{5,4},{6,7},{7,6},{8,9},{9,8},{10,11... | collective-permute-start | bytes 589832 | tf_op jit(solution)/shard_map/ppermute | solution.py:35
  5.9 8.2 %collective-permute-start.1 = (bf16[768,128]{1,0:T(8,128)(2,1)S(1)}, bf16[768,128]{1,0:T(8,128)(2,1)S(1)}, u32[]{:S(2)}, u32[]{:S(2)}) collective-permute-start(bf16[768,128]{1,0:T(8,128)(2,1)S(1)} %part_sum.1.after_ref.s_ref), channel_id=1, source_target_pairs={{0,2},{1,3},{2,0},{3,1},{4,6},{5,7},{6,4},{7,5},{8,10},{9,11},{10,... | collective-permute-start | bytes 589832 | tf_op jit(solution)/shard_map/ppermute | solution.py:35
  8.5 5.6 %copy-start.1 = (bf16[384,1024]{1,0:T(8,128)(2,1)S(1)}, bf16[384,1024]{1,0:T(8,128)(2,1)}, u32[]{:S(2)}) copy-start(bf16[384,1024]{1,0:T(8,128)(2,1)} %x_ref.1) | copy-start | bytes 2359300
  8.5 5.6 %copy-start.2 = (bf16[384,1024]{1,0:T(8,128)(2,1)S(1)}, bf16[384,1024]{1,0:T(8,128)(2,1)}, u32[]{:S(2)}) copy-start(bf16[384,1024]{1,0:T(8,128)(2,1)} %v_ref.1) | copy-start | bytes 2359300
  14.7 3.4 %collective-permute-start.4 = (bf16[544,1152]{1,0:T(8,128)(2,1)S(1)}, bf16[544,1152]{1,0:T(8,128)(2,1)S(1)}, u32[]{:S(2)}, u32[]{:S(2)}) collective-permute-start(bf16[544,1152]{1,0:T(8,128)(2,1)S(1)} %get-tuple-element.43.diag_ref), channel_id=1, source_target_pairs={{0,1},{1,0},{2,3},{3,2},{4,5},{5,4},{6,7},{7,6},{8,9},{9,8},{10,11... | collective-permute-start | bytes 3760136 | tf_op jit(solution)/shard_map/ppermute | solution.py:35
  14.8 6.0 %collective-permute-start.2 = (bf16[512,128]{1,0:T(8,128)(2,1)S(1)}, bf16[512,128]{1,0:T(8,128)(2,1)S(1)}, u32[]{:S(2)}, u32[]{:S(2)}) collective-permute-start(bf16[512,128]{1,0:T(8,128)(2,1)S(1)} %get-tuple-element.39.after_ref), channel_id=1, source_target_pairs={{0,4},{4,0},{8,12},{12,8},{1,5},{5,1},{9,13},{13,9},{2,6},{6,2},{1... | collective-permute-start | bytes 393224 | tf_op jit(solution)/shard_map/ppermute | solution.py:35
  16.7 5.6 %collective-permute-start.3 = (bf16[512,128]{1,0:T(8,128)(2,1)S(1)}, bf16[512,128]{1,0:T(8,128)(2,1)S(1)}, u32[]{:S(2)}, u32[]{:S(2)}) collective-permute-start(bf16[512,128]{1,0:T(8,128)(2,1)S(1)} %get-tuple-element.41), channel_id=1, source_target_pairs={{0,16},{16,0},{1,17},{17,1},{2,18},{18,2},{3,19},{19,3},{4,20},{20... | collective-permute-start | bytes 393224 | tf_op jit(solution)/shard_map/ppermute | solution.py:35
  22.3 7.4 %collective-permute-start.5 = (bf16[256,128]{1,0:T(8,128)(2,1)S(1)}, bf16[256,128]{1,0:T(8,128)(2,1)S(1)}, u32[]{:S(2)}, u32[]{:S(2)}) collective-permute-start(bf16[256,128]{1,0:T(8,128)(2,1)S(1)} %get-tuple-element.44.after_ref), channel_id=1, source_target_pairs={{0,8},{4,12},{8,0},{12,4},{1,9},{5,13},{9,1},{13,5},{2,10},{6,14},... | collective-permute-start | bytes 196616 | tf_op jit(solution)/shard_map/ppermute | solution.py:35
  25.0 4.7 %collective-permute-start.6 = (bf16[256,128]{1,0:T(8,128)(2,1)S(1)}, bf16[256,128]{1,0:T(8,128)(2,1)S(1)}, u32[]{:S(2)}, u32[]{:S(2)}) collective-permute-start(bf16[256,128]{1,0:T(8,128)(2,1)S(1)} %get-tuple-element.47), channel_id=1, source_target_pairs={{0,4},{4,0},{8,12},{12,8},{1,5},{5,1},{9,13},{13,9},{2,6},{6,2},{1... | collective-permute-start | bytes 196616 | tf_op jit(solution)/shard_map/ppermute | solution.py:35
  28.1 3.6 %copy-start.4 = (s32[256]{0:T(256)S(1)}, s32[256]{0:T(256)}, u32[]{:S(2)}) copy-start(s32[256]{0:T(256)} %param.15) | copy-start | bytes 3076
  28.1 31.3 %collective-permute-start.12 = (bf16[544,1152]{1,0:T(8,128)(2,1)S(1)}, bf16[544,1152]{1,0:T(8,128)(2,1)S(1)}, u32[]{:S(2)}, u32[]{:S(2)}) collective-permute-start(bf16[544,1152]{1,0:T(8,128)(2,1)S(1)} %far.1.refs_4_.far_ref), channel_id=1, source_target_pairs={{0,2},{1,3},{2,0},{3,1},{4,6},{5,7},{6,4},{7,5},{8,10},{9,11},{10,... | collective-permute-start | bytes 3760136 | tf_op jit(solution)/shard_map/ppermute | solution.py:35
  29.8 6.4 %collective-permute-start.7 = (bf16[256,128]{1,0:T(8,128)(2,1)S(1)}, bf16[256,128]{1,0:T(8,128)(2,1)S(1)}, u32[]{:S(2)}, u32[]{:S(2)}) collective-permute-start(bf16[256,128]{1,0:T(8,128)(2,1)S(1)} %get-tuple-element.48.after_ref.refs_0_), channel_id=1, source_target_pairs={{0,16},{16,0},{1,17},{17,1},{2,18},{18,2},{3,19},{19,3},{4,20},{20... | collective-permute-start | bytes 196616 | tf_op jit(solution)/shard_map/ppermute | solution.py:35
  31.3 4.8 %collective-permute-start.8 = (bf16[128,128]{1,0:T(8,128)(2,1)S(1)}, bf16[128,128]{1,0:T(8,128)(2,1)S(1)}, u32[]{:S(2)}, u32[]{:S(2)}) collective-permute-start(bf16[128,128]{1,0:T(8,128)(2,1)S(1)} %get-tuple-element.50), channel_id=1, source_target_pairs={{0,8},{4,12},{8,0},{12,4},{1,9},{5,13},{9,1},{13,5},{2,10},{6,14},... | collective-permute-start | bytes 98312 | tf_op jit(solution)/shard_map/ppermute | solution.py:35
  36.2 5.7 %collective-permute-start.9 = (bf16[256,128]{1,0:T(8,128)(2,1)S(1)}, bf16[256,128]{1,0:T(8,128)(2,1)S(1)}, u32[]{:S(2)}, u32[]{:S(2)}) collective-permute-start(bf16[256,128]{1,0:T(8,128)(2,1)S(1)} %get-tuple-element.51.after_ref.refs_0_), channel_id=1, source_target_pairs={{0,8},{4,12},{8,0},{12,4},{1,9},{5,13},{9,1},{13,5},{2,10},{6,14},... | collective-permute-start | bytes 196616 | tf_op jit(solution)/shard_map/ppermute | solution.py:35
  36.7 5.1 %collective-permute-start.10 = (bf16[128,128]{1,0:T(8,128)(2,1)S(1)}, bf16[128,128]{1,0:T(8,128)(2,1)S(1)}, u32[]{:S(2)}, u32[]{:S(2)}) collective-permute-start(bf16[128,128]{1,0:T(8,128)(2,1)S(1)} %get-tuple-element.52.refs_2_), channel_id=1, source_target_pairs={{0,8},{4,12},{8,0},{12,4},{1,9},{5,13},{9,1},{13,5},{2,10},{6,14},... | collective-permute-start | bytes 98312 | tf_op jit(solution)/shard_map/ppermute | solution.py:35
  41.9 17.5 %collective-permute-start.11 = (bf16[512,1024]{1,0:T(8,128)(2,1)S(1)}, bf16[512,1024]{1,0:T(8,128)(2,1)S(1)}, u32[]{:S(2)}, u32[]{:S(2)}) collective-permute-start(bf16[512,1024]{1,0:T(8,128)(2,1)S(1)} %get-tuple-element.53), channel_id=1, source_target_pairs={{0,1},{1,0},{2,3},{3,2},{4,5},{5,4},{6,7},{7,6},{8,9},{9,8},{10,11... | collective-permute-start | bytes 3145736 | tf_op jit(solution)/shard_map/ppermute | solution.py:35
  42.0 7.3 %collective-permute-start.13 = (bf16[512,128]{1,0:T(8,128)(2,1)S(1)}, bf16[512,128]{1,0:T(8,128)(2,1)S(1)}, u32[]{:S(2)}, u32[]{:S(2)}) collective-permute-start(bf16[512,128]{1,0:T(8,128)(2,1)S(1)} %get-tuple-element.54.mine_a), channel_id=1, source_target_pairs={{0,4},{4,0},{8,12},{12,8},{1,5},{5,1},{9,13},{13,9},{2,6},{6,2},{1... | collective-permute-start | bytes 393224 | tf_op jit(solution)/shard_map/ppermute | solution.py:35
  43.6 5.7 %collective-permute-start.14 = (bf16[256,128]{1,0:T(8,128)(2,1)S(1)}, bf16[256,128]{1,0:T(8,128)(2,1)S(1)}, u32[]{:S(2)}, u32[]{:S(2)}) collective-permute-start(bf16[256,128]{1,0:T(8,128)(2,1)S(1)} %get-tuple-element.55.mine_b), channel_id=1, source_target_pairs={{0,4},{4,0},{8,12},{12,8},{1,5},{5,1},{9,13},{13,9},{2,6},{6,2},{1... | collective-permute-start | bytes 196616 | tf_op jit(solution)/shard_map/ppermute | solution.py:35
  49.8 1.4 %collective-permute-start.15 = (bf16[544,128]{1,0:T(8,128)(2,1)S(1)}, bf16[544,128]{1,0:T(8,128)(2,1)S(1)}, u32[]{:S(2)}, u32[]{:S(2)}) collective-permute-start(bf16[544,128]{1,0:T(8,128)(2,1)S(1)} %get-tuple-element.56.a_ref), channel_id=1, source_target_pairs={{0,1},{1,0},{2,3},{3,2},{4,5},{5,4},{6,7},{7,6},{8,9},{9,8},{10,11... | collective-permute-start | bytes 417800 | tf_op jit(solution)/shard_map/ppermute | solution.py:35
  49.9 5.9 %collective-permute-start.17 = (bf16[512,128]{1,0:T(8,128)(2,1)S(1)}, bf16[512,128]{1,0:T(8,128)(2,1)S(1)}, u32[]{:S(2)}, u32[]{:S(2)}) collective-permute-start(bf16[512,128]{1,0:T(8,128)(2,1)S(1)} %get-tuple-element.60.mine_b), channel_id=1, source_target_pairs={{0,16},{16,0},{1,17},{17,1},{2,18},{18,2},{3,19},{19,3},{4,20},{20... | collective-permute-start | bytes 393224 | tf_op jit(solution)/shard_map/ppermute | solution.py:35
  51.3 9.8 %collective-permute-start.16 = (bf16[544,128]{1,0:T(8,128)(2,1)S(1)}, bf16[544,128]{1,0:T(8,128)(2,1)S(1)}, u32[]{:S(2)}, u32[]{:S(2)}) collective-permute-start(bf16[544,128]{1,0:T(8,128)(2,1)S(1)} %merge.1.after_ref.s_ref), channel_id=1, source_target_pairs={{0,2},{1,3},{2,0},{3,1},{4,6},{5,7},{6,4},{7,5},{8,10},{9,11},{10,... | collective-permute-start | bytes 417800 | tf_op jit(solution)/shard_map/ppermute | solution.py:35
  56.1 1.2 %collective-permute-start.18 = (bf16[32,128]{1,0:T(8,128)(2,1)S(1)}, bf16[32,128]{1,0:T(8,128)(2,1)S(1)}, u32[]{:S(2)}, u32[]{:S(2)}) collective-permute-start(bf16[32,128]{1,0:T(8,128)(2,1)S(1)} %get-tuple-element.61.a_ref), channel_id=1, source_target_pairs={{0,1},{1,0},{2,3},{3,2},{4,5},{5,4},{6,7},{7,6},{8,9},{9,8},{10,11... | collective-permute-start | bytes 24584 | tf_op jit(solution)/shard_map/ppermute | solution.py:35
  57.3 3.7 %copy-start = (f32[1024,128]{1,0:T(8,128)S(1)}, f32[1024,128]{1,0:T(8,128)}, u32[]{:S(2)}) copy-start(f32[1024,128]{1,0:T(8,128)} %a_ref.1) | copy-start | bytes 1572868
  57.3 3.7 %copy-start.3 = (f32[128,1024]{1,0:T(8,128)S(1)}, f32[128,1024]{1,0:T(8,128)}, u32[]{:S(2)}) copy-start(f32[128,1024]{1,0:T(8,128)} %b_ref.1) | copy-start | bytes 1572868
  57.4 3.7 %collective-permute-start.19 = (bf16[32,128]{1,0:T(8,128)(2,1)S(1)}, bf16[32,128]{1,0:T(8,128)(2,1)S(1)}, u32[]{:S(2)}, u32[]{:S(2)}) collective-permute-start(bf16[32,128]{1,0:T(8,128)(2,1)S(1)} %norm_merge.1.sn_ref), channel_id=1, source_target_pairs={{0,2},{1,3},{2,0},{3,1},{4,6},{5,7},{6,4},{7,5},{8,10},{9,11},{10,... | collective-permute-start | bytes 24584 | tf_op jit(solution)/shard_map/ppermute | solution.py:35

commit v9 on v8

--- a/solution.py
+++ b/solution.py
@@ -169,25 +169,10 @@
     out_ref[...] = (keep_ref[...].astype(F32) + got_ref[...].astype(F32)).astype(BF)
 
 
-def halved(plan):
-    return sum(step[0] == "halve" for step in plan)
-
-
-def step_kernel(plan, *refs):
-    ins, outs = list(refs[: 2 * len(plan)]), list(refs[2 * len(plan) :])
-    waits, passed = plan[0][3]
-    outs = outs[waits + passed :]
-    outs = outs[: len(outs) - passed - halved(plan)] + outs[len(outs) - halved(plan) :]
-    for kind, axis, bit, _ in plan:
-        mine, got = ins.pop(0), ins.pop(0)
-        if kind == "halve":
-            total = outs.pop()
-            total[...] = mine[...] + got[...].astype(F32)
-            halve(axis, bit, total, outs.pop(0), outs.pop(0))
-        elif kind == "sum":
-            sum_kernel(mine, got, outs.pop(0))
-        else:
-            join(axis, bit, mine, got, outs.pop(0))
+def step_kernel(waits, mine_a, got_a, mine_b, got_b, *refs):
+    sum_a, sum_b = refs[waits : waits + 2]
+    sum_kernel(mine_a, got_a, sum_a)
+    sum_kernel(mine_b, got_b, sum_b)
 
 
 def place_kernel(pos_ref, after_ref, out_ref):
@@ -199,21 +184,12 @@
     return jnp.broadcast_to(jnp.sum(x * x), (8, LANES))
 
 
-def low_kernel(axis, bit, hg_ref, mine_a, got_a, mine_b, got_b, pack_ref, ga_ref, gb_ref):
-    join(axis, bit, mine_a, got_a, ga_ref)
+def low_kernel(way_a, way_b, hg_ref, mine_a, got_a, mine_b, got_b, pack_ref, ga_ref, gb_ref):
+    join(*way_a, mine_a, got_a, ga_ref)
     count = hg_ref.shape[0]
     pack_ref[:count] = dot(hg_ref[...], ga_ref[...]).astype(BF)
-    pack_ref[count:] = split_terms(square_sum(ga_ref))
-    join(axis, bit, mine_b, got_b, gb_ref)
-
-
-def norm_kernel(axis, bit, mine_b, got_b, gb_ref, norm_ref):
-    join(axis, bit, mine_b, got_b, gb_ref)
-    norm_ref[...] = split_terms(square_sum(gb_ref))
-
-
-def norm_merge_kernel(a_ref, b_ref, out_ref):
-    out_ref[...] = split_terms(join_terms(a_ref[...]) + join_terms(b_ref[...]))
+    join(*way_b, mine_b, got_b, gb_ref)
+    pack_ref[count:] = split_terms(square_sum(ga_ref) + square_sum(gb_ref))
 
 
 def base_kernel(mine_ref, near_ref, far_ref, far_got, after_ref, base_ref, low_ref, scale_ref):
@@ -230,12 +206,11 @@
 
 
 def final_kernel(
-    base_ref, low_ref, scale_ref, s_ref, r_ref, sn_ref, rn_ref, ga_ref, gb_ref, a_ref, b_ref, cos_ref, sin_ref,
+    base_ref, low_ref, scale_ref, s_ref, r_ref, ga_ref, gb_ref, a_ref, b_ref, cos_ref, sin_ref,
     a_hbm, b_hbm, q_hbm, new_a, new_b, half_b, out, sems,
 ):
     count, width = base_ref.shape
     total = join_terms(s_ref[count:]) + join_terms(r_ref[count:])
-    total = total + (join_terms(sn_ref[...]) + join_terms(rn_ref[...]))
     rate = (LEARN * lax.rsqrt(total + NORM_EPS))[0:1]
     for c in blocks_of(width):
         fresh = b_ref[:, c] - rate * gb_ref[c].astype(F32)
@@ -302,12 +277,7 @@
     def cross(x, axis, bit):
         return swap(x, axis, sizes[axis], 1 << bit)
 
-    def path(down, across):
-        ways = down + across + down[::-1]
-        after = [("halve",) + way for way in down[1:]] + [("sum", None, None)] * (1 + len(across))
-        return list(zip(ways, after + [("join",) + way for way in down[::-1]]))
-
-    path_a, path_b = path(z_bits, x_bits), path(x_bits + z_bits, [])
+    path_a, path_b = z_bits + x_bits + z_bits[:1], x_bits[:1] + z_bits + x_bits[1:] + x_bits[:1]
 
     def on_device(
         train_inputs, train_cotangent, factor_a, factor_b, base_weight, incoming, norm_gain, positions
@@ -358,7 +328,7 @@
         diag, distant = query((3, 2), [wide, tall], part_sum, "query_far")
         half = width // 2
         keep_a, send_a, keep_b, send_b, diag = call(
-            functools.partial(grad_kernel, (path_a[0][0], path_b[0][0])),
+            functools.partial(grad_kernel, (path_a[0], path_b[0])),
             [shape((half, rank), F32), shape((half, rank), BF)] * 2 + [wide],
             [VMEM] * 4 + [ANY],
             (train_inputs, train_cotangent, part_sum, part_far, diag),
@@ -371,76 +341,40 @@
         far = call(far_kernel, wide, [VMEM] * 3 + [ANY], (distant, diag, diag_got, send_a), "far")
         far_got = swap(far, "tp", n_tp, 2)
 
-        def step_call(parts, after, name, passed=()):
-            ins, outs, scratch = [], [], []
-            for step, (mine, got) in parts:
-                size = mine.shape[0]
-                ins += [mine, got]
-                if step[0] == "halve":
-                    outs += [shape((size // 2, rank), F32), shape((size // 2, rank), BF)]
-                    scratch.append(vmem(size))
-                else:
-                    outs.append(shape((2 * size if step[0] == "join" else size, rank), BF))
-            first = len(ins) + len(after)
-            made = call(
-                functools.partial(step_kernel, [step + ((len(after), len(passed)),) for step, _ in parts]),
-                outs + [shape(x.shape, x.dtype) for x in passed],
-                [VMEM] * len(ins) + [ANY] * (len(after) + len(passed)),
-                (*ins, *after, *passed),
-                name,
-                scratch,
-                [VMEM] * len(outs) + [ANY] * len(passed),
-                aliases={first + i: len(outs) + i for i in range(len(passed))},
+        (close,) = query((0,), [tall], far, "query_close")
+        mine_a, mine_b, after, passed = keep_a, keep_b, [close], []
+        for i, (way_a, way_b) in enumerate(zip(path_a[:-1], path_b[:-1])):
+            got_a, got_b = cross(send_a, *way_a), cross(send_b, *way_b)
+            mine_a, mine_b, *made = call(
+                functools.partial(step_kernel, len(after) + len(passed)),
+                [shape((half, rank), BF)] * 2 + [shape(x.shape, x.dtype) for x in passed],
+                [VMEM] * 4 + [ANY] * (len(after) + len(passed)),
+                (mine_a, got_a, mine_b, got_b, *after, *passed),
+                f"step_{i}",
+                out_specs=[VMEM] * 2 + [ANY] * len(passed),
+                aliases={4 + len(after) + k: 2 + k for k in range(len(passed))},
             )
-            made = list(made)
-            return [[made.pop(0) for _ in range(1 + (step[0] == "halve"))] for step, _ in parts] + made
-
-        state_a, state_b, after, passed = [keep_a, send_a], [keep_b, send_b], [far], []
-        for i, ((way_a, step_a), (way_b, step_b)) in enumerate(zip(path_a[:-1], path_b)):
-            got_a, got_b = cross(state_a[-1], *way_a), cross(state_b[-1], *way_b)
-            state_a, state_b, *made = step_call(
-                [(step_a, (state_a[0], got_a)), (step_b, (state_b[0], got_b))], after, f"step_{i}", passed
-            )
+            send_a, send_b = mine_a, mine_b
             after, passed = [], []
             if made:
                 beside_got = swap(made[0], "tp", n_tp, 1)
             if i == 0:
-                after = query((0,), [tall], state_a[-1], "query_close")
-                (close,) = after
-            if i == 1:
+                passed = query((1,), [tall], mine_a, "query_beside")
                 pos = positions.reshape(-1, LANES)
-                places = call(place_kernel, shape(pos.shape, F32), [VMEM, ANY], (pos, state_a[-1]), "places")
-                after = list(turn_tables(places.reshape(rows), steps))
-                cos, sin = after
-            if i == 2:
-                passed = query((1,), [tall], state_a[-1], "query_beside")
-        way = path_a[-1][0]
-        mine_a, mine_b = state_a[-1], state_b[-1]
-        step_pack, grad_a, mine_b = call(
-            functools.partial(low_kernel, *way),
-            [shape((count + EXTRA, rank), BF), shape((width, rank), BF), shape((2 * mine_b.shape[0], rank), BF)],
+                places = call(place_kernel, shape(pos.shape, F32), [VMEM, ANY], (pos, mine_a), "places")
+                cos, sin = turn_tables(places.reshape(rows), steps)
+                after = [cos, sin]
+        step_pack, grad_a, grad_b = call(
+            functools.partial(low_kernel, path_a[-1], path_b[-1]),
+            [shape((count + EXTRA, rank), BF), shape((width, rank), BF), shape((width, rank), BF)],
             [VMEM] * 5,
-            (gained, mine_a, cross(mine_a, *way), mine_b, cross(mine_b, *way)),
+            (gained, mine_a, cross(mine_a, *path_a[-1]), mine_b, cross(mine_b, *path_b[-1])),
             "low_rank",
         )
         step_got = swap(step_pack, "tp", n_tp, 1)
         step_sum = call(merge_kernel, shape((count + EXTRA, rank), BF), [VMEM] * 2, (step_pack, step_got), "merge")
         step_far = swap(step_sum, "tp", n_tp, 2)
 
-        for way_b, step_b in path_b[len(path_a) : -1]:
-            ((mine_b,),) = step_call([(step_b, (mine_b, cross(mine_b, *way_b)))], [], "join_b")
-        way = path_b[-1][0]
-        grad_b, norm = call(
-            functools.partial(norm_kernel, *way),
-            [shape((width, rank), BF), shape((EXTRA, LANES), BF)],
-            [VMEM] * 2,
-            (mine_b, cross(mine_b, *way)),
-            "norm",
-        )
-        norm = call(
-            norm_merge_kernel, shape((EXTRA, LANES), BF), [VMEM] * 2, (norm, swap(norm, "tp", n_tp, 1)), "norm_merge"
-        )
-        norm_far = swap(norm, "tp", n_tp, 2)
         base, low, scale = call(
             base_kernel,
             [shape((count, width), F32), shape((count, rank), F32), shape((count, LANES), F32)],
@@ -451,8 +385,8 @@
         new_a, new_b, queries = call(
             final_kernel,
             [shape((width, rank), F32), shape((rank, width), F32), tall],
-            [VMEM] * 13,
-            (base, low, scale, step_sum, step_far, norm, norm_far, grad_a, grad_b, factor_a, factor_b, cos, sin),
+            [VMEM] * 11,
+            (base, low, scale, step_sum, step_far, grad_a, grad_b, factor_a, factor_b, cos, sin),
             "final",
             [pltpu.VMEM((width, rank), F32), pltpu.VMEM((rank, width), F32),
              pltpu.VMEM((rank, width), BF), pltpu.VMEM((count, width), BF), dma(2 + count // LANES)],

time: 63 us -> 56.9 us (0.903)
  starting transfers between devices: 23.3 us -> 17.6 us
    ppermute x20 -> x15, starting transfers between devices: 23.3 us -> 17.6 us  [swap(): return lax.ppermute(x, axis, [(i, i ^ k) for i in range(n)])]
    pallas_call x19 -> x16, Pallas kernels: 18.5 us -> 18.2 us  [call(): pl.pallas_call(kernel, out_shape=outs, in_specs=in_specs, out_specs=out_s...]
    ppermute x20 -> x15, waiting for transfers between devices: 19 us -> 18.9 us  [swap(): return lax.ppermute(x, axis, [(i, i ^ k) for i in range(n)])]
  transfers between devices with their start and end apart: 20 -> 15, of which waited for: 9 -> 9; matrix products, arithmetic and copies ran while one was open for 2% -> 2% of each run, Pallas kernels for 21% -> 23%
where the time goes in v9:
time: 56.9 us; the launch traced here: 56.7 us
  waiting for transfers between devices  18.9 us (33%)
  Pallas kernels  18.2 us (32%)
  starting transfers between devices  17.6 us (31%)
  other arithmetic  1.21 us (2%)
  between operations  0.79 us (1%)
    ppermute x15, waiting for transfers between devices, swap(): return lax.ppermute(x, axis, [(i, i ^ k) for i in range(n)])  18.9 us
    pallas_call x16, Pallas kernels, call(): pl.pallas_call(kernel, out_shape=outs, in_specs=in_specs, out_specs=out_s...  18.2 us
    ppermute x15, starting transfers between devices, swap(): return lax.ppermute(x, axis, [(i, i ^ k) for i in range(n)])  17.6 us
  transfers between devices with their start and end apart: 15, of which 9 were waited for; matrix products, arithmetic and copies ran while one was open for 2% of the time, Pallas kernels for 23%

profile of v9, /device:TPU:0, one launch (start us, length us, event | category | flops | bytes accessed | tf_op | source)
XLA Modules:
  0.0 56.7 jit_solution(14097425263913809498)
XLA Ops:
  0.6 2.4 %rank.1.x_ref = bf16[768,128]{1,0:T(8,128)(2,1)S(1)} custom-call(bf16[384,1024]{1,0:T(8,128)(2,1)} %x_ref.1, bf16[384,1024]{1,0:T(8,128)(2,1)} %v_ref.1, f32[1024,128]{1,0:T(8,128)} %a_ref.1, f32[128,1024]{1,0:T(8,128)} %b_ref.1), custom_call_target="tpu_custom_call" | custom-call | tf_op jit(solution)/shard_map/rank/pallas_call | solution.py:244
  3.1 0.5 collective-permute-start
  3.6 2.2 %prep.1 = (bf16[512,1024]{1,0:T(8,128)(2,1)S(1)}, bf16[544,128]{1,0:T(8,128)(2,1)S(1)}) custom-call(bf16[512,1024]{1,0:T(8,128)(2,1)} %bitcast.8, f32[1,1024]{1,0:T(1,128)} %bitcast.9, f32[1024,128]{1,0:T(8,128)} %a_ref.1), custom_call_target="tpu_custom_call" | custom-call | tf_op jit(solution)/shard_map/prep/pallas_call | solution.py:244
  5.8 0.0 collective-permute-done.got_ref
  5.9 2.6 %collective-permute-start.1 = (bf16[768,128]{1,0:T(8,128)(2,1)S(1)}, bf16[768,128]{1,0:T(8,128)(2,1)S(1)}, u32[]{:S(2)}, u32[]{:S(2)}) collective-permute-start(bf16[768,128]{1,0:T(8,128)(2,1)S(1)} %part_sum.1.after_ref.s_ref), channel_id=1, source_target_pairs={{0,2},{1,3},{2,0},{3,1},{4,6},{5,7},{6,4},{7,5},{8,10},{9,11},{10,... | collective-permute-start | bytes 589832 | tf_op jit(solution)/shard_map/ppermute | solution.py:35
  8.5 4.2 %query_far.1 = (bf16[544,1152]{1,0:T(8,128)(2,1)S(1)}, bf16[512,1024]{1,0:T(8,128)(2,1)S(1)}) custom-call(bf16[512,1024]{1,0:T(8,128)(2,1)S(1)} %get-tuple-element.28.hg_ref, bf16[1024,4096]{1,0:T(8,128)(2,1)} %w_hbm.5, bf16[544,128]{1,0:T(8,128)(2,1)S(1)} %get-tuple-element.29.after_ref.pack_ref, bf16[768,128]{1,0:T(8,128)(2,1)S(1)} %part_sum.1.after_ref.s_ref), custom_call_target="tpu_custom_call" | custom-call | tf_op jit(solution)/shard_map/query_far/pallas_call | solution.py:244
  12.7 1.3 %collective-permute-done.1.r_ref = bf16[768,128]{1,0:T(8,128)(2,1)S(1)} collective-permute-done((bf16[768,128]{1,0:T(8,128)(2,1)S(1)}, bf16[768,128]{1,0:T(8,128)(2,1)S(1)}, u32[]{:S(2)}, u32[]{:S(2)}) %collective-permute-start.1) | collective-permute-done | bytes 196640 | tf_op jit(solution)/shard_map/ppermute | solution.py:35
  14.1 0.0 copy-done.2
  14.1 0.7 %grads.1 = (f32[512,128]{1,0:T(8,128)S(1)}, bf16[512,128]{1,0:T(8,128)(2,1)S(1)}, f32[512,128]{1,0:T(8,128)S(1)}, bf16[512,128]{1,0:T(8,128)(2,1)S(1)}, bf16[544,1152]{1,0:T(8,128)(2,1)S(1)}) custom-call(bf16[384,1024]{1,0:T(8,128)(2,1)S(1)} %copy-done.1, bf16[384,1024]{1,0:T(8,128)(2,1)S(1)} %copy-done.2, ...), custom_call_target="tpu_custom_call", output_to_operand_aliasing={{4}: (4, {})} | custom-call | tf_op jit(solution)/shard_map/grads/pallas_call | solution.py:244
  14.7 0.1 collective-permute-start.2
  14.8 1.9 %collective-permute-start.3 = (bf16[512,128]{1,0:T(8,128)(2,1)S(1)}, bf16[512,128]{1,0:T(8,128)(2,1)S(1)}, u32[]{:S(2)}, u32[]{:S(2)}) collective-permute-start(bf16[512,128]{1,0:T(8,128)(2,1)S(1)} %get-tuple-element.33.after_ref), channel_id=1, source_target_pairs={{0,4},{4,0},{8,12},{12,8},{1,5},{5,1},{9,13},{13,9},{2,6},{6,2},{1... | collective-permute-start | bytes 393224 | tf_op jit(solution)/shard_map/ppermute | solution.py:35
  16.7 1.5 %collective-permute-start.4 = (bf16[512,128]{1,0:T(8,128)(2,1)S(1)}, bf16[512,128]{1,0:T(8,128)(2,1)S(1)}, u32[]{:S(2)}, u32[]{:S(2)}) collective-permute-start(bf16[512,128]{1,0:T(8,128)(2,1)S(1)} %get-tuple-element.36), channel_id=1, source_target_pairs={{0,16},{16,0},{1,17},{17,1},{2,18},{18,2},{3,19},{19,3},{4,20},{20... | collective-permute-start | bytes 393224 | tf_op jit(solution)/shard_map/ppermute | solution.py:35
  18.2 0.0 collective-permute-done.2.got_ref
  18.2 0.3 far.1.after_ref.far_ref
  18.5 2.7 %query_close.1.refs_0_.mine_ref = bf16[512,1024]{1,0:T(8,128)(2,1)S(1)} custom-call(bf16[512,1024]{1,0:T(8,128)(2,1)S(1)} %get-tuple-element.28.hg_ref, bf16[1024,4096]{1,0:T(8,128)(2,1)} %w_hbm.5, bf16[544,128]{1,0:T(8,128)(2,1)S(1)} %get-tuple-element.29.after_ref.pack_ref, bf16[544,1152]{1,0:T(8,128)(2,1)S(1)} %far.1.after_ref.far_ref), custom_call_target="tpu_custom_call" | custom-call | tf_op jit(solution)/shard_map/query_close/pallas_call | solution.py:244
  21.2 0.0 copy-start.4
  21.2 1.6 %collective-permute-start.8 = (bf16[544,1152]{1,0:T(8,128)(2,1)S(1)}, bf16[544,1152]{1,0:T(8,128)(2,1)S(1)}, u32[]{:S(2)}, u32[]{:S(2)}) collective-permute-start(bf16[544,1152]{1,0:T(8,128)(2,1)S(1)} %far.1.after_ref.far_ref), channel_id=1, source_target_pairs={{0,2},{1,3},{2,0},{3,1},{4,6},{5,7},{6,4},{7,5},{8,10},{9,11},{10,... | collective-permute-start | bytes 3760136 | tf_op jit(solution)/shard_map/ppermute | solution.py:35
  22.8 0.0 collective-permute-done.3.got_a
  22.8 0.0 collective-permute-done.4.got_b
  22.8 2.7 %collective-permute-start.5 = (bf16[512,128]{1,0:T(8,128)(2,1)S(1)}, bf16[512,128]{1,0:T(8,128)(2,1)S(1)}, u32[]{:S(2)}, u32[]{:S(2)}) collective-permute-start(bf16[512,128]{1,0:T(8,128)(2,1)S(1)} %get-tuple-element.37.after_ref.mine_a), channel_id=1, source_target_pairs={{0,8},{4,12},{8,0},{12,4},{1,9},{5,13},{9,1},{13,5},{2,10},{6,14},... | collective-permute-start | bytes 393224 | tf_op jit(solution)/shard_map/ppermute | solution.py:35
  25.5 1.4 %collective-permute-start.6 = (bf16[512,128]{1,0:T(8,128)(2,1)S(1)}, bf16[512,128]{1,0:T(8,128)(2,1)S(1)}, u32[]{:S(2)}, u32[]{:S(2)}) collective-permute-start(bf16[512,128]{1,0:T(8,128)(2,1)S(1)} %get-tuple-element.38.mine_b), channel_id=1, source_target_pairs={{0,4},{4,0},{8,12},{12,8},{1,5},{5,1},{9,13},{13,9},{2,6},{6,2},{1... | collective-permute-start | bytes 393224 | tf_op jit(solution)/shard_map/ppermute | solution.py:35
  26.9 1.0 %fusion = (f32[256,64]{1,0:T(8,128)S(1)}, f32[256,64]{1,0:T(8,128)S(1)}, f32[256,64]{1,0:T(8,128)S(1)}, f32[256,64]{1,0:T(8,128)S(1)}, f32[256,64]{1,0:T(8,128)S(1)}, /*index=5*/f32[256,64]{1,0:T(8,128)S(1)}) fusion(f32[64]{0:T(128)S(1)} %multiply_power_fusion, f32[256]{0:T(256)S(1)} %bitcast.6, f32[256]{0:T(256)S(1)} %broadcast_add_fusion), kind=kLoop, calls=%fused_computation.6 | loop fusion | flops 65536 | bytes 395520 | tf_op jit(solution)/shard_map/neg | solution.py:264
  27.9 2.7 %query_beside.1.refs_2_ = bf16[512,1024]{1,0:T(8,128)(2,1)S(1)} custom-call(bf16[512,1024]{1,0:T(8,128)(2,1)S(1)} %get-tuple-element.28.hg_ref, bf16[1024,4096]{1,0:T(8,128)(2,1)} %w_hbm.5, bf16[544,128]{1,0:T(8,128)(2,1)S(1)} %get-tuple-element.29.after_ref.pack_ref, bf16[512,128]{1,0:T(8,128)(2,1)S(1)} %get-tuple-element.37.after_ref.mine_a), custom_call_target="tpu_custom_call" | custom-call | tf_op jit(solution)/shard_map/query_beside/pallas_call | solution.py:244
  30.6 0.2 maximum_maximum_fusion
  30.8 0.9 %collective-permute-done.5.got_a = bf16[512,128]{1,0:T(8,128)(2,1)S(1)} collective-permute-done((bf16[512,128]{1,0:T(8,128)(2,1)S(1)}, bf16[512,128]{1,0:T(8,128)(2,1)S(1)}, u32[]{:S(2)}, u32[]{:S(2)}) %collective-permute-start.5) | collective-permute-done | bytes 131104 | tf_op jit(solution)/shard_map/ppermute | solution.py:35
  31.7 0.4 collective-permute-done.6.got_b
  32.1 0.1 step_1.1
  32.2 0.1 collective-permute-start.7
  32.3 1.2 %collective-permute-start.10 = (bf16[512,128]{1,0:T(8,128)(2,1)S(1)}, bf16[512,128]{1,0:T(8,128)(2,1)S(1)}, u32[]{:S(2)}, u32[]{:S(2)}) collective-permute-start(bf16[512,128]{1,0:T(8,128)(2,1)S(1)} %get-tuple-element.41.mine_b), channel_id=1, source_target_pairs={{0,8},{4,12},{8,0},{12,4},{1,9},{5,13},{9,1},{13,5},{2,10},{6,14},... | collective-permute-start | bytes 393224 | tf_op jit(solution)/shard_map/ppermute | solution.py:35
  33.5 1.5 %collective-permute-start.9 = (bf16[512,128]{1,0:T(8,128)(2,1)S(1)}, bf16[512,128]{1,0:T(8,128)(2,1)S(1)}, u32[]{:S(2)}, u32[]{:S(2)}) collective-permute-start(bf16[512,128]{1,0:T(8,128)(2,1)S(1)} %get-tuple-element.40.mine_a), channel_id=1, source_target_pairs={{0,16},{16,0},{1,17},{17,1},{2,18},{18,2},{3,19},{19,3},{4,20},{20... | collective-permute-start | bytes 393224 | tf_op jit(solution)/shard_map/ppermute | solution.py:35
  35.0 6.9 %collective-permute-done.10.got_b = bf16[512,128]{1,0:T(8,128)(2,1)S(1)} collective-permute-done((bf16[512,128]{1,0:T(8,128)(2,1)S(1)}, bf16[512,128]{1,0:T(8,128)(2,1)S(1)}, u32[]{:S(2)}, u32[]{:S(2)}) %collective-permute-start.10) | collective-permute-done | bytes 131104 | tf_op jit(solution)/shard_map/ppermute | solution.py:35
  41.9 0.0 collective-permute-done.9.got_a
  41.9 0.1 step_2.1
  41.9 0.1 collective-permute-start.11
  42.0 1.4 %collective-permute-start.12 = (bf16[512,128]{1,0:T(8,128)(2,1)S(1)}, bf16[512,128]{1,0:T(8,128)(2,1)S(1)}, u32[]{:S(2)}, u32[]{:S(2)}) collective-permute-start(bf16[512,128]{1,0:T(8,128)(2,1)S(1)} %get-tuple-element.43.mine_b), channel_id=1, source_target_pairs={{0,16},{16,0},{1,17},{17,1},{2,18},{18,2},{3,19},{19,3},{4,20},{20... | collective-permute-start | bytes 393224 | tf_op jit(solution)/shard_map/ppermute | solution.py:35
  43.5 3.6 %collective-permute-done.11.got_a = bf16[512,128]{1,0:T(8,128)(2,1)S(1)} collective-permute-done((bf16[512,128]{1,0:T(8,128)(2,1)S(1)}, bf16[512,128]{1,0:T(8,128)(2,1)S(1)}, u32[]{:S(2)}, u32[]{:S(2)}) %collective-permute-start.11) | collective-permute-done | bytes 131104 | tf_op jit(solution)/shard_map/ppermute | solution.py:35
  47.1 0.1 collective-permute-done.12.got_b
  47.2 0.5 low_rank.1
  47.7 0.1 collective-permute-start.13
  47.8 1.3 %collective-permute-done.13.b_ref = bf16[544,128]{1,0:T(8,128)(2,1)S(1)} collective-permute-done((bf16[544,128]{1,0:T(8,128)(2,1)S(1)}, bf16[544,128]{1,0:T(8,128)(2,1)S(1)}, u32[]{:S(2)}, u32[]{:S(2)}) %collective-permute-start.13) | collective-permute-done | bytes 139296 | tf_op jit(solution)/shard_map/ppermute | solution.py:35
  49.2 0.0 copy-start
  49.2 0.0 copy-start.3
  49.2 1.0 %collective-permute-start.14 = (bf16[544,128]{1,0:T(8,128)(2,1)S(1)}, bf16[544,128]{1,0:T(8,128)(2,1)S(1)}, u32[]{:S(2)}, u32[]{:S(2)}) collective-permute-start(bf16[544,128]{1,0:T(8,128)(2,1)S(1)} %merge.1.after_ref.s_ref), channel_id=1, source_target_pairs={{0,2},{1,3},{2,0},{3,1},{4,6},{5,7},{6,4},{7,5},{8,10},{9,11},{10,... | collective-permute-start | bytes 417800 | tf_op jit(solution)/shard_map/ppermute | solution.py:35
  50.2 0.0 collective-permute-done.7.near_ref
  50.2 0.4 collective-permute-done.8.far_got
  50.6 0.5 base.1
  51.1 3.9 %collective-permute-done.14.r_ref = bf16[544,128]{1,0:T(8,128)(2,1)S(1)} collective-permute-done((bf16[544,128]{1,0:T(8,128)(2,1)S(1)}, bf16[544,128]{1,0:T(8,128)(2,1)S(1)}, u32[]{:S(2)}, u32[]{:S(2)}) %collective-permute-start.14) | collective-permute-done | bytes 139296 | tf_op jit(solution)/shard_map/ppermute | solution.py:35
  55.0 1.7 %final.1 = (f32[1024,128]{1,0:T(8,128)}, f32[128,1024]{1,0:T(8,128)}, bf16[512,1024]{1,0:T(8,128)(2,1)}) custom-call(f32[512,1024]{1,0:T(8,128)S(1)} %get-tuple-element.45.base_ref, f32[512,128]{1,0:T(8,128)S(1)} %get-tuple-element.46.low_ref, f32[512,128]{1,0:T(8,128)S(1)} %get-tuple-element.47.scale_ref, bf16[544,128]{1,0:T(8,128)(2,1)S(1)} %merge.1.after_ref.s_ref, ...), custom_call_target="tpu_custom_call" | custom-call | tf_op jit(solution)/shard_map/final/pallas_call | solution.py:244
  (12 shorter events, 0.2 us)
Async XLA Ops:
  3.1 2.8 %collective-permute-start = (bf16[768,128]{1,0:T(8,128)(2,1)S(1)}, bf16[768,128]{1,0:T(8,128)(2,1)S(1)}, u32[]{:S(2)}, u32[]{:S(2)}) collective-permute-start(bf16[768,128]{1,0:T(8,128)(2,1)S(1)} %rank.1.x_ref), channel_id=1, source_target_pairs={{0,1},{1,0},{2,3},{3,2},{4,5},{5,4},{6,7},{7,6},{8,9},{9,8},{10,11... | collective-permute-start | bytes 589832 | tf_op jit(solution)/shard_map/ppermute | solution.py:35
  5.9 8.2 %collective-permute-start.1 = (bf16[768,128]{1,0:T(8,128)(2,1)S(1)}, bf16[768,128]{1,0:T(8,128)(2,1)S(1)}, u32[]{:S(2)}, u32[]{:S(2)}) collective-permute-start(bf16[768,128]{1,0:T(8,128)(2,1)S(1)} %part_sum.1.after_ref.s_ref), channel_id=1, source_target_pairs={{0,2},{1,3},{2,0},{3,1},{4,6},{5,7},{6,4},{7,5},{8,10},{9,11},{10,... | collective-permute-start | bytes 589832 | tf_op jit(solution)/shard_map/ppermute | solution.py:35
  8.5 5.6 %copy-start.1 = (bf16[384,1024]{1,0:T(8,128)(2,1)S(1)}, bf16[384,1024]{1,0:T(8,128)(2,1)}, u32[]{:S(2)}) copy-start(bf16[384,1024]{1,0:T(8,128)(2,1)} %x_ref.1) | copy-start | bytes 2359300
  8.5 5.6 %copy-start.2 = (bf16[384,1024]{1,0:T(8,128)(2,1)S(1)}, bf16[384,1024]{1,0:T(8,128)(2,1)}, u32[]{:S(2)}) copy-start(bf16[384,1024]{1,0:T(8,128)(2,1)} %v_ref.1) | copy-start | bytes 2359300
  14.7 3.5 %collective-permute-start.2 = (bf16[544,1152]{1,0:T(8,128)(2,1)S(1)}, bf16[544,1152]{1,0:T(8,128)(2,1)S(1)}, u32[]{:S(2)}, u32[]{:S(2)}) collective-permute-start(bf16[544,1152]{1,0:T(8,128)(2,1)S(1)} %get-tuple-element.32.diag_ref), channel_id=1, source_target_pairs={{0,1},{1,0},{2,3},{3,2},{4,5},{5,4},{6,7},{7,6},{8,9},{9,8},{10,11... | collective-permute-start | bytes 3760136 | tf_op jit(solution)/shard_map/ppermute | solution.py:35
  14.8 7.9 %collective-permute-start.3 = (bf16[512,128]{1,0:T(8,128)(2,1)S(1)}, bf16[512,128]{1,0:T(8,128)(2,1)S(1)}, u32[]{:S(2)}, u32[]{:S(2)}) collective-permute-start(bf16[512,128]{1,0:T(8,128)(2,1)S(1)} %get-tuple-element.33.after_ref), channel_id=1, source_target_pairs={{0,4},{4,0},{8,12},{12,8},{1,5},{5,1},{9,13},{13,9},{2,6},{6,2},{1... | collective-permute-start | bytes 393224 | tf_op jit(solution)/shard_map/ppermute | solution.py:35
  16.7 6.1 %collective-permute-start.4 = (bf16[512,128]{1,0:T(8,128)(2,1)S(1)}, bf16[512,128]{1,0:T(8,128)(2,1)S(1)}, u32[]{:S(2)}, u32[]{:S(2)}) collective-permute-start(bf16[512,128]{1,0:T(8,128)(2,1)S(1)} %get-tuple-element.36), channel_id=1, source_target_pairs={{0,16},{16,0},{1,17},{17,1},{2,18},{18,2},{3,19},{19,3},{4,20},{20... | collective-permute-start | bytes 393224 | tf_op jit(solution)/shard_map/ppermute | solution.py:35
  21.2 4.3 %copy-start.4 = (s32[256]{0:T(256)S(1)}, s32[256]{0:T(256)}, u32[]{:S(2)}) copy-start(s32[256]{0:T(256)} %param.15) | copy-start | bytes 3076
  21.2 29.4 %collective-permute-start.8 = (bf16[544,1152]{1,0:T(8,128)(2,1)S(1)}, bf16[544,1152]{1,0:T(8,128)(2,1)S(1)}, u32[]{:S(2)}, u32[]{:S(2)}) collective-permute-start(bf16[544,1152]{1,0:T(8,128)(2,1)S(1)} %far.1.after_ref.far_ref), channel_id=1, source_target_pairs={{0,2},{1,3},{2,0},{3,1},{4,6},{5,7},{6,4},{7,5},{8,10},{9,11},{10,... | collective-permute-start | bytes 3760136 | tf_op jit(solution)/shard_map/ppermute | solution.py:35
  22.8 8.9 %collective-permute-start.5 = (bf16[512,128]{1,0:T(8,128)(2,1)S(1)}, bf16[512,128]{1,0:T(8,128)(2,1)S(1)}, u32[]{:S(2)}, u32[]{:S(2)}) collective-permute-start(bf16[512,128]{1,0:T(8,128)(2,1)S(1)} %get-tuple-element.37.after_ref.mine_a), channel_id=1, source_target_pairs={{0,8},{4,12},{8,0},{12,4},{1,9},{5,13},{9,1},{13,5},{2,10},{6,14},... | collective-permute-start | bytes 393224 | tf_op jit(solution)/shard_map/ppermute | solution.py:35
  25.5 6.6 %collective-permute-start.6 = (bf16[512,128]{1,0:T(8,128)(2,1)S(1)}, bf16[512,128]{1,0:T(8,128)(2,1)S(1)}, u32[]{:S(2)}, u32[]{:S(2)}) collective-permute-start(bf16[512,128]{1,0:T(8,128)(2,1)S(1)} %get-tuple-element.38.mine_b), channel_id=1, source_target_pairs={{0,4},{4,0},{8,12},{12,8},{1,5},{5,1},{9,13},{13,9},{2,6},{6,2},{1... | collective-permute-start | bytes 393224 | tf_op jit(solution)/shard_map/ppermute | solution.py:35
  32.2 18.1 %collective-permute-start.7 = (bf16[512,1024]{1,0:T(8,128)(2,1)S(1)}, bf16[512,1024]{1,0:T(8,128)(2,1)S(1)}, u32[]{:S(2)}, u32[]{:S(2)}) collective-permute-start(bf16[512,1024]{1,0:T(8,128)(2,1)S(1)} %get-tuple-element.39), channel_id=1, source_target_pairs={{0,1},{1,0},{2,3},{3,2},{4,5},{5,4},{6,7},{7,6},{8,9},{9,8},{10,11... | collective-permute-start | bytes 3145736 | tf_op jit(solution)/shard_map/ppermute | solution.py:35
  32.3 9.6 %collective-permute-start.10 = (bf16[512,128]{1,0:T(8,128)(2,1)S(1)}, bf16[512,128]{1,0:T(8,128)(2,1)S(1)}, u32[]{:S(2)}, u32[]{:S(2)}) collective-permute-start(bf16[512,128]{1,0:T(8,128)(2,1)S(1)} %get-tuple-element.41.mine_b), channel_id=1, source_target_pairs={{0,8},{4,12},{8,0},{12,4},{1,9},{5,13},{9,1},{13,5},{2,10},{6,14},... | collective-permute-start | bytes 393224 | tf_op jit(solution)/shard_map/ppermute | solution.py:35
  33.5 8.4 %collective-permute-start.9 = (bf16[512,128]{1,0:T(8,128)(2,1)S(1)}, bf16[512,128]{1,0:T(8,128)(2,1)S(1)}, u32[]{:S(2)}, u32[]{:S(2)}) collective-permute-start(bf16[512,128]{1,0:T(8,128)(2,1)S(1)} %get-tuple-element.40.mine_a), channel_id=1, source_target_pairs={{0,16},{16,0},{1,17},{17,1},{2,18},{18,2},{3,19},{19,3},{4,20},{20... | collective-permute-start | bytes 393224 | tf_op jit(solution)/shard_map/ppermute | solution.py:35
  41.9 5.1 %collective-permute-start.11 = (bf16[512,128]{1,0:T(8,128)(2,1)S(1)}, bf16[512,128]{1,0:T(8,128)(2,1)S(1)}, u32[]{:S(2)}, u32[]{:S(2)}) collective-permute-start(bf16[512,128]{1,0:T(8,128)(2,1)S(1)} %get-tuple-element.42.mine_a), channel_id=1, source_target_pairs={{0,4},{4,0},{8,12},{12,8},{1,5},{5,1},{9,13},{13,9},{2,6},{6,2},{1... | collective-permute-start | bytes 393224 | tf_op jit(solution)/shard_map/ppermute | solution.py:35
  42.0 5.1 %collective-permute-start.12 = (bf16[512,128]{1,0:T(8,128)(2,1)S(1)}, bf16[512,128]{1,0:T(8,128)(2,1)S(1)}, u32[]{:S(2)}, u32[]{:S(2)}) collective-permute-start(bf16[512,128]{1,0:T(8,128)(2,1)S(1)} %get-tuple-element.43.mine_b), channel_id=1, source_target_pairs={{0,16},{16,0},{1,17},{17,1},{2,18},{18,2},{3,19},{19,3},{4,20},{20... | collective-permute-start | bytes 393224 | tf_op jit(solution)/shard_map/ppermute | solution.py:35
  47.7 1.4 %collective-permute-start.13 = (bf16[544,128]{1,0:T(8,128)(2,1)S(1)}, bf16[544,128]{1,0:T(8,128)(2,1)S(1)}, u32[]{:S(2)}, u32[]{:S(2)}) collective-permute-start(bf16[544,128]{1,0:T(8,128)(2,1)S(1)} %get-tuple-element.44.a_ref), channel_id=1, source_target_pairs={{0,1},{1,0},{2,3},{3,2},{4,5},{5,4},{6,7},{7,6},{8,9},{9,8},{10,11... | collective-permute-start | bytes 417800 | tf_op jit(solution)/shard_map/ppermute | solution.py:35
  49.2 5.8 %copy-start = (f32[1024,128]{1,0:T(8,128)S(1)}, f32[1024,128]{1,0:T(8,128)}, u32[]{:S(2)}) copy-start(f32[1024,128]{1,0:T(8,128)} %a_ref.1) | copy-start | bytes 1572868
  49.2 5.8 %copy-start.3 = (f32[128,1024]{1,0:T(8,128)S(1)}, f32[128,1024]{1,0:T(8,128)}, u32[]{:S(2)}) copy-start(f32[128,1024]{1,0:T(8,128)} %b_ref.1) | copy-start | bytes 1572868
  49.2 5.8 %collective-permute-start.14 = (bf16[544,128]{1,0:T(8,128)(2,1)S(1)}, bf16[544,128]{1,0:T(8,128)(2,1)S(1)}, u32[]{:S(2)}, u32[]{:S(2)}) collective-permute-start(bf16[544,128]{1,0:T(8,128)(2,1)S(1)} %merge.1.after_ref.s_ref), channel_id=1, source_target_pairs={{0,2},{1,3},{2,0},{3,1},{4,6},{5,7},{6,4},{7,5},{8,10},{9,11},{10,... | collective-permute-start | bytes 417800 | tf_op jit(solution)/shard_map/ppermute | solution.py:35

commit v10 on v9

--- a/solution.py
+++ b/solution.py
@@ -59,15 +59,18 @@
     return [slice(i, i + LANES) for i in range(0, count, LANES)]
 
 
-def rank_kernel(x_hbm, v_hbm, a_hbm, b_hbm, out_ref, x_ref, v_ref, a_ref, b_ref, sems):
-    copies = fetch((x_hbm, a_hbm, v_hbm, b_hbm), (x_ref, a_ref, v_ref, b_ref), sems)
+def rank_kernel(x_hbm, v_hbm, a_hbm, b_hbm, h_hbm, out_ref, a16_ref, h_ref, x_ref, v_ref, a_ref, b_ref, sems):
+    copies = fetch((x_hbm, a_hbm, v_hbm, b_hbm, h_hbm), (x_ref, a_ref, v_ref, b_ref, h_ref), sems)
     count = x_ref.shape[0]
+    copies[1].wait()
+    a16_ref[...] = a_ref[...].astype(BF)
     copies[0].wait()
-    copies[1].wait()
-    out_ref[:count] = dot(x_ref[...], a_ref[...].astype(BF)).astype(BF)
+    out_ref[:count] = dot(x_ref[...], a16_ref[...]).astype(BF)
+    copies[3].wait()
+    b16 = b_ref[...].astype(BF)
     copies[2].wait()
-    copies[3].wait()
-    out_ref[count:] = dot(v_ref[...], b_ref[...].astype(BF), ((1,), (1,))).astype(BF)
+    out_ref[count:] = dot(v_ref[...], b16, ((1,), (1,))).astype(BF)
+    copies[4].wait()
 
 
 def weight_blocks(peers, w_hbm, w_ref):
@@ -81,18 +84,10 @@
     return sources, [w_ref.at[i] for i in range(len(sources))]
 
 
-def prep_kernel(h_hbm, gain_hbm, a_hbm, hg_ref, pack_ref, h_ref, gain_ref, a_ref, sems):
+def prep_kernel(h_ref, gain_ref, a16_ref, hg_ref, pack_ref):
     count, width = h_ref.shape
-    blocks = blocks_of(count)
-    copies = fetch(
-        [gain_hbm] + [h_hbm.at[b] for b in blocks] + [a_hbm],
-        [gain_ref] + [h_ref.at[b] for b in blocks] + [a_ref],
-        sems,
-    )
-    copies[0].wait()
     rows = []
-    for i, b in enumerate(blocks):
-        copies[1 + i].wait()
+    for b in blocks_of(count):
         wide = h_ref[b].astype(F32)
         hg_ref[b] = (wide * gain_ref[...]).astype(BF)
         sums = jnp.sum(wide * wide, axis=-1, keepdims=True)
@@ -100,8 +95,7 @@
     if len(rows) < 8:
         rows.append(jnp.zeros((8 - len(rows), LANES), F32))
     pack_ref[count:] = split_terms(jnp.concatenate(rows, axis=0))
-    copies[-1].wait()
-    pack_ref[:count] = dot(hg_ref[...], a_ref[...].astype(BF)).astype(BF)
+    pack_ref[:count] = dot(hg_ref[...], a16_ref[...]).astype(BF)
 
 
 def part_kernel(x_ref, got_ref, after_ref, out_ref):
@@ -123,7 +117,7 @@
         outs[i // per][:count, i % per * cut : (i % per + 1) * cut] = block
 
 
-def far_kernel(mine_ref, diag_ref, got_ref, after_ref, out_ref):
+def far_kernel(mine_ref, diag_ref, got_ref, after_ref, pass_ref, out_ref, pass_out):
     count, width = mine_ref.shape
     out_ref[:count, :width] = (mine_ref[...].astype(F32) + got_ref[:count, :width].astype(F32)).astype(BF)
     out_ref[count:, :width] = jnp.zeros((EXTRA, width), BF)
@@ -289,27 +283,27 @@
         dma = lambda n: pltpu.SemaphoreType.DMA((n,))
         vmem = lambda n, dtype=F32: pltpu.VMEM((n, rank), dtype)
 
-        part = call(
+        tall = shape((count, width), BF)
+        part, half_a, hidden = call(
             rank_kernel,
-            shape((2 * tokens, rank), BF),
-            [HBM] * 4,
-            tuple(map(keep_hbm, (train_inputs, train_cotangent, factor_a, factor_b))),
+            [shape((2 * tokens, rank), BF), shape(factor_a.shape, BF), tall],
+            [HBM] * 5,
+            tuple(
+                map(keep_hbm, (train_inputs, train_cotangent, factor_a, factor_b, incoming.reshape(count, width)))
+            ),
             "rank",
             [pltpu.VMEM(train_inputs.shape, BF), pltpu.VMEM(train_inputs.shape, BF),
-             pltpu.VMEM(factor_a.shape, F32), pltpu.VMEM(factor_b.shape, F32), dma(4)],
+             pltpu.VMEM(factor_a.shape, F32), pltpu.VMEM(factor_b.shape, F32), dma(5)],
         )
         part_got = swap(part, "tp", n_tp, 1)
         cut = 512
         wide = shape((count + EXTRA, width + rank), BF)
-        tall = shape((count, width), BF)
         gained, pack = call(
             prep_kernel,
             [tall, shape((count + EXTRA, rank), BF)],
-            [HBM] * 3,
-            tuple(map(keep_hbm, (incoming.reshape(count, width), norm_gain[None, :], factor_a))),
+            [VMEM] * 3,
+            (hidden, norm_gain[None, :], half_a),
             "prep",
-            [pltpu.VMEM((count, width), BF), pltpu.VMEM((1, width), F32), pltpu.VMEM(factor_a.shape, F32),
-             dma(2 + count // LANES)],
         )
         part_sum = call(part_kernel, shape(part.shape, BF), [VMEM] * 2 + [ANY], (part, part_got, pack), "part_sum")
         part_far = swap(part_sum, "tp", n_tp, 2)
@@ -325,7 +319,7 @@
                 [pltpu.VMEM((blocks, width, cut), BF), dma(blocks)],
             )
 
-        diag, distant = query((3, 2), [wide, tall], part_sum, "query_far")
+        diag, distant, beside = query((3, 2, 1), [wide, tall, tall], part_sum, "query_far")
         half = width // 2
         keep_a, send_a, keep_b, send_b, diag = call(
             functools.partial(grad_kernel, (path_a[0], path_b[0])),
@@ -338,32 +332,35 @@
             aliases={4: 4},
         )
         diag_got = swap(diag, "tp", n_tp, 1)
-        far = call(far_kernel, wide, [VMEM] * 3 + [ANY], (distant, diag, diag_got, send_a), "far")
+        far, beside = call(
+            far_kernel,
+            [wide, tall],
+            [VMEM] * 3 + [ANY] * 2,
+            (distant, diag, diag_got, send_a, beside),
+            "far",
+            out_specs=[VMEM, ANY],
+            aliases={4: 1},
+        )
         far_got = swap(far, "tp", n_tp, 2)
-
-        (close,) = query((0,), [tall], far, "query_close")
-        mine_a, mine_b, after, passed = keep_a, keep_b, [close], []
+        beside_got = swap(beside, "tp", n_tp, 1)
+
+        mine_a, mine_b, after = keep_a, keep_b, [far]
         for i, (way_a, way_b) in enumerate(zip(path_a[:-1], path_b[:-1])):
             got_a, got_b = cross(send_a, *way_a), cross(send_b, *way_b)
-            mine_a, mine_b, *made = call(
-                functools.partial(step_kernel, len(after) + len(passed)),
-                [shape((half, rank), BF)] * 2 + [shape(x.shape, x.dtype) for x in passed],
-                [VMEM] * 4 + [ANY] * (len(after) + len(passed)),
-                (mine_a, got_a, mine_b, got_b, *after, *passed),
+            mine_a, mine_b = call(
+                functools.partial(step_kernel, len(after)),
+                [shape((half, rank), BF)] * 2,
+                [VMEM] * 4 + [ANY] * len(after),
+                (mine_a, got_a, mine_b, got_b, *after),
                 f"step_{i}",
-                out_specs=[VMEM] * 2 + [ANY] * len(passed),
-                aliases={4 + len(after) + k: 2 + k for k in range(len(passed))},
             )
-            send_a, send_b = mine_a, mine_b
-            after, passed = [], []
-            if made:
-                beside_got = swap(made[0], "tp", n_tp, 1)
+            send_a, send_b, after = mine_a, mine_b, []
             if i == 0:
-                passed = query((1,), [tall], mine_a, "query_beside")
                 pos = positions.reshape(-1, LANES)
                 places = call(place_kernel, shape(pos.shape, F32), [VMEM, ANY], (pos, mine_a), "places")
-                cos, sin = turn_tables(places.reshape(rows), steps)
-                after = [cos, sin]
+                cos, sin = after = turn_tables(places.reshape(rows), steps)
+            if i == 1:
+                (close,) = after = query((0,), [tall], mine_a, "query_close")
         step_pack, grad_a, grad_b = call(
             functools.partial(low_kernel, path_a[-1], path_b[-1]),
             [shape((count + EXTRA, rank), BF), shape((width, rank), BF), shape((width, rank), BF)],

time: 56.9 us -> 53.8 us (0.946)
  Pallas kernels: 18.2 us -> 15.4 us
  starting transfers between devices: 17.6 us -> 15.7 us
  waiting for transfers between devices: 18.9 us -> 20.4 us
    pallas_call x16 -> x15, Pallas kernels: 18.2 us -> 15.4 us  [call(): pl.pallas_call(kernel, out_shape=outs, in_specs=in_specs, out_specs=out_s...]
    ppermute x15, starting transfers between devices: 17.6 us -> 15.7 us  [swap(): return lax.ppermute(x, axis, [(i, i ^ k) for i in range(n)])]
    ppermute x15, waiting for transfers between devices: 18.9 us -> 20.4 us  [swap(): return lax.ppermute(x, axis, [(i, i ^ k) for i in range(n)])]
  transfers between devices with their start and end apart: 15 -> 15, of which waited for: 9 -> 10; matrix products, arithmetic and copies ran while one was open for 2% -> 2% of each run, Pallas kernels for 23% -> 20%
where the time goes in v10:
time: 53.8 us; the launch traced here: 53.6 us
  waiting for transfers between devices  20.4 us (38%)
  starting transfers between devices  15.7 us (29%)
  Pallas kernels  15.4 us (29%)
  other arithmetic  1.21 us (2%)
  between operations  0.8 us (1%)
    ppermute x15, waiting for transfers between devices, swap(): return lax.ppermute(x, axis, [(i, i ^ k) for i in range(n)])  20.4 us
    ppermute x15, starting transfers between devices, swap(): return lax.ppermute(x, axis, [(i, i ^ k) for i in range(n)])  15.7 us
    pallas_call x15, Pallas kernels, call(): pl.pallas_call(kernel, out_shape=outs, in_specs=in_specs, out_specs=out_s...  15.4 us
  transfers between devices with their start and end apart: 15, of which 10 were waited for; matrix products, arithmetic and copies ran while one was open for 2% of the time, Pallas kernels for 20%

profile of v10, /device:TPU:0, one launch (start us, length us, event | category | flops | bytes accessed | tf_op | source)
XLA Modules:
  0.0 53.6 jit_solution(13729597488199529784)
XLA Ops:
  0.6 0.0 copy-start.4
  0.6 2.5 %rank.1 = (bf16[768,128]{1,0:T(8,128)(2,1)S(1)}, bf16[1024,128]{1,0:T(8,128)(2,1)S(1)}, bf16[512,1024]{1,0:T(8,128)(2,1)S(1)}) custom-call(bf16[384,1024]{1,0:T(8,128)(2,1)} %x_ref.1, bf16[384,1024]{1,0:T(8,128)(2,1)} %v_ref.1, f32[1024,128]{1,0:T(8,128)} %a_ref.1, f32[128,1024]{1,0:T(8,128)} %b_ref.1, bf16[512,1024]{1,0:T(8,128)(2,1)} %bitcast.9), custom_call_target="tpu_custom_call" | custom-call | tf_op jit(solution)/shard_map/rank/pallas_call | solution.py:238
  3.1 0.5 collective-permute-start
  3.7 0.6 %prep.1 = (bf16[512,1024]{1,0:T(8,128)(2,1)S(1)}, bf16[544,128]{1,0:T(8,128)(2,1)S(1)}) custom-call(bf16[512,1024]{1,0:T(8,128)(2,1)S(1)} %get-tuple-element.33.h_ref, f32[1,1024]{1,0:T(1,128)S(1)} %bitcast.7, bf16[1024,128]{1,0:T(8,128)(2,1)S(1)} %get-tuple-element.34.a16_ref), custom_call_target="tpu_custom_call" | custom-call | tf_op jit(solution)/shard_map/prep/pallas_call | solution.py:238
  4.2 0.5 collective-permute-done.got_ref
  4.8 3.0 %collective-permute-start.1 = (bf16[768,128]{1,0:T(8,128)(2,1)S(1)}, bf16[768,128]{1,0:T(8,128)(2,1)S(1)}, u32[]{:S(2)}, u32[]{:S(2)}) collective-permute-start(bf16[768,128]{1,0:T(8,128)(2,1)S(1)} %part_sum.1.after_ref.s_ref), channel_id=1, source_target_pairs={{0,2},{1,3},{2,0},{3,1},{4,6},{5,7},{6,4},{7,5},{8,10},{9,11},{10,... | collective-permute-start | bytes 589832 | tf_op jit(solution)/shard_map/ppermute | solution.py:35
  7.7 5.7 %query_far.1 = (bf16[544,1152]{1,0:T(8,128)(2,1)S(1)}, bf16[512,1024]{1,0:T(8,128)(2,1)S(1)}, bf16[512,1024]{1,0:T(8,128)(2,1)S(1)}) custom-call(bf16[512,1024]{1,0:T(8,128)(2,1)S(1)} %get-tuple-element.35.hg_ref, bf16[1024,4096]{1,0:T(8,128)(2,1)} %w_hbm.3, bf16[544,128]{1,0:T(8,128)(2,1)S(1)} %get-tuple-element.36.after_ref.pack_ref, ...), custom_call_target="tpu_custom_call" | custom-call | tf_op jit(solution)/shard_map/query_far/pallas_call | solution.py:238
  13.4 0.0 collective-permute-done.1.r_ref
  13.4 0.7 %grads.1 = (f32[512,128]{1,0:T(8,128)S(1)}, bf16[512,128]{1,0:T(8,128)(2,1)S(1)}, f32[512,128]{1,0:T(8,128)S(1)}, bf16[512,128]{1,0:T(8,128)(2,1)S(1)}, bf16[544,1152]{1,0:T(8,128)(2,1)S(1)}) custom-call(bf16[384,1024]{1,0:T(8,128)(2,1)S(1)} %copy-done, bf16[384,1024]{1,0:T(8,128)(2,1)S(1)} %copy-done.1, ...), custom_call_target="tpu_custom_call", output_to_operand_aliasing={{4}: (4, {})} | custom-call | tf_op jit(solution)/shard_map/grads/pallas_call | solution.py:238
  14.1 0.1 collective-permute-start.4
  14.2 1.6 %collective-permute-start.2 = (bf16[512,128]{1,0:T(8,128)(2,1)S(1)}, bf16[512,128]{1,0:T(8,128)(2,1)S(1)}, u32[]{:S(2)}, u32[]{:S(2)}) collective-permute-start(bf16[512,128]{1,0:T(8,128)(2,1)S(1)} %get-tuple-element.40.after_ref), channel_id=1, source_target_pairs={{0,4},{4,0},{8,12},{12,8},{1,5},{5,1},{9,13},{13,9},{2,6},{6,2},{1... | collective-permute-start | bytes 393224 | tf_op jit(solution)/shard_map/ppermute | solution.py:35
  15.8 1.5 %collective-permute-start.3 = (bf16[512,128]{1,0:T(8,128)(2,1)S(1)}, bf16[512,128]{1,0:T(8,128)(2,1)S(1)}, u32[]{:S(2)}, u32[]{:S(2)}) collective-permute-start(bf16[512,128]{1,0:T(8,128)(2,1)S(1)} %get-tuple-element.42), channel_id=1, source_target_pairs={{0,16},{16,0},{1,17},{17,1},{2,18},{18,2},{3,19},{19,3},{4,20},{20... | collective-permute-start | bytes 393224 | tf_op jit(solution)/shard_map/ppermute | solution.py:35
  17.3 0.0 collective-permute-done.4.got_ref
  17.3 0.3 far.1
  17.7 0.0 copy-start.5
  17.7 1.3 %collective-permute-start.8 = (bf16[544,1152]{1,0:T(8,128)(2,1)S(1)}, bf16[544,1152]{1,0:T(8,128)(2,1)S(1)}, u32[]{:S(2)}, u32[]{:S(2)}) collective-permute-start(bf16[544,1152]{1,0:T(8,128)(2,1)S(1)} %get-tuple-element.46.refs_0_.far_ref), channel_id=1, source_target_pairs={{0,2},{1,3},{2,0},{3,1},{4,6},{5,7},{6,4},{7,5},{8,10},{9,11},{10,... | collective-permute-start | bytes 3760136 | tf_op jit(solution)/shard_map/ppermute | solution.py:35
  19.0 1.1 %collective-permute-done.2.got_a = bf16[512,128]{1,0:T(8,128)(2,1)S(1)} collective-permute-done((bf16[512,128]{1,0:T(8,128)(2,1)S(1)}, bf16[512,128]{1,0:T(8,128)(2,1)S(1)}, u32[]{:S(2)}, u32[]{:S(2)}) %collective-permute-start.2) | collective-permute-done | bytes 131104 | tf_op jit(solution)/shard_map/ppermute | solution.py:35
  20.1 1.3 %collective-permute-done.3.got_b = bf16[512,128]{1,0:T(8,128)(2,1)S(1)} collective-permute-done((bf16[512,128]{1,0:T(8,128)(2,1)S(1)}, bf16[512,128]{1,0:T(8,128)(2,1)S(1)}, u32[]{:S(2)}, u32[]{:S(2)}) %collective-permute-start.3) | collective-permute-done | bytes 131104 | tf_op jit(solution)/shard_map/ppermute | solution.py:35
  21.4 0.1 step_0.1
  21.5 2.7 %collective-permute-start.5 = (bf16[512,128]{1,0:T(8,128)(2,1)S(1)}, bf16[512,128]{1,0:T(8,128)(2,1)S(1)}, u32[]{:S(2)}, u32[]{:S(2)}) collective-permute-start(bf16[512,128]{1,0:T(8,128)(2,1)S(1)} %get-tuple-element.47.after_ref.mine_a), channel_id=1, source_target_pairs={{0,8},{4,12},{8,0},{12,4},{1,9},{5,13},{9,1},{13,5},{2,10},{6,14},... | collective-permute-start | bytes 393224 | tf_op jit(solution)/shard_map/ppermute | solution.py:35
  24.1 0.4 collective-permute-start.6
  24.6 0.0 collective-permute-start.7
  24.6 1.0 %fusion = (f32[256,64]{1,0:T(8,128)S(1)}, f32[256,64]{1,0:T(8,128)S(1)}, f32[256,64]{1,0:T(8,128)S(1)}, f32[256,64]{1,0:T(8,128)S(1)}, f32[256,64]{1,0:T(8,128)S(1)}, /*index=5*/f32[256,64]{1,0:T(8,128)S(1)}) fusion(f32[64]{0:T(128)S(1)} %multiply_power_fusion, f32[256]{0:T(256)S(1)} %bitcast.6, f32[256]{0:T(256)S(1)} %broadcast_add_fusion), kind=kLoop, calls=%fused_computation.6 | loop fusion | flops 65536 | bytes 395520 | tf_op jit(solution)/shard_map/neg | solution.py:258
  25.6 0.2 maximum_maximum_fusion
  25.8 4.2 %collective-permute-done.5.got_a = bf16[512,128]{1,0:T(8,128)(2,1)S(1)} collective-permute-done((bf16[512,128]{1,0:T(8,128)(2,1)S(1)}, bf16[512,128]{1,0:T(8,128)(2,1)S(1)}, u32[]{:S(2)}, u32[]{:S(2)}) %collective-permute-start.5) | collective-permute-done | bytes 131104 | tf_op jit(solution)/shard_map/ppermute | solution.py:35
  30.1 1.2 %collective-permute-done.6.got_b = bf16[512,128]{1,0:T(8,128)(2,1)S(1)} collective-permute-done((bf16[512,128]{1,0:T(8,128)(2,1)S(1)}, bf16[512,128]{1,0:T(8,128)(2,1)S(1)}, u32[]{:S(2)}, u32[]{:S(2)}) %collective-permute-start.6) | collective-permute-done | bytes 131104 | tf_op jit(solution)/shard_map/ppermute | solution.py:35
  31.3 0.1 step_1.1
  31.3 0.1 collective-permute-start.10
  31.4 1.6 %collective-permute-start.9 = (bf16[512,128]{1,0:T(8,128)(2,1)S(1)}, bf16[512,128]{1,0:T(8,128)(2,1)S(1)}, u32[]{:S(2)}, u32[]{:S(2)}) collective-permute-start(bf16[512,128]{1,0:T(8,128)(2,1)S(1)} %get-tuple-element.49.after_ref.mine_a), channel_id=1, source_target_pairs={{0,16},{16,0},{1,17},{17,1},{2,18},{18,2},{3,19},{19,3},{4,20},{20... | collective-permute-start | bytes 393224 | tf_op jit(solution)/shard_map/ppermute | solution.py:35
  33.0 2.7 %query_close.1.refs_0_.mine_ref = bf16[512,1024]{1,0:T(8,128)(2,1)S(1)} custom-call(bf16[512,1024]{1,0:T(8,128)(2,1)S(1)} %get-tuple-element.35.hg_ref, bf16[1024,4096]{1,0:T(8,128)(2,1)} %w_hbm.3, bf16[544,128]{1,0:T(8,128)(2,1)S(1)} %get-tuple-element.36.after_ref.pack_ref, bf16[512,128]{1,0:T(8,128)(2,1)S(1)} %get-tuple-element.49.after_ref.mine_a), custom_call_target="tpu_custom_call" | custom-call | tf_op jit(solution)/shard_map/query_close/pallas_call | solution.py:238
  35.6 3.2 %collective-permute-done.10.got_b = bf16[512,128]{1,0:T(8,128)(2,1)S(1)} collective-permute-done((bf16[512,128]{1,0:T(8,128)(2,1)S(1)}, bf16[512,128]{1,0:T(8,128)(2,1)S(1)}, u32[]{:S(2)}, u32[]{:S(2)}) %collective-permute-start.10) | collective-permute-done | bytes 131104 | tf_op jit(solution)/shard_map/ppermute | solution.py:35
  38.9 0.0 collective-permute-done.9.got_a
  38.9 0.1 step_2.1
  38.9 0.1 collective-permute-start.11
  39.0 1.6 %collective-permute-start.12 = (bf16[512,128]{1,0:T(8,128)(2,1)S(1)}, bf16[512,128]{1,0:T(8,128)(2,1)S(1)}, u32[]{:S(2)}, u32[]{:S(2)}) collective-permute-start(bf16[512,128]{1,0:T(8,128)(2,1)S(1)} %get-tuple-element.53.mine_b), channel_id=1, source_target_pairs={{0,16},{16,0},{1,17},{17,1},{2,18},{18,2},{3,19},{19,3},{4,20},{20... | collective-permute-start | bytes 393224 | tf_op jit(solution)/shard_map/ppermute | solution.py:35
  40.6 3.4 %collective-permute-done.11.got_a = bf16[512,128]{1,0:T(8,128)(2,1)S(1)} collective-permute-done((bf16[512,128]{1,0:T(8,128)(2,1)S(1)}, bf16[512,128]{1,0:T(8,128)(2,1)S(1)}, u32[]{:S(2)}, u32[]{:S(2)}) %collective-permute-start.11) | collective-permute-done | bytes 131104 | tf_op jit(solution)/shard_map/ppermute | solution.py:35
  44.0 0.1 collective-permute-done.12.got_b
  44.0 0.5 %low_rank.1 = (bf16[544,128]{1,0:T(8,128)(2,1)S(1)}, bf16[1024,128]{1,0:T(8,128)(2,1)S(1)}, bf16[1024,128]{1,0:T(8,128)(2,1)S(1)}) custom-call(bf16[512,1024]{1,0:T(8,128)(2,1)S(1)} %get-tuple-element.35.hg_ref, bf16[512,128]{1,0:T(8,128)(2,1)S(1)} %get-tuple-element.52.mine_a, bf16[512,128]{1,0:T(8,128)(2,1)S(1)} %collective-permute-done.11.got_a, ...), custom_call_target="tpu_custom_call" | custom-call | tf_op jit(solution)/shard_map/low_rank/pallas_call | solution.py:238
  44.6 0.1 collective-permute-start.13
  44.7 1.3 %collective-permute-done.13.b_ref = bf16[544,128]{1,0:T(8,128)(2,1)S(1)} collective-permute-done((bf16[544,128]{1,0:T(8,128)(2,1)S(1)}, bf16[544,128]{1,0:T(8,128)(2,1)S(1)}, u32[]{:S(2)}, u32[]{:S(2)}) %collective-permute-start.13) | collective-permute-done | bytes 139296 | tf_op jit(solution)/shard_map/ppermute | solution.py:35
  46.1 0.0 copy-start.2
  46.1 0.0 copy-start.3
  46.1 1.3 %collective-permute-start.14 = (bf16[544,128]{1,0:T(8,128)(2,1)S(1)}, bf16[544,128]{1,0:T(8,128)(2,1)S(1)}, u32[]{:S(2)}, u32[]{:S(2)}) collective-permute-start(bf16[544,128]{1,0:T(8,128)(2,1)S(1)} %merge.1.after_ref.s_ref), channel_id=1, source_target_pairs={{0,2},{1,3},{2,0},{3,1},{4,6},{5,7},{6,4},{7,5},{8,10},{9,11},{10,... | collective-permute-start | bytes 417800 | tf_op jit(solution)/shard_map/ppermute | solution.py:35
  47.4 0.0 collective-permute-done.7.near_ref
  47.4 0.0 collective-permute-done.8.far_got
  47.4 0.5 base.1
  47.9 4.0 %collective-permute-done.14.r_ref = bf16[544,128]{1,0:T(8,128)(2,1)S(1)} collective-permute-done((bf16[544,128]{1,0:T(8,128)(2,1)S(1)}, bf16[544,128]{1,0:T(8,128)(2,1)S(1)}, u32[]{:S(2)}, u32[]{:S(2)}) %collective-permute-start.14) | collective-permute-done | bytes 139296 | tf_op jit(solution)/shard_map/ppermute | solution.py:35
  51.9 1.7 %final.1 = (f32[1024,128]{1,0:T(8,128)}, f32[128,1024]{1,0:T(8,128)}, bf16[512,1024]{1,0:T(8,128)(2,1)}) custom-call(f32[512,1024]{1,0:T(8,128)S(1)} %get-tuple-element.55.base_ref, f32[512,128]{1,0:T(8,128)S(1)} %get-tuple-element.56.low_ref, f32[512,128]{1,0:T(8,128)S(1)} %get-tuple-element.57.scale_ref, bf16[544,128]{1,0:T(8,128)(2,1)S(1)} %merge.1.after_ref.s_ref, ...), custom_call_target="tpu_custom_call" | custom-call | tf_op jit(solution)/shard_map/final/pallas_call | solution.py:238
  (13 shorter events, 0.1 us)
Async XLA Ops:
  0.6 3.0 %copy-start.4 = (f32[1024]{0:T(1024)S(1)}, f32[1024]{0:T(1024)}, u32[]{:S(2)}) copy-start(f32[1024]{0:T(1024)} %param.14) | copy-start | bytes 12292
  3.1 1.6 %collective-permute-start = (bf16[768,128]{1,0:T(8,128)(2,1)S(1)}, bf16[768,128]{1,0:T(8,128)(2,1)S(1)}, u32[]{:S(2)}, u32[]{:S(2)}) collective-permute-start(bf16[768,128]{1,0:T(8,128)(2,1)S(1)} %get-tuple-element.37.x_ref), channel_id=1, source_target_pairs={{0,1},{1,0},{2,3},{3,2},{4,5},{5,4},{6,7},{7,6},{8,9},{9,8},{10,11... | collective-permute-start | bytes 589832 | tf_op jit(solution)/shard_map/ppermute | solution.py:35
  4.8 8.6 %collective-permute-start.1 = (bf16[768,128]{1,0:T(8,128)(2,1)S(1)}, bf16[768,128]{1,0:T(8,128)(2,1)S(1)}, u32[]{:S(2)}, u32[]{:S(2)}) collective-permute-start(bf16[768,128]{1,0:T(8,128)(2,1)S(1)} %part_sum.1.after_ref.s_ref), channel_id=1, source_target_pairs={{0,2},{1,3},{2,0},{3,1},{4,6},{5,7},{6,4},{7,5},{8,10},{9,11},{10,... | collective-permute-start | bytes 589832 | tf_op jit(solution)/shard_map/ppermute | solution.py:35
  7.7 5.7 %copy-start = (bf16[384,1024]{1,0:T(8,128)(2,1)S(1)}, bf16[384,1024]{1,0:T(8,128)(2,1)}, u32[]{:S(2)}) copy-start(bf16[384,1024]{1,0:T(8,128)(2,1)} %x_ref.1) | copy-start | bytes 2359300
  7.7 5.7 %copy-start.1 = (bf16[384,1024]{1,0:T(8,128)(2,1)S(1)}, bf16[384,1024]{1,0:T(8,128)(2,1)}, u32[]{:S(2)}) copy-start(bf16[384,1024]{1,0:T(8,128)(2,1)} %v_ref.1) | copy-start | bytes 2359300
  14.1 3.2 %collective-permute-start.4 = (bf16[544,1152]{1,0:T(8,128)(2,1)S(1)}, bf16[544,1152]{1,0:T(8,128)(2,1)S(1)}, u32[]{:S(2)}, u32[]{:S(2)}) collective-permute-start(bf16[544,1152]{1,0:T(8,128)(2,1)S(1)} %get-tuple-element.44.diag_ref), channel_id=1, source_target_pairs={{0,1},{1,0},{2,3},{3,2},{4,5},{5,4},{6,7},{7,6},{8,9},{9,8},{10,11... | collective-permute-start | bytes 3760136 | tf_op jit(solution)/shard_map/ppermute | solution.py:35
  14.2 5.9 %collective-permute-start.2 = (bf16[512,128]{1,0:T(8,128)(2,1)S(1)}, bf16[512,128]{1,0:T(8,128)(2,1)S(1)}, u32[]{:S(2)}, u32[]{:S(2)}) collective-permute-start(bf16[512,128]{1,0:T(8,128)(2,1)S(1)} %get-tuple-element.40.after_ref), channel_id=1, source_target_pairs={{0,4},{4,0},{8,12},{12,8},{1,5},{5,1},{9,13},{13,9},{2,6},{6,2},{1... | collective-permute-start | bytes 393224 | tf_op jit(solution)/shard_map/ppermute | solution.py:35
  15.8 5.6 %collective-permute-start.3 = (bf16[512,128]{1,0:T(8,128)(2,1)S(1)}, bf16[512,128]{1,0:T(8,128)(2,1)S(1)}, u32[]{:S(2)}, u32[]{:S(2)}) collective-permute-start(bf16[512,128]{1,0:T(8,128)(2,1)S(1)} %get-tuple-element.42), channel_id=1, source_target_pairs={{0,16},{16,0},{1,17},{17,1},{2,18},{18,2},{3,19},{19,3},{4,20},{20... | collective-permute-start | bytes 393224 | tf_op jit(solution)/shard_map/ppermute | solution.py:35
  17.7 6.5 %copy-start.5 = (s32[256]{0:T(256)S(1)}, s32[256]{0:T(256)}, u32[]{:S(2)}) copy-start(s32[256]{0:T(256)} %param.15) | copy-start | bytes 3076
  17.7 29.7 %collective-permute-start.8 = (bf16[544,1152]{1,0:T(8,128)(2,1)S(1)}, bf16[544,1152]{1,0:T(8,128)(2,1)S(1)}, u32[]{:S(2)}, u32[]{:S(2)}) collective-permute-start(bf16[544,1152]{1,0:T(8,128)(2,1)S(1)} %get-tuple-element.46.refs_0_.far_ref), channel_id=1, source_target_pairs={{0,2},{1,3},{2,0},{3,1},{4,6},{5,7},{6,4},{7,5},{8,10},{9,11},{10,... | collective-permute-start | bytes 3760136 | tf_op jit(solution)/shard_map/ppermute | solution.py:35
  21.5 8.6 %collective-permute-start.5 = (bf16[512,128]{1,0:T(8,128)(2,1)S(1)}, bf16[512,128]{1,0:T(8,128)(2,1)S(1)}, u32[]{:S(2)}, u32[]{:S(2)}) collective-permute-start(bf16[512,128]{1,0:T(8,128)(2,1)S(1)} %get-tuple-element.47.after_ref.mine_a), channel_id=1, source_target_pairs={{0,8},{4,12},{8,0},{12,4},{1,9},{5,13},{9,1},{13,5},{2,10},{6,14},... | collective-permute-start | bytes 393224 | tf_op jit(solution)/shard_map/ppermute | solution.py:35
  24.1 7.1 %collective-permute-start.6 = (bf16[512,128]{1,0:T(8,128)(2,1)S(1)}, bf16[512,128]{1,0:T(8,128)(2,1)S(1)}, u32[]{:S(2)}, u32[]{:S(2)}) collective-permute-start(bf16[512,128]{1,0:T(8,128)(2,1)S(1)} %get-tuple-element.48.mine_b), channel_id=1, source_target_pairs={{0,4},{4,0},{8,12},{12,8},{1,5},{5,1},{9,13},{13,9},{2,6},{6,2},{1... | collective-permute-start | bytes 393224 | tf_op jit(solution)/shard_map/ppermute | solution.py:35
  24.6 22.8 %collective-permute-start.7 = (bf16[512,1024]{1,0:T(8,128)(2,1)S(1)}, bf16[512,1024]{1,0:T(8,128)(2,1)S(1)}, u32[]{:S(2)}, u32[]{:S(2)}) collective-permute-start(bf16[512,1024]{1,0:T(8,128)(2,1)S(1)} %get-tuple-element.50), channel_id=1, source_target_pairs={{0,1},{1,0},{2,3},{3,2},{4,5},{5,4},{6,7},{7,6},{8,9},{9,8},{10,11... | collective-permute-start | bytes 3145736 | tf_op jit(solution)/shard_map/ppermute | solution.py:35
  31.3 7.5 %collective-permute-start.10 = (bf16[512,128]{1,0:T(8,128)(2,1)S(1)}, bf16[512,128]{1,0:T(8,128)(2,1)S(1)}, u32[]{:S(2)}, u32[]{:S(2)}) collective-permute-start(bf16[512,128]{1,0:T(8,128)(2,1)S(1)} %get-tuple-element.51.mine_b), channel_id=1, source_target_pairs={{0,8},{4,12},{8,0},{12,4},{1,9},{5,13},{9,1},{13,5},{2,10},{6,14},... | collective-permute-start | bytes 393224 | tf_op jit(solution)/shard_map/ppermute | solution.py:35
  31.4 7.5 %collective-permute-start.9 = (bf16[512,128]{1,0:T(8,128)(2,1)S(1)}, bf16[512,128]{1,0:T(8,128)(2,1)S(1)}, u32[]{:S(2)}, u32[]{:S(2)}) collective-permute-start(bf16[512,128]{1,0:T(8,128)(2,1)S(1)} %get-tuple-element.49.after_ref.mine_a), channel_id=1, source_target_pairs={{0,16},{16,0},{1,17},{17,1},{2,18},{18,2},{3,19},{19,3},{4,20},{20... | collective-permute-start | bytes 393224 | tf_op jit(solution)/shard_map/ppermute | solution.py:35
  38.9 5.0 %collective-permute-start.11 = (bf16[512,128]{1,0:T(8,128)(2,1)S(1)}, bf16[512,128]{1,0:T(8,128)(2,1)S(1)}, u32[]{:S(2)}, u32[]{:S(2)}) collective-permute-start(bf16[512,128]{1,0:T(8,128)(2,1)S(1)} %get-tuple-element.52.mine_a), channel_id=1, source_target_pairs={{0,4},{4,0},{8,12},{12,8},{1,5},{5,1},{9,13},{13,9},{2,6},{6,2},{1... | collective-permute-start | bytes 393224 | tf_op jit(solution)/shard_map/ppermute | solution.py:35
  39.0 5.0 %collective-permute-start.12 = (bf16[512,128]{1,0:T(8,128)(2,1)S(1)}, bf16[512,128]{1,0:T(8,128)(2,1)S(1)}, u32[]{:S(2)}, u32[]{:S(2)}) collective-permute-start(bf16[512,128]{1,0:T(8,128)(2,1)S(1)} %get-tuple-element.53.mine_b), channel_id=1, source_target_pairs={{0,16},{16,0},{1,17},{17,1},{2,18},{18,2},{3,19},{19,3},{4,20},{20... | collective-permute-start | bytes 393224 | tf_op jit(solution)/shard_map/ppermute | solution.py:35
  44.6 1.4 %collective-permute-start.13 = (bf16[544,128]{1,0:T(8,128)(2,1)S(1)}, bf16[544,128]{1,0:T(8,128)(2,1)S(1)}, u32[]{:S(2)}, u32[]{:S(2)}) collective-permute-start(bf16[544,128]{1,0:T(8,128)(2,1)S(1)} %get-tuple-element.54.a_ref), channel_id=1, source_target_pairs={{0,1},{1,0},{2,3},{3,2},{4,5},{5,4},{6,7},{7,6},{8,9},{9,8},{10,11... | collective-permute-start | bytes 417800 | tf_op jit(solution)/shard_map/ppermute | solution.py:35
  46.1 5.8 %copy-start.2 = (f32[1024,128]{1,0:T(8,128)S(1)}, f32[1024,128]{1,0:T(8,128)}, u32[]{:S(2)}) copy-start(f32[1024,128]{1,0:T(8,128)} %a_ref.1) | copy-start | bytes 1572868
  46.1 5.8 %copy-start.3 = (f32[128,1024]{1,0:T(8,128)S(1)}, f32[128,1024]{1,0:T(8,128)}, u32[]{:S(2)}) copy-start(f32[128,1024]{1,0:T(8,128)} %b_ref.1) | copy-start | bytes 1572868
  46.1 5.8 %collective-permute-start.14 = (bf16[544,128]{1,0:T(8,128)(2,1)S(1)}, bf16[544,128]{1,0:T(8,128)(2,1)S(1)}, u32[]{:S(2)}, u32[]{:S(2)}) collective-permute-start(bf16[544,128]{1,0:T(8,128)(2,1)S(1)} %merge.1.after_ref.s_ref), channel_id=1, source_target_pairs={{0,2},{1,3},{2,0},{3,1},{4,6},{5,7},{6,4},{7,5},{8,10},{9,11},{10,... | collective-permute-start | bytes 417800 | tf_op jit(solution)/shard_map/ppermute | solution.py:35

commit v11 on v10

--- a/solution.py
+++ b/solution.py
@@ -84,7 +84,7 @@
     return sources, [w_ref.at[i] for i in range(len(sources))]
 
 
-def prep_kernel(h_ref, gain_ref, a16_ref, hg_ref, pack_ref):
+def prep_kernel(h_ref, gain_ref, a16_ref, hg_ref, low_ref, sums_ref):
     count, width = h_ref.shape
     rows = []
     for b in blocks_of(count):
@@ -94,35 +94,30 @@
         rows.append(jnp.broadcast_to(sums, (LANES, LANES)).T[0:1])
     if len(rows) < 8:
         rows.append(jnp.zeros((8 - len(rows), LANES), F32))
-    pack_ref[count:] = split_terms(jnp.concatenate(rows, axis=0))
-    pack_ref[:count] = dot(hg_ref[...], a16_ref[...]).astype(BF)
+    sums_ref[...] = jnp.concatenate(rows, axis=0)
+    low_ref[...] = dot(hg_ref[...], a16_ref[...]).astype(BF)
 
 
 def part_kernel(x_ref, got_ref, after_ref, out_ref):
     sum_kernel(x_ref, got_ref, out_ref)
 
 
-def query_kernel(peers, hg_ref, w_hbm, pack_ref, after_ref, *rest):
+def query_kernel(peers, hg_ref, w_hbm, low_ref, after_ref, *rest):
     outs, (w_ref, sems) = rest[:-2], rest[-2:]
     _, width, cut = w_ref.shape
     copies = fetch(*weight_blocks(peers, w_hbm, w_ref), sems)
-    count = hg_ref.shape[0]
-    if outs[0].shape[0] > count:
-        outs[0][count:, :width] = jnp.zeros((EXTRA, width), BF)
-        outs[0][:, width:] = pack_ref[...]
+    if outs[0].shape[1] > width:
+        outs[0][:, width:] = low_ref[...]
     per = width // cut
     for i, copy in enumerate(copies):
         copy.wait()
-        block = dot(hg_ref[...], w_ref[i]).astype(BF)
-        outs[i // per][:count, i % per * cut : (i % per + 1) * cut] = block
-
-
-def far_kernel(mine_ref, diag_ref, got_ref, after_ref, pass_ref, out_ref, pass_out):
-    count, width = mine_ref.shape
-    out_ref[:count, :width] = (mine_ref[...].astype(F32) + got_ref[:count, :width].astype(F32)).astype(BF)
-    out_ref[count:, :width] = jnp.zeros((EXTRA, width), BF)
-    out_ref[:count, width:] = (diag_ref[:count, width:].astype(F32) + got_ref[:count, width:].astype(F32)).astype(BF)
-    out_ref[count:, width:] = split_terms(join_terms(diag_ref[count:, width:]) + join_terms(got_ref[count:, width:]))
+        outs[i // per][:, i % per * cut : (i % per + 1) * cut] = dot(hg_ref[...], w_ref[i]).astype(BF)
+
+
+def far_kernel(mine_ref, diag_ref, got_ref, after_ref, out_ref):
+    width = mine_ref.shape[1]
+    sum_kernel(mine_ref, got_ref.at[:, :width], out_ref.at[:, :width])
+    sum_kernel(diag_ref.at[:, width:], got_ref.at[:, width:], out_ref.at[:, width:])
 
 
 def merge_kernel(a_ref, b_ref, out_ref):
@@ -148,7 +143,7 @@
     out_ref[other] = got_ref[...]
 
 
-def grad_kernel(axes, x_ref, v_ref, s_ref, r_ref, pass_ref, keep_a, send_a, keep_b, send_b, pass_out, ga, gb):
+def grad_kernel(axes, x_ref, v_ref, s_ref, r_ref, after_ref, keep_a, send_a, keep_b, send_b, ga, gb):
     count, width = x_ref.shape
     low = (s_ref[...].astype(F32) + r_ref[...].astype(F32)).astype(BF)
     ga[...] = SCALE * dot(x_ref[...], low[count:], ((0,), (0,)))
@@ -163,10 +158,8 @@
     out_ref[...] = (keep_ref[...].astype(F32) + got_ref[...].astype(F32)).astype(BF)
 
 
-def step_kernel(waits, mine_a, got_a, mine_b, got_b, *refs):
-    sum_a, sum_b = refs[waits : waits + 2]
-    sum_kernel(mine_a, got_a, sum_a)
-    sum_kernel(mine_b, got_b, sum_b)
+def step_kernel(mine_ref, got_ref, *rest):
+    sum_kernel(mine_ref, got_ref, rest[len(rest) // 2])
 
 
 def place_kernel(pos_ref, after_ref, out_ref):
@@ -178,34 +171,30 @@
     return jnp.broadcast_to(jnp.sum(x * x), (8, LANES))
 
 
-def low_kernel(way_a, way_b, hg_ref, mine_a, got_a, mine_b, got_b, pack_ref, ga_ref, gb_ref):
+def low_kernel(way_a, way_b, hg_ref, sums_ref, mine_a, got_a, mine_b, got_b, pack_ref, ga_ref, gb_ref):
     join(*way_a, mine_a, got_a, ga_ref)
     count = hg_ref.shape[0]
     pack_ref[:count] = dot(hg_ref[...], ga_ref[...]).astype(BF)
     join(*way_b, mine_b, got_b, gb_ref)
-    pack_ref[count:] = split_terms(square_sum(ga_ref) + square_sum(gb_ref))
-
-
-def base_kernel(mine_ref, near_ref, far_ref, far_got, after_ref, base_ref, low_ref, scale_ref):
-    count, width = mine_ref.shape
-    sums = join_terms(far_ref[count:, width:]) + join_terms(far_got[count:, width:])
-    scale = lax.rsqrt(sums / D + EPS)
-    for i, b in enumerate(blocks_of(count)):
-        block = jnp.broadcast_to(scale[i : i + 1], (LANES, LANES)).T
-        scale_ref[b] = block
-        low_ref[b] = (far_ref[b, width:].astype(F32) + far_got[b, width:].astype(F32)) * block
-        for c in blocks_of(width):
-            total = mine_ref[b, c].astype(F32) + near_ref[b, c].astype(F32) + far_got[b, c].astype(F32)
-            base_ref[b, c] = total * block
+    row = lax.broadcasted_iota(jnp.int32, (8, LANES), 0)
+    pack_ref[count:] = split_terms(jnp.where(row == 7, square_sum(ga_ref) + square_sum(gb_ref), sums_ref[...]))
+
+
+def base_kernel(mine_ref, near_ref, far_ref, far_got, after_ref, base_ref, low_ref):
+    width = mine_ref.shape[1]
+    low_ref[...] = far_ref[:, width:].astype(F32) + far_got[:, width:].astype(F32)
+    for c in blocks_of(width):
+        base_ref[:, c] = mine_ref[:, c].astype(F32) + near_ref[:, c].astype(F32) + far_got[:, c].astype(F32)
 
 
 def final_kernel(
-    base_ref, low_ref, scale_ref, s_ref, r_ref, ga_ref, gb_ref, a_ref, b_ref, cos_ref, sin_ref,
+    base_ref, low_ref, s_ref, r_ref, ga_ref, gb_ref, a_ref, b_ref, cos_ref, sin_ref,
     a_hbm, b_hbm, q_hbm, new_a, new_b, half_b, out, sems,
 ):
     count, width = base_ref.shape
     total = join_terms(s_ref[count:]) + join_terms(r_ref[count:])
-    rate = (LEARN * lax.rsqrt(total + NORM_EPS))[0:1]
+    rate = (LEARN * lax.rsqrt(total + NORM_EPS))[7:8]
+    scales = lax.rsqrt(total / D + EPS)
     for c in blocks_of(width):
         fresh = b_ref[:, c] - rate * gb_ref[c].astype(F32)
         new_b[:, c] = fresh
@@ -217,11 +206,12 @@
     copies[-1].start()
     for i, b in enumerate(blocks_of(count)):
         low = s_ref[b].astype(F32) + r_ref[b].astype(F32)
-        mix = (low_ref[b] - rate * (low * scale_ref[b])) * SCALE
+        scale = jnp.broadcast_to(scales[i : i + 1], (LANES, LANES)).T
+        mix = (low_ref[b] - rate * low) * scale * SCALE
         update = dot(mix.astype(BF), half_b[...])
         cos, sin = cos_ref[b], sin_ref[b]
         for c in blocks_of(width):
-            query = base_ref[b, c] + update[:, c]
+            query = base_ref[b, c] * scale + update[:, c]
             other = pltpu.roll(query, HEAD // 2, 1)
             out[b, c] = (query * cos + other * sin).astype(BF)
         copies.append(pltpu.make_async_copy(out.at[b], q_hbm.at[b], sems.at[2 + i]))
@@ -232,6 +222,13 @@
 
 def keep_hbm(x):
     return pltpu.with_memory_space_constraint(x, pltpu.HBM)
+
+
+WEIGHTS = {
+    "rank": 2.4, "prep": 0.6, "query_diag": 40.0, "query_distant": 0.01, "query_beside": 1.0, "query_close": 0.5, "grads": 40.0,
+    "final": 1.8,
+}
+FLOPS_PER_WEIGHT = 1_150_000_000
 
 
 def call(kernel, outs, in_specs, args, name, scratch=(), out_specs=None, limit=16, aliases=None):
@@ -243,6 +240,9 @@
         scratch_shapes=list(scratch),
         compiler_params=pltpu.CompilerParams(vmem_limit_bytes=int(limit * 1024 * 1024)),
         input_output_aliases=aliases or {},
+        cost_estimate=pl.CostEstimate(
+            flops=int(WEIGHTS.get(name, 0.01) * FLOPS_PER_WEIGHT), bytes_accessed=0, transcendentals=0
+        ),
         name=name,
     )(*args)
 
@@ -297,15 +297,15 @@
         )
         part_got = swap(part, "tp", n_tp, 1)
         cut = 512
-        wide = shape((count + EXTRA, width + rank), BF)
-        gained, pack = call(
+        wide = shape((count, width + rank), BF)
+        gained, low, sums = call(
             prep_kernel,
-            [tall, shape((count + EXTRA, rank), BF)],
+            [tall, shape((count, rank), BF), shape((8, LANES), F32)],
             [VMEM] * 3,
             (hidden, norm_gain[None, :], half_a),
             "prep",
         )
-        part_sum = call(part_kernel, shape(part.shape, BF), [VMEM] * 2 + [ANY], (part, part_got, pack), "part_sum")
+        part_sum = call(part_kernel, shape(part.shape, BF), [VMEM] * 2 + [ANY], (part, part_got, low), "part_sum")
         part_far = swap(part_sum, "tp", n_tp, 2)
 
         def query(peers, outs, after, name):
@@ -314,67 +314,73 @@
                 functools.partial(query_kernel, peers),
                 outs,
                 [VMEM, HBM, VMEM, ANY],
-                (gained, keep_hbm(base_weight), pack, after),
-                name,
+                (gained, keep_hbm(base_weight), low, after),
+                "query_" + name,
                 [pltpu.VMEM((blocks, width, cut), BF), dma(blocks)],
             )
 
-        diag, distant, beside = query((3, 2, 1), [wide, tall, tall], part_sum, "query_far")
+        (diag,) = query((3,), [wide], part_sum, "diag")
+        diag_got = swap(diag, "tp", n_tp, 1)
+        (distant,) = query((2,), [tall], diag, "distant")
+
         half = width // 2
-        keep_a, send_a, keep_b, send_b, diag = call(
+        keep_a, send_a, keep_b, send_b = call(
             functools.partial(grad_kernel, (path_a[0], path_b[0])),
-            [shape((half, rank), F32), shape((half, rank), BF)] * 2 + [wide],
+            [shape((half, rank), F32), shape((half, rank), BF)] * 2,
             [VMEM] * 4 + [ANY],
-            (train_inputs, train_cotangent, part_sum, part_far, diag),
+            (train_inputs, train_cotangent, part_sum, part_far, distant),
             "grads",
             [vmem(width), vmem(width)],
-            out_specs=[VMEM] * 4 + [ANY],
-            aliases={4: 4},
-        )
-        diag_got = swap(diag, "tp", n_tp, 1)
-        far, beside = call(
-            far_kernel,
-            [wide, tall],
-            [VMEM] * 3 + [ANY] * 2,
-            (distant, diag, diag_got, send_a, beside),
-            "far",
-            out_specs=[VMEM, ANY],
-            aliases={4: 1},
-        )
+        )
+        far = call(far_kernel, wide, [VMEM] * 3 + [ANY], (distant, diag, diag_got, send_a), "far")
         far_got = swap(far, "tp", n_tp, 2)
-        beside_got = swap(beside, "tp", n_tp, 1)
-
-        mine_a, mine_b, after = keep_a, keep_b, [far]
-        for i, (way_a, way_b) in enumerate(zip(path_a[:-1], path_b[:-1])):
-            got_a, got_b = cross(send_a, *way_a), cross(send_b, *way_b)
-            mine_a, mine_b = call(
-                functools.partial(step_kernel, len(after)),
-                [shape((half, rank), BF)] * 2,
-                [VMEM] * 4 + [ANY] * len(after),
-                (mine_a, got_a, mine_b, got_b, *after),
-                f"step_{i}",
+
+        def step(mine, send, way, after, passed, name):
+            return call(
+                step_kernel,
+                [shape((half, rank), BF)] + [shape(x.shape, x.dtype) for x in passed],
+                [VMEM] * 2 + [ANY] * (1 + len(passed)),
+                (mine, cross(send, *way), after, *passed),
+                name,
+                out_specs=[VMEM] + [ANY] * len(passed),
+                aliases={3 + k: 1 + k for k in range(len(passed))},
             )
-            send_a, send_b, after = mine_a, mine_b, []
-            if i == 0:
+
+        mine_a, mine_b, after, passed = keep_a, keep_b, far, []
+        order = ["a", "b", "n", "b", "a", "c", "t", "a", "b"] if n_dp * n_roll == 8 else ["a", "b", "n", "b", "t", "a", "c"] + ["a", "b"] * (len(path_a) - 3)
+        steps_a, steps_b = iter(path_a[:-1]), iter(path_b[:-1])
+        for i, which in enumerate(order):
+            if which == "a":
+                mine_a = send_a = after = step(mine_a, send_a, next(steps_a), after, [], f"step_a{i}")[0]
+            elif which == "b":
+                mine_b, *made = step(mine_b, send_b, next(steps_b), after, passed, f"step_b{i}")
+                send_b = after = mine_b
+                if made:
+                    beside_got, passed = swap(made[0], "tp", n_tp, 1), []
+            elif which == "t":
                 pos = positions.reshape(-1, LANES)
-                places = call(place_kernel, shape(pos.shape, F32), [VMEM, ANY], (pos, mine_a), "places")
-                cos, sin = after = turn_tables(places.reshape(rows), steps)
-            if i == 1:
-                (close,) = after = query((0,), [tall], mine_a, "query_close")
+                places = call(place_kernel, shape(pos.shape, F32), [VMEM, ANY], (pos, after), "places")
+                cos, sin = turn_tables(places.reshape(rows), steps)
+                after = sin
+            elif which == "n":
+                passed = query((1,), [tall], after, "beside")
+            else:
+                (close,) = query((0,), [tall], after, "close")
+                after = close
         step_pack, grad_a, grad_b = call(
             functools.partial(low_kernel, path_a[-1], path_b[-1]),
             [shape((count + EXTRA, rank), BF), shape((width, rank), BF), shape((width, rank), BF)],
-            [VMEM] * 5,
-            (gained, mine_a, cross(mine_a, *path_a[-1]), mine_b, cross(mine_b, *path_b[-1])),
+            [VMEM] * 6,
+            (gained, sums, mine_a, cross(mine_a, *path_a[-1]), mine_b, cross(mine_b, *path_b[-1])),
             "low_rank",
         )
         step_got = swap(step_pack, "tp", n_tp, 1)
         step_sum = call(merge_kernel, shape((count + EXTRA, rank), BF), [VMEM] * 2, (step_pack, step_got), "merge")
         step_far = swap(step_sum, "tp", n_tp, 2)
 
-        base, low, scale = call(
+        base, low_all = call(
             base_kernel,
-            [shape((count, width), F32), shape((count, rank), F32), shape((count, LANES), F32)],
+            [shape((count, width), F32), shape((count, rank), F32)],
             [VMEM] * 4 + [ANY],
             (close, beside_got, far, far_got, step_sum),
             "base",
@@ -382,8 +388,8 @@
         new_a, new_b, queries = call(
             final_kernel,
             [shape((width, rank), F32), shape((rank, width), F32), tall],
-            [VMEM] * 11,
-            (base, low, scale, step_sum, step_far, grad_a, grad_b, factor_a, factor_b, cos, sin),
+            [VMEM] * 10,
+            (base, low_all, step_sum, step_far, grad_a, grad_b, factor_a, factor_b, cos, sin),
             "final",
             [pltpu.VMEM((width, rank), F32), pltpu.VMEM((rank, width), F32),
              pltpu.VMEM((rank, width), BF), pltpu.VMEM((count, width), BF), dma(2 + count // LANES)],

time: 53.8 us -> 52.9 us (0.983)
  waiting for transfers between devices: 20.4 us -> 15.5 us
  Pallas kernels: 15.4 us -> 18 us
  starting transfers between devices: 15.7 us -> 17 us
    ppermute x15, waiting for transfers between devices: 20.4 us -> 15.5 us  [swap(): return lax.ppermute(x, axis, [(i, i ^ k) for i in range(n)])]
    pallas_call x15 -> x20, Pallas kernels: 15.4 us -> 18 us  [call(): pl.pallas_call(kernel, out_shape=outs, in_specs=in_specs, out_specs=out_s...]
    ppermute x15, starting transfers between devices: 15.7 us -> 17 us  [swap(): return lax.ppermute(x, axis, [(i, i ^ k) for i in range(n)])]
    cos x0 -> x1, other arithmetic: none -> 0.99 us  [turn_tables(): c, s = (jnp.cos(angle), jnp.sin(angle))]
    neg x1 -> x0, other arithmetic: 0.99 us -> none  [turn_tables(): sin.append(jnp.concatenate([-s, s], axis=-1))]
  transfers between devices with their start and end apart: 15 -> 15, of which waited for: 10 -> 8; matrix products, arithmetic and copies ran while one was open for 2% -> 2% of each run, Pallas kernels for 20% -> 26%
where the time goes in v11:
time: 52.9 us; the launch traced here: 52.7 us
  Pallas kernels  18 us (34%)
  starting transfers between devices  17 us (32%)
  waiting for transfers between devices  15.5 us (29%)
  other arithmetic  1.28 us (2%)
  between operations  0.89 us (2%)
    pallas_call x20, Pallas kernels, call(): pl.pallas_call(kernel, out_shape=outs, in_specs=in_specs, out_specs=out_s...  18 us
    ppermute x15, starting transfers between devices, swap(): return lax.ppermute(x, axis, [(i, i ^ k) for i in range(n)])  17 us
    ppermute x15, waiting for transfers between devices, swap(): return lax.ppermute(x, axis, [(i, i ^ k) for i in range(n)])  15.5 us
  transfers between devices with their start and end apart: 15, of which 8 were waited for; matrix products, arithmetic and copies ran while one was open for 2% of the time, Pallas kernels for 26%

profile of v11, /device:TPU:0, one launch (start us, length us, event | category | flops | bytes accessed | tf_op | source)
XLA Modules:
  0.0 52.7 jit_solution(12279103982218420381)
XLA Ops:
  0.6 2.5 %rank.1 = (bf16[768,128]{1,0:T(8,128)(2,1)S(1)}, bf16[1024,128]{1,0:T(8,128)(2,1)S(1)}, bf16[512,1024]{1,0:T(8,128)(2,1)S(1)}) custom-call(bf16[384,1024]{1,0:T(8,128)(2,1)} %x_ref.1, bf16[384,1024]{1,0:T(8,128)(2,1)} %v_ref.1, f32[1024,128]{1,0:T(8,128)} %a_ref.1, f32[128,1024]{1,0:T(8,128)} %b_ref.1, bf16[512,1024]{1,0:T(8,128)(2,1)} %bitcast.9), custom_call_target="tpu_custom_call" | custom-call | flops 2760000000 | tf_op jit(solution)/shard_map/rank/pallas_call | solution.py:235
  3.1 0.5 collective-permute-start
  3.7 0.6 %prep.1 = (bf16[512,1024]{1,0:T(8,128)(2,1)S(1)}, bf16[512,128]{1,0:T(8,128)(2,1)S(1)}, f32[8,128]{1,0:T(8,128)S(1)}) custom-call(bf16[512,1024]{1,0:T(8,128)(2,1)S(1)} %get-tuple-element.23.h_ref, f32[1,1024]{1,0:T(1,128)S(1)} %bitcast.8, bf16[1024,128]{1,0:T(8,128)(2,1)S(1)} %get-tuple-element.24.a16_ref), custom_call_target="tpu_custom_call" | custom-call | flops 690000000 | tf_op jit(solution)/shard_map/prep/pallas_call | solution.py:235
  4.2 0.5 collective-permute-done.got_ref
  4.8 3.0 %collective-permute-start.1 = (bf16[768,128]{1,0:T(8,128)(2,1)S(1)}, bf16[768,128]{1,0:T(8,128)(2,1)S(1)}, u32[]{:S(2)}, u32[]{:S(2)}) collective-permute-start(bf16[768,128]{1,0:T(8,128)(2,1)S(1)} %part_sum.1.after_ref.s_ref), channel_id=1, source_target_pairs={{0,2},{1,3},{2,0},{3,1},{4,6},{5,7},{6,4},{7,5},{8,10},{9,11},{10,... | collective-permute-start | bytes 589832 | tf_op jit(solution)/shard_map/ppermute | solution.py:35
  7.7 2.7 %query_diag.1.after_ref.diag_ref = bf16[512,1152]{1,0:T(8,128)(2,1)S(1)} custom-call(bf16[512,1024]{1,0:T(8,128)(2,1)S(1)} %get-tuple-element.25.hg_ref, bf16[1024,4096]{1,0:T(8,128)(2,1)} %w_hbm.7, bf16[512,128]{1,0:T(8,128)(2,1)S(1)} %get-tuple-element.26.after_ref.low_ref, bf16[768,128]{1,0:T(8,128)(2,1)S(1)} %part_sum.1.after_ref.s_ref), custom_call_target="tpu_custom_call" | custom-call | flops 46000001024 | tf_op jit(solution)/shard_map/query_diag/pallas_call | solution.py:235
  10.4 0.0 copy-start.1
  10.4 0.0 copy-start.2
  10.4 0.1 collective-permute-start.3
  10.5 2.8 %query_distant.1.after_ref.mine_ref = bf16[512,1024]{1,0:T(8,128)(2,1)S(1)} custom-call(bf16[512,1024]{1,0:T(8,128)(2,1)S(1)} %get-tuple-element.25.hg_ref, bf16[1024,4096]{1,0:T(8,128)(2,1)} %w_hbm.7, bf16[512,128]{1,0:T(8,128)(2,1)S(1)} %get-tuple-element.26.after_ref.low_ref, bf16[512,1152]{1,0:T(8,128)(2,1)S(1)} %query_diag.1.after_ref.diag_ref), custom_call_target="tpu_custom_call" | custom-call | flops 11500000 | tf_op jit(solution)/shard_map/query_distant/pallas_call | solution.py:235
  13.3 0.0 collective-permute-done.1.r_ref
  13.3 0.7 %grads.1 = (f32[512,128]{1,0:T(8,128)S(1)}, bf16[512,128]{1,0:T(8,128)(2,1)S(1)}, f32[512,128]{1,0:T(8,128)S(1)}, bf16[512,128]{1,0:T(8,128)(2,1)S(1)}) custom-call(bf16[384,1024]{1,0:T(8,128)(2,1)S(1)} %copy-done.1, bf16[384,1024]{1,0:T(8,128)(2,1)S(1)} %copy-done.2, bf16[768,128]{1,0:T(8,128)(2,1)S(1)} %part_sum.1.after_ref.s_ref, ...), custom_call_target="tpu_custom_call" | custom-call | flops 46000001024 | tf_op jit(solution)/shard_map/grads/pallas_call | solution.py:235
  14.0 1.7 %collective-permute-start.2 = (bf16[512,128]{1,0:T(8,128)(2,1)S(1)}, bf16[512,128]{1,0:T(8,128)(2,1)S(1)}, u32[]{:S(2)}, u32[]{:S(2)}) collective-permute-start(bf16[512,128]{1,0:T(8,128)(2,1)S(1)} %get-tuple-element.29.after_ref), channel_id=1, source_target_pairs={{0,4},{4,0},{8,12},{12,8},{1,5},{5,1},{9,13},{13,9},{2,6},{6,2},{1... | collective-permute-start | bytes 393224 | tf_op jit(solution)/shard_map/ppermute | solution.py:35
  15.7 1.5 %collective-permute-start.5 = (bf16[512,128]{1,0:T(8,128)(2,1)S(1)}, bf16[512,128]{1,0:T(8,128)(2,1)S(1)}, u32[]{:S(2)}, u32[]{:S(2)}) collective-permute-start(bf16[512,128]{1,0:T(8,128)(2,1)S(1)} %get-tuple-element.31), channel_id=1, source_target_pairs={{0,16},{16,0},{1,17},{17,1},{2,18},{18,2},{3,19},{19,3},{4,20},{20... | collective-permute-start | bytes 393224 | tf_op jit(solution)/shard_map/ppermute | solution.py:35
  17.2 0.0 collective-permute-done.3.got_ref
  17.2 0.3 far.1.rest_0_.far_ref
  17.5 1.4 %collective-permute-start.8 = (bf16[512,1152]{1,0:T(8,128)(2,1)S(1)}, bf16[512,1152]{1,0:T(8,128)(2,1)S(1)}, u32[]{:S(2)}, u32[]{:S(2)}) collective-permute-start(bf16[512,1152]{1,0:T(8,128)(2,1)S(1)} %far.1.rest_0_.far_ref), channel_id=1, source_target_pairs={{0,2},{1,3},{2,0},{3,1},{4,6},{5,7},{6,4},{7,5},{8,10},{9,11},{10,... | collective-permute-start | bytes 3538952 | tf_op jit(solution)/shard_map/ppermute | solution.py:35
  18.9 1.0 %collective-permute-done.2.got_ref = bf16[512,128]{1,0:T(8,128)(2,1)S(1)} collective-permute-done((bf16[512,128]{1,0:T(8,128)(2,1)S(1)}, bf16[512,128]{1,0:T(8,128)(2,1)S(1)}, u32[]{:S(2)}, u32[]{:S(2)}) %collective-permute-start.2) | collective-permute-done | bytes 131104 | tf_op jit(solution)/shard_map/ppermute | solution.py:35
  19.9 2.7 %collective-permute-start.4 = (bf16[512,128]{1,0:T(8,128)(2,1)S(1)}, bf16[512,128]{1,0:T(8,128)(2,1)S(1)}, u32[]{:S(2)}, u32[]{:S(2)}) collective-permute-start(bf16[512,128]{1,0:T(8,128)(2,1)S(1)} %step_a0.1.rest_0_.mine_ref), channel_id=1, source_target_pairs={{0,8},{4,12},{8,0},{12,4},{1,9},{5,13},{9,1},{13,5},{2,10},{6,14},... | collective-permute-start | bytes 393224 | tf_op jit(solution)/shard_map/ppermute | solution.py:35
  22.5 0.0 collective-permute-done.5.got_ref
  22.6 1.6 %collective-permute-start.6 = (bf16[512,128]{1,0:T(8,128)(2,1)S(1)}, bf16[512,128]{1,0:T(8,128)(2,1)S(1)}, u32[]{:S(2)}, u32[]{:S(2)}) collective-permute-start(bf16[512,128]{1,0:T(8,128)(2,1)S(1)} %step_b1.1.after_ref.mine_ref.rest_0_), channel_id=1, source_target_pairs={{0,4},{4,0},{8,12},{12,8},{1,5},{5,1},{9,13},{13,9},{2,6},{6,2},{1... | collective-permute-start | bytes 393224 | tf_op jit(solution)/shard_map/ppermute | solution.py:35
  24.2 2.7 %query_beside.1.rest_1_ = bf16[512,1024]{1,0:T(8,128)(2,1)S(1)} custom-call(bf16[512,1024]{1,0:T(8,128)(2,1)S(1)} %get-tuple-element.25.hg_ref, bf16[1024,4096]{1,0:T(8,128)(2,1)} %w_hbm.7, bf16[512,128]{1,0:T(8,128)(2,1)S(1)} %get-tuple-element.26.after_ref.low_ref, bf16[512,128]{1,0:T(8,128)(2,1)S(1)} %step_b1.1.after_ref.mine_ref.rest_0_), custom_call_target="tpu_custom_call" | custom-call | flops 1150000000 | tf_op jit(solution)/shard_map/query_beside/pallas_call | solution.py:235
  26.9 2.1 %collective-permute-done.6.got_ref = bf16[512,128]{1,0:T(8,128)(2,1)S(1)} collective-permute-done((bf16[512,128]{1,0:T(8,128)(2,1)S(1)}, bf16[512,128]{1,0:T(8,128)(2,1)S(1)}, u32[]{:S(2)}, u32[]{:S(2)}) %collective-permute-start.6) | collective-permute-done | bytes 131104 | tf_op jit(solution)/shard_map/ppermute | solution.py:35
  29.1 1.3 %collective-permute-start.11 = (bf16[512,128]{1,0:T(8,128)(2,1)S(1)}, bf16[512,128]{1,0:T(8,128)(2,1)S(1)}, u32[]{:S(2)}, u32[]{:S(2)}) collective-permute-start(bf16[512,128]{1,0:T(8,128)(2,1)S(1)} %get-tuple-element.32.rest_0_.mine_ref), channel_id=1, source_target_pairs={{0,8},{4,12},{8,0},{12,4},{1,9},{5,13},{9,1},{13,5},{2,10},{6,14},... | collective-permute-start | bytes 393224 | tf_op jit(solution)/shard_map/ppermute | solution.py:35
  30.4 0.0 collective-permute-done.4.got_ref
  30.4 1.6 %collective-permute-start.9 = (bf16[512,128]{1,0:T(8,128)(2,1)S(1)}, bf16[512,128]{1,0:T(8,128)(2,1)S(1)}, u32[]{:S(2)}, u32[]{:S(2)}) collective-permute-start(bf16[512,128]{1,0:T(8,128)(2,1)S(1)} %step_a4.1.after_ref.mine_ref), channel_id=1, source_target_pairs={{0,16},{16,0},{1,17},{17,1},{2,18},{18,2},{3,19},{19,3},{4,20},{20... | collective-permute-start | bytes 393224 | tf_op jit(solution)/shard_map/ppermute | solution.py:35
  32.0 0.0 collective-permute-start.7
  32.0 2.7 %query_close.1.after_ref.mine_ref = bf16[512,1024]{1,0:T(8,128)(2,1)S(1)} custom-call(bf16[512,1024]{1,0:T(8,128)(2,1)S(1)} %get-tuple-element.25.hg_ref, bf16[1024,4096]{1,0:T(8,128)(2,1)} %w_hbm.7, bf16[512,128]{1,0:T(8,128)(2,1)S(1)} %get-tuple-element.26.after_ref.low_ref, bf16[512,128]{1,0:T(8,128)(2,1)S(1)} %step_a4.1.after_ref.mine_ref), custom_call_target="tpu_custom_call" | custom-call | flops 575000000 | tf_op jit(solution)/shard_map/query_close/pallas_call | solution.py:235
  34.7 1.0 %multiply_cosine_fusion.1 = (f32[256,64]{1,0:T(8,128)S(1)}, f32[256,64]{1,0:T(8,128)S(1)}, f32[256,64]{1,0:T(8,128)S(1)}, f32[256,64]{1,0:T(8,128)S(1)}, f32[256,64]{1,0:T(8,128)S(1)}, /*index=5*/f32[256,64]{1,0:T(8,128)S(1)}) fusion(f32[64]{0:T(128)S(1)} %multiply_power_fusion, f32[256]{0:T(256)S(1)} %bitcast.6, f32[256]{0:T(256)S(1)} %broadcast_add_fusion), kind=kLoop, calls=%fused_computation.4 | loop fusion | flops 65536 | bytes 395520 | tf_op jit(solution)/shard_map/cos | solution.py:256
  35.7 0.1 maximum_maximum_fusion.rest_0_.sin_ref
  35.8 0.0 collective-permute-done.9.got_ref
  35.9 0.5 collective-permute-done.11.got_ref
  36.4 1.6 %collective-permute-start.12 = (bf16[512,128]{1,0:T(8,128)(2,1)S(1)}, bf16[512,128]{1,0:T(8,128)(2,1)S(1)}, u32[]{:S(2)}, u32[]{:S(2)}) collective-permute-start(bf16[512,128]{1,0:T(8,128)(2,1)S(1)} %step_b8.1.mine_b), channel_id=1, source_target_pairs={{0,16},{16,0},{1,17},{17,1},{2,18},{18,2},{3,19},{19,3},{4,20},{20... | collective-permute-start | bytes 393224 | tf_op jit(solution)/shard_map/ppermute | solution.py:35
  38.0 0.0 collective-permute-start.10
  38.0 3.9 %collective-permute-done.12.got_b = bf16[512,128]{1,0:T(8,128)(2,1)S(1)} collective-permute-done((bf16[512,128]{1,0:T(8,128)(2,1)S(1)}, bf16[512,128]{1,0:T(8,128)(2,1)S(1)}, u32[]{:S(2)}, u32[]{:S(2)}) %collective-permute-start.12) | collective-permute-done | bytes 131104 | tf_op jit(solution)/shard_map/ppermute | solution.py:35
  41.9 1.1 %collective-permute-done.10.got_a = bf16[512,128]{1,0:T(8,128)(2,1)S(1)} collective-permute-done((bf16[512,128]{1,0:T(8,128)(2,1)S(1)}, bf16[512,128]{1,0:T(8,128)(2,1)S(1)}, u32[]{:S(2)}, u32[]{:S(2)}) %collective-permute-start.10) | collective-permute-done | bytes 131104 | tf_op jit(solution)/shard_map/ppermute | solution.py:35
  43.0 0.5 %low_rank.1 = (bf16[544,128]{1,0:T(8,128)(2,1)S(1)}, bf16[1024,128]{1,0:T(8,128)(2,1)S(1)}, bf16[1024,128]{1,0:T(8,128)(2,1)S(1)}) custom-call(bf16[512,1024]{1,0:T(8,128)(2,1)S(1)} %get-tuple-element.25.hg_ref, f32[8,128]{1,0:T(8,128)S(1)} %get-tuple-element.34.sums_ref, bf16[512,128]{1,0:T(8,128)(2,1)S(1)} %step_a7.1.rest_0_.mine_a, ...), custom_call_target="tpu_custom_call" | custom-call | flops 11500000 | tf_op jit(solution)/shard_map/low_rank/pallas_call | solution.py:235
  43.5 0.1 collective-permute-start.13
  43.6 1.3 %collective-permute-done.13.b_ref = bf16[544,128]{1,0:T(8,128)(2,1)S(1)} collective-permute-done((bf16[544,128]{1,0:T(8,128)(2,1)S(1)}, bf16[544,128]{1,0:T(8,128)(2,1)S(1)}, u32[]{:S(2)}, u32[]{:S(2)}) %collective-permute-start.13) | collective-permute-done | bytes 139296 | tf_op jit(solution)/shard_map/ppermute | solution.py:35
  45.0 0.1 collective-permute-start.14
  45.1 0.1 maximum_maximum_fusion.1.cos_ref
  45.2 0.0 copy-start.3
  45.2 0.0 copy-start.4
  45.2 0.0 collective-permute-done.7.near_ref
  45.2 0.0 collective-permute-done.8.far_got
  45.2 0.5 base.1
  45.7 5.0 %collective-permute-done.14.r_ref = bf16[544,128]{1,0:T(8,128)(2,1)S(1)} collective-permute-done((bf16[544,128]{1,0:T(8,128)(2,1)S(1)}, bf16[544,128]{1,0:T(8,128)(2,1)S(1)}, u32[]{:S(2)}, u32[]{:S(2)}) %collective-permute-start.14) | collective-permute-done | bytes 139296 | tf_op jit(solution)/shard_map/ppermute | solution.py:35
  50.8 2.0 %final.1 = (f32[1024,128]{1,0:T(8,128)}, f32[128,1024]{1,0:T(8,128)}, bf16[512,1024]{1,0:T(8,128)(2,1)}) custom-call(f32[512,1024]{1,0:T(8,128)S(1)} %get-tuple-element.36.base_ref, f32[512,128]{1,0:T(8,128)S(1)} %get-tuple-element.37.low_ref, bf16[544,128]{1,0:T(8,128)(2,1)S(1)} %merge.1.after_ref.s_ref, ...), custom_call_target="tpu_custom_call" | custom-call | flops 2070000000 | tf_op jit(solution)/shard_map/final/pallas_call | solution.py:235
  (19 shorter events, 0.3 us)
Async XLA Ops:
  0.6 3.0 %copy-start.5 = (f32[1024]{0:T(1024)S(1)}, f32[1024]{0:T(1024)}, u32[]{:S(2)}) copy-start(f32[1024]{0:T(1024)} %param.14) | copy-start | bytes 12292
  3.1 1.6 %collective-permute-start = (bf16[768,128]{1,0:T(8,128)(2,1)S(1)}, bf16[768,128]{1,0:T(8,128)(2,1)S(1)}, u32[]{:S(2)}, u32[]{:S(2)}) collective-permute-start(bf16[768,128]{1,0:T(8,128)(2,1)S(1)} %get-tuple-element.27.x_ref), channel_id=1, source_target_pairs={{0,1},{1,0},{2,3},{3,2},{4,5},{5,4},{6,7},{7,6},{8,9},{9,8},{10,11... | collective-permute-start | bytes 589832 | tf_op jit(solution)/shard_map/ppermute | solution.py:35
  4.8 8.5 %collective-permute-start.1 = (bf16[768,128]{1,0:T(8,128)(2,1)S(1)}, bf16[768,128]{1,0:T(8,128)(2,1)S(1)}, u32[]{:S(2)}, u32[]{:S(2)}) collective-permute-start(bf16[768,128]{1,0:T(8,128)(2,1)S(1)} %part_sum.1.after_ref.s_ref), channel_id=1, source_target_pairs={{0,2},{1,3},{2,0},{3,1},{4,6},{5,7},{6,4},{7,5},{8,10},{9,11},{10,... | collective-permute-start | bytes 589832 | tf_op jit(solution)/shard_map/ppermute | solution.py:35
  10.4 2.9 %copy-start.1 = (bf16[384,1024]{1,0:T(8,128)(2,1)S(1)}, bf16[384,1024]{1,0:T(8,128)(2,1)}, u32[]{:S(2)}) copy-start(bf16[384,1024]{1,0:T(8,128)(2,1)} %x_ref.1) | copy-start | bytes 2359300
  10.4 2.9 %copy-start.2 = (bf16[384,1024]{1,0:T(8,128)(2,1)S(1)}, bf16[384,1024]{1,0:T(8,128)(2,1)}, u32[]{:S(2)}) copy-start(bf16[384,1024]{1,0:T(8,128)(2,1)} %v_ref.1) | copy-start | bytes 2359300
  10.4 6.7 %collective-permute-start.3 = (bf16[512,1152]{1,0:T(8,128)(2,1)S(1)}, bf16[512,1152]{1,0:T(8,128)(2,1)S(1)}, u32[]{:S(2)}, u32[]{:S(2)}) collective-permute-start(bf16[512,1152]{1,0:T(8,128)(2,1)S(1)} %query_diag.1.after_ref.diag_ref), channel_id=1, source_target_pairs={{0,1},{1,0},{2,3},{3,2},{4,5},{5,4},{6,7},{7,6},{8,9},{9,8},{10,11... | collective-permute-start | bytes 3538952 | tf_op jit(solution)/shard_map/ppermute | solution.py:35
  14.0 5.9 %collective-permute-start.2 = (bf16[512,128]{1,0:T(8,128)(2,1)S(1)}, bf16[512,128]{1,0:T(8,128)(2,1)S(1)}, u32[]{:S(2)}, u32[]{:S(2)}) collective-permute-start(bf16[512,128]{1,0:T(8,128)(2,1)S(1)} %get-tuple-element.29.after_ref), channel_id=1, source_target_pairs={{0,4},{4,0},{8,12},{12,8},{1,5},{5,1},{9,13},{13,9},{2,6},{6,2},{1... | collective-permute-start | bytes 393224 | tf_op jit(solution)/shard_map/ppermute | solution.py:35
  15.7 6.9 %collective-permute-start.5 = (bf16[512,128]{1,0:T(8,128)(2,1)S(1)}, bf16[512,128]{1,0:T(8,128)(2,1)S(1)}, u32[]{:S(2)}, u32[]{:S(2)}) collective-permute-start(bf16[512,128]{1,0:T(8,128)(2,1)S(1)} %get-tuple-element.31), channel_id=1, source_target_pairs={{0,16},{16,0},{1,17},{17,1},{2,18},{18,2},{3,19},{19,3},{4,20},{20... | collective-permute-start | bytes 393224 | tf_op jit(solution)/shard_map/ppermute | solution.py:35
  17.5 27.8 %collective-permute-start.8 = (bf16[512,1152]{1,0:T(8,128)(2,1)S(1)}, bf16[512,1152]{1,0:T(8,128)(2,1)S(1)}, u32[]{:S(2)}, u32[]{:S(2)}) collective-permute-start(bf16[512,1152]{1,0:T(8,128)(2,1)S(1)} %far.1.rest_0_.far_ref), channel_id=1, source_target_pairs={{0,2},{1,3},{2,0},{3,1},{4,6},{5,7},{6,4},{7,5},{8,10},{9,11},{10,... | collective-permute-start | bytes 3538952 | tf_op jit(solution)/shard_map/ppermute | solution.py:35
  19.9 10.5 %collective-permute-start.4 = (bf16[512,128]{1,0:T(8,128)(2,1)S(1)}, bf16[512,128]{1,0:T(8,128)(2,1)S(1)}, u32[]{:S(2)}, u32[]{:S(2)}) collective-permute-start(bf16[512,128]{1,0:T(8,128)(2,1)S(1)} %step_a0.1.rest_0_.mine_ref), channel_id=1, source_target_pairs={{0,8},{4,12},{8,0},{12,4},{1,9},{5,13},{9,1},{13,5},{2,10},{6,14},... | collective-permute-start | bytes 393224 | tf_op jit(solution)/shard_map/ppermute | solution.py:35
  22.6 6.4 %collective-permute-start.6 = (bf16[512,128]{1,0:T(8,128)(2,1)S(1)}, bf16[512,128]{1,0:T(8,128)(2,1)S(1)}, u32[]{:S(2)}, u32[]{:S(2)}) collective-permute-start(bf16[512,128]{1,0:T(8,128)(2,1)S(1)} %step_b1.1.after_ref.mine_ref.rest_0_), channel_id=1, source_target_pairs={{0,4},{4,0},{8,12},{12,8},{1,5},{5,1},{9,13},{13,9},{2,6},{6,2},{1... | collective-permute-start | bytes 393224 | tf_op jit(solution)/shard_map/ppermute | solution.py:35
  29.1 7.3 %collective-permute-start.11 = (bf16[512,128]{1,0:T(8,128)(2,1)S(1)}, bf16[512,128]{1,0:T(8,128)(2,1)S(1)}, u32[]{:S(2)}, u32[]{:S(2)}) collective-permute-start(bf16[512,128]{1,0:T(8,128)(2,1)S(1)} %get-tuple-element.32.rest_0_.mine_ref), channel_id=1, source_target_pairs={{0,8},{4,12},{8,0},{12,4},{1,9},{5,13},{9,1},{13,5},{2,10},{6,14},... | collective-permute-start | bytes 393224 | tf_op jit(solution)/shard_map/ppermute | solution.py:35
  30.4 5.4 %collective-permute-start.9 = (bf16[512,128]{1,0:T(8,128)(2,1)S(1)}, bf16[512,128]{1,0:T(8,128)(2,1)S(1)}, u32[]{:S(2)}, u32[]{:S(2)}) collective-permute-start(bf16[512,128]{1,0:T(8,128)(2,1)S(1)} %step_a4.1.after_ref.mine_ref), channel_id=1, source_target_pairs={{0,16},{16,0},{1,17},{17,1},{2,18},{18,2},{3,19},{19,3},{4,20},{20... | collective-permute-start | bytes 393224 | tf_op jit(solution)/shard_map/ppermute | solution.py:35
  32.0 2.7 %copy-start = (s32[256]{0:T(256)S(1)}, s32[256]{0:T(256)}, u32[]{:S(2)}) copy-start(s32[256]{0:T(256)} %param.15) | copy-start | bytes 3076
  32.0 13.3 %collective-permute-start.7 = (bf16[512,1024]{1,0:T(8,128)(2,1)S(1)}, bf16[512,1024]{1,0:T(8,128)(2,1)S(1)}, u32[]{:S(2)}, u32[]{:S(2)}) collective-permute-start(bf16[512,1024]{1,0:T(8,128)(2,1)S(1)} %get-tuple-element.33), channel_id=1, source_target_pairs={{0,1},{1,0},{2,3},{3,2},{4,5},{5,4},{6,7},{7,6},{8,9},{9,8},{10,11... | collective-permute-start | bytes 3145736 | tf_op jit(solution)/shard_map/ppermute | solution.py:35
  36.4 5.5 %collective-permute-start.12 = (bf16[512,128]{1,0:T(8,128)(2,1)S(1)}, bf16[512,128]{1,0:T(8,128)(2,1)S(1)}, u32[]{:S(2)}, u32[]{:S(2)}) collective-permute-start(bf16[512,128]{1,0:T(8,128)(2,1)S(1)} %step_b8.1.mine_b), channel_id=1, source_target_pairs={{0,16},{16,0},{1,17},{17,1},{2,18},{18,2},{3,19},{19,3},{4,20},{20... | collective-permute-start | bytes 393224 | tf_op jit(solution)/shard_map/ppermute | solution.py:35
  38.0 5.0 %collective-permute-start.10 = (bf16[512,128]{1,0:T(8,128)(2,1)S(1)}, bf16[512,128]{1,0:T(8,128)(2,1)S(1)}, u32[]{:S(2)}, u32[]{:S(2)}) collective-permute-start(bf16[512,128]{1,0:T(8,128)(2,1)S(1)} %step_a7.1.rest_0_.mine_a), channel_id=1, source_target_pairs={{0,4},{4,0},{8,12},{12,8},{1,5},{5,1},{9,13},{13,9},{2,6},{6,2},{1... | collective-permute-start | bytes 393224 | tf_op jit(solution)/shard_map/ppermute | solution.py:35
  43.5 1.4 %collective-permute-start.13 = (bf16[544,128]{1,0:T(8,128)(2,1)S(1)}, bf16[544,128]{1,0:T(8,128)(2,1)S(1)}, u32[]{:S(2)}, u32[]{:S(2)}) collective-permute-start(bf16[544,128]{1,0:T(8,128)(2,1)S(1)} %get-tuple-element.35.a_ref), channel_id=1, source_target_pairs={{0,1},{1,0},{2,3},{3,2},{4,5},{5,4},{6,7},{7,6},{8,9},{9,8},{10,11... | collective-permute-start | bytes 417800 | tf_op jit(solution)/shard_map/ppermute | solution.py:35
  45.0 5.8 %collective-permute-start.14 = (bf16[544,128]{1,0:T(8,128)(2,1)S(1)}, bf16[544,128]{1,0:T(8,128)(2,1)S(1)}, u32[]{:S(2)}, u32[]{:S(2)}) collective-permute-start(bf16[544,128]{1,0:T(8,128)(2,1)S(1)} %merge.1.after_ref.s_ref), channel_id=1, source_target_pairs={{0,2},{1,3},{2,0},{3,1},{4,6},{5,7},{6,4},{7,5},{8,10},{9,11},{10,... | collective-permute-start | bytes 417800 | tf_op jit(solution)/shard_map/ppermute | solution.py:35
  45.2 5.6 %copy-start.3 = (f32[1024,128]{1,0:T(8,128)S(1)}, f32[1024,128]{1,0:T(8,128)}, u32[]{:S(2)}) copy-start(f32[1024,128]{1,0:T(8,128)} %a_ref.1) | copy-start | bytes 1572868
  45.2 5.6 %copy-start.4 = (f32[128,1024]{1,0:T(8,128)S(1)}, f32[128,1024]{1,0:T(8,128)}, u32[]{:S(2)}) copy-start(f32[128,1024]{1,0:T(8,128)} %b_ref.1) | copy-start | bytes 1572868

commit v12 on v11

--- a/solution.py
+++ b/solution.py
@@ -60,17 +60,24 @@
 
 
 def rank_kernel(x_hbm, v_hbm, a_hbm, b_hbm, h_hbm, out_ref, a16_ref, h_ref, x_ref, v_ref, a_ref, b_ref, sems):
-    copies = fetch((x_hbm, a_hbm, v_hbm, b_hbm, h_hbm), (x_ref, a_ref, v_ref, b_ref, h_ref), sems)
     count = x_ref.shape[0]
+    half = count // 2
+    copies = fetch(
+        (a_hbm, x_hbm, b_hbm, v_hbm.at[:half], v_hbm.at[half:], h_hbm),
+        (a_ref, x_ref, b_ref, v_ref.at[:half], v_ref.at[half:], h_ref),
+        sems,
+    )
+    copies[0].wait()
+    a16_ref[...] = a_ref[...].astype(BF)
     copies[1].wait()
-    a16_ref[...] = a_ref[...].astype(BF)
-    copies[0].wait()
     out_ref[:count] = dot(x_ref[...], a16_ref[...]).astype(BF)
+    copies[2].wait()
+    b16 = b_ref[...].astype(BF)
     copies[3].wait()
-    b16 = b_ref[...].astype(BF)
-    copies[2].wait()
-    out_ref[count:] = dot(v_ref[...], b16, ((1,), (1,))).astype(BF)
+    out_ref[count : count + half] = dot(v_ref[:half], b16, ((1,), (1,))).astype(BF)
     copies[4].wait()
+    out_ref[count + half :] = dot(v_ref[half:], b16, ((1,), (1,))).astype(BF)
+    copies[5].wait()
 
 
 def weight_blocks(peers, w_hbm, w_ref):
@@ -102,18 +109,36 @@
     sum_kernel(x_ref, got_ref, out_ref)
 
 
-def query_kernel(peers, hg_ref, w_hbm, low_ref, after_ref, *rest):
+def query_kernel(peers, hg_ref, w_hbm, after_ref, *rest):
     outs, (w_ref, sems) = rest[:-2], rest[-2:]
     _, width, cut = w_ref.shape
     copies = fetch(*weight_blocks(peers, w_hbm, w_ref), sems)
-    if outs[0].shape[1] > width:
-        outs[0][:, width:] = low_ref[...]
     per = width // cut
     for i, copy in enumerate(copies):
         copy.wait()
         outs[i // per][:, i % per * cut : (i % per + 1) * cut] = dot(hg_ref[...], w_ref[i]).astype(BF)
 
 
+def diag_kernel(hg_ref, w_hbm, low_ref, after_ref, out_ref, next_ref, w_ref, sems):
+    _, width, cut = w_ref.shape
+    per = width // cut
+    mine, targets = weight_blocks((3,), w_hbm, w_ref)
+    later, next_targets = weight_blocks((2,), w_hbm, next_ref)
+    copies = fetch(mine + later, targets + next_targets, sems)
+    out_ref[:, width:] = low_ref[...]
+    for i in range(per):
+        copies[i].wait()
+        out_ref[:, i * cut : (i + 1) * cut] = dot(hg_ref[...], w_ref[i]).astype(BF)
+    for copy in copies[per:]:
+        copy.wait()
+
+
+def distant_kernel(hg_ref, w_ref, after_ref, out_ref):
+    per, _, cut = w_ref.shape
+    for i in range(per):
+        out_ref[:, i * cut : (i + 1) * cut] = dot(hg_ref[...], w_ref[i]).astype(BF)
+
+
 def far_kernel(mine_ref, diag_ref, got_ref, after_ref, out_ref):
     width = mine_ref.shape[1]
     sum_kernel(mine_ref, got_ref.at[:, :width], out_ref.at[:, :width])
@@ -131,27 +156,24 @@
     return pl.ds(pl.multiple_of(mine, size), size), pl.ds(pl.multiple_of(size - mine, size), size)
 
 
-def halve(axis, bit, total_ref, keep_ref, send_ref):
-    mine, other = halves(axis, bit, keep_ref.shape[0])
-    keep_ref[...] = total_ref[mine]
-    send_ref[...] = total_ref[other].astype(BF)
-
-
 def join(axis, bit, mine_ref, got_ref, out_ref):
     mine, other = halves(axis, bit, mine_ref.shape[0])
     out_ref[mine] = mine_ref[...]
     out_ref[other] = got_ref[...]
 
 
-def grad_kernel(axes, x_ref, v_ref, s_ref, r_ref, after_ref, keep_a, send_a, keep_b, send_b, ga, gb):
+def grad_kernel(axes, x_ref, v_ref, s_ref, r_ref, after_ref, keep_a, send_a, keep_b, send_b):
     count, width = x_ref.shape
     low = (s_ref[...].astype(F32) + r_ref[...].astype(F32)).astype(BF)
-    ga[...] = SCALE * dot(x_ref[...], low[count:], ((0,), (0,)))
-    halve(*axes[0], ga, keep_a, send_a)
-    turned = SCALE * dot(low[:count], v_ref[...], ((0,), (0,)))
-    for b in blocks_of(width):
-        gb[b] = turned[:, b]
-    halve(*axes[1], gb, keep_b, send_b)
+    mine, other = halves(*axes[0], width // 2)
+    send_a[...] = (SCALE * dot(x_ref[:, other], low[count:], ((0,), (0,)))).astype(BF)
+    keep_a[...] = SCALE * dot(x_ref[:, mine], low[count:], ((0,), (0,)))
+    mine, other = halves(*axes[1], width // 2)
+    sent = (SCALE * dot(low[:count], v_ref[:, other], ((0,), (0,)))).astype(BF)
+    kept = SCALE * dot(low[:count], v_ref[:, mine], ((0,), (0,)))
+    for b in blocks_of(width // 2):
+        send_b[b] = sent[:, b]
+        keep_b[b] = kept[:, b]
 
 
 def sum_kernel(keep_ref, got_ref, out_ref):
@@ -171,13 +193,23 @@
     return jnp.broadcast_to(jnp.sum(x * x), (8, LANES))
 
 
-def low_kernel(way_a, way_b, hg_ref, sums_ref, mine_a, got_a, mine_b, got_b, pack_ref, ga_ref, gb_ref):
+def own_kernel(way, hg_ref, sums_ref, mine_a, mine_b, after_ref, low_ref, sums_out):
+    mine, _ = halves(*way, mine_a.shape[0])
+    low_ref[...] = dot(hg_ref[:, mine], mine_a[...])
+    sums_out[0] = sums_ref[...]
+    sums_out[1] = square_sum(mine_a)
+    sums_out[2] = square_sum(mine_b)
+
+
+def low_kernel(way_a, way_b, hg_ref, low_ref, sums_ref, mine_a, got_a, mine_b, got_b, pack_ref, ga_ref, gb_ref):
     join(*way_a, mine_a, got_a, ga_ref)
     count = hg_ref.shape[0]
-    pack_ref[:count] = dot(hg_ref[...], ga_ref[...]).astype(BF)
+    _, other = halves(*way_a, mine_a.shape[0])
+    pack_ref[:count] = (low_ref[...] + dot(hg_ref[:, other], got_a[...])).astype(BF)
     join(*way_b, mine_b, got_b, gb_ref)
+    squares = (sums_ref[1] + square_sum(got_a)) + (sums_ref[2] + square_sum(got_b))
     row = lax.broadcasted_iota(jnp.int32, (8, LANES), 0)
-    pack_ref[count:] = split_terms(jnp.where(row == 7, square_sum(ga_ref) + square_sum(gb_ref), sums_ref[...]))
+    pack_ref[count:] = split_terms(jnp.where(row == 7, squares, sums_ref[0]))
 
 
 def base_kernel(mine_ref, near_ref, far_ref, far_got, after_ref, base_ref, low_ref):
@@ -224,10 +256,7 @@
     return pltpu.with_memory_space_constraint(x, pltpu.HBM)
 
 
-WEIGHTS = {
-    "rank": 2.4, "prep": 0.6, "query_diag": 40.0, "query_distant": 0.01, "query_beside": 1.0, "query_close": 0.5, "grads": 40.0,
-    "final": 1.8,
-}
+WEIGHTS = {"rank": 2.4, "prep": 0.6, "query_diag": 40.0, "query_distant": 0.01, "query_beside": 1.0, "query_close": 0.5, "grads": 40.0, "final": 1.8}
 FLOPS_PER_WEIGHT = 1_150_000_000
 
 
@@ -293,7 +322,7 @@
             ),
             "rank",
             [pltpu.VMEM(train_inputs.shape, BF), pltpu.VMEM(train_inputs.shape, BF),
-             pltpu.VMEM(factor_a.shape, F32), pltpu.VMEM(factor_b.shape, F32), dma(5)],
+             pltpu.VMEM(factor_a.shape, F32), pltpu.VMEM(factor_b.shape, F32), dma(6)],
         )
         part_got = swap(part, "tp", n_tp, 1)
         cut = 512
@@ -313,15 +342,23 @@
             return call(
                 functools.partial(query_kernel, peers),
                 outs,
-                [VMEM, HBM, VMEM, ANY],
-                (gained, keep_hbm(base_weight), low, after),
+                [VMEM, HBM, ANY],
+                (gained, keep_hbm(base_weight), after),
                 "query_" + name,
                 [pltpu.VMEM((blocks, width, cut), BF), dma(blocks)],
             )
 
-        (diag,) = query((3,), [wide], part_sum, "diag")
+        per = width // cut
+        diag, columns = call(
+            diag_kernel,
+            [wide, shape((per, width, cut), BF)],
+            [VMEM, HBM, VMEM, ANY],
+            (gained, keep_hbm(base_weight), low, part_sum),
+            "query_diag",
+            [pltpu.VMEM((per, width, cut), BF), dma(2 * per)],
+        )
         diag_got = swap(diag, "tp", n_tp, 1)
-        (distant,) = query((2,), [tall], diag, "distant")
+        distant = call(distant_kernel, tall, [VMEM, VMEM, ANY], (gained, columns, diag), "query_distant")
 
         half = width // 2
         keep_a, send_a, keep_b, send_b = call(
@@ -330,7 +367,6 @@
             [VMEM] * 4 + [ANY],
             (train_inputs, train_cotangent, part_sum, part_far, distant),
             "grads",
-            [vmem(width), vmem(width)],
         )
         far = call(far_kernel, wide, [VMEM] * 3 + [ANY], (distant, diag, diag_got, send_a), "far")
         far_got = swap(far, "tp", n_tp, 2)
@@ -367,11 +403,18 @@
             else:
                 (close,) = query((0,), [tall], after, "close")
                 after = close
+        own_low, own_sums = call(
+            functools.partial(own_kernel, path_a[-1]),
+            [shape((count, rank), F32), shape((3, 8, LANES), F32)],
+            [VMEM] * 4 + [ANY],
+            (gained, sums, mine_a, mine_b, after),
+            "own_half",
+        )
         step_pack, grad_a, grad_b = call(
             functools.partial(low_kernel, path_a[-1], path_b[-1]),
             [shape((count + EXTRA, rank), BF), shape((width, rank), BF), shape((width, rank), BF)],
-            [VMEM] * 6,
-            (gained, sums, mine_a, cross(mine_a, *path_a[-1]), mine_b, cross(mine_b, *path_b[-1])),
+            [VMEM] * 7,
+            (gained, own_low, own_sums, mine_a, cross(mine_a, *path_a[-1]), mine_b, cross(mine_b, *path_b[-1])),
             "low_rank",
         )
         step_got = swap(step_pack, "tp", n_tp, 1)

time: 52.9 us -> 50.4 us (0.953)
  waiting for transfers between devices: 15.5 us -> 13.4 us
  Pallas kernels: 18 us -> 16.7 us
  starting transfers between devices: 17 us -> 17.9 us
    ppermute x15, waiting for transfers between devices: 15.5 us -> 13.4 us  [swap(): return lax.ppermute(x, axis, [(i, i ^ k) for i in range(n)])]
    pallas_call x20 -> x21, Pallas kernels: 18 us -> 16.7 us  [call(): pl.pallas_call(kernel, out_shape=outs, in_specs=in_specs, out_specs=out_s...]
    ppermute x15, starting transfers between devices: 17 us -> 17.9 us  [swap(): return lax.ppermute(x, axis, [(i, i ^ k) for i in range(n)])]
  transfers between devices with their start and end apart: 15 -> 15, of which waited for: 8 -> 8; matrix products, arithmetic and copies ran while one was open for 2% -> 3% of each run, Pallas kernels for 26% -> 24%
where the time goes in v12:
time: 50.4 us; the launch traced here: 50.2 us
  starting transfers between devices  17.9 us (36%)
  Pallas kernels  16.7 us (33%)
  waiting for transfers between devices  13.4 us (27%)
  other arithmetic  1.28 us (3%)
  between operations  0.86 us (2%)
    ppermute x15, starting transfers between devices, swap(): return lax.ppermute(x, axis, [(i, i ^ k) for i in range(n)])  17.9 us
    pallas_call x21, Pallas kernels, call(): pl.pallas_call(kernel, out_shape=outs, in_specs=in_specs, out_specs=out_s...  16.7 us
    ppermute x15, waiting for transfers between devices, swap(): return lax.ppermute(x, axis, [(i, i ^ k) for i in range(n)])  13.4 us
  transfers between devices with their start and end apart: 15, of which 8 were waited for; matrix products, arithmetic and copies ran while one was open for 3% of the time, Pallas kernels for 24%

profile of v12, /device:TPU:0, one launch (start us, length us, event | category | flops | bytes accessed | tf_op | source)
XLA Modules:
  0.0 50.2 jit_solution(17075505503042423433)
XLA Ops:
  0.6 2.6 %rank.1 = (bf16[768,128]{1,0:T(8,128)(2,1)S(1)}, bf16[1024,128]{1,0:T(8,128)(2,1)S(1)}, bf16[512,1024]{1,0:T(8,128)(2,1)S(1)}) custom-call(bf16[384,1024]{1,0:T(8,128)(2,1)} %x_ref.1, bf16[384,1024]{1,0:T(8,128)(2,1)} %v_ref.1, f32[1024,128]{1,0:T(8,128)} %a_ref.1, f32[128,1024]{1,0:T(8,128)} %b_ref.1, bf16[512,1024]{1,0:T(8,128)(2,1)} %bitcast.9), custom_call_target="tpu_custom_call" | custom-call | flops 2760000000 | tf_op jit(solution)/shard_map/rank/pallas_call | solution.py:264
  3.3 0.5 %collective-permute-start = (bf16[768,128]{1,0:T(8,128)(2,1)S(1)}, bf16[768,128]{1,0:T(8,128)(2,1)S(1)}, u32[]{:S(2)}, u32[]{:S(2)}) collective-permute-start(bf16[768,128]{1,0:T(8,128)(2,1)S(1)} %get-tuple-element.30.x_ref), channel_id=1, source_target_pairs={{0,1},{1,0},{2,3},{3,2},{4,5},{5,4},{6,7},{7,6},{8,9},{9,8},{10,11... | collective-permute-start | bytes 589832 | tf_op jit(solution)/shard_map/ppermute | solution.py:35
  3.8 0.6 %prep.1 = (bf16[512,1024]{1,0:T(8,128)(2,1)S(1)}, bf16[512,128]{1,0:T(8,128)(2,1)S(1)}, f32[8,128]{1,0:T(8,128)S(1)}) custom-call(bf16[512,1024]{1,0:T(8,128)(2,1)S(1)} %get-tuple-element.27.h_ref, f32[1,1024]{1,0:T(1,128)S(1)} %bitcast.8, bf16[1024,128]{1,0:T(8,128)(2,1)S(1)} %get-tuple-element.28.a16_ref), custom_call_target="tpu_custom_call" | custom-call | flops 690000000 | tf_op jit(solution)/shard_map/prep/pallas_call | solution.py:264
  4.4 0.5 collective-permute-done.got_ref
  4.9 2.9 %collective-permute-start.1 = (bf16[768,128]{1,0:T(8,128)(2,1)S(1)}, bf16[768,128]{1,0:T(8,128)(2,1)S(1)}, u32[]{:S(2)}, u32[]{:S(2)}) collective-permute-start(bf16[768,128]{1,0:T(8,128)(2,1)S(1)} %part_sum.1.after_ref.s_ref), channel_id=1, source_target_pairs={{0,2},{1,3},{2,0},{3,1},{4,6},{5,7},{6,4},{7,5},{8,10},{9,11},{10,... | collective-permute-start | bytes 589832 | tf_op jit(solution)/shard_map/ppermute | solution.py:35
  7.9 2.7 %query_diag.1 = (bf16[512,1152]{1,0:T(8,128)(2,1)S(1)}, bf16[2,1024,512]{2,1,0:T(8,128)(2,1)S(1)}) custom-call(bf16[512,1024]{1,0:T(8,128)(2,1)S(1)} %get-tuple-element.29.hg_ref, bf16[1024,4096]{1,0:T(8,128)(2,1)} %w_hbm.5, bf16[512,128]{1,0:T(8,128)(2,1)S(1)} %get-tuple-element.31.after_ref.low_ref, bf16[768,128]{1,0:T(8,128)(2,1)S(1)} %part_sum.1.after_ref.s_ref), custom_call_target="tpu_custom_call" | custom-call | flops 46000001024 | tf_op jit(solution)/shard_map/query_diag/pallas_call | solution.py:264
  10.6 0.1 collective-permute-start.3
  10.7 0.0 copy-start.1
  10.7 0.0 copy-start.2
  10.7 1.2 %query_distant.1.after_ref.mine_ref = bf16[512,1024]{1,0:T(8,128)(2,1)S(1)} custom-call(bf16[512,1024]{1,0:T(8,128)(2,1)S(1)} %get-tuple-element.29.hg_ref, bf16[2,1024,512]{2,1,0:T(8,128)(2,1)S(1)} %get-tuple-element.32.w_ref, bf16[512,1152]{1,0:T(8,128)(2,1)S(1)} %get-tuple-element.33.after_ref.diag_ref), custom_call_target="tpu_custom_call" | custom-call | flops 11500000 | tf_op jit(solution)/shard_map/query_distant/pallas_call | solution.py:264
  11.9 1.1 %collective-permute-done.1.r_ref = bf16[768,128]{1,0:T(8,128)(2,1)S(1)} collective-permute-done((bf16[768,128]{1,0:T(8,128)(2,1)S(1)}, bf16[768,128]{1,0:T(8,128)(2,1)S(1)}, u32[]{:S(2)}, u32[]{:S(2)}) %collective-permute-start.1) | collective-permute-done | bytes 196640 | tf_op jit(solution)/shard_map/ppermute | solution.py:35
  13.1 0.6 %grads.1 = (f32[512,128]{1,0:T(8,128)S(1)}, bf16[512,128]{1,0:T(8,128)(2,1)S(1)}, f32[512,128]{1,0:T(8,128)S(1)}, bf16[512,128]{1,0:T(8,128)(2,1)S(1)}) custom-call(bf16[384,1024]{1,0:T(8,128)(2,1)S(1)} %copy-done.1, bf16[384,1024]{1,0:T(8,128)(2,1)S(1)} %copy-done.2, bf16[768,128]{1,0:T(8,128)(2,1)S(1)} %part_sum.1.after_ref.s_ref, ...), custom_call_target="tpu_custom_call" | custom-call | flops 46000001024 | tf_op jit(solution)/shard_map/grads/pallas_call | solution.py:264
  13.6 1.9 %collective-permute-start.2 = (bf16[512,128]{1,0:T(8,128)(2,1)S(1)}, bf16[512,128]{1,0:T(8,128)(2,1)S(1)}, u32[]{:S(2)}, u32[]{:S(2)}) collective-permute-start(bf16[512,128]{1,0:T(8,128)(2,1)S(1)} %get-tuple-element.35.after_ref), channel_id=1, source_target_pairs={{0,4},{4,0},{8,12},{12,8},{1,5},{5,1},{9,13},{13,9},{2,6},{6,2},{1... | collective-permute-start | bytes 393224 | tf_op jit(solution)/shard_map/ppermute | solution.py:35
  15.5 1.5 %collective-permute-start.5 = (bf16[512,128]{1,0:T(8,128)(2,1)S(1)}, bf16[512,128]{1,0:T(8,128)(2,1)S(1)}, u32[]{:S(2)}, u32[]{:S(2)}) collective-permute-start(bf16[512,128]{1,0:T(8,128)(2,1)S(1)} %get-tuple-element.37), channel_id=1, source_target_pairs={{0,16},{16,0},{1,17},{17,1},{2,18},{18,2},{3,19},{19,3},{4,20},{20... | collective-permute-start | bytes 393224 | tf_op jit(solution)/shard_map/ppermute | solution.py:35
  17.0 0.0 collective-permute-done.3.got_ref
  17.0 0.3 far.1.rest_0_.far_ref
  17.3 1.6 %collective-permute-start.8 = (bf16[512,1152]{1,0:T(8,128)(2,1)S(1)}, bf16[512,1152]{1,0:T(8,128)(2,1)S(1)}, u32[]{:S(2)}, u32[]{:S(2)}) collective-permute-start(bf16[512,1152]{1,0:T(8,128)(2,1)S(1)} %far.1.rest_0_.far_ref), channel_id=1, source_target_pairs={{0,2},{1,3},{2,0},{3,1},{4,6},{5,7},{6,4},{7,5},{8,10},{9,11},{10,... | collective-permute-start | bytes 3538952 | tf_op jit(solution)/shard_map/ppermute | solution.py:35
  18.9 0.0 collective-permute-done.2.got_ref
  18.9 2.7 %collective-permute-start.4 = (bf16[512,128]{1,0:T(8,128)(2,1)S(1)}, bf16[512,128]{1,0:T(8,128)(2,1)S(1)}, u32[]{:S(2)}, u32[]{:S(2)}) collective-permute-start(bf16[512,128]{1,0:T(8,128)(2,1)S(1)} %step_a0.1.rest_0_.mine_ref), channel_id=1, source_target_pairs={{0,8},{4,12},{8,0},{12,4},{1,9},{5,13},{9,1},{13,5},{2,10},{6,14},... | collective-permute-start | bytes 393224 | tf_op jit(solution)/shard_map/ppermute | solution.py:35
  21.6 0.0 collective-permute-done.5.got_ref
  21.6 1.6 %collective-permute-start.6 = (bf16[512,128]{1,0:T(8,128)(2,1)S(1)}, bf16[512,128]{1,0:T(8,128)(2,1)S(1)}, u32[]{:S(2)}, u32[]{:S(2)}) collective-permute-start(bf16[512,128]{1,0:T(8,128)(2,1)S(1)} %step_b1.1.after_ref.mine_ref.rest_0_), channel_id=1, source_target_pairs={{0,4},{4,0},{8,12},{12,8},{1,5},{5,1},{9,13},{13,9},{2,6},{6,2},{1... | collective-permute-start | bytes 393224 | tf_op jit(solution)/shard_map/ppermute | solution.py:35
  23.3 2.7 %query_beside.1.rest_1_ = bf16[512,1024]{1,0:T(8,128)(2,1)S(1)} custom-call(bf16[512,1024]{1,0:T(8,128)(2,1)S(1)} %get-tuple-element.29.hg_ref, bf16[1024,4096]{1,0:T(8,128)(2,1)} %w_hbm.5, bf16[512,128]{1,0:T(8,128)(2,1)S(1)} %step_b1.1.after_ref.mine_ref.rest_0_), custom_call_target="tpu_custom_call" | custom-call | flops 1150000000 | tf_op jit(solution)/shard_map/query_beside/pallas_call | solution.py:264
  25.9 1.4 %collective-permute-done.6.got_ref = bf16[512,128]{1,0:T(8,128)(2,1)S(1)} collective-permute-done((bf16[512,128]{1,0:T(8,128)(2,1)S(1)}, bf16[512,128]{1,0:T(8,128)(2,1)S(1)}, u32[]{:S(2)}, u32[]{:S(2)}) %collective-permute-start.6) | collective-permute-done | bytes 131104 | tf_op jit(solution)/shard_map/ppermute | solution.py:35
  27.4 0.9 %collective-permute-start.10 = (bf16[512,128]{1,0:T(8,128)(2,1)S(1)}, bf16[512,128]{1,0:T(8,128)(2,1)S(1)}, u32[]{:S(2)}, u32[]{:S(2)}) collective-permute-start(bf16[512,128]{1,0:T(8,128)(2,1)S(1)} %get-tuple-element.38.rest_0_.mine_ref), channel_id=1, source_target_pairs={{0,8},{4,12},{8,0},{12,4},{1,9},{5,13},{9,1},{13,5},{2,10},{6,14},... | collective-permute-start | bytes 393224 | tf_op jit(solution)/shard_map/ppermute | solution.py:35
  28.3 0.0 collective-permute-done.4.got_ref
  28.3 1.6 %collective-permute-start.9 = (bf16[512,128]{1,0:T(8,128)(2,1)S(1)}, bf16[512,128]{1,0:T(8,128)(2,1)S(1)}, u32[]{:S(2)}, u32[]{:S(2)}) collective-permute-start(bf16[512,128]{1,0:T(8,128)(2,1)S(1)} %step_a4.1.after_ref.mine_ref), channel_id=1, source_target_pairs={{0,16},{16,0},{1,17},{17,1},{2,18},{18,2},{3,19},{19,3},{4,20},{20... | collective-permute-start | bytes 393224 | tf_op jit(solution)/shard_map/ppermute | solution.py:35
  29.9 0.0 collective-permute-start.7
  29.9 2.7 %query_close.1.after_ref.mine_ref = bf16[512,1024]{1,0:T(8,128)(2,1)S(1)} custom-call(bf16[512,1024]{1,0:T(8,128)(2,1)S(1)} %get-tuple-element.29.hg_ref, bf16[1024,4096]{1,0:T(8,128)(2,1)} %w_hbm.5, bf16[512,128]{1,0:T(8,128)(2,1)S(1)} %step_a4.1.after_ref.mine_ref), custom_call_target="tpu_custom_call" | custom-call | flops 575000000 | tf_op jit(solution)/shard_map/query_close/pallas_call | solution.py:264
  32.6 1.0 %multiply_cosine_fusion.1 = (f32[256,64]{1,0:T(8,128)S(1)}, f32[256,64]{1,0:T(8,128)S(1)}, f32[256,64]{1,0:T(8,128)S(1)}, f32[256,64]{1,0:T(8,128)S(1)}, f32[256,64]{1,0:T(8,128)S(1)}, /*index=5*/f32[256,64]{1,0:T(8,128)S(1)}) fusion(f32[64]{0:T(128)S(1)} %multiply_power_fusion, f32[256]{0:T(256)S(1)} %bitcast.6, f32[256]{0:T(256)S(1)} %broadcast_add_fusion), kind=kLoop, calls=%fused_computation.4 | loop fusion | flops 65536 | bytes 395520 | tf_op jit(solution)/shard_map/cos | solution.py:285
  33.6 0.1 maximum_maximum_fusion.rest_0_.sin_ref
  33.7 0.0 collective-permute-done.9.got_ref
  33.8 1.0 %collective-permute-done.10.got_ref = bf16[512,128]{1,0:T(8,128)(2,1)S(1)} collective-permute-done((bf16[512,128]{1,0:T(8,128)(2,1)S(1)}, bf16[512,128]{1,0:T(8,128)(2,1)S(1)}, u32[]{:S(2)}, u32[]{:S(2)}) %collective-permute-start.10) | collective-permute-done | bytes 131104 | tf_op jit(solution)/shard_map/ppermute | solution.py:35
  34.8 0.9 %collective-permute-start.12 = (bf16[512,128]{1,0:T(8,128)(2,1)S(1)}, bf16[512,128]{1,0:T(8,128)(2,1)S(1)}, u32[]{:S(2)}, u32[]{:S(2)}) collective-permute-start(bf16[512,128]{1,0:T(8,128)(2,1)S(1)} %step_b8.1.mine_b.after_ref), channel_id=1, source_target_pairs={{0,16},{16,0},{1,17},{17,1},{2,18},{18,2},{3,19},{19,3},{4,20},{20... | collective-permute-start | bytes 393224 | tf_op jit(solution)/shard_map/ppermute | solution.py:35
  35.7 0.2 collective-permute-start.11
  35.9 0.3 own_half.1
  36.2 3.6 %collective-permute-done.12.got_b = bf16[512,128]{1,0:T(8,128)(2,1)S(1)} collective-permute-done((bf16[512,128]{1,0:T(8,128)(2,1)S(1)}, bf16[512,128]{1,0:T(8,128)(2,1)S(1)}, u32[]{:S(2)}, u32[]{:S(2)}) %collective-permute-start.12) | collective-permute-done | bytes 131104 | tf_op jit(solution)/shard_map/ppermute | solution.py:35
  39.8 0.8 %collective-permute-done.11.got_a = bf16[512,128]{1,0:T(8,128)(2,1)S(1)} collective-permute-done((bf16[512,128]{1,0:T(8,128)(2,1)S(1)}, bf16[512,128]{1,0:T(8,128)(2,1)S(1)}, u32[]{:S(2)}, u32[]{:S(2)}) %collective-permute-start.11) | collective-permute-done | bytes 131104 | tf_op jit(solution)/shard_map/ppermute | solution.py:35
  40.6 0.4 low_rank.1
  41.0 0.1 collective-permute-start.13
  41.1 1.3 %collective-permute-done.13.b_ref = bf16[544,128]{1,0:T(8,128)(2,1)S(1)} collective-permute-done((bf16[544,128]{1,0:T(8,128)(2,1)S(1)}, bf16[544,128]{1,0:T(8,128)(2,1)S(1)}, u32[]{:S(2)}, u32[]{:S(2)}) %collective-permute-start.13) | collective-permute-done | bytes 139296 | tf_op jit(solution)/shard_map/ppermute | solution.py:35
  42.5 1.6 %collective-permute-start.14 = (bf16[544,128]{1,0:T(8,128)(2,1)S(1)}, bf16[544,128]{1,0:T(8,128)(2,1)S(1)}, u32[]{:S(2)}, u32[]{:S(2)}) collective-permute-start(bf16[544,128]{1,0:T(8,128)(2,1)S(1)} %merge.1.after_ref.s_ref), channel_id=1, source_target_pairs={{0,2},{1,3},{2,0},{3,1},{4,6},{5,7},{6,4},{7,5},{8,10},{9,11},{10,... | collective-permute-start | bytes 417800 | tf_op jit(solution)/shard_map/ppermute | solution.py:35
  44.0 0.1 maximum_maximum_fusion.1.cos_ref
  44.2 0.0 copy-start.3
  44.2 0.0 copy-start.4
  44.2 0.0 collective-permute-done.8.far_got
  44.2 0.5 base.1
  44.7 3.5 %collective-permute-done.14.r_ref = bf16[544,128]{1,0:T(8,128)(2,1)S(1)} collective-permute-done((bf16[544,128]{1,0:T(8,128)(2,1)S(1)}, bf16[544,128]{1,0:T(8,128)(2,1)S(1)}, u32[]{:S(2)}, u32[]{:S(2)}) %collective-permute-start.14) | collective-permute-done | bytes 139296 | tf_op jit(solution)/shard_map/ppermute | solution.py:35
  48.3 2.0 %final.1 = (f32[1024,128]{1,0:T(8,128)}, f32[128,1024]{1,0:T(8,128)}, bf16[512,1024]{1,0:T(8,128)(2,1)}) custom-call(f32[512,1024]{1,0:T(8,128)S(1)} %get-tuple-element.44.base_ref, f32[512,128]{1,0:T(8,128)S(1)} %get-tuple-element.45.low_ref, bf16[544,128]{1,0:T(8,128)(2,1)S(1)} %merge.1.after_ref.s_ref, ...), custom_call_target="tpu_custom_call" | custom-call | flops 2070000000 | tf_op jit(solution)/shard_map/final/pallas_call | solution.py:264
  (20 shorter events, 0.3 us)
Async XLA Ops:
  0.6 3.2 %copy-start.5 = (f32[1024]{0:T(1024)S(1)}, f32[1024]{0:T(1024)}, u32[]{:S(2)}) copy-start(f32[1024]{0:T(1024)} %param.14) | copy-start | bytes 12292
  3.3 1.6 %collective-permute-start = (bf16[768,128]{1,0:T(8,128)(2,1)S(1)}, bf16[768,128]{1,0:T(8,128)(2,1)S(1)}, u32[]{:S(2)}, u32[]{:S(2)}) collective-permute-start(bf16[768,128]{1,0:T(8,128)(2,1)S(1)} %get-tuple-element.30.x_ref), channel_id=1, source_target_pairs={{0,1},{1,0},{2,3},{3,2},{4,5},{5,4},{6,7},{7,6},{8,9},{9,8},{10,11... | collective-permute-start | bytes 589832 | tf_op jit(solution)/shard_map/ppermute | solution.py:35
  4.9 8.2 %collective-permute-start.1 = (bf16[768,128]{1,0:T(8,128)(2,1)S(1)}, bf16[768,128]{1,0:T(8,128)(2,1)S(1)}, u32[]{:S(2)}, u32[]{:S(2)}) collective-permute-start(bf16[768,128]{1,0:T(8,128)(2,1)S(1)} %part_sum.1.after_ref.s_ref), channel_id=1, source_target_pairs={{0,2},{1,3},{2,0},{3,1},{4,6},{5,7},{6,4},{7,5},{8,10},{9,11},{10,... | collective-permute-start | bytes 589832 | tf_op jit(solution)/shard_map/ppermute | solution.py:35
  10.6 6.4 %collective-permute-start.3 = (bf16[512,1152]{1,0:T(8,128)(2,1)S(1)}, bf16[512,1152]{1,0:T(8,128)(2,1)S(1)}, u32[]{:S(2)}, u32[]{:S(2)}) collective-permute-start(bf16[512,1152]{1,0:T(8,128)(2,1)S(1)} %get-tuple-element.33.after_ref.diag_ref), channel_id=1, source_target_pairs={{0,1},{1,0},{2,3},{3,2},{4,5},{5,4},{6,7},{7,6},{8,9},{9,8},{10,11... | collective-permute-start | bytes 3538952 | tf_op jit(solution)/shard_map/ppermute | solution.py:35
  10.7 2.4 %copy-start.1 = (bf16[384,1024]{1,0:T(8,128)(2,1)S(1)}, bf16[384,1024]{1,0:T(8,128)(2,1)}, u32[]{:S(2)}) copy-start(bf16[384,1024]{1,0:T(8,128)(2,1)} %x_ref.1) | copy-start | bytes 2359300
  10.7 2.4 %copy-start.2 = (bf16[384,1024]{1,0:T(8,128)(2,1)S(1)}, bf16[384,1024]{1,0:T(8,128)(2,1)}, u32[]{:S(2)}) copy-start(bf16[384,1024]{1,0:T(8,128)(2,1)} %v_ref.1) | copy-start | bytes 2359300
  13.6 5.3 %collective-permute-start.2 = (bf16[512,128]{1,0:T(8,128)(2,1)S(1)}, bf16[512,128]{1,0:T(8,128)(2,1)S(1)}, u32[]{:S(2)}, u32[]{:S(2)}) collective-permute-start(bf16[512,128]{1,0:T(8,128)(2,1)S(1)} %get-tuple-element.35.after_ref), channel_id=1, source_target_pairs={{0,4},{4,0},{8,12},{12,8},{1,5},{5,1},{9,13},{13,9},{2,6},{6,2},{1... | collective-permute-start | bytes 393224 | tf_op jit(solution)/shard_map/ppermute | solution.py:35
  15.5 6.1 %collective-permute-start.5 = (bf16[512,128]{1,0:T(8,128)(2,1)S(1)}, bf16[512,128]{1,0:T(8,128)(2,1)S(1)}, u32[]{:S(2)}, u32[]{:S(2)}) collective-permute-start(bf16[512,128]{1,0:T(8,128)(2,1)S(1)} %get-tuple-element.37), channel_id=1, source_target_pairs={{0,16},{16,0},{1,17},{17,1},{2,18},{18,2},{3,19},{19,3},{4,20},{20... | collective-permute-start | bytes 393224 | tf_op jit(solution)/shard_map/ppermute | solution.py:35
  17.3 26.9 %collective-permute-start.8 = (bf16[512,1152]{1,0:T(8,128)(2,1)S(1)}, bf16[512,1152]{1,0:T(8,128)(2,1)S(1)}, u32[]{:S(2)}, u32[]{:S(2)}) collective-permute-start(bf16[512,1152]{1,0:T(8,128)(2,1)S(1)} %far.1.rest_0_.far_ref), channel_id=1, source_target_pairs={{0,2},{1,3},{2,0},{3,1},{4,6},{5,7},{6,4},{7,5},{8,10},{9,11},{10,... | collective-permute-start | bytes 3538952 | tf_op jit(solution)/shard_map/ppermute | solution.py:35
  18.9 9.3 %collective-permute-start.4 = (bf16[512,128]{1,0:T(8,128)(2,1)S(1)}, bf16[512,128]{1,0:T(8,128)(2,1)S(1)}, u32[]{:S(2)}, u32[]{:S(2)}) collective-permute-start(bf16[512,128]{1,0:T(8,128)(2,1)S(1)} %step_a0.1.rest_0_.mine_ref), channel_id=1, source_target_pairs={{0,8},{4,12},{8,0},{12,4},{1,9},{5,13},{9,1},{13,5},{2,10},{6,14},... | collective-permute-start | bytes 393224 | tf_op jit(solution)/shard_map/ppermute | solution.py:35
  21.6 5.8 %collective-permute-start.6 = (bf16[512,128]{1,0:T(8,128)(2,1)S(1)}, bf16[512,128]{1,0:T(8,128)(2,1)S(1)}, u32[]{:S(2)}, u32[]{:S(2)}) collective-permute-start(bf16[512,128]{1,0:T(8,128)(2,1)S(1)} %step_b1.1.after_ref.mine_ref.rest_0_), channel_id=1, source_target_pairs={{0,4},{4,0},{8,12},{12,8},{1,5},{5,1},{9,13},{13,9},{2,6},{6,2},{1... | collective-permute-start | bytes 393224 | tf_op jit(solution)/shard_map/ppermute | solution.py:35
  27.4 7.3 %collective-permute-start.10 = (bf16[512,128]{1,0:T(8,128)(2,1)S(1)}, bf16[512,128]{1,0:T(8,128)(2,1)S(1)}, u32[]{:S(2)}, u32[]{:S(2)}) collective-permute-start(bf16[512,128]{1,0:T(8,128)(2,1)S(1)} %get-tuple-element.38.rest_0_.mine_ref), channel_id=1, source_target_pairs={{0,8},{4,12},{8,0},{12,4},{1,9},{5,13},{9,1},{13,5},{2,10},{6,14},... | collective-permute-start | bytes 393224 | tf_op jit(solution)/shard_map/ppermute | solution.py:35
  28.3 5.4 %collective-permute-start.9 = (bf16[512,128]{1,0:T(8,128)(2,1)S(1)}, bf16[512,128]{1,0:T(8,128)(2,1)S(1)}, u32[]{:S(2)}, u32[]{:S(2)}) collective-permute-start(bf16[512,128]{1,0:T(8,128)(2,1)S(1)} %step_a4.1.after_ref.mine_ref), channel_id=1, source_target_pairs={{0,16},{16,0},{1,17},{17,1},{2,18},{18,2},{3,19},{19,3},{4,20},{20... | collective-permute-start | bytes 393224 | tf_op jit(solution)/shard_map/ppermute | solution.py:35
  29.9 2.7 %copy-start = (s32[256]{0:T(256)S(1)}, s32[256]{0:T(256)}, u32[]{:S(2)}) copy-start(s32[256]{0:T(256)} %param.15) | copy-start | bytes 3076
  29.9 14.3 %collective-permute-start.7 = (bf16[512,1024]{1,0:T(8,128)(2,1)S(1)}, bf16[512,1024]{1,0:T(8,128)(2,1)S(1)}, u32[]{:S(2)}, u32[]{:S(2)}) collective-permute-start(bf16[512,1024]{1,0:T(8,128)(2,1)S(1)} %get-tuple-element.39), channel_id=1, source_target_pairs={{0,1},{1,0},{2,3},{3,2},{4,5},{5,4},{6,7},{7,6},{8,9},{9,8},{10,11... | collective-permute-start | bytes 3145736 | tf_op jit(solution)/shard_map/ppermute | solution.py:35
  34.8 5.0 %collective-permute-start.12 = (bf16[512,128]{1,0:T(8,128)(2,1)S(1)}, bf16[512,128]{1,0:T(8,128)(2,1)S(1)}, u32[]{:S(2)}, u32[]{:S(2)}) collective-permute-start(bf16[512,128]{1,0:T(8,128)(2,1)S(1)} %step_b8.1.mine_b.after_ref), channel_id=1, source_target_pairs={{0,16},{16,0},{1,17},{17,1},{2,18},{18,2},{3,19},{19,3},{4,20},{20... | collective-permute-start | bytes 393224 | tf_op jit(solution)/shard_map/ppermute | solution.py:35
  35.7 5.0 %collective-permute-start.11 = (bf16[512,128]{1,0:T(8,128)(2,1)S(1)}, bf16[512,128]{1,0:T(8,128)(2,1)S(1)}, u32[]{:S(2)}, u32[]{:S(2)}) collective-permute-start(bf16[512,128]{1,0:T(8,128)(2,1)S(1)} %step_a7.1.rest_0_.mine_a), channel_id=1, source_target_pairs={{0,4},{4,0},{8,12},{12,8},{1,5},{5,1},{9,13},{13,9},{2,6},{6,2},{1... | collective-permute-start | bytes 393224 | tf_op jit(solution)/shard_map/ppermute | solution.py:35
  41.0 1.4 %collective-permute-start.13 = (bf16[544,128]{1,0:T(8,128)(2,1)S(1)}, bf16[544,128]{1,0:T(8,128)(2,1)S(1)}, u32[]{:S(2)}, u32[]{:S(2)}) collective-permute-start(bf16[544,128]{1,0:T(8,128)(2,1)S(1)} %get-tuple-element.43.a_ref), channel_id=1, source_target_pairs={{0,1},{1,0},{2,3},{3,2},{4,5},{5,4},{6,7},{7,6},{8,9},{9,8},{10,11... | collective-permute-start | bytes 417800 | tf_op jit(solution)/shard_map/ppermute | solution.py:35
  42.5 5.8 %collective-permute-start.14 = (bf16[544,128]{1,0:T(8,128)(2,1)S(1)}, bf16[544,128]{1,0:T(8,128)(2,1)S(1)}, u32[]{:S(2)}, u32[]{:S(2)}) collective-permute-start(bf16[544,128]{1,0:T(8,128)(2,1)S(1)} %merge.1.after_ref.s_ref), channel_id=1, source_target_pairs={{0,2},{1,3},{2,0},{3,1},{4,6},{5,7},{6,4},{7,5},{8,10},{9,11},{10,... | collective-permute-start | bytes 417800 | tf_op jit(solution)/shard_map/ppermute | solution.py:35
  44.2 4.1 %copy-start.3 = (f32[1024,128]{1,0:T(8,128)S(1)}, f32[1024,128]{1,0:T(8,128)}, u32[]{:S(2)}) copy-start(f32[1024,128]{1,0:T(8,128)} %a_ref.1) | copy-start | bytes 1572868
  44.2 4.1 %copy-start.4 = (f32[128,1024]{1,0:T(8,128)S(1)}, f32[128,1024]{1,0:T(8,128)}, u32[]{:S(2)}) copy-start(f32[128,1024]{1,0:T(8,128)} %b_ref.1) | copy-start | bytes 1572868

commit v13 on v12

--- a/solution.py
+++ b/solution.py
@@ -59,25 +59,20 @@
     return [slice(i, i + LANES) for i in range(0, count, LANES)]
 
 
-def rank_kernel(x_hbm, v_hbm, a_hbm, b_hbm, h_hbm, out_ref, a16_ref, h_ref, x_ref, v_ref, a_ref, b_ref, sems):
-    count = x_ref.shape[0]
-    half = count // 2
-    copies = fetch(
-        (a_hbm, x_hbm, b_hbm, v_hbm.at[:half], v_hbm.at[half:], h_hbm),
-        (a_ref, x_ref, b_ref, v_ref.at[:half], v_ref.at[half:], h_ref),
-        sems,
-    )
+def rank_v_kernel(x_hbm, v_hbm, a_hbm, b_hbm, h_hbm, out_ref, x_ref, v_ref, a16_ref, h_ref, a_ref, b_ref, sems):
+    copies = fetch((v_hbm, b_hbm, x_hbm, a_hbm, h_hbm), (v_ref, b_ref, x_ref, a_ref, h_ref), sems)
+    copies[1].wait()
+    b16 = b_ref[...].astype(BF)
     copies[0].wait()
+    out_ref[...] = dot(v_ref[...], b16, ((1,), (1,))).astype(BF)
+    copies[3].wait()
     a16_ref[...] = a_ref[...].astype(BF)
-    copies[1].wait()
-    out_ref[:count] = dot(x_ref[...], a16_ref[...]).astype(BF)
     copies[2].wait()
-    b16 = b_ref[...].astype(BF)
-    copies[3].wait()
-    out_ref[count : count + half] = dot(v_ref[:half], b16, ((1,), (1,))).astype(BF)
     copies[4].wait()
-    out_ref[count + half :] = dot(v_ref[half:], b16, ((1,), (1,))).astype(BF)
-    copies[5].wait()
+
+
+def rank_u_kernel(x_ref, a16_ref, out_ref):
+    out_ref[...] = dot(x_ref[...], a16_ref[...]).astype(BF)
 
 
 def weight_blocks(peers, w_hbm, w_ref):
@@ -162,18 +157,21 @@
     out_ref[other] = got_ref[...]
 
 
-def grad_kernel(axes, x_ref, v_ref, s_ref, r_ref, after_ref, keep_a, send_a, keep_b, send_b):
-    count, width = x_ref.shape
+def grad_a_kernel(way, x_ref, s_ref, r_ref, after_ref, keep_ref, send_ref):
     low = (s_ref[...].astype(F32) + r_ref[...].astype(F32)).astype(BF)
-    mine, other = halves(*axes[0], width // 2)
-    send_a[...] = (SCALE * dot(x_ref[:, other], low[count:], ((0,), (0,)))).astype(BF)
-    keep_a[...] = SCALE * dot(x_ref[:, mine], low[count:], ((0,), (0,)))
-    mine, other = halves(*axes[1], width // 2)
-    sent = (SCALE * dot(low[:count], v_ref[:, other], ((0,), (0,)))).astype(BF)
-    kept = SCALE * dot(low[:count], v_ref[:, mine], ((0,), (0,)))
-    for b in blocks_of(width // 2):
-        send_b[b] = sent[:, b]
-        keep_b[b] = kept[:, b]
+    mine, other = halves(*way, x_ref.shape[1] // 2)
+    send_ref[...] = (SCALE * dot(x_ref[:, other], low, ((0,), (0,)))).astype(BF)
+    keep_ref[...] = SCALE * dot(x_ref[:, mine], low, ((0,), (0,)))
+
+
+def grad_b_kernel(way, v_ref, s_ref, r_ref, after_ref, keep_ref, send_ref):
+    low = (s_ref[...].astype(F32) + r_ref[...].astype(F32)).astype(BF)
+    mine, other = halves(*way, v_ref.shape[1] // 2)
+    sent = (SCALE * dot(low, v_ref[:, other], ((0,), (0,)))).astype(BF)
+    kept = SCALE * dot(low, v_ref[:, mine], ((0,), (0,)))
+    for b in blocks_of(v_ref.shape[1] // 2):
+        send_ref[b] = sent[:, b]
+        keep_ref[b] = kept[:, b]
 
 
 def sum_kernel(keep_ref, got_ref, out_ref):
@@ -193,23 +191,20 @@
     return jnp.broadcast_to(jnp.sum(x * x), (8, LANES))
 
 
-def own_kernel(way, hg_ref, sums_ref, mine_a, mine_b, after_ref, low_ref, sums_out):
-    mine, _ = halves(*way, mine_a.shape[0])
-    low_ref[...] = dot(hg_ref[:, mine], mine_a[...])
-    sums_out[0] = sums_ref[...]
-    sums_out[1] = square_sum(mine_a)
-    sums_out[2] = square_sum(mine_b)
-
-
-def low_kernel(way_a, way_b, hg_ref, low_ref, sums_ref, mine_a, got_a, mine_b, got_b, pack_ref, ga_ref, gb_ref):
-    join(*way_a, mine_a, got_a, ga_ref)
-    count = hg_ref.shape[0]
-    _, other = halves(*way_a, mine_a.shape[0])
-    pack_ref[:count] = (low_ref[...] + dot(hg_ref[:, other], got_a[...])).astype(BF)
-    join(*way_b, mine_b, got_b, gb_ref)
-    squares = (sums_ref[1] + square_sum(got_a)) + (sums_ref[2] + square_sum(got_b))
+def update_kernel(way, hg_ref, mine_a, got_a, mine_b, low_ref, ga_ref, squares_ref):
+    join(*way, mine_a, got_a, ga_ref)
+    low_ref[...] = dot(hg_ref[...], ga_ref[...]).astype(BF)
+    squares_ref[0] = square_sum(mine_a) + square_sum(got_a)
+    squares_ref[1] = square_sum(mine_b)
+
+
+def pack_kernel(way, low_ref, sums_ref, squares_ref, mine_b, got_b, pack_ref, gb_ref):
+    count = low_ref.shape[0]
+    pack_ref[:count] = low_ref[...]
     row = lax.broadcasted_iota(jnp.int32, (8, LANES), 0)
-    pack_ref[count:] = split_terms(jnp.where(row == 7, squares, sums_ref[0]))
+    squares = squares_ref[0] + (squares_ref[1] + square_sum(got_b))
+    pack_ref[count:] = split_terms(jnp.where(row == 7, squares, sums_ref[...]))
+    join(*way, mine_b, got_b, gb_ref)
 
 
 def base_kernel(mine_ref, near_ref, far_ref, far_got, after_ref, base_ref, low_ref):
@@ -256,7 +251,9 @@
     return pltpu.with_memory_space_constraint(x, pltpu.HBM)
 
 
-WEIGHTS = {"rank": 2.4, "prep": 0.6, "query_diag": 40.0, "query_distant": 0.01, "query_beside": 1.0, "query_close": 0.5, "grads": 40.0, "final": 1.8}
+WEIGHTS = {
+    "rank_v": 2.4, "prep": 0.6, "query_diag": 40.0, "query_beside": 1.0, "query_close": 0.5, "grad_b": 40.0, "final": 1.8,
+}
 FLOPS_PER_WEIGHT = 1_150_000_000
 
 
@@ -313,18 +310,20 @@
         vmem = lambda n, dtype=F32: pltpu.VMEM((n, rank), dtype)
 
         tall = shape((count, width), BF)
-        part, half_a, hidden = call(
-            rank_kernel,
-            [shape((2 * tokens, rank), BF), shape(factor_a.shape, BF), tall],
+        low_shape = shape((tokens, rank), BF)
+        part_v, inputs, cotangent, half_a, hidden = call(
+            rank_v_kernel,
+            [low_shape, shape(train_inputs.shape, BF), shape(train_inputs.shape, BF), shape(factor_a.shape, BF), tall],
             [HBM] * 5,
             tuple(
                 map(keep_hbm, (train_inputs, train_cotangent, factor_a, factor_b, incoming.reshape(count, width)))
             ),
-            "rank",
-            [pltpu.VMEM(train_inputs.shape, BF), pltpu.VMEM(train_inputs.shape, BF),
-             pltpu.VMEM(factor_a.shape, F32), pltpu.VMEM(factor_b.shape, F32), dma(6)],
-        )
-        part_got = swap(part, "tp", n_tp, 1)
+            "rank_v",
+            [pltpu.VMEM(factor_a.shape, F32), pltpu.VMEM(factor_b.shape, F32), dma(5)],
+        )
+        got_v = swap(part_v, "tp", n_tp, 1)
+        part_u = call(rank_u_kernel, low_shape, [VMEM] * 2, (inputs, half_a), "rank_u")
+        got_u = swap(part_u, "tp", n_tp, 1)
         cut = 512
         wide = shape((count, width + rank), BF)
         gained, low, sums = call(
@@ -334,8 +333,10 @@
             (hidden, norm_gain[None, :], half_a),
             "prep",
         )
-        part_sum = call(part_kernel, shape(part.shape, BF), [VMEM] * 2 + [ANY], (part, part_got, low), "part_sum")
-        part_far = swap(part_sum, "tp", n_tp, 2)
+        low_v = call(part_kernel, low_shape, [VMEM] * 2 + [ANY], (part_v, got_v, low), "low_v")
+        far_v = swap(low_v, "tp", n_tp, 2)
+        low_u = call(part_kernel, low_shape, [VMEM] * 2 + [ANY], (part_u, got_u, low_v), "low_u")
+        far_u = swap(low_u, "tp", n_tp, 2)
 
         def query(peers, outs, after, name):
             blocks = len(peers) * width // cut
@@ -353,22 +354,29 @@
             diag_kernel,
             [wide, shape((per, width, cut), BF)],
             [VMEM, HBM, VMEM, ANY],
-            (gained, keep_hbm(base_weight), low, part_sum),
+            (gained, keep_hbm(base_weight), low, low_u),
             "query_diag",
             [pltpu.VMEM((per, width, cut), BF), dma(2 * per)],
         )
         diag_got = swap(diag, "tp", n_tp, 1)
-        distant = call(distant_kernel, tall, [VMEM, VMEM, ANY], (gained, columns, diag), "query_distant")
 
         half = width // 2
-        keep_a, send_a, keep_b, send_b = call(
-            functools.partial(grad_kernel, (path_a[0], path_b[0])),
-            [shape((half, rank), F32), shape((half, rank), BF)] * 2,
-            [VMEM] * 4 + [ANY],
-            (train_inputs, train_cotangent, part_sum, part_far, distant),
-            "grads",
-        )
-        far = call(far_kernel, wide, [VMEM] * 3 + [ANY], (distant, diag, diag_got, send_a), "far")
+        keep_a, send_a = call(
+            functools.partial(grad_a_kernel, path_a[0]),
+            [shape((half, rank), F32), shape((half, rank), BF)],
+            [VMEM] * 3 + [ANY],
+            (inputs, low_v, far_v, diag),
+            "grad_a",
+        )
+        keep_b, send_b = call(
+            functools.partial(grad_b_kernel, path_b[0]),
+            [shape((half, rank), F32), shape((half, rank), BF)],
+            [VMEM] * 3 + [ANY],
+            (cotangent, low_u, far_u, send_a),
+            "grad_b",
+        )
+        distant = call(distant_kernel, tall, [VMEM, VMEM, ANY], (gained, columns, send_b), "query_distant")
+        far = call(far_kernel, wide, [VMEM] * 3 + [ANY], (distant, diag, diag_got, send_b), "far")
         far_got = swap(far, "tp", n_tp, 2)
 
         def step(mine, send, way, after, passed, name):
@@ -403,19 +411,19 @@
             else:
                 (close,) = query((0,), [tall], after, "close")
                 after = close
-        own_low, own_sums = call(
-            functools.partial(own_kernel, path_a[-1]),
-            [shape((count, rank), F32), shape((3, 8, LANES), F32)],
-            [VMEM] * 4 + [ANY],
-            (gained, sums, mine_a, mine_b, after),
-            "own_half",
-        )
-        step_pack, grad_a, grad_b = call(
-            functools.partial(low_kernel, path_a[-1], path_b[-1]),
-            [shape((count + EXTRA, rank), BF), shape((width, rank), BF), shape((width, rank), BF)],
-            [VMEM] * 7,
-            (gained, own_low, own_sums, mine_a, cross(mine_a, *path_a[-1]), mine_b, cross(mine_b, *path_b[-1])),
-            "low_rank",
+        step_low, grad_a, squares = call(
+            functools.partial(update_kernel, path_a[-1]),
+            [shape((count, rank), BF), shape((width, rank), BF), shape((2, 8, LANES), F32)],
+            [VMEM] * 4,
+            (gained, mine_a, cross(mine_a, *path_a[-1]), mine_b),
+            "update",
+        )
+        step_pack, grad_b = call(
+            functools.partial(pack_kernel, path_b[-1]),
+            [shape((count + EXTRA, rank), BF), shape((width, rank), BF)],
+            [VMEM] * 5,
+            (step_low, sums, squares, mine_b, cross(mine_b, *path_b[-1])),
+            "pack",
         )
         step_got = swap(step_pack, "tp", n_tp, 1)
         step_sum = call(merge_kernel, shape((count + EXTRA, rank), BF), [VMEM] * 2, (step_pack, step_got), "merge")

time: 50.4 us -> 50 us (level)
  starting transfers between devices: 17.9 us -> 15.5 us
  waiting for transfers between devices: 13.4 us -> 15.4 us
    ppermute x15 -> x17, starting transfers between devices: 17.9 us -> 15.5 us  [swap(): return lax.ppermute(x, axis, [(i, i ^ k) for i in range(n)])]
    ppermute x15 -> x17, waiting for transfers between devices: 13.4 us -> 15.4 us  [swap(): return lax.ppermute(x, axis, [(i, i ^ k) for i in range(n)])]
    pallas_call x21 -> x24, Pallas kernels: 16.7 us -> 16.7 us  [call(): pl.pallas_call(kernel, out_shape=outs, in_specs=in_specs, out_specs=out_s...]
  transfers between devices with their start and end apart: 15 -> 17, of which waited for: 8 -> 9; matrix products, arithmetic and copies ran while one was open for 3% -> 3% of each run, Pallas kernels for 24% -> 25%
where the time goes in v13:
time: 50 us; the launch traced here: 49.8 us
  Pallas kernels  16.7 us (33%)
  starting transfers between devices  15.5 us (31%)
  waiting for transfers between devices  15.4 us (31%)
  other arithmetic  1.28 us (3%)
  between operations  0.88 us (2%)
    pallas_call x24, Pallas kernels, call(): pl.pallas_call(kernel, out_shape=outs, in_specs=in_specs, out_specs=out_s...  16.7 us
    ppermute x17, starting transfers between devices, swap(): return lax.ppermute(x, axis, [(i, i ^ k) for i in range(n)])  15.5 us
    ppermute x17, waiting for transfers between devices, swap(): return lax.ppermute(x, axis, [(i, i ^ k) for i in range(n)])  15.4 us
  transfers between devices with their start and end apart: 17, of which 9 were waited for; matrix products, arithmetic and copies ran while one was open for 3% of the time, Pallas kernels for 25%

profile of v13, /device:TPU:0, one launch (start us, length us, event | category | flops | bytes accessed | tf_op | source)
XLA Modules:
  0.0 49.8 jit_solution(3250248854541582700)
XLA Ops:
  0.6 2.1 %rank_v.1 = (bf16[384,128]{1,0:T(8,128)(2,1)S(1)}, bf16[384,1024]{1,0:T(8,128)(2,1)S(1)}, bf16[384,1024]{1,0:T(8,128)(2,1)S(1)}, bf16[1024,128]{1,0:T(8,128)(2,1)S(1)}, bf16[512,1024]{1,0:T(8,128)(2,1)S(1)}) custom-call(bf16[384,1024]{1,0:T(8,128)(2,1)} %x_hbm.1, bf16[384,1024]{1,0:T(8,128)(2,1)} %v_hbm.1, f32[1024,128]{1,0:T(8,128)} %a_ref.1, ...), custom_call_target="tpu_custom_call" | custom-call | flops 2760000000 | tf_op jit(solution)/shard_map/rank_v/pallas_call | solution.py:261
  2.7 0.5 %collective-permute-start = (bf16[384,128]{1,0:T(8,128)(2,1)S(1)}, bf16[384,128]{1,0:T(8,128)(2,1)S(1)}, u32[]{:S(2)}, u32[]{:S(2)}) collective-permute-start(bf16[384,128]{1,0:T(8,128)(2,1)S(1)} %get-tuple-element.33.x_ref), channel_id=1, source_target_pairs={{0,1},{1,0},{2,3},{3,2},{4,5},{5,4},{6,7},{7,6},{8,9},{9,8},{10,11... | collective-permute-start | bytes 294920 | tf_op jit(solution)/shard_map/ppermute | solution.py:35
  3.2 0.4 rank_u.1.x_ref
  3.6 0.1 collective-permute-start.2
  3.7 0.6 %prep.1 = (bf16[512,1024]{1,0:T(8,128)(2,1)S(1)}, bf16[512,128]{1,0:T(8,128)(2,1)S(1)}, f32[8,128]{1,0:T(8,128)S(1)}) custom-call(bf16[512,1024]{1,0:T(8,128)(2,1)S(1)} %get-tuple-element.29.h_ref, f32[1,1024]{1,0:T(1,128)S(1)} %bitcast.8, bf16[1024,128]{1,0:T(8,128)(2,1)S(1)} %get-tuple-element.30.a16_ref), custom_call_target="tpu_custom_call" | custom-call | flops 690000000 | tf_op jit(solution)/shard_map/prep/pallas_call | solution.py:261
  4.3 0.0 collective-permute-done.got_ref
  4.3 3.0 %collective-permute-start.1 = (bf16[384,128]{1,0:T(8,128)(2,1)S(1)}, bf16[384,128]{1,0:T(8,128)(2,1)S(1)}, u32[]{:S(2)}, u32[]{:S(2)}) collective-permute-start(bf16[384,128]{1,0:T(8,128)(2,1)S(1)} %low_v.1.after_ref.s_ref), channel_id=1, source_target_pairs={{0,2},{1,3},{2,0},{3,1},{4,6},{5,7},{6,4},{7,5},{8,10},{9,11},{10,... | collective-permute-start | bytes 294920 | tf_op jit(solution)/shard_map/ppermute | solution.py:35
  7.4 0.0 collective-permute-done.2.got_ref
  7.4 0.3 collective-permute-start.4
  7.7 2.7 %query_diag.1 = (bf16[512,1152]{1,0:T(8,128)(2,1)S(1)}, bf16[2,1024,512]{2,1,0:T(8,128)(2,1)S(1)}) custom-call(bf16[512,1024]{1,0:T(8,128)(2,1)S(1)} %get-tuple-element.31.hg_ref, bf16[1024,4096]{1,0:T(8,128)(2,1)} %w_hbm.5, bf16[512,128]{1,0:T(8,128)(2,1)S(1)} %get-tuple-element.34.after_ref.low_ref, bf16[384,128]{1,0:T(8,128)(2,1)S(1)} %low_u.1.after_ref.s_ref), custom_call_target="tpu_custom_call" | custom-call | flops 46000001024 | tf_op jit(solution)/shard_map/query_diag/pallas_call | solution.py:261
  10.5 0.1 collective-permute-start.5
  10.6 0.3 collective-permute-done.1.r_ref
  10.9 0.4 grad_a.1
  11.3 2.1 %collective-permute-start.3 = (bf16[512,128]{1,0:T(8,128)(2,1)S(1)}, bf16[512,128]{1,0:T(8,128)(2,1)S(1)}, u32[]{:S(2)}, u32[]{:S(2)}) collective-permute-start(bf16[512,128]{1,0:T(8,128)(2,1)S(1)} %get-tuple-element.37.after_ref), channel_id=1, source_target_pairs={{0,4},{4,0},{8,12},{12,8},{1,5},{5,1},{9,13},{13,9},{2,6},{6,2},{1... | collective-permute-start | bytes 393224 | tf_op jit(solution)/shard_map/ppermute | solution.py:35
  13.4 0.0 collective-permute-done.4.r_ref
  13.4 0.3 grad_b.1
  13.7 1.6 %collective-permute-start.7 = (bf16[512,128]{1,0:T(8,128)(2,1)S(1)}, bf16[512,128]{1,0:T(8,128)(2,1)S(1)}, u32[]{:S(2)}, u32[]{:S(2)}) collective-permute-start(bf16[512,128]{1,0:T(8,128)(2,1)S(1)} %get-tuple-element.40.after_ref), channel_id=1, source_target_pairs={{0,16},{16,0},{1,17},{17,1},{2,18},{18,2},{3,19},{19,3},{4,20},{20... | collective-permute-start | bytes 393224 | tf_op jit(solution)/shard_map/ppermute | solution.py:35
  15.3 1.2 %query_distant.1.mine_ref = bf16[512,1024]{1,0:T(8,128)(2,1)S(1)} custom-call(bf16[512,1024]{1,0:T(8,128)(2,1)S(1)} %get-tuple-element.31.hg_ref, bf16[2,1024,512]{2,1,0:T(8,128)(2,1)S(1)} %get-tuple-element.38.w_ref, bf16[512,128]{1,0:T(8,128)(2,1)S(1)} %get-tuple-element.40.after_ref), custom_call_target="tpu_custom_call" | custom-call | flops 11500000 | tf_op jit(solution)/shard_map/query_distant/pallas_call | solution.py:261
  16.6 0.3 far.1.rest_0_.far_ref
  16.9 1.8 %collective-permute-start.10 = (bf16[512,1152]{1,0:T(8,128)(2,1)S(1)}, bf16[512,1152]{1,0:T(8,128)(2,1)S(1)}, u32[]{:S(2)}, u32[]{:S(2)}) collective-permute-start(bf16[512,1152]{1,0:T(8,128)(2,1)S(1)} %far.1.rest_0_.far_ref), channel_id=1, source_target_pairs={{0,2},{1,3},{2,0},{3,1},{4,6},{5,7},{6,4},{7,5},{8,10},{9,11},{10,... | collective-permute-start | bytes 3538952 | tf_op jit(solution)/shard_map/ppermute | solution.py:35
  18.6 0.0 collective-permute-done.3.got_ref
  18.6 2.7 %collective-permute-start.6 = (bf16[512,128]{1,0:T(8,128)(2,1)S(1)}, bf16[512,128]{1,0:T(8,128)(2,1)S(1)}, u32[]{:S(2)}, u32[]{:S(2)}) collective-permute-start(bf16[512,128]{1,0:T(8,128)(2,1)S(1)} %step_a0.1.rest_0_.mine_ref), channel_id=1, source_target_pairs={{0,8},{4,12},{8,0},{12,4},{1,9},{5,13},{9,1},{13,5},{2,10},{6,14},... | collective-permute-start | bytes 393224 | tf_op jit(solution)/shard_map/ppermute | solution.py:35
  21.3 0.8 %collective-permute-start.8 = (bf16[512,128]{1,0:T(8,128)(2,1)S(1)}, bf16[512,128]{1,0:T(8,128)(2,1)S(1)}, u32[]{:S(2)}, u32[]{:S(2)}) collective-permute-start(bf16[512,128]{1,0:T(8,128)(2,1)S(1)} %step_b1.1.after_ref.mine_ref.rest_0_), channel_id=1, source_target_pairs={{0,4},{4,0},{8,12},{12,8},{1,5},{5,1},{9,13},{13,9},{2,6},{6,2},{1... | collective-permute-start | bytes 393224 | tf_op jit(solution)/shard_map/ppermute | solution.py:35
  22.1 2.7 %query_beside.1.rest_1_ = bf16[512,1024]{1,0:T(8,128)(2,1)S(1)} custom-call(bf16[512,1024]{1,0:T(8,128)(2,1)S(1)} %get-tuple-element.31.hg_ref, bf16[1024,4096]{1,0:T(8,128)(2,1)} %w_hbm.5, bf16[512,128]{1,0:T(8,128)(2,1)S(1)} %step_b1.1.after_ref.mine_ref.rest_0_), custom_call_target="tpu_custom_call" | custom-call | flops 1150000000 | tf_op jit(solution)/shard_map/query_beside/pallas_call | solution.py:261
  24.8 3.2 %collective-permute-done.8.got_ref = bf16[512,128]{1,0:T(8,128)(2,1)S(1)} collective-permute-done((bf16[512,128]{1,0:T(8,128)(2,1)S(1)}, bf16[512,128]{1,0:T(8,128)(2,1)S(1)}, u32[]{:S(2)}, u32[]{:S(2)}) %collective-permute-start.8) | collective-permute-done | bytes 131104 | tf_op jit(solution)/shard_map/ppermute | solution.py:35
  28.0 0.1 collective-permute-start.13
  28.2 0.6 %collective-permute-start.11 = (bf16[512,128]{1,0:T(8,128)(2,1)S(1)}, bf16[512,128]{1,0:T(8,128)(2,1)S(1)}, u32[]{:S(2)}, u32[]{:S(2)}) collective-permute-start(bf16[512,128]{1,0:T(8,128)(2,1)S(1)} %step_a4.1.after_ref.mine_ref), channel_id=1, source_target_pairs={{0,16},{16,0},{1,17},{17,1},{2,18},{18,2},{3,19},{19,3},{4,20},{20... | collective-permute-start | bytes 393224 | tf_op jit(solution)/shard_map/ppermute | solution.py:35
  28.8 2.7 %query_close.1.after_ref.mine_ref = bf16[512,1024]{1,0:T(8,128)(2,1)S(1)} custom-call(bf16[512,1024]{1,0:T(8,128)(2,1)S(1)} %get-tuple-element.31.hg_ref, bf16[1024,4096]{1,0:T(8,128)(2,1)} %w_hbm.5, bf16[512,128]{1,0:T(8,128)(2,1)S(1)} %step_a4.1.after_ref.mine_ref), custom_call_target="tpu_custom_call" | custom-call | flops 575000000 | tf_op jit(solution)/shard_map/query_close/pallas_call | solution.py:261
  31.5 1.0 %multiply_cosine_fusion.1 = (f32[256,64]{1,0:T(8,128)S(1)}, f32[256,64]{1,0:T(8,128)S(1)}, f32[256,64]{1,0:T(8,128)S(1)}, f32[256,64]{1,0:T(8,128)S(1)}, f32[256,64]{1,0:T(8,128)S(1)}, /*index=5*/f32[256,64]{1,0:T(8,128)S(1)}) fusion(f32[64]{0:T(128)S(1)} %multiply_power_fusion, f32[256]{0:T(256)S(1)} %bitcast.6, f32[256]{0:T(256)S(1)} %broadcast_add_fusion), kind=kLoop, calls=%fused_computation.4 | loop fusion | flops 65536 | bytes 395520 | tf_op jit(solution)/shard_map/cos | solution.py:282
  32.5 0.1 maximum_maximum_fusion.rest_0_.sin_ref
  32.6 0.6 %collective-permute-done.11.got_ref = bf16[512,128]{1,0:T(8,128)(2,1)S(1)} collective-permute-done((bf16[512,128]{1,0:T(8,128)(2,1)S(1)}, bf16[512,128]{1,0:T(8,128)(2,1)S(1)}, u32[]{:S(2)}, u32[]{:S(2)}) %collective-permute-start.11) | collective-permute-done | bytes 131104 | tf_op jit(solution)/shard_map/ppermute | solution.py:35
  33.2 1.0 %collective-permute-start.12 = (bf16[512,128]{1,0:T(8,128)(2,1)S(1)}, bf16[512,128]{1,0:T(8,128)(2,1)S(1)}, u32[]{:S(2)}, u32[]{:S(2)}) collective-permute-start(bf16[512,128]{1,0:T(8,128)(2,1)S(1)} %step_a7.1.rest_0_.mine_a), channel_id=1, source_target_pairs={{0,4},{4,0},{8,12},{12,8},{1,5},{5,1},{9,13},{13,9},{2,6},{6,2},{1... | collective-permute-start | bytes 393224 | tf_op jit(solution)/shard_map/ppermute | solution.py:35
  34.2 1.0 %collective-permute-done.13.got_ref = bf16[512,128]{1,0:T(8,128)(2,1)S(1)} collective-permute-done((bf16[512,128]{1,0:T(8,128)(2,1)S(1)}, bf16[512,128]{1,0:T(8,128)(2,1)S(1)}, u32[]{:S(2)}, u32[]{:S(2)}) %collective-permute-start.13) | collective-permute-done | bytes 131104 | tf_op jit(solution)/shard_map/ppermute | solution.py:35
  35.3 0.2 collective-permute-start.14
  35.5 3.2 %collective-permute-done.12.got_a = bf16[512,128]{1,0:T(8,128)(2,1)S(1)} collective-permute-done((bf16[512,128]{1,0:T(8,128)(2,1)S(1)}, bf16[512,128]{1,0:T(8,128)(2,1)S(1)}, u32[]{:S(2)}, u32[]{:S(2)}) %collective-permute-start.12) | collective-permute-done | bytes 131104 | tf_op jit(solution)/shard_map/ppermute | solution.py:35
  38.7 0.5 update.1
  39.1 1.2 %collective-permute-done.14.got_b = bf16[512,128]{1,0:T(8,128)(2,1)S(1)} collective-permute-done((bf16[512,128]{1,0:T(8,128)(2,1)S(1)}, bf16[512,128]{1,0:T(8,128)(2,1)S(1)}, u32[]{:S(2)}, u32[]{:S(2)}) %collective-permute-start.14) | collective-permute-done | bytes 131104 | tf_op jit(solution)/shard_map/ppermute | solution.py:35
  40.3 0.2 pack.1
  40.5 0.1 collective-permute-start.15
  40.6 1.3 %collective-permute-done.15.b_ref = bf16[544,128]{1,0:T(8,128)(2,1)S(1)} collective-permute-done((bf16[544,128]{1,0:T(8,128)(2,1)S(1)}, bf16[544,128]{1,0:T(8,128)(2,1)S(1)}, u32[]{:S(2)}, u32[]{:S(2)}) %collective-permute-start.15) | collective-permute-done | bytes 139296 | tf_op jit(solution)/shard_map/ppermute | solution.py:35
  42.0 0.7 %collective-permute-start.16 = (bf16[544,128]{1,0:T(8,128)(2,1)S(1)}, bf16[544,128]{1,0:T(8,128)(2,1)S(1)}, u32[]{:S(2)}, u32[]{:S(2)}) collective-permute-start(bf16[544,128]{1,0:T(8,128)(2,1)S(1)} %merge.1.after_ref.s_ref), channel_id=1, source_target_pairs={{0,2},{1,3},{2,0},{3,1},{4,6},{5,7},{6,4},{7,5},{8,10},{9,11},{10,... | collective-permute-start | bytes 417800 | tf_op jit(solution)/shard_map/ppermute | solution.py:35
  42.7 0.1 maximum_maximum_fusion.1.cos_ref
  42.8 0.0 copy-start.1
  42.9 0.0 copy-start.2
  42.9 1.3 %collective-permute-done.10.far_got = bf16[512,1152]{1,0:T(8,128)(2,1)S(1)} collective-permute-done((bf16[512,1152]{1,0:T(8,128)(2,1)S(1)}, bf16[512,1152]{1,0:T(8,128)(2,1)S(1)}, u32[]{:S(2)}, u32[]{:S(2)}) %collective-permute-start.10) | collective-permute-done | bytes 1179680 | tf_op jit(solution)/shard_map/ppermute | solution.py:35
  44.1 0.5 base.1
  44.6 3.2 %collective-permute-done.16.r_ref = bf16[544,128]{1,0:T(8,128)(2,1)S(1)} collective-permute-done((bf16[544,128]{1,0:T(8,128)(2,1)S(1)}, bf16[544,128]{1,0:T(8,128)(2,1)S(1)}, u32[]{:S(2)}, u32[]{:S(2)}) %collective-permute-start.16) | collective-permute-done | bytes 139296 | tf_op jit(solution)/shard_map/ppermute | solution.py:35
  47.8 2.0 %final.1 = (f32[1024,128]{1,0:T(8,128)}, f32[128,1024]{1,0:T(8,128)}, bf16[512,1024]{1,0:T(8,128)(2,1)}) custom-call(f32[512,1024]{1,0:T(8,128)S(1)} %get-tuple-element.48.base_ref, f32[512,128]{1,0:T(8,128)S(1)} %get-tuple-element.49.low_ref, bf16[544,128]{1,0:T(8,128)(2,1)S(1)} %merge.1.after_ref.s_ref, ...), custom_call_target="tpu_custom_call" | custom-call | flops 2070000000 | tf_op jit(solution)/shard_map/final/pallas_call | solution.py:261
  (23 shorter events, 0.3 us)
Async XLA Ops:
  0.6 3.1 %copy-start.3 = (f32[1024]{0:T(1024)S(1)}, f32[1024]{0:T(1024)}, u32[]{:S(2)}) copy-start(f32[1024]{0:T(1024)} %param.14) | copy-start | bytes 12292
  2.7 1.6 %collective-permute-start = (bf16[384,128]{1,0:T(8,128)(2,1)S(1)}, bf16[384,128]{1,0:T(8,128)(2,1)S(1)}, u32[]{:S(2)}, u32[]{:S(2)}) collective-permute-start(bf16[384,128]{1,0:T(8,128)(2,1)S(1)} %get-tuple-element.33.x_ref), channel_id=1, source_target_pairs={{0,1},{1,0},{2,3},{3,2},{4,5},{5,4},{6,7},{7,6},{8,9},{9,8},{10,11... | collective-permute-start | bytes 294920 | tf_op jit(solution)/shard_map/ppermute | solution.py:35
  3.6 3.8 %collective-permute-start.2 = (bf16[384,128]{1,0:T(8,128)(2,1)S(1)}, bf16[384,128]{1,0:T(8,128)(2,1)S(1)}, u32[]{:S(2)}, u32[]{:S(2)}) collective-permute-start(bf16[384,128]{1,0:T(8,128)(2,1)S(1)} %rank_u.1.x_ref), channel_id=1, source_target_pairs={{0,1},{1,0},{2,3},{3,2},{4,5},{5,4},{6,7},{7,6},{8,9},{9,8},{10,11... | collective-permute-start | bytes 294920 | tf_op jit(solution)/shard_map/ppermute | solution.py:35
  4.3 6.6 %collective-permute-start.1 = (bf16[384,128]{1,0:T(8,128)(2,1)S(1)}, bf16[384,128]{1,0:T(8,128)(2,1)S(1)}, u32[]{:S(2)}, u32[]{:S(2)}) collective-permute-start(bf16[384,128]{1,0:T(8,128)(2,1)S(1)} %low_v.1.after_ref.s_ref), channel_id=1, source_target_pairs={{0,2},{1,3},{2,0},{3,1},{4,6},{5,7},{6,4},{7,5},{8,10},{9,11},{10,... | collective-permute-start | bytes 294920 | tf_op jit(solution)/shard_map/ppermute | solution.py:35
  7.4 6.0 %collective-permute-start.4 = (bf16[384,128]{1,0:T(8,128)(2,1)S(1)}, bf16[384,128]{1,0:T(8,128)(2,1)S(1)}, u32[]{:S(2)}, u32[]{:S(2)}) collective-permute-start(bf16[384,128]{1,0:T(8,128)(2,1)S(1)} %low_u.1.after_ref.s_ref), channel_id=1, source_target_pairs={{0,2},{1,3},{2,0},{3,1},{4,6},{5,7},{6,4},{7,5},{8,10},{9,11},{10,... | collective-permute-start | bytes 294920 | tf_op jit(solution)/shard_map/ppermute | solution.py:35
  10.5 6.1 %collective-permute-start.5 = (bf16[512,1152]{1,0:T(8,128)(2,1)S(1)}, bf16[512,1152]{1,0:T(8,128)(2,1)S(1)}, u32[]{:S(2)}, u32[]{:S(2)}) collective-permute-start(bf16[512,1152]{1,0:T(8,128)(2,1)S(1)} %get-tuple-element.35.after_ref.diag_ref), channel_id=1, source_target_pairs={{0,1},{1,0},{2,3},{3,2},{4,5},{5,4},{6,7},{7,6},{8,9},{9,8},{10,11... | collective-permute-start | bytes 3538952 | tf_op jit(solution)/shard_map/ppermute | solution.py:35
  11.3 7.3 %collective-permute-start.3 = (bf16[512,128]{1,0:T(8,128)(2,1)S(1)}, bf16[512,128]{1,0:T(8,128)(2,1)S(1)}, u32[]{:S(2)}, u32[]{:S(2)}) collective-permute-start(bf16[512,128]{1,0:T(8,128)(2,1)S(1)} %get-tuple-element.37.after_ref), channel_id=1, source_target_pairs={{0,4},{4,0},{8,12},{12,8},{1,5},{5,1},{9,13},{13,9},{2,6},{6,2},{1... | collective-permute-start | bytes 393224 | tf_op jit(solution)/shard_map/ppermute | solution.py:35
  13.7 7.6 %collective-permute-start.7 = (bf16[512,128]{1,0:T(8,128)(2,1)S(1)}, bf16[512,128]{1,0:T(8,128)(2,1)S(1)}, u32[]{:S(2)}, u32[]{:S(2)}) collective-permute-start(bf16[512,128]{1,0:T(8,128)(2,1)S(1)} %get-tuple-element.40.after_ref), channel_id=1, source_target_pairs={{0,16},{16,0},{1,17},{17,1},{2,18},{18,2},{3,19},{19,3},{4,20},{20... | collective-permute-start | bytes 393224 | tf_op jit(solution)/shard_map/ppermute | solution.py:35
  16.9 27.3 %collective-permute-start.10 = (bf16[512,1152]{1,0:T(8,128)(2,1)S(1)}, bf16[512,1152]{1,0:T(8,128)(2,1)S(1)}, u32[]{:S(2)}, u32[]{:S(2)}) collective-permute-start(bf16[512,1152]{1,0:T(8,128)(2,1)S(1)} %far.1.rest_0_.far_ref), channel_id=1, source_target_pairs={{0,2},{1,3},{2,0},{3,1},{4,6},{5,7},{6,4},{7,5},{8,10},{9,11},{10,... | collective-permute-start | bytes 3538952 | tf_op jit(solution)/shard_map/ppermute | solution.py:35
  18.6 9.5 %collective-permute-start.6 = (bf16[512,128]{1,0:T(8,128)(2,1)S(1)}, bf16[512,128]{1,0:T(8,128)(2,1)S(1)}, u32[]{:S(2)}, u32[]{:S(2)}) collective-permute-start(bf16[512,128]{1,0:T(8,128)(2,1)S(1)} %step_a0.1.rest_0_.mine_ref), channel_id=1, source_target_pairs={{0,8},{4,12},{8,0},{12,4},{1,9},{5,13},{9,1},{13,5},{2,10},{6,14},... | collective-permute-start | bytes 393224 | tf_op jit(solution)/shard_map/ppermute | solution.py:35
  21.3 6.7 %collective-permute-start.8 = (bf16[512,128]{1,0:T(8,128)(2,1)S(1)}, bf16[512,128]{1,0:T(8,128)(2,1)S(1)}, u32[]{:S(2)}, u32[]{:S(2)}) collective-permute-start(bf16[512,128]{1,0:T(8,128)(2,1)S(1)} %step_b1.1.after_ref.mine_ref.rest_0_), channel_id=1, source_target_pairs={{0,4},{4,0},{8,12},{12,8},{1,5},{5,1},{9,13},{13,9},{2,6},{6,2},{1... | collective-permute-start | bytes 393224 | tf_op jit(solution)/shard_map/ppermute | solution.py:35
  28.0 7.2 %collective-permute-start.13 = (bf16[512,128]{1,0:T(8,128)(2,1)S(1)}, bf16[512,128]{1,0:T(8,128)(2,1)S(1)}, u32[]{:S(2)}, u32[]{:S(2)}) collective-permute-start(bf16[512,128]{1,0:T(8,128)(2,1)S(1)} %get-tuple-element.42.rest_0_.mine_ref), channel_id=1, source_target_pairs={{0,8},{4,12},{8,0},{12,4},{1,9},{5,13},{9,1},{13,5},{2,10},{6,14},... | collective-permute-start | bytes 393224 | tf_op jit(solution)/shard_map/ppermute | solution.py:35
  28.2 5.0 %collective-permute-start.11 = (bf16[512,128]{1,0:T(8,128)(2,1)S(1)}, bf16[512,128]{1,0:T(8,128)(2,1)S(1)}, u32[]{:S(2)}, u32[]{:S(2)}) collective-permute-start(bf16[512,128]{1,0:T(8,128)(2,1)S(1)} %step_a4.1.after_ref.mine_ref), channel_id=1, source_target_pairs={{0,16},{16,0},{1,17},{17,1},{2,18},{18,2},{3,19},{19,3},{4,20},{20... | collective-permute-start | bytes 393224 | tf_op jit(solution)/shard_map/ppermute | solution.py:35
  28.8 2.7 %copy-start = (s32[256]{0:T(256)S(1)}, s32[256]{0:T(256)}, u32[]{:S(2)}) copy-start(s32[256]{0:T(256)} %param.15) | copy-start | bytes 3076
  28.8 14.1 %collective-permute-start.9 = (bf16[512,1024]{1,0:T(8,128)(2,1)S(1)}, bf16[512,1024]{1,0:T(8,128)(2,1)S(1)}, u32[]{:S(2)}, u32[]{:S(2)}) collective-permute-start(bf16[512,1024]{1,0:T(8,128)(2,1)S(1)} %get-tuple-element.43), channel_id=1, source_target_pairs={{0,1},{1,0},{2,3},{3,2},{4,5},{5,4},{6,7},{7,6},{8,9},{9,8},{10,11... | collective-permute-start | bytes 3145736 | tf_op jit(solution)/shard_map/ppermute | solution.py:35
  33.2 5.4 %collective-permute-start.12 = (bf16[512,128]{1,0:T(8,128)(2,1)S(1)}, bf16[512,128]{1,0:T(8,128)(2,1)S(1)}, u32[]{:S(2)}, u32[]{:S(2)}) collective-permute-start(bf16[512,128]{1,0:T(8,128)(2,1)S(1)} %step_a7.1.rest_0_.mine_a), channel_id=1, source_target_pairs={{0,4},{4,0},{8,12},{12,8},{1,5},{5,1},{9,13},{13,9},{2,6},{6,2},{1... | collective-permute-start | bytes 393224 | tf_op jit(solution)/shard_map/ppermute | solution.py:35
  35.3 5.0 %collective-permute-start.14 = (bf16[512,128]{1,0:T(8,128)(2,1)S(1)}, bf16[512,128]{1,0:T(8,128)(2,1)S(1)}, u32[]{:S(2)}, u32[]{:S(2)}) collective-permute-start(bf16[512,128]{1,0:T(8,128)(2,1)S(1)} %step_b8.1.mine_b), channel_id=1, source_target_pairs={{0,16},{16,0},{1,17},{17,1},{2,18},{18,2},{3,19},{19,3},{4,20},{20... | collective-permute-start | bytes 393224 | tf_op jit(solution)/shard_map/ppermute | solution.py:35
  40.5 1.4 %collective-permute-start.15 = (bf16[544,128]{1,0:T(8,128)(2,1)S(1)}, bf16[544,128]{1,0:T(8,128)(2,1)S(1)}, u32[]{:S(2)}, u32[]{:S(2)}) collective-permute-start(bf16[544,128]{1,0:T(8,128)(2,1)S(1)} %get-tuple-element.47.a_ref), channel_id=1, source_target_pairs={{0,1},{1,0},{2,3},{3,2},{4,5},{5,4},{6,7},{7,6},{8,9},{9,8},{10,11... | collective-permute-start | bytes 417800 | tf_op jit(solution)/shard_map/ppermute | solution.py:35
  42.0 5.8 %collective-permute-start.16 = (bf16[544,128]{1,0:T(8,128)(2,1)S(1)}, bf16[544,128]{1,0:T(8,128)(2,1)S(1)}, u32[]{:S(2)}, u32[]{:S(2)}) collective-permute-start(bf16[544,128]{1,0:T(8,128)(2,1)S(1)} %merge.1.after_ref.s_ref), channel_id=1, source_target_pairs={{0,2},{1,3},{2,0},{3,1},{4,6},{5,7},{6,4},{7,5},{8,10},{9,11},{10,... | collective-permute-start | bytes 417800 | tf_op jit(solution)/shard_map/ppermute | solution.py:35
  42.8 5.0 %copy-start.1 = (f32[1024,128]{1,0:T(8,128)S(1)}, f32[1024,128]{1,0:T(8,128)}, u32[]{:S(2)}) copy-start(f32[1024,128]{1,0:T(8,128)} %a_ref.1) | copy-start | bytes 1572868
  42.9 5.0 %copy-start.2 = (f32[128,1024]{1,0:T(8,128)S(1)}, f32[128,1024]{1,0:T(8,128)}, u32[]{:S(2)}) copy-start(f32[128,1024]{1,0:T(8,128)} %b_ref.1) | copy-start | bytes 1572868

commit v14 on v13

--- a/solution.py
+++ b/solution.py
@@ -114,18 +114,23 @@
         outs[i // per][:, i % per * cut : (i % per + 1) * cut] = dot(hg_ref[...], w_ref[i]).astype(BF)
 
 
-def diag_kernel(hg_ref, w_hbm, low_ref, after_ref, out_ref, next_ref, w_ref, sems):
-    _, width, cut = w_ref.shape
-    per = width // cut
-    mine, targets = weight_blocks((3,), w_hbm, w_ref)
-    later, next_targets = weight_blocks((2,), w_hbm, next_ref)
-    copies = fetch(mine + later, targets + next_targets, sems)
+def diag_first_kernel(hg_ref, w_hbm, after_ref, out_ref, rest_ref, next_ref, w_ref, sems):
+    width, cut = w_ref.shape
+    mine, _ = weight_blocks((3,), w_hbm, next_ref)
+    later, targets = weight_blocks((2,), w_hbm, next_ref)
+    copies = fetch(mine + later, [w_ref] + [rest_ref.at[i] for i in range(len(mine) - 1)] + targets, sems)
+    copies[0].wait()
+    out_ref[...] = dot(hg_ref[...], w_ref[...]).astype(BF)
+    for copy in copies[1:]:
+        copy.wait()
+
+
+def diag_kernel(hg_ref, w_ref, first_ref, low_ref, after_ref, out_ref):
+    per, width, cut = w_ref.shape
+    out_ref[:, :cut] = first_ref[...]
+    for i in range(per):
+        out_ref[:, (i + 1) * cut : (i + 2) * cut] = dot(hg_ref[...], w_ref[i]).astype(BF)
     out_ref[:, width:] = low_ref[...]
-    for i in range(per):
-        copies[i].wait()
-        out_ref[:, i * cut : (i + 1) * cut] = dot(hg_ref[...], w_ref[i]).astype(BF)
-    for copy in copies[per:]:
-        copy.wait()
 
 
 def distant_kernel(hg_ref, w_ref, after_ref, out_ref):
@@ -191,7 +196,7 @@
     return jnp.broadcast_to(jnp.sum(x * x), (8, LANES))
 
 
-def update_kernel(way, hg_ref, mine_a, got_a, mine_b, low_ref, ga_ref, squares_ref):
+def update_kernel(way, hg_ref, mine_a, got_a, mine_b, after_ref, low_ref, ga_ref, squares_ref):
     join(*way, mine_a, got_a, ga_ref)
     low_ref[...] = dot(hg_ref[...], ga_ref[...]).astype(BF)
     squares_ref[0] = square_sum(mine_a) + square_sum(got_a)
@@ -252,7 +257,7 @@
 
 
 WEIGHTS = {
-    "rank_v": 2.4, "prep": 0.6, "query_diag": 40.0, "query_beside": 1.0, "query_close": 0.5, "grad_b": 40.0, "final": 1.8,
+    "rank_v": 2.4, "prep": 0.6, "diag_first": 40.0, "query_beside": 2.7, "query_close": 2.7, "grad_b": 40.0, "final": 1.8,
 }
 FLOPS_PER_WEIGHT = 1_150_000_000
 
@@ -350,29 +355,31 @@
             )
 
         per = width // cut
-        diag, columns = call(
-            diag_kernel,
-            [wide, shape((per, width, cut), BF)],
-            [VMEM, HBM, VMEM, ANY],
-            (gained, keep_hbm(base_weight), low, low_u),
-            "query_diag",
-            [pltpu.VMEM((per, width, cut), BF), dma(2 * per)],
-        )
-        diag_got = swap(diag, "tp", n_tp, 1)
-
+        diag_first, rest, columns = call(
+            diag_first_kernel,
+            [shape((count, cut), BF), shape((per - 1, width, cut), BF), shape((per, width, cut), BF)],
+            [VMEM, HBM, ANY],
+            (gained, keep_hbm(base_weight), low_u),
+            "diag_first",
+            [pltpu.VMEM((width, cut), BF), dma(2 * per)],
+        )
         half = width // 2
         keep_a, send_a = call(
             functools.partial(grad_a_kernel, path_a[0]),
             [shape((half, rank), F32), shape((half, rank), BF)],
             [VMEM] * 3 + [ANY],
-            (inputs, low_v, far_v, diag),
+            (inputs, low_v, far_v, diag_first),
             "grad_a",
         )
+        diag = call(
+            diag_kernel, wide, [VMEM] * 4 + [ANY], (gained, rest, diag_first, low, send_a), "query_diag"
+        )
+        diag_got = swap(diag, "tp", n_tp, 1)
         keep_b, send_b = call(
             functools.partial(grad_b_kernel, path_b[0]),
             [shape((half, rank), F32), shape((half, rank), BF)],
             [VMEM] * 3 + [ANY],
-            (cotangent, low_u, far_u, send_a),
+            (cotangent, low_u, far_u, diag),
             "grad_b",
         )
         distant = call(distant_kernel, tall, [VMEM, VMEM, ANY], (gained, columns, send_b), "query_distant")
@@ -391,16 +398,16 @@
             )
 
         mine_a, mine_b, after, passed = keep_a, keep_b, far, []
-        order = ["a", "b", "n", "b", "a", "c", "t", "a", "b"] if n_dp * n_roll == 8 else ["a", "b", "n", "b", "t", "a", "c"] + ["a", "b"] * (len(path_a) - 3)
+        order = ["a", "b", "n", "b", "a", "c", "a", "b", "t"] if n_dp * n_roll == 8 else ["a", "b", "n", "b", "a", "c"] + ["a", "b"] * (len(path_a) - 3) + ["t"]
         steps_a, steps_b = iter(path_a[:-1]), iter(path_b[:-1])
         for i, which in enumerate(order):
             if which == "a":
-                mine_a = send_a = after = step(mine_a, send_a, next(steps_a), after, [], f"step_a{i}")[0]
-            elif which == "b":
-                mine_b, *made = step(mine_b, send_b, next(steps_b), after, passed, f"step_b{i}")
-                send_b = after = mine_b
+                mine_a, *made = step(mine_a, send_a, next(steps_a), after, passed, f"step_a{i}")
+                send_a = after = mine_a
                 if made:
                     beside_got, passed = swap(made[0], "tp", n_tp, 1), []
+            elif which == "b":
+                mine_b = send_b = after = step(mine_b, send_b, next(steps_b), after, [], f"step_b{i}")[0]
             elif which == "t":
                 pos = positions.reshape(-1, LANES)
                 places = call(place_kernel, shape(pos.shape, F32), [VMEM, ANY], (pos, after), "places")
@@ -414,8 +421,8 @@
         step_low, grad_a, squares = call(
             functools.partial(update_kernel, path_a[-1]),
             [shape((count, rank), BF), shape((width, rank), BF), shape((2, 8, LANES), F32)],
-            [VMEM] * 4,
-            (gained, mine_a, cross(mine_a, *path_a[-1]), mine_b),
+            [VMEM] * 4 + [ANY],
+            (gained, mine_a, cross(mine_a, *path_a[-1]), mine_b, after),
             "update",
         )
         step_pack, grad_b = call(

time: 50 us -> 52.9 us (1.058)
  waiting for transfers between devices: 15.4 us -> 17.7 us
    ppermute x17, waiting for transfers between devices: 15.4 us -> 17.7 us  [swap(): return lax.ppermute(x, axis, [(i, i ^ k) for i in range(n)])]
    pallas_call x24 -> x25, Pallas kernels: 16.7 us -> 17 us  [call(): pl.pallas_call(kernel, out_shape=outs, in_specs=in_specs, out_specs=out_s...]
  transfers between devices with their start and end apart: 17 -> 17, of which waited for: 9 -> 9; matrix products, arithmetic and copies ran while one was open for 3% -> 2% of each run, Pallas kernels for 25% -> 25%
where the time goes in v14:
time: 52.9 us; the launch traced here: 52.7 us
  waiting for transfers between devices  17.7 us (33%)
  Pallas kernels  17 us (32%)
  starting transfers between devices  15.9 us (30%)
  other arithmetic  1.28 us (2%)
  between operations  0.89 us (2%)
    ppermute x17, waiting for transfers between devices, swap(): return lax.ppermute(x, axis, [(i, i ^ k) for i in range(n)])  17.7 us
    pallas_call x25, Pallas kernels, call(): pl.pallas_call(kernel, out_shape=outs, in_specs=in_specs, out_specs=out_s...  17 us
    ppermute x17, starting transfers between devices, swap(): return lax.ppermute(x, axis, [(i, i ^ k) for i in range(n)])  15.9 us
  transfers between devices with their start and end apart: 17, of which 9 were waited for; matrix products, arithmetic and copies ran while one was open for 2% of the time, Pallas kernels for 25%

profile of v14, /device:TPU:0, one launch (start us, length us, event | category | flops | bytes accessed | tf_op | source)
XLA Modules:
  0.0 52.7 jit_solution(6782455142777280995)
XLA Ops:
  0.6 2.1 %rank_v.1 = (bf16[384,128]{1,0:T(8,128)(2,1)S(1)}, bf16[384,1024]{1,0:T(8,128)(2,1)S(1)}, bf16[384,1024]{1,0:T(8,128)(2,1)S(1)}, bf16[1024,128]{1,0:T(8,128)(2,1)S(1)}, bf16[512,1024]{1,0:T(8,128)(2,1)S(1)}) custom-call(bf16[384,1024]{1,0:T(8,128)(2,1)} %x_hbm.1, bf16[384,1024]{1,0:T(8,128)(2,1)} %v_hbm.1, f32[1024,128]{1,0:T(8,128)} %a_ref.1, ...), custom_call_target="tpu_custom_call" | custom-call | flops 2760000000 | tf_op jit(solution)/shard_map/rank_v/pallas_call | solution.py:266
  2.7 0.5 collective-permute-start
  3.2 0.4 rank_u.1.x_ref
  3.6 0.1 collective-permute-start.2
  3.7 0.6 %prep.1 = (bf16[512,1024]{1,0:T(8,128)(2,1)S(1)}, bf16[512,128]{1,0:T(8,128)(2,1)S(1)}, f32[8,128]{1,0:T(8,128)S(1)}) custom-call(bf16[512,1024]{1,0:T(8,128)(2,1)S(1)} %get-tuple-element.30.h_ref, f32[1,1024]{1,0:T(1,128)S(1)} %bitcast.8, bf16[1024,128]{1,0:T(8,128)(2,1)S(1)} %get-tuple-element.31.a16_ref), custom_call_target="tpu_custom_call" | custom-call | flops 690000000 | tf_op jit(solution)/shard_map/prep/pallas_call | solution.py:266
  4.4 3.0 %collective-permute-start.1 = (bf16[384,128]{1,0:T(8,128)(2,1)S(1)}, bf16[384,128]{1,0:T(8,128)(2,1)S(1)}, u32[]{:S(2)}, u32[]{:S(2)}) collective-permute-start(bf16[384,128]{1,0:T(8,128)(2,1)S(1)} %low_v.1.after_ref.s_ref), channel_id=1, source_target_pairs={{0,2},{1,3},{2,0},{3,1},{4,6},{5,7},{6,4},{7,5},{8,10},{9,11},{10,... | collective-permute-start | bytes 294920 | tf_op jit(solution)/shard_map/ppermute | solution.py:35
  7.4 0.0 collective-permute-done.2.got_ref
  7.4 0.3 collective-permute-start.4
  7.7 2.2 %diag_first.1 = (bf16[512,512]{1,0:T(8,128)(2,1)S(1)}, bf16[1,1024,512]{2,1,0:T(8,128)(2,1)S(1)}, bf16[2,1024,512]{2,1,0:T(8,128)(2,1)S(1)}) custom-call(bf16[512,1024]{1,0:T(8,128)(2,1)S(1)} %get-tuple-element.32.hg_ref, bf16[1024,4096]{1,0:T(8,128)(2,1)} %w_hbm.5, bf16[384,128]{1,0:T(8,128)(2,1)S(1)} %low_u.1.after_ref.s_ref), custom_call_target="tpu_custom_call" | custom-call | flops 46000001024 | tf_op jit(solution)/shard_map/diag_first/pallas_call | solution.py:266
  10.0 1.0 %collective-permute-done.1.r_ref = bf16[384,128]{1,0:T(8,128)(2,1)S(1)} collective-permute-done((bf16[384,128]{1,0:T(8,128)(2,1)S(1)}, bf16[384,128]{1,0:T(8,128)(2,1)S(1)}, u32[]{:S(2)}, u32[]{:S(2)}) %collective-permute-start.1) | collective-permute-done | bytes 98336 | tf_op jit(solution)/shard_map/ppermute | solution.py:35
  10.9 0.4 grad_a.1
  11.4 2.1 %collective-permute-start.3 = (bf16[512,128]{1,0:T(8,128)(2,1)S(1)}, bf16[512,128]{1,0:T(8,128)(2,1)S(1)}, u32[]{:S(2)}, u32[]{:S(2)}) collective-permute-start(bf16[512,128]{1,0:T(8,128)(2,1)S(1)} %get-tuple-element.38.after_ref), channel_id=1, source_target_pairs={{0,4},{4,0},{8,12},{12,8},{1,5},{5,1},{9,13},{13,9},{2,6},{6,2},{1... | collective-permute-start | bytes 393224 | tf_op jit(solution)/shard_map/ppermute | solution.py:35
  13.4 0.7 %query_diag.1.after_ref.diag_ref = bf16[512,1152]{1,0:T(8,128)(2,1)S(1)} custom-call(bf16[512,1024]{1,0:T(8,128)(2,1)S(1)} %get-tuple-element.32.hg_ref, bf16[1,1024,512]{2,1,0:T(8,128)(2,1)S(1)} %get-tuple-element.41.w_ref, bf16[512,512]{1,0:T(8,128)(2,1)S(1)} %get-tuple-element.36.after_ref.first_ref, ...), custom_call_target="tpu_custom_call" | custom-call | flops 11500000 | tf_op jit(solution)/shard_map/query_diag/pallas_call | solution.py:266
  14.2 0.1 collective-permute-start.5
  14.2 0.0 collective-permute-done.4.r_ref
  14.2 0.3 grad_b.1
  14.6 1.5 %collective-permute-start.7 = (bf16[512,128]{1,0:T(8,128)(2,1)S(1)}, bf16[512,128]{1,0:T(8,128)(2,1)S(1)}, u32[]{:S(2)}, u32[]{:S(2)}) collective-permute-start(bf16[512,128]{1,0:T(8,128)(2,1)S(1)} %get-tuple-element.42.after_ref), channel_id=1, source_target_pairs={{0,16},{16,0},{1,17},{17,1},{2,18},{18,2},{3,19},{19,3},{4,20},{20... | collective-permute-start | bytes 393224 | tf_op jit(solution)/shard_map/ppermute | solution.py:35
  16.1 1.2 %query_distant.1.mine_ref = bf16[512,1024]{1,0:T(8,128)(2,1)S(1)} custom-call(bf16[512,1024]{1,0:T(8,128)(2,1)S(1)} %get-tuple-element.32.hg_ref, bf16[2,1024,512]{2,1,0:T(8,128)(2,1)S(1)} %get-tuple-element.39.w_ref, bf16[512,128]{1,0:T(8,128)(2,1)S(1)} %get-tuple-element.42.after_ref), custom_call_target="tpu_custom_call" | custom-call | flops 11500000 | tf_op jit(solution)/shard_map/query_distant/pallas_call | solution.py:266
  17.4 0.3 far.1.rest_0_.far_ref
  17.7 1.8 %collective-permute-start.10 = (bf16[512,1152]{1,0:T(8,128)(2,1)S(1)}, bf16[512,1152]{1,0:T(8,128)(2,1)S(1)}, u32[]{:S(2)}, u32[]{:S(2)}) collective-permute-start(bf16[512,1152]{1,0:T(8,128)(2,1)S(1)} %far.1.rest_0_.far_ref), channel_id=1, source_target_pairs={{0,2},{1,3},{2,0},{3,1},{4,6},{5,7},{6,4},{7,5},{8,10},{9,11},{10,... | collective-permute-start | bytes 3538952 | tf_op jit(solution)/shard_map/ppermute | solution.py:35
  19.5 2.6 %collective-permute-start.6 = (bf16[512,128]{1,0:T(8,128)(2,1)S(1)}, bf16[512,128]{1,0:T(8,128)(2,1)S(1)}, u32[]{:S(2)}, u32[]{:S(2)}) collective-permute-start(bf16[512,128]{1,0:T(8,128)(2,1)S(1)} %step_a0.1.rest_0_.mine_ref), channel_id=1, source_target_pairs={{0,8},{4,12},{8,0},{12,4},{1,9},{5,13},{9,1},{13,5},{2,10},{6,14},... | collective-permute-start | bytes 393224 | tf_op jit(solution)/shard_map/ppermute | solution.py:35
  22.2 0.5 collective-permute-start.8
  22.7 2.7 %query_beside.1.rest_1_ = bf16[512,1024]{1,0:T(8,128)(2,1)S(1)} custom-call(bf16[512,1024]{1,0:T(8,128)(2,1)S(1)} %get-tuple-element.32.hg_ref, bf16[1024,4096]{1,0:T(8,128)(2,1)} %w_hbm.5, bf16[512,128]{1,0:T(8,128)(2,1)S(1)} %step_b1.1.mine_ref.rest_0_.after_ref), custom_call_target="tpu_custom_call" | custom-call | flops 3104999936 | tf_op jit(solution)/shard_map/query_beside/pallas_call | solution.py:266
  25.3 4.6 %collective-permute-done.8.got_ref = bf16[512,128]{1,0:T(8,128)(2,1)S(1)} collective-permute-done((bf16[512,128]{1,0:T(8,128)(2,1)S(1)}, bf16[512,128]{1,0:T(8,128)(2,1)S(1)}, u32[]{:S(2)}, u32[]{:S(2)}) %collective-permute-start.8) | collective-permute-done | bytes 131104 | tf_op jit(solution)/shard_map/ppermute | solution.py:35
  30.0 0.1 collective-permute-start.13
  30.2 1.1 %collective-permute-start.11 = (bf16[512,128]{1,0:T(8,128)(2,1)S(1)}, bf16[512,128]{1,0:T(8,128)(2,1)S(1)}, u32[]{:S(2)}, u32[]{:S(2)}) collective-permute-start(bf16[512,128]{1,0:T(8,128)(2,1)S(1)} %get-tuple-element.44.after_ref.mine_ref), channel_id=1, source_target_pairs={{0,16},{16,0},{1,17},{17,1},{2,18},{18,2},{3,19},{19,3},{4,20},{20... | collective-permute-start | bytes 393224 | tf_op jit(solution)/shard_map/ppermute | solution.py:35
  31.3 2.7 %query_close.1.rest_0_.mine_ref = bf16[512,1024]{1,0:T(8,128)(2,1)S(1)} custom-call(bf16[512,1024]{1,0:T(8,128)(2,1)S(1)} %get-tuple-element.32.hg_ref, bf16[1024,4096]{1,0:T(8,128)(2,1)} %w_hbm.5, bf16[512,128]{1,0:T(8,128)(2,1)S(1)} %get-tuple-element.44.after_ref.mine_ref), custom_call_target="tpu_custom_call" | custom-call | flops 3104999936 | tf_op jit(solution)/shard_map/query_close/pallas_call | solution.py:266
  34.0 0.0 copy-start
  34.0 1.2 %collective-permute-done.11.got_ref = bf16[512,128]{1,0:T(8,128)(2,1)S(1)} collective-permute-done((bf16[512,128]{1,0:T(8,128)(2,1)S(1)}, bf16[512,128]{1,0:T(8,128)(2,1)S(1)}, u32[]{:S(2)}, u32[]{:S(2)}) %collective-permute-start.11) | collective-permute-done | bytes 131104 | tf_op jit(solution)/shard_map/ppermute | solution.py:35
  35.2 0.7 %collective-permute-start.12 = (bf16[512,128]{1,0:T(8,128)(2,1)S(1)}, bf16[512,128]{1,0:T(8,128)(2,1)S(1)}, u32[]{:S(2)}, u32[]{:S(2)}) collective-permute-start(bf16[512,128]{1,0:T(8,128)(2,1)S(1)} %step_a6.1.rest_0_.mine_a), channel_id=1, source_target_pairs={{0,4},{4,0},{8,12},{12,8},{1,5},{5,1},{9,13},{13,9},{2,6},{6,2},{1... | collective-permute-start | bytes 393224 | tf_op jit(solution)/shard_map/ppermute | solution.py:35
  35.9 2.2 %collective-permute-done.13.got_ref = bf16[512,128]{1,0:T(8,128)(2,1)S(1)} collective-permute-done((bf16[512,128]{1,0:T(8,128)(2,1)S(1)}, bf16[512,128]{1,0:T(8,128)(2,1)S(1)}, u32[]{:S(2)}, u32[]{:S(2)}) %collective-permute-start.13) | collective-permute-done | bytes 131104 | tf_op jit(solution)/shard_map/ppermute | solution.py:35
  38.2 1.1 %collective-permute-start.14 = (bf16[512,128]{1,0:T(8,128)(2,1)S(1)}, bf16[512,128]{1,0:T(8,128)(2,1)S(1)}, u32[]{:S(2)}, u32[]{:S(2)}) collective-permute-start(bf16[512,128]{1,0:T(8,128)(2,1)S(1)} %step_b7.1.after_ref.mine_b), channel_id=1, source_target_pairs={{0,16},{16,0},{1,17},{17,1},{2,18},{18,2},{3,19},{19,3},{4,20},{20... | collective-permute-start | bytes 393224 | tf_op jit(solution)/shard_map/ppermute | solution.py:35
  39.3 1.0 %multiply_cosine_fusion.1 = (f32[256,64]{1,0:T(8,128)S(1)}, f32[256,64]{1,0:T(8,128)S(1)}, f32[256,64]{1,0:T(8,128)S(1)}, f32[256,64]{1,0:T(8,128)S(1)}, f32[256,64]{1,0:T(8,128)S(1)}, /*index=5*/f32[256,64]{1,0:T(8,128)S(1)}) fusion(f32[64]{0:T(128)S(1)} %multiply_power_fusion, f32[256]{0:T(256)S(1)} %bitcast.6, f32[256]{0:T(256)S(1)} %broadcast_add_fusion), kind=kLoop, calls=%fused_computation.4 | loop fusion | flops 65536 | bytes 395520 | tf_op jit(solution)/shard_map/cos | solution.py:287
  40.3 0.1 maximum_maximum_fusion.after_ref.sin_ref
  40.4 0.5 collective-permute-done.12.got_a
  40.9 0.5 update.1
  41.4 1.9 %collective-permute-done.14.got_b = bf16[512,128]{1,0:T(8,128)(2,1)S(1)} collective-permute-done((bf16[512,128]{1,0:T(8,128)(2,1)S(1)}, bf16[512,128]{1,0:T(8,128)(2,1)S(1)}, u32[]{:S(2)}, u32[]{:S(2)}) %collective-permute-start.14) | collective-permute-done | bytes 131104 | tf_op jit(solution)/shard_map/ppermute | solution.py:35
  43.2 0.2 pack.1
  43.4 0.1 collective-permute-start.15
  43.5 1.3 %collective-permute-done.15.b_ref = bf16[544,128]{1,0:T(8,128)(2,1)S(1)} collective-permute-done((bf16[544,128]{1,0:T(8,128)(2,1)S(1)}, bf16[544,128]{1,0:T(8,128)(2,1)S(1)}, u32[]{:S(2)}, u32[]{:S(2)}) %collective-permute-start.15) | collective-permute-done | bytes 139296 | tf_op jit(solution)/shard_map/ppermute | solution.py:35
  44.9 0.2 collective-permute-start.16
  45.1 0.1 maximum_maximum_fusion.1.cos_ref
  45.3 0.0 copy-start.1
  45.3 0.0 copy-start.2
  45.3 0.5 collective-permute-done.10.far_got
  45.8 0.5 base.1
  46.3 4.4 %collective-permute-done.16.r_ref = bf16[544,128]{1,0:T(8,128)(2,1)S(1)} collective-permute-done((bf16[544,128]{1,0:T(8,128)(2,1)S(1)}, bf16[544,128]{1,0:T(8,128)(2,1)S(1)}, u32[]{:S(2)}, u32[]{:S(2)}) %collective-permute-start.16) | collective-permute-done | bytes 139296 | tf_op jit(solution)/shard_map/ppermute | solution.py:35
  50.7 2.0 %final.1 = (f32[1024,128]{1,0:T(8,128)}, f32[128,1024]{1,0:T(8,128)}, bf16[512,1024]{1,0:T(8,128)(2,1)}) custom-call(f32[512,1024]{1,0:T(8,128)S(1)} %get-tuple-element.50.base_ref, f32[512,128]{1,0:T(8,128)S(1)} %get-tuple-element.51.low_ref, bf16[544,128]{1,0:T(8,128)(2,1)S(1)} %merge.1.after_ref.s_ref, ...), custom_call_target="tpu_custom_call" | custom-call | flops 2070000000 | tf_op jit(solution)/shard_map/final/pallas_call | solution.py:266
  (24 shorter events, 0.3 us)
Async XLA Ops:
  0.6 3.1 %copy-start.3 = (f32[1024]{0:T(1024)S(1)}, f32[1024]{0:T(1024)}, u32[]{:S(2)}) copy-start(f32[1024]{0:T(1024)} %param.14) | copy-start | bytes 12292
  2.7 1.6 %collective-permute-start = (bf16[384,128]{1,0:T(8,128)(2,1)S(1)}, bf16[384,128]{1,0:T(8,128)(2,1)S(1)}, u32[]{:S(2)}, u32[]{:S(2)}) collective-permute-start(bf16[384,128]{1,0:T(8,128)(2,1)S(1)} %get-tuple-element.34.x_ref), channel_id=1, source_target_pairs={{0,1},{1,0},{2,3},{3,2},{4,5},{5,4},{6,7},{7,6},{8,9},{9,8},{10,11... | collective-permute-start | bytes 294920 | tf_op jit(solution)/shard_map/ppermute | solution.py:35
  3.6 3.8 %collective-permute-start.2 = (bf16[384,128]{1,0:T(8,128)(2,1)S(1)}, bf16[384,128]{1,0:T(8,128)(2,1)S(1)}, u32[]{:S(2)}, u32[]{:S(2)}) collective-permute-start(bf16[384,128]{1,0:T(8,128)(2,1)S(1)} %rank_u.1.x_ref), channel_id=1, source_target_pairs={{0,1},{1,0},{2,3},{3,2},{4,5},{5,4},{6,7},{7,6},{8,9},{9,8},{10,11... | collective-permute-start | bytes 294920 | tf_op jit(solution)/shard_map/ppermute | solution.py:35
  4.4 6.6 %collective-permute-start.1 = (bf16[384,128]{1,0:T(8,128)(2,1)S(1)}, bf16[384,128]{1,0:T(8,128)(2,1)S(1)}, u32[]{:S(2)}, u32[]{:S(2)}) collective-permute-start(bf16[384,128]{1,0:T(8,128)(2,1)S(1)} %low_v.1.after_ref.s_ref), channel_id=1, source_target_pairs={{0,2},{1,3},{2,0},{3,1},{4,6},{5,7},{6,4},{7,5},{8,10},{9,11},{10,... | collective-permute-start | bytes 294920 | tf_op jit(solution)/shard_map/ppermute | solution.py:35
  7.4 6.8 %collective-permute-start.4 = (bf16[384,128]{1,0:T(8,128)(2,1)S(1)}, bf16[384,128]{1,0:T(8,128)(2,1)S(1)}, u32[]{:S(2)}, u32[]{:S(2)}) collective-permute-start(bf16[384,128]{1,0:T(8,128)(2,1)S(1)} %low_u.1.after_ref.s_ref), channel_id=1, source_target_pairs={{0,2},{1,3},{2,0},{3,1},{4,6},{5,7},{6,4},{7,5},{8,10},{9,11},{10,... | collective-permute-start | bytes 294920 | tf_op jit(solution)/shard_map/ppermute | solution.py:35
  11.4 8.1 %collective-permute-start.3 = (bf16[512,128]{1,0:T(8,128)(2,1)S(1)}, bf16[512,128]{1,0:T(8,128)(2,1)S(1)}, u32[]{:S(2)}, u32[]{:S(2)}) collective-permute-start(bf16[512,128]{1,0:T(8,128)(2,1)S(1)} %get-tuple-element.38.after_ref), channel_id=1, source_target_pairs={{0,4},{4,0},{8,12},{12,8},{1,5},{5,1},{9,13},{13,9},{2,6},{6,2},{1... | collective-permute-start | bytes 393224 | tf_op jit(solution)/shard_map/ppermute | solution.py:35
  14.2 3.2 %collective-permute-start.5 = (bf16[512,1152]{1,0:T(8,128)(2,1)S(1)}, bf16[512,1152]{1,0:T(8,128)(2,1)S(1)}, u32[]{:S(2)}, u32[]{:S(2)}) collective-permute-start(bf16[512,1152]{1,0:T(8,128)(2,1)S(1)} %query_diag.1.after_ref.diag_ref), channel_id=1, source_target_pairs={{0,1},{1,0},{2,3},{3,2},{4,5},{5,4},{6,7},{7,6},{8,9},{9,8},{10,11... | collective-permute-start | bytes 3538952 | tf_op jit(solution)/shard_map/ppermute | solution.py:35
  14.6 7.5 %collective-permute-start.7 = (bf16[512,128]{1,0:T(8,128)(2,1)S(1)}, bf16[512,128]{1,0:T(8,128)(2,1)S(1)}, u32[]{:S(2)}, u32[]{:S(2)}) collective-permute-start(bf16[512,128]{1,0:T(8,128)(2,1)S(1)} %get-tuple-element.42.after_ref), channel_id=1, source_target_pairs={{0,16},{16,0},{1,17},{17,1},{2,18},{18,2},{3,19},{19,3},{4,20},{20... | collective-permute-start | bytes 393224 | tf_op jit(solution)/shard_map/ppermute | solution.py:35
  17.7 28.1 %collective-permute-start.10 = (bf16[512,1152]{1,0:T(8,128)(2,1)S(1)}, bf16[512,1152]{1,0:T(8,128)(2,1)S(1)}, u32[]{:S(2)}, u32[]{:S(2)}) collective-permute-start(bf16[512,1152]{1,0:T(8,128)(2,1)S(1)} %far.1.rest_0_.far_ref), channel_id=1, source_target_pairs={{0,2},{1,3},{2,0},{3,1},{4,6},{5,7},{6,4},{7,5},{8,10},{9,11},{10,... | collective-permute-start | bytes 3538952 | tf_op jit(solution)/shard_map/ppermute | solution.py:35
  19.5 10.6 %collective-permute-start.6 = (bf16[512,128]{1,0:T(8,128)(2,1)S(1)}, bf16[512,128]{1,0:T(8,128)(2,1)S(1)}, u32[]{:S(2)}, u32[]{:S(2)}) collective-permute-start(bf16[512,128]{1,0:T(8,128)(2,1)S(1)} %step_a0.1.rest_0_.mine_ref), channel_id=1, source_target_pairs={{0,8},{4,12},{8,0},{12,4},{1,9},{5,13},{9,1},{13,5},{2,10},{6,14},... | collective-permute-start | bytes 393224 | tf_op jit(solution)/shard_map/ppermute | solution.py:35
  22.2 7.8 %collective-permute-start.8 = (bf16[512,128]{1,0:T(8,128)(2,1)S(1)}, bf16[512,128]{1,0:T(8,128)(2,1)S(1)}, u32[]{:S(2)}, u32[]{:S(2)}) collective-permute-start(bf16[512,128]{1,0:T(8,128)(2,1)S(1)} %step_b1.1.mine_ref.rest_0_.after_ref), channel_id=1, source_target_pairs={{0,4},{4,0},{8,12},{12,8},{1,5},{5,1},{9,13},{13,9},{2,6},{6,2},{1... | collective-permute-start | bytes 393224 | tf_op jit(solution)/shard_map/ppermute | solution.py:35
  30.0 8.1 %collective-permute-start.13 = (bf16[512,128]{1,0:T(8,128)(2,1)S(1)}, bf16[512,128]{1,0:T(8,128)(2,1)S(1)}, u32[]{:S(2)}, u32[]{:S(2)}) collective-permute-start(bf16[512,128]{1,0:T(8,128)(2,1)S(1)} %step_b3.1.rest_0_.mine_ref), channel_id=1, source_target_pairs={{0,8},{4,12},{8,0},{12,4},{1,9},{5,13},{9,1},{13,5},{2,10},{6,14},... | collective-permute-start | bytes 393224 | tf_op jit(solution)/shard_map/ppermute | solution.py:35
  30.2 5.0 %collective-permute-start.11 = (bf16[512,128]{1,0:T(8,128)(2,1)S(1)}, bf16[512,128]{1,0:T(8,128)(2,1)S(1)}, u32[]{:S(2)}, u32[]{:S(2)}) collective-permute-start(bf16[512,128]{1,0:T(8,128)(2,1)S(1)} %get-tuple-element.44.after_ref.mine_ref), channel_id=1, source_target_pairs={{0,16},{16,0},{1,17},{17,1},{2,18},{18,2},{3,19},{19,3},{4,20},{20... | collective-permute-start | bytes 393224 | tf_op jit(solution)/shard_map/ppermute | solution.py:35
  31.3 14.0 %collective-permute-start.9 = (bf16[512,1024]{1,0:T(8,128)(2,1)S(1)}, bf16[512,1024]{1,0:T(8,128)(2,1)S(1)}, u32[]{:S(2)}, u32[]{:S(2)}) collective-permute-start(bf16[512,1024]{1,0:T(8,128)(2,1)S(1)} %get-tuple-element.45), channel_id=1, source_target_pairs={{0,1},{1,0},{2,3},{3,2},{4,5},{5,4},{6,7},{7,6},{8,9},{9,8},{10,11... | collective-permute-start | bytes 3145736 | tf_op jit(solution)/shard_map/ppermute | solution.py:35
  34.0 5.3 %copy-start = (s32[256]{0:T(256)S(1)}, s32[256]{0:T(256)}, u32[]{:S(2)}) copy-start(s32[256]{0:T(256)} %param.15) | copy-start | bytes 3076
  35.2 5.7 %collective-permute-start.12 = (bf16[512,128]{1,0:T(8,128)(2,1)S(1)}, bf16[512,128]{1,0:T(8,128)(2,1)S(1)}, u32[]{:S(2)}, u32[]{:S(2)}) collective-permute-start(bf16[512,128]{1,0:T(8,128)(2,1)S(1)} %step_a6.1.rest_0_.mine_a), channel_id=1, source_target_pairs={{0,4},{4,0},{8,12},{12,8},{1,5},{5,1},{9,13},{13,9},{2,6},{6,2},{1... | collective-permute-start | bytes 393224 | tf_op jit(solution)/shard_map/ppermute | solution.py:35
  38.2 5.0 %collective-permute-start.14 = (bf16[512,128]{1,0:T(8,128)(2,1)S(1)}, bf16[512,128]{1,0:T(8,128)(2,1)S(1)}, u32[]{:S(2)}, u32[]{:S(2)}) collective-permute-start(bf16[512,128]{1,0:T(8,128)(2,1)S(1)} %step_b7.1.after_ref.mine_b), channel_id=1, source_target_pairs={{0,16},{16,0},{1,17},{17,1},{2,18},{18,2},{3,19},{19,3},{4,20},{20... | collective-permute-start | bytes 393224 | tf_op jit(solution)/shard_map/ppermute | solution.py:35
  43.4 1.4 %collective-permute-start.15 = (bf16[544,128]{1,0:T(8,128)(2,1)S(1)}, bf16[544,128]{1,0:T(8,128)(2,1)S(1)}, u32[]{:S(2)}, u32[]{:S(2)}) collective-permute-start(bf16[544,128]{1,0:T(8,128)(2,1)S(1)} %get-tuple-element.49.a_ref), channel_id=1, source_target_pairs={{0,1},{1,0},{2,3},{3,2},{4,5},{5,4},{6,7},{7,6},{8,9},{9,8},{10,11... | collective-permute-start | bytes 417800 | tf_op jit(solution)/shard_map/ppermute | solution.py:35
  44.9 5.8 %collective-permute-start.16 = (bf16[544,128]{1,0:T(8,128)(2,1)S(1)}, bf16[544,128]{1,0:T(8,128)(2,1)S(1)}, u32[]{:S(2)}, u32[]{:S(2)}) collective-permute-start(bf16[544,128]{1,0:T(8,128)(2,1)S(1)} %merge.1.after_ref.s_ref), channel_id=1, source_target_pairs={{0,2},{1,3},{2,0},{3,1},{4,6},{5,7},{6,4},{7,5},{8,10},{9,11},{10,... | collective-permute-start | bytes 417800 | tf_op jit(solution)/shard_map/ppermute | solution.py:35
  45.3 5.4 %copy-start.1 = (f32[1024,128]{1,0:T(8,128)S(1)}, f32[1024,128]{1,0:T(8,128)}, u32[]{:S(2)}) copy-start(f32[1024,128]{1,0:T(8,128)} %a_ref.1) | copy-start | bytes 1572868
  45.3 5.4 %copy-start.2 = (f32[128,1024]{1,0:T(8,128)S(1)}, f32[128,1024]{1,0:T(8,128)}, u32[]{:S(2)}) copy-start(f32[128,1024]{1,0:T(8,128)} %b_ref.1) | copy-start | bytes 1572868

commit v15 on v13

--- a/solution.py
+++ b/solution.py
@@ -59,31 +59,34 @@
     return [slice(i, i + LANES) for i in range(0, count, LANES)]
 
 
-def rank_v_kernel(x_hbm, v_hbm, a_hbm, b_hbm, h_hbm, out_ref, x_ref, v_ref, a16_ref, h_ref, a_ref, b_ref, sems):
-    copies = fetch((v_hbm, b_hbm, x_hbm, a_hbm, h_hbm), (v_ref, b_ref, x_ref, a_ref, h_ref), sems)
+def rank_v_kernel(
+    x_hbm, v_hbm, a_hbm, b_hbm, h_hbm, w_hbm, out_ref, x_ref, v_ref, a16_ref, h_ref, w_ref, a_ref, b_ref, sems
+):
+    first = weight_blocks((3,), w_hbm, w_ref.shape[1])[0]
+    copies = fetch((v_hbm, b_hbm, x_hbm, a_hbm, h_hbm, first), (v_ref, b_ref, x_ref, a_ref, h_ref, w_ref), sems)
     copies[1].wait()
     b16 = b_ref[...].astype(BF)
     copies[0].wait()
     out_ref[...] = dot(v_ref[...], b16, ((1,), (1,))).astype(BF)
     copies[3].wait()
     a16_ref[...] = a_ref[...].astype(BF)
-    copies[2].wait()
-    copies[4].wait()
+    for i in (2, 4, 5):
+        copies[i].wait()
 
 
 def rank_u_kernel(x_ref, a16_ref, out_ref):
     out_ref[...] = dot(x_ref[...], a16_ref[...]).astype(BF)
 
 
-def weight_blocks(peers, w_hbm, w_ref):
-    _, width, cut = w_ref.shape
+def weight_blocks(peers, w_hbm, cut):
+    width = w_hbm.shape[0]
     mine = lax.axis_index("tp")
     sources = []
     for peer in peers:
         for i in range(width // cut):
             start = (mine ^ peer) * width + i * cut
             sources.append(w_hbm.at[:, pl.ds(pl.multiple_of(start, cut), cut)])
-    return sources, [w_ref.at[i] for i in range(len(sources))]
+    return sources
 
 
 def prep_kernel(h_ref, gain_ref, a16_ref, hg_ref, low_ref, sums_ref):
@@ -107,24 +110,24 @@
 def query_kernel(peers, hg_ref, w_hbm, after_ref, *rest):
     outs, (w_ref, sems) = rest[:-2], rest[-2:]
     _, width, cut = w_ref.shape
-    copies = fetch(*weight_blocks(peers, w_hbm, w_ref), sems)
+    copies = fetch(weight_blocks(peers, w_hbm, cut), [w_ref.at[i] for i in range(w_ref.shape[0])], sems)
     per = width // cut
     for i, copy in enumerate(copies):
         copy.wait()
         outs[i // per][:, i % per * cut : (i % per + 1) * cut] = dot(hg_ref[...], w_ref[i]).astype(BF)
 
 
-def diag_kernel(hg_ref, w_hbm, low_ref, after_ref, out_ref, next_ref, w_ref, sems):
-    _, width, cut = w_ref.shape
-    per = width // cut
-    mine, targets = weight_blocks((3,), w_hbm, w_ref)
-    later, next_targets = weight_blocks((2,), w_hbm, next_ref)
-    copies = fetch(mine + later, targets + next_targets, sems)
+def diag_kernel(hg_ref, w_ref, w_hbm, low_ref, after_ref, out_ref, next_ref, rest_ref, sems):
+    per, width, cut = next_ref.shape
+    sources = weight_blocks((3, 2), w_hbm, cut)[1:]
+    targets = [rest_ref.at[i] for i in range(per - 1)] + [next_ref.at[i] for i in range(per)]
+    copies = fetch(sources, targets, sems)
+    out_ref[:, :cut] = dot(hg_ref[...], w_ref[...]).astype(BF)
     out_ref[:, width:] = low_ref[...]
-    for i in range(per):
-        copies[i].wait()
-        out_ref[:, i * cut : (i + 1) * cut] = dot(hg_ref[...], w_ref[i]).astype(BF)
-    for copy in copies[per:]:
+    for i in range(1, per):
+        copies[i - 1].wait()
+        out_ref[:, i * cut : (i + 1) * cut] = dot(hg_ref[...], rest_ref[i - 1]).astype(BF)
+    for copy in copies[per - 1 :]:
         copy.wait()
 
 
@@ -191,7 +194,7 @@
     return jnp.broadcast_to(jnp.sum(x * x), (8, LANES))
 
 
-def update_kernel(way, hg_ref, mine_a, got_a, mine_b, low_ref, ga_ref, squares_ref):
+def update_kernel(way, hg_ref, mine_a, got_a, mine_b, after_ref, low_ref, ga_ref, squares_ref):
     join(*way, mine_a, got_a, ga_ref)
     low_ref[...] = dot(hg_ref[...], ga_ref[...]).astype(BF)
     squares_ref[0] = square_sum(mine_a) + square_sum(got_a)
@@ -251,9 +254,7 @@
     return pltpu.with_memory_space_constraint(x, pltpu.HBM)
 
 
-WEIGHTS = {
-    "rank_v": 2.4, "prep": 0.6, "query_diag": 40.0, "query_beside": 1.0, "query_close": 0.5, "grad_b": 40.0, "final": 1.8,
-}
+WEIGHTS = {"rank_v": 2.4, "prep": 0.6, "query_diag": 40.0, "query_beside": 2.7, "query_close": 2.7, "grad_b": 40.0, "final": 1.8}
 FLOPS_PER_WEIGHT = 1_150_000_000
 
 
@@ -309,22 +310,26 @@
         dma = lambda n: pltpu.SemaphoreType.DMA((n,))
         vmem = lambda n, dtype=F32: pltpu.VMEM((n, rank), dtype)
 
+        cut = 512
         tall = shape((count, width), BF)
         low_shape = shape((tokens, rank), BF)
-        part_v, inputs, cotangent, half_a, hidden = call(
+        part_v, inputs, cotangent, half_a, hidden, first_columns = call(
             rank_v_kernel,
-            [low_shape, shape(train_inputs.shape, BF), shape(train_inputs.shape, BF), shape(factor_a.shape, BF), tall],
-            [HBM] * 5,
+            [low_shape, shape(train_inputs.shape, BF), shape(train_inputs.shape, BF), shape(factor_a.shape, BF), tall,
+             shape((width, cut), BF)],
+            [HBM] * 6,
             tuple(
-                map(keep_hbm, (train_inputs, train_cotangent, factor_a, factor_b, incoming.reshape(count, width)))
+                map(
+                    keep_hbm,
+                    (train_inputs, train_cotangent, factor_a, factor_b, incoming.reshape(count, width), base_weight),
+                )
             ),
             "rank_v",
-            [pltpu.VMEM(factor_a.shape, F32), pltpu.VMEM(factor_b.shape, F32), dma(5)],
+            [pltpu.VMEM(factor_a.shape, F32), pltpu.VMEM(factor_b.shape, F32), dma(6)],
         )
         got_v = swap(part_v, "tp", n_tp, 1)
         part_u = call(rank_u_kernel, low_shape, [VMEM] * 2, (inputs, half_a), "rank_u")
         got_u = swap(part_u, "tp", n_tp, 1)
-        cut = 512
         wide = shape((count, width + rank), BF)
         gained, low, sums = call(
             prep_kernel,
@@ -353,10 +358,10 @@
         diag, columns = call(
             diag_kernel,
             [wide, shape((per, width, cut), BF)],
-            [VMEM, HBM, VMEM, ANY],
-            (gained, keep_hbm(base_weight), low, low_u),
+            [VMEM, VMEM, HBM, VMEM, ANY],
+            (gained, first_columns, keep_hbm(base_weight), low, low_u),
             "query_diag",
-            [pltpu.VMEM((per, width, cut), BF), dma(2 * per)],
+            [pltpu.VMEM((per - 1, width, cut), BF), dma(2 * per - 1)],
         )
         diag_got = swap(diag, "tp", n_tp, 1)
 
@@ -391,16 +396,16 @@
             )
 
         mine_a, mine_b, after, passed = keep_a, keep_b, far, []
-        order = ["a", "b", "n", "b", "a", "c", "t", "a", "b"] if n_dp * n_roll == 8 else ["a", "b", "n", "b", "t", "a", "c"] + ["a", "b"] * (len(path_a) - 3)
+        order = ["a", "b", "n", "b", "a", "c", "a", "b", "t"] if n_dp * n_roll == 8 else ["a", "b", "n", "b", "a", "c"] + ["a", "b"] * (len(path_a) - 3) + ["t"]
         steps_a, steps_b = iter(path_a[:-1]), iter(path_b[:-1])
         for i, which in enumerate(order):
             if which == "a":
-                mine_a = send_a = after = step(mine_a, send_a, next(steps_a), after, [], f"step_a{i}")[0]
-            elif which == "b":
-                mine_b, *made = step(mine_b, send_b, next(steps_b), after, passed, f"step_b{i}")
-                send_b = after = mine_b
+                mine_a, *made = step(mine_a, send_a, next(steps_a), after, passed, f"step_a{i}")
+                send_a = after = mine_a
                 if made:
                     beside_got, passed = swap(made[0], "tp", n_tp, 1), []
+            elif which == "b":
+                mine_b = send_b = after = step(mine_b, send_b, next(steps_b), after, [], f"step_b{i}")[0]
             elif which == "t":
                 pos = positions.reshape(-1, LANES)
                 places = call(place_kernel, shape(pos.shape, F32), [VMEM, ANY], (pos, after), "places")
@@ -414,8 +419,8 @@
         step_low, grad_a, squares = call(
             functools.partial(update_kernel, path_a[-1]),
             [shape((count, rank), BF), shape((width, rank), BF), shape((2, 8, LANES), F32)],
-            [VMEM] * 4,
-            (gained, mine_a, cross(mine_a, *path_a[-1]), mine_b),
+            [VMEM] * 4 + [ANY],
+            (gained, mine_a, cross(mine_a, *path_a[-1]), mine_b, after),
             "update",
         )
         step_pack, grad_b = call(

time: 50 us -> 49.6 us (level)
  starting transfers between devices: 15.5 us -> 17.1 us
  waiting for transfers between devices: 15.4 us -> 13.9 us
    ppermute x17, starting transfers between devices: 15.5 us -> 17.1 us  [swap(): return lax.ppermute(x, axis, [(i, i ^ k) for i in range(n)])]
    ppermute x17, waiting for transfers between devices: 15.4 us -> 13.9 us  [swap(): return lax.ppermute(x, axis, [(i, i ^ k) for i in range(n)])]
  transfers between devices with their start and end apart: 17 -> 17, of which waited for: 9 -> 9; matrix products, arithmetic and copies ran while one was open for 3% -> 3% of each run, Pallas kernels for 25% -> 24%
where the time goes in v15:
time: 49.6 us; the launch traced here: 49.4 us
  starting transfers between devices  17.1 us (34%)
  Pallas kernels  16.3 us (33%)
  waiting for transfers between devices  13.9 us (28%)
  other arithmetic  1.28 us (3%)
  between operations  0.85 us (2%)
    ppermute x17, starting transfers between devices, swap(): return lax.ppermute(x, axis, [(i, i ^ k) for i in range(n)])  17.1 us
    pallas_call x24, Pallas kernels, call(): pl.pallas_call(kernel, out_shape=outs, in_specs=in_specs, out_specs=out_s...  16.3 us
    ppermute x17, waiting for transfers between devices, swap(): return lax.ppermute(x, axis, [(i, i ^ k) for i in range(n)])  13.9 us
    cos x1, other arithmetic, turn_tables(): c, s = (jnp.cos(angle), jnp.sin(angle))  0.99 us
  transfers between devices with their start and end apart: 17, of which 9 were waited for; matrix products, arithmetic and copies ran while one was open for 3% of the time, Pallas kernels for 24%

profile of v15, /device:TPU:0, one launch (start us, length us, event | category | flops | bytes accessed | tf_op | source)
XLA Modules:
  0.0 49.4 jit_solution(7938640860419759797)
XLA Ops:
  0.6 2.4 %rank_v.1 = (bf16[384,128]{1,0:T(8,128)(2,1)S(1)}, bf16[384,1024]{1,0:T(8,128)(2,1)S(1)}, bf16[384,1024]{1,0:T(8,128)(2,1)S(1)}, bf16[1024,128]{1,0:T(8,128)(2,1...) custom-call(bf16[384,1024]{1,0:T(8,128)(2,1)} %x_hbm.1, bf16[384,1024]{1,0:T(8,128)(2,1)} %v_hbm.1, ...), custom_call_target="tpu_custom_call" | custom-call | flops 2760000000 | tf_op jit(solution)/shard_map/rank_v/pallas_call | solution.py:262
  3.0 0.5 %collective-permute-start = (bf16[384,128]{1,0:T(8,128)(2,1)S(1)}, bf16[384,128]{1,0:T(8,128)(2,1)S(1)}, u32[]{:S(2)}, u32[]{:S(2)}) collective-permute-start(bf16[384,128]{1,0:T(8,128)(2,1)S(1)} %get-tuple-element.34.x_ref), channel_id=1, source_target_pairs={{0,1},{1,0},{2,3},{3,2},{4,5},{5,4},{6,7},{7,6},{8,9},{9,8},{10,11... | collective-permute-start | bytes 294920 | tf_op jit(solution)/shard_map/ppermute | solution.py:35
  3.6 0.4 rank_u.1.x_ref
  3.9 0.1 collective-permute-start.2
  4.1 0.6 %prep.1 = (bf16[512,1024]{1,0:T(8,128)(2,1)S(1)}, bf16[512,128]{1,0:T(8,128)(2,1)S(1)}, f32[8,128]{1,0:T(8,128)S(1)}) custom-call(bf16[512,1024]{1,0:T(8,128)(2,1)S(1)} %get-tuple-element.30.h_ref, f32[1,1024]{1,0:T(1,128)S(1)} %bitcast.8, bf16[1024,128]{1,0:T(8,128)(2,1)S(1)} %get-tuple-element.31.a16_ref), custom_call_target="tpu_custom_call" | custom-call | flops 690000000 | tf_op jit(solution)/shard_map/prep/pallas_call | solution.py:262
  4.6 0.0 collective-permute-done.got_ref
  4.7 3.0 %collective-permute-start.1 = (bf16[384,128]{1,0:T(8,128)(2,1)S(1)}, bf16[384,128]{1,0:T(8,128)(2,1)S(1)}, u32[]{:S(2)}, u32[]{:S(2)}) collective-permute-start(bf16[384,128]{1,0:T(8,128)(2,1)S(1)} %low_v.1.after_ref.s_ref), channel_id=1, source_target_pairs={{0,2},{1,3},{2,0},{3,1},{4,6},{5,7},{6,4},{7,5},{8,10},{9,11},{10,... | collective-permute-start | bytes 294920 | tf_op jit(solution)/shard_map/ppermute | solution.py:35
  7.7 0.3 collective-permute-start.4
  8.1 2.0 %query_diag.1 = (bf16[512,1152]{1,0:T(8,128)(2,1)S(1)}, bf16[2,1024,512]{2,1,0:T(8,128)(2,1)S(1)}) custom-call(bf16[512,1024]{1,0:T(8,128)(2,1)S(1)} %get-tuple-element.32.hg_ref, bf16[1024,512]{1,0:T(8,128)(2,1)S(1)} %get-tuple-element.36.w_ref, bf16[1024,4096]{1,0:T(8,128)(2,1)} %w_hbm.7, bf16[512,128]{1,0:T(8,128)(2,1)S(1)} %get-tuple-element.35.after_ref.low_ref, ...), custom_call_target="tpu_custom_call" | custom-call | flops 46000001024 | tf_op jit(solution)/shard_map/query_diag/pallas_call | solution.py:262
  10.1 0.1 collective-permute-start.5
  10.2 1.1 %collective-permute-done.1.r_ref = bf16[384,128]{1,0:T(8,128)(2,1)S(1)} collective-permute-done((bf16[384,128]{1,0:T(8,128)(2,1)S(1)}, bf16[384,128]{1,0:T(8,128)(2,1)S(1)}, u32[]{:S(2)}, u32[]{:S(2)}) %collective-permute-start.1) | collective-permute-done | bytes 98336 | tf_op jit(solution)/shard_map/ppermute | solution.py:35
  11.3 0.4 grad_a.1
  11.7 2.1 %collective-permute-start.3 = (bf16[512,128]{1,0:T(8,128)(2,1)S(1)}, bf16[512,128]{1,0:T(8,128)(2,1)S(1)}, u32[]{:S(2)}, u32[]{:S(2)}) collective-permute-start(bf16[512,128]{1,0:T(8,128)(2,1)S(1)} %get-tuple-element.39.after_ref), channel_id=1, source_target_pairs={{0,4},{4,0},{8,12},{12,8},{1,5},{5,1},{9,13},{13,9},{2,6},{6,2},{1... | collective-permute-start | bytes 393224 | tf_op jit(solution)/shard_map/ppermute | solution.py:35
  13.7 0.0 collective-permute-done.4.r_ref
  13.7 0.3 grad_b.1
  14.1 1.6 %collective-permute-start.7 = (bf16[512,128]{1,0:T(8,128)(2,1)S(1)}, bf16[512,128]{1,0:T(8,128)(2,1)S(1)}, u32[]{:S(2)}, u32[]{:S(2)}) collective-permute-start(bf16[512,128]{1,0:T(8,128)(2,1)S(1)} %get-tuple-element.42.after_ref), channel_id=1, source_target_pairs={{0,16},{16,0},{1,17},{17,1},{2,18},{18,2},{3,19},{19,3},{4,20},{20... | collective-permute-start | bytes 393224 | tf_op jit(solution)/shard_map/ppermute | solution.py:35
  15.7 1.2 %query_distant.1.mine_ref = bf16[512,1024]{1,0:T(8,128)(2,1)S(1)} custom-call(bf16[512,1024]{1,0:T(8,128)(2,1)S(1)} %get-tuple-element.32.hg_ref, bf16[2,1024,512]{2,1,0:T(8,128)(2,1)S(1)} %get-tuple-element.40.w_ref, bf16[512,128]{1,0:T(8,128)(2,1)S(1)} %get-tuple-element.42.after_ref), custom_call_target="tpu_custom_call" | custom-call | flops 11500000 | tf_op jit(solution)/shard_map/query_distant/pallas_call | solution.py:262
  16.9 0.0 collective-permute-done.5.got_ref
  16.9 0.3 far.1.rest_0_.far_ref
  17.2 1.8 %collective-permute-start.10 = (bf16[512,1152]{1,0:T(8,128)(2,1)S(1)}, bf16[512,1152]{1,0:T(8,128)(2,1)S(1)}, u32[]{:S(2)}, u32[]{:S(2)}) collective-permute-start(bf16[512,1152]{1,0:T(8,128)(2,1)S(1)} %far.1.rest_0_.far_ref), channel_id=1, source_target_pairs={{0,2},{1,3},{2,0},{3,1},{4,6},{5,7},{6,4},{7,5},{8,10},{9,11},{10,... | collective-permute-start | bytes 3538952 | tf_op jit(solution)/shard_map/ppermute | solution.py:35
  19.0 2.7 %collective-permute-start.6 = (bf16[512,128]{1,0:T(8,128)(2,1)S(1)}, bf16[512,128]{1,0:T(8,128)(2,1)S(1)}, u32[]{:S(2)}, u32[]{:S(2)}) collective-permute-start(bf16[512,128]{1,0:T(8,128)(2,1)S(1)} %step_a0.1.rest_0_.mine_ref), channel_id=1, source_target_pairs={{0,8},{4,12},{8,0},{12,4},{1,9},{5,13},{9,1},{13,5},{2,10},{6,14},... | collective-permute-start | bytes 393224 | tf_op jit(solution)/shard_map/ppermute | solution.py:35
  21.7 0.7 %collective-permute-start.8 = (bf16[512,128]{1,0:T(8,128)(2,1)S(1)}, bf16[512,128]{1,0:T(8,128)(2,1)S(1)}, u32[]{:S(2)}, u32[]{:S(2)}) collective-permute-start(bf16[512,128]{1,0:T(8,128)(2,1)S(1)} %step_b1.1.mine_ref.rest_0_.after_ref), channel_id=1, source_target_pairs={{0,4},{4,0},{8,12},{12,8},{1,5},{5,1},{9,13},{13,9},{2,6},{6,2},{1... | collective-permute-start | bytes 393224 | tf_op jit(solution)/shard_map/ppermute | solution.py:35
  22.4 2.7 %query_beside.1.rest_1_ = bf16[512,1024]{1,0:T(8,128)(2,1)S(1)} custom-call(bf16[512,1024]{1,0:T(8,128)(2,1)S(1)} %get-tuple-element.32.hg_ref, bf16[1024,4096]{1,0:T(8,128)(2,1)} %w_hbm.7, bf16[512,128]{1,0:T(8,128)(2,1)S(1)} %step_b1.1.mine_ref.rest_0_.after_ref), custom_call_target="tpu_custom_call" | custom-call | flops 3104999936 | tf_op jit(solution)/shard_map/query_beside/pallas_call | solution.py:262
  25.1 2.4 %collective-permute-done.8.got_ref = bf16[512,128]{1,0:T(8,128)(2,1)S(1)} collective-permute-done((bf16[512,128]{1,0:T(8,128)(2,1)S(1)}, bf16[512,128]{1,0:T(8,128)(2,1)S(1)}, u32[]{:S(2)}, u32[]{:S(2)}) %collective-permute-start.8) | collective-permute-done | bytes 131104 | tf_op jit(solution)/shard_map/ppermute | solution.py:35
  27.5 0.2 collective-permute-start.13
  27.7 0.8 %collective-permute-start.11 = (bf16[512,128]{1,0:T(8,128)(2,1)S(1)}, bf16[512,128]{1,0:T(8,128)(2,1)S(1)}, u32[]{:S(2)}, u32[]{:S(2)}) collective-permute-start(bf16[512,128]{1,0:T(8,128)(2,1)S(1)} %get-tuple-element.44.after_ref.mine_ref), channel_id=1, source_target_pairs={{0,16},{16,0},{1,17},{17,1},{2,18},{18,2},{3,19},{19,3},{4,20},{20... | collective-permute-start | bytes 393224 | tf_op jit(solution)/shard_map/ppermute | solution.py:35
  28.5 2.7 %query_close.1.rest_0_.mine_ref = bf16[512,1024]{1,0:T(8,128)(2,1)S(1)} custom-call(bf16[512,1024]{1,0:T(8,128)(2,1)S(1)} %get-tuple-element.32.hg_ref, bf16[1024,4096]{1,0:T(8,128)(2,1)} %w_hbm.7, bf16[512,128]{1,0:T(8,128)(2,1)S(1)} %get-tuple-element.44.after_ref.mine_ref), custom_call_target="tpu_custom_call" | custom-call | flops 3104999936 | tf_op jit(solution)/shard_map/query_close/pallas_call | solution.py:262
  31.1 0.0 copy-start.2
  31.2 1.6 %collective-permute-done.11.got_ref = bf16[512,128]{1,0:T(8,128)(2,1)S(1)} collective-permute-done((bf16[512,128]{1,0:T(8,128)(2,1)S(1)}, bf16[512,128]{1,0:T(8,128)(2,1)S(1)}, u32[]{:S(2)}, u32[]{:S(2)}) %collective-permute-start.11) | collective-permute-done | bytes 131104 | tf_op jit(solution)/shard_map/ppermute | solution.py:35
  32.8 1.7 %collective-permute-start.12 = (bf16[512,128]{1,0:T(8,128)(2,1)S(1)}, bf16[512,128]{1,0:T(8,128)(2,1)S(1)}, u32[]{:S(2)}, u32[]{:S(2)}) collective-permute-start(bf16[512,128]{1,0:T(8,128)(2,1)S(1)} %step_a6.1.rest_0_.mine_a), channel_id=1, source_target_pairs={{0,4},{4,0},{8,12},{12,8},{1,5},{5,1},{9,13},{13,9},{2,6},{6,2},{1... | collective-permute-start | bytes 393224 | tf_op jit(solution)/shard_map/ppermute | solution.py:35
  34.5 0.4 collective-permute-done.13.got_ref
  34.9 0.6 %collective-permute-start.14 = (bf16[512,128]{1,0:T(8,128)(2,1)S(1)}, bf16[512,128]{1,0:T(8,128)(2,1)S(1)}, u32[]{:S(2)}, u32[]{:S(2)}) collective-permute-start(bf16[512,128]{1,0:T(8,128)(2,1)S(1)} %step_b7.1.after_ref.mine_b), channel_id=1, source_target_pairs={{0,16},{16,0},{1,17},{17,1},{2,18},{18,2},{3,19},{19,3},{4,20},{20... | collective-permute-start | bytes 393224 | tf_op jit(solution)/shard_map/ppermute | solution.py:35
  35.5 1.0 %multiply_cosine_fusion.1 = (f32[256,64]{1,0:T(8,128)S(1)}, f32[256,64]{1,0:T(8,128)S(1)}, f32[256,64]{1,0:T(8,128)S(1)}, f32[256,64]{1,0:T(8,128)S(1)}, f32[256,64]{1,0:T(8,128)S(1)}, /*index=5*/f32[256,64]{1,0:T(8,128)S(1)}) fusion(f32[64]{0:T(128)S(1)} %multiply_power_fusion, f32[256]{0:T(256)S(1)} %bitcast.6, f32[256]{0:T(256)S(1)} %broadcast_add_fusion), kind=kLoop, calls=%fused_computation.4 | loop fusion | flops 65536 | bytes 395520 | tf_op jit(solution)/shard_map/cos | solution.py:283
  36.5 0.1 maximum_maximum_fusion.after_ref.sin_ref
  36.7 1.2 %collective-permute-done.12.got_a = bf16[512,128]{1,0:T(8,128)(2,1)S(1)} collective-permute-done((bf16[512,128]{1,0:T(8,128)(2,1)S(1)}, bf16[512,128]{1,0:T(8,128)(2,1)S(1)}, u32[]{:S(2)}, u32[]{:S(2)}) %collective-permute-start.12) | collective-permute-done | bytes 131104 | tf_op jit(solution)/shard_map/ppermute | solution.py:35
  37.8 0.5 update.1
  38.3 1.7 %collective-permute-done.14.got_b = bf16[512,128]{1,0:T(8,128)(2,1)S(1)} collective-permute-done((bf16[512,128]{1,0:T(8,128)(2,1)S(1)}, bf16[512,128]{1,0:T(8,128)(2,1)S(1)}, u32[]{:S(2)}, u32[]{:S(2)}) %collective-permute-start.14) | collective-permute-done | bytes 131104 | tf_op jit(solution)/shard_map/ppermute | solution.py:35
  40.0 0.2 pack.1
  40.2 0.1 collective-permute-start.15
  40.3 1.3 %collective-permute-done.15.b_ref = bf16[544,128]{1,0:T(8,128)(2,1)S(1)} collective-permute-done((bf16[544,128]{1,0:T(8,128)(2,1)S(1)}, bf16[544,128]{1,0:T(8,128)(2,1)S(1)}, u32[]{:S(2)}, u32[]{:S(2)}) %collective-permute-start.15) | collective-permute-done | bytes 139296 | tf_op jit(solution)/shard_map/ppermute | solution.py:35
  41.7 1.0 %collective-permute-start.16 = (bf16[544,128]{1,0:T(8,128)(2,1)S(1)}, bf16[544,128]{1,0:T(8,128)(2,1)S(1)}, u32[]{:S(2)}, u32[]{:S(2)}) collective-permute-start(bf16[544,128]{1,0:T(8,128)(2,1)S(1)} %merge.1.after_ref.s_ref), channel_id=1, source_target_pairs={{0,2},{1,3},{2,0},{3,1},{4,6},{5,7},{6,4},{7,5},{8,10},{9,11},{10,... | collective-permute-start | bytes 417800 | tf_op jit(solution)/shard_map/ppermute | solution.py:35
  42.6 0.1 maximum_maximum_fusion.1.cos_ref
  42.8 0.0 copy-start
  42.8 0.0 copy-start.1
  42.8 1.0 %collective-permute-done.10.far_got = bf16[512,1152]{1,0:T(8,128)(2,1)S(1)} collective-permute-done((bf16[512,1152]{1,0:T(8,128)(2,1)S(1)}, bf16[512,1152]{1,0:T(8,128)(2,1)S(1)}, u32[]{:S(2)}, u32[]{:S(2)}) %collective-permute-start.10) | collective-permute-done | bytes 1179680 | tf_op jit(solution)/shard_map/ppermute | solution.py:35
  43.8 0.5 base.1
  44.3 3.1 %collective-permute-done.16.r_ref = bf16[544,128]{1,0:T(8,128)(2,1)S(1)} collective-permute-done((bf16[544,128]{1,0:T(8,128)(2,1)S(1)}, bf16[544,128]{1,0:T(8,128)(2,1)S(1)}, u32[]{:S(2)}, u32[]{:S(2)}) %collective-permute-start.16) | collective-permute-done | bytes 139296 | tf_op jit(solution)/shard_map/ppermute | solution.py:35
  47.5 2.0 %final.1 = (f32[1024,128]{1,0:T(8,128)}, f32[128,1024]{1,0:T(8,128)}, bf16[512,1024]{1,0:T(8,128)(2,1)}) custom-call(f32[512,1024]{1,0:T(8,128)S(1)} %get-tuple-element.50.base_ref, f32[512,128]{1,0:T(8,128)S(1)} %get-tuple-element.51.low_ref, bf16[544,128]{1,0:T(8,128)(2,1)S(1)} %merge.1.after_ref.s_ref, ...), custom_call_target="tpu_custom_call" | custom-call | flops 2070000000 | tf_op jit(solution)/shard_map/final/pallas_call | solution.py:262
  (23 shorter events, 0.3 us)
Async XLA Ops:
  0.6 3.4 %copy-start.3 = (f32[1024]{0:T(1024)S(1)}, f32[1024]{0:T(1024)}, u32[]{:S(2)}) copy-start(f32[1024]{0:T(1024)} %param.14) | copy-start | bytes 12292
  3.0 1.6 %collective-permute-start = (bf16[384,128]{1,0:T(8,128)(2,1)S(1)}, bf16[384,128]{1,0:T(8,128)(2,1)S(1)}, u32[]{:S(2)}, u32[]{:S(2)}) collective-permute-start(bf16[384,128]{1,0:T(8,128)(2,1)S(1)} %get-tuple-element.34.x_ref), channel_id=1, source_target_pairs={{0,1},{1,0},{2,3},{3,2},{4,5},{5,4},{6,7},{7,6},{8,9},{9,8},{10,11... | collective-permute-start | bytes 294920 | tf_op jit(solution)/shard_map/ppermute | solution.py:35
  3.9 3.8 %collective-permute-start.2 = (bf16[384,128]{1,0:T(8,128)(2,1)S(1)}, bf16[384,128]{1,0:T(8,128)(2,1)S(1)}, u32[]{:S(2)}, u32[]{:S(2)}) collective-permute-start(bf16[384,128]{1,0:T(8,128)(2,1)S(1)} %rank_u.1.x_ref), channel_id=1, source_target_pairs={{0,1},{1,0},{2,3},{3,2},{4,5},{5,4},{6,7},{7,6},{8,9},{9,8},{10,11... | collective-permute-start | bytes 294920 | tf_op jit(solution)/shard_map/ppermute | solution.py:35
  4.7 6.6 %collective-permute-start.1 = (bf16[384,128]{1,0:T(8,128)(2,1)S(1)}, bf16[384,128]{1,0:T(8,128)(2,1)S(1)}, u32[]{:S(2)}, u32[]{:S(2)}) collective-permute-start(bf16[384,128]{1,0:T(8,128)(2,1)S(1)} %low_v.1.after_ref.s_ref), channel_id=1, source_target_pairs={{0,2},{1,3},{2,0},{3,1},{4,6},{5,7},{6,4},{7,5},{8,10},{9,11},{10,... | collective-permute-start | bytes 294920 | tf_op jit(solution)/shard_map/ppermute | solution.py:35
  7.7 6.0 %collective-permute-start.4 = (bf16[384,128]{1,0:T(8,128)(2,1)S(1)}, bf16[384,128]{1,0:T(8,128)(2,1)S(1)}, u32[]{:S(2)}, u32[]{:S(2)}) collective-permute-start(bf16[384,128]{1,0:T(8,128)(2,1)S(1)} %low_u.1.after_ref.s_ref), channel_id=1, source_target_pairs={{0,2},{1,3},{2,0},{3,1},{4,6},{5,7},{6,4},{7,5},{8,10},{9,11},{10,... | collective-permute-start | bytes 294920 | tf_op jit(solution)/shard_map/ppermute | solution.py:35
  10.1 6.9 %collective-permute-start.5 = (bf16[512,1152]{1,0:T(8,128)(2,1)S(1)}, bf16[512,1152]{1,0:T(8,128)(2,1)S(1)}, u32[]{:S(2)}, u32[]{:S(2)}) collective-permute-start(bf16[512,1152]{1,0:T(8,128)(2,1)S(1)} %get-tuple-element.37.after_ref.diag_ref), channel_id=1, source_target_pairs={{0,1},{1,0},{2,3},{3,2},{4,5},{5,4},{6,7},{7,6},{8,9},{9,8},{10,11... | collective-permute-start | bytes 3538952 | tf_op jit(solution)/shard_map/ppermute | solution.py:35
  11.7 7.3 %collective-permute-start.3 = (bf16[512,128]{1,0:T(8,128)(2,1)S(1)}, bf16[512,128]{1,0:T(8,128)(2,1)S(1)}, u32[]{:S(2)}, u32[]{:S(2)}) collective-permute-start(bf16[512,128]{1,0:T(8,128)(2,1)S(1)} %get-tuple-element.39.after_ref), channel_id=1, source_target_pairs={{0,4},{4,0},{8,12},{12,8},{1,5},{5,1},{9,13},{13,9},{2,6},{6,2},{1... | collective-permute-start | bytes 393224 | tf_op jit(solution)/shard_map/ppermute | solution.py:35
  14.1 7.6 %collective-permute-start.7 = (bf16[512,128]{1,0:T(8,128)(2,1)S(1)}, bf16[512,128]{1,0:T(8,128)(2,1)S(1)}, u32[]{:S(2)}, u32[]{:S(2)}) collective-permute-start(bf16[512,128]{1,0:T(8,128)(2,1)S(1)} %get-tuple-element.42.after_ref), channel_id=1, source_target_pairs={{0,16},{16,0},{1,17},{17,1},{2,18},{18,2},{3,19},{19,3},{4,20},{20... | collective-permute-start | bytes 393224 | tf_op jit(solution)/shard_map/ppermute | solution.py:35
  17.2 26.6 %collective-permute-start.10 = (bf16[512,1152]{1,0:T(8,128)(2,1)S(1)}, bf16[512,1152]{1,0:T(8,128)(2,1)S(1)}, u32[]{:S(2)}, u32[]{:S(2)}) collective-permute-start(bf16[512,1152]{1,0:T(8,128)(2,1)S(1)} %far.1.rest_0_.far_ref), channel_id=1, source_target_pairs={{0,2},{1,3},{2,0},{3,1},{4,6},{5,7},{6,4},{7,5},{8,10},{9,11},{10,... | collective-permute-start | bytes 3538952 | tf_op jit(solution)/shard_map/ppermute | solution.py:35
  19.0 8.7 %collective-permute-start.6 = (bf16[512,128]{1,0:T(8,128)(2,1)S(1)}, bf16[512,128]{1,0:T(8,128)(2,1)S(1)}, u32[]{:S(2)}, u32[]{:S(2)}) collective-permute-start(bf16[512,128]{1,0:T(8,128)(2,1)S(1)} %step_a0.1.rest_0_.mine_ref), channel_id=1, source_target_pairs={{0,8},{4,12},{8,0},{12,4},{1,9},{5,13},{9,1},{13,5},{2,10},{6,14},... | collective-permute-start | bytes 393224 | tf_op jit(solution)/shard_map/ppermute | solution.py:35
  21.7 5.8 %collective-permute-start.8 = (bf16[512,128]{1,0:T(8,128)(2,1)S(1)}, bf16[512,128]{1,0:T(8,128)(2,1)S(1)}, u32[]{:S(2)}, u32[]{:S(2)}) collective-permute-start(bf16[512,128]{1,0:T(8,128)(2,1)S(1)} %step_b1.1.mine_ref.rest_0_.after_ref), channel_id=1, source_target_pairs={{0,4},{4,0},{8,12},{12,8},{1,5},{5,1},{9,13},{13,9},{2,6},{6,2},{1... | collective-permute-start | bytes 393224 | tf_op jit(solution)/shard_map/ppermute | solution.py:35
  27.5 7.4 %collective-permute-start.13 = (bf16[512,128]{1,0:T(8,128)(2,1)S(1)}, bf16[512,128]{1,0:T(8,128)(2,1)S(1)}, u32[]{:S(2)}, u32[]{:S(2)}) collective-permute-start(bf16[512,128]{1,0:T(8,128)(2,1)S(1)} %step_b3.1.rest_0_.mine_ref), channel_id=1, source_target_pairs={{0,8},{4,12},{8,0},{12,4},{1,9},{5,13},{9,1},{13,5},{2,10},{6,14},... | collective-permute-start | bytes 393224 | tf_op jit(solution)/shard_map/ppermute | solution.py:35
  27.7 5.0 %collective-permute-start.11 = (bf16[512,128]{1,0:T(8,128)(2,1)S(1)}, bf16[512,128]{1,0:T(8,128)(2,1)S(1)}, u32[]{:S(2)}, u32[]{:S(2)}) collective-permute-start(bf16[512,128]{1,0:T(8,128)(2,1)S(1)} %get-tuple-element.44.after_ref.mine_ref), channel_id=1, source_target_pairs={{0,16},{16,0},{1,17},{17,1},{2,18},{18,2},{3,19},{19,3},{4,20},{20... | collective-permute-start | bytes 393224 | tf_op jit(solution)/shard_map/ppermute | solution.py:35
  28.5 14.3 %collective-permute-start.9 = (bf16[512,1024]{1,0:T(8,128)(2,1)S(1)}, bf16[512,1024]{1,0:T(8,128)(2,1)S(1)}, u32[]{:S(2)}, u32[]{:S(2)}) collective-permute-start(bf16[512,1024]{1,0:T(8,128)(2,1)S(1)} %get-tuple-element.45), channel_id=1, source_target_pairs={{0,1},{1,0},{2,3},{3,2},{4,5},{5,4},{6,7},{7,6},{8,9},{9,8},{10,11... | collective-permute-start | bytes 3145736 | tf_op jit(solution)/shard_map/ppermute | solution.py:35
  31.1 4.3 %copy-start.2 = (s32[256]{0:T(256)S(1)}, s32[256]{0:T(256)}, u32[]{:S(2)}) copy-start(s32[256]{0:T(256)} %param.15) | copy-start | bytes 3076
  32.8 5.0 %collective-permute-start.12 = (bf16[512,128]{1,0:T(8,128)(2,1)S(1)}, bf16[512,128]{1,0:T(8,128)(2,1)S(1)}, u32[]{:S(2)}, u32[]{:S(2)}) collective-permute-start(bf16[512,128]{1,0:T(8,128)(2,1)S(1)} %step_a6.1.rest_0_.mine_a), channel_id=1, source_target_pairs={{0,4},{4,0},{8,12},{12,8},{1,5},{5,1},{9,13},{13,9},{2,6},{6,2},{1... | collective-permute-start | bytes 393224 | tf_op jit(solution)/shard_map/ppermute | solution.py:35
  34.9 5.0 %collective-permute-start.14 = (bf16[512,128]{1,0:T(8,128)(2,1)S(1)}, bf16[512,128]{1,0:T(8,128)(2,1)S(1)}, u32[]{:S(2)}, u32[]{:S(2)}) collective-permute-start(bf16[512,128]{1,0:T(8,128)(2,1)S(1)} %step_b7.1.after_ref.mine_b), channel_id=1, source_target_pairs={{0,16},{16,0},{1,17},{17,1},{2,18},{18,2},{3,19},{19,3},{4,20},{20... | collective-permute-start | bytes 393224 | tf_op jit(solution)/shard_map/ppermute | solution.py:35
  40.2 1.4 %collective-permute-start.15 = (bf16[544,128]{1,0:T(8,128)(2,1)S(1)}, bf16[544,128]{1,0:T(8,128)(2,1)S(1)}, u32[]{:S(2)}, u32[]{:S(2)}) collective-permute-start(bf16[544,128]{1,0:T(8,128)(2,1)S(1)} %get-tuple-element.49.a_ref), channel_id=1, source_target_pairs={{0,1},{1,0},{2,3},{3,2},{4,5},{5,4},{6,7},{7,6},{8,9},{9,8},{10,11... | collective-permute-start | bytes 417800 | tf_op jit(solution)/shard_map/ppermute | solution.py:35
  41.7 5.8 %collective-permute-start.16 = (bf16[544,128]{1,0:T(8,128)(2,1)S(1)}, bf16[544,128]{1,0:T(8,128)(2,1)S(1)}, u32[]{:S(2)}, u32[]{:S(2)}) collective-permute-start(bf16[544,128]{1,0:T(8,128)(2,1)S(1)} %merge.1.after_ref.s_ref), channel_id=1, source_target_pairs={{0,2},{1,3},{2,0},{3,1},{4,6},{5,7},{6,4},{7,5},{8,10},{9,11},{10,... | collective-permute-start | bytes 417800 | tf_op jit(solution)/shard_map/ppermute | solution.py:35
  42.8 4.7 %copy-start = (f32[1024,128]{1,0:T(8,128)S(1)}, f32[1024,128]{1,0:T(8,128)}, u32[]{:S(2)}) copy-start(f32[1024,128]{1,0:T(8,128)} %a_ref.1) | copy-start | bytes 1572868
  42.8 4.7 %copy-start.1 = (f32[128,1024]{1,0:T(8,128)S(1)}, f32[128,1024]{1,0:T(8,128)}, u32[]{:S(2)}) copy-start(f32[128,1024]{1,0:T(8,128)} %b_ref.1) | copy-start | bytes 1572868

commit v16 on v15

--- a/solution.py
+++ b/solution.py
@@ -117,10 +117,12 @@
         outs[i // per][:, i % per * cut : (i % per + 1) * cut] = dot(hg_ref[...], w_ref[i]).astype(BF)
 
 
-def diag_kernel(hg_ref, w_ref, w_hbm, low_ref, after_ref, out_ref, next_ref, rest_ref, sems):
-    per, width, cut = next_ref.shape
+def diag_kernel(hg_ref, w_ref, w_hbm, low_ref, after_ref, out_ref, *refs):
+    *next_refs, rest_ref, sems = refs
+    width, cut = w_ref.shape
+    per = width // cut
     sources = weight_blocks((3, 2), w_hbm, cut)[1:]
-    targets = [rest_ref.at[i] for i in range(per - 1)] + [next_ref.at[i] for i in range(per)]
+    targets = [rest_ref.at[i] for i in range(per - 1)] + next_refs
     copies = fetch(sources, targets, sems)
     out_ref[:, :cut] = dot(hg_ref[...], w_ref[...]).astype(BF)
     out_ref[:, width:] = low_ref[...]
@@ -131,15 +133,15 @@
         copy.wait()
 
 
-def distant_kernel(hg_ref, w_ref, after_ref, out_ref):
-    per, _, cut = w_ref.shape
-    for i in range(per):
-        out_ref[:, i * cut : (i + 1) * cut] = dot(hg_ref[...], w_ref[i]).astype(BF)
-
-
-def far_kernel(mine_ref, diag_ref, got_ref, after_ref, out_ref):
-    width = mine_ref.shape[1]
-    sum_kernel(mine_ref, got_ref.at[:, :width], out_ref.at[:, :width])
+def block_kernel(hg_ref, w_ref, after_ref, out_ref):
+    out_ref[...] = dot(hg_ref[...], w_ref[...]).astype(BF)
+
+
+def far_kernel(first_ref, rest_ref, diag_ref, got_ref, out_ref):
+    cut = first_ref.shape[1]
+    width = 2 * cut
+    sum_kernel(first_ref, got_ref.at[:, :cut], out_ref.at[:, :cut])
+    sum_kernel(rest_ref, got_ref.at[:, cut:width], out_ref.at[:, cut:width])
     sum_kernel(diag_ref.at[:, width:], got_ref.at[:, width:], out_ref.at[:, width:])
 
 
@@ -355,9 +357,9 @@
             )
 
         per = width // cut
-        diag, columns = call(
+        diag, *columns = call(
             diag_kernel,
-            [wide, shape((per, width, cut), BF)],
+            [wide] + [shape((width, cut), BF)] * per,
             [VMEM, VMEM, HBM, VMEM, ANY],
             (gained, first_columns, keep_hbm(base_weight), low, low_u),
             "query_diag",
@@ -365,12 +367,14 @@
         )
         diag_got = swap(diag, "tp", n_tp, 1)
 
+        block = shape((count, cut), BF)
+        distant_first = call(block_kernel, block, [VMEM] * 2 + [ANY], (gained, columns[0], diag), "distant_first")
         half = width // 2
         keep_a, send_a = call(
             functools.partial(grad_a_kernel, path_a[0]),
             [shape((half, rank), F32), shape((half, rank), BF)],
             [VMEM] * 3 + [ANY],
-            (inputs, low_v, far_v, diag),
+            (inputs, low_v, far_v, distant_first),
             "grad_a",
         )
         keep_b, send_b = call(
@@ -380,8 +384,8 @@
             (cotangent, low_u, far_u, send_a),
             "grad_b",
         )
-        distant = call(distant_kernel, tall, [VMEM, VMEM, ANY], (gained, columns, send_b), "query_distant")
-        far = call(far_kernel, wide, [VMEM] * 3 + [ANY], (distant, diag, diag_got, send_b), "far")
+        distant_rest = call(block_kernel, block, [VMEM] * 2 + [ANY], (gained, columns[1], send_b), "distant_rest")
+        far = call(far_kernel, wide, [VMEM] * 4, (distant_first, distant_rest, diag, diag_got), "far")
         far_got = swap(far, "tp", n_tp, 2)
 
         def step(mine, send, way, after, passed, name):

time: 49.6 us -> 49.7 us (level)
  waiting for transfers between devices: 13.9 us -> 13 us
  Pallas kernels: 16.3 us -> 16.8 us
  starting transfers between devices: 17.1 us -> 17.6 us
    ppermute x17, waiting for transfers between devices: 13.9 us -> 13 us  [swap(): return lax.ppermute(x, axis, [(i, i ^ k) for i in range(n)])]
    ppermute x17, starting transfers between devices: 17.1 us -> 17.6 us  [swap(): return lax.ppermute(x, axis, [(i, i ^ k) for i in range(n)])]
    pallas_call x24 -> x25, Pallas kernels: 16.3 us -> 16.8 us  [call(): pl.pallas_call(kernel, out_shape=outs, in_specs=in_specs, out_specs=out_s...]
  transfers between devices with their start and end apart: 17 -> 17, of which waited for: 9 -> 8; matrix products, arithmetic and copies ran while one was open for 3% -> 3% of each run, Pallas kernels for 24% -> 25%
where the time goes in v16:
time: 49.7 us; the launch traced here: 49.5 us
  starting transfers between devices  17.6 us (35%)
  Pallas kernels  16.8 us (34%)
  waiting for transfers between devices  13 us (26%)
  other arithmetic  1.28 us (3%)
  between operations  0.86 us (2%)
    ppermute x17, starting transfers between devices, swap(): return lax.ppermute(x, axis, [(i, i ^ k) for i in range(n)])  17.6 us
    pallas_call x25, Pallas kernels, call(): pl.pallas_call(kernel, out_shape=outs, in_specs=in_specs, out_specs=out_s...  16.8 us
    ppermute x17, waiting for transfers between devices, swap(): return lax.ppermute(x, axis, [(i, i ^ k) for i in range(n)])  13 us
  transfers between devices with their start and end apart: 17, of which 8 were waited for; matrix products, arithmetic and copies ran while one was open for 3% of the time, Pallas kernels for 25%

profile of v16, /device:TPU:0, one launch (start us, length us, event | category | flops | bytes accessed | tf_op | source)
XLA Modules:
  0.0 49.5 jit_solution(6473798671398194333)
XLA Ops:
  0.6 2.4 %rank_v.1 = (bf16[384,128]{1,0:T(8,128)(2,1)S(1)}, bf16[384,1024]{1,0:T(8,128)(2,1)S(1)}, bf16[384,1024]{1,0:T(8,128)(2,1)S(1)}, bf16[1024,128]{1,0:T(8,128)(2,1...) custom-call(bf16[384,1024]{1,0:T(8,128)(2,1)} %x_hbm.1, bf16[384,1024]{1,0:T(8,128)(2,1)} %v_hbm.1, ...), custom_call_target="tpu_custom_call" | custom-call | flops 2760000000 | tf_op jit(solution)/shard_map/rank_v/pallas_call | solution.py:264
  3.0 0.5 %collective-permute-start = (bf16[384,128]{1,0:T(8,128)(2,1)S(1)}, bf16[384,128]{1,0:T(8,128)(2,1)S(1)}, u32[]{:S(2)}, u32[]{:S(2)}) collective-permute-start(bf16[384,128]{1,0:T(8,128)(2,1)S(1)} %get-tuple-element.35.x_ref), channel_id=1, source_target_pairs={{0,1},{1,0},{2,3},{3,2},{4,5},{5,4},{6,7},{7,6},{8,9},{9,8},{10,11... | collective-permute-start | bytes 294920 | tf_op jit(solution)/shard_map/ppermute | solution.py:35
  3.6 0.4 rank_u.1.x_ref
  3.9 0.1 collective-permute-start.2
  4.1 0.6 %prep.1 = (bf16[512,1024]{1,0:T(8,128)(2,1)S(1)}, bf16[512,128]{1,0:T(8,128)(2,1)S(1)}, f32[8,128]{1,0:T(8,128)S(1)}) custom-call(bf16[512,1024]{1,0:T(8,128)(2,1)S(1)} %get-tuple-element.31.h_ref, f32[1,1024]{1,0:T(1,128)S(1)} %bitcast.8, bf16[1024,128]{1,0:T(8,128)(2,1)S(1)} %get-tuple-element.32.a16_ref), custom_call_target="tpu_custom_call" | custom-call | flops 690000000 | tf_op jit(solution)/shard_map/prep/pallas_call | solution.py:264
  4.6 0.0 collective-permute-done.got_ref
  4.7 3.0 %collective-permute-start.1 = (bf16[384,128]{1,0:T(8,128)(2,1)S(1)}, bf16[384,128]{1,0:T(8,128)(2,1)S(1)}, u32[]{:S(2)}, u32[]{:S(2)}) collective-permute-start(bf16[384,128]{1,0:T(8,128)(2,1)S(1)} %low_v.1.after_ref.s_ref), channel_id=1, source_target_pairs={{0,2},{1,3},{2,0},{3,1},{4,6},{5,7},{6,4},{7,5},{8,10},{9,11},{10,... | collective-permute-start | bytes 294920 | tf_op jit(solution)/shard_map/ppermute | solution.py:35
  7.7 0.3 collective-permute-start.4
  8.1 2.3 %query_diag.1 = (bf16[512,1152]{1,0:T(8,128)(2,1)S(1)}, bf16[1024,512]{1,0:T(8,128)(2,1)S(1)}, bf16[1024,512]{1,0:T(8,128)(2,1)S(1)}) custom-call(bf16[512,1024]{1,0:T(8,128)(2,1)S(1)} %get-tuple-element.33.hg_ref, bf16[1024,512]{1,0:T(8,128)(2,1)S(1)} %get-tuple-element.37.w_ref, bf16[1024,4096]{1,0:T(8,128)(2,1)} %w_hbm.7, ...), custom_call_target="tpu_custom_call" | custom-call | flops 46000001024 | tf_op jit(solution)/shard_map/query_diag/pallas_call | solution.py:264
  10.4 0.1 collective-permute-start.5
  10.5 0.7 %distant_first.1.after_ref.first_ref = bf16[512,512]{1,0:T(8,128)(2,1)S(1)} custom-call(bf16[512,1024]{1,0:T(8,128)(2,1)S(1)} %get-tuple-element.33.hg_ref, bf16[1024,512]{1,0:T(8,128)(2,1)S(1)} %get-tuple-element.38.w_ref, bf16[512,1152]{1,0:T(8,128)(2,1)S(1)} %get-tuple-element.39.after_ref.diag_ref), custom_call_target="tpu_custom_call" | custom-call | flops 11500000 | tf_op jit(solution)/shard_map/distant_first/pallas_call | solution.py:264
  11.2 0.0 collective-permute-done.1.r_ref
  11.2 0.4 grad_a.1
  11.7 2.1 %collective-permute-start.3 = (bf16[512,128]{1,0:T(8,128)(2,1)S(1)}, bf16[512,128]{1,0:T(8,128)(2,1)S(1)}, u32[]{:S(2)}, u32[]{:S(2)}) collective-permute-start(bf16[512,128]{1,0:T(8,128)(2,1)S(1)} %get-tuple-element.41.after_ref), channel_id=1, source_target_pairs={{0,4},{4,0},{8,12},{12,8},{1,5},{5,1},{9,13},{13,9},{2,6},{6,2},{1... | collective-permute-start | bytes 393224 | tf_op jit(solution)/shard_map/ppermute | solution.py:35
  13.7 0.3 grad_b.1
  14.1 1.6 %collective-permute-start.7 = (bf16[512,128]{1,0:T(8,128)(2,1)S(1)}, bf16[512,128]{1,0:T(8,128)(2,1)S(1)}, u32[]{:S(2)}, u32[]{:S(2)}) collective-permute-start(bf16[512,128]{1,0:T(8,128)(2,1)S(1)} %get-tuple-element.44.after_ref), channel_id=1, source_target_pairs={{0,16},{16,0},{1,17},{17,1},{2,18},{18,2},{3,19},{19,3},{4,20},{20... | collective-permute-start | bytes 393224 | tf_op jit(solution)/shard_map/ppermute | solution.py:35
  15.7 0.7 %distant_rest.1.rest_ref = bf16[512,512]{1,0:T(8,128)(2,1)S(1)} custom-call(bf16[512,1024]{1,0:T(8,128)(2,1)S(1)} %get-tuple-element.33.hg_ref, bf16[1024,512]{1,0:T(8,128)(2,1)S(1)} %get-tuple-element.42.w_ref, bf16[512,128]{1,0:T(8,128)(2,1)S(1)} %get-tuple-element.44.after_ref), custom_call_target="tpu_custom_call" | custom-call | flops 11500000 | tf_op jit(solution)/shard_map/distant_rest/pallas_call | solution.py:264
  16.4 0.0 collective-permute-done.5.got_ref
  16.4 0.3 far.1.rest_0_.far_ref
  16.7 1.7 %collective-permute-start.10 = (bf16[512,1152]{1,0:T(8,128)(2,1)S(1)}, bf16[512,1152]{1,0:T(8,128)(2,1)S(1)}, u32[]{:S(2)}, u32[]{:S(2)}) collective-permute-start(bf16[512,1152]{1,0:T(8,128)(2,1)S(1)} %far.1.rest_0_.far_ref), channel_id=1, source_target_pairs={{0,2},{1,3},{2,0},{3,1},{4,6},{5,7},{6,4},{7,5},{8,10},{9,11},{10,... | collective-permute-start | bytes 3538952 | tf_op jit(solution)/shard_map/ppermute | solution.py:35
  18.4 2.7 %collective-permute-start.6 = (bf16[512,128]{1,0:T(8,128)(2,1)S(1)}, bf16[512,128]{1,0:T(8,128)(2,1)S(1)}, u32[]{:S(2)}, u32[]{:S(2)}) collective-permute-start(bf16[512,128]{1,0:T(8,128)(2,1)S(1)} %step_a0.1.rest_0_.mine_ref), channel_id=1, source_target_pairs={{0,8},{4,12},{8,0},{12,4},{1,9},{5,13},{9,1},{13,5},{2,10},{6,14},... | collective-permute-start | bytes 393224 | tf_op jit(solution)/shard_map/ppermute | solution.py:35
  21.1 1.1 %collective-permute-start.8 = (bf16[512,128]{1,0:T(8,128)(2,1)S(1)}, bf16[512,128]{1,0:T(8,128)(2,1)S(1)}, u32[]{:S(2)}, u32[]{:S(2)}) collective-permute-start(bf16[512,128]{1,0:T(8,128)(2,1)S(1)} %step_b1.1.mine_ref.rest_0_.after_ref), channel_id=1, source_target_pairs={{0,4},{4,0},{8,12},{12,8},{1,5},{5,1},{9,13},{13,9},{2,6},{6,2},{1... | collective-permute-start | bytes 393224 | tf_op jit(solution)/shard_map/ppermute | solution.py:35
  22.2 2.7 %query_beside.1.rest_1_ = bf16[512,1024]{1,0:T(8,128)(2,1)S(1)} custom-call(bf16[512,1024]{1,0:T(8,128)(2,1)S(1)} %get-tuple-element.33.hg_ref, bf16[1024,4096]{1,0:T(8,128)(2,1)} %w_hbm.7, bf16[512,128]{1,0:T(8,128)(2,1)S(1)} %step_b1.1.mine_ref.rest_0_.after_ref), custom_call_target="tpu_custom_call" | custom-call | flops 3104999936 | tf_op jit(solution)/shard_map/query_beside/pallas_call | solution.py:264
  24.9 2.8 %collective-permute-done.8.got_ref = bf16[512,128]{1,0:T(8,128)(2,1)S(1)} collective-permute-done((bf16[512,128]{1,0:T(8,128)(2,1)S(1)}, bf16[512,128]{1,0:T(8,128)(2,1)S(1)}, u32[]{:S(2)}, u32[]{:S(2)}) %collective-permute-start.8) | collective-permute-done | bytes 131104 | tf_op jit(solution)/shard_map/ppermute | solution.py:35
  27.7 0.6 %collective-permute-start.13 = (bf16[512,128]{1,0:T(8,128)(2,1)S(1)}, bf16[512,128]{1,0:T(8,128)(2,1)S(1)}, u32[]{:S(2)}, u32[]{:S(2)}) collective-permute-start(bf16[512,128]{1,0:T(8,128)(2,1)S(1)} %step_b3.1.rest_0_.mine_ref), channel_id=1, source_target_pairs={{0,8},{4,12},{8,0},{12,4},{1,9},{5,13},{9,1},{13,5},{2,10},{6,14},... | collective-permute-start | bytes 393224 | tf_op jit(solution)/shard_map/ppermute | solution.py:35
  28.3 1.5 %collective-permute-start.11 = (bf16[512,128]{1,0:T(8,128)(2,1)S(1)}, bf16[512,128]{1,0:T(8,128)(2,1)S(1)}, u32[]{:S(2)}, u32[]{:S(2)}) collective-permute-start(bf16[512,128]{1,0:T(8,128)(2,1)S(1)} %get-tuple-element.46.after_ref.mine_ref), channel_id=1, source_target_pairs={{0,16},{16,0},{1,17},{17,1},{2,18},{18,2},{3,19},{19,3},{4,20},{20... | collective-permute-start | bytes 393224 | tf_op jit(solution)/shard_map/ppermute | solution.py:35
  29.8 2.7 %query_close.1.rest_0_.mine_ref = bf16[512,1024]{1,0:T(8,128)(2,1)S(1)} custom-call(bf16[512,1024]{1,0:T(8,128)(2,1)S(1)} %get-tuple-element.33.hg_ref, bf16[1024,4096]{1,0:T(8,128)(2,1)} %w_hbm.7, bf16[512,128]{1,0:T(8,128)(2,1)S(1)} %get-tuple-element.46.after_ref.mine_ref), custom_call_target="tpu_custom_call" | custom-call | flops 3104999936 | tf_op jit(solution)/shard_map/query_close/pallas_call | solution.py:264
  32.5 0.0 copy-start.2
  32.5 0.8 %collective-permute-done.11.got_ref = bf16[512,128]{1,0:T(8,128)(2,1)S(1)} collective-permute-done((bf16[512,128]{1,0:T(8,128)(2,1)S(1)}, bf16[512,128]{1,0:T(8,128)(2,1)S(1)}, u32[]{:S(2)}, u32[]{:S(2)}) %collective-permute-start.11) | collective-permute-done | bytes 131104 | tf_op jit(solution)/shard_map/ppermute | solution.py:35
  33.4 0.6 %collective-permute-start.12 = (bf16[512,128]{1,0:T(8,128)(2,1)S(1)}, bf16[512,128]{1,0:T(8,128)(2,1)S(1)}, u32[]{:S(2)}, u32[]{:S(2)}) collective-permute-start(bf16[512,128]{1,0:T(8,128)(2,1)S(1)} %step_a6.1.rest_0_.mine_a), channel_id=1, source_target_pairs={{0,4},{4,0},{8,12},{12,8},{1,5},{5,1},{9,13},{13,9},{2,6},{6,2},{1... | collective-permute-start | bytes 393224 | tf_op jit(solution)/shard_map/ppermute | solution.py:35
  34.0 1.0 %collective-permute-done.13.got_ref = bf16[512,128]{1,0:T(8,128)(2,1)S(1)} collective-permute-done((bf16[512,128]{1,0:T(8,128)(2,1)S(1)}, bf16[512,128]{1,0:T(8,128)(2,1)S(1)}, u32[]{:S(2)}, u32[]{:S(2)}) %collective-permute-start.13) | collective-permute-done | bytes 131104 | tf_op jit(solution)/shard_map/ppermute | solution.py:35
  35.1 0.8 %collective-permute-start.14 = (bf16[512,128]{1,0:T(8,128)(2,1)S(1)}, bf16[512,128]{1,0:T(8,128)(2,1)S(1)}, u32[]{:S(2)}, u32[]{:S(2)}) collective-permute-start(bf16[512,128]{1,0:T(8,128)(2,1)S(1)} %step_b7.1.after_ref.mine_b), channel_id=1, source_target_pairs={{0,16},{16,0},{1,17},{17,1},{2,18},{18,2},{3,19},{19,3},{4,20},{20... | collective-permute-start | bytes 393224 | tf_op jit(solution)/shard_map/ppermute | solution.py:35
  35.9 1.0 %multiply_cosine_fusion.1 = (f32[256,64]{1,0:T(8,128)S(1)}, f32[256,64]{1,0:T(8,128)S(1)}, f32[256,64]{1,0:T(8,128)S(1)}, f32[256,64]{1,0:T(8,128)S(1)}, f32[256,64]{1,0:T(8,128)S(1)}, /*index=5*/f32[256,64]{1,0:T(8,128)S(1)}) fusion(f32[64]{0:T(128)S(1)} %multiply_power_fusion, f32[256]{0:T(256)S(1)} %bitcast.6, f32[256]{0:T(256)S(1)} %broadcast_add_fusion), kind=kLoop, calls=%fused_computation.4 | loop fusion | flops 65536 | bytes 395520 | tf_op jit(solution)/shard_map/cos | solution.py:285
  36.9 0.1 maximum_maximum_fusion.after_ref.sin_ref
  37.0 1.5 %collective-permute-done.12.got_a = bf16[512,128]{1,0:T(8,128)(2,1)S(1)} collective-permute-done((bf16[512,128]{1,0:T(8,128)(2,1)S(1)}, bf16[512,128]{1,0:T(8,128)(2,1)S(1)}, u32[]{:S(2)}, u32[]{:S(2)}) %collective-permute-start.12) | collective-permute-done | bytes 131104 | tf_op jit(solution)/shard_map/ppermute | solution.py:35
  38.5 0.5 update.1
  39.0 1.1 %collective-permute-done.14.got_b = bf16[512,128]{1,0:T(8,128)(2,1)S(1)} collective-permute-done((bf16[512,128]{1,0:T(8,128)(2,1)S(1)}, bf16[512,128]{1,0:T(8,128)(2,1)S(1)}, u32[]{:S(2)}, u32[]{:S(2)}) %collective-permute-start.14) | collective-permute-done | bytes 131104 | tf_op jit(solution)/shard_map/ppermute | solution.py:35
  40.1 0.2 pack.1
  40.3 0.1 collective-permute-start.15
  40.4 1.3 %collective-permute-done.15.b_ref = bf16[544,128]{1,0:T(8,128)(2,1)S(1)} collective-permute-done((bf16[544,128]{1,0:T(8,128)(2,1)S(1)}, bf16[544,128]{1,0:T(8,128)(2,1)S(1)}, u32[]{:S(2)}, u32[]{:S(2)}) %collective-permute-start.15) | collective-permute-done | bytes 139296 | tf_op jit(solution)/shard_map/ppermute | solution.py:35
  41.8 0.8 %collective-permute-start.16 = (bf16[544,128]{1,0:T(8,128)(2,1)S(1)}, bf16[544,128]{1,0:T(8,128)(2,1)S(1)}, u32[]{:S(2)}, u32[]{:S(2)}) collective-permute-start(bf16[544,128]{1,0:T(8,128)(2,1)S(1)} %merge.1.after_ref.s_ref), channel_id=1, source_target_pairs={{0,2},{1,3},{2,0},{3,1},{4,6},{5,7},{6,4},{7,5},{8,10},{9,11},{10,... | collective-permute-start | bytes 417800 | tf_op jit(solution)/shard_map/ppermute | solution.py:35
  42.6 0.1 maximum_maximum_fusion.1.cos_ref
  42.7 0.0 copy-start
  42.7 0.0 copy-start.1
  42.7 1.6 %collective-permute-done.10.far_got = bf16[512,1152]{1,0:T(8,128)(2,1)S(1)} collective-permute-done((bf16[512,1152]{1,0:T(8,128)(2,1)S(1)}, bf16[512,1152]{1,0:T(8,128)(2,1)S(1)}, u32[]{:S(2)}, u32[]{:S(2)}) %collective-permute-start.10) | collective-permute-done | bytes 1179680 | tf_op jit(solution)/shard_map/ppermute | solution.py:35
  44.3 0.5 base.1
  44.8 2.8 %collective-permute-done.16.r_ref = bf16[544,128]{1,0:T(8,128)(2,1)S(1)} collective-permute-done((bf16[544,128]{1,0:T(8,128)(2,1)S(1)}, bf16[544,128]{1,0:T(8,128)(2,1)S(1)}, u32[]{:S(2)}, u32[]{:S(2)}) %collective-permute-start.16) | collective-permute-done | bytes 139296 | tf_op jit(solution)/shard_map/ppermute | solution.py:35
  47.6 2.0 %final.1 = (f32[1024,128]{1,0:T(8,128)}, f32[128,1024]{1,0:T(8,128)}, bf16[512,1024]{1,0:T(8,128)(2,1)}) custom-call(f32[512,1024]{1,0:T(8,128)S(1)} %get-tuple-element.52.base_ref, f32[512,128]{1,0:T(8,128)S(1)} %get-tuple-element.53.low_ref, bf16[544,128]{1,0:T(8,128)(2,1)S(1)} %merge.1.after_ref.s_ref, ...), custom_call_target="tpu_custom_call" | custom-call | flops 2070000000 | tf_op jit(solution)/shard_map/final/pallas_call | solution.py:264
  (24 shorter events, 0.3 us)
Async XLA Ops:
  0.6 3.4 %copy-start.3 = (f32[1024]{0:T(1024)S(1)}, f32[1024]{0:T(1024)}, u32[]{:S(2)}) copy-start(f32[1024]{0:T(1024)} %param.14) | copy-start | bytes 12292
  3.0 1.6 %collective-permute-start = (bf16[384,128]{1,0:T(8,128)(2,1)S(1)}, bf16[384,128]{1,0:T(8,128)(2,1)S(1)}, u32[]{:S(2)}, u32[]{:S(2)}) collective-permute-start(bf16[384,128]{1,0:T(8,128)(2,1)S(1)} %get-tuple-element.35.x_ref), channel_id=1, source_target_pairs={{0,1},{1,0},{2,3},{3,2},{4,5},{5,4},{6,7},{7,6},{8,9},{9,8},{10,11... | collective-permute-start | bytes 294920 | tf_op jit(solution)/shard_map/ppermute | solution.py:35
  3.9 3.8 %collective-permute-start.2 = (bf16[384,128]{1,0:T(8,128)(2,1)S(1)}, bf16[384,128]{1,0:T(8,128)(2,1)S(1)}, u32[]{:S(2)}, u32[]{:S(2)}) collective-permute-start(bf16[384,128]{1,0:T(8,128)(2,1)S(1)} %rank_u.1.x_ref), channel_id=1, source_target_pairs={{0,1},{1,0},{2,3},{3,2},{4,5},{5,4},{6,7},{7,6},{8,9},{9,8},{10,11... | collective-permute-start | bytes 294920 | tf_op jit(solution)/shard_map/ppermute | solution.py:35
  4.7 6.6 %collective-permute-start.1 = (bf16[384,128]{1,0:T(8,128)(2,1)S(1)}, bf16[384,128]{1,0:T(8,128)(2,1)S(1)}, u32[]{:S(2)}, u32[]{:S(2)}) collective-permute-start(bf16[384,128]{1,0:T(8,128)(2,1)S(1)} %low_v.1.after_ref.s_ref), channel_id=1, source_target_pairs={{0,2},{1,3},{2,0},{3,1},{4,6},{5,7},{6,4},{7,5},{8,10},{9,11},{10,... | collective-permute-start | bytes 294920 | tf_op jit(solution)/shard_map/ppermute | solution.py:35
  7.7 6.0 %collective-permute-start.4 = (bf16[384,128]{1,0:T(8,128)(2,1)S(1)}, bf16[384,128]{1,0:T(8,128)(2,1)S(1)}, u32[]{:S(2)}, u32[]{:S(2)}) collective-permute-start(bf16[384,128]{1,0:T(8,128)(2,1)S(1)} %low_u.1.after_ref.s_ref), channel_id=1, source_target_pairs={{0,2},{1,3},{2,0},{3,1},{4,6},{5,7},{6,4},{7,5},{8,10},{9,11},{10,... | collective-permute-start | bytes 294920 | tf_op jit(solution)/shard_map/ppermute | solution.py:35
  10.4 6.0 %collective-permute-start.5 = (bf16[512,1152]{1,0:T(8,128)(2,1)S(1)}, bf16[512,1152]{1,0:T(8,128)(2,1)S(1)}, u32[]{:S(2)}, u32[]{:S(2)}) collective-permute-start(bf16[512,1152]{1,0:T(8,128)(2,1)S(1)} %get-tuple-element.39.after_ref.diag_ref), channel_id=1, source_target_pairs={{0,1},{1,0},{2,3},{3,2},{4,5},{5,4},{6,7},{7,6},{8,9},{9,8},{10,11... | collective-permute-start | bytes 3538952 | tf_op jit(solution)/shard_map/ppermute | solution.py:35
  11.7 6.7 %collective-permute-start.3 = (bf16[512,128]{1,0:T(8,128)(2,1)S(1)}, bf16[512,128]{1,0:T(8,128)(2,1)S(1)}, u32[]{:S(2)}, u32[]{:S(2)}) collective-permute-start(bf16[512,128]{1,0:T(8,128)(2,1)S(1)} %get-tuple-element.41.after_ref), channel_id=1, source_target_pairs={{0,4},{4,0},{8,12},{12,8},{1,5},{5,1},{9,13},{13,9},{2,6},{6,2},{1... | collective-permute-start | bytes 393224 | tf_op jit(solution)/shard_map/ppermute | solution.py:35
  14.1 7.0 %collective-permute-start.7 = (bf16[512,128]{1,0:T(8,128)(2,1)S(1)}, bf16[512,128]{1,0:T(8,128)(2,1)S(1)}, u32[]{:S(2)}, u32[]{:S(2)}) collective-permute-start(bf16[512,128]{1,0:T(8,128)(2,1)S(1)} %get-tuple-element.44.after_ref), channel_id=1, source_target_pairs={{0,16},{16,0},{1,17},{17,1},{2,18},{18,2},{3,19},{19,3},{4,20},{20... | collective-permute-start | bytes 393224 | tf_op jit(solution)/shard_map/ppermute | solution.py:35
  16.7 27.6 %collective-permute-start.10 = (bf16[512,1152]{1,0:T(8,128)(2,1)S(1)}, bf16[512,1152]{1,0:T(8,128)(2,1)S(1)}, u32[]{:S(2)}, u32[]{:S(2)}) collective-permute-start(bf16[512,1152]{1,0:T(8,128)(2,1)S(1)} %far.1.rest_0_.far_ref), channel_id=1, source_target_pairs={{0,2},{1,3},{2,0},{3,1},{4,6},{5,7},{6,4},{7,5},{8,10},{9,11},{10,... | collective-permute-start | bytes 3538952 | tf_op jit(solution)/shard_map/ppermute | solution.py:35
  18.4 9.8 %collective-permute-start.6 = (bf16[512,128]{1,0:T(8,128)(2,1)S(1)}, bf16[512,128]{1,0:T(8,128)(2,1)S(1)}, u32[]{:S(2)}, u32[]{:S(2)}) collective-permute-start(bf16[512,128]{1,0:T(8,128)(2,1)S(1)} %step_a0.1.rest_0_.mine_ref), channel_id=1, source_target_pairs={{0,8},{4,12},{8,0},{12,4},{1,9},{5,13},{9,1},{13,5},{2,10},{6,14},... | collective-permute-start | bytes 393224 | tf_op jit(solution)/shard_map/ppermute | solution.py:35
  21.1 6.5 %collective-permute-start.8 = (bf16[512,128]{1,0:T(8,128)(2,1)S(1)}, bf16[512,128]{1,0:T(8,128)(2,1)S(1)}, u32[]{:S(2)}, u32[]{:S(2)}) collective-permute-start(bf16[512,128]{1,0:T(8,128)(2,1)S(1)} %step_b1.1.mine_ref.rest_0_.after_ref), channel_id=1, source_target_pairs={{0,4},{4,0},{8,12},{12,8},{1,5},{5,1},{9,13},{13,9},{2,6},{6,2},{1... | collective-permute-start | bytes 393224 | tf_op jit(solution)/shard_map/ppermute | solution.py:35
  27.7 7.3 %collective-permute-start.13 = (bf16[512,128]{1,0:T(8,128)(2,1)S(1)}, bf16[512,128]{1,0:T(8,128)(2,1)S(1)}, u32[]{:S(2)}, u32[]{:S(2)}) collective-permute-start(bf16[512,128]{1,0:T(8,128)(2,1)S(1)} %step_b3.1.rest_0_.mine_ref), channel_id=1, source_target_pairs={{0,8},{4,12},{8,0},{12,4},{1,9},{5,13},{9,1},{13,5},{2,10},{6,14},... | collective-permute-start | bytes 393224 | tf_op jit(solution)/shard_map/ppermute | solution.py:35
  28.3 5.0 %collective-permute-start.11 = (bf16[512,128]{1,0:T(8,128)(2,1)S(1)}, bf16[512,128]{1,0:T(8,128)(2,1)S(1)}, u32[]{:S(2)}, u32[]{:S(2)}) collective-permute-start(bf16[512,128]{1,0:T(8,128)(2,1)S(1)} %get-tuple-element.46.after_ref.mine_ref), channel_id=1, source_target_pairs={{0,16},{16,0},{1,17},{17,1},{2,18},{18,2},{3,19},{19,3},{4,20},{20... | collective-permute-start | bytes 393224 | tf_op jit(solution)/shard_map/ppermute | solution.py:35
  29.8 12.9 %collective-permute-start.9 = (bf16[512,1024]{1,0:T(8,128)(2,1)S(1)}, bf16[512,1024]{1,0:T(8,128)(2,1)S(1)}, u32[]{:S(2)}, u32[]{:S(2)}) collective-permute-start(bf16[512,1024]{1,0:T(8,128)(2,1)S(1)} %get-tuple-element.47), channel_id=1, source_target_pairs={{0,1},{1,0},{2,3},{3,2},{4,5},{5,4},{6,7},{7,6},{8,9},{9,8},{10,11... | collective-permute-start | bytes 3145736 | tf_op jit(solution)/shard_map/ppermute | solution.py:35
  32.5 3.4 %copy-start.2 = (s32[256]{0:T(256)S(1)}, s32[256]{0:T(256)}, u32[]{:S(2)}) copy-start(s32[256]{0:T(256)} %param.15) | copy-start | bytes 3076
  33.4 5.1 %collective-permute-start.12 = (bf16[512,128]{1,0:T(8,128)(2,1)S(1)}, bf16[512,128]{1,0:T(8,128)(2,1)S(1)}, u32[]{:S(2)}, u32[]{:S(2)}) collective-permute-start(bf16[512,128]{1,0:T(8,128)(2,1)S(1)} %step_a6.1.rest_0_.mine_a), channel_id=1, source_target_pairs={{0,4},{4,0},{8,12},{12,8},{1,5},{5,1},{9,13},{13,9},{2,6},{6,2},{1... | collective-permute-start | bytes 393224 | tf_op jit(solution)/shard_map/ppermute | solution.py:35
  35.1 5.0 %collective-permute-start.14 = (bf16[512,128]{1,0:T(8,128)(2,1)S(1)}, bf16[512,128]{1,0:T(8,128)(2,1)S(1)}, u32[]{:S(2)}, u32[]{:S(2)}) collective-permute-start(bf16[512,128]{1,0:T(8,128)(2,1)S(1)} %step_b7.1.after_ref.mine_b), channel_id=1, source_target_pairs={{0,16},{16,0},{1,17},{17,1},{2,18},{18,2},{3,19},{19,3},{4,20},{20... | collective-permute-start | bytes 393224 | tf_op jit(solution)/shard_map/ppermute | solution.py:35
  40.3 1.4 %collective-permute-start.15 = (bf16[544,128]{1,0:T(8,128)(2,1)S(1)}, bf16[544,128]{1,0:T(8,128)(2,1)S(1)}, u32[]{:S(2)}, u32[]{:S(2)}) collective-permute-start(bf16[544,128]{1,0:T(8,128)(2,1)S(1)} %get-tuple-element.51.a_ref), channel_id=1, source_target_pairs={{0,1},{1,0},{2,3},{3,2},{4,5},{5,4},{6,7},{7,6},{8,9},{9,8},{10,11... | collective-permute-start | bytes 417800 | tf_op jit(solution)/shard_map/ppermute | solution.py:35
  41.8 5.8 %collective-permute-start.16 = (bf16[544,128]{1,0:T(8,128)(2,1)S(1)}, bf16[544,128]{1,0:T(8,128)(2,1)S(1)}, u32[]{:S(2)}, u32[]{:S(2)}) collective-permute-start(bf16[544,128]{1,0:T(8,128)(2,1)S(1)} %merge.1.after_ref.s_ref), channel_id=1, source_target_pairs={{0,2},{1,3},{2,0},{3,1},{4,6},{5,7},{6,4},{7,5},{8,10},{9,11},{10,... | collective-permute-start | bytes 417800 | tf_op jit(solution)/shard_map/ppermute | solution.py:35
  42.7 4.9 %copy-start = (f32[1024,128]{1,0:T(8,128)S(1)}, f32[1024,128]{1,0:T(8,128)}, u32[]{:S(2)}) copy-start(f32[1024,128]{1,0:T(8,128)} %a_ref.1) | copy-start | bytes 1572868
  42.7 4.9 %copy-start.1 = (f32[128,1024]{1,0:T(8,128)S(1)}, f32[128,1024]{1,0:T(8,128)}, u32[]{:S(2)}) copy-start(f32[128,1024]{1,0:T(8,128)} %b_ref.1) | copy-start | bytes 1572868

commit v17 on v15

--- a/solution.py
+++ b/solution.py
@@ -143,10 +143,8 @@
     sum_kernel(diag_ref.at[:, width:], got_ref.at[:, width:], out_ref.at[:, width:])
 
 
-def merge_kernel(a_ref, b_ref, out_ref):
-    count = a_ref.shape[0] - EXTRA
-    out_ref[:count] = (a_ref[:count].astype(F32) + b_ref[:count].astype(F32)).astype(BF)
-    out_ref[count:] = split_terms(join_terms(a_ref[count:]) + join_terms(b_ref[count:]))
+def merge_kernel(a_ref, b_ref, after_ref, out_ref):
+    out_ref[...] = split_terms(join_terms(a_ref[...]) + join_terms(b_ref[...]))
 
 
 def halves(axis, bit, size):
@@ -201,12 +199,10 @@
     squares_ref[1] = square_sum(mine_b)
 
 
-def pack_kernel(way, low_ref, sums_ref, squares_ref, mine_b, got_b, pack_ref, gb_ref):
-    count = low_ref.shape[0]
-    pack_ref[:count] = low_ref[...]
+def norm_kernel(way, sums_ref, squares_ref, mine_b, got_b, after_ref, norm_ref, gb_ref):
     row = lax.broadcasted_iota(jnp.int32, (8, LANES), 0)
     squares = squares_ref[0] + (squares_ref[1] + square_sum(got_b))
-    pack_ref[count:] = split_terms(jnp.where(row == 7, squares, sums_ref[...]))
+    norm_ref[...] = split_terms(jnp.where(row == 7, squares, sums_ref[...]))
     join(*way, mine_b, got_b, gb_ref)
 
 
@@ -218,11 +214,11 @@
 
 
 def final_kernel(
-    base_ref, low_ref, s_ref, r_ref, ga_ref, gb_ref, a_ref, b_ref, cos_ref, sin_ref,
+    base_ref, low_ref, s_ref, r_ref, sn_ref, rn_ref, ga_ref, gb_ref, a_ref, b_ref, cos_ref, sin_ref,
     a_hbm, b_hbm, q_hbm, new_a, new_b, half_b, out, sems,
 ):
     count, width = base_ref.shape
-    total = join_terms(s_ref[count:]) + join_terms(r_ref[count:])
+    total = join_terms(sn_ref[...]) + join_terms(rn_ref[...])
     rate = (LEARN * lax.rsqrt(total + NORM_EPS))[7:8]
     scales = lax.rsqrt(total / D + EPS)
     for c in blocks_of(width):
@@ -254,7 +250,9 @@
     return pltpu.with_memory_space_constraint(x, pltpu.HBM)
 
 
-WEIGHTS = {"rank_v": 2.4, "prep": 0.6, "query_diag": 40.0, "query_beside": 2.7, "query_close": 2.7, "grad_b": 40.0, "final": 1.8}
+WEIGHTS = {
+    "rank_v": 2.4, "prep": 0.6, "query_diag": 40.0, "query_beside": 2.7, "query_close": 2.7, "base": 1.0, "grad_b": 40.0, "final": 1.8,
+}
 FLOPS_PER_WEIGHT = 1_150_000_000
 
 
@@ -423,17 +421,23 @@
             (gained, mine_a, cross(mine_a, *path_a[-1]), mine_b, after),
             "update",
         )
-        step_pack, grad_b = call(
-            functools.partial(pack_kernel, path_b[-1]),
-            [shape((count + EXTRA, rank), BF), shape((width, rank), BF)],
-            [VMEM] * 5,
-            (step_low, sums, squares, mine_b, cross(mine_b, *path_b[-1])),
-            "pack",
-        )
-        step_got = swap(step_pack, "tp", n_tp, 1)
-        step_sum = call(merge_kernel, shape((count + EXTRA, rank), BF), [VMEM] * 2, (step_pack, step_got), "merge")
+        step_got = swap(step_low, "tp", n_tp, 1)
+        norm, grad_b = call(
+            functools.partial(norm_kernel, path_b[-1]),
+            [shape((EXTRA, LANES), BF), shape((width, rank), BF)],
+            [VMEM] * 4 + [ANY],
+            (sums, squares, mine_b, cross(mine_b, *path_b[-1]), step_low),
+            "norm",
+        )
+        norm_got = swap(norm, "tp", n_tp, 1)
+        step_sum = call(
+            part_kernel, shape((count, rank), BF), [VMEM] * 2 + [ANY], (step_low, step_got, norm), "merge"
+        )
         step_far = swap(step_sum, "tp", n_tp, 2)
-
+        norm_sum = call(
+            merge_kernel, shape((EXTRA, LANES), BF), [VMEM] * 2 + [ANY], (norm, norm_got, step_sum), "norm_merge"
+        )
+        norm_far = swap(norm_sum, "tp", n_tp, 2)
         base, low_all = call(
             base_kernel,
             [shape((count, width), F32), shape((count, rank), F32)],
@@ -444,8 +448,8 @@
         new_a, new_b, queries = call(
             final_kernel,
             [shape((width, rank), F32), shape((rank, width), F32), tall],
-            [VMEM] * 10,
-            (base, low_all, step_sum, step_far, grad_a, grad_b, factor_a, factor_b, cos, sin),
+            [VMEM] * 12,
+            (base, low_all, step_sum, step_far, norm_sum, norm_far, grad_a, grad_b, factor_a, factor_b, cos, sin),
             "final",
             [pltpu.VMEM((width, rank), F32), pltpu.VMEM((rank, width), F32),
              pltpu.VMEM((rank, width), BF), pltpu.VMEM((count, width), BF), dma(2 + count // LANES)],

time: 49.6 us -> 49.1 us (0.990)
  waiting for transfers between devices: 13.9 us -> 11.8 us
  starting transfers between devices: 17.1 us -> 18.6 us
    ppermute x17 -> x19, waiting for transfers between devices: 13.9 us -> 11.8 us  [swap(): return lax.ppermute(x, axis, [(i, i ^ k) for i in range(n)])]
    ppermute x17 -> x19, starting transfers between devices: 17.1 us -> 18.6 us  [swap(): return lax.ppermute(x, axis, [(i, i ^ k) for i in range(n)])]
    pallas_call x24 -> x25, Pallas kernels: 16.3 us -> 16.3 us  [call(): pl.pallas_call(kernel, out_shape=outs, in_specs=in_specs, out_specs=out_s...]
  transfers between devices with their start and end apart: 17 -> 19, of which waited for: 9 -> 7; matrix products, arithmetic and copies ran while one was open for 3% -> 3% of each run, Pallas kernels for 24% -> 24%
where the time goes in v17:
time: 49.1 us; the launch traced here: 48.9 us
  starting transfers between devices  18.6 us (38%)
  Pallas kernels  16.3 us (33%)
  waiting for transfers between devices  11.8 us (24%)
  other arithmetic  1.28 us (3%)
  between operations  0.89 us (2%)
    ppermute x19, starting transfers between devices, swap(): return lax.ppermute(x, axis, [(i, i ^ k) for i in range(n)])  18.6 us
    pallas_call x25, Pallas kernels, call(): pl.pallas_call(kernel, out_shape=outs, in_specs=in_specs, out_specs=out_s...  16.3 us
    ppermute x19, waiting for transfers between devices, swap(): return lax.ppermute(x, axis, [(i, i ^ k) for i in range(n)])  11.8 us
    cos x1, other arithmetic, turn_tables(): c, s = (jnp.cos(angle), jnp.sin(angle))  0.99 us
  transfers between devices with their start and end apart: 19, of which 7 were waited for; matrix products, arithmetic and copies ran while one was open for 3% of the time, Pallas kernels for 24%

profile of v17, /device:TPU:0, one launch (start us, length us, event | category | flops | bytes accessed | tf_op | source)
XLA Modules:
  0.0 48.9 jit_solution(11734135618444415630)
XLA Ops:
  0.6 2.4 %rank_v.1 = (bf16[384,128]{1,0:T(8,128)(2,1)S(1)}, bf16[384,1024]{1,0:T(8,128)(2,1)S(1)}, bf16[384,1024]{1,0:T(8,128)(2,1)S(1)}, bf16[1024,128]{1,0:T(8,128)(2,1...) custom-call(bf16[384,1024]{1,0:T(8,128)(2,1)} %x_hbm.1, bf16[384,1024]{1,0:T(8,128)(2,1)} %v_hbm.1, ...), custom_call_target="tpu_custom_call" | custom-call | flops 2760000000 | tf_op jit(solution)/shard_map/rank_v/pallas_call | solution.py:260
  3.0 0.5 %collective-permute-start = (bf16[384,128]{1,0:T(8,128)(2,1)S(1)}, bf16[384,128]{1,0:T(8,128)(2,1)S(1)}, u32[]{:S(2)}, u32[]{:S(2)}) collective-permute-start(bf16[384,128]{1,0:T(8,128)(2,1)S(1)} %get-tuple-element.34.x_ref), channel_id=1, source_target_pairs={{0,1},{1,0},{2,3},{3,2},{4,5},{5,4},{6,7},{7,6},{8,9},{9,8},{10,11... | collective-permute-start | bytes 294920 | tf_op jit(solution)/shard_map/ppermute | solution.py:35
  3.6 0.4 rank_u.1.x_ref
  3.9 0.1 collective-permute-start.2
  4.1 0.6 %prep.1 = (bf16[512,1024]{1,0:T(8,128)(2,1)S(1)}, bf16[512,128]{1,0:T(8,128)(2,1)S(1)}, f32[8,128]{1,0:T(8,128)S(1)}) custom-call(bf16[512,1024]{1,0:T(8,128)(2,1)S(1)} %get-tuple-element.30.h_ref, f32[1,1024]{1,0:T(1,128)S(1)} %bitcast.8, bf16[1024,128]{1,0:T(8,128)(2,1)S(1)} %get-tuple-element.31.a16_ref), custom_call_target="tpu_custom_call" | custom-call | flops 690000000 | tf_op jit(solution)/shard_map/prep/pallas_call | solution.py:260
  4.7 3.0 %collective-permute-start.1 = (bf16[384,128]{1,0:T(8,128)(2,1)S(1)}, bf16[384,128]{1,0:T(8,128)(2,1)S(1)}, u32[]{:S(2)}, u32[]{:S(2)}) collective-permute-start(bf16[384,128]{1,0:T(8,128)(2,1)S(1)} %low_v.1.after_ref.s_ref), channel_id=1, source_target_pairs={{0,2},{1,3},{2,0},{3,1},{4,6},{5,7},{6,4},{7,5},{8,10},{9,11},{10,... | collective-permute-start | bytes 294920 | tf_op jit(solution)/shard_map/ppermute | solution.py:35
  7.7 0.0 collective-permute-done.2.got_ref
  7.7 0.3 collective-permute-start.4
  8.1 2.0 %query_diag.1 = (bf16[512,1152]{1,0:T(8,128)(2,1)S(1)}, bf16[2,1024,512]{2,1,0:T(8,128)(2,1)S(1)}) custom-call(bf16[512,1024]{1,0:T(8,128)(2,1)S(1)} %get-tuple-element.32.hg_ref, bf16[1024,512]{1,0:T(8,128)(2,1)S(1)} %get-tuple-element.36.w_ref, bf16[1024,4096]{1,0:T(8,128)(2,1)} %w_hbm.7, bf16[512,128]{1,0:T(8,128)(2,1)S(1)} %get-tuple-element.35.after_ref.low_ref, ...), custom_call_target="tpu_custom_call" | custom-call | flops 46000001024 | tf_op jit(solution)/shard_map/query_diag/pallas_call | solution.py:260
  10.1 0.1 collective-permute-start.5
  10.2 1.1 %collective-permute-done.1.r_ref = bf16[384,128]{1,0:T(8,128)(2,1)S(1)} collective-permute-done((bf16[384,128]{1,0:T(8,128)(2,1)S(1)}, bf16[384,128]{1,0:T(8,128)(2,1)S(1)}, u32[]{:S(2)}, u32[]{:S(2)}) %collective-permute-start.1) | collective-permute-done | bytes 98336 | tf_op jit(solution)/shard_map/ppermute | solution.py:35
  11.2 0.4 grad_a.1
  11.7 2.1 %collective-permute-start.3 = (bf16[512,128]{1,0:T(8,128)(2,1)S(1)}, bf16[512,128]{1,0:T(8,128)(2,1)S(1)}, u32[]{:S(2)}, u32[]{:S(2)}) collective-permute-start(bf16[512,128]{1,0:T(8,128)(2,1)S(1)} %get-tuple-element.39.after_ref), channel_id=1, source_target_pairs={{0,4},{4,0},{8,12},{12,8},{1,5},{5,1},{9,13},{13,9},{2,6},{6,2},{1... | collective-permute-start | bytes 393224 | tf_op jit(solution)/shard_map/ppermute | solution.py:35
  13.7 0.0 collective-permute-done.4.r_ref
  13.7 0.3 grad_b.1
  14.1 1.5 %collective-permute-start.7 = (bf16[512,128]{1,0:T(8,128)(2,1)S(1)}, bf16[512,128]{1,0:T(8,128)(2,1)S(1)}, u32[]{:S(2)}, u32[]{:S(2)}) collective-permute-start(bf16[512,128]{1,0:T(8,128)(2,1)S(1)} %get-tuple-element.42.after_ref), channel_id=1, source_target_pairs={{0,16},{16,0},{1,17},{17,1},{2,18},{18,2},{3,19},{19,3},{4,20},{20... | collective-permute-start | bytes 393224 | tf_op jit(solution)/shard_map/ppermute | solution.py:35
  15.7 1.2 %query_distant.1.mine_ref = bf16[512,1024]{1,0:T(8,128)(2,1)S(1)} custom-call(bf16[512,1024]{1,0:T(8,128)(2,1)S(1)} %get-tuple-element.32.hg_ref, bf16[2,1024,512]{2,1,0:T(8,128)(2,1)S(1)} %get-tuple-element.40.w_ref, bf16[512,128]{1,0:T(8,128)(2,1)S(1)} %get-tuple-element.42.after_ref), custom_call_target="tpu_custom_call" | custom-call | flops 11500000 | tf_op jit(solution)/shard_map/query_distant/pallas_call | solution.py:260
  16.9 0.3 far.1.rest_0_.far_ref
  17.2 1.7 %collective-permute-start.10 = (bf16[512,1152]{1,0:T(8,128)(2,1)S(1)}, bf16[512,1152]{1,0:T(8,128)(2,1)S(1)}, u32[]{:S(2)}, u32[]{:S(2)}) collective-permute-start(bf16[512,1152]{1,0:T(8,128)(2,1)S(1)} %far.1.rest_0_.far_ref), channel_id=1, source_target_pairs={{0,2},{1,3},{2,0},{3,1},{4,6},{5,7},{6,4},{7,5},{8,10},{9,11},{10,... | collective-permute-start | bytes 3538952 | tf_op jit(solution)/shard_map/ppermute | solution.py:35
  19.0 2.7 %collective-permute-start.6 = (bf16[512,128]{1,0:T(8,128)(2,1)S(1)}, bf16[512,128]{1,0:T(8,128)(2,1)S(1)}, u32[]{:S(2)}, u32[]{:S(2)}) collective-permute-start(bf16[512,128]{1,0:T(8,128)(2,1)S(1)} %step_a0.1.rest_0_.mine_ref), channel_id=1, source_target_pairs={{0,8},{4,12},{8,0},{12,4},{1,9},{5,13},{9,1},{13,5},{2,10},{6,14},... | collective-permute-start | bytes 393224 | tf_op jit(solution)/shard_map/ppermute | solution.py:35
  21.7 0.7 %collective-permute-start.8 = (bf16[512,128]{1,0:T(8,128)(2,1)S(1)}, bf16[512,128]{1,0:T(8,128)(2,1)S(1)}, u32[]{:S(2)}, u32[]{:S(2)}) collective-permute-start(bf16[512,128]{1,0:T(8,128)(2,1)S(1)} %step_b1.1.mine_ref.rest_0_.after_ref), channel_id=1, source_target_pairs={{0,4},{4,0},{8,12},{12,8},{1,5},{5,1},{9,13},{13,9},{2,6},{6,2},{1... | collective-permute-start | bytes 393224 | tf_op jit(solution)/shard_map/ppermute | solution.py:35
  22.4 2.7 %query_beside.1.rest_1_ = bf16[512,1024]{1,0:T(8,128)(2,1)S(1)} custom-call(bf16[512,1024]{1,0:T(8,128)(2,1)S(1)} %get-tuple-element.32.hg_ref, bf16[1024,4096]{1,0:T(8,128)(2,1)} %w_hbm.7, bf16[512,128]{1,0:T(8,128)(2,1)S(1)} %step_b1.1.mine_ref.rest_0_.after_ref), custom_call_target="tpu_custom_call" | custom-call | flops 3104999936 | tf_op jit(solution)/shard_map/query_beside/pallas_call | solution.py:260
  25.1 2.4 %collective-permute-done.8.got_ref = bf16[512,128]{1,0:T(8,128)(2,1)S(1)} collective-permute-done((bf16[512,128]{1,0:T(8,128)(2,1)S(1)}, bf16[512,128]{1,0:T(8,128)(2,1)S(1)}, u32[]{:S(2)}, u32[]{:S(2)}) %collective-permute-start.8) | collective-permute-done | bytes 131104 | tf_op jit(solution)/shard_map/ppermute | solution.py:35
  27.5 0.2 collective-permute-start.13
  27.7 0.1 collective-permute-start.9
  27.8 0.8 %collective-permute-start.11 = (bf16[512,128]{1,0:T(8,128)(2,1)S(1)}, bf16[512,128]{1,0:T(8,128)(2,1)S(1)}, u32[]{:S(2)}, u32[]{:S(2)}) collective-permute-start(bf16[512,128]{1,0:T(8,128)(2,1)S(1)} %get-tuple-element.44.after_ref.mine_ref), channel_id=1, source_target_pairs={{0,16},{16,0},{1,17},{17,1},{2,18},{18,2},{3,19},{19,3},{4,20},{20... | collective-permute-start | bytes 393224 | tf_op jit(solution)/shard_map/ppermute | solution.py:35
  28.5 2.7 %query_close.1.rest_0_.mine_ref = bf16[512,1024]{1,0:T(8,128)(2,1)S(1)} custom-call(bf16[512,1024]{1,0:T(8,128)(2,1)S(1)} %get-tuple-element.32.hg_ref, bf16[1024,4096]{1,0:T(8,128)(2,1)} %w_hbm.7, bf16[512,128]{1,0:T(8,128)(2,1)S(1)} %get-tuple-element.44.after_ref.mine_ref), custom_call_target="tpu_custom_call" | custom-call | flops 3104999936 | tf_op jit(solution)/shard_map/query_close/pallas_call | solution.py:260
  31.2 0.0 copy-start.2
  31.2 2.4 %collective-permute-done.11.got_ref = bf16[512,128]{1,0:T(8,128)(2,1)S(1)} collective-permute-done((bf16[512,128]{1,0:T(8,128)(2,1)S(1)}, bf16[512,128]{1,0:T(8,128)(2,1)S(1)}, u32[]{:S(2)}, u32[]{:S(2)}) %collective-permute-start.11) | collective-permute-done | bytes 131104 | tf_op jit(solution)/shard_map/ppermute | solution.py:35
  33.7 1.7 %collective-permute-start.12 = (bf16[512,128]{1,0:T(8,128)(2,1)S(1)}, bf16[512,128]{1,0:T(8,128)(2,1)S(1)}, u32[]{:S(2)}, u32[]{:S(2)}) collective-permute-start(bf16[512,128]{1,0:T(8,128)(2,1)S(1)} %step_a6.1.rest_0_.mine_a), channel_id=1, source_target_pairs={{0,4},{4,0},{8,12},{12,8},{1,5},{5,1},{9,13},{13,9},{2,6},{6,2},{1... | collective-permute-start | bytes 393224 | tf_op jit(solution)/shard_map/ppermute | solution.py:35
  35.4 0.6 %collective-permute-start.15 = (bf16[512,128]{1,0:T(8,128)(2,1)S(1)}, bf16[512,128]{1,0:T(8,128)(2,1)S(1)}, u32[]{:S(2)}, u32[]{:S(2)}) collective-permute-start(bf16[512,128]{1,0:T(8,128)(2,1)S(1)} %step_b7.1.after_ref.mine_b), channel_id=1, source_target_pairs={{0,16},{16,0},{1,17},{17,1},{2,18},{18,2},{3,19},{19,3},{4,20},{20... | collective-permute-start | bytes 393224 | tf_op jit(solution)/shard_map/ppermute | solution.py:35
  36.0 1.0 %multiply_cosine_fusion.1 = (f32[256,64]{1,0:T(8,128)S(1)}, f32[256,64]{1,0:T(8,128)S(1)}, f32[256,64]{1,0:T(8,128)S(1)}, f32[256,64]{1,0:T(8,128)S(1)}, f32[256,64]{1,0:T(8,128)S(1)}, /*index=5*/f32[256,64]{1,0:T(8,128)S(1)}) fusion(f32[64]{0:T(128)S(1)} %multiply_power_fusion, f32[256]{0:T(256)S(1)} %bitcast.6, f32[256]{0:T(256)S(1)} %broadcast_add_fusion), kind=kLoop, calls=%fused_computation.4 | loop fusion | flops 65536 | bytes 395520 | tf_op jit(solution)/shard_map/cos | solution.py:281
  37.0 0.1 maximum_maximum_fusion.after_ref.sin_ref
  37.2 1.6 %collective-permute-done.12.got_a = bf16[512,128]{1,0:T(8,128)(2,1)S(1)} collective-permute-done((bf16[512,128]{1,0:T(8,128)(2,1)S(1)}, bf16[512,128]{1,0:T(8,128)(2,1)S(1)}, u32[]{:S(2)}, u32[]{:S(2)}) %collective-permute-start.12) | collective-permute-done | bytes 131104 | tf_op jit(solution)/shard_map/ppermute | solution.py:35
  38.8 0.5 update.1
  39.3 0.1 collective-permute-start.14
  39.4 1.1 %collective-permute-done.15.got_b = bf16[512,128]{1,0:T(8,128)(2,1)S(1)} collective-permute-done((bf16[512,128]{1,0:T(8,128)(2,1)S(1)}, bf16[512,128]{1,0:T(8,128)(2,1)S(1)}, u32[]{:S(2)}, u32[]{:S(2)}) %collective-permute-start.15) | collective-permute-done | bytes 131104 | tf_op jit(solution)/shard_map/ppermute | solution.py:35
  40.5 0.2 norm.1
  40.7 0.1 collective-permute-start.17
  40.8 1.3 %collective-permute-start.16 = (bf16[512,128]{1,0:T(8,128)(2,1)S(1)}, bf16[512,128]{1,0:T(8,128)(2,1)S(1)}, u32[]{:S(2)}, u32[]{:S(2)}) collective-permute-start(bf16[512,128]{1,0:T(8,128)(2,1)S(1)} %merge.1.after_ref.s_ref), channel_id=1, source_target_pairs={{0,2},{1,3},{2,0},{3,1},{4,6},{5,7},{6,4},{7,5},{8,10},{9,11},{10,... | collective-permute-start | bytes 393224 | tf_op jit(solution)/shard_map/ppermute | solution.py:35
  42.1 0.1 maximum_maximum_fusion.1.cos_ref
  42.3 0.0 copy-start
  42.3 0.0 copy-start.1
  42.3 0.9 %collective-permute-start.18 = (bf16[32,128]{1,0:T(8,128)(2,1)S(1)}, bf16[32,128]{1,0:T(8,128)(2,1)S(1)}, u32[]{:S(2)}, u32[]{:S(2)}) collective-permute-start(bf16[32,128]{1,0:T(8,128)(2,1)S(1)} %norm_merge.1.sn_ref), channel_id=1, source_target_pairs={{0,2},{1,3},{2,0},{3,1},{4,6},{5,7},{6,4},{7,5},{8,10},{9,11},{10,... | collective-permute-start | bytes 24584 | tf_op jit(solution)/shard_map/ppermute | solution.py:35
  43.2 0.5 %collective-permute-done.10.far_got = bf16[512,1152]{1,0:T(8,128)(2,1)S(1)} collective-permute-done((bf16[512,1152]{1,0:T(8,128)(2,1)S(1)}, bf16[512,1152]{1,0:T(8,128)(2,1)S(1)}, u32[]{:S(2)}, u32[]{:S(2)}) %collective-permute-start.10) | collective-permute-done | bytes 1179680 | tf_op jit(solution)/shard_map/ppermute | solution.py:35
  43.8 0.5 base.1
  44.2 2.7 %collective-permute-done.18.rn_ref = bf16[32,128]{1,0:T(8,128)(2,1)S(1)} collective-permute-done((bf16[32,128]{1,0:T(8,128)(2,1)S(1)}, bf16[32,128]{1,0:T(8,128)(2,1)S(1)}, u32[]{:S(2)}, u32[]{:S(2)}) %collective-permute-start.18) | collective-permute-done | bytes 8224 | tf_op jit(solution)/shard_map/ppermute | solution.py:35
  46.9 2.0 %final.1 = (f32[1024,128]{1,0:T(8,128)}, f32[128,1024]{1,0:T(8,128)}, bf16[512,1024]{1,0:T(8,128)(2,1)}) custom-call(f32[512,1024]{1,0:T(8,128)S(1)} %get-tuple-element.50.base_ref, f32[512,128]{1,0:T(8,128)S(1)} %get-tuple-element.51.low_ref, bf16[512,128]{1,0:T(8,128)(2,1)S(1)} %merge.1.after_ref.s_ref, ...), custom_call_target="tpu_custom_call" | custom-call | flops 2070000000 | tf_op jit(solution)/shard_map/final/pallas_call | solution.py:260
  (28 shorter events, 0.3 us)
Async XLA Ops:
  0.6 3.4 %copy-start.3 = (f32[1024]{0:T(1024)S(1)}, f32[1024]{0:T(1024)}, u32[]{:S(2)}) copy-start(f32[1024]{0:T(1024)} %param.14) | copy-start | bytes 12292
  3.0 1.6 %collective-permute-start = (bf16[384,128]{1,0:T(8,128)(2,1)S(1)}, bf16[384,128]{1,0:T(8,128)(2,1)S(1)}, u32[]{:S(2)}, u32[]{:S(2)}) collective-permute-start(bf16[384,128]{1,0:T(8,128)(2,1)S(1)} %get-tuple-element.34.x_ref), channel_id=1, source_target_pairs={{0,1},{1,0},{2,3},{3,2},{4,5},{5,4},{6,7},{7,6},{8,9},{9,8},{10,11... | collective-permute-start | bytes 294920 | tf_op jit(solution)/shard_map/ppermute | solution.py:35
  3.9 3.8 %collective-permute-start.2 = (bf16[384,128]{1,0:T(8,128)(2,1)S(1)}, bf16[384,128]{1,0:T(8,128)(2,1)S(1)}, u32[]{:S(2)}, u32[]{:S(2)}) collective-permute-start(bf16[384,128]{1,0:T(8,128)(2,1)S(1)} %rank_u.1.x_ref), channel_id=1, source_target_pairs={{0,1},{1,0},{2,3},{3,2},{4,5},{5,4},{6,7},{7,6},{8,9},{9,8},{10,11... | collective-permute-start | bytes 294920 | tf_op jit(solution)/shard_map/ppermute | solution.py:35
  4.7 6.6 %collective-permute-start.1 = (bf16[384,128]{1,0:T(8,128)(2,1)S(1)}, bf16[384,128]{1,0:T(8,128)(2,1)S(1)}, u32[]{:S(2)}, u32[]{:S(2)}) collective-permute-start(bf16[384,128]{1,0:T(8,128)(2,1)S(1)} %low_v.1.after_ref.s_ref), channel_id=1, source_target_pairs={{0,2},{1,3},{2,0},{3,1},{4,6},{5,7},{6,4},{7,5},{8,10},{9,11},{10,... | collective-permute-start | bytes 294920 | tf_op jit(solution)/shard_map/ppermute | solution.py:35
  7.7 6.0 %collective-permute-start.4 = (bf16[384,128]{1,0:T(8,128)(2,1)S(1)}, bf16[384,128]{1,0:T(8,128)(2,1)S(1)}, u32[]{:S(2)}, u32[]{:S(2)}) collective-permute-start(bf16[384,128]{1,0:T(8,128)(2,1)S(1)} %low_u.1.after_ref.s_ref), channel_id=1, source_target_pairs={{0,2},{1,3},{2,0},{3,1},{4,6},{5,7},{6,4},{7,5},{8,10},{9,11},{10,... | collective-permute-start | bytes 294920 | tf_op jit(solution)/shard_map/ppermute | solution.py:35
  10.1 6.8 %collective-permute-start.5 = (bf16[512,1152]{1,0:T(8,128)(2,1)S(1)}, bf16[512,1152]{1,0:T(8,128)(2,1)S(1)}, u32[]{:S(2)}, u32[]{:S(2)}) collective-permute-start(bf16[512,1152]{1,0:T(8,128)(2,1)S(1)} %get-tuple-element.37.after_ref.diag_ref), channel_id=1, source_target_pairs={{0,1},{1,0},{2,3},{3,2},{4,5},{5,4},{6,7},{7,6},{8,9},{9,8},{10,11... | collective-permute-start | bytes 3538952 | tf_op jit(solution)/shard_map/ppermute | solution.py:35
  11.7 7.3 %collective-permute-start.3 = (bf16[512,128]{1,0:T(8,128)(2,1)S(1)}, bf16[512,128]{1,0:T(8,128)(2,1)S(1)}, u32[]{:S(2)}, u32[]{:S(2)}) collective-permute-start(bf16[512,128]{1,0:T(8,128)(2,1)S(1)} %get-tuple-element.39.after_ref), channel_id=1, source_target_pairs={{0,4},{4,0},{8,12},{12,8},{1,5},{5,1},{9,13},{13,9},{2,6},{6,2},{1... | collective-permute-start | bytes 393224 | tf_op jit(solution)/shard_map/ppermute | solution.py:35
  14.1 7.5 %collective-permute-start.7 = (bf16[512,128]{1,0:T(8,128)(2,1)S(1)}, bf16[512,128]{1,0:T(8,128)(2,1)S(1)}, u32[]{:S(2)}, u32[]{:S(2)}) collective-permute-start(bf16[512,128]{1,0:T(8,128)(2,1)S(1)} %get-tuple-element.42.after_ref), channel_id=1, source_target_pairs={{0,16},{16,0},{1,17},{17,1},{2,18},{18,2},{3,19},{19,3},{4,20},{20... | collective-permute-start | bytes 393224 | tf_op jit(solution)/shard_map/ppermute | solution.py:35
  17.2 26.6 %collective-permute-start.10 = (bf16[512,1152]{1,0:T(8,128)(2,1)S(1)}, bf16[512,1152]{1,0:T(8,128)(2,1)S(1)}, u32[]{:S(2)}, u32[]{:S(2)}) collective-permute-start(bf16[512,1152]{1,0:T(8,128)(2,1)S(1)} %far.1.rest_0_.far_ref), channel_id=1, source_target_pairs={{0,2},{1,3},{2,0},{3,1},{4,6},{5,7},{6,4},{7,5},{8,10},{9,11},{10,... | collective-permute-start | bytes 3538952 | tf_op jit(solution)/shard_map/ppermute | solution.py:35
  19.0 8.7 %collective-permute-start.6 = (bf16[512,128]{1,0:T(8,128)(2,1)S(1)}, bf16[512,128]{1,0:T(8,128)(2,1)S(1)}, u32[]{:S(2)}, u32[]{:S(2)}) collective-permute-start(bf16[512,128]{1,0:T(8,128)(2,1)S(1)} %step_a0.1.rest_0_.mine_ref), channel_id=1, source_target_pairs={{0,8},{4,12},{8,0},{12,4},{1,9},{5,13},{9,1},{13,5},{2,10},{6,14},... | collective-permute-start | bytes 393224 | tf_op jit(solution)/shard_map/ppermute | solution.py:35
  21.7 5.8 %collective-permute-start.8 = (bf16[512,128]{1,0:T(8,128)(2,1)S(1)}, bf16[512,128]{1,0:T(8,128)(2,1)S(1)}, u32[]{:S(2)}, u32[]{:S(2)}) collective-permute-start(bf16[512,128]{1,0:T(8,128)(2,1)S(1)} %step_b1.1.mine_ref.rest_0_.after_ref), channel_id=1, source_target_pairs={{0,4},{4,0},{8,12},{12,8},{1,5},{5,1},{9,13},{13,9},{2,6},{6,2},{1... | collective-permute-start | bytes 393224 | tf_op jit(solution)/shard_map/ppermute | solution.py:35
  27.5 7.9 %collective-permute-start.13 = (bf16[512,128]{1,0:T(8,128)(2,1)S(1)}, bf16[512,128]{1,0:T(8,128)(2,1)S(1)}, u32[]{:S(2)}, u32[]{:S(2)}) collective-permute-start(bf16[512,128]{1,0:T(8,128)(2,1)S(1)} %step_b3.1.rest_0_.mine_ref), channel_id=1, source_target_pairs={{0,8},{4,12},{8,0},{12,4},{1,9},{5,13},{9,1},{13,5},{2,10},{6,14},... | collective-permute-start | bytes 393224 | tf_op jit(solution)/shard_map/ppermute | solution.py:35
  27.7 15.5 %collective-permute-start.9 = (bf16[512,1024]{1,0:T(8,128)(2,1)S(1)}, bf16[512,1024]{1,0:T(8,128)(2,1)S(1)}, u32[]{:S(2)}, u32[]{:S(2)}) collective-permute-start(bf16[512,1024]{1,0:T(8,128)(2,1)S(1)} %get-tuple-element.45), channel_id=1, source_target_pairs={{0,1},{1,0},{2,3},{3,2},{4,5},{5,4},{6,7},{7,6},{8,9},{9,8},{10,11... | collective-permute-start | bytes 3145736 | tf_op jit(solution)/shard_map/ppermute | solution.py:35
  27.8 5.9 %collective-permute-start.11 = (bf16[512,128]{1,0:T(8,128)(2,1)S(1)}, bf16[512,128]{1,0:T(8,128)(2,1)S(1)}, u32[]{:S(2)}, u32[]{:S(2)}) collective-permute-start(bf16[512,128]{1,0:T(8,128)(2,1)S(1)} %get-tuple-element.44.after_ref.mine_ref), channel_id=1, source_target_pairs={{0,16},{16,0},{1,17},{17,1},{2,18},{18,2},{3,19},{19,3},{4,20},{20... | collective-permute-start | bytes 393224 | tf_op jit(solution)/shard_map/ppermute | solution.py:35
  31.2 4.8 %copy-start.2 = (s32[256]{0:T(256)S(1)}, s32[256]{0:T(256)}, u32[]{:S(2)}) copy-start(s32[256]{0:T(256)} %param.15) | copy-start | bytes 3076
  33.7 5.1 %collective-permute-start.12 = (bf16[512,128]{1,0:T(8,128)(2,1)S(1)}, bf16[512,128]{1,0:T(8,128)(2,1)S(1)}, u32[]{:S(2)}, u32[]{:S(2)}) collective-permute-start(bf16[512,128]{1,0:T(8,128)(2,1)S(1)} %step_a6.1.rest_0_.mine_a), channel_id=1, source_target_pairs={{0,4},{4,0},{8,12},{12,8},{1,5},{5,1},{9,13},{13,9},{2,6},{6,2},{1... | collective-permute-start | bytes 393224 | tf_op jit(solution)/shard_map/ppermute | solution.py:35
  35.4 5.0 %collective-permute-start.15 = (bf16[512,128]{1,0:T(8,128)(2,1)S(1)}, bf16[512,128]{1,0:T(8,128)(2,1)S(1)}, u32[]{:S(2)}, u32[]{:S(2)}) collective-permute-start(bf16[512,128]{1,0:T(8,128)(2,1)S(1)} %step_b7.1.after_ref.mine_b), channel_id=1, source_target_pairs={{0,16},{16,0},{1,17},{17,1},{2,18},{18,2},{3,19},{19,3},{4,20},{20... | collective-permute-start | bytes 393224 | tf_op jit(solution)/shard_map/ppermute | solution.py:35
  39.3 1.4 %collective-permute-start.14 = (bf16[512,128]{1,0:T(8,128)(2,1)S(1)}, bf16[512,128]{1,0:T(8,128)(2,1)S(1)}, u32[]{:S(2)}, u32[]{:S(2)}) collective-permute-start(bf16[512,128]{1,0:T(8,128)(2,1)S(1)} %get-tuple-element.46.after_ref.x_ref), channel_id=1, source_target_pairs={{0,1},{1,0},{2,3},{3,2},{4,5},{5,4},{6,7},{7,6},{8,9},{9,8},{10,11... | collective-permute-start | bytes 393224 | tf_op jit(solution)/shard_map/ppermute | solution.py:35
  40.7 1.6 %collective-permute-start.17 = (bf16[32,128]{1,0:T(8,128)(2,1)S(1)}, bf16[32,128]{1,0:T(8,128)(2,1)S(1)}, u32[]{:S(2)}, u32[]{:S(2)}) collective-permute-start(bf16[32,128]{1,0:T(8,128)(2,1)S(1)} %get-tuple-element.49.after_ref.a_ref), channel_id=1, source_target_pairs={{0,1},{1,0},{2,3},{3,2},{4,5},{5,4},{6,7},{7,6},{8,9},{9,8},{10,11... | collective-permute-start | bytes 24584 | tf_op jit(solution)/shard_map/ppermute | solution.py:35
  40.8 6.1 %collective-permute-start.16 = (bf16[512,128]{1,0:T(8,128)(2,1)S(1)}, bf16[512,128]{1,0:T(8,128)(2,1)S(1)}, u32[]{:S(2)}, u32[]{:S(2)}) collective-permute-start(bf16[512,128]{1,0:T(8,128)(2,1)S(1)} %merge.1.after_ref.s_ref), channel_id=1, source_target_pairs={{0,2},{1,3},{2,0},{3,1},{4,6},{5,7},{6,4},{7,5},{8,10},{9,11},{10,... | collective-permute-start | bytes 393224 | tf_op jit(solution)/shard_map/ppermute | solution.py:35
  42.3 4.6 %copy-start = (f32[1024,128]{1,0:T(8,128)S(1)}, f32[1024,128]{1,0:T(8,128)}, u32[]{:S(2)}) copy-start(f32[1024,128]{1,0:T(8,128)} %a_ref.1) | copy-start | bytes 1572868
  42.3 4.6 %copy-start.1 = (f32[128,1024]{1,0:T(8,128)S(1)}, f32[128,1024]{1,0:T(8,128)}, u32[]{:S(2)}) copy-start(f32[128,1024]{1,0:T(8,128)} %b_ref.1) | copy-start | bytes 1572868
  42.3 4.6 %collective-permute-start.18 = (bf16[32,128]{1,0:T(8,128)(2,1)S(1)}, bf16[32,128]{1,0:T(8,128)(2,1)S(1)}, u32[]{:S(2)}, u32[]{:S(2)}) collective-permute-start(bf16[32,128]{1,0:T(8,128)(2,1)S(1)} %norm_merge.1.sn_ref), channel_id=1, source_target_pairs={{0,2},{1,3},{2,0},{3,1},{4,6},{5,7},{6,4},{7,5},{8,10},{9,11},{10,... | collective-permute-start | bytes 24584 | tf_op jit(solution)/shard_map/ppermute | solution.py:35

commit v18 on v17

--- a/solution.py
+++ b/solution.py
@@ -250,9 +250,7 @@
     return pltpu.with_memory_space_constraint(x, pltpu.HBM)
 
 
-WEIGHTS = {
-    "rank_v": 2.4, "prep": 0.6, "query_diag": 40.0, "query_beside": 2.7, "query_close": 2.7, "base": 1.0, "grad_b": 40.0, "final": 1.8,
-}
+WEIGHTS = {"rank_v": 2.4, "prep": 0.6, "query_diag": 40.0, "query_beside": 1.8, "query_close": 2.7, "base": 1.0, "grad_b": 40.0, "final": 1.8, "update": 3.0}
 FLOPS_PER_WEIGHT = 1_150_000_000
 
 

time: 49.1 us -> 48.9 us (level)
  transfers between devices with their start and end apart: 19 -> 19, of which waited for: 7 -> 8; matrix products, arithmetic and copies ran while one was open for 3% -> 3% of each run, Pallas kernels for 24% -> 24%
where the time goes in v18:
time: 48.9 us; the launch traced here: 48.8 us
  starting transfers between devices  18.4 us (38%)
  Pallas kernels  16.3 us (33%)
  waiting for transfers between devices  11.9 us (24%)
  other arithmetic  1.28 us (3%)
  between operations  0.89 us (2%)
    ppermute x19, starting transfers between devices, swap(): return lax.ppermute(x, axis, [(i, i ^ k) for i in range(n)])  18.4 us
    pallas_call x25, Pallas kernels, call(): pl.pallas_call(kernel, out_shape=outs, in_specs=in_specs, out_specs=out_s...  16.3 us
    ppermute x19, waiting for transfers between devices, swap(): return lax.ppermute(x, axis, [(i, i ^ k) for i in range(n)])  11.9 us
    cos x1, other arithmetic, turn_tables(): c, s = (jnp.cos(angle), jnp.sin(angle))  0.99 us
  transfers between devices with their start and end apart: 19, of which 8 were waited for; matrix products, arithmetic and copies ran while one was open for 3% of the time, Pallas kernels for 24%

profile of v18, /device:TPU:0, one launch (start us, length us, event | category | flops | bytes accessed | tf_op | source)
XLA Modules:
  0.0 48.8 jit_solution(2199435703488483171)
XLA Ops:
  0.6 2.4 %rank_v.1 = (bf16[384,128]{1,0:T(8,128)(2,1)S(1)}, bf16[384,1024]{1,0:T(8,128)(2,1)S(1)}, bf16[384,1024]{1,0:T(8,128)(2,1)S(1)}, bf16[1024,128]{1,0:T(8,128)(2,1...) custom-call(bf16[384,1024]{1,0:T(8,128)(2,1)} %x_hbm.1, bf16[384,1024]{1,0:T(8,128)(2,1)} %v_hbm.1, ...), custom_call_target="tpu_custom_call" | custom-call | flops 2760000000 | tf_op jit(solution)/shard_map/rank_v/pallas_call | solution.py:258
  3.0 0.5 %collective-permute-start = (bf16[384,128]{1,0:T(8,128)(2,1)S(1)}, bf16[384,128]{1,0:T(8,128)(2,1)S(1)}, u32[]{:S(2)}, u32[]{:S(2)}) collective-permute-start(bf16[384,128]{1,0:T(8,128)(2,1)S(1)} %get-tuple-element.34.x_ref), channel_id=1, source_target_pairs={{0,1},{1,0},{2,3},{3,2},{4,5},{5,4},{6,7},{7,6},{8,9},{9,8},{10,11... | collective-permute-start | bytes 294920 | tf_op jit(solution)/shard_map/ppermute | solution.py:35
  3.6 0.4 rank_u.1.x_ref
  3.9 0.1 collective-permute-start.2
  4.1 0.6 %prep.1 = (bf16[512,1024]{1,0:T(8,128)(2,1)S(1)}, bf16[512,128]{1,0:T(8,128)(2,1)S(1)}, f32[8,128]{1,0:T(8,128)S(1)}) custom-call(bf16[512,1024]{1,0:T(8,128)(2,1)S(1)} %get-tuple-element.30.h_ref, f32[1,1024]{1,0:T(1,128)S(1)} %bitcast.8, bf16[1024,128]{1,0:T(8,128)(2,1)S(1)} %get-tuple-element.31.a16_ref), custom_call_target="tpu_custom_call" | custom-call | flops 690000000 | tf_op jit(solution)/shard_map/prep/pallas_call | solution.py:258
  4.6 0.0 collective-permute-done.got_ref
  4.7 3.0 %collective-permute-start.1 = (bf16[384,128]{1,0:T(8,128)(2,1)S(1)}, bf16[384,128]{1,0:T(8,128)(2,1)S(1)}, u32[]{:S(2)}, u32[]{:S(2)}) collective-permute-start(bf16[384,128]{1,0:T(8,128)(2,1)S(1)} %low_v.1.after_ref.s_ref), channel_id=1, source_target_pairs={{0,2},{1,3},{2,0},{3,1},{4,6},{5,7},{6,4},{7,5},{8,10},{9,11},{10,... | collective-permute-start | bytes 294920 | tf_op jit(solution)/shard_map/ppermute | solution.py:35
  7.7 0.3 collective-permute-start.4
  8.1 2.0 %query_diag.1 = (bf16[512,1152]{1,0:T(8,128)(2,1)S(1)}, bf16[2,1024,512]{2,1,0:T(8,128)(2,1)S(1)}) custom-call(bf16[512,1024]{1,0:T(8,128)(2,1)S(1)} %get-tuple-element.32.hg_ref, bf16[1024,512]{1,0:T(8,128)(2,1)S(1)} %get-tuple-element.36.w_ref, bf16[1024,4096]{1,0:T(8,128)(2,1)} %w_hbm.7, bf16[512,128]{1,0:T(8,128)(2,1)S(1)} %get-tuple-element.35.after_ref.low_ref, ...), custom_call_target="tpu_custom_call" | custom-call | flops 46000001024 | tf_op jit(solution)/shard_map/query_diag/pallas_call | solution.py:258
  10.1 0.1 collective-permute-start.5
  10.2 1.1 %collective-permute-done.1.r_ref = bf16[384,128]{1,0:T(8,128)(2,1)S(1)} collective-permute-done((bf16[384,128]{1,0:T(8,128)(2,1)S(1)}, bf16[384,128]{1,0:T(8,128)(2,1)S(1)}, u32[]{:S(2)}, u32[]{:S(2)}) %collective-permute-start.1) | collective-permute-done | bytes 98336 | tf_op jit(solution)/shard_map/ppermute | solution.py:35
  11.2 0.4 grad_a.1
  11.7 2.1 %collective-permute-start.3 = (bf16[512,128]{1,0:T(8,128)(2,1)S(1)}, bf16[512,128]{1,0:T(8,128)(2,1)S(1)}, u32[]{:S(2)}, u32[]{:S(2)}) collective-permute-start(bf16[512,128]{1,0:T(8,128)(2,1)S(1)} %get-tuple-element.39.after_ref), channel_id=1, source_target_pairs={{0,4},{4,0},{8,12},{12,8},{1,5},{5,1},{9,13},{13,9},{2,6},{6,2},{1... | collective-permute-start | bytes 393224 | tf_op jit(solution)/shard_map/ppermute | solution.py:35
  13.7 0.3 grad_b.1
  14.1 1.5 %collective-permute-start.7 = (bf16[512,128]{1,0:T(8,128)(2,1)S(1)}, bf16[512,128]{1,0:T(8,128)(2,1)S(1)}, u32[]{:S(2)}, u32[]{:S(2)}) collective-permute-start(bf16[512,128]{1,0:T(8,128)(2,1)S(1)} %get-tuple-element.42.after_ref), channel_id=1, source_target_pairs={{0,16},{16,0},{1,17},{17,1},{2,18},{18,2},{3,19},{19,3},{4,20},{20... | collective-permute-start | bytes 393224 | tf_op jit(solution)/shard_map/ppermute | solution.py:35
  15.6 1.2 %query_distant.1.mine_ref = bf16[512,1024]{1,0:T(8,128)(2,1)S(1)} custom-call(bf16[512,1024]{1,0:T(8,128)(2,1)S(1)} %get-tuple-element.32.hg_ref, bf16[2,1024,512]{2,1,0:T(8,128)(2,1)S(1)} %get-tuple-element.40.w_ref, bf16[512,128]{1,0:T(8,128)(2,1)S(1)} %get-tuple-element.42.after_ref), custom_call_target="tpu_custom_call" | custom-call | flops 11500000 | tf_op jit(solution)/shard_map/query_distant/pallas_call | solution.py:258
  16.9 0.3 far.1.rest_0_.far_ref
  17.2 1.7 %collective-permute-start.10 = (bf16[512,1152]{1,0:T(8,128)(2,1)S(1)}, bf16[512,1152]{1,0:T(8,128)(2,1)S(1)}, u32[]{:S(2)}, u32[]{:S(2)}) collective-permute-start(bf16[512,1152]{1,0:T(8,128)(2,1)S(1)} %far.1.rest_0_.far_ref), channel_id=1, source_target_pairs={{0,2},{1,3},{2,0},{3,1},{4,6},{5,7},{6,4},{7,5},{8,10},{9,11},{10,... | collective-permute-start | bytes 3538952 | tf_op jit(solution)/shard_map/ppermute | solution.py:35
  19.0 2.7 %collective-permute-start.6 = (bf16[512,128]{1,0:T(8,128)(2,1)S(1)}, bf16[512,128]{1,0:T(8,128)(2,1)S(1)}, u32[]{:S(2)}, u32[]{:S(2)}) collective-permute-start(bf16[512,128]{1,0:T(8,128)(2,1)S(1)} %step_a0.1.rest_0_.mine_ref), channel_id=1, source_target_pairs={{0,8},{4,12},{8,0},{12,4},{1,9},{5,13},{9,1},{13,5},{2,10},{6,14},... | collective-permute-start | bytes 393224 | tf_op jit(solution)/shard_map/ppermute | solution.py:35
  21.7 0.7 %collective-permute-start.8 = (bf16[512,128]{1,0:T(8,128)(2,1)S(1)}, bf16[512,128]{1,0:T(8,128)(2,1)S(1)}, u32[]{:S(2)}, u32[]{:S(2)}) collective-permute-start(bf16[512,128]{1,0:T(8,128)(2,1)S(1)} %step_b1.1.mine_ref.rest_0_.after_ref), channel_id=1, source_target_pairs={{0,4},{4,0},{8,12},{12,8},{1,5},{5,1},{9,13},{13,9},{2,6},{6,2},{1... | collective-permute-start | bytes 393224 | tf_op jit(solution)/shard_map/ppermute | solution.py:35
  22.4 2.7 %query_beside.1.rest_1_ = bf16[512,1024]{1,0:T(8,128)(2,1)S(1)} custom-call(bf16[512,1024]{1,0:T(8,128)(2,1)S(1)} %get-tuple-element.32.hg_ref, bf16[1024,4096]{1,0:T(8,128)(2,1)} %w_hbm.7, bf16[512,128]{1,0:T(8,128)(2,1)S(1)} %step_b1.1.mine_ref.rest_0_.after_ref), custom_call_target="tpu_custom_call" | custom-call | flops 2070000000 | tf_op jit(solution)/shard_map/query_beside/pallas_call | solution.py:258
  25.1 2.4 %collective-permute-done.8.got_ref = bf16[512,128]{1,0:T(8,128)(2,1)S(1)} collective-permute-done((bf16[512,128]{1,0:T(8,128)(2,1)S(1)}, bf16[512,128]{1,0:T(8,128)(2,1)S(1)}, u32[]{:S(2)}, u32[]{:S(2)}) %collective-permute-start.8) | collective-permute-done | bytes 131104 | tf_op jit(solution)/shard_map/ppermute | solution.py:35
  27.5 0.2 collective-permute-start.13
  27.7 0.8 %collective-permute-start.11 = (bf16[512,128]{1,0:T(8,128)(2,1)S(1)}, bf16[512,128]{1,0:T(8,128)(2,1)S(1)}, u32[]{:S(2)}, u32[]{:S(2)}) collective-permute-start(bf16[512,128]{1,0:T(8,128)(2,1)S(1)} %get-tuple-element.44.after_ref.mine_ref), channel_id=1, source_target_pairs={{0,16},{16,0},{1,17},{17,1},{2,18},{18,2},{3,19},{19,3},{4,20},{20... | collective-permute-start | bytes 393224 | tf_op jit(solution)/shard_map/ppermute | solution.py:35
  28.5 2.7 %query_close.1.rest_0_.mine_ref = bf16[512,1024]{1,0:T(8,128)(2,1)S(1)} custom-call(bf16[512,1024]{1,0:T(8,128)(2,1)S(1)} %get-tuple-element.32.hg_ref, bf16[1024,4096]{1,0:T(8,128)(2,1)} %w_hbm.7, bf16[512,128]{1,0:T(8,128)(2,1)S(1)} %get-tuple-element.44.after_ref.mine_ref), custom_call_target="tpu_custom_call" | custom-call | flops 3104999936 | tf_op jit(solution)/shard_map/query_close/pallas_call | solution.py:258
  31.1 0.0 copy-start.2
  31.1 0.1 collective-permute-start.9
  31.2 1.5 %collective-permute-done.11.got_ref = bf16[512,128]{1,0:T(8,128)(2,1)S(1)} collective-permute-done((bf16[512,128]{1,0:T(8,128)(2,1)S(1)}, bf16[512,128]{1,0:T(8,128)(2,1)S(1)}, u32[]{:S(2)}, u32[]{:S(2)}) %collective-permute-start.11) | collective-permute-done | bytes 131104 | tf_op jit(solution)/shard_map/ppermute | solution.py:35
  32.7 1.7 %collective-permute-start.12 = (bf16[512,128]{1,0:T(8,128)(2,1)S(1)}, bf16[512,128]{1,0:T(8,128)(2,1)S(1)}, u32[]{:S(2)}, u32[]{:S(2)}) collective-permute-start(bf16[512,128]{1,0:T(8,128)(2,1)S(1)} %step_a6.1.rest_0_.mine_a), channel_id=1, source_target_pairs={{0,4},{4,0},{8,12},{12,8},{1,5},{5,1},{9,13},{13,9},{2,6},{6,2},{1... | collective-permute-start | bytes 393224 | tf_op jit(solution)/shard_map/ppermute | solution.py:35
  34.4 0.4 collective-permute-done.13.got_ref
  34.9 0.5 %collective-permute-start.15 = (bf16[512,128]{1,0:T(8,128)(2,1)S(1)}, bf16[512,128]{1,0:T(8,128)(2,1)S(1)}, u32[]{:S(2)}, u32[]{:S(2)}) collective-permute-start(bf16[512,128]{1,0:T(8,128)(2,1)S(1)} %step_b7.1.after_ref.mine_b), channel_id=1, source_target_pairs={{0,16},{16,0},{1,17},{17,1},{2,18},{18,2},{3,19},{19,3},{4,20},{20... | collective-permute-start | bytes 393224 | tf_op jit(solution)/shard_map/ppermute | solution.py:35
  35.4 1.0 %multiply_cosine_fusion.1 = (f32[256,64]{1,0:T(8,128)S(1)}, f32[256,64]{1,0:T(8,128)S(1)}, f32[256,64]{1,0:T(8,128)S(1)}, f32[256,64]{1,0:T(8,128)S(1)}, f32[256,64]{1,0:T(8,128)S(1)}, /*index=5*/f32[256,64]{1,0:T(8,128)S(1)}) fusion(f32[64]{0:T(128)S(1)} %multiply_power_fusion, f32[256]{0:T(256)S(1)} %bitcast.6, f32[256]{0:T(256)S(1)} %broadcast_add_fusion), kind=kLoop, calls=%fused_computation.4 | loop fusion | flops 65536 | bytes 395520 | tf_op jit(solution)/shard_map/cos | solution.py:279
  36.4 0.1 maximum_maximum_fusion.after_ref.sin_ref
  36.6 1.2 %collective-permute-done.12.got_a = bf16[512,128]{1,0:T(8,128)(2,1)S(1)} collective-permute-done((bf16[512,128]{1,0:T(8,128)(2,1)S(1)}, bf16[512,128]{1,0:T(8,128)(2,1)S(1)}, u32[]{:S(2)}, u32[]{:S(2)}) %collective-permute-start.12) | collective-permute-done | bytes 131104 | tf_op jit(solution)/shard_map/ppermute | solution.py:35
  37.8 0.5 update.1
  38.3 0.1 collective-permute-start.14
  38.3 1.6 %collective-permute-done.15.got_b = bf16[512,128]{1,0:T(8,128)(2,1)S(1)} collective-permute-done((bf16[512,128]{1,0:T(8,128)(2,1)S(1)}, bf16[512,128]{1,0:T(8,128)(2,1)S(1)}, u32[]{:S(2)}, u32[]{:S(2)}) %collective-permute-start.15) | collective-permute-done | bytes 131104 | tf_op jit(solution)/shard_map/ppermute | solution.py:35
  39.9 0.2 norm.1
  40.1 0.1 collective-permute-start.17
  40.3 1.1 %collective-permute-start.16 = (bf16[512,128]{1,0:T(8,128)(2,1)S(1)}, bf16[512,128]{1,0:T(8,128)(2,1)S(1)}, u32[]{:S(2)}, u32[]{:S(2)}) collective-permute-start(bf16[512,128]{1,0:T(8,128)(2,1)S(1)} %merge.1.after_ref.s_ref), channel_id=1, source_target_pairs={{0,2},{1,3},{2,0},{3,1},{4,6},{5,7},{6,4},{7,5},{8,10},{9,11},{10,... | collective-permute-start | bytes 393224 | tf_op jit(solution)/shard_map/ppermute | solution.py:35
  41.4 0.1 maximum_maximum_fusion.1.cos_ref
  41.5 0.0 copy-start
  41.5 0.0 copy-start.1
  41.6 1.1 %collective-permute-start.18 = (bf16[32,128]{1,0:T(8,128)(2,1)S(1)}, bf16[32,128]{1,0:T(8,128)(2,1)S(1)}, u32[]{:S(2)}, u32[]{:S(2)}) collective-permute-start(bf16[32,128]{1,0:T(8,128)(2,1)S(1)} %norm_merge.1.sn_ref), channel_id=1, source_target_pairs={{0,2},{1,3},{2,0},{3,1},{4,6},{5,7},{6,4},{7,5},{8,10},{9,11},{10,... | collective-permute-start | bytes 24584 | tf_op jit(solution)/shard_map/ppermute | solution.py:35
  42.6 1.5 %collective-permute-done.10.far_got = bf16[512,1152]{1,0:T(8,128)(2,1)S(1)} collective-permute-done((bf16[512,1152]{1,0:T(8,128)(2,1)S(1)}, bf16[512,1152]{1,0:T(8,128)(2,1)S(1)}, u32[]{:S(2)}, u32[]{:S(2)}) %collective-permute-start.10) | collective-permute-done | bytes 1179680 | tf_op jit(solution)/shard_map/ppermute | solution.py:35
  44.1 0.5 base.1
  44.6 2.2 %collective-permute-done.18.rn_ref = bf16[32,128]{1,0:T(8,128)(2,1)S(1)} collective-permute-done((bf16[32,128]{1,0:T(8,128)(2,1)S(1)}, bf16[32,128]{1,0:T(8,128)(2,1)S(1)}, u32[]{:S(2)}, u32[]{:S(2)}) %collective-permute-start.18) | collective-permute-done | bytes 8224 | tf_op jit(solution)/shard_map/ppermute | solution.py:35
  46.8 2.0 %final.1 = (f32[1024,128]{1,0:T(8,128)}, f32[128,1024]{1,0:T(8,128)}, bf16[512,1024]{1,0:T(8,128)(2,1)}) custom-call(f32[512,1024]{1,0:T(8,128)S(1)} %get-tuple-element.50.base_ref, f32[512,128]{1,0:T(8,128)S(1)} %get-tuple-element.51.low_ref, bf16[512,128]{1,0:T(8,128)(2,1)S(1)} %merge.1.after_ref.s_ref, ...), custom_call_target="tpu_custom_call" | custom-call | flops 2070000000 | tf_op jit(solution)/shard_map/final/pallas_call | solution.py:258
  (28 shorter events, 0.3 us)
Async XLA Ops:
  0.6 3.4 %copy-start.3 = (f32[1024]{0:T(1024)S(1)}, f32[1024]{0:T(1024)}, u32[]{:S(2)}) copy-start(f32[1024]{0:T(1024)} %param.14) | copy-start | bytes 12292
  3.0 1.6 %collective-permute-start = (bf16[384,128]{1,0:T(8,128)(2,1)S(1)}, bf16[384,128]{1,0:T(8,128)(2,1)S(1)}, u32[]{:S(2)}, u32[]{:S(2)}) collective-permute-start(bf16[384,128]{1,0:T(8,128)(2,1)S(1)} %get-tuple-element.34.x_ref), channel_id=1, source_target_pairs={{0,1},{1,0},{2,3},{3,2},{4,5},{5,4},{6,7},{7,6},{8,9},{9,8},{10,11... | collective-permute-start | bytes 294920 | tf_op jit(solution)/shard_map/ppermute | solution.py:35
  3.9 3.8 %collective-permute-start.2 = (bf16[384,128]{1,0:T(8,128)(2,1)S(1)}, bf16[384,128]{1,0:T(8,128)(2,1)S(1)}, u32[]{:S(2)}, u32[]{:S(2)}) collective-permute-start(bf16[384,128]{1,0:T(8,128)(2,1)S(1)} %rank_u.1.x_ref), channel_id=1, source_target_pairs={{0,1},{1,0},{2,3},{3,2},{4,5},{5,4},{6,7},{7,6},{8,9},{9,8},{10,11... | collective-permute-start | bytes 294920 | tf_op jit(solution)/shard_map/ppermute | solution.py:35
  4.7 6.6 %collective-permute-start.1 = (bf16[384,128]{1,0:T(8,128)(2,1)S(1)}, bf16[384,128]{1,0:T(8,128)(2,1)S(1)}, u32[]{:S(2)}, u32[]{:S(2)}) collective-permute-start(bf16[384,128]{1,0:T(8,128)(2,1)S(1)} %low_v.1.after_ref.s_ref), channel_id=1, source_target_pairs={{0,2},{1,3},{2,0},{3,1},{4,6},{5,7},{6,4},{7,5},{8,10},{9,11},{10,... | collective-permute-start | bytes 294920 | tf_op jit(solution)/shard_map/ppermute | solution.py:35
  7.7 6.0 %collective-permute-start.4 = (bf16[384,128]{1,0:T(8,128)(2,1)S(1)}, bf16[384,128]{1,0:T(8,128)(2,1)S(1)}, u32[]{:S(2)}, u32[]{:S(2)}) collective-permute-start(bf16[384,128]{1,0:T(8,128)(2,1)S(1)} %low_u.1.after_ref.s_ref), channel_id=1, source_target_pairs={{0,2},{1,3},{2,0},{3,1},{4,6},{5,7},{6,4},{7,5},{8,10},{9,11},{10,... | collective-permute-start | bytes 294920 | tf_op jit(solution)/shard_map/ppermute | solution.py:35
  10.1 6.8 %collective-permute-start.5 = (bf16[512,1152]{1,0:T(8,128)(2,1)S(1)}, bf16[512,1152]{1,0:T(8,128)(2,1)S(1)}, u32[]{:S(2)}, u32[]{:S(2)}) collective-permute-start(bf16[512,1152]{1,0:T(8,128)(2,1)S(1)} %get-tuple-element.37.after_ref.diag_ref), channel_id=1, source_target_pairs={{0,1},{1,0},{2,3},{3,2},{4,5},{5,4},{6,7},{7,6},{8,9},{9,8},{10,11... | collective-permute-start | bytes 3538952 | tf_op jit(solution)/shard_map/ppermute | solution.py:35
  11.7 7.3 %collective-permute-start.3 = (bf16[512,128]{1,0:T(8,128)(2,1)S(1)}, bf16[512,128]{1,0:T(8,128)(2,1)S(1)}, u32[]{:S(2)}, u32[]{:S(2)}) collective-permute-start(bf16[512,128]{1,0:T(8,128)(2,1)S(1)} %get-tuple-element.39.after_ref), channel_id=1, source_target_pairs={{0,4},{4,0},{8,12},{12,8},{1,5},{5,1},{9,13},{13,9},{2,6},{6,2},{1... | collective-permute-start | bytes 393224 | tf_op jit(solution)/shard_map/ppermute | solution.py:35
  14.1 7.6 %collective-permute-start.7 = (bf16[512,128]{1,0:T(8,128)(2,1)S(1)}, bf16[512,128]{1,0:T(8,128)(2,1)S(1)}, u32[]{:S(2)}, u32[]{:S(2)}) collective-permute-start(bf16[512,128]{1,0:T(8,128)(2,1)S(1)} %get-tuple-element.42.after_ref), channel_id=1, source_target_pairs={{0,16},{16,0},{1,17},{17,1},{2,18},{18,2},{3,19},{19,3},{4,20},{20... | collective-permute-start | bytes 393224 | tf_op jit(solution)/shard_map/ppermute | solution.py:35
  17.2 26.9 %collective-permute-start.10 = (bf16[512,1152]{1,0:T(8,128)(2,1)S(1)}, bf16[512,1152]{1,0:T(8,128)(2,1)S(1)}, u32[]{:S(2)}, u32[]{:S(2)}) collective-permute-start(bf16[512,1152]{1,0:T(8,128)(2,1)S(1)} %far.1.rest_0_.far_ref), channel_id=1, source_target_pairs={{0,2},{1,3},{2,0},{3,1},{4,6},{5,7},{6,4},{7,5},{8,10},{9,11},{10,... | collective-permute-start | bytes 3538952 | tf_op jit(solution)/shard_map/ppermute | solution.py:35
  19.0 8.7 %collective-permute-start.6 = (bf16[512,128]{1,0:T(8,128)(2,1)S(1)}, bf16[512,128]{1,0:T(8,128)(2,1)S(1)}, u32[]{:S(2)}, u32[]{:S(2)}) collective-permute-start(bf16[512,128]{1,0:T(8,128)(2,1)S(1)} %step_a0.1.rest_0_.mine_ref), channel_id=1, source_target_pairs={{0,8},{4,12},{8,0},{12,4},{1,9},{5,13},{9,1},{13,5},{2,10},{6,14},... | collective-permute-start | bytes 393224 | tf_op jit(solution)/shard_map/ppermute | solution.py:35
  21.7 5.8 %collective-permute-start.8 = (bf16[512,128]{1,0:T(8,128)(2,1)S(1)}, bf16[512,128]{1,0:T(8,128)(2,1)S(1)}, u32[]{:S(2)}, u32[]{:S(2)}) collective-permute-start(bf16[512,128]{1,0:T(8,128)(2,1)S(1)} %step_b1.1.mine_ref.rest_0_.after_ref), channel_id=1, source_target_pairs={{0,4},{4,0},{8,12},{12,8},{1,5},{5,1},{9,13},{13,9},{2,6},{6,2},{1... | collective-permute-start | bytes 393224 | tf_op jit(solution)/shard_map/ppermute | solution.py:35
  27.5 7.4 %collective-permute-start.13 = (bf16[512,128]{1,0:T(8,128)(2,1)S(1)}, bf16[512,128]{1,0:T(8,128)(2,1)S(1)}, u32[]{:S(2)}, u32[]{:S(2)}) collective-permute-start(bf16[512,128]{1,0:T(8,128)(2,1)S(1)} %step_b3.1.rest_0_.mine_ref), channel_id=1, source_target_pairs={{0,8},{4,12},{8,0},{12,4},{1,9},{5,13},{9,1},{13,5},{2,10},{6,14},... | collective-permute-start | bytes 393224 | tf_op jit(solution)/shard_map/ppermute | solution.py:35
  27.7 5.0 %collective-permute-start.11 = (bf16[512,128]{1,0:T(8,128)(2,1)S(1)}, bf16[512,128]{1,0:T(8,128)(2,1)S(1)}, u32[]{:S(2)}, u32[]{:S(2)}) collective-permute-start(bf16[512,128]{1,0:T(8,128)(2,1)S(1)} %get-tuple-element.44.after_ref.mine_ref), channel_id=1, source_target_pairs={{0,16},{16,0},{1,17},{17,1},{2,18},{18,2},{3,19},{19,3},{4,20},{20... | collective-permute-start | bytes 393224 | tf_op jit(solution)/shard_map/ppermute | solution.py:35
  31.1 4.3 %copy-start.2 = (s32[256]{0:T(256)S(1)}, s32[256]{0:T(256)}, u32[]{:S(2)}) copy-start(s32[256]{0:T(256)} %param.15) | copy-start | bytes 3076
  31.1 11.5 %collective-permute-start.9 = (bf16[512,1024]{1,0:T(8,128)(2,1)S(1)}, bf16[512,1024]{1,0:T(8,128)(2,1)S(1)}, u32[]{:S(2)}, u32[]{:S(2)}) collective-permute-start(bf16[512,1024]{1,0:T(8,128)(2,1)S(1)} %get-tuple-element.45), channel_id=1, source_target_pairs={{0,1},{1,0},{2,3},{3,2},{4,5},{5,4},{6,7},{7,6},{8,9},{9,8},{10,11... | collective-permute-start | bytes 3145736 | tf_op jit(solution)/shard_map/ppermute | solution.py:35
  32.7 5.0 %collective-permute-start.12 = (bf16[512,128]{1,0:T(8,128)(2,1)S(1)}, bf16[512,128]{1,0:T(8,128)(2,1)S(1)}, u32[]{:S(2)}, u32[]{:S(2)}) collective-permute-start(bf16[512,128]{1,0:T(8,128)(2,1)S(1)} %step_a6.1.rest_0_.mine_a), channel_id=1, source_target_pairs={{0,4},{4,0},{8,12},{12,8},{1,5},{5,1},{9,13},{13,9},{2,6},{6,2},{1... | collective-permute-start | bytes 393224 | tf_op jit(solution)/shard_map/ppermute | solution.py:35
  34.9 5.0 %collective-permute-start.15 = (bf16[512,128]{1,0:T(8,128)(2,1)S(1)}, bf16[512,128]{1,0:T(8,128)(2,1)S(1)}, u32[]{:S(2)}, u32[]{:S(2)}) collective-permute-start(bf16[512,128]{1,0:T(8,128)(2,1)S(1)} %step_b7.1.after_ref.mine_b), channel_id=1, source_target_pairs={{0,16},{16,0},{1,17},{17,1},{2,18},{18,2},{3,19},{19,3},{4,20},{20... | collective-permute-start | bytes 393224 | tf_op jit(solution)/shard_map/ppermute | solution.py:35
  38.3 1.9 %collective-permute-start.14 = (bf16[512,128]{1,0:T(8,128)(2,1)S(1)}, bf16[512,128]{1,0:T(8,128)(2,1)S(1)}, u32[]{:S(2)}, u32[]{:S(2)}) collective-permute-start(bf16[512,128]{1,0:T(8,128)(2,1)S(1)} %get-tuple-element.46.after_ref.x_ref), channel_id=1, source_target_pairs={{0,1},{1,0},{2,3},{3,2},{4,5},{5,4},{6,7},{7,6},{8,9},{9,8},{10,11... | collective-permute-start | bytes 393224 | tf_op jit(solution)/shard_map/ppermute | solution.py:35
  40.1 1.4 %collective-permute-start.17 = (bf16[32,128]{1,0:T(8,128)(2,1)S(1)}, bf16[32,128]{1,0:T(8,128)(2,1)S(1)}, u32[]{:S(2)}, u32[]{:S(2)}) collective-permute-start(bf16[32,128]{1,0:T(8,128)(2,1)S(1)} %get-tuple-element.49.after_ref.a_ref), channel_id=1, source_target_pairs={{0,1},{1,0},{2,3},{3,2},{4,5},{5,4},{6,7},{7,6},{8,9},{9,8},{10,11... | collective-permute-start | bytes 24584 | tf_op jit(solution)/shard_map/ppermute | solution.py:35
  40.3 6.5 %collective-permute-start.16 = (bf16[512,128]{1,0:T(8,128)(2,1)S(1)}, bf16[512,128]{1,0:T(8,128)(2,1)S(1)}, u32[]{:S(2)}, u32[]{:S(2)}) collective-permute-start(bf16[512,128]{1,0:T(8,128)(2,1)S(1)} %merge.1.after_ref.s_ref), channel_id=1, source_target_pairs={{0,2},{1,3},{2,0},{3,1},{4,6},{5,7},{6,4},{7,5},{8,10},{9,11},{10,... | collective-permute-start | bytes 393224 | tf_op jit(solution)/shard_map/ppermute | solution.py:35
  41.5 5.2 %copy-start = (f32[1024,128]{1,0:T(8,128)S(1)}, f32[1024,128]{1,0:T(8,128)}, u32[]{:S(2)}) copy-start(f32[1024,128]{1,0:T(8,128)} %a_ref.1) | copy-start | bytes 1572868
  41.5 5.2 %copy-start.1 = (f32[128,1024]{1,0:T(8,128)S(1)}, f32[128,1024]{1,0:T(8,128)}, u32[]{:S(2)}) copy-start(f32[128,1024]{1,0:T(8,128)} %b_ref.1) | copy-start | bytes 1572868
  41.6 5.2 %collective-permute-start.18 = (bf16[32,128]{1,0:T(8,128)(2,1)S(1)}, bf16[32,128]{1,0:T(8,128)(2,1)S(1)}, u32[]{:S(2)}, u32[]{:S(2)}) collective-permute-start(bf16[32,128]{1,0:T(8,128)(2,1)S(1)} %norm_merge.1.sn_ref), channel_id=1, source_target_pairs={{0,2},{1,3},{2,0},{3,1},{4,6},{5,7},{6,4},{7,5},{8,10},{9,11},{10,... | collective-permute-start | bytes 24584 | tf_op jit(solution)/shard_map/ppermute | solution.py:35

commit v19 on v18

--- a/solution.py
+++ b/solution.py
@@ -117,10 +117,12 @@
         outs[i // per][:, i % per * cut : (i % per + 1) * cut] = dot(hg_ref[...], w_ref[i]).astype(BF)
 
 
-def diag_kernel(hg_ref, w_ref, w_hbm, low_ref, after_ref, out_ref, next_ref, rest_ref, sems):
-    per, width, cut = next_ref.shape
+def diag_kernel(hg_ref, w_ref, w_hbm, low_ref, after_ref, out_ref, *refs):
+    *next_refs, rest_ref, sems = refs
+    width, cut = w_ref.shape
+    per = width // cut
     sources = weight_blocks((3, 2), w_hbm, cut)[1:]
-    targets = [rest_ref.at[i] for i in range(per - 1)] + [next_ref.at[i] for i in range(per)]
+    targets = [rest_ref.at[i] for i in range(per - 1)] + next_refs
     copies = fetch(sources, targets, sems)
     out_ref[:, :cut] = dot(hg_ref[...], w_ref[...]).astype(BF)
     out_ref[:, width:] = low_ref[...]
@@ -131,15 +133,15 @@
         copy.wait()
 
 
-def distant_kernel(hg_ref, w_ref, after_ref, out_ref):
-    per, _, cut = w_ref.shape
-    for i in range(per):
-        out_ref[:, i * cut : (i + 1) * cut] = dot(hg_ref[...], w_ref[i]).astype(BF)
-
-
-def far_kernel(mine_ref, diag_ref, got_ref, after_ref, out_ref):
-    width = mine_ref.shape[1]
-    sum_kernel(mine_ref, got_ref.at[:, :width], out_ref.at[:, :width])
+def block_kernel(hg_ref, w_ref, after_ref, out_ref):
+    out_ref[...] = dot(hg_ref[...], w_ref[...]).astype(BF)
+
+
+def far_kernel(first_ref, rest_ref, diag_ref, got_ref, out_ref):
+    cut = first_ref.shape[1]
+    width = 2 * cut
+    sum_kernel(first_ref, got_ref.at[:, :cut], out_ref.at[:, :cut])
+    sum_kernel(rest_ref, got_ref.at[:, cut:width], out_ref.at[:, cut:width])
     sum_kernel(diag_ref.at[:, width:], got_ref.at[:, width:], out_ref.at[:, width:])
 
 
@@ -351,9 +353,9 @@
             )
 
         per = width // cut
-        diag, columns = call(
+        diag, *columns = call(
             diag_kernel,
-            [wide, shape((per, width, cut), BF)],
+            [wide] + [shape((width, cut), BF)] * per,
             [VMEM, VMEM, HBM, VMEM, ANY],
             (gained, first_columns, keep_hbm(base_weight), low, low_u),
             "query_diag",
@@ -361,12 +363,14 @@
         )
         diag_got = swap(diag, "tp", n_tp, 1)
 
+        block = shape((count, cut), BF)
+        distant_first = call(block_kernel, block, [VMEM] * 2 + [ANY], (gained, columns[0], diag), "distant_first")
         half = width // 2
         keep_a, send_a = call(
             functools.partial(grad_a_kernel, path_a[0]),
             [shape((half, rank), F32), shape((half, rank), BF)],
             [VMEM] * 3 + [ANY],
-            (inputs, low_v, far_v, diag),
+            (inputs, low_v, far_v, distant_first),
             "grad_a",
         )
         keep_b, send_b = call(
@@ -376,8 +380,8 @@
             (cotangent, low_u, far_u, send_a),
             "grad_b",
         )
-        distant = call(distant_kernel, tall, [VMEM, VMEM, ANY], (gained, columns, send_b), "query_distant")
-        far = call(far_kernel, wide, [VMEM] * 3 + [ANY], (distant, diag, diag_got, send_b), "far")
+        distant_rest = call(block_kernel, block, [VMEM] * 2 + [ANY], (gained, columns[1], send_b), "distant_rest")
+        far = call(far_kernel, wide, [VMEM] * 4, (distant_first, distant_rest, diag, diag_got), "far")
         far_got = swap(far, "tp", n_tp, 2)
 
         def step(mine, send, way, after, passed, name):

time: 48.9 us -> 49.4 us (1.010)
  starting transfers between devices: 18.4 us -> 19.2 us
  waiting for transfers between devices: 11.9 us -> 11.1 us
  Pallas kernels: 16.3 us -> 16.8 us
    ppermute x19, waiting for transfers between devices: 11.9 us -> 11.1 us  [swap(): return lax.ppermute(x, axis, [(i, i ^ k) for i in range(n)])]
    ppermute x19, starting transfers between devices: 18.4 us -> 19.2 us  [swap(): return lax.ppermute(x, axis, [(i, i ^ k) for i in range(n)])]
    pallas_call x25 -> x26, Pallas kernels: 16.3 us -> 16.8 us  [call(): pl.pallas_call(kernel, out_shape=outs, in_specs=in_specs, out_specs=out_s...]
  transfers between devices with their start and end apart: 19 -> 19, of which waited for: 8 -> 8; matrix products, arithmetic and copies ran while one was open for 3% -> 3% of each run, Pallas kernels for 24% -> 25%
where the time goes in v19:
time: 49.4 us; the launch traced here: 49.3 us
  starting transfers between devices  19.2 us (39%)
  Pallas kernels  16.8 us (34%)
  waiting for transfers between devices  11.1 us (22%)
  other arithmetic  1.28 us (3%)
  between operations  0.88 us (2%)
    ppermute x19, starting transfers between devices, swap(): return lax.ppermute(x, axis, [(i, i ^ k) for i in range(n)])  19.2 us
    pallas_call x26, Pallas kernels, call(): pl.pallas_call(kernel, out_shape=outs, in_specs=in_specs, out_specs=out_s...  16.8 us
    ppermute x19, waiting for transfers between devices, swap(): return lax.ppermute(x, axis, [(i, i ^ k) for i in range(n)])  11.1 us
    cos x1, other arithmetic, turn_tables(): c, s = (jnp.cos(angle), jnp.sin(angle))  0.99 us
  transfers between devices with their start and end apart: 19, of which 8 were waited for; matrix products, arithmetic and copies ran while one was open for 3% of the time, Pallas kernels for 25%

profile of v19, /device:TPU:0, one launch (start us, length us, event | category | flops | bytes accessed | tf_op | source)
XLA Modules:
  0.0 49.3 jit_solution(13081928324230235565)
XLA Ops:
  0.6 2.4 %rank_v.1 = (bf16[384,128]{1,0:T(8,128)(2,1)S(1)}, bf16[384,1024]{1,0:T(8,128)(2,1)S(1)}, bf16[384,1024]{1,0:T(8,128)(2,1)S(1)}, bf16[1024,128]{1,0:T(8,128)(2,1...) custom-call(bf16[384,1024]{1,0:T(8,128)(2,1)} %x_hbm.1, bf16[384,1024]{1,0:T(8,128)(2,1)} %v_hbm.1, ...), custom_call_target="tpu_custom_call" | custom-call | flops 2760000000 | tf_op jit(solution)/shard_map/rank_v/pallas_call | solution.py:260
  3.0 0.5 %collective-permute-start = (bf16[384,128]{1,0:T(8,128)(2,1)S(1)}, bf16[384,128]{1,0:T(8,128)(2,1)S(1)}, u32[]{:S(2)}, u32[]{:S(2)}) collective-permute-start(bf16[384,128]{1,0:T(8,128)(2,1)S(1)} %get-tuple-element.35.x_ref), channel_id=1, source_target_pairs={{0,1},{1,0},{2,3},{3,2},{4,5},{5,4},{6,7},{7,6},{8,9},{9,8},{10,11... | collective-permute-start | bytes 294920 | tf_op jit(solution)/shard_map/ppermute | solution.py:35
  3.6 0.4 rank_u.1.x_ref
  3.9 0.1 collective-permute-start.2
  4.1 0.6 %prep.1 = (bf16[512,1024]{1,0:T(8,128)(2,1)S(1)}, bf16[512,128]{1,0:T(8,128)(2,1)S(1)}, f32[8,128]{1,0:T(8,128)S(1)}) custom-call(bf16[512,1024]{1,0:T(8,128)(2,1)S(1)} %get-tuple-element.31.h_ref, f32[1,1024]{1,0:T(1,128)S(1)} %bitcast.8, bf16[1024,128]{1,0:T(8,128)(2,1)S(1)} %get-tuple-element.32.a16_ref), custom_call_target="tpu_custom_call" | custom-call | flops 690000000 | tf_op jit(solution)/shard_map/prep/pallas_call | solution.py:260
  4.7 3.0 %collective-permute-start.1 = (bf16[384,128]{1,0:T(8,128)(2,1)S(1)}, bf16[384,128]{1,0:T(8,128)(2,1)S(1)}, u32[]{:S(2)}, u32[]{:S(2)}) collective-permute-start(bf16[384,128]{1,0:T(8,128)(2,1)S(1)} %low_v.1.after_ref.s_ref), channel_id=1, source_target_pairs={{0,2},{1,3},{2,0},{3,1},{4,6},{5,7},{6,4},{7,5},{8,10},{9,11},{10,... | collective-permute-start | bytes 294920 | tf_op jit(solution)/shard_map/ppermute | solution.py:35
  7.7 0.3 collective-permute-start.4
  8.1 2.3 %query_diag.1 = (bf16[512,1152]{1,0:T(8,128)(2,1)S(1)}, bf16[1024,512]{1,0:T(8,128)(2,1)S(1)}, bf16[1024,512]{1,0:T(8,128)(2,1)S(1)}) custom-call(bf16[512,1024]{1,0:T(8,128)(2,1)S(1)} %get-tuple-element.33.hg_ref, bf16[1024,512]{1,0:T(8,128)(2,1)S(1)} %get-tuple-element.37.w_ref, bf16[1024,4096]{1,0:T(8,128)(2,1)} %w_hbm.7, ...), custom_call_target="tpu_custom_call" | custom-call | flops 46000001024 | tf_op jit(solution)/shard_map/query_diag/pallas_call | solution.py:260
  10.4 0.1 collective-permute-start.5
  10.5 0.7 %distant_first.1.after_ref.first_ref = bf16[512,512]{1,0:T(8,128)(2,1)S(1)} custom-call(bf16[512,1024]{1,0:T(8,128)(2,1)S(1)} %get-tuple-element.33.hg_ref, bf16[1024,512]{1,0:T(8,128)(2,1)S(1)} %get-tuple-element.38.w_ref, bf16[512,1152]{1,0:T(8,128)(2,1)S(1)} %get-tuple-element.39.after_ref.diag_ref), custom_call_target="tpu_custom_call" | custom-call | flops 11500000 | tf_op jit(solution)/shard_map/distant_first/pallas_call | solution.py:260
  11.2 0.0 collective-permute-done.1.r_ref
  11.2 0.4 grad_a.1
  11.7 2.1 %collective-permute-start.3 = (bf16[512,128]{1,0:T(8,128)(2,1)S(1)}, bf16[512,128]{1,0:T(8,128)(2,1)S(1)}, u32[]{:S(2)}, u32[]{:S(2)}) collective-permute-start(bf16[512,128]{1,0:T(8,128)(2,1)S(1)} %get-tuple-element.41.after_ref), channel_id=1, source_target_pairs={{0,4},{4,0},{8,12},{12,8},{1,5},{5,1},{9,13},{13,9},{2,6},{6,2},{1... | collective-permute-start | bytes 393224 | tf_op jit(solution)/shard_map/ppermute | solution.py:35
  13.7 0.3 grad_b.1
  14.1 1.5 %collective-permute-start.7 = (bf16[512,128]{1,0:T(8,128)(2,1)S(1)}, bf16[512,128]{1,0:T(8,128)(2,1)S(1)}, u32[]{:S(2)}, u32[]{:S(2)}) collective-permute-start(bf16[512,128]{1,0:T(8,128)(2,1)S(1)} %get-tuple-element.44.after_ref), channel_id=1, source_target_pairs={{0,16},{16,0},{1,17},{17,1},{2,18},{18,2},{3,19},{19,3},{4,20},{20... | collective-permute-start | bytes 393224 | tf_op jit(solution)/shard_map/ppermute | solution.py:35
  15.6 0.7 %distant_rest.1.rest_ref = bf16[512,512]{1,0:T(8,128)(2,1)S(1)} custom-call(bf16[512,1024]{1,0:T(8,128)(2,1)S(1)} %get-tuple-element.33.hg_ref, bf16[1024,512]{1,0:T(8,128)(2,1)S(1)} %get-tuple-element.42.w_ref, bf16[512,128]{1,0:T(8,128)(2,1)S(1)} %get-tuple-element.44.after_ref), custom_call_target="tpu_custom_call" | custom-call | flops 11500000 | tf_op jit(solution)/shard_map/distant_rest/pallas_call | solution.py:260
  16.4 0.3 far.1.rest_0_.far_ref
  16.7 1.7 %collective-permute-start.10 = (bf16[512,1152]{1,0:T(8,128)(2,1)S(1)}, bf16[512,1152]{1,0:T(8,128)(2,1)S(1)}, u32[]{:S(2)}, u32[]{:S(2)}) collective-permute-start(bf16[512,1152]{1,0:T(8,128)(2,1)S(1)} %far.1.rest_0_.far_ref), channel_id=1, source_target_pairs={{0,2},{1,3},{2,0},{3,1},{4,6},{5,7},{6,4},{7,5},{8,10},{9,11},{10,... | collective-permute-start | bytes 3538952 | tf_op jit(solution)/shard_map/ppermute | solution.py:35
  18.4 2.7 %collective-permute-start.6 = (bf16[512,128]{1,0:T(8,128)(2,1)S(1)}, bf16[512,128]{1,0:T(8,128)(2,1)S(1)}, u32[]{:S(2)}, u32[]{:S(2)}) collective-permute-start(bf16[512,128]{1,0:T(8,128)(2,1)S(1)} %step_a0.1.rest_0_.mine_ref), channel_id=1, source_target_pairs={{0,8},{4,12},{8,0},{12,4},{1,9},{5,13},{9,1},{13,5},{2,10},{6,14},... | collective-permute-start | bytes 393224 | tf_op jit(solution)/shard_map/ppermute | solution.py:35
  21.1 1.1 %collective-permute-start.8 = (bf16[512,128]{1,0:T(8,128)(2,1)S(1)}, bf16[512,128]{1,0:T(8,128)(2,1)S(1)}, u32[]{:S(2)}, u32[]{:S(2)}) collective-permute-start(bf16[512,128]{1,0:T(8,128)(2,1)S(1)} %step_b1.1.mine_ref.rest_0_.after_ref), channel_id=1, source_target_pairs={{0,4},{4,0},{8,12},{12,8},{1,5},{5,1},{9,13},{13,9},{2,6},{6,2},{1... | collective-permute-start | bytes 393224 | tf_op jit(solution)/shard_map/ppermute | solution.py:35
  22.2 2.7 %query_beside.1.rest_1_ = bf16[512,1024]{1,0:T(8,128)(2,1)S(1)} custom-call(bf16[512,1024]{1,0:T(8,128)(2,1)S(1)} %get-tuple-element.33.hg_ref, bf16[1024,4096]{1,0:T(8,128)(2,1)} %w_hbm.7, bf16[512,128]{1,0:T(8,128)(2,1)S(1)} %step_b1.1.mine_ref.rest_0_.after_ref), custom_call_target="tpu_custom_call" | custom-call | flops 2070000000 | tf_op jit(solution)/shard_map/query_beside/pallas_call | solution.py:260
  24.9 2.8 %collective-permute-done.8.got_ref = bf16[512,128]{1,0:T(8,128)(2,1)S(1)} collective-permute-done((bf16[512,128]{1,0:T(8,128)(2,1)S(1)}, bf16[512,128]{1,0:T(8,128)(2,1)S(1)}, u32[]{:S(2)}, u32[]{:S(2)}) %collective-permute-start.8) | collective-permute-done | bytes 131104 | tf_op jit(solution)/shard_map/ppermute | solution.py:35
  27.7 0.6 %collective-permute-start.13 = (bf16[512,128]{1,0:T(8,128)(2,1)S(1)}, bf16[512,128]{1,0:T(8,128)(2,1)S(1)}, u32[]{:S(2)}, u32[]{:S(2)}) collective-permute-start(bf16[512,128]{1,0:T(8,128)(2,1)S(1)} %step_b3.1.rest_0_.mine_ref), channel_id=1, source_target_pairs={{0,8},{4,12},{8,0},{12,4},{1,9},{5,13},{9,1},{13,5},{2,10},{6,14},... | collective-permute-start | bytes 393224 | tf_op jit(solution)/shard_map/ppermute | solution.py:35
  28.3 1.5 %collective-permute-start.11 = (bf16[512,128]{1,0:T(8,128)(2,1)S(1)}, bf16[512,128]{1,0:T(8,128)(2,1)S(1)}, u32[]{:S(2)}, u32[]{:S(2)}) collective-permute-start(bf16[512,128]{1,0:T(8,128)(2,1)S(1)} %get-tuple-element.46.after_ref.mine_ref), channel_id=1, source_target_pairs={{0,16},{16,0},{1,17},{17,1},{2,18},{18,2},{3,19},{19,3},{4,20},{20... | collective-permute-start | bytes 393224 | tf_op jit(solution)/shard_map/ppermute | solution.py:35
  29.8 2.7 %query_close.1.rest_0_.mine_ref = bf16[512,1024]{1,0:T(8,128)(2,1)S(1)} custom-call(bf16[512,1024]{1,0:T(8,128)(2,1)S(1)} %get-tuple-element.33.hg_ref, bf16[1024,4096]{1,0:T(8,128)(2,1)} %w_hbm.7, bf16[512,128]{1,0:T(8,128)(2,1)S(1)} %get-tuple-element.46.after_ref.mine_ref), custom_call_target="tpu_custom_call" | custom-call | flops 3104999936 | tf_op jit(solution)/shard_map/query_close/pallas_call | solution.py:260
  32.5 0.0 copy-start.2
  32.5 0.1 collective-permute-start.9
  32.6 0.7 %collective-permute-done.11.got_ref = bf16[512,128]{1,0:T(8,128)(2,1)S(1)} collective-permute-done((bf16[512,128]{1,0:T(8,128)(2,1)S(1)}, bf16[512,128]{1,0:T(8,128)(2,1)S(1)}, u32[]{:S(2)}, u32[]{:S(2)}) %collective-permute-start.11) | collective-permute-done | bytes 131104 | tf_op jit(solution)/shard_map/ppermute | solution.py:35
  33.4 0.7 %collective-permute-start.12 = (bf16[512,128]{1,0:T(8,128)(2,1)S(1)}, bf16[512,128]{1,0:T(8,128)(2,1)S(1)}, u32[]{:S(2)}, u32[]{:S(2)}) collective-permute-start(bf16[512,128]{1,0:T(8,128)(2,1)S(1)} %step_a6.1.rest_0_.mine_a), channel_id=1, source_target_pairs={{0,4},{4,0},{8,12},{12,8},{1,5},{5,1},{9,13},{13,9},{2,6},{6,2},{1... | collective-permute-start | bytes 393224 | tf_op jit(solution)/shard_map/ppermute | solution.py:35
  34.1 1.0 %collective-permute-done.13.got_ref = bf16[512,128]{1,0:T(8,128)(2,1)S(1)} collective-permute-done((bf16[512,128]{1,0:T(8,128)(2,1)S(1)}, bf16[512,128]{1,0:T(8,128)(2,1)S(1)}, u32[]{:S(2)}, u32[]{:S(2)}) %collective-permute-start.13) | collective-permute-done | bytes 131104 | tf_op jit(solution)/shard_map/ppermute | solution.py:35
  35.0 0.8 %collective-permute-start.15 = (bf16[512,128]{1,0:T(8,128)(2,1)S(1)}, bf16[512,128]{1,0:T(8,128)(2,1)S(1)}, u32[]{:S(2)}, u32[]{:S(2)}) collective-permute-start(bf16[512,128]{1,0:T(8,128)(2,1)S(1)} %step_b7.1.after_ref.mine_b), channel_id=1, source_target_pairs={{0,16},{16,0},{1,17},{17,1},{2,18},{18,2},{3,19},{19,3},{4,20},{20... | collective-permute-start | bytes 393224 | tf_op jit(solution)/shard_map/ppermute | solution.py:35
  35.9 1.0 %multiply_cosine_fusion.1 = (f32[256,64]{1,0:T(8,128)S(1)}, f32[256,64]{1,0:T(8,128)S(1)}, f32[256,64]{1,0:T(8,128)S(1)}, f32[256,64]{1,0:T(8,128)S(1)}, f32[256,64]{1,0:T(8,128)S(1)}, /*index=5*/f32[256,64]{1,0:T(8,128)S(1)}) fusion(f32[64]{0:T(128)S(1)} %multiply_power_fusion, f32[256]{0:T(256)S(1)} %bitcast.6, f32[256]{0:T(256)S(1)} %broadcast_add_fusion), kind=kLoop, calls=%fused_computation.4 | loop fusion | flops 65536 | bytes 395520 | tf_op jit(solution)/shard_map/cos | solution.py:281
  36.9 0.1 maximum_maximum_fusion.after_ref.sin_ref
  37.0 1.6 %collective-permute-done.12.got_a = bf16[512,128]{1,0:T(8,128)(2,1)S(1)} collective-permute-done((bf16[512,128]{1,0:T(8,128)(2,1)S(1)}, bf16[512,128]{1,0:T(8,128)(2,1)S(1)}, u32[]{:S(2)}, u32[]{:S(2)}) %collective-permute-start.12) | collective-permute-done | bytes 131104 | tf_op jit(solution)/shard_map/ppermute | solution.py:35
  38.6 0.5 update.1
  39.1 0.1 collective-permute-start.14
  39.2 0.9 %collective-permute-done.15.got_b = bf16[512,128]{1,0:T(8,128)(2,1)S(1)} collective-permute-done((bf16[512,128]{1,0:T(8,128)(2,1)S(1)}, bf16[512,128]{1,0:T(8,128)(2,1)S(1)}, u32[]{:S(2)}, u32[]{:S(2)}) %collective-permute-start.15) | collective-permute-done | bytes 131104 | tf_op jit(solution)/shard_map/ppermute | solution.py:35
  40.1 0.2 norm.1
  40.3 0.1 collective-permute-start.17
  40.4 0.1 collective-permute-done.14.got_ref
  40.5 1.4 %collective-permute-start.16 = (bf16[512,128]{1,0:T(8,128)(2,1)S(1)}, bf16[512,128]{1,0:T(8,128)(2,1)S(1)}, u32[]{:S(2)}, u32[]{:S(2)}) collective-permute-start(bf16[512,128]{1,0:T(8,128)(2,1)S(1)} %merge.1.after_ref.s_ref), channel_id=1, source_target_pairs={{0,2},{1,3},{2,0},{3,1},{4,6},{5,7},{6,4},{7,5},{8,10},{9,11},{10,... | collective-permute-start | bytes 393224 | tf_op jit(solution)/shard_map/ppermute | solution.py:35
  41.9 0.1 maximum_maximum_fusion.1.cos_ref
  42.1 0.0 copy-start
  42.1 0.8 %collective-permute-start.18 = (bf16[32,128]{1,0:T(8,128)(2,1)S(1)}, bf16[32,128]{1,0:T(8,128)(2,1)S(1)}, u32[]{:S(2)}, u32[]{:S(2)}) collective-permute-start(bf16[32,128]{1,0:T(8,128)(2,1)S(1)} %norm_merge.1.sn_ref), channel_id=1, source_target_pairs={{0,2},{1,3},{2,0},{3,1},{4,6},{5,7},{6,4},{7,5},{8,10},{9,11},{10,... | collective-permute-start | bytes 24584 | tf_op jit(solution)/shard_map/ppermute | solution.py:35
  42.9 2.0 %collective-permute-done.10.far_got = bf16[512,1152]{1,0:T(8,128)(2,1)S(1)} collective-permute-done((bf16[512,1152]{1,0:T(8,128)(2,1)S(1)}, bf16[512,1152]{1,0:T(8,128)(2,1)S(1)}, u32[]{:S(2)}, u32[]{:S(2)}) %collective-permute-start.10) | collective-permute-done | bytes 1179680 | tf_op jit(solution)/shard_map/ppermute | solution.py:35
  44.9 0.5 base.1
  45.4 1.9 %collective-permute-done.18.rn_ref = bf16[32,128]{1,0:T(8,128)(2,1)S(1)} collective-permute-done((bf16[32,128]{1,0:T(8,128)(2,1)S(1)}, bf16[32,128]{1,0:T(8,128)(2,1)S(1)}, u32[]{:S(2)}, u32[]{:S(2)}) %collective-permute-start.18) | collective-permute-done | bytes 8224 | tf_op jit(solution)/shard_map/ppermute | solution.py:35
  47.3 2.0 %final.1 = (f32[1024,128]{1,0:T(8,128)}, f32[128,1024]{1,0:T(8,128)}, bf16[512,1024]{1,0:T(8,128)(2,1)}) custom-call(f32[512,1024]{1,0:T(8,128)S(1)} %get-tuple-element.52.base_ref, f32[512,128]{1,0:T(8,128)S(1)} %get-tuple-element.53.low_ref, bf16[512,128]{1,0:T(8,128)(2,1)S(1)} %merge.1.after_ref.s_ref, ...), custom_call_target="tpu_custom_call" | custom-call | flops 2070000000 | tf_op jit(solution)/shard_map/final/pallas_call | solution.py:260
  (29 shorter events, 0.3 us)
Async XLA Ops:
  0.6 3.4 %copy-start.3 = (f32[1024]{0:T(1024)S(1)}, f32[1024]{0:T(1024)}, u32[]{:S(2)}) copy-start(f32[1024]{0:T(1024)} %param.14) | copy-start | bytes 12292
  3.0 1.6 %collective-permute-start = (bf16[384,128]{1,0:T(8,128)(2,1)S(1)}, bf16[384,128]{1,0:T(8,128)(2,1)S(1)}, u32[]{:S(2)}, u32[]{:S(2)}) collective-permute-start(bf16[384,128]{1,0:T(8,128)(2,1)S(1)} %get-tuple-element.35.x_ref), channel_id=1, source_target_pairs={{0,1},{1,0},{2,3},{3,2},{4,5},{5,4},{6,7},{7,6},{8,9},{9,8},{10,11... | collective-permute-start | bytes 294920 | tf_op jit(solution)/shard_map/ppermute | solution.py:35
  3.9 3.8 %collective-permute-start.2 = (bf16[384,128]{1,0:T(8,128)(2,1)S(1)}, bf16[384,128]{1,0:T(8,128)(2,1)S(1)}, u32[]{:S(2)}, u32[]{:S(2)}) collective-permute-start(bf16[384,128]{1,0:T(8,128)(2,1)S(1)} %rank_u.1.x_ref), channel_id=1, source_target_pairs={{0,1},{1,0},{2,3},{3,2},{4,5},{5,4},{6,7},{7,6},{8,9},{9,8},{10,11... | collective-permute-start | bytes 294920 | tf_op jit(solution)/shard_map/ppermute | solution.py:35
  4.7 6.6 %collective-permute-start.1 = (bf16[384,128]{1,0:T(8,128)(2,1)S(1)}, bf16[384,128]{1,0:T(8,128)(2,1)S(1)}, u32[]{:S(2)}, u32[]{:S(2)}) collective-permute-start(bf16[384,128]{1,0:T(8,128)(2,1)S(1)} %low_v.1.after_ref.s_ref), channel_id=1, source_target_pairs={{0,2},{1,3},{2,0},{3,1},{4,6},{5,7},{6,4},{7,5},{8,10},{9,11},{10,... | collective-permute-start | bytes 294920 | tf_op jit(solution)/shard_map/ppermute | solution.py:35
  7.7 6.0 %collective-permute-start.4 = (bf16[384,128]{1,0:T(8,128)(2,1)S(1)}, bf16[384,128]{1,0:T(8,128)(2,1)S(1)}, u32[]{:S(2)}, u32[]{:S(2)}) collective-permute-start(bf16[384,128]{1,0:T(8,128)(2,1)S(1)} %low_u.1.after_ref.s_ref), channel_id=1, source_target_pairs={{0,2},{1,3},{2,0},{3,1},{4,6},{5,7},{6,4},{7,5},{8,10},{9,11},{10,... | collective-permute-start | bytes 294920 | tf_op jit(solution)/shard_map/ppermute | solution.py:35
  10.4 6.0 %collective-permute-start.5 = (bf16[512,1152]{1,0:T(8,128)(2,1)S(1)}, bf16[512,1152]{1,0:T(8,128)(2,1)S(1)}, u32[]{:S(2)}, u32[]{:S(2)}) collective-permute-start(bf16[512,1152]{1,0:T(8,128)(2,1)S(1)} %get-tuple-element.39.after_ref.diag_ref), channel_id=1, source_target_pairs={{0,1},{1,0},{2,3},{3,2},{4,5},{5,4},{6,7},{7,6},{8,9},{9,8},{10,11... | collective-permute-start | bytes 3538952 | tf_op jit(solution)/shard_map/ppermute | solution.py:35
  11.7 6.7 %collective-permute-start.3 = (bf16[512,128]{1,0:T(8,128)(2,1)S(1)}, bf16[512,128]{1,0:T(8,128)(2,1)S(1)}, u32[]{:S(2)}, u32[]{:S(2)}) collective-permute-start(bf16[512,128]{1,0:T(8,128)(2,1)S(1)} %get-tuple-element.41.after_ref), channel_id=1, source_target_pairs={{0,4},{4,0},{8,12},{12,8},{1,5},{5,1},{9,13},{13,9},{2,6},{6,2},{1... | collective-permute-start | bytes 393224 | tf_op jit(solution)/shard_map/ppermute | solution.py:35
  14.1 7.0 %collective-permute-start.7 = (bf16[512,128]{1,0:T(8,128)(2,1)S(1)}, bf16[512,128]{1,0:T(8,128)(2,1)S(1)}, u32[]{:S(2)}, u32[]{:S(2)}) collective-permute-start(bf16[512,128]{1,0:T(8,128)(2,1)S(1)} %get-tuple-element.44.after_ref), channel_id=1, source_target_pairs={{0,16},{16,0},{1,17},{17,1},{2,18},{18,2},{3,19},{19,3},{4,20},{20... | collective-permute-start | bytes 393224 | tf_op jit(solution)/shard_map/ppermute | solution.py:35
  16.7 28.3 %collective-permute-start.10 = (bf16[512,1152]{1,0:T(8,128)(2,1)S(1)}, bf16[512,1152]{1,0:T(8,128)(2,1)S(1)}, u32[]{:S(2)}, u32[]{:S(2)}) collective-permute-start(bf16[512,1152]{1,0:T(8,128)(2,1)S(1)} %far.1.rest_0_.far_ref), channel_id=1, source_target_pairs={{0,2},{1,3},{2,0},{3,1},{4,6},{5,7},{6,4},{7,5},{8,10},{9,11},{10,... | collective-permute-start | bytes 3538952 | tf_op jit(solution)/shard_map/ppermute | solution.py:35
  18.4 9.8 %collective-permute-start.6 = (bf16[512,128]{1,0:T(8,128)(2,1)S(1)}, bf16[512,128]{1,0:T(8,128)(2,1)S(1)}, u32[]{:S(2)}, u32[]{:S(2)}) collective-permute-start(bf16[512,128]{1,0:T(8,128)(2,1)S(1)} %step_a0.1.rest_0_.mine_ref), channel_id=1, source_target_pairs={{0,8},{4,12},{8,0},{12,4},{1,9},{5,13},{9,1},{13,5},{2,10},{6,14},... | collective-permute-start | bytes 393224 | tf_op jit(solution)/shard_map/ppermute | solution.py:35
  21.1 6.5 %collective-permute-start.8 = (bf16[512,128]{1,0:T(8,128)(2,1)S(1)}, bf16[512,128]{1,0:T(8,128)(2,1)S(1)}, u32[]{:S(2)}, u32[]{:S(2)}) collective-permute-start(bf16[512,128]{1,0:T(8,128)(2,1)S(1)} %step_b1.1.mine_ref.rest_0_.after_ref), channel_id=1, source_target_pairs={{0,4},{4,0},{8,12},{12,8},{1,5},{5,1},{9,13},{13,9},{2,6},{6,2},{1... | collective-permute-start | bytes 393224 | tf_op jit(solution)/shard_map/ppermute | solution.py:35
  27.7 7.3 %collective-permute-start.13 = (bf16[512,128]{1,0:T(8,128)(2,1)S(1)}, bf16[512,128]{1,0:T(8,128)(2,1)S(1)}, u32[]{:S(2)}, u32[]{:S(2)}) collective-permute-start(bf16[512,128]{1,0:T(8,128)(2,1)S(1)} %step_b3.1.rest_0_.mine_ref), channel_id=1, source_target_pairs={{0,8},{4,12},{8,0},{12,4},{1,9},{5,13},{9,1},{13,5},{2,10},{6,14},... | collective-permute-start | bytes 393224 | tf_op jit(solution)/shard_map/ppermute | solution.py:35
  28.3 5.0 %collective-permute-start.11 = (bf16[512,128]{1,0:T(8,128)(2,1)S(1)}, bf16[512,128]{1,0:T(8,128)(2,1)S(1)}, u32[]{:S(2)}, u32[]{:S(2)}) collective-permute-start(bf16[512,128]{1,0:T(8,128)(2,1)S(1)} %get-tuple-element.46.after_ref.mine_ref), channel_id=1, source_target_pairs={{0,16},{16,0},{1,17},{17,1},{2,18},{18,2},{3,19},{19,3},{4,20},{20... | collective-permute-start | bytes 393224 | tf_op jit(solution)/shard_map/ppermute | solution.py:35
  32.5 3.3 %copy-start.2 = (s32[256]{0:T(256)S(1)}, s32[256]{0:T(256)}, u32[]{:S(2)}) copy-start(s32[256]{0:T(256)} %param.15) | copy-start | bytes 3076
  32.5 10.4 %collective-permute-start.9 = (bf16[512,1024]{1,0:T(8,128)(2,1)S(1)}, bf16[512,1024]{1,0:T(8,128)(2,1)S(1)}, u32[]{:S(2)}, u32[]{:S(2)}) collective-permute-start(bf16[512,1024]{1,0:T(8,128)(2,1)S(1)} %get-tuple-element.47), channel_id=1, source_target_pairs={{0,1},{1,0},{2,3},{3,2},{4,5},{5,4},{6,7},{7,6},{8,9},{9,8},{10,11... | collective-permute-start | bytes 3145736 | tf_op jit(solution)/shard_map/ppermute | solution.py:35
  33.4 5.2 %collective-permute-start.12 = (bf16[512,128]{1,0:T(8,128)(2,1)S(1)}, bf16[512,128]{1,0:T(8,128)(2,1)S(1)}, u32[]{:S(2)}, u32[]{:S(2)}) collective-permute-start(bf16[512,128]{1,0:T(8,128)(2,1)S(1)} %step_a6.1.rest_0_.mine_a), channel_id=1, source_target_pairs={{0,4},{4,0},{8,12},{12,8},{1,5},{5,1},{9,13},{13,9},{2,6},{6,2},{1... | collective-permute-start | bytes 393224 | tf_op jit(solution)/shard_map/ppermute | solution.py:35
  35.0 5.0 %collective-permute-start.15 = (bf16[512,128]{1,0:T(8,128)(2,1)S(1)}, bf16[512,128]{1,0:T(8,128)(2,1)S(1)}, u32[]{:S(2)}, u32[]{:S(2)}) collective-permute-start(bf16[512,128]{1,0:T(8,128)(2,1)S(1)} %step_b7.1.after_ref.mine_b), channel_id=1, source_target_pairs={{0,16},{16,0},{1,17},{17,1},{2,18},{18,2},{3,19},{19,3},{4,20},{20... | collective-permute-start | bytes 393224 | tf_op jit(solution)/shard_map/ppermute | solution.py:35
  39.1 1.4 %collective-permute-start.14 = (bf16[512,128]{1,0:T(8,128)(2,1)S(1)}, bf16[512,128]{1,0:T(8,128)(2,1)S(1)}, u32[]{:S(2)}, u32[]{:S(2)}) collective-permute-start(bf16[512,128]{1,0:T(8,128)(2,1)S(1)} %get-tuple-element.48.after_ref.x_ref), channel_id=1, source_target_pairs={{0,1},{1,0},{2,3},{3,2},{4,5},{5,4},{6,7},{7,6},{8,9},{9,8},{10,11... | collective-permute-start | bytes 393224 | tf_op jit(solution)/shard_map/ppermute | solution.py:35
  40.3 1.8 %collective-permute-start.17 = (bf16[32,128]{1,0:T(8,128)(2,1)S(1)}, bf16[32,128]{1,0:T(8,128)(2,1)S(1)}, u32[]{:S(2)}, u32[]{:S(2)}) collective-permute-start(bf16[32,128]{1,0:T(8,128)(2,1)S(1)} %get-tuple-element.51.after_ref.a_ref), channel_id=1, source_target_pairs={{0,1},{1,0},{2,3},{3,2},{4,5},{5,4},{6,7},{7,6},{8,9},{9,8},{10,11... | collective-permute-start | bytes 24584 | tf_op jit(solution)/shard_map/ppermute | solution.py:35
  40.5 6.7 %collective-permute-start.16 = (bf16[512,128]{1,0:T(8,128)(2,1)S(1)}, bf16[512,128]{1,0:T(8,128)(2,1)S(1)}, u32[]{:S(2)}, u32[]{:S(2)}) collective-permute-start(bf16[512,128]{1,0:T(8,128)(2,1)S(1)} %merge.1.after_ref.s_ref), channel_id=1, source_target_pairs={{0,2},{1,3},{2,0},{3,1},{4,6},{5,7},{6,4},{7,5},{8,10},{9,11},{10,... | collective-permute-start | bytes 393224 | tf_op jit(solution)/shard_map/ppermute | solution.py:35
  42.1 5.2 %copy-start = (f32[1024,128]{1,0:T(8,128)S(1)}, f32[1024,128]{1,0:T(8,128)}, u32[]{:S(2)}) copy-start(f32[1024,128]{1,0:T(8,128)} %a_ref.1) | copy-start | bytes 1572868
  42.1 5.2 %copy-start.1 = (f32[128,1024]{1,0:T(8,128)S(1)}, f32[128,1024]{1,0:T(8,128)}, u32[]{:S(2)}) copy-start(f32[128,1024]{1,0:T(8,128)} %b_ref.1) | copy-start | bytes 1572868
  42.1 5.2 %collective-permute-start.18 = (bf16[32,128]{1,0:T(8,128)(2,1)S(1)}, bf16[32,128]{1,0:T(8,128)(2,1)S(1)}, u32[]{:S(2)}, u32[]{:S(2)}) collective-permute-start(bf16[32,128]{1,0:T(8,128)(2,1)S(1)} %norm_merge.1.sn_ref), channel_id=1, source_target_pairs={{0,2},{1,3},{2,0},{3,1},{4,6},{5,7},{6,4},{7,5},{8,10},{9,11},{10,... | collective-permute-start | bytes 24584 | tf_op jit(solution)/shard_map/ppermute | solution.py:35

commit v20 on v18

--- a/solution.py
+++ b/solution.py
@@ -227,9 +227,6 @@
         half_b[:, c] = fresh.astype(BF)
     copies = [pltpu.make_async_copy(new_b, b_hbm, sems.at[0])]
     copies[-1].start()
-    new_a[...] = a_ref[...] - rate * ga_ref[...].astype(F32)
-    copies.append(pltpu.make_async_copy(new_a, a_hbm, sems.at[1]))
-    copies[-1].start()
     for i, b in enumerate(blocks_of(count)):
         low = s_ref[b].astype(F32) + r_ref[b].astype(F32)
         scale = jnp.broadcast_to(scales[i : i + 1], (LANES, LANES)).T
@@ -240,7 +237,12 @@
             query = base_ref[b, c] * scale + update[:, c]
             other = pltpu.roll(query, HEAD // 2, 1)
             out[b, c] = (query * cos + other * sin).astype(BF)
-        copies.append(pltpu.make_async_copy(out.at[b], q_hbm.at[b], sems.at[2 + i]))
+        copies.append(pltpu.make_async_copy(out.at[b], q_hbm.at[b], sems.at[1 + i]))
+        copies[-1].start()
+        part = a_ref.shape[0] * LANES // count
+        rows = slice(i * part, (i + 1) * part)
+        new_a[rows] = a_ref[rows] - rate * ga_ref[rows].astype(F32)
+        copies.append(pltpu.make_async_copy(new_a.at[rows], a_hbm.at[rows], sems.at[1 + count // LANES + i]))
         copies[-1].start()
     for copy in copies:
         copy.wait()
@@ -450,7 +452,7 @@
             (base, low_all, step_sum, step_far, norm_sum, norm_far, grad_a, grad_b, factor_a, factor_b, cos, sin),
             "final",
             [pltpu.VMEM((width, rank), F32), pltpu.VMEM((rank, width), F32),
-             pltpu.VMEM((rank, width), BF), pltpu.VMEM((count, width), BF), dma(2 + count // LANES)],
+             pltpu.VMEM((rank, width), BF), pltpu.VMEM((count, width), BF), dma(1 + 2 * (count // LANES))],
             [HBM] * 3,
         )
         return new_a, new_b, queries.reshape(steps, rows, width)

time: 48.9 us -> 48.9 us (level)
  transfers between devices with their start and end apart: 19 -> 19, of which waited for: 8 -> 8; matrix products, arithmetic and copies ran while one was open for 3% -> 3% of each run, Pallas kernels for 24% -> 25%
where the time goes in v20:
time: 48.9 us; the launch traced here: 48.7 us
  starting transfers between devices  18.4 us (38%)
  Pallas kernels  16.3 us (33%)
  waiting for transfers between devices  11.9 us (24%)
  other arithmetic  1.28 us (3%)
  between operations  0.89 us (2%)
    ppermute x19, starting transfers between devices, swap(): return lax.ppermute(x, axis, [(i, i ^ k) for i in range(n)])  18.4 us
    pallas_call x25, Pallas kernels, call(): pl.pallas_call(kernel, out_shape=outs, in_specs=in_specs, out_specs=out_s...  16.3 us
    ppermute x19, waiting for transfers between devices, swap(): return lax.ppermute(x, axis, [(i, i ^ k) for i in range(n)])  11.9 us
    cos x1, other arithmetic, turn_tables(): c, s = (jnp.cos(angle), jnp.sin(angle))  0.99 us
  transfers between devices with their start and end apart: 19, of which 8 were waited for; matrix products, arithmetic and copies ran while one was open for 3% of the time, Pallas kernels for 25%

profile of v20, /device:TPU:0, one launch (start us, length us, event | category | flops | bytes accessed | tf_op | source)
XLA Modules:
  0.0 48.7 jit_solution(12374463532131859243)
XLA Ops:
  0.6 2.4 %rank_v.1 = (bf16[384,128]{1,0:T(8,128)(2,1)S(1)}, bf16[384,1024]{1,0:T(8,128)(2,1)S(1)}, bf16[384,1024]{1,0:T(8,128)(2,1)S(1)}, bf16[1024,128]{1,0:T(8,128)(2,1...) custom-call(bf16[384,1024]{1,0:T(8,128)(2,1)} %x_hbm.1, bf16[384,1024]{1,0:T(8,128)(2,1)} %v_hbm.1, ...), custom_call_target="tpu_custom_call" | custom-call | flops 2760000000 | tf_op jit(solution)/shard_map/rank_v/pallas_call | solution.py:260
  3.0 0.5 %collective-permute-start = (bf16[384,128]{1,0:T(8,128)(2,1)S(1)}, bf16[384,128]{1,0:T(8,128)(2,1)S(1)}, u32[]{:S(2)}, u32[]{:S(2)}) collective-permute-start(bf16[384,128]{1,0:T(8,128)(2,1)S(1)} %get-tuple-element.34.x_ref), channel_id=1, source_target_pairs={{0,1},{1,0},{2,3},{3,2},{4,5},{5,4},{6,7},{7,6},{8,9},{9,8},{10,11... | collective-permute-start | bytes 294920 | tf_op jit(solution)/shard_map/ppermute | solution.py:35
  3.6 0.4 rank_u.1.x_ref
  3.9 0.1 collective-permute-start.2
  4.1 0.6 %prep.1 = (bf16[512,1024]{1,0:T(8,128)(2,1)S(1)}, bf16[512,128]{1,0:T(8,128)(2,1)S(1)}, f32[8,128]{1,0:T(8,128)S(1)}) custom-call(bf16[512,1024]{1,0:T(8,128)(2,1)S(1)} %get-tuple-element.30.h_ref, f32[1,1024]{1,0:T(1,128)S(1)} %bitcast.8, bf16[1024,128]{1,0:T(8,128)(2,1)S(1)} %get-tuple-element.31.a16_ref), custom_call_target="tpu_custom_call" | custom-call | flops 690000000 | tf_op jit(solution)/shard_map/prep/pallas_call | solution.py:260
  4.6 0.0 collective-permute-done.got_ref
  4.7 3.0 %collective-permute-start.1 = (bf16[384,128]{1,0:T(8,128)(2,1)S(1)}, bf16[384,128]{1,0:T(8,128)(2,1)S(1)}, u32[]{:S(2)}, u32[]{:S(2)}) collective-permute-start(bf16[384,128]{1,0:T(8,128)(2,1)S(1)} %low_v.1.after_ref.s_ref), channel_id=1, source_target_pairs={{0,2},{1,3},{2,0},{3,1},{4,6},{5,7},{6,4},{7,5},{8,10},{9,11},{10,... | collective-permute-start | bytes 294920 | tf_op jit(solution)/shard_map/ppermute | solution.py:35
  7.7 0.3 collective-permute-start.4
  8.1 2.0 %query_diag.1 = (bf16[512,1152]{1,0:T(8,128)(2,1)S(1)}, bf16[2,1024,512]{2,1,0:T(8,128)(2,1)S(1)}) custom-call(bf16[512,1024]{1,0:T(8,128)(2,1)S(1)} %get-tuple-element.32.hg_ref, bf16[1024,512]{1,0:T(8,128)(2,1)S(1)} %get-tuple-element.36.w_ref, bf16[1024,4096]{1,0:T(8,128)(2,1)} %w_hbm.7, bf16[512,128]{1,0:T(8,128)(2,1)S(1)} %get-tuple-element.35.after_ref.low_ref, ...), custom_call_target="tpu_custom_call" | custom-call | flops 46000001024 | tf_op jit(solution)/shard_map/query_diag/pallas_call | solution.py:260
  10.1 0.1 collective-permute-start.5
  10.2 1.1 %collective-permute-done.1.r_ref = bf16[384,128]{1,0:T(8,128)(2,1)S(1)} collective-permute-done((bf16[384,128]{1,0:T(8,128)(2,1)S(1)}, bf16[384,128]{1,0:T(8,128)(2,1)S(1)}, u32[]{:S(2)}, u32[]{:S(2)}) %collective-permute-start.1) | collective-permute-done | bytes 98336 | tf_op jit(solution)/shard_map/ppermute | solution.py:35
  11.2 0.4 grad_a.1
  11.7 2.1 %collective-permute-start.3 = (bf16[512,128]{1,0:T(8,128)(2,1)S(1)}, bf16[512,128]{1,0:T(8,128)(2,1)S(1)}, u32[]{:S(2)}, u32[]{:S(2)}) collective-permute-start(bf16[512,128]{1,0:T(8,128)(2,1)S(1)} %get-tuple-element.39.after_ref), channel_id=1, source_target_pairs={{0,4},{4,0},{8,12},{12,8},{1,5},{5,1},{9,13},{13,9},{2,6},{6,2},{1... | collective-permute-start | bytes 393224 | tf_op jit(solution)/shard_map/ppermute | solution.py:35
  13.7 0.3 grad_b.1
  14.1 1.5 %collective-permute-start.7 = (bf16[512,128]{1,0:T(8,128)(2,1)S(1)}, bf16[512,128]{1,0:T(8,128)(2,1)S(1)}, u32[]{:S(2)}, u32[]{:S(2)}) collective-permute-start(bf16[512,128]{1,0:T(8,128)(2,1)S(1)} %get-tuple-element.42.after_ref), channel_id=1, source_target_pairs={{0,16},{16,0},{1,17},{17,1},{2,18},{18,2},{3,19},{19,3},{4,20},{20... | collective-permute-start | bytes 393224 | tf_op jit(solution)/shard_map/ppermute | solution.py:35
  15.6 1.2 %query_distant.1.mine_ref = bf16[512,1024]{1,0:T(8,128)(2,1)S(1)} custom-call(bf16[512,1024]{1,0:T(8,128)(2,1)S(1)} %get-tuple-element.32.hg_ref, bf16[2,1024,512]{2,1,0:T(8,128)(2,1)S(1)} %get-tuple-element.40.w_ref, bf16[512,128]{1,0:T(8,128)(2,1)S(1)} %get-tuple-element.42.after_ref), custom_call_target="tpu_custom_call" | custom-call | flops 11500000 | tf_op jit(solution)/shard_map/query_distant/pallas_call | solution.py:260
  16.9 0.3 far.1.rest_0_.far_ref
  17.2 1.7 %collective-permute-start.10 = (bf16[512,1152]{1,0:T(8,128)(2,1)S(1)}, bf16[512,1152]{1,0:T(8,128)(2,1)S(1)}, u32[]{:S(2)}, u32[]{:S(2)}) collective-permute-start(bf16[512,1152]{1,0:T(8,128)(2,1)S(1)} %far.1.rest_0_.far_ref), channel_id=1, source_target_pairs={{0,2},{1,3},{2,0},{3,1},{4,6},{5,7},{6,4},{7,5},{8,10},{9,11},{10,... | collective-permute-start | bytes 3538952 | tf_op jit(solution)/shard_map/ppermute | solution.py:35
  19.0 2.7 %collective-permute-start.6 = (bf16[512,128]{1,0:T(8,128)(2,1)S(1)}, bf16[512,128]{1,0:T(8,128)(2,1)S(1)}, u32[]{:S(2)}, u32[]{:S(2)}) collective-permute-start(bf16[512,128]{1,0:T(8,128)(2,1)S(1)} %step_a0.1.rest_0_.mine_ref), channel_id=1, source_target_pairs={{0,8},{4,12},{8,0},{12,4},{1,9},{5,13},{9,1},{13,5},{2,10},{6,14},... | collective-permute-start | bytes 393224 | tf_op jit(solution)/shard_map/ppermute | solution.py:35
  21.7 0.7 %collective-permute-start.8 = (bf16[512,128]{1,0:T(8,128)(2,1)S(1)}, bf16[512,128]{1,0:T(8,128)(2,1)S(1)}, u32[]{:S(2)}, u32[]{:S(2)}) collective-permute-start(bf16[512,128]{1,0:T(8,128)(2,1)S(1)} %step_b1.1.mine_ref.rest_0_.after_ref), channel_id=1, source_target_pairs={{0,4},{4,0},{8,12},{12,8},{1,5},{5,1},{9,13},{13,9},{2,6},{6,2},{1... | collective-permute-start | bytes 393224 | tf_op jit(solution)/shard_map/ppermute | solution.py:35
  22.4 2.7 %query_beside.1.rest_1_ = bf16[512,1024]{1,0:T(8,128)(2,1)S(1)} custom-call(bf16[512,1024]{1,0:T(8,128)(2,1)S(1)} %get-tuple-element.32.hg_ref, bf16[1024,4096]{1,0:T(8,128)(2,1)} %w_hbm.7, bf16[512,128]{1,0:T(8,128)(2,1)S(1)} %step_b1.1.mine_ref.rest_0_.after_ref), custom_call_target="tpu_custom_call" | custom-call | flops 2070000000 | tf_op jit(solution)/shard_map/query_beside/pallas_call | solution.py:260
  25.1 2.4 %collective-permute-done.8.got_ref = bf16[512,128]{1,0:T(8,128)(2,1)S(1)} collective-permute-done((bf16[512,128]{1,0:T(8,128)(2,1)S(1)}, bf16[512,128]{1,0:T(8,128)(2,1)S(1)}, u32[]{:S(2)}, u32[]{:S(2)}) %collective-permute-start.8) | collective-permute-done | bytes 131104 | tf_op jit(solution)/shard_map/ppermute | solution.py:35
  27.5 0.2 collective-permute-start.13
  27.7 0.8 %collective-permute-start.11 = (bf16[512,128]{1,0:T(8,128)(2,1)S(1)}, bf16[512,128]{1,0:T(8,128)(2,1)S(1)}, u32[]{:S(2)}, u32[]{:S(2)}) collective-permute-start(bf16[512,128]{1,0:T(8,128)(2,1)S(1)} %get-tuple-element.44.after_ref.mine_ref), channel_id=1, source_target_pairs={{0,16},{16,0},{1,17},{17,1},{2,18},{18,2},{3,19},{19,3},{4,20},{20... | collective-permute-start | bytes 393224 | tf_op jit(solution)/shard_map/ppermute | solution.py:35
  28.5 2.7 %query_close.1.rest_0_.mine_ref = bf16[512,1024]{1,0:T(8,128)(2,1)S(1)} custom-call(bf16[512,1024]{1,0:T(8,128)(2,1)S(1)} %get-tuple-element.32.hg_ref, bf16[1024,4096]{1,0:T(8,128)(2,1)} %w_hbm.7, bf16[512,128]{1,0:T(8,128)(2,1)S(1)} %get-tuple-element.44.after_ref.mine_ref), custom_call_target="tpu_custom_call" | custom-call | flops 3104999936 | tf_op jit(solution)/shard_map/query_close/pallas_call | solution.py:260
  31.1 0.0 copy-start.2
  31.1 0.1 collective-permute-start.9
  31.2 1.5 %collective-permute-done.11.got_ref = bf16[512,128]{1,0:T(8,128)(2,1)S(1)} collective-permute-done((bf16[512,128]{1,0:T(8,128)(2,1)S(1)}, bf16[512,128]{1,0:T(8,128)(2,1)S(1)}, u32[]{:S(2)}, u32[]{:S(2)}) %collective-permute-start.11) | collective-permute-done | bytes 131104 | tf_op jit(solution)/shard_map/ppermute | solution.py:35
  32.7 1.7 %collective-permute-start.12 = (bf16[512,128]{1,0:T(8,128)(2,1)S(1)}, bf16[512,128]{1,0:T(8,128)(2,1)S(1)}, u32[]{:S(2)}, u32[]{:S(2)}) collective-permute-start(bf16[512,128]{1,0:T(8,128)(2,1)S(1)} %step_a6.1.rest_0_.mine_a), channel_id=1, source_target_pairs={{0,4},{4,0},{8,12},{12,8},{1,5},{5,1},{9,13},{13,9},{2,6},{6,2},{1... | collective-permute-start | bytes 393224 | tf_op jit(solution)/shard_map/ppermute | solution.py:35
  34.4 0.4 collective-permute-done.13.got_ref
  34.9 0.5 %collective-permute-start.15 = (bf16[512,128]{1,0:T(8,128)(2,1)S(1)}, bf16[512,128]{1,0:T(8,128)(2,1)S(1)}, u32[]{:S(2)}, u32[]{:S(2)}) collective-permute-start(bf16[512,128]{1,0:T(8,128)(2,1)S(1)} %step_b7.1.after_ref.mine_b), channel_id=1, source_target_pairs={{0,16},{16,0},{1,17},{17,1},{2,18},{18,2},{3,19},{19,3},{4,20},{20... | collective-permute-start | bytes 393224 | tf_op jit(solution)/shard_map/ppermute | solution.py:35
  35.4 1.0 %multiply_cosine_fusion.1 = (f32[256,64]{1,0:T(8,128)S(1)}, f32[256,64]{1,0:T(8,128)S(1)}, f32[256,64]{1,0:T(8,128)S(1)}, f32[256,64]{1,0:T(8,128)S(1)}, f32[256,64]{1,0:T(8,128)S(1)}, /*index=5*/f32[256,64]{1,0:T(8,128)S(1)}) fusion(f32[64]{0:T(128)S(1)} %multiply_power_fusion, f32[256]{0:T(256)S(1)} %bitcast.6, f32[256]{0:T(256)S(1)} %broadcast_add_fusion), kind=kLoop, calls=%fused_computation.4 | loop fusion | flops 65536 | bytes 395520 | tf_op jit(solution)/shard_map/cos | solution.py:281
  36.4 0.1 maximum_maximum_fusion.after_ref.sin_ref
  36.6 1.2 %collective-permute-done.12.got_a = bf16[512,128]{1,0:T(8,128)(2,1)S(1)} collective-permute-done((bf16[512,128]{1,0:T(8,128)(2,1)S(1)}, bf16[512,128]{1,0:T(8,128)(2,1)S(1)}, u32[]{:S(2)}, u32[]{:S(2)}) %collective-permute-start.12) | collective-permute-done | bytes 131104 | tf_op jit(solution)/shard_map/ppermute | solution.py:35
  37.8 0.5 update.1
  38.3 0.1 collective-permute-start.14
  38.3 1.6 %collective-permute-done.15.got_b = bf16[512,128]{1,0:T(8,128)(2,1)S(1)} collective-permute-done((bf16[512,128]{1,0:T(8,128)(2,1)S(1)}, bf16[512,128]{1,0:T(8,128)(2,1)S(1)}, u32[]{:S(2)}, u32[]{:S(2)}) %collective-permute-start.15) | collective-permute-done | bytes 131104 | tf_op jit(solution)/shard_map/ppermute | solution.py:35
  39.9 0.2 norm.1
  40.1 0.1 collective-permute-start.17
  40.3 1.1 %collective-permute-start.16 = (bf16[512,128]{1,0:T(8,128)(2,1)S(1)}, bf16[512,128]{1,0:T(8,128)(2,1)S(1)}, u32[]{:S(2)}, u32[]{:S(2)}) collective-permute-start(bf16[512,128]{1,0:T(8,128)(2,1)S(1)} %merge.1.after_ref.s_ref), channel_id=1, source_target_pairs={{0,2},{1,3},{2,0},{3,1},{4,6},{5,7},{6,4},{7,5},{8,10},{9,11},{10,... | collective-permute-start | bytes 393224 | tf_op jit(solution)/shard_map/ppermute | solution.py:35
  41.4 0.1 maximum_maximum_fusion.1.cos_ref
  41.5 0.0 copy-start
  41.5 0.0 copy-start.1
  41.6 1.1 %collective-permute-start.18 = (bf16[32,128]{1,0:T(8,128)(2,1)S(1)}, bf16[32,128]{1,0:T(8,128)(2,1)S(1)}, u32[]{:S(2)}, u32[]{:S(2)}) collective-permute-start(bf16[32,128]{1,0:T(8,128)(2,1)S(1)} %norm_merge.1.sn_ref), channel_id=1, source_target_pairs={{0,2},{1,3},{2,0},{3,1},{4,6},{5,7},{6,4},{7,5},{8,10},{9,11},{10,... | collective-permute-start | bytes 24584 | tf_op jit(solution)/shard_map/ppermute | solution.py:35
  42.6 1.5 %collective-permute-done.10.far_got = bf16[512,1152]{1,0:T(8,128)(2,1)S(1)} collective-permute-done((bf16[512,1152]{1,0:T(8,128)(2,1)S(1)}, bf16[512,1152]{1,0:T(8,128)(2,1)S(1)}, u32[]{:S(2)}, u32[]{:S(2)}) %collective-permute-start.10) | collective-permute-done | bytes 1179680 | tf_op jit(solution)/shard_map/ppermute | solution.py:35
  44.1 0.5 base.1
  44.6 2.2 %collective-permute-done.18.rn_ref = bf16[32,128]{1,0:T(8,128)(2,1)S(1)} collective-permute-done((bf16[32,128]{1,0:T(8,128)(2,1)S(1)}, bf16[32,128]{1,0:T(8,128)(2,1)S(1)}, u32[]{:S(2)}, u32[]{:S(2)}) %collective-permute-start.18) | collective-permute-done | bytes 8224 | tf_op jit(solution)/shard_map/ppermute | solution.py:35
  46.8 2.0 %final.1 = (f32[1024,128]{1,0:T(8,128)}, f32[128,1024]{1,0:T(8,128)}, bf16[512,1024]{1,0:T(8,128)(2,1)}) custom-call(f32[512,1024]{1,0:T(8,128)S(1)} %get-tuple-element.50.base_ref, f32[512,128]{1,0:T(8,128)S(1)} %get-tuple-element.51.low_ref, bf16[512,128]{1,0:T(8,128)(2,1)S(1)} %merge.1.after_ref.s_ref, ...), custom_call_target="tpu_custom_call" | custom-call | flops 2070000000 | tf_op jit(solution)/shard_map/final/pallas_call | solution.py:260
  (28 shorter events, 0.3 us)
Async XLA Ops:
  0.6 3.4 %copy-start.3 = (f32[1024]{0:T(1024)S(1)}, f32[1024]{0:T(1024)}, u32[]{:S(2)}) copy-start(f32[1024]{0:T(1024)} %param.14) | copy-start | bytes 12292
  3.0 1.6 %collective-permute-start = (bf16[384,128]{1,0:T(8,128)(2,1)S(1)}, bf16[384,128]{1,0:T(8,128)(2,1)S(1)}, u32[]{:S(2)}, u32[]{:S(2)}) collective-permute-start(bf16[384,128]{1,0:T(8,128)(2,1)S(1)} %get-tuple-element.34.x_ref), channel_id=1, source_target_pairs={{0,1},{1,0},{2,3},{3,2},{4,5},{5,4},{6,7},{7,6},{8,9},{9,8},{10,11... | collective-permute-start | bytes 294920 | tf_op jit(solution)/shard_map/ppermute | solution.py:35
  3.9 3.8 %collective-permute-start.2 = (bf16[384,128]{1,0:T(8,128)(2,1)S(1)}, bf16[384,128]{1,0:T(8,128)(2,1)S(1)}, u32[]{:S(2)}, u32[]{:S(2)}) collective-permute-start(bf16[384,128]{1,0:T(8,128)(2,1)S(1)} %rank_u.1.x_ref), channel_id=1, source_target_pairs={{0,1},{1,0},{2,3},{3,2},{4,5},{5,4},{6,7},{7,6},{8,9},{9,8},{10,11... | collective-permute-start | bytes 294920 | tf_op jit(solution)/shard_map/ppermute | solution.py:35
  4.7 6.6 %collective-permute-start.1 = (bf16[384,128]{1,0:T(8,128)(2,1)S(1)}, bf16[384,128]{1,0:T(8,128)(2,1)S(1)}, u32[]{:S(2)}, u32[]{:S(2)}) collective-permute-start(bf16[384,128]{1,0:T(8,128)(2,1)S(1)} %low_v.1.after_ref.s_ref), channel_id=1, source_target_pairs={{0,2},{1,3},{2,0},{3,1},{4,6},{5,7},{6,4},{7,5},{8,10},{9,11},{10,... | collective-permute-start | bytes 294920 | tf_op jit(solution)/shard_map/ppermute | solution.py:35
  7.7 6.0 %collective-permute-start.4 = (bf16[384,128]{1,0:T(8,128)(2,1)S(1)}, bf16[384,128]{1,0:T(8,128)(2,1)S(1)}, u32[]{:S(2)}, u32[]{:S(2)}) collective-permute-start(bf16[384,128]{1,0:T(8,128)(2,1)S(1)} %low_u.1.after_ref.s_ref), channel_id=1, source_target_pairs={{0,2},{1,3},{2,0},{3,1},{4,6},{5,7},{6,4},{7,5},{8,10},{9,11},{10,... | collective-permute-start | bytes 294920 | tf_op jit(solution)/shard_map/ppermute | solution.py:35
  10.1 6.8 %collective-permute-start.5 = (bf16[512,1152]{1,0:T(8,128)(2,1)S(1)}, bf16[512,1152]{1,0:T(8,128)(2,1)S(1)}, u32[]{:S(2)}, u32[]{:S(2)}) collective-permute-start(bf16[512,1152]{1,0:T(8,128)(2,1)S(1)} %get-tuple-element.37.after_ref.diag_ref), channel_id=1, source_target_pairs={{0,1},{1,0},{2,3},{3,2},{4,5},{5,4},{6,7},{7,6},{8,9},{9,8},{10,11... | collective-permute-start | bytes 3538952 | tf_op jit(solution)/shard_map/ppermute | solution.py:35
  11.7 7.3 %collective-permute-start.3 = (bf16[512,128]{1,0:T(8,128)(2,1)S(1)}, bf16[512,128]{1,0:T(8,128)(2,1)S(1)}, u32[]{:S(2)}, u32[]{:S(2)}) collective-permute-start(bf16[512,128]{1,0:T(8,128)(2,1)S(1)} %get-tuple-element.39.after_ref), channel_id=1, source_target_pairs={{0,4},{4,0},{8,12},{12,8},{1,5},{5,1},{9,13},{13,9},{2,6},{6,2},{1... | collective-permute-start | bytes 393224 | tf_op jit(solution)/shard_map/ppermute | solution.py:35
  14.1 7.6 %collective-permute-start.7 = (bf16[512,128]{1,0:T(8,128)(2,1)S(1)}, bf16[512,128]{1,0:T(8,128)(2,1)S(1)}, u32[]{:S(2)}, u32[]{:S(2)}) collective-permute-start(bf16[512,128]{1,0:T(8,128)(2,1)S(1)} %get-tuple-element.42.after_ref), channel_id=1, source_target_pairs={{0,16},{16,0},{1,17},{17,1},{2,18},{18,2},{3,19},{19,3},{4,20},{20... | collective-permute-start | bytes 393224 | tf_op jit(solution)/shard_map/ppermute | solution.py:35
  17.2 26.9 %collective-permute-start.10 = (bf16[512,1152]{1,0:T(8,128)(2,1)S(1)}, bf16[512,1152]{1,0:T(8,128)(2,1)S(1)}, u32[]{:S(2)}, u32[]{:S(2)}) collective-permute-start(bf16[512,1152]{1,0:T(8,128)(2,1)S(1)} %far.1.rest_0_.far_ref), channel_id=1, source_target_pairs={{0,2},{1,3},{2,0},{3,1},{4,6},{5,7},{6,4},{7,5},{8,10},{9,11},{10,... | collective-permute-start | bytes 3538952 | tf_op jit(solution)/shard_map/ppermute | solution.py:35
  19.0 8.7 %collective-permute-start.6 = (bf16[512,128]{1,0:T(8,128)(2,1)S(1)}, bf16[512,128]{1,0:T(8,128)(2,1)S(1)}, u32[]{:S(2)}, u32[]{:S(2)}) collective-permute-start(bf16[512,128]{1,0:T(8,128)(2,1)S(1)} %step_a0.1.rest_0_.mine_ref), channel_id=1, source_target_pairs={{0,8},{4,12},{8,0},{12,4},{1,9},{5,13},{9,1},{13,5},{2,10},{6,14},... | collective-permute-start | bytes 393224 | tf_op jit(solution)/shard_map/ppermute | solution.py:35
  21.7 5.8 %collective-permute-start.8 = (bf16[512,128]{1,0:T(8,128)(2,1)S(1)}, bf16[512,128]{1,0:T(8,128)(2,1)S(1)}, u32[]{:S(2)}, u32[]{:S(2)}) collective-permute-start(bf16[512,128]{1,0:T(8,128)(2,1)S(1)} %step_b1.1.mine_ref.rest_0_.after_ref), channel_id=1, source_target_pairs={{0,4},{4,0},{8,12},{12,8},{1,5},{5,1},{9,13},{13,9},{2,6},{6,2},{1... | collective-permute-start | bytes 393224 | tf_op jit(solution)/shard_map/ppermute | solution.py:35
  27.5 7.4 %collective-permute-start.13 = (bf16[512,128]{1,0:T(8,128)(2,1)S(1)}, bf16[512,128]{1,0:T(8,128)(2,1)S(1)}, u32[]{:S(2)}, u32[]{:S(2)}) collective-permute-start(bf16[512,128]{1,0:T(8,128)(2,1)S(1)} %step_b3.1.rest_0_.mine_ref), channel_id=1, source_target_pairs={{0,8},{4,12},{8,0},{12,4},{1,9},{5,13},{9,1},{13,5},{2,10},{6,14},... | collective-permute-start | bytes 393224 | tf_op jit(solution)/shard_map/ppermute | solution.py:35
  27.7 5.0 %collective-permute-start.11 = (bf16[512,128]{1,0:T(8,128)(2,1)S(1)}, bf16[512,128]{1,0:T(8,128)(2,1)S(1)}, u32[]{:S(2)}, u32[]{:S(2)}) collective-permute-start(bf16[512,128]{1,0:T(8,128)(2,1)S(1)} %get-tuple-element.44.after_ref.mine_ref), channel_id=1, source_target_pairs={{0,16},{16,0},{1,17},{17,1},{2,18},{18,2},{3,19},{19,3},{4,20},{20... | collective-permute-start | bytes 393224 | tf_op jit(solution)/shard_map/ppermute | solution.py:35
  31.1 4.3 %copy-start.2 = (s32[256]{0:T(256)S(1)}, s32[256]{0:T(256)}, u32[]{:S(2)}) copy-start(s32[256]{0:T(256)} %param.15) | copy-start | bytes 3076
  31.1 11.5 %collective-permute-start.9 = (bf16[512,1024]{1,0:T(8,128)(2,1)S(1)}, bf16[512,1024]{1,0:T(8,128)(2,1)S(1)}, u32[]{:S(2)}, u32[]{:S(2)}) collective-permute-start(bf16[512,1024]{1,0:T(8,128)(2,1)S(1)} %get-tuple-element.45), channel_id=1, source_target_pairs={{0,1},{1,0},{2,3},{3,2},{4,5},{5,4},{6,7},{7,6},{8,9},{9,8},{10,11... | collective-permute-start | bytes 3145736 | tf_op jit(solution)/shard_map/ppermute | solution.py:35
  32.7 5.0 %collective-permute-start.12 = (bf16[512,128]{1,0:T(8,128)(2,1)S(1)}, bf16[512,128]{1,0:T(8,128)(2,1)S(1)}, u32[]{:S(2)}, u32[]{:S(2)}) collective-permute-start(bf16[512,128]{1,0:T(8,128)(2,1)S(1)} %step_a6.1.rest_0_.mine_a), channel_id=1, source_target_pairs={{0,4},{4,0},{8,12},{12,8},{1,5},{5,1},{9,13},{13,9},{2,6},{6,2},{1... | collective-permute-start | bytes 393224 | tf_op jit(solution)/shard_map/ppermute | solution.py:35
  34.9 5.0 %collective-permute-start.15 = (bf16[512,128]{1,0:T(8,128)(2,1)S(1)}, bf16[512,128]{1,0:T(8,128)(2,1)S(1)}, u32[]{:S(2)}, u32[]{:S(2)}) collective-permute-start(bf16[512,128]{1,0:T(8,128)(2,1)S(1)} %step_b7.1.after_ref.mine_b), channel_id=1, source_target_pairs={{0,16},{16,0},{1,17},{17,1},{2,18},{18,2},{3,19},{19,3},{4,20},{20... | collective-permute-start | bytes 393224 | tf_op jit(solution)/shard_map/ppermute | solution.py:35
  38.3 1.9 %collective-permute-start.14 = (bf16[512,128]{1,0:T(8,128)(2,1)S(1)}, bf16[512,128]{1,0:T(8,128)(2,1)S(1)}, u32[]{:S(2)}, u32[]{:S(2)}) collective-permute-start(bf16[512,128]{1,0:T(8,128)(2,1)S(1)} %get-tuple-element.46.after_ref.x_ref), channel_id=1, source_target_pairs={{0,1},{1,0},{2,3},{3,2},{4,5},{5,4},{6,7},{7,6},{8,9},{9,8},{10,11... | collective-permute-start | bytes 393224 | tf_op jit(solution)/shard_map/ppermute | solution.py:35
  40.1 1.4 %collective-permute-start.17 = (bf16[32,128]{1,0:T(8,128)(2,1)S(1)}, bf16[32,128]{1,0:T(8,128)(2,1)S(1)}, u32[]{:S(2)}, u32[]{:S(2)}) collective-permute-start(bf16[32,128]{1,0:T(8,128)(2,1)S(1)} %get-tuple-element.49.after_ref.a_ref), channel_id=1, source_target_pairs={{0,1},{1,0},{2,3},{3,2},{4,5},{5,4},{6,7},{7,6},{8,9},{9,8},{10,11... | collective-permute-start | bytes 24584 | tf_op jit(solution)/shard_map/ppermute | solution.py:35
  40.3 6.5 %collective-permute-start.16 = (bf16[512,128]{1,0:T(8,128)(2,1)S(1)}, bf16[512,128]{1,0:T(8,128)(2,1)S(1)}, u32[]{:S(2)}, u32[]{:S(2)}) collective-permute-start(bf16[512,128]{1,0:T(8,128)(2,1)S(1)} %merge.1.after_ref.s_ref), channel_id=1, source_target_pairs={{0,2},{1,3},{2,0},{3,1},{4,6},{5,7},{6,4},{7,5},{8,10},{9,11},{10,... | collective-permute-start | bytes 393224 | tf_op jit(solution)/shard_map/ppermute | solution.py:35
  41.5 5.2 %copy-start = (f32[1024,128]{1,0:T(8,128)S(1)}, f32[1024,128]{1,0:T(8,128)}, u32[]{:S(2)}) copy-start(f32[1024,128]{1,0:T(8,128)} %a_ref.1) | copy-start | bytes 1572868
  41.5 5.2 %copy-start.1 = (f32[128,1024]{1,0:T(8,128)S(1)}, f32[128,1024]{1,0:T(8,128)}, u32[]{:S(2)}) copy-start(f32[128,1024]{1,0:T(8,128)} %b_ref.1) | copy-start | bytes 1572868
  41.6 5.2 %collective-permute-start.18 = (bf16[32,128]{1,0:T(8,128)(2,1)S(1)}, bf16[32,128]{1,0:T(8,128)(2,1)S(1)}, u32[]{:S(2)}, u32[]{:S(2)}) collective-permute-start(bf16[32,128]{1,0:T(8,128)(2,1)S(1)} %norm_merge.1.sn_ref), channel_id=1, source_target_pairs={{0,2},{1,3},{2,0},{3,1},{4,6},{5,7},{6,4},{7,5},{8,10},{9,11},{10,... | collective-permute-start | bytes 24584 | tf_op jit(solution)/shard_map/ppermute | solution.py:35
